TPU v7x, 32 devices: a whole 2x2x4 slice. The times are simulated.
32 devices in a mesh: groups: 2 (over y), space: 4 (over z), rep: 4 (over x, core).
Axes of the slice: x: 2, y: 2, z: 4, core: 2. Of those that a mesh axis runs over, the one named last changes fastest.
Arguments:
- grid_latent: bfloat16 [8, 512, 512], P(('groups', 'rep'), 'space'), parts along dimension 0, may hold values from -6 to 6
- mesh_latent: bfloat16 [8, 256, 512], P(('groups', 'rep'), 'space'), parts along dimension 0, may hold values from -6 to 6
- mesh_cotangent: bfloat16 [8, 256, 512], P(('groups', 'rep'), 'space'), parts along dimension 0, may hold values from -6 to 6
- weights: bfloat16 [512, 2048], replicated, may hold values from -0.25 to 0.25
- g2m_pick: int32 [4, 3, 16], P('space'), may hold values from 0 to 127
- g2m_sender: int32 [1024], P('space'), may hold values from 0 to 47, as said below
- g2m_receiver: int32 [1024], P('space'), may hold values from 0 to 63
- m2m_pick: int32 [4, 4, 8], P('space'), may hold values from 0 to 63
- m2m_sender: int32 [1024], P('space'), may hold values from 0 to 31, as said below
- m2m_receiver: int32 [1024], P('space'), may hold values from 0 to 63
Outputs:
- mesh_out: bfloat16 [8, 256, 512], P(('groups', 'rep'), 'space'), parts along dimension 0
- grid_grad: bfloat16 [8, 512, 512], P(('groups', 'rep'), 'space'), parts along dimension 0
- weight_grad: float32 [1024, 2048], P(('groups', 'space')), parts along dimension 0
There are 2 independent parts, one for each index of `groups`. A program takes and returns all parts, laid end to end along the dimension named above; an argument that names none is the same for every part. Nothing has to cross between parts.
Inputs may be any that keep to these rules, and one draw needn't show every extreme that they name: `g2m_sender`: for a g2m edge of block d with sender value j*16+k, the source block d+j-1 lies within 0 to 3. `m2m_sender`: for an edge of block d with sender value s*8+k: s is d, d-1 or d+1, or else k < 2; both bounds are reached in every block.
All inputs are finite; a program needn't handle non-finite values.
Results may differ from a plain program's by a relative error of at most 0.014.
Values may be sent and summed in bfloat16 or wider, within the bound.
No kernel may reach another device: no remote copies, remote signals or barrier semaphores. Data moves between devices by JAX's collectives and lax.ppermute only.
A program may use at most 64 MiB of HBM per device.

v0:
```python
import jax
import jax.numpy as jnp
from jax import lax
from jax.sharding import PartitionSpec as P

EPSILON = 1e-05


def with_halo(cells, sides, width):
    for axis, dim in sides:
        count = lax.axis_size(axis)
        ends = count - 1
        head = lax.slice_in_dim(cells, 0, width, axis=dim)
        tail = lax.slice_in_dim(cells, cells.shape[dim] - width, cells.shape[dim], axis=dim)
        cells = jnp.concatenate(
            [
                lax.ppermute(tail, axis, [(i, (i + 1) % count) for i in range(ends)]),
                cells,
                lax.ppermute(head, axis, [((i + 1) % count, i) for i in range(ends)]),
            ],
            axis=dim,
        )
    return cells


def swish(values):
    return values * jax.nn.sigmoid(values)


def swish_slope(values):
    squash = jax.nn.sigmoid(values)
    return squash * (1.0 + values * (1.0 - squash))


def norm_rows(values):
    centred = values - jnp.mean(values, -1, keepdims=True)
    return centred * lax.rsqrt(jnp.mean(centred * centred, -1, keepdims=True) + EPSILON)


def norm_rows_back(values, upstream):
    centred = values - jnp.mean(values, -1, keepdims=True)
    scaled = lax.rsqrt(jnp.mean(centred * centred, -1, keepdims=True) + EPSILON)
    normed = centred * scaled
    return scaled * (
        upstream
        - jnp.mean(upstream, -1, keepdims=True)
        - normed * jnp.mean(upstream * normed, -1, keepdims=True)
    )


def slot_rows(pick_row):
    listed = pick_row.reshape(-1)
    return listed


def mesh_route(outgoing, capacity, peer_count):
    columns = outgoing.shape[1]
    pieces = lax.all_to_all(
        outgoing.reshape(peer_count, capacity, columns),
        "space",
        split_axis=0,
        concat_axis=0,
        tiled=True,
    )
    arrived = pieces.reshape(peer_count * capacity, columns)
    return arrived


def grid_route(outgoing, capacity):
    columns = outgoing.shape[1]
    lists = outgoing.reshape(3, capacity, columns)
    rims = with_halo(jnp.stack([lists[0], lists[2]]), (("space", 0),), 1)
    return jnp.concatenate([rims[0], lists[1], rims[3]], axis=0)


def edge_pass(arrived, recv_table, located, receiver, w_send, w_recv):
    recv_proj = jnp.dot(recv_table, w_recv, preferred_element_type=jnp.float32)
    slot_proj = jnp.dot(arrived, w_send, preferred_element_type=jnp.float32)
    activation = slot_proj[located] + recv_proj[receiver]
    message = swish(activation).astype(jnp.bfloat16)
    member = (
        receiver[None, :] == jnp.arange(recv_table.shape[0], dtype=jnp.int32)[:, None]
    ).astype(jnp.bfloat16)
    summed = jnp.dot(member, message, preferred_element_type=jnp.float32)
    return (activation, member, summed)


def backward_pass(slot_count, located, activation, member, receiver, agg_grad, w_send):
    edge_grad = (agg_grad[receiver] * swish_slope(activation)).astype(jnp.bfloat16)
    recv_sum = jnp.dot(member, edge_grad, preferred_element_type=jnp.float32).astype(jnp.bfloat16)
    slot_member = (located[None, :] == jnp.arange(slot_count, dtype=jnp.int32)[:, None]).astype(
        jnp.bfloat16
    )
    slot_sum = jnp.dot(slot_member, edge_grad, preferred_element_type=jnp.float32).astype(
        jnp.bfloat16
    )
    returned = jnp.dot(slot_sum, w_send.T, preferred_element_type=jnp.float32).astype(jnp.bfloat16)
    return (recv_sum, slot_sum, returned)


def gather_back(listed, back_rows, row_count):
    owner = (listed[None, :] == jnp.arange(row_count, dtype=jnp.int32)[:, None]).astype(
        jnp.bfloat16
    )
    return jnp.dot(owner, back_rows, preferred_element_type=jnp.float32)


def body(
    grid_latent,
    mesh_latent,
    mesh_cotangent,
    weights,
    g2m_pick,
    g2m_sender,
    g2m_receiver,
    m2m_pick,
    m2m_sender,
    m2m_receiver,
):
    grid_rows = grid_latent[0]
    mesh_rows = mesh_latent[0]
    upstream = mesh_cotangent[0].astype(jnp.float32)
    latent = weights.shape[0]
    encode_sender = weights[:, :latent]
    encode_receiver = weights[:, latent : 2 * latent]
    process_sender = weights[:, 2 * latent : 3 * latent]
    process_receiver = weights[:, 3 * latent :]
    peer_count = lax.axis_size("space")
    grid_cap = g2m_pick.shape[2]
    mesh_cap = m2m_pick.shape[2]
    grid_listed = g2m_pick[0].reshape(-1)
    grid_arrived = grid_route(grid_rows[grid_listed], grid_cap)
    act_first, member_first, summed_first = edge_pass(
        grid_arrived, mesh_rows, g2m_sender, g2m_receiver, encode_sender, encode_receiver
    )
    mesh_first = (mesh_rows.astype(jnp.float32) + norm_rows(summed_first)).astype(jnp.bfloat16)
    mesh_listed = slot_rows(m2m_pick[0])
    mesh_arrived = mesh_route(mesh_first[mesh_listed], mesh_cap, peer_count)
    act_second, member_second, summed_second = edge_pass(
        mesh_arrived, mesh_first, m2m_sender, m2m_receiver, process_sender, process_receiver
    )
    mesh_final = (mesh_first.astype(jnp.float32) + norm_rows(summed_second)).astype(jnp.bfloat16)
    agg_second = norm_rows_back(summed_second, upstream)
    recv_second, slot_second, returned_second = backward_pass(
        mesh_arrived.shape[0],
        m2m_sender,
        act_second,
        member_second,
        m2m_receiver,
        agg_second,
        process_sender,
    )
    back_second = mesh_route(returned_second, mesh_cap, peer_count)
    mesh_grad = upstream + jnp.dot(
        recv_second, process_receiver.T, preferred_element_type=jnp.float32
    )
    mesh_grad = mesh_grad + gather_back(mesh_listed, back_second, mesh_rows.shape[0])
    agg_first = norm_rows_back(summed_first, mesh_grad)
    recv_first, slot_first, returned_first = backward_pass(
        grid_arrived.shape[0],
        g2m_sender,
        act_first,
        member_first,
        g2m_receiver,
        agg_first,
        encode_sender,
    )
    back_first = grid_route(returned_first, grid_cap)
    grid_grad = gather_back(grid_listed, back_first, grid_rows.shape[0]).astype(jnp.bfloat16)
    factor_pairs = (
        (grid_arrived, slot_first),
        (mesh_rows, recv_first),
        (mesh_arrived, slot_second),
        (mesh_first, recv_second),
    )
    blocks = []
    for first_factor, second_factor in factor_pairs:
        blocks.append(
            lax.dot_general(
                first_factor,
                second_factor,
                (((0,), (0,)), ((), ())),
                preferred_element_type=jnp.float32,
            )
        )
    shares = lax.psum_scatter(
        jnp.concatenate(blocks, axis=1).astype(jnp.bfloat16),
        "space",
        scatter_dimension=0,
        tiled=True,
    )
    weight_grad = lax.psum(shares, "rep").astype(jnp.float32)
    return (mesh_final[None], grid_grad[None], weight_grad)


def solution(mesh):
    return jax.shard_map(
        body,
        mesh=mesh,
        in_specs=(
            P(("groups", "rep"), "space", None),
            P(("groups", "rep"), "space", None),
            P(("groups", "rep"), "space", None),
            P(),
            P("space", None, None),
            P("space"),
            P("space"),
            P("space", None, None),
            P("space"),
            P("space"),
        ),
        out_specs=(
            P(("groups", "rep"), "space", None),
            P(("groups", "rep"), "space", None),
            P(("groups", "space"), None),
        ),
        check_vma=False,
    )
```

profile of v0, /device:TPU:0, one launch (start us, length us, event | category | flops | bytes accessed | tf_op | source)
XLA Modules:
  0.0 159.3 jit_solution(14490734945860943134)
XLA Ops:
  9.2 4.9 %collective-permute-start = (bf16[1,16,512]{2,1,0:T(8,128)(2,1)S(1)}, bf16[1,16,512]{2,1,0:T(8,128)(2,1)S(1)}, u32[]{:S(2)}, u32[]{:S(2)}) collective-permute-start(bf16[1,16,512]{2,1,0:T(8,128)(2,1)S(1)} %get-tuple-element.16), channel_id=1, source_target_pairs={{0,4},{4,8},{8,12},{1,5},{5,9},{9,13},{2,6},{6,10},{10,14},{3,7},{... | collective-permute-start | bytes 49160 | tf_op jit(solution)/shard_map/ppermute | solution.py:17
  14.1 1.3 collective-permute-start.1
  19.0 1.5 convert_reduce_fusion
  20.5 1.3 fusion.4
  21.8 1.3 eq.95
  23.1 1.0 gather_fusion.2
  24.9 1.0 gather_fusion.1
  27.0 1.2 gather_fusion.3
  28.3 5.9 %all-to-all-start = ((bf16[4,8,512]{2,1,0:T(8,128)(2,1)}), bf16[4,8,512]{2,1,0:T(8,128)(2,1)S(1)}, u32[]{:S(2)}, u32[]{:S(2)}) async-start(bf16[4,8,512]{2,1,0:T(8,128)(2,1)} %bitcast.8), calls=%async_computation | async-start | bytes 65536 | tf_op jit(solution)/shard_map/all_to_all | solution.py:58
  34.4 1.8 %gather_fusion.5 = f32[256,512]{1,0:T(8,128)} fusion(f32[64,512]{1,0:T(8,128)S(1)} %fusion.7, s32[1024]{0:T(1024)S(1)} %pad_clamp_fusion), kind=kCustom, calls=%fused_computation.5 | custom fusion | bytes 1049600 | tf_op jit(solution)/shard_map/gather | solution.py:79
  36.2 3.7 %all-to-all-done = bf16[4,8,512]{2,1,0:T(8,128)(2,1)S(1)} async-done(((bf16[4,8,512]{2,1,0:T(8,128)(2,1)}), bf16[4,8,512]{2,1,0:T(8,128)(2,1)S(1)}, u32[]{:S(2)}, u32[]{:S(2)}) %all-to-all-start) | async-done | bytes 32800 | tf_op jit(solution)/shard_map/all_to_all | solution.py:58
  40.5 1.8 %gather_fusion.4 = f32[256,512]{1,0:T(8,128)} fusion(f32[32,512]{1,0:T(8,128)S(1)} %fusion.10, s32[1024]{0:T(1024)S(1)} %pad_clamp_fusion.1), kind=kCustom, calls=%fused_computation.4 | custom fusion | bytes 1049600 | tf_op jit(solution)/shard_map/gather | solution.py:79
  42.2 1.6 %fusion.54 = (f32[64]{0:T(128)S(1)}, f32[64,512]{1,0:T(8,128)S(1)}) fusion(f32[256,512]{1,0:T(8,128)} %gather_fusion.4, f32[256,512]{1,0:T(8,128)} %gather_fusion.5, s32[256]{0:T(256)S(1)} %copy-done.21), kind=kOutput, calls=%fused_computation.121 | convolution fusion | flops 17612736 | bytes 1180928 | tf_op jit(solution)/shard_map/dot_general | solution.py:84
  45.0 1.9 %gather_fusion.6 = f32[256,512]{1,0:T(8,128)} fusion(f32[64,512]{1,0:T(8,128)S(1)} %get-tuple-element.11, s32[1024]{0:T(1024)} %copy-done.18), kind=kCustom, calls=%fused_computation.6 | custom fusion | bytes 1049600 | tf_op jit(solution)/shard_map/gather | solution.py:89
  46.9 1.6 %multiply_convert_fusion.1 = bf16[256,512]{1,0:T(8,128)(2,1)S(1)} fusion(f32[256,512]{1,0:T(8,128)} %gather_fusion.6, f32[256,512]{1,0:T(8,128)} %gather_fusion.4, f32[256,512]{1,0:T(8,128)} %gather_fusion.5), kind=kLoop, calls=%fused_computation.26 | loop fusion | flops 1310720 | bytes 1835008 | tf_op jit(solution)/shard_map/convert_element_type | solution.py:89
  51.1 3.9 %all-to-all-start.1 = ((bf16[4,8,512]{2,1,0:T(8,128)(2,1)}), bf16[4,8,512]{2,1,0:T(8,128)(2,1)}, u32[]{:S(2)}, u32[]{:S(2)}) async-start(bf16[4,8,512]{2,1,0:T(8,128)(2,1)} %fusion.3), calls=%async_computation.1 | async-start | bytes 65536 | tf_op jit(solution)/shard_map/all_to_all | solution.py:58
  55.0 2.0 %convolution_convert_fusion = bf16[512,512]{0,1:T(8,128)(2,1)} fusion(bf16[64,512]{1,0:T(8,128)(2,1)S(1)} %add_convert_fusion.1, bf16[64,512]{1,0:T(8,128)(2,1)} %convolution_convert_fusion.6), kind=kOutput, calls=%fused_computation.9 | convolution fusion | flops 33816576 | bytes 655360 | tf_op jit(solution)/shard_map/dot_general | solution.py:179
  57.0 1.9 %convolution_convert_fusion.1 = bf16[512,512]{0,1:T(8,128)(2,1)} fusion(bf16[32,512]{1,0:T(8,128)(2,1)} %copy-done.9, bf16[4,8,512]{2,1,0:T(8,128)(2,1)} %copy-done.10), kind=kOutput, calls=%fused_computation.10 | convolution fusion | flops 17039360 | bytes 589824 | tf_op jit(solution)/shard_map/dot_general | solution.py:179
  58.9 1.8 %all-to-all-done.1 = bf16[4,8,512]{2,1,0:T(8,128)(2,1)} async-done(((bf16[4,8,512]{2,1,0:T(8,128)(2,1)}), bf16[4,8,512]{2,1,0:T(8,128)(2,1)}, u32[]{:S(2)}, u32[]{:S(2)}) %all-to-all-start.1) | async-done | bytes 32800 | tf_op jit(solution)/shard_map/all_to_all | solution.py:58
  61.6 1.2 fusion.52
  63.6 1.2 gather_fusion.7
  65.7 1.3 fusion
  67.4 1.2 pad_maximum_fusion
  68.6 2.5 %copy.15 = bf16[512,2048]{1,0:T(8,128)(2,1)} copy(bf16[512,2048]{0,1:T(8,128)(2,1)S(1)} %pad_maximum_fusion) | data formatting | bytes 4194304
  71.1 1.3 convolution_convert_fusion.8
  72.4 42.2 %reduce-scatter.4.cloned.1.call-done = bf16[128,2048]{1,0:T(8,128)(2,1)} async-done(((bf16[512,2048]{1,0:T(8,128)(2,1)}), bf16[128,2048]{1,0:T(8,128)(2,1)}) %reduce-scatter.4.cloned.1.call-update) | async-done | bytes 524304
  114.7 2.0 %copy.16 = bf16[128,2048]{0,1:T(8,128)(2,1)} copy(bf16[128,2048]{1,0:T(8,128)(2,1)} %reduce-scatter.4.cloned.1.call-done) | data formatting | bytes 1048576
  116.7 1.3 collective-permute-start.2
  118.0 1.3 collective-permute-start.3
  119.5 5.1 %collective-permute-done.3 = bf16[1,16,512]{2,1,0:T(8,128)(2,1)S(1)} collective-permute-done((bf16[1,16,512]{2,1,0:T(8,128)(2,1)S(1)}, bf16[1,16,512]{2,1,0:T(8,128)(2,1)S(1)}, u32[]{:S(2)}, u32[]{:S(2)}) %collective-permute-start.3) | collective-permute-done | bytes 16416 | tf_op jit(solution)/shard_map/ppermute | solution.py:19
  125.4 24.8 %all-reduce.2.cloned.1.call-done = bf16[128,2048]{0,1:T(8,128)(2,1)} async-done(((bf16[128,2048]{0,1:T(8,128)(2,1)}), bf16[128,2048]{0,1:T(8,128)(2,1)}) %all-reduce.2.cloned.1.call-update) | async-done | bytes 524304 | tf_op jit(solution)/shard_map/psum | solution.py:192
  150.2 2.2 %copy.14 = f32[128,2048]{1,0:T(8,128)} copy(bf16[128,2048]{0,1:T(8,128)(2,1)} %all-reduce.2.cloned.1.call-done) | data formatting | bytes 1572864
  (105 shorter events, 15.7 us)
Async XLA Ops:
  7.2 1.3 copy-start
  9.2 14.9 %collective-permute-start = (bf16[1,16,512]{2,1,0:T(8,128)(2,1)S(1)}, bf16[1,16,512]{2,1,0:T(8,128)(2,1)S(1)}, u32[]{:S(2)}, u32[]{:S(2)}) collective-permute-start(bf16[1,16,512]{2,1,0:T(8,128)(2,1)S(1)} %get-tuple-element.16), channel_id=1, source_target_pairs={{0,4},{4,8},{8,12},{1,5},{5,9},{9,13},{2,6},{6,10},{10,14},{3,7},{... | collective-permute-start | bytes 49160 | tf_op jit(solution)/shard_map/ppermute | solution.py:17
  14.1 10.0 %collective-permute-start.1 = (bf16[1,16,512]{2,1,0:T(8,128)(2,1)S(1)}, bf16[1,16,512]{2,1,0:T(8,128)(2,1)S(1)}, u32[]{:S(2)}, u32[]{:S(2)}) collective-permute-start(bf16[1,16,512]{2,1,0:T(8,128)(2,1)S(1)} %get-tuple-element.18), channel_id=1, source_target_pairs={{4,0},{8,4},{12,8},{5,1},{9,5},{13,9},{6,2},{10,6},{14,10},{7,3},{... | collective-permute-start | bytes 49160 | tf_op jit(solution)/shard_map/ppermute | solution.py:19
  16.8 7.3 %copy-start.17 = (s32[1024]{0:T(1024)}, s32[1024]{0:T(1024)S(1)}, u32[]{:S(2)}) copy-start(s32[1024]{0:T(1024)S(1)} %pad_clamp_fusion.3) | copy-start | bytes 12292
  17.5 17.0 %copy-start.18 = (s32[1024]{0:T(1024)}, s32[1024]{0:T(1024)S(1)}, u32[]{:S(2)}) copy-start(s32[1024]{0:T(1024)S(1)} %pad_clamp_fusion) | copy-start | bytes 12292
  23.1 1.6 copy-start.1
  24.1 1.8 %copy-start.13 = (bf16[1,16,512]{2,1,0:T(8,128)(2,1)}, bf16[1,16,512]{2,1,0:T(8,128)(2,1)S(1)}, u32[]{:S(2)}) copy-start(bf16[1,16,512]{2,1,0:T(8,128)(2,1)S(1)} %collective-permute-done) | copy-start | bytes 49156
  24.1 1.8 %copy-start.15 = (bf16[1,16,512]{2,1,0:T(8,128)(2,1)}, bf16[1,16,512]{2,1,0:T(8,128)(2,1)S(1)}, u32[]{:S(2)}) copy-start(bf16[1,16,512]{2,1,0:T(8,128)(2,1)S(1)} %collective-permute-done.1) | copy-start | bytes 49156
  24.9 1.0 copy-start.24
  25.9 1.1 copy-start.7
  26.3 9.9 %copy-start.19 = (f32[64]{0:T(128)}, f32[64]{0:T(128)S(1)}, u32[]{:S(2)}) copy-start(f32[64]{0:T(128)S(1)} %broadcast_multiply_fusion.5) | copy-start | bytes 772
  26.9 9.3 %copy-start.20 = (f32[64]{0:T(128)}, f32[64]{0:T(128)S(1)}, u32[]{:S(2)}) copy-start(f32[64]{0:T(128)S(1)} %add_rsqrt_fusion.1) | copy-start | bytes 772
  28.3 11.6 %all-to-all-start = ((bf16[4,8,512]{2,1,0:T(8,128)(2,1)}), bf16[4,8,512]{2,1,0:T(8,128)(2,1)S(1)}, u32[]{:S(2)}, u32[]{:S(2)}) async-start(bf16[4,8,512]{2,1,0:T(8,128)(2,1)} %bitcast.8), calls=%async_computation | async-start | bytes 65536 | tf_op jit(solution)/shard_map/all_to_all | solution.py:58
  40.5 1.8 %copy-start.21 = (s32[256]{0:T(256)S(1)}, s32[256]{0:T(256)}, u32[]{:S(2)}) copy-start(s32[256]{0:T(256)} %param.19) | copy-start | bytes 3076
  42.2 1.8 %copy-start.26 = (f32[64]{0:T(128)S(1)}, f32[64]{0:T(128)}, u32[]{:S(2)}) copy-start(f32[64]{0:T(128)} %convert_reduce_fusion) | copy-start | bytes 772
  42.2 1.9 %copy-start.6 = (bf16[1,64,512]{2,1,0:T(8,128)(2,1)S(1)}, bf16[1,64,512]{2,1,0:T(8,128)(2,1)}, u32[]{:S(2)}) copy-start(bf16[1,64,512]{2,1,0:T(8,128)(2,1)} %param.12) | copy-start | bytes 196612
  46.9 2.5 %copy-start.22 = (s32[256]{0:T(256)S(1)}, s32[256]{0:T(256)}, u32[]{:S(2)}) copy-start(s32[256]{0:T(256)} %param.19) | copy-start | bytes 3076
  46.9 14.6 %copy-start.3 = (f32[64,512]{1,0:T(8,128)S(1)}, f32[64,512]{1,0:T(8,128)}, u32[]{:S(2)}) copy-start(f32[64,512]{1,0:T(8,128)} %copy-done.2) | copy-start | bytes 393220
  49.4 0.8 copy-start.9
  51.1 9.6 %all-to-all-start.1 = ((bf16[4,8,512]{2,1,0:T(8,128)(2,1)}), bf16[4,8,512]{2,1,0:T(8,128)(2,1)}, u32[]{:S(2)}, u32[]{:S(2)}) async-start(bf16[4,8,512]{2,1,0:T(8,128)(2,1)} %fusion.3), calls=%async_computation.1 | async-start | bytes 65536 | tf_op jit(solution)/shard_map/all_to_all | solution.py:58
  55.0 59.7 %reduce-scatter.4.cloned.1.call-start = ((), (), s32[]{:S(2)}) async-start(), calls=%async_computation.4 | async-start | bytes 2621440
  63.6 1.6 copy-start.23
  64.9 0.8 copy-start.8
  64.9 0.8 copy-start.25
  64.9 2.1 %copy-start.14 = (bf16[1,16,512]{2,1,0:T(8,128)(2,1)S(1)}, bf16[1,16,512]{2,1,0:T(8,128)(2,1)}, u32[]{:S(2)}) copy-start(bf16[1,16,512]{2,1,0:T(8,128)(2,1)} %copy-done.13) | copy-start | bytes 49156
  64.9 2.1 %copy-start.16 = (bf16[1,16,512]{2,1,0:T(8,128)(2,1)S(1)}, bf16[1,16,512]{2,1,0:T(8,128)(2,1)}, u32[]{:S(2)}) copy-start(bf16[1,16,512]{2,1,0:T(8,128)(2,1)} %copy-done.15) | copy-start | bytes 49156
  64.9 2.4 %copy-start.4 = (bf16[512,512]{0,1:T(8,128)(2,1)S(1)}, bf16[512,512]{0,1:T(8,128)(2,1)}, u32[]{:S(2)}) copy-start(bf16[512,512]{0,1:T(8,128)(2,1)} %convolution_convert_fusion) | copy-start | bytes 1572868
  64.9 2.4 %copy-start.5 = (bf16[512,512]{0,1:T(8,128)(2,1)S(1)}, bf16[512,512]{0,1:T(8,128)(2,1)}, u32[]{:S(2)}) copy-start(bf16[512,512]{0,1:T(8,128)(2,1)} %convolution_convert_fusion.1) | copy-start | bytes 1572868
  71.0 48.3 %copy-start.12 = (s32[3,16]{1,0:T(4,128)S(1)}, s32[3,16]{1,0:T(4,128)}, u32[]{:S(2)}) copy-start(s32[3,16]{1,0:T(4,128)} %copy-done.11) | copy-start | bytes 580
  71.1 79.2 %all-reduce.2.cloned.1.call-start = ((), (), s32[]{:S(2)}) async-start(), calls=%async_computation.3 | async-start | bytes 1048576 | tf_op jit(solution)/shard_map/psum | solution.py:192
  116.7 2.7 %collective-permute-start.2 = (bf16[1,16,512]{2,1,0:T(8,128)(2,1)S(1)}, bf16[1,16,512]{2,1,0:T(8,128)(2,1)S(1)}, u32[]{:S(2)}, u32[]{:S(2)}) collective-permute-start(bf16[1,16,512]{2,1,0:T(8,128)(2,1)S(1)} %get-tuple-element.13), channel_id=1, source_target_pairs={{0,4},{4,8},{8,12},{1,5},{5,9},{9,13},{2,6},{6,10},{10,14},{3,7},{... | collective-permute-start | bytes 49160 | tf_op jit(solution)/shard_map/ppermute | solution.py:17
  118.0 6.5 %collective-permute-start.3 = (bf16[1,16,512]{2,1,0:T(8,128)(2,1)S(1)}, bf16[1,16,512]{2,1,0:T(8,128)(2,1)S(1)}, u32[]{:S(2)}, u32[]{:S(2)}) collective-permute-start(bf16[1,16,512]{2,1,0:T(8,128)(2,1)S(1)} %get-tuple-element.14), channel_id=1, source_target_pairs={{4,0},{8,4},{12,8},{5,1},{9,5},{13,9},{6,2},{10,6},{14,10},{7,3},{... | collective-permute-start | bytes 49160 | tf_op jit(solution)/shard_map/ppermute | solution.py:19
  (3 other events, 1.8 us)
Sparse Core Ops, SparseCore 0:
  71.2 43.4 reduce-scatter.3
  117.7 32.4 all-reduce.1
where the time goes:
time: 160 us; the launch traced here: 159 us
  waiting for transfers between devices  77.7 us (49%)
  local copies, waits for them, and re-layouts  21.8 us (14%)
  starting transfers between devices  18.7 us (12%)
  matrix products  16.3 us (10%)
  between operations  14.5 us (9%)
  other arithmetic  10.3 us (6%)
    unnamed x3, waiting for transfers between devices  42.3 us
    psum x1, waiting for transfers between devices, body(): weight_grad = lax.psum(shares, 'rep').astype(jnp.float32)  24.8 us
    all_to_all x2, starting transfers between devices, mesh_route(): lax.all_to_all(outgoing.reshape(peer_count, capacity, columns), 'space',...  9.81 us
    unnamed x57, local copies, waits for them, and re-layouts  9.09 us
    ppermute x2, starting transfers between devices, with_halo(): lax.ppermute(tail, axis, [(i, (i + 1) % count) for i in range(ends)])  6.22 us
    dot_general x4, matrix products, body(): lax.dot_general(first_factor, second_factor, (((0,), (0,)), ((), ())), pr...  5.49 us
    all_to_all x2, waiting for transfers between devices, mesh_route(): lax.all_to_all(outgoing.reshape(peer_count, capacity, columns), 'space',...  5.46 us
    gather x4, local copies, waits for them, and re-layouts, edge_pass(): activation = slot_proj[located] + recv_proj[receiver]  5.45 us
  transfers between devices with their start and end apart: 8, of which 5 were waited for; matrix products, arithmetic and copies ran while one was open for 10% of the time, Pallas kernels for 0%

commit v1 on v0

--- a/solution.py
+++ b/solution.py
@@ -1,6 +1,10 @@
+import functools
+
 import jax
 import jax.numpy as jnp
 from jax import lax
+from jax.experimental import pallas as pl
+from jax.experimental.pallas import tpu as pltpu
 from jax.sharding import PartitionSpec as P
 
 EPSILON = 1e-05
@@ -105,7 +109,7 @@
     return jnp.dot(owner, back_rows, preferred_element_type=jnp.float32)
 
 
-def body(
+def partitioned_body(
     grid_latent,
     mesh_latent,
     mesh_cotangent,
@@ -193,26 +197,494 @@
     return (mesh_final[None], grid_grad[None], weight_grad)
 
 
+F32 = jnp.float32
+BF16 = jnp.bfloat16
+INDEX_ROWS = 16
+SAMPLE_EDGE_BYTES = 8 << 20
+
+
+def dot(left, right):
+    return jnp.dot(left, right, preferred_element_type=F32)
+
+
+def dot_first(left, right):
+    return lax.dot_general(left, right, (((0,), (0,)), ((), ())), preferred_element_type=F32)
+
+
+def dot_last(left, right):
+    return lax.dot_general(left, right, (((1,), (1,)), ((), ())), preferred_element_type=F32)
+
+
+def one_hot(labels, count):
+    rows = lax.broadcasted_iota(jnp.int32, (count, labels.shape[-1]), 0)
+    return (rows == labels).astype(F32).astype(BF16)
+
+
+def row_moments(values):
+    centred = values - jnp.mean(values, -1, keepdims=True)
+    return centred, lax.rsqrt(jnp.mean(centred * centred, -1, keepdims=True) + EPSILON)
+
+
+def moments_back(normed, scaled, upstream):
+    return scaled * (
+        upstream
+        - jnp.mean(upstream, -1, keepdims=True)
+        - normed * jnp.mean(upstream * normed, -1, keepdims=True)
+    )
+
+
+def pack_kernel(
+    grid_ref,
+    mesh_ref,
+    g2m_pick_ref,
+    g2m_sender_ref,
+    g2m_receiver_ref,
+    m2m_pick_ref,
+    m2m_sender_ref,
+    m2m_receiver_ref,
+    packed_ref,
+    index_ref,
+):
+    lists, capacity = g2m_pick_ref.shape[1:]
+    mesh_count = mesh_ref.shape[1]
+    regions, mesh_cap = m2m_pick_ref.shape[1:]
+    edges = g2m_sender_ref.shape[1]
+    grid_rows = grid_ref[0]
+    for i in range(lists):
+        picked = one_hot(g2m_pick_ref[0, i : i + 1, :], grid_rows.shape[0])
+        packed_ref[i * capacity : (i + 1) * capacity, :] = dot_first(picked, grid_rows).astype(BF16)
+    first = lists * capacity
+    packed_ref[first : first + mesh_count, :] = mesh_ref[0]
+    index_ref[...] = jnp.zeros_like(index_ref)
+    index_ref[0:1, 0:edges] = g2m_sender_ref[...].astype(F32)
+    index_ref[0:1, edges : 2 * edges] = g2m_receiver_ref[...].astype(F32)
+    index_ref[1:2, 0:edges] = m2m_sender_ref[...].astype(F32)
+    index_ref[1:2, edges : 2 * edges] = m2m_receiver_ref[...].astype(F32)
+    slots = regions * mesh_cap
+    lane = lax.broadcasted_iota(jnp.int32, (mesh_cap, slots), 1)
+    spread = (lane % mesh_cap == lax.broadcasted_iota(jnp.int32, (mesh_cap, slots), 0)).astype(F32)
+    spread = dot(m2m_pick_ref[0].astype(F32).astype(BF16), spread.astype(BF16))
+    lane = lax.broadcasted_iota(jnp.int32, (regions, slots), 1)
+    owned = lane // mesh_cap == lax.broadcasted_iota(jnp.int32, (regions, slots), 0)
+    index_ref[2:3, 0:slots] = jnp.sum(jnp.where(owned, spread, 0.0), 0, keepdims=True)
+    packed_ref[first + mesh_count :, :] = index_ref[...].astype(BF16)
+
+
+def edge_forward(table, hot, hot_receiver, slope_ref, first):
+    activation = dot_first(hot, table)
+    squash = 0.5 + 0.5 * jnp.tanh(0.5 * activation)
+    message = activation * squash
+    slope_ref[first : first + activation.shape[0], :] = (
+        squash + message * (1.0 - squash)
+    ).astype(BF16)
+    return dot(hot_receiver, message.astype(BF16))
+
+
+def forward_kernel(
+    regions,
+    listed,
+    mesh_count,
+    mesh_cap,
+    *refs,
+):
+    packed_refs = refs[:regions]
+    (
+        weights_ref,
+        mesh_out_ref,
+        grid_ref,
+        mesh_ref,
+        first_ref,
+        sent_ref,
+        index_ref,
+        slope_one_ref,
+        slope_two_ref,
+        normed_one_ref,
+        scaled_one_ref,
+        normed_two_ref,
+        scaled_two_ref,
+        packed_index,
+    ) = refs[regions:]
+    latent = weights_ref.shape[0]
+    edges = slope_one_ref.shape[0] // regions
+    capacity = listed // 3
+    slots = regions * mesh_cap
+    me = lax.axis_index("space")
+    for back, packed_ref in enumerate(packed_refs):
+        region = lax.rem(me + (regions - back), regions)
+        at = lambda rows: pl.ds(pl.multiple_of(region * rows, rows), rows)
+        grid_ref[at(listed), :] = packed_ref[:listed, :]
+        mesh_ref[at(mesh_count), :] = packed_ref[listed : listed + mesh_count, :]
+        packed_index[at(INDEX_ROWS), :] = packed_ref[listed + mesh_count :, :]
+    index_ref[...] = packed_index[...].astype(F32).astype(jnp.int32)
+
+    grid_proj = dot(grid_ref[...], weights_ref[:, :latent])
+    mesh_proj = dot(mesh_ref[...], weights_ref[:, latent : 2 * latent])
+    blank = jnp.zeros((capacity, latent), F32)
+    for d in range(regions):
+        hot_sender = one_hot(index_ref[d * INDEX_ROWS : d * INDEX_ROWS + 1, :edges], listed)
+        hot_receiver = one_hot(
+            index_ref[d * INDEX_ROWS : d * INDEX_ROWS + 1, edges:], mesh_count
+        )
+        before = (d - 1) * listed + 2 * capacity
+        within = d * listed + capacity
+        after = (d + 1) * listed
+        table = jnp.concatenate(
+            [
+                grid_proj[before : before + capacity] if d > 0 else blank,
+                grid_proj[within : within + capacity],
+                grid_proj[after : after + capacity] if d < regions - 1 else blank,
+                mesh_proj[d * mesh_count : (d + 1) * mesh_count],
+            ],
+            axis=0,
+        ).astype(BF16)
+        summed = edge_forward(
+            table,
+            jnp.concatenate([hot_sender, hot_receiver], axis=0),
+            hot_receiver,
+            slope_one_ref,
+            d * edges,
+        )
+        centred, scaled = row_moments(summed)
+        normed = centred * scaled
+        rows = slice(d * mesh_count, (d + 1) * mesh_count)
+        normed_one_ref[rows, :] = normed
+        scaled_one_ref[rows, :] = jnp.broadcast_to(scaled, (mesh_count, scaled_one_ref.shape[1]))
+        first_ref[rows, :] = (mesh_ref[rows, :].astype(F32) + normed).astype(BF16)
+
+    for s in range(regions):
+        hot = one_hot(index_ref[s * INDEX_ROWS + 2 : s * INDEX_ROWS + 3, :slots], mesh_count)
+        sent_ref[s * slots : (s + 1) * slots, :] = dot_first(
+            hot, first_ref[s * mesh_count : (s + 1) * mesh_count, :]
+        ).astype(BF16)
+    sent_proj = dot(sent_ref[...], weights_ref[:, 2 * latent : 3 * latent])
+    first_proj = dot(first_ref[...], weights_ref[:, 3 * latent :])
+    for d in range(regions):
+        hot_sender = one_hot(index_ref[d * INDEX_ROWS + 1 : d * INDEX_ROWS + 2, :edges], slots)
+        hot_receiver = one_hot(
+            index_ref[d * INDEX_ROWS + 1 : d * INDEX_ROWS + 2, edges:], mesh_count
+        )
+        pieces = [
+            sent_proj[s * slots + d * mesh_cap : s * slots + (d + 1) * mesh_cap]
+            for s in range(regions)
+        ]
+        table = jnp.concatenate(
+            pieces + [first_proj[d * mesh_count : (d + 1) * mesh_count]], axis=0
+        ).astype(BF16)
+        summed = edge_forward(
+            table,
+            jnp.concatenate([hot_sender, hot_receiver], axis=0),
+            hot_receiver,
+            slope_two_ref,
+            d * edges,
+        )
+        centred, scaled = row_moments(summed)
+        rows = slice(d * mesh_count, (d + 1) * mesh_count)
+        normed_two_ref[rows, :] = centred * scaled
+        scaled_two_ref[rows, :] = jnp.broadcast_to(scaled, (mesh_count, scaled_two_ref.shape[1]))
+    own = pl.ds(pl.multiple_of(me * mesh_count, mesh_count), mesh_count)
+    mesh_out_ref[0] = (first_ref[own, :].astype(F32) + normed_two_ref[own, :]).astype(BF16)
+
+
+def edge_backward(agg_grad, hot, hot_receiver, slope):
+    edge_grad = (dot_first(hot_receiver, agg_grad) * slope.astype(F32)).astype(BF16)
+    return dot(hot, edge_grad)
+
+
+def process_back_kernel(regions, mesh_cap, *refs):
+    cotangent_refs = refs[:regions]
+    (
+        weights_ref,
+        first_ref,
+        sent_ref,
+        index_ref,
+        slope_ref,
+        normed_ref,
+        scaled_ref,
+        mesh_grad_ref,
+        share_ref,
+        upstream_ref,
+        slot_ref,
+        recv_ref,
+    ) = refs[regions:]
+    latent = first_ref.shape[1]
+    mesh_count = first_ref.shape[0] // regions
+    edges = slope_ref.shape[0] // regions
+    slots = regions * mesh_cap
+    me = lax.axis_index("space")
+    for back, cotangent_ref in enumerate(cotangent_refs):
+        region = lax.rem(me + (regions - back), regions)
+        at = pl.ds(pl.multiple_of(region * mesh_count, mesh_count), mesh_count)
+        upstream_ref[at, :] = cotangent_ref[0].astype(F32)
+    agg_grad = moments_back(normed_ref[...], scaled_ref[:, 0:1], upstream_ref[...]).astype(BF16)
+    for d in range(regions):
+        labels = slice(d * INDEX_ROWS + 1, d * INDEX_ROWS + 2)
+        hot_sender = one_hot(index_ref[labels, :edges], slots)
+        hot_receiver = one_hot(index_ref[labels, edges:], mesh_count)
+        rows = slice(d * mesh_count, (d + 1) * mesh_count)
+        sums = edge_backward(
+            agg_grad[rows],
+            jnp.concatenate([hot_sender, hot_receiver], axis=0),
+            hot_receiver,
+            slope_ref[d * edges : (d + 1) * edges, :],
+        )
+        for s in range(regions):
+            first = s * slots + d * mesh_cap
+            slot_ref[first : first + mesh_cap, :] = sums[s * mesh_cap : (s + 1) * mesh_cap]
+        recv_ref[rows, :] = sums[slots:].astype(BF16)
+    slot_sum = slot_ref[...].astype(BF16)
+    columns = share_ref.shape[0]
+    mine = pl.ds(pl.multiple_of(me * columns, columns), columns)
+    share_ref[:, :latent] = dot_first(sent_ref[:, mine], slot_sum).astype(BF16)
+    share_ref[:, latent:] = dot_first(first_ref[:, mine], recv_ref[...]).astype(BF16)
+    returned = dot_last(slot_sum, weights_ref[:, 2 * latent : 3 * latent]).astype(BF16)
+    grad = upstream_ref[...] + dot_last(recv_ref[...], weights_ref[:, 3 * latent :])
+    for s in range(regions):
+        hot = one_hot(index_ref[s * INDEX_ROWS + 2 : s * INDEX_ROWS + 3, :slots], mesh_count)
+        rows = slice(s * mesh_count, (s + 1) * mesh_count)
+        mesh_grad_ref[rows, :] = grad[rows] + dot(hot, returned[s * slots : (s + 1) * slots])
+
+
+def encode_back_kernel(
+    regions,
+    weights_ref,
+    pick_ref,
+    grid_ref,
+    mesh_ref,
+    index_ref,
+    slope_ref,
+    normed_ref,
+    scaled_ref,
+    mesh_grad_ref,
+    grid_grad_ref,
+    share_ref,
+    slot_ref,
+    recv_ref,
+):
+    latent = mesh_ref.shape[1]
+    mesh_count = mesh_ref.shape[0] // regions
+    listed = grid_ref.shape[0] // regions
+    capacity = listed // 3
+    edges = slope_ref.shape[0] // regions
+    me = lax.axis_index("space")
+    agg_grad = moments_back(normed_ref[...], scaled_ref[:, 0:1], mesh_grad_ref[...]).astype(BF16)
+    blank = jnp.zeros((capacity, latent), BF16)
+    slot_ref[0:capacity, :] = blank
+    slot_ref[regions * listed - capacity :, :] = blank
+    for d in range(regions):
+        labels = slice(d * INDEX_ROWS, d * INDEX_ROWS + 1)
+        hot_sender = one_hot(index_ref[labels, :edges], listed)
+        hot_receiver = one_hot(index_ref[labels, edges:], mesh_count)
+        rows = slice(d * mesh_count, (d + 1) * mesh_count)
+        sums = edge_backward(
+            agg_grad[rows],
+            jnp.concatenate([hot_sender, hot_receiver], axis=0),
+            hot_receiver,
+            slope_ref[d * edges : (d + 1) * edges, :],
+        ).astype(BF16)
+        for j in range(3):
+            source = d + j - 1
+            if 0 <= source < regions:
+                first = source * listed + (2 - j) * capacity
+                slot_ref[first : first + capacity, :] = sums[j * capacity : (j + 1) * capacity]
+        recv_ref[rows, :] = sums[listed:]
+    columns = share_ref.shape[0]
+    mine = pl.ds(pl.multiple_of(me * columns, columns), columns)
+    share_ref[:, :latent] = dot_first(grid_ref[:, mine], slot_ref[...]).astype(BF16)
+    share_ref[:, latent:] = dot_first(mesh_ref[:, mine], recv_ref[...]).astype(BF16)
+    own = pl.ds(pl.multiple_of(me * listed, listed), listed)
+    returned = dot_last(slot_ref[own, :], weights_ref[:, :latent]).astype(BF16)
+    total = None
+    for i in range(3):
+        owner = one_hot(pick_ref[0, i : i + 1, :], grid_grad_ref.shape[1])
+        part = dot(owner, returned[i * capacity : (i + 1) * capacity])
+        total = part if total is None else total + part
+    grid_grad_ref[0] = total.astype(BF16)
+
+
+VMEM = pl.BlockSpec(memory_space=pltpu.VMEM)
+
+
+def call(kernel, operands, outputs, scratch, flops):
+    return pl.pallas_call(
+        kernel,
+        out_shape=[jax.ShapeDtypeStruct(shape, kind) for shape, kind in outputs],
+        in_specs=[VMEM] * len(operands),
+        out_specs=[VMEM] * len(outputs),
+        scratch_shapes=[pltpu.VMEM(shape, kind) for shape, kind in scratch],
+        compiler_params=pltpu.CompilerParams(vmem_limit_bytes=40 << 20),
+        cost_estimate=pl.CostEstimate(flops=flops, bytes_accessed=4 << 20, transcendentals=0),
+    )(*operands)
+
+
+def from_others(block):
+    count = lax.axis_size("space")
+    return [block] + [
+        lax.ppermute(block, "space", [(i, (i + step) % count) for i in range(count)])
+        for step in range(1, count)
+    ]
+
+
+def pair_sums(share):
+    count = lax.axis_size("rep")
+    bit = 1
+    total = share
+    while bit < count:
+        other = lax.ppermute(
+            total.astype(BF16), "rep", [(i, i ^ bit) for i in range(count)]
+        )
+        total = total.astype(F32) + other.astype(F32)
+        bit *= 2
+        if bit < count:
+            total = total.astype(BF16)
+    return total
+
+
+def whole_sample_body(
+    grid_latent,
+    mesh_latent,
+    mesh_cotangent,
+    weights,
+    g2m_pick,
+    g2m_sender,
+    g2m_receiver,
+    m2m_pick,
+    m2m_sender,
+    m2m_receiver,
+):
+    regions = lax.axis_size("space")
+    latent = weights.shape[0]
+    listed = g2m_pick.shape[1] * g2m_pick.shape[2]
+    mesh_count = mesh_latent.shape[1]
+    mesh_cap = m2m_pick.shape[2]
+    edges = g2m_sender.shape[0]
+    columns = latent // regions
+    packed = call(
+        pack_kernel,
+        (
+            grid_latent,
+            mesh_latent,
+            g2m_pick,
+            g2m_sender.reshape(1, -1),
+            g2m_receiver.reshape(1, -1),
+            m2m_pick,
+            m2m_sender.reshape(1, -1),
+            m2m_receiver.reshape(1, -1),
+        ),
+        [((listed + mesh_count + INDEX_ROWS, latent), BF16)],
+        [((INDEX_ROWS, latent), F32)],
+        10**7,
+    )[0]
+    packed, cotangent = lax.optimization_barrier((packed, mesh_cotangent))
+    packs = from_others(packed)
+    cotangents = from_others(cotangent)
+    rows = regions * mesh_count
+    (
+        mesh_out,
+        grid_all,
+        mesh_all,
+        mesh_first,
+        mesh_sent,
+        index,
+        slope_one,
+        slope_two,
+        normed_one,
+        scaled_one,
+        normed_two,
+        scaled_two,
+    ) = call(
+        functools.partial(forward_kernel, regions, listed, mesh_count, mesh_cap),
+        (*packs, weights),
+        [
+            (mesh_latent.shape, BF16),
+            ((regions * listed, latent), BF16),
+            ((rows, latent), BF16),
+            ((rows, latent), BF16),
+            ((regions * regions * mesh_cap, latent), BF16),
+            ((regions * INDEX_ROWS, latent), jnp.int32),
+            ((regions * edges, latent), BF16),
+            ((regions * edges, latent), BF16),
+            ((rows, latent), F32),
+            ((rows, 128), F32),
+            ((rows, latent), F32),
+            ((rows, 128), F32),
+        ],
+        [((regions * INDEX_ROWS, latent), BF16)],
+        2 * 10**9,
+    )
+    mesh_grad, share_two = call(
+        functools.partial(process_back_kernel, regions, mesh_cap),
+        (
+            *cotangents,
+            weights,
+            mesh_first,
+            mesh_sent,
+            index,
+            slope_two,
+            normed_two,
+            scaled_two,
+        ),
+        [((rows, latent), F32), ((columns, 2 * latent), BF16)],
+        [
+            ((rows, latent), F32),
+            ((regions * regions * mesh_cap, latent), F32),
+            ((rows, latent), BF16),
+        ],
+        10**9,
+    )
+    grid_grad, share_one = call(
+        functools.partial(encode_back_kernel, regions),
+        (
+            weights,
+            g2m_pick,
+            grid_all,
+            mesh_all,
+            index,
+            slope_one,
+            normed_one,
+            scaled_one,
+            mesh_grad,
+        ),
+        [(grid_latent.shape, BF16), ((columns, 2 * latent), BF16)],
+        [((regions * listed, latent), BF16), ((rows, latent), BF16)],
+        10**9,
+    )
+    weight_grad = jnp.concatenate([pair_sums(share_one), pair_sums(share_two)], axis=1)
+    return (mesh_out, grid_grad, weight_grad)
+
+
 def solution(mesh):
-    return jax.shard_map(
-        body,
-        mesh=mesh,
-        in_specs=(
-            P(("groups", "rep"), "space", None),
-            P(("groups", "rep"), "space", None),
-            P(("groups", "rep"), "space", None),
-            P(),
-            P("space", None, None),
-            P("space"),
-            P("space"),
-            P("space", None, None),
-            P("space"),
-            P("space"),
-        ),
-        out_specs=(
-            P(("groups", "rep"), "space", None),
-            P(("groups", "rep"), "space", None),
-            P(("groups", "space"), None),
-        ),
-        check_vma=False,
-    )
+    regions = mesh.shape["space"]
+    samples = mesh.shape["rep"]
+
+    def whole(*arguments):
+        edges = arguments[5].shape[0] + arguments[8].shape[0]
+        latent = arguments[3].shape[0]
+        fits = edges * latent * 4 <= SAMPLE_EDGE_BYTES and latent % (128 * regions) == 0
+        paired = samples & (samples - 1) == 0
+        return sharded(whole_sample_body if fits and paired else partitioned_body)(*arguments)
+
+    def sharded(body):
+        return jax.shard_map(
+            body,
+            mesh=mesh,
+            in_specs=(
+                P(("groups", "rep"), "space", None),
+                P(("groups", "rep"), "space", None),
+                P(("groups", "rep"), "space", None),
+                P(),
+                P("space", None, None),
+                P("space"),
+                P("space"),
+                P("space", None, None),
+                P("space"),
+                P("space"),
+            ),
+            out_specs=(
+                P(("groups", "rep"), "space", None),
+                P(("groups", "rep"), "space", None),
+                P(("groups", "space"), None),
+            ),
+            check_vma=False,
+        )
+
+    return whole

time: 160 us -> 54.1 us (0.34)
  waiting for transfers between devices: 77.7 us -> 22.6 us
  matrix products: 16.3 us -> 0 us
  local copies, waits for them, and re-layouts: 21.8 us -> 7.42 us
  between operations: 14.5 us -> 0.71 us
  Pallas kernels: 0 us -> 9.08 us
  other arithmetic: 10.3 us -> 1.29 us
  starting transfers between devices: 18.7 us -> 12.7 us
    unnamed x3 -> x0, waiting for transfers between devices: 42.3 us -> none
    psum x1 -> x0, waiting for transfers between devices: 24.8 us -> none  [body(): weight_grad = lax.psum(shares, 'rep').astype(jnp.float32)]
    ppermute x4 -> x10, waiting for transfers between devices: 5.15 us -> 22.6 us  [the longest x4 12.8 us: pair_sums(): lax.ppermute(total.astype(BF16), 'rep', [(i, i ^ bit) for i in range(coun...]
    dot_general x18 -> x0, matrix products: 16.3 us -> none  [the longest x4 5.49 us: body(): lax.dot_general(first_factor, second_factor, (((0,), (0,)), ((), ())), pr...]
    gather x8 -> x0, local copies, waits for them, and re-layouts: 10.5 us -> none  [the longest x4 5.45 us: edge_pass(): activation = slot_proj[located] + recv_proj[receiver]]
    all_to_all x2 -> x0, starting transfers between devices: 9.81 us -> none  [mesh_route(): lax.all_to_all(outgoing.reshape(peer_count, capacity, columns), 'space',...]
    pallas_call x0 -> x4, Pallas kernels: none -> 9.08 us  [call(): pl.pallas_call(kernel, out_shape=[jax.ShapeDtypeStruct(shape, kind) for s...]
    all_to_all x2 -> x0, waiting for transfers between devices: 5.46 us -> none  [mesh_route(): lax.all_to_all(outgoing.reshape(peer_count, capacity, columns), 'space',...]
  transfers between devices with their start and end apart: 8 -> 10, of which waited for: 5 -> 4; matrix products, arithmetic and copies ran while one was open for 10% -> 0% of each run, Pallas kernels for 0% -> 9%
where the time goes in v1:
time: 54.1 us; the launch traced here: 53.8 us
  waiting for transfers between devices  22.6 us (42%)
  starting transfers between devices  12.7 us (23%)
  Pallas kernels  9.08 us (17%)
  local copies, waits for them, and re-layouts  7.42 us (14%)
  other arithmetic  1.29 us (2%)
  between operations  0.71 us (1%)
    ppermute x4, waiting for transfers between devices, pair_sums(): lax.ppermute(total.astype(BF16), 'rep', [(i, i ^ bit) for i in range(coun...  12.8 us
    ppermute x6, starting transfers between devices, from_others(): lax.ppermute(block, 'space', [(i, (i + step) % count) for i in range(coun...  10.1 us
    ppermute x6, waiting for transfers between devices, from_others(): lax.ppermute(block, 'space', [(i, (i + step) % count) for i in range(coun...  9.82 us
    pallas_call x4, Pallas kernels, call(): pl.pallas_call(kernel, out_shape=[jax.ShapeDtypeStruct(shape, kind) for s...  9.08 us
    unnamed x21, local copies, waits for them, and re-layouts  7.42 us
    ppermute x4, starting transfers between devices, pair_sums(): lax.ppermute(total.astype(BF16), 'rep', [(i, i ^ bit) for i in range(coun...  2.67 us
  transfers between devices with their start and end apart: 10, of which 4 were waited for; matrix products, arithmetic and copies ran while one was open for 0% of the time, Pallas kernels for 9%

profile of v1, /device:TPU:0, one launch (start us, length us, event | category | flops | bytes accessed | tf_op | source)
XLA Modules:
  0.0 53.8 jit_solution(13247958679001420926)
XLA Ops:
  0.6 0.7 %copy.13.g2m_pick_ref.pick_ref = s32[1,3,16]{2,1,0:T(4,128)S(1)} copy(s32[1,3,16]{2,0,1:T(1,128)} %param.14) | data formatting | bytes 384 | tf_op args[4]
  1.3 0.9 %copy-done.2 = bf16[1,128,512]{2,1,0:T(8,128)(2,1)S(1)} copy-done((bf16[1,128,512]{2,1,0:T(8,128)(2,1)S(1)}, bf16[1,128,512]{2,1,0:T(8,128)(2,1)}, u32[]{:S(2)}) %copy-start.2) | copy-done | bytes 131096
  2.2 0.8 %copy-done.4 = bf16[1,64,512]{2,1,0:T(8,128)(2,1)S(1)} copy-done((bf16[1,64,512]{2,1,0:T(8,128)(2,1)S(1)}, bf16[1,64,512]{2,1,0:T(8,128)(2,1)}, u32[]{:S(2)}) %copy-start.4) | copy-done | bytes 65560
  3.1 0.7 %copy-done.5 = s32[1,4,8]{2,1,0:T(4,128)S(1)} copy-done((s32[1,4,8]{2,1,0:T(4,128)S(1)}, s32[1,4,8]{2,1,0:T(4,128)}, u32[]{:S(2)}) %copy-start.5) | copy-done | bytes 152
  3.7 0.7 %copy-done.6 = s32[256]{0:T(256)S(1)} copy-done((s32[256]{0:T(256)S(1)}, s32[256]{0:T(256)}, u32[]{:S(2)}) %copy-start.6) | copy-done | bytes 1048
  4.4 0.7 %copy-done.7 = s32[256]{0:T(256)S(1)} copy-done((s32[256]{0:T(256)S(1)}, s32[256]{0:T(256)}, u32[]{:S(2)}) %copy-start.7) | copy-done | bytes 1048
  5.1 0.7 %copy-done.8 = s32[256]{0:T(256)S(1)} copy-done((s32[256]{0:T(256)S(1)}, s32[256]{0:T(256)}, u32[]{:S(2)}) %copy-start.8) | copy-done | bytes 1048
  5.8 0.7 %copy-done.9 = s32[256]{0:T(256)S(1)} copy-done((s32[256]{0:T(256)S(1)}, s32[256]{0:T(256)}, u32[]{:S(2)}) %copy-start.9) | copy-done | bytes 1048
  6.5 0.2 shard_map.121.refs_0_
  6.7 5.1 %collective-permute-start.2 = (bf16[128,512]{1,0:T(8,128)(2,1)S(1)}, bf16[128,512]{1,0:T(8,128)(2,1)S(1)}, u32[]{:S(2)}, u32[]{:S(2)}) collective-permute-start(bf16[128,512]{1,0:T(8,128)(2,1)S(1)} %shard_map.121.refs_0_), channel_id=1, source_target_pairs={{0,12},{4,0},{8,4},{12,8},{1,13},{5,1},{9,5},{13,9},{2,14},{6,2},{... | collective-permute-start | bytes 393224 | tf_op jit(solution)/shard_map/ppermute | solution.py:522
  11.8 0.0 collective-permute-start.1
  11.8 1.0 %collective-permute-start = (bf16[128,512]{1,0:T(8,128)(2,1)S(1)}, bf16[128,512]{1,0:T(8,128)(2,1)S(1)}, u32[]{:S(2)}, u32[]{:S(2)}) collective-permute-start(bf16[128,512]{1,0:T(8,128)(2,1)S(1)} %shard_map.121.refs_0_), channel_id=1, source_target_pairs={{0,4},{4,8},{8,12},{12,0},{1,5},{5,9},{9,13},{13,1},{2,6},{6,10},{... | collective-permute-start | bytes 393224 | tf_op jit(solution)/shard_map/ppermute | solution.py:522
  12.8 2.8 %collective-permute-start.5 = (bf16[1,64,512]{2,1,0:T(8,128)(2,1)}, bf16[1,64,512]{2,1,0:T(8,128)(2,1)S(1)}, u32[]{:S(2)}, u32[]{:S(2)}) collective-permute-start(bf16[1,64,512]{2,1,0:T(8,128)(2,1)} %refs_0_), channel_id=1, source_target_pairs={{0,12},{4,0},{8,4},{12,8},{1,13},{5,1},{9,5},{13,9},{2,14},{6,2},{... | collective-permute-start | bytes 196616 | tf_op jit(solution)/shard_map/ppermute | solution.py:522
  15.6 1.1 %collective-permute-start.4 = (bf16[1,64,512]{2,1,0:T(8,128)(2,1)}, bf16[1,64,512]{2,1,0:T(8,128)(2,1)S(1)}, u32[]{:S(2)}, u32[]{:S(2)}) collective-permute-start(bf16[1,64,512]{2,1,0:T(8,128)(2,1)} %refs_0_), channel_id=1, source_target_pairs={{0,8},{4,12},{8,0},{12,4},{1,9},{5,13},{9,1},{13,5},{2,10},{6,14},... | collective-permute-start | bytes 196616 | tf_op jit(solution)/shard_map/ppermute | solution.py:522
  16.7 0.0 collective-permute-start.3
  16.7 9.8 %collective-permute-done.1.refs_2_ = bf16[128,512]{1,0:T(8,128)(2,1)S(1)} collective-permute-done((bf16[128,512]{1,0:T(8,128)(2,1)S(1)}, bf16[128,512]{1,0:T(8,128)(2,1)S(1)}, u32[]{:S(2)}, u32[]{:S(2)}) %collective-permute-start.1) | collective-permute-done | bytes 131104 | tf_op jit(solution)/shard_map/ppermute | solution.py:522
  26.6 1.6 %copy-done = bf16[512,2048]{1,0:T(8,128)(2,1)S(1)} copy-done((bf16[512,2048]{1,0:T(8,128)(2,1)S(1)}, bf16[512,2048]{1,0:T(8,128)(2,1)}, u32[]{:S(2)}) %copy-start) | copy-done | bytes 2097176
  28.1 4.6 %shard_map.122 = (bf16[1,64,512]{2,1,0:T(8,128)(2,1)}, bf16[192,512]{1,0:T(8,128)(2,1)S(1)}, bf16[256,512]{1,0:T(8,128)(2,1)S(1)}, bf16[256,512]{1,0:T(8,128)(2,...) custom-call(bf16[128,512]{1,0:T(8,128)(2,1)S(1)} %shard_map.121.refs, ...), custom_call_target="tpu_custom_call" | custom-call | flops 2000000000 | bytes 4194304 | tf_op jit(solution)/shard_map/pallas_call | solution.py:508
  32.8 0.0 collective-permute-done.5.refs_3_
  32.8 1.8 %shard_map.123 = (f32[256,512]{1,0:T(8,128)S(1)}, bf16[128,1024]{1,0:T(8,128)(2,1)S(1)}) custom-call(bf16[1,64,512]{2,1,0:T(8,128)(2,1)S(1)} %copy-done.3, bf16[1,64,512]{2,1,0:T(8,128)(2,1)S(1)} %collective-permute-done.3.refs_1_, bf16[1,64,512]{2,1,0:T(8,128)(2,1)S(1)} %collective-permute-done.4.refs_2_, ...), custom_call_target="tpu_custom_call" | custom-call | flops 1000000000 | bytes 4194304 | tf_op jit(solution)/shard_map/pallas_call | solution.py:508
  34.7 2.4 %shard_map.124 = (bf16[1,128,512]{2,1,0:T(8,128)(2,1)}, bf16[128,1024]{1,0:T(8,128)(2,1)S(1)}) custom-call(bf16[512,2048]{1,0:T(8,128)(2,1)S(1)} %copy-done.1, s32[1,3,16]{2,1,0:T(4,128)S(1)} %copy.13.g2m_pick_ref.pick_ref, bf16[192,512]{1,0:T(8,128)(2,1)S(1)} %get-tuple-element.23.grid_ref, bf16[256,512]{1,0:T(8,128)(2,1)S(1)} %get-tuple-element.24.mesh_ref, ...), custom_call_target="tpu_custom_call" | custom-call | flops 1000000000 | bytes 4194304 | tf_op jit(solution)/shard_map/pallas_call | solution.py:508
  37.1 0.5 collective-permute-start.8
  37.6 1.0 %collective-permute-done.6 = bf16[128,1024]{1,0:T(8,128)(2,1)S(1)} collective-permute-done((bf16[128,1024]{1,0:T(8,128)(2,1)S(1)}, bf16[128,1024]{1,0:T(8,128)(2,1)S(1)}, u32[]{:S(2)}, u32[]{:S(2)}) %collective-permute-start.6) | collective-permute-done | bytes 262176 | tf_op jit(solution)/shard_map/ppermute | solution.py:532
  38.6 0.1 add_convert_fusion.1
  38.7 1.6 %collective-permute-start.7 = (bf16[128,1024]{1,0:T(8,128)(2,1)S(1)}, bf16[128,1024]{1,0:T(8,128)(2,1)S(1)}, u32[]{:S(2)}, u32[]{:S(2)}) collective-permute-start(bf16[128,1024]{1,0:T(8,128)(2,1)S(1)} %add_convert_fusion.1), channel_id=1, source_target_pairs={{0,2},{1,3},{2,0},{3,1},{4,6},{5,7},{6,4},{7,5},{8,10},{9,11},{10,... | collective-permute-start | bytes 786440 | tf_op jit(solution)/shard_map/ppermute | solution.py:532
  40.2 0.1 add_convert_fusion
  40.3 0.6 %collective-permute-start.9 = (bf16[128,1024]{1,0:T(8,128)(2,1)S(1)}, bf16[128,1024]{1,0:T(8,128)(2,1)S(1)}, u32[]{:S(2)}, u32[]{:S(2)}) collective-permute-start(bf16[128,1024]{1,0:T(8,128)(2,1)S(1)} %add_convert_fusion), channel_id=1, source_target_pairs={{0,2},{1,3},{2,0},{3,1},{4,6},{5,7},{6,4},{7,5},{8,10},{9,11},{10,... | collective-permute-start | bytes 786440 | tf_op jit(solution)/shard_map/ppermute | solution.py:532
  40.9 7.0 %collective-permute-done.7 = bf16[128,1024]{1,0:T(8,128)(2,1)S(1)} collective-permute-done((bf16[128,1024]{1,0:T(8,128)(2,1)S(1)}, bf16[128,1024]{1,0:T(8,128)(2,1)S(1)}, u32[]{:S(2)}, u32[]{:S(2)}) %collective-permute-start.7) | collective-permute-done | bytes 262176 | tf_op jit(solution)/shard_map/ppermute | solution.py:532
  47.9 0.1 convert_add_fusion.1
  47.9 4.7 %collective-permute-done.9 = bf16[128,1024]{1,0:T(8,128)(2,1)S(1)} collective-permute-done((bf16[128,1024]{1,0:T(8,128)(2,1)S(1)}, bf16[128,1024]{1,0:T(8,128)(2,1)S(1)}, u32[]{:S(2)}, u32[]{:S(2)}) %collective-permute-start.9) | collective-permute-done | bytes 262176 | tf_op jit(solution)/shard_map/ppermute | solution.py:532
  52.7 0.1 convert_add_fusion
  52.8 1.0 %pad_maximum_fusion = f32[128,2048]{1,0:T(8,128)} fusion(f32[128,1024]{1,0:T(8,128)S(1)} %convert_add_fusion, f32[128,1024]{1,0:T(8,128)S(1)} %convert_add_fusion.1), kind=kLoop, calls=%fused_computation | loop fusion | flops 262144 | bytes 2097152 | tf_op jit(solution)/shard_map/concatenate | solution.py:651
  (18 shorter events, 0.0 us)
Async XLA Ops:
  1.3 0.9 %copy-start.2 = (bf16[1,128,512]{2,1,0:T(8,128)(2,1)S(1)}, bf16[1,128,512]{2,1,0:T(8,128)(2,1)}, u32[]{:S(2)}) copy-start(bf16[1,128,512]{2,1,0:T(8,128)(2,1)} %grid_ref.1) | copy-start | bytes 393220
  2.2 0.8 %copy-start.4 = (bf16[1,64,512]{2,1,0:T(8,128)(2,1)S(1)}, bf16[1,64,512]{2,1,0:T(8,128)(2,1)}, u32[]{:S(2)}) copy-start(bf16[1,64,512]{2,1,0:T(8,128)(2,1)} %mesh_ref.1) | copy-start | bytes 196612
  3.1 0.7 %copy-start.5 = (s32[1,4,8]{2,1,0:T(4,128)S(1)}, s32[1,4,8]{2,1,0:T(4,128)}, u32[]{:S(2)}) copy-start(s32[1,4,8]{2,1,0:T(4,128)} %m2m_pick_ref.1) | copy-start | bytes 388
  3.7 0.7 %copy-start.6 = (s32[256]{0:T(256)S(1)}, s32[256]{0:T(256)}, u32[]{:S(2)}) copy-start(s32[256]{0:T(256)} %param.15) | copy-start | bytes 3076
  4.4 0.7 %copy-start.7 = (s32[256]{0:T(256)S(1)}, s32[256]{0:T(256)}, u32[]{:S(2)}) copy-start(s32[256]{0:T(256)} %param.16) | copy-start | bytes 3076
  5.1 0.7 %copy-start.8 = (s32[256]{0:T(256)S(1)}, s32[256]{0:T(256)}, u32[]{:S(2)}) copy-start(s32[256]{0:T(256)} %param.18) | copy-start | bytes 3076
  5.8 0.7 %copy-start.9 = (s32[256]{0:T(256)S(1)}, s32[256]{0:T(256)}, u32[]{:S(2)}) copy-start(s32[256]{0:T(256)} %param.19) | copy-start | bytes 3076
  6.5 26.3 %copy-start.3 = (bf16[1,64,512]{2,1,0:T(8,128)(2,1)S(1)}, bf16[1,64,512]{2,1,0:T(8,128)(2,1)}, u32[]{:S(2)}) copy-start(bf16[1,64,512]{2,1,0:T(8,128)(2,1)} %refs_0_) | copy-start | bytes 196612
  6.7 10.1 %collective-permute-start.2 = (bf16[128,512]{1,0:T(8,128)(2,1)S(1)}, bf16[128,512]{1,0:T(8,128)(2,1)S(1)}, u32[]{:S(2)}, u32[]{:S(2)}) collective-permute-start(bf16[128,512]{1,0:T(8,128)(2,1)S(1)} %shard_map.121.refs_0_), channel_id=1, source_target_pairs={{0,12},{4,0},{8,4},{12,8},{1,13},{5,1},{9,5},{13,9},{2,14},{6,2},{... | collective-permute-start | bytes 393224 | tf_op jit(solution)/shard_map/ppermute | solution.py:522
  11.8 14.8 %collective-permute-start.1 = (bf16[128,512]{1,0:T(8,128)(2,1)S(1)}, bf16[128,512]{1,0:T(8,128)(2,1)S(1)}, u32[]{:S(2)}, u32[]{:S(2)}) collective-permute-start(bf16[128,512]{1,0:T(8,128)(2,1)S(1)} %shard_map.121.refs_0_), channel_id=1, source_target_pairs={{0,8},{4,12},{8,0},{12,4},{1,9},{5,13},{9,1},{13,5},{2,10},{6,14},... | collective-permute-start | bytes 393224 | tf_op jit(solution)/shard_map/ppermute | solution.py:522
  11.8 14.8 %collective-permute-start = (bf16[128,512]{1,0:T(8,128)(2,1)S(1)}, bf16[128,512]{1,0:T(8,128)(2,1)S(1)}, u32[]{:S(2)}, u32[]{:S(2)}) collective-permute-start(bf16[128,512]{1,0:T(8,128)(2,1)S(1)} %shard_map.121.refs_0_), channel_id=1, source_target_pairs={{0,4},{4,8},{8,12},{12,0},{1,5},{5,9},{9,13},{13,1},{2,6},{6,10},{... | collective-permute-start | bytes 393224 | tf_op jit(solution)/shard_map/ppermute | solution.py:522
  12.8 20.0 %collective-permute-start.5 = (bf16[1,64,512]{2,1,0:T(8,128)(2,1)}, bf16[1,64,512]{2,1,0:T(8,128)(2,1)S(1)}, u32[]{:S(2)}, u32[]{:S(2)}) collective-permute-start(bf16[1,64,512]{2,1,0:T(8,128)(2,1)} %refs_0_), channel_id=1, source_target_pairs={{0,12},{4,0},{8,4},{12,8},{1,13},{5,1},{9,5},{13,9},{2,14},{6,2},{... | collective-permute-start | bytes 196616 | tf_op jit(solution)/shard_map/ppermute | solution.py:522
  15.6 17.2 %collective-permute-start.4 = (bf16[1,64,512]{2,1,0:T(8,128)(2,1)}, bf16[1,64,512]{2,1,0:T(8,128)(2,1)S(1)}, u32[]{:S(2)}, u32[]{:S(2)}) collective-permute-start(bf16[1,64,512]{2,1,0:T(8,128)(2,1)} %refs_0_), channel_id=1, source_target_pairs={{0,8},{4,12},{8,0},{12,4},{1,9},{5,13},{9,1},{13,5},{2,10},{6,14},... | collective-permute-start | bytes 196616 | tf_op jit(solution)/shard_map/ppermute | solution.py:522
  16.7 16.1 %collective-permute-start.3 = (bf16[1,64,512]{2,1,0:T(8,128)(2,1)}, bf16[1,64,512]{2,1,0:T(8,128)(2,1)S(1)}, u32[]{:S(2)}, u32[]{:S(2)}) collective-permute-start(bf16[1,64,512]{2,1,0:T(8,128)(2,1)} %refs_0_), channel_id=1, source_target_pairs={{0,4},{4,8},{8,12},{12,0},{1,5},{5,9},{9,13},{13,1},{2,6},{6,10},{... | collective-permute-start | bytes 196616 | tf_op jit(solution)/shard_map/ppermute | solution.py:522
  26.6 1.6 %copy-start = (bf16[512,2048]{1,0:T(8,128)(2,1)S(1)}, bf16[512,2048]{1,0:T(8,128)(2,1)}, u32[]{:S(2)}) copy-start(bf16[512,2048]{1,0:T(8,128)(2,1)} %weights_ref.1) | copy-start | bytes 6291460
  28.1 4.7 %copy-start.1 = (bf16[512,2048]{1,0:T(8,128)(2,1)S(1)}, bf16[512,2048]{1,0:T(8,128)(2,1)}, u32[]{:S(2)}) copy-start(bf16[512,2048]{1,0:T(8,128)(2,1)} %weights_ref.1) | copy-start | bytes 6291460
  37.1 1.5 %collective-permute-start.6 = (bf16[128,1024]{1,0:T(8,128)(2,1)S(1)}, bf16[128,1024]{1,0:T(8,128)(2,1)S(1)}, u32[]{:S(2)}, u32[]{:S(2)}) collective-permute-start(bf16[128,1024]{1,0:T(8,128)(2,1)S(1)} %get-tuple-element.37), channel_id=1, source_target_pairs={{0,1},{1,0},{2,3},{3,2},{4,5},{5,4},{6,7},{7,6},{8,9},{9,8},{10,11... | collective-permute-start | bytes 786440 | tf_op jit(solution)/shard_map/ppermute | solution.py:532
  37.1 3.2 %collective-permute-start.8 = (bf16[128,1024]{1,0:T(8,128)(2,1)S(1)}, bf16[128,1024]{1,0:T(8,128)(2,1)S(1)}, u32[]{:S(2)}, u32[]{:S(2)}) collective-permute-start(bf16[128,1024]{1,0:T(8,128)(2,1)S(1)} %get-tuple-element.38), channel_id=1, source_target_pairs={{0,1},{1,0},{2,3},{3,2},{4,5},{5,4},{6,7},{7,6},{8,9},{9,8},{10,11... | collective-permute-start | bytes 786440 | tf_op jit(solution)/shard_map/ppermute | solution.py:532
  38.7 9.2 %collective-permute-start.7 = (bf16[128,1024]{1,0:T(8,128)(2,1)S(1)}, bf16[128,1024]{1,0:T(8,128)(2,1)S(1)}, u32[]{:S(2)}, u32[]{:S(2)}) collective-permute-start(bf16[128,1024]{1,0:T(8,128)(2,1)S(1)} %add_convert_fusion.1), channel_id=1, source_target_pairs={{0,2},{1,3},{2,0},{3,1},{4,6},{5,7},{6,4},{7,5},{8,10},{9,11},{10,... | collective-permute-start | bytes 786440 | tf_op jit(solution)/shard_map/ppermute | solution.py:532
  40.3 12.4 %collective-permute-start.9 = (bf16[128,1024]{1,0:T(8,128)(2,1)S(1)}, bf16[128,1024]{1,0:T(8,128)(2,1)S(1)}, u32[]{:S(2)}, u32[]{:S(2)}) collective-permute-start(bf16[128,1024]{1,0:T(8,128)(2,1)S(1)} %add_convert_fusion), channel_id=1, source_target_pairs={{0,2},{1,3},{2,0},{3,1},{4,6},{5,7},{6,4},{7,5},{8,10},{9,11},{10,... | collective-permute-start | bytes 786440 | tf_op jit(solution)/shard_map/ppermute | solution.py:532

commit v2 on v1

--- a/solution.py
+++ b/solution.py
@@ -211,10 +211,6 @@
     return lax.dot_general(left, right, (((0,), (0,)), ((), ())), preferred_element_type=F32)
 
 
-def dot_last(left, right):
-    return lax.dot_general(left, right, (((1,), (1,)), ((), ())), preferred_element_type=F32)
-
-
 def one_hot(labels, count):
     rows = lax.broadcasted_iota(jnp.int32, (count, labels.shape[-1]), 0)
     return (rows == labels).astype(F32).astype(BF16)
@@ -233,25 +229,38 @@
     )
 
 
-def pack_kernel(
-    grid_ref,
-    mesh_ref,
-    g2m_pick_ref,
-    g2m_sender_ref,
-    g2m_receiver_ref,
-    m2m_pick_ref,
-    m2m_sender_ref,
-    m2m_receiver_ref,
-    packed_ref,
-    index_ref,
-):
-    lists, capacity = g2m_pick_ref.shape[1:]
+def fetch(pairs, semaphores):
+    copies = [
+        pltpu.make_async_copy(source, target, semaphores.at[n])
+        for n, (source, target) in enumerate(pairs)
+    ]
+    for copy in copies:
+        copy.start()
+    for copy in copies:
+        copy.wait()
+
+
+def pack_kernel(*refs):
+    sources, packed_ref, index_ref = refs[:8], refs[8], refs[9]
+    local, semaphores = refs[10:18], refs[18]
+    fetch(list(zip(sources, local)), semaphores)
+    (
+        grid_ref,
+        mesh_ref,
+        g2m_pick_ref,
+        g2m_sender_ref,
+        g2m_receiver_ref,
+        m2m_pick_ref,
+        m2m_sender_ref,
+        m2m_receiver_ref,
+    ) = local
+    lists, _, capacity = g2m_pick_ref.shape
     mesh_count = mesh_ref.shape[1]
     regions, mesh_cap = m2m_pick_ref.shape[1:]
     edges = g2m_sender_ref.shape[1]
     grid_rows = grid_ref[0]
     for i in range(lists):
-        picked = one_hot(g2m_pick_ref[0, i : i + 1, :], grid_rows.shape[0])
+        picked = one_hot(g2m_pick_ref[i], grid_rows.shape[0])
         packed_ref[i * capacity : (i + 1) * capacity, :] = dot_first(picked, grid_rows).astype(BF16)
     first = lists * capacity
     packed_ref[first : first + mesh_count, :] = mesh_ref[0]
@@ -268,6 +277,15 @@
     owned = lane // mesh_cap == lax.broadcasted_iota(jnp.int32, (regions, slots), 0)
     index_ref[2:3, 0:slots] = jnp.sum(jnp.where(owned, spread, 0.0), 0, keepdims=True)
     packed_ref[first + mesh_count :, :] = index_ref[...].astype(BF16)
+
+
+def weights_kernel(source_ref, weights_ref, turned_ref, semaphores):
+    fetch([(source_ref, weights_ref)], semaphores)
+    latent = weights_ref.shape[0]
+    for n, block in enumerate((0, 2, 3)):
+        turned_ref[:, n * latent : (n + 1) * latent] = weights_ref[
+            :, block * latent : (block + 1) * latent
+        ].T
 
 
 def edge_forward(table, hot, hot_receiver, slope_ref, first):
@@ -310,7 +328,7 @@
     slots = regions * mesh_cap
     me = lax.axis_index("space")
     for back, packed_ref in enumerate(packed_refs):
-        region = lax.rem(me + (regions - back), regions)
+        region = lax.bitwise_xor(me, back)
         at = lambda rows: pl.ds(pl.multiple_of(region * rows, rows), rows)
         grid_ref[at(listed), :] = packed_ref[:listed, :]
         mesh_ref[at(mesh_count), :] = packed_ref[listed : listed + mesh_count, :]
@@ -390,10 +408,17 @@
     return dot(hot, edge_grad)
 
 
+def halve(share_ref, keep_ref, give_ref):
+    half = keep_ref.shape[0]
+    core = lax.bitwise_and(lax.axis_index("rep"), 1)
+    keep_ref[...] = share_ref[pl.ds(pl.multiple_of(core * half, half), half), :]
+    give_ref[...] = share_ref[pl.ds(pl.multiple_of((1 - core) * half, half), half), :]
+
+
 def process_back_kernel(regions, mesh_cap, *refs):
     cotangent_refs = refs[:regions]
     (
-        weights_ref,
+        turned_ref,
         first_ref,
         sent_ref,
         index_ref,
@@ -401,10 +426,12 @@
         normed_ref,
         scaled_ref,
         mesh_grad_ref,
-        share_ref,
+        keep_ref,
+        give_ref,
         upstream_ref,
         slot_ref,
         recv_ref,
+        share_ref,
     ) = refs[regions:]
     latent = first_ref.shape[1]
     mesh_count = first_ref.shape[0] // regions
@@ -412,7 +439,7 @@
     slots = regions * mesh_cap
     me = lax.axis_index("space")
     for back, cotangent_ref in enumerate(cotangent_refs):
-        region = lax.rem(me + (regions - back), regions)
+        region = lax.bitwise_xor(me, back)
         at = pl.ds(pl.multiple_of(region * mesh_count, mesh_count), mesh_count)
         upstream_ref[at, :] = cotangent_ref[0].astype(F32)
     agg_grad = moments_back(normed_ref[...], scaled_ref[:, 0:1], upstream_ref[...]).astype(BF16)
@@ -436,8 +463,9 @@
     mine = pl.ds(pl.multiple_of(me * columns, columns), columns)
     share_ref[:, :latent] = dot_first(sent_ref[:, mine], slot_sum).astype(BF16)
     share_ref[:, latent:] = dot_first(first_ref[:, mine], recv_ref[...]).astype(BF16)
-    returned = dot_last(slot_sum, weights_ref[:, 2 * latent : 3 * latent]).astype(BF16)
-    grad = upstream_ref[...] + dot_last(recv_ref[...], weights_ref[:, 3 * latent :])
+    halve(share_ref, keep_ref, give_ref)
+    returned = dot(slot_sum, turned_ref[:, latent : 2 * latent]).astype(BF16)
+    grad = upstream_ref[...] + dot(recv_ref[...], turned_ref[:, 2 * latent :])
     for s in range(regions):
         hot = one_hot(index_ref[s * INDEX_ROWS + 2 : s * INDEX_ROWS + 3, :slots], mesh_count)
         rows = slice(s * mesh_count, (s + 1) * mesh_count)
@@ -446,8 +474,6 @@
 
 def encode_back_kernel(
     regions,
-    weights_ref,
-    pick_ref,
     grid_ref,
     mesh_ref,
     index_ref,
@@ -455,10 +481,12 @@
     normed_ref,
     scaled_ref,
     mesh_grad_ref,
-    grid_grad_ref,
-    share_ref,
+    own_slot_ref,
+    keep_ref,
+    give_ref,
     slot_ref,
     recv_ref,
+    share_ref,
 ):
     latent = mesh_ref.shape[1]
     mesh_count = mesh_ref.shape[0] // regions
@@ -491,52 +519,66 @@
     mine = pl.ds(pl.multiple_of(me * columns, columns), columns)
     share_ref[:, :latent] = dot_first(grid_ref[:, mine], slot_ref[...]).astype(BF16)
     share_ref[:, latent:] = dot_first(mesh_ref[:, mine], recv_ref[...]).astype(BF16)
+    halve(share_ref, keep_ref, give_ref)
     own = pl.ds(pl.multiple_of(me * listed, listed), listed)
-    returned = dot_last(slot_ref[own, :], weights_ref[:, :latent]).astype(BF16)
+    own_slot_ref[...] = slot_ref[own, :]
+
+
+def grid_back_kernel(turned_ref, pick_ref, own_slot_ref, grid_grad_ref):
+    lists, _, capacity = pick_ref.shape
+    latent = own_slot_ref.shape[1]
+    returned = dot(own_slot_ref[...], turned_ref[:, :latent]).astype(BF16)
     total = None
-    for i in range(3):
-        owner = one_hot(pick_ref[0, i : i + 1, :], grid_grad_ref.shape[1])
+    for i in range(lists):
+        owner = one_hot(pick_ref[i], grid_grad_ref.shape[1])
         part = dot(owner, returned[i * capacity : (i + 1) * capacity])
         total = part if total is None else total + part
     grid_grad_ref[0] = total.astype(BF16)
 
 
+def finish_kernel(one_ref, other_one_ref, two_ref, other_two_ref, weight_grad_ref):
+    half, width = one_ref.shape
+    core = lax.bitwise_and(lax.axis_index("rep"), 1)
+    mine = pl.ds(pl.multiple_of(core * half, half), half)
+    other = pl.ds(pl.multiple_of((1 - core) * half, half), half)
+    weight_grad_ref[mine, :width] = one_ref[...].astype(F32)
+    weight_grad_ref[other, :width] = other_one_ref[...].astype(F32)
+    weight_grad_ref[mine, width:] = two_ref[...].astype(F32)
+    weight_grad_ref[other, width:] = other_two_ref[...].astype(F32)
+
+
 VMEM = pl.BlockSpec(memory_space=pltpu.VMEM)
 
 
-def call(kernel, operands, outputs, scratch, flops):
+def call(kernel, operands, outputs, scratch, flops, fetched=0, megabytes=40):
+    hbm = pl.BlockSpec(memory_space=pltpu.HBM)
     return pl.pallas_call(
         kernel,
         out_shape=[jax.ShapeDtypeStruct(shape, kind) for shape, kind in outputs],
-        in_specs=[VMEM] * len(operands),
+        in_specs=[hbm] * fetched + [VMEM] * (len(operands) - fetched),
         out_specs=[VMEM] * len(outputs),
-        scratch_shapes=[pltpu.VMEM(shape, kind) for shape, kind in scratch],
-        compiler_params=pltpu.CompilerParams(vmem_limit_bytes=40 << 20),
+        scratch_shapes=[pltpu.VMEM(shape, kind) for shape, kind in scratch]
+        + ([pltpu.SemaphoreType.DMA((fetched,))] if fetched else []),
+        compiler_params=pltpu.CompilerParams(vmem_limit_bytes=megabytes << 20),
         cost_estimate=pl.CostEstimate(flops=flops, bytes_accessed=4 << 20, transcendentals=0),
     )(*operands)
 
 
-def from_others(block):
-    count = lax.axis_size("space")
-    return [block] + [
-        lax.ppermute(block, "space", [(i, (i + step) % count) for i in range(count)])
-        for step in range(1, count)
-    ]
-
-
-def pair_sums(share):
-    count = lax.axis_size("rep")
-    bit = 1
-    total = share
-    while bit < count:
-        other = lax.ppermute(
-            total.astype(BF16), "rep", [(i, i ^ bit) for i in range(count)]
-        )
-        total = total.astype(F32) + other.astype(F32)
+def swap(block, axis, bits):
+    return lax.ppermute(block, axis, [(i, i ^ bits) for i in range(lax.axis_size(axis))])
+
+
+def added(left, right):
+    return (left.astype(F32) + right.astype(F32)).astype(BF16)
+
+
+def summed_half(keep, give):
+    half = added(keep, swap(give, "rep", 1))
+    bit = 2
+    while bit < lax.axis_size("rep"):
+        half = added(half, swap(half, "rep", bit))
         bit *= 2
-        if bit < count:
-            total = total.astype(BF16)
-    return total
+    return half, swap(half, "rep", 1)
 
 
 def whole_sample_body(
@@ -558,25 +600,46 @@
     mesh_cap = m2m_pick.shape[2]
     edges = g2m_sender.shape[0]
     columns = latent // regions
+    half = columns // 2
+    g2m_pick = g2m_pick.transpose(1, 0, 2)
+    sources = (
+        grid_latent,
+        mesh_latent,
+        g2m_pick,
+        g2m_sender.reshape(1, -1),
+        g2m_receiver.reshape(1, -1),
+        m2m_pick,
+        m2m_sender.reshape(1, -1),
+        m2m_receiver.reshape(1, -1),
+    )
     packed = call(
         pack_kernel,
-        (
-            grid_latent,
-            mesh_latent,
-            g2m_pick,
-            g2m_sender.reshape(1, -1),
-            g2m_receiver.reshape(1, -1),
-            m2m_pick,
-            m2m_sender.reshape(1, -1),
-            m2m_receiver.reshape(1, -1),
-        ),
+        sources,
         [((listed + mesh_count + INDEX_ROWS, latent), BF16)],
-        [((INDEX_ROWS, latent), F32)],
+        [((INDEX_ROWS, latent), F32)] + [(source.shape, source.dtype) for source in sources],
         10**7,
+        fetched=len(sources),
+        megabytes=56,
     )[0]
-    packed, cotangent = lax.optimization_barrier((packed, mesh_cotangent))
-    packs = from_others(packed)
-    cotangents = from_others(cotangent)
+    packed, cotangent, weights = lax.optimization_barrier((packed, mesh_cotangent, weights))
+    steps = sorted(range(1, regions), key=lambda step: -step)
+    packs = {step: swap(packed, "space", step) for step in steps}
+    cotangents = {1: swap(cotangent, "space", 1)}
+    weights, turned = call(
+        weights_kernel,
+        (weights,),
+        [(weights.shape, BF16), ((latent, 3 * latent), BF16)],
+        [],
+        10**8,
+        fetched=1,
+    )
+    *packs, cotangent = lax.optimization_barrier(
+        [packed] + [packs[step] for step in range(1, regions)] + [cotangent]
+    )
+    for step in steps:
+        if step > 1:
+            cotangents[step] = swap(cotangent, "space", step)
+    cotangents = [cotangent] + [cotangents[step] for step in range(1, regions)]
     rows = regions * mesh_count
     (
         mesh_out,
@@ -611,11 +674,11 @@
         [((regions * INDEX_ROWS, latent), BF16)],
         2 * 10**9,
     )
-    mesh_grad, share_two = call(
+    mesh_grad, keep_two, give_two = call(
         functools.partial(process_back_kernel, regions, mesh_cap),
         (
             *cotangents,
-            weights,
+            turned,
             mesh_first,
             mesh_sent,
             index,
@@ -623,19 +686,18 @@
             normed_two,
             scaled_two,
         ),
-        [((rows, latent), F32), ((columns, 2 * latent), BF16)],
+        [((rows, latent), F32)] + [((half, 2 * latent), BF16)] * 2,
         [
             ((rows, latent), F32),
             ((regions * regions * mesh_cap, latent), F32),
             ((rows, latent), BF16),
+            ((columns, 2 * latent), BF16),
         ],
         10**9,
     )
-    grid_grad, share_one = call(
+    own_slots, keep_one, give_one = call(
         functools.partial(encode_back_kernel, regions),
         (
-            weights,
-            g2m_pick,
             grid_all,
             mesh_all,
             index,
@@ -644,11 +706,28 @@
             scaled_one,
             mesh_grad,
         ),
-        [(grid_latent.shape, BF16), ((columns, 2 * latent), BF16)],
-        [((regions * listed, latent), BF16), ((rows, latent), BF16)],
+        [((listed, latent), BF16)] + [((half, 2 * latent), BF16)] * 2,
+        [
+            ((regions * listed, latent), BF16),
+            ((rows, latent), BF16),
+            ((columns, 2 * latent), BF16),
+        ],
         10**9,
     )
-    weight_grad = jnp.concatenate([pair_sums(share_one), pair_sums(share_two)], axis=1)
+    grid_grad = call(
+        grid_back_kernel,
+        (turned, g2m_pick, own_slots),
+        [(grid_latent.shape, BF16)],
+        [],
+        10**8,
+    )[0]
+    weight_grad = call(
+        finish_kernel,
+        (*summed_half(keep_one, give_one), *summed_half(keep_two, give_two)),
+        [((columns, 4 * latent), F32)],
+        [],
+        10**6,
+    )[0]
     return (mesh_out, grid_grad, weight_grad)
 
 
@@ -660,7 +739,7 @@
         edges = arguments[5].shape[0] + arguments[8].shape[0]
         latent = arguments[3].shape[0]
         fits = edges * latent * 4 <= SAMPLE_EDGE_BYTES and latent % (128 * regions) == 0
-        paired = samples & (samples - 1) == 0
+        paired = all(n > 1 and n & (n - 1) == 0 for n in (regions, samples))
         return sharded(whole_sample_body if fits and paired else partitioned_body)(*arguments)
 
     def sharded(body):

time: 54.1 us -> 42.8 us (0.79)
  waiting for transfers between devices: 22.6 us -> 13.6 us
  local copies, waits for them, and re-layouts: 7.42 us -> 1.61 us
  Pallas kernels: 9.08 us -> 12.4 us
  starting transfers between devices: 12.7 us -> 14.2 us
  other arithmetic: 1.29 us -> 0.14 us
    ppermute x10 -> x12, waiting for transfers between devices: 22.6 us -> 13.6 us  [swap(): lax.ppermute(block, axis, [(i, i ^ bits) for i in range(lax.axis_size(axi...]
    unnamed x21 -> x8, local copies, waits for them, and re-layouts: 7.42 us -> 1.61 us
    pallas_call x4 -> x7, Pallas kernels: 9.08 us -> 12.4 us  [call(): pl.pallas_call(kernel, out_shape=[jax.ShapeDtypeStruct(shape, kind) for s...]
    ppermute x10 -> x12, starting transfers between devices: 12.7 us -> 14.2 us  [swap(): lax.ppermute(block, axis, [(i, i ^ bits) for i in range(lax.axis_size(axi...]
    concatenate x1 -> x0, other arithmetic: 1.04 us -> none  [whole_sample_body(): jnp.concatenate([pair_sums(share_one), pair_sums(share_two)], axis=1)]
  transfers between devices with their start and end apart: 10 -> 12, of which waited for: 4 -> 5; matrix products, arithmetic and copies ran while one was open for 0% -> 0% of each run, Pallas kernels for 9% -> 18%
where the time goes in v2:
time: 42.8 us; the launch traced here: 42.7 us
  starting transfers between devices  14.2 us (33%)
  waiting for transfers between devices  13.6 us (32%)
  Pallas kernels  12.4 us (29%)
  local copies, waits for them, and re-layouts  1.61 us (4%)
  between operations  0.75 us (2%)
    ppermute x12, starting transfers between devices, swap(): lax.ppermute(block, axis, [(i, i ^ bits) for i in range(lax.axis_size(axi...  14.2 us
    ppermute x12, waiting for transfers between devices, swap(): lax.ppermute(block, axis, [(i, i ^ bits) for i in range(lax.axis_size(axi...  13.6 us
    pallas_call x7, Pallas kernels, call(): pl.pallas_call(kernel, out_shape=[jax.ShapeDtypeStruct(shape, kind) for s...  12.4 us
    unnamed x8, local copies, waits for them, and re-layouts  1.61 us
  transfers between devices with their start and end apart: 12, of which 5 were waited for; matrix products, arithmetic and copies ran while one was open for 0% of the time, Pallas kernels for 18%

profile of v2, /device:TPU:0, one launch (start us, length us, event | category | flops | bytes accessed | tf_op | source)
XLA Modules:
  0.0 42.7 jit_solution(3090404047386847922)
XLA Ops:
  0.6 0.0 copy-start.2
  0.6 1.9 %shard_map.121.refs_0_ = bf16[128,512]{1,0:T(8,128)(2,1)} custom-call(bf16[1,128,512]{2,1,0:T(8,128)(2,1)} %refs_0_.1, bf16[1,64,512]{2,1,0:T(8,128)(2,1)} %refs_1_.1, s32[3,1,16]{2,1,0:T(1,128)} %bitcast.5, s32[1,256]{1,0:T(1,128)} %bitcast.7, s32[1,256]{1,0:T(1,128)} %bitcast.8, s32[1,4,8]{2,1,0:T(4,128)} %refs_5_.1, s32[1,256]{1,0:T(1,128)} %bitcast.9, ...), custom_call_target="tpu_custom_call" | custom-call | flops 10000000 | bytes 4194304 | tf_op jit(solution)/shard_map/pallas_call | solution.py:555
  2.6 3.1 %collective-permute-start = (bf16[128,512]{1,0:T(8,128)(2,1)}, bf16[128,512]{1,0:T(8,128)(2,1)S(1)}, u32[]{:S(2)}, u32[]{:S(2)}) collective-permute-start(bf16[128,512]{1,0:T(8,128)(2,1)} %shard_map.121.refs_0_), channel_id=1, source_target_pairs={{0,4},{4,0},{8,12},{12,8},{1,5},{5,1},{9,13},{13,9},{2,6},{6,2},{1... | collective-permute-start | bytes 393224 | tf_op jit(solution)/shard_map/ppermute | solution.py:568
  5.6 2.6 %collective-permute-start.1 = (bf16[128,512]{1,0:T(8,128)(2,1)}, bf16[128,512]{1,0:T(8,128)(2,1)S(1)}, u32[]{:S(2)}, u32[]{:S(2)}) collective-permute-start(bf16[128,512]{1,0:T(8,128)(2,1)} %shard_map.121.refs_0_), channel_id=1, source_target_pairs={{0,8},{4,12},{8,0},{12,4},{1,9},{5,13},{9,1},{13,5},{2,10},{6,14},... | collective-permute-start | bytes 393224 | tf_op jit(solution)/shard_map/ppermute | solution.py:568
  8.2 0.0 collective-permute-start.2
  8.2 0.9 %collective-permute-start.3 = (bf16[1,64,512]{2,1,0:T(8,128)(2,1)}, bf16[1,64,512]{2,1,0:T(8,128)(2,1)S(1)}, u32[]{:S(2)}, u32[]{:S(2)}) collective-permute-start(bf16[1,64,512]{2,1,0:T(8,128)(2,1)} %refs_0_.2), channel_id=1, source_target_pairs={{0,4},{4,0},{8,12},{12,8},{1,5},{5,1},{9,13},{13,9},{2,6},{6,2},{1... | collective-permute-start | bytes 196616 | tf_op jit(solution)/shard_map/ppermute | solution.py:568
  9.1 1.6 %copy-done = bf16[512,2048]{1,0:T(8,128)(2,1)S(1)} copy-done((bf16[512,2048]{1,0:T(8,128)(2,1)S(1)}, bf16[512,2048]{1,0:T(8,128)(2,1)}, u32[]{:S(2)}) %copy-start) | copy-done | bytes 2097176
  10.7 0.6 %shard_map.122 = (bf16[512,2048]{1,0:T(8,128)(2,1)S(1)}, bf16[512,1536]{1,0:T(8,128)(2,1)S(1)}) custom-call(bf16[512,2048]{1,0:T(8,128)(2,1)S(1)} %copy-done), custom_call_target="tpu_custom_call" | custom-call | flops 100000000 | bytes 4194304 | tf_op jit(solution)/shard_map/pallas_call | solution.py:555
  11.3 0.0 collective-permute-done.refs_1_
  11.4 7.4 %collective-permute-done.1.refs_2_ = bf16[128,512]{1,0:T(8,128)(2,1)S(1)} collective-permute-done((bf16[128,512]{1,0:T(8,128)(2,1)}, bf16[128,512]{1,0:T(8,128)(2,1)S(1)}, u32[]{:S(2)}, u32[]{:S(2)}) %collective-permute-start.1) | collective-permute-done | bytes 131104 | tf_op jit(solution)/shard_map/ppermute | solution.py:568
  18.8 0.0 collective-permute-done.2.refs_3_
  18.8 3.2 %collective-permute-start.4 = (bf16[1,64,512]{2,1,0:T(8,128)(2,1)S(1)}, bf16[1,64,512]{2,1,0:T(8,128)(2,1)S(1)}, u32[]{:S(2)}, u32[]{:S(2)}) collective-permute-start(bf16[1,64,512]{2,1,0:T(8,128)(2,1)S(1)} %copy-done.2), channel_id=1, source_target_pairs={{0,8},{4,12},{8,0},{12,4},{1,9},{5,13},{9,1},{13,5},{2,10},{6,14},... | collective-permute-start | bytes 196616 | tf_op jit(solution)/shard_map/ppermute | solution.py:568
  22.0 1.1 %collective-permute-start.5 = (bf16[1,64,512]{2,1,0:T(8,128)(2,1)S(1)}, bf16[1,64,512]{2,1,0:T(8,128)(2,1)S(1)}, u32[]{:S(2)}, u32[]{:S(2)}) collective-permute-start(bf16[1,64,512]{2,1,0:T(8,128)(2,1)S(1)} %copy-done.2), channel_id=1, source_target_pairs={{0,12},{4,8},{8,4},{12,0},{1,13},{5,9},{9,5},{13,1},{2,14},{6,10},... | collective-permute-start | bytes 196616 | tf_op jit(solution)/shard_map/ppermute | solution.py:568
  23.1 4.6 %shard_map.123 = (bf16[1,64,512]{2,1,0:T(8,128)(2,1)}, bf16[192,512]{1,0:T(8,128)(2,1)S(1)}, bf16[256,512]{1,0:T(8,128)(2,1)S(1)}, bf16[256,512]{1,0:T(8,128)(2,...) custom-call(bf16[128,512]{1,0:T(8,128)(2,1)S(1)} %copy-done.1, ...), custom_call_target="tpu_custom_call" | custom-call | flops 2000000000 | bytes 4194304 | tf_op jit(solution)/shard_map/pallas_call | solution.py:555
  27.8 0.0 collective-permute-done.3.refs_1_
  27.8 0.0 collective-permute-done.4.refs_2_
  27.8 0.3 collective-permute-done.5.refs_3_
  28.1 1.7 %shard_map.124 = (f32[256,512]{1,0:T(8,128)S(1)}, bf16[64,1024]{1,0:T(8,128)(2,1)S(1)}, bf16[64,1024]{1,0:T(8,128)(2,1)S(1)}) custom-call(bf16[1,64,512]{2,1,0:T(8,128)(2,1)S(1)} %copy-done.2, bf16[1,64,512]{2,1,0:T(8,128)(2,1)S(1)} %collective-permute-done.3.refs_1_, bf16[1,64,512]{2,1,0:T(8,128)(2,1)S(1)} %collective-permute-done.4.refs_2_, ...), custom_call_target="tpu_custom_call" | custom-call | flops 1000000000 | bytes 4194304 | tf_op jit(solution)/shard_map/pallas_call | solution.py:555
  29.8 0.1 collective-permute-start.9
  29.9 0.0 copy-start.3
  29.9 1.4 %shard_map.125 = (bf16[48,512]{1,0:T(8,128)(2,1)S(1)}, bf16[64,1024]{1,0:T(8,128)(2,1)S(1)}, bf16[64,1024]{1,0:T(8,128)(2,1)S(1)}) custom-call(bf16[192,512]{1,0:T(8,128)(2,1)S(1)} %get-tuple-element.41.grid_ref, bf16[256,512]{1,0:T(8,128)(2,1)S(1)} %get-tuple-element.42.mesh_ref, s32[64,512]{1,0:T(8,128)S(1)} %get-tuple-element.43.refs_7_.index_ref, ...), custom_call_target="tpu_custom_call" | custom-call | flops 1000000000 | bytes 4194304 | tf_op jit(solution)/shard_map/pallas_call | solution.py:555
  31.3 0.6 %collective-permute-start.6 = (bf16[64,1024]{1,0:T(8,128)(2,1)S(1)}, bf16[64,1024]{1,0:T(8,128)(2,1)S(1)}, u32[]{:S(2)}, u32[]{:S(2)}) collective-permute-start(bf16[64,1024]{1,0:T(8,128)(2,1)S(1)} %get-tuple-element.56), channel_id=1, source_target_pairs={{0,1},{1,0},{2,3},{3,2},{4,5},{5,4},{6,7},{7,6},{8,9},{9,8},{10,11... | collective-permute-start | bytes 393224 | tf_op jit(solution)/shard_map/ppermute | solution.py:568
  31.9 1.5 %collective-permute-start.10 = (bf16[64,1024]{1,0:T(8,128)(2,1)S(1)}, bf16[64,1024]{1,0:T(8,128)(2,1)S(1)}, u32[]{:S(2)}, u32[]{:S(2)}) collective-permute-start(bf16[64,1024]{1,0:T(8,128)(2,1)S(1)} %add_convert_fusion.1), channel_id=1, source_target_pairs={{0,2},{1,3},{2,0},{3,1},{4,6},{5,7},{6,4},{7,5},{8,10},{9,11},{10,... | collective-permute-start | bytes 393224 | tf_op jit(solution)/shard_map/ppermute | solution.py:568
  33.5 1.0 %collective-permute-start.7 = (bf16[64,1024]{1,0:T(8,128)(2,1)S(1)}, bf16[64,1024]{1,0:T(8,128)(2,1)S(1)}, u32[]{:S(2)}, u32[]{:S(2)}) collective-permute-start(bf16[64,1024]{1,0:T(8,128)(2,1)S(1)} %add_convert_fusion.3), channel_id=1, source_target_pairs={{0,2},{1,3},{2,0},{3,1},{4,6},{5,7},{6,4},{7,5},{8,10},{9,11},{10,... | collective-permute-start | bytes 393224 | tf_op jit(solution)/shard_map/ppermute | solution.py:568
  34.4 3.9 %collective-permute-done.10 = bf16[64,1024]{1,0:T(8,128)(2,1)S(1)} collective-permute-done((bf16[64,1024]{1,0:T(8,128)(2,1)S(1)}, bf16[64,1024]{1,0:T(8,128)(2,1)S(1)}, u32[]{:S(2)}, u32[]{:S(2)}) %collective-permute-start.10) | collective-permute-done | bytes 131104 | tf_op jit(solution)/shard_map/ppermute | solution.py:568
  38.3 0.1 collective-permute-start.11
  38.4 1.8 %collective-permute-done.7 = bf16[64,1024]{1,0:T(8,128)(2,1)S(1)} collective-permute-done((bf16[64,1024]{1,0:T(8,128)(2,1)S(1)}, bf16[64,1024]{1,0:T(8,128)(2,1)S(1)}, u32[]{:S(2)}, u32[]{:S(2)}) %collective-permute-start.7) | collective-permute-done | bytes 131104 | tf_op jit(solution)/shard_map/ppermute | solution.py:568
  40.2 0.1 collective-permute-start.8
  40.3 1.1 %shard_map.126 = bf16[1,128,512]{2,1,0:T(8,128)(2,1)} custom-call(bf16[512,1536]{1,0:T(8,128)(2,1)S(1)} %get-tuple-element.40.refs_4_.turned_ref, s32[3,1,16]{2,1,0:T(1,128)S(1)} %bitcast.6, bf16[48,512]{1,0:T(8,128)(2,1)S(1)} %get-tuple-element.54.own_slot_ref), custom_call_target="tpu_custom_call" | custom-call | flops 100000000 | bytes 4194304 | tf_op jit(solution)/shard_map/pallas_call | solution.py:555
  41.4 0.0 collective-permute-done.11.other_two_ref
  41.4 0.2 collective-permute-done.8.other_one_ref
  41.6 1.0 %shard_map.127 = f32[128,2048]{1,0:T(8,128)} custom-call(bf16[64,1024]{1,0:T(8,128)(2,1)S(1)} %add_convert_fusion.2.one_ref, bf16[64,1024]{1,0:T(8,128)(2,1)S(1)} %collective-permute-done.8.other_one_ref, bf16[64,1024]{1,0:T(8,128)(2,1)S(1)} %add_convert_fusion.two_ref, bf16[64,1024]{1,0:T(8,128)(2,1)S(1)} %collective-permute-done.11.other_two_ref), custom_call_target="tpu_custom_call" | custom-call | flops 1000000 | bytes 4194304 | tf_op jit(solution)/shard_map/pallas_call | solution.py:555
  (11 shorter events, 0.2 us)
Async XLA Ops:
  0.6 18.2 %copy-start.2 = (bf16[1,64,512]{2,1,0:T(8,128)(2,1)S(1)}, bf16[1,64,512]{2,1,0:T(8,128)(2,1)}, u32[]{:S(2)}) copy-start(bf16[1,64,512]{2,1,0:T(8,128)(2,1)} %refs_0_.2) | copy-start | bytes 196612
  2.6 8.8 %collective-permute-start = (bf16[128,512]{1,0:T(8,128)(2,1)}, bf16[128,512]{1,0:T(8,128)(2,1)S(1)}, u32[]{:S(2)}, u32[]{:S(2)}) collective-permute-start(bf16[128,512]{1,0:T(8,128)(2,1)} %shard_map.121.refs_0_), channel_id=1, source_target_pairs={{0,4},{4,0},{8,12},{12,8},{1,5},{5,1},{9,13},{13,9},{2,6},{6,2},{1... | collective-permute-start | bytes 393224 | tf_op jit(solution)/shard_map/ppermute | solution.py:568
  5.6 13.2 %collective-permute-start.1 = (bf16[128,512]{1,0:T(8,128)(2,1)}, bf16[128,512]{1,0:T(8,128)(2,1)S(1)}, u32[]{:S(2)}, u32[]{:S(2)}) collective-permute-start(bf16[128,512]{1,0:T(8,128)(2,1)} %shard_map.121.refs_0_), channel_id=1, source_target_pairs={{0,8},{4,12},{8,0},{12,4},{1,9},{5,13},{9,1},{13,5},{2,10},{6,14},... | collective-permute-start | bytes 393224 | tf_op jit(solution)/shard_map/ppermute | solution.py:568
  8.2 10.6 %collective-permute-start.2 = (bf16[128,512]{1,0:T(8,128)(2,1)}, bf16[128,512]{1,0:T(8,128)(2,1)S(1)}, u32[]{:S(2)}, u32[]{:S(2)}) collective-permute-start(bf16[128,512]{1,0:T(8,128)(2,1)} %shard_map.121.refs_0_), channel_id=1, source_target_pairs={{0,12},{4,8},{8,4},{12,0},{1,13},{5,9},{9,5},{13,1},{2,14},{6,10},... | collective-permute-start | bytes 393224 | tf_op jit(solution)/shard_map/ppermute | solution.py:568
  8.2 19.5 %collective-permute-start.3 = (bf16[1,64,512]{2,1,0:T(8,128)(2,1)}, bf16[1,64,512]{2,1,0:T(8,128)(2,1)S(1)}, u32[]{:S(2)}, u32[]{:S(2)}) collective-permute-start(bf16[1,64,512]{2,1,0:T(8,128)(2,1)} %refs_0_.2), channel_id=1, source_target_pairs={{0,4},{4,0},{8,12},{12,8},{1,5},{5,1},{9,13},{13,9},{2,6},{6,2},{1... | collective-permute-start | bytes 196616 | tf_op jit(solution)/shard_map/ppermute | solution.py:568
  9.1 1.6 %copy-start = (bf16[512,2048]{1,0:T(8,128)(2,1)S(1)}, bf16[512,2048]{1,0:T(8,128)(2,1)}, u32[]{:S(2)}) copy-start(bf16[512,2048]{1,0:T(8,128)(2,1)} %source_ref) | copy-start | bytes 6291460
  10.7 12.4 %copy-start.1 = (bf16[128,512]{1,0:T(8,128)(2,1)S(1)}, bf16[128,512]{1,0:T(8,128)(2,1)}, u32[]{:S(2)}) copy-start(bf16[128,512]{1,0:T(8,128)(2,1)} %shard_map.121.refs_0_) | copy-start | bytes 393220
  18.8 9.0 %collective-permute-start.4 = (bf16[1,64,512]{2,1,0:T(8,128)(2,1)S(1)}, bf16[1,64,512]{2,1,0:T(8,128)(2,1)S(1)}, u32[]{:S(2)}, u32[]{:S(2)}) collective-permute-start(bf16[1,64,512]{2,1,0:T(8,128)(2,1)S(1)} %copy-done.2), channel_id=1, source_target_pairs={{0,8},{4,12},{8,0},{12,4},{1,9},{5,13},{9,1},{13,5},{2,10},{6,14},... | collective-permute-start | bytes 196616 | tf_op jit(solution)/shard_map/ppermute | solution.py:568
  22.0 6.1 %collective-permute-start.5 = (bf16[1,64,512]{2,1,0:T(8,128)(2,1)S(1)}, bf16[1,64,512]{2,1,0:T(8,128)(2,1)S(1)}, u32[]{:S(2)}, u32[]{:S(2)}) collective-permute-start(bf16[1,64,512]{2,1,0:T(8,128)(2,1)S(1)} %copy-done.2), channel_id=1, source_target_pairs={{0,12},{4,8},{8,4},{12,0},{1,13},{5,9},{9,5},{13,1},{2,14},{6,10},... | collective-permute-start | bytes 196616 | tf_op jit(solution)/shard_map/ppermute | solution.py:568
  29.8 2.1 %collective-permute-start.9 = (bf16[64,1024]{1,0:T(8,128)(2,1)S(1)}, bf16[64,1024]{1,0:T(8,128)(2,1)S(1)}, u32[]{:S(2)}, u32[]{:S(2)}) collective-permute-start(bf16[64,1024]{1,0:T(8,128)(2,1)S(1)} %get-tuple-element.58), channel_id=1, source_target_pairs={{0,1},{1,0},{2,3},{3,2},{4,5},{5,4},{6,7},{7,6},{8,9},{9,8},{10,11... | collective-permute-start | bytes 393224 | tf_op jit(solution)/shard_map/ppermute | solution.py:568
  29.9 10.4 %copy-start.3 = (s32[1,3,16]{2,0,1:T(1,128)S(1)}, s32[1,3,16]{2,0,1:T(1,128)}, u32[]{:S(2)}) copy-start(s32[1,3,16]{2,0,1:T(1,128)} %param.14) | copy-start | bytes 580
  31.3 2.1 %collective-permute-start.6 = (bf16[64,1024]{1,0:T(8,128)(2,1)S(1)}, bf16[64,1024]{1,0:T(8,128)(2,1)S(1)}, u32[]{:S(2)}, u32[]{:S(2)}) collective-permute-start(bf16[64,1024]{1,0:T(8,128)(2,1)S(1)} %get-tuple-element.56), channel_id=1, source_target_pairs={{0,1},{1,0},{2,3},{3,2},{4,5},{5,4},{6,7},{7,6},{8,9},{9,8},{10,11... | collective-permute-start | bytes 393224 | tf_op jit(solution)/shard_map/ppermute | solution.py:568
  31.9 6.4 %collective-permute-start.10 = (bf16[64,1024]{1,0:T(8,128)(2,1)S(1)}, bf16[64,1024]{1,0:T(8,128)(2,1)S(1)}, u32[]{:S(2)}, u32[]{:S(2)}) collective-permute-start(bf16[64,1024]{1,0:T(8,128)(2,1)S(1)} %add_convert_fusion.1), channel_id=1, source_target_pairs={{0,2},{1,3},{2,0},{3,1},{4,6},{5,7},{6,4},{7,5},{8,10},{9,11},{10,... | collective-permute-start | bytes 393224 | tf_op jit(solution)/shard_map/ppermute | solution.py:568
  33.5 6.7 %collective-permute-start.7 = (bf16[64,1024]{1,0:T(8,128)(2,1)S(1)}, bf16[64,1024]{1,0:T(8,128)(2,1)S(1)}, u32[]{:S(2)}, u32[]{:S(2)}) collective-permute-start(bf16[64,1024]{1,0:T(8,128)(2,1)S(1)} %add_convert_fusion.3), channel_id=1, source_target_pairs={{0,2},{1,3},{2,0},{3,1},{4,6},{5,7},{6,4},{7,5},{8,10},{9,11},{10,... | collective-permute-start | bytes 393224 | tf_op jit(solution)/shard_map/ppermute | solution.py:568
  38.3 3.0 %collective-permute-start.11 = (bf16[64,1024]{1,0:T(8,128)(2,1)S(1)}, bf16[64,1024]{1,0:T(8,128)(2,1)S(1)}, u32[]{:S(2)}, u32[]{:S(2)}) collective-permute-start(bf16[64,1024]{1,0:T(8,128)(2,1)S(1)} %add_convert_fusion.two_ref), channel_id=1, source_target_pairs={{0,1},{1,0},{2,3},{3,2},{4,5},{5,4},{6,7},{7,6},{8,9},{9,8},{10,11... | collective-permute-start | bytes 393224 | tf_op jit(solution)/shard_map/ppermute | solution.py:568
  40.2 1.4 %collective-permute-start.8 = (bf16[64,1024]{1,0:T(8,128)(2,1)S(1)}, bf16[64,1024]{1,0:T(8,128)(2,1)S(1)}, u32[]{:S(2)}, u32[]{:S(2)}) collective-permute-start(bf16[64,1024]{1,0:T(8,128)(2,1)S(1)} %add_convert_fusion.2.one_ref), channel_id=1, source_target_pairs={{0,1},{1,0},{2,3},{3,2},{4,5},{5,4},{6,7},{7,6},{8,9},{9,8},{10,11... | collective-permute-start | bytes 393224 | tf_op jit(solution)/shard_map/ppermute | solution.py:568

commit v3 on v2

--- a/solution.py
+++ b/solution.py
@@ -241,12 +241,11 @@
 
 
 def pack_kernel(*refs):
-    sources, packed_ref, index_ref = refs[:8], refs[8], refs[9]
-    local, semaphores = refs[10:18], refs[18]
+    sources, packed_ref, index_ref = refs[:7], refs[7], refs[8]
+    local, semaphores = refs[9:16], refs[16]
     fetch(list(zip(sources, local)), semaphores)
     (
         grid_ref,
-        mesh_ref,
         g2m_pick_ref,
         g2m_sender_ref,
         g2m_receiver_ref,
@@ -255,7 +254,6 @@
         m2m_receiver_ref,
     ) = local
     lists, _, capacity = g2m_pick_ref.shape
-    mesh_count = mesh_ref.shape[1]
     regions, mesh_cap = m2m_pick_ref.shape[1:]
     edges = g2m_sender_ref.shape[1]
     grid_rows = grid_ref[0]
@@ -263,7 +261,6 @@
         picked = one_hot(g2m_pick_ref[i], grid_rows.shape[0])
         packed_ref[i * capacity : (i + 1) * capacity, :] = dot_first(picked, grid_rows).astype(BF16)
     first = lists * capacity
-    packed_ref[first : first + mesh_count, :] = mesh_ref[0]
     index_ref[...] = jnp.zeros_like(index_ref)
     index_ref[0:1, 0:edges] = g2m_sender_ref[...].astype(F32)
     index_ref[0:1, edges : 2 * edges] = g2m_receiver_ref[...].astype(F32)
@@ -276,7 +273,7 @@
     lane = lax.broadcasted_iota(jnp.int32, (regions, slots), 1)
     owned = lane // mesh_cap == lax.broadcasted_iota(jnp.int32, (regions, slots), 0)
     index_ref[2:3, 0:slots] = jnp.sum(jnp.where(owned, spread, 0.0), 0, keepdims=True)
-    packed_ref[first + mesh_count :, :] = index_ref[...].astype(BF16)
+    packed_ref[first:, :] = index_ref[...].astype(BF16)
 
 
 def weights_kernel(source_ref, weights_ref, turned_ref, semaphores):
@@ -305,7 +302,7 @@
     mesh_cap,
     *refs,
 ):
-    packed_refs = refs[:regions]
+    packed_refs, latent_refs = refs[:regions], refs[regions : 2 * regions]
     (
         weights_ref,
         mesh_out_ref,
@@ -321,18 +318,18 @@
         normed_two_ref,
         scaled_two_ref,
         packed_index,
-    ) = refs[regions:]
+    ) = refs[2 * regions :]
     latent = weights_ref.shape[0]
     edges = slope_one_ref.shape[0] // regions
     capacity = listed // 3
     slots = regions * mesh_cap
     me = lax.axis_index("space")
-    for back, packed_ref in enumerate(packed_refs):
+    for back, (packed_ref, latent_ref) in enumerate(zip(packed_refs, latent_refs)):
         region = lax.bitwise_xor(me, back)
         at = lambda rows: pl.ds(pl.multiple_of(region * rows, rows), rows)
         grid_ref[at(listed), :] = packed_ref[:listed, :]
-        mesh_ref[at(mesh_count), :] = packed_ref[listed : listed + mesh_count, :]
-        packed_index[at(INDEX_ROWS), :] = packed_ref[listed + mesh_count :, :]
+        mesh_ref[at(mesh_count), :] = latent_ref[0]
+        packed_index[at(INDEX_ROWS), :] = packed_ref[listed:, :]
     index_ref[...] = packed_index[...].astype(F32).astype(jnp.int32)
 
     grid_proj = dot(grid_ref[...], weights_ref[:, :latent])
@@ -536,15 +533,40 @@
     grid_grad_ref[0] = total.astype(BF16)
 
 
-def finish_kernel(one_ref, other_one_ref, two_ref, other_two_ref, weight_grad_ref):
-    half, width = one_ref.shape
+def place(pairs, stages, semaphores):
+    copies = []
+    for n, (block_ref, target) in enumerate(pairs):
+        stages[n][...] = block_ref[...].astype(F32)
+        copies.append(pltpu.make_async_copy(stages[n], target, semaphores.at[n]))
+        copies[n].start()
+    for copy in copies:
+        copy.wait()
+
+
+def half_rows(half):
     core = lax.bitwise_and(lax.axis_index("rep"), 1)
     mine = pl.ds(pl.multiple_of(core * half, half), half)
-    other = pl.ds(pl.multiple_of((1 - core) * half, half), half)
-    weight_grad_ref[mine, :width] = one_ref[...].astype(F32)
-    weight_grad_ref[other, :width] = other_one_ref[...].astype(F32)
-    weight_grad_ref[mine, width:] = two_ref[...].astype(F32)
-    weight_grad_ref[other, width:] = other_two_ref[...].astype(F32)
+    return mine, pl.ds(pl.multiple_of((1 - core) * half, half), half)
+
+
+def settle_kernel(one_ref, two_ref, other_two_ref, weight_grad_ref, *scratch):
+    half, width = one_ref.shape
+    mine, other = half_rows(half)
+    place(
+        [
+            (two_ref, weight_grad_ref.at[mine, width:]),
+            (other_two_ref, weight_grad_ref.at[other, width:]),
+            (one_ref, weight_grad_ref.at[mine, :width]),
+        ],
+        scratch[:3],
+        scratch[3],
+    )
+
+
+def finish_kernel(other_one_ref, settled_ref, weight_grad_ref, stage, semaphores):
+    half, width = other_one_ref.shape
+    _, other = half_rows(half)
+    place([(other_one_ref, weight_grad_ref.at[other, :width])], [stage], semaphores)
 
 
 VMEM = pl.BlockSpec(memory_space=pltpu.VMEM)
@@ -604,7 +626,6 @@
     g2m_pick = g2m_pick.transpose(1, 0, 2)
     sources = (
         grid_latent,
-        mesh_latent,
         g2m_pick,
         g2m_sender.reshape(1, -1),
         g2m_receiver.reshape(1, -1),
@@ -615,16 +636,17 @@
     packed = call(
         pack_kernel,
         sources,
-        [((listed + mesh_count + INDEX_ROWS, latent), BF16)],
+        [((listed + INDEX_ROWS, latent), BF16)],
         [((INDEX_ROWS, latent), F32)] + [(source.shape, source.dtype) for source in sources],
         10**7,
         fetched=len(sources),
         megabytes=56,
     )[0]
+    steps = range(1, regions)
+    latents = [mesh_latent] + [swap(mesh_latent, "space", step) for step in steps]
     packed, cotangent, weights = lax.optimization_barrier((packed, mesh_cotangent, weights))
-    steps = sorted(range(1, regions), key=lambda step: -step)
-    packs = {step: swap(packed, "space", step) for step in steps}
-    cotangents = {1: swap(cotangent, "space", 1)}
+    packs = [packed] + [swap(packed, "space", step) for step in steps]
+    cotangents = [cotangent, swap(cotangent, "space", 1)]
     weights, turned = call(
         weights_kernel,
         (weights,),
@@ -633,13 +655,11 @@
         10**8,
         fetched=1,
     )
-    *packs, cotangent = lax.optimization_barrier(
-        [packed] + [packs[step] for step in range(1, regions)] + [cotangent]
-    )
-    for step in steps:
-        if step > 1:
-            cotangents[step] = swap(cotangent, "space", step)
-    cotangents = [cotangent] + [cotangents[step] for step in range(1, regions)]
+    near = regions - 1
+    *nearer, cotangent = lax.optimization_barrier(packs[:near] + latents[:near] + [cotangent])
+    packs = nearer[:near] + packs[near:]
+    latents = nearer[near:] + latents[near:]
+    cotangents = cotangents + [swap(cotangent, "space", step) for step in steps if step > 1]
     rows = regions * mesh_count
     (
         mesh_out,
@@ -656,7 +676,7 @@
         scaled_two,
     ) = call(
         functools.partial(forward_kernel, regions, listed, mesh_count, mesh_cap),
-        (*packs, weights),
+        (*packs, *latents, weights),
         [
             (mesh_latent.shape, BF16),
             ((regions * listed, latent), BF16),
@@ -721,13 +741,26 @@
         [],
         10**8,
     )[0]
-    weight_grad = call(
+    one, other_one = summed_half(keep_one, give_one)
+    two, other_two = summed_half(keep_two, give_two)
+    hbm = pl.BlockSpec(memory_space=pltpu.HBM)
+    stage = pltpu.VMEM((half, 2 * latent), F32)
+    weight_shape = jax.ShapeDtypeStruct((columns, 4 * latent), F32)
+    settled = pl.pallas_call(
+        settle_kernel,
+        out_shape=weight_shape,
+        in_specs=[VMEM] * 3,
+        out_specs=hbm,
+        scratch_shapes=[stage] * 3 + [pltpu.SemaphoreType.DMA((3,))],
+    )(one, two, other_two)
+    weight_grad = pl.pallas_call(
         finish_kernel,
-        (*summed_half(keep_one, give_one), *summed_half(keep_two, give_two)),
-        [((columns, 4 * latent), F32)],
-        [],
-        10**6,
-    )[0]
+        out_shape=weight_shape,
+        in_specs=[VMEM, hbm],
+        out_specs=hbm,
+        scratch_shapes=[stage, pltpu.SemaphoreType.DMA((1,))],
+        input_output_aliases={1: 0},
+    )(other_one, settled)
     return (mesh_out, grid_grad, weight_grad)
 
 

time: 42.8 us -> 44.8 us (1.047)
  the two profiles are of different devices: /device:TPU:0 before, /device:TPU:15 now
where the time goes in v3:
time: 44.8 us; the launch traced here: 44.6 us
  starting transfers between devices  18.1 us (40%)
  Pallas kernels  14.9 us (33%)
  waiting for transfers between devices  7.77 us (17%)
  local copies, waits for them, and re-layouts  2.89 us (6%)
  between operations  0.79 us (2%)
    ppermute x15, starting transfers between devices, swap(): lax.ppermute(block, axis, [(i, i ^ bits) for i in range(lax.axis_size(axi...  18.1 us
    pallas_call x6, Pallas kernels, call(): pl.pallas_call(kernel, out_shape=[jax.ShapeDtypeStruct(shape, kind) for s...  11.3 us
    ppermute x15, waiting for transfers between devices, swap(): lax.ppermute(block, axis, [(i, i ^ bits) for i in range(lax.axis_size(axi...  7.77 us
    unnamed x18, local copies, waits for them, and re-layouts  2.89 us
    pallas_call x1, Pallas kernels, whole_sample_body(): pl.pallas_call(settle_kernel, out_shape=weight_shape, in_specs=[VMEM] * 3...  1.95 us
    pallas_call x1, Pallas kernels, whole_sample_body(): pl.pallas_call(finish_kernel, out_shape=weight_shape, in_specs=[VMEM, hbm...  1.63 us
  transfers between devices with their start and end apart: 15, of which 5 were waited for; matrix products, arithmetic and copies ran while one was open for 0% of the time, Pallas kernels for 22%

profile of v3, /device:TPU:15, one launch (start us, length us, event | category | flops | bytes accessed | tf_op | source)
XLA Modules:
  0.0 44.6 jit_solution(3545436794445568635)
XLA Ops:
  0.6 0.0 copy-start.4
  0.7 1.9 %shard_map.121.refs_0_ = bf16[64,512]{1,0:T(8,128)(2,1)} custom-call(bf16[1,128,512]{2,1,0:T(8,128)(2,1)} %refs_0_.1, s32[3,1,16]{2,1,0:T(1,128)} %bitcast.5, s32[1,256]{1,0:T(1,128)} %bitcast.7, s32[1,256]{1,0:T(1,128)} %bitcast.8, s32[1,4,8]{2,1,0:T(4,128)} %refs_4_.1, s32[1,256]{1,0:T(1,128)} %bitcast.9, s32[1,256]{1,0:T(1,128)} %bitcast.10), custom_call_target="tpu_custom_call" | custom-call | flops 10000000 | bytes 4194304 | tf_op jit(solution)/shard_map/pallas_call | solution.py:577
  2.5 0.2 collective-permute-start
  2.8 2.3 %collective-permute-start.1 = (bf16[64,512]{1,0:T(8,128)(2,1)}, bf16[64,512]{1,0:T(8,128)(2,1)S(1)}, u32[]{:S(2)}, u32[]{:S(2)}) collective-permute-start(bf16[64,512]{1,0:T(8,128)(2,1)} %shard_map.121.refs_0_), channel_id=1, source_target_pairs={{0,8},{4,12},{8,0},{12,4},{1,9},{5,13},{9,1},{13,5},{2,10},{6,14},... | collective-permute-start | bytes 196616 | tf_op jit(solution)/shard_map/ppermute | solution.py:590
  5.1 1.3 %collective-permute-start.2 = (bf16[1,64,512]{2,1,0:T(8,128)(2,1)}, bf16[1,64,512]{2,1,0:T(8,128)(2,1)S(1)}, u32[]{:S(2)}, u32[]{:S(2)}) collective-permute-start(bf16[1,64,512]{2,1,0:T(8,128)(2,1)} %refs_4_.2), channel_id=1, source_target_pairs={{0,4},{4,0},{8,12},{12,8},{1,5},{5,1},{9,13},{13,9},{2,6},{6,2},{1... | collective-permute-start | bytes 196616 | tf_op jit(solution)/shard_map/ppermute | solution.py:590
  6.4 0.1 collective-permute-start.3
  6.4 1.3 %collective-permute-start.4 = (bf16[64,512]{1,0:T(8,128)(2,1)}, bf16[64,512]{1,0:T(8,128)(2,1)S(1)}, u32[]{:S(2)}, u32[]{:S(2)}) collective-permute-start(bf16[64,512]{1,0:T(8,128)(2,1)} %shard_map.121.refs_0_), channel_id=1, source_target_pairs={{0,12},{4,8},{8,4},{12,0},{1,13},{5,9},{9,5},{13,1},{2,14},{6,10},... | collective-permute-start | bytes 196616 | tf_op jit(solution)/shard_map/ppermute | solution.py:590
  7.7 0.2 collective-permute-start.5
  7.9 1.6 %copy-done = bf16[512,2048]{1,0:T(8,128)(2,1)S(1)} copy-done((bf16[512,2048]{1,0:T(8,128)(2,1)S(1)}, bf16[512,2048]{1,0:T(8,128)(2,1)}, u32[]{:S(2)}) %copy-start) | copy-done | bytes 2097176
  9.5 0.6 %shard_map.122 = (bf16[512,2048]{1,0:T(8,128)(2,1)S(1)}, bf16[512,1536]{1,0:T(8,128)(2,1)S(1)}) custom-call(bf16[512,2048]{1,0:T(8,128)(2,1)S(1)} %copy-done), custom_call_target="tpu_custom_call" | custom-call | flops 100000000 | bytes 4194304 | tf_op jit(solution)/shard_map/pallas_call | solution.py:577
  10.1 2.1 %collective-permute-start.6 = (bf16[1,64,512]{2,1,0:T(8,128)(2,1)S(1)}, bf16[1,64,512]{2,1,0:T(8,128)(2,1)S(1)}, u32[]{:S(2)}, u32[]{:S(2)}) collective-permute-start(bf16[1,64,512]{2,1,0:T(8,128)(2,1)S(1)} %copy-done.1), channel_id=1, source_target_pairs={{0,4},{4,0},{8,12},{12,8},{1,5},{5,1},{9,13},{13,9},{2,6},{6,2},{1... | collective-permute-start | bytes 196616 | tf_op jit(solution)/shard_map/ppermute | solution.py:590
  12.3 2.1 %collective-permute-start.7 = (bf16[1,64,512]{2,1,0:T(8,128)(2,1)S(1)}, bf16[1,64,512]{2,1,0:T(8,128)(2,1)S(1)}, u32[]{:S(2)}, u32[]{:S(2)}) collective-permute-start(bf16[1,64,512]{2,1,0:T(8,128)(2,1)S(1)} %copy-done.1), channel_id=1, source_target_pairs={{0,8},{4,12},{8,0},{12,4},{1,9},{5,13},{9,1},{13,5},{2,10},{6,14},... | collective-permute-start | bytes 196616 | tf_op jit(solution)/shard_map/ppermute | solution.py:590
  14.4 0.3 collective-permute-start.8
  14.7 0.5 %collective-permute-done.4.refs_3_ = bf16[64,512]{1,0:T(8,128)(2,1)S(1)} collective-permute-done((bf16[64,512]{1,0:T(8,128)(2,1)}, bf16[64,512]{1,0:T(8,128)(2,1)S(1)}, u32[]{:S(2)}, u32[]{:S(2)}) %collective-permute-start.4) | collective-permute-done | bytes 65568 | tf_op jit(solution)/shard_map/ppermute | solution.py:590
  15.2 2.8 %collective-permute-done.5.refs_7_ = bf16[1,64,512]{2,1,0:T(8,128)(2,1)S(1)} collective-permute-done((bf16[1,64,512]{2,1,0:T(8,128)(2,1)}, bf16[1,64,512]{2,1,0:T(8,128)(2,1)S(1)}, u32[]{:S(2)}, u32[]{:S(2)}) %collective-permute-start.5) | collective-permute-done | bytes 65568 | tf_op jit(solution)/shard_map/ppermute | solution.py:590
  18.0 4.6 %shard_map.123 = (bf16[1,64,512]{2,1,0:T(8,128)(2,1)}, bf16[192,512]{1,0:T(8,128)(2,1)S(1)}, bf16[256,512]{1,0:T(8,128)(2,1)S(1)}, bf16[256,512]{1,0:T(8,128)(2,...) custom-call(bf16[64,512]{1,0:T(8,128)(2,1)S(1)} %copy-done.2, ...), custom_call_target="tpu_custom_call" | custom-call | flops 2000000000 | bytes 4194304 | tf_op jit(solution)/shard_map/pallas_call | solution.py:577
  22.7 1.7 %shard_map.124 = (f32[256,512]{1,0:T(8,128)S(1)}, bf16[64,1024]{1,0:T(8,128)(2,1)S(1)}, bf16[64,1024]{1,0:T(8,128)(2,1)S(1)}) custom-call(bf16[1,64,512]{2,1,0:T(8,128)(2,1)S(1)} %copy-done.1, bf16[1,64,512]{2,1,0:T(8,128)(2,1)S(1)} %collective-permute-done.6.refs_1_, bf16[1,64,512]{2,1,0:T(8,128)(2,1)S(1)} %collective-permute-done.7.refs_2_, ...), custom_call_target="tpu_custom_call" | custom-call | flops 1000000000 | bytes 4194304 | tf_op jit(solution)/shard_map/pallas_call | solution.py:577
  24.4 3.8 %collective-permute-start.12 = (bf16[64,1024]{1,0:T(8,128)(2,1)S(1)}, bf16[64,1024]{1,0:T(8,128)(2,1)S(1)}, u32[]{:S(2)}, u32[]{:S(2)}) collective-permute-start(bf16[64,1024]{1,0:T(8,128)(2,1)S(1)} %get-tuple-element.62), channel_id=1, source_target_pairs={{0,1},{1,0},{2,3},{3,2},{4,5},{5,4},{6,7},{7,6},{8,9},{9,8},{10,11... | collective-permute-start | bytes 393224 | tf_op jit(solution)/shard_map/ppermute | solution.py:590
  28.1 1.4 %shard_map.125 = (bf16[48,512]{1,0:T(8,128)(2,1)S(1)}, bf16[64,1024]{1,0:T(8,128)(2,1)S(1)}, bf16[64,1024]{1,0:T(8,128)(2,1)S(1)}) custom-call(bf16[192,512]{1,0:T(8,128)(2,1)S(1)} %get-tuple-element.45.grid_ref, bf16[256,512]{1,0:T(8,128)(2,1)S(1)} %get-tuple-element.46.mesh_ref, s32[64,512]{1,0:T(8,128)S(1)} %get-tuple-element.47.refs_7_.index_ref, ...), custom_call_target="tpu_custom_call" | custom-call | flops 1000000000 | bytes 4194304 | tf_op jit(solution)/shard_map/pallas_call | solution.py:577
  29.5 0.1 collective-permute-start.9
  29.7 0.3 collective-permute-start.13
  30.0 1.0 %collective-permute-done.9 = bf16[64,1024]{1,0:T(8,128)(2,1)S(1)} collective-permute-done((bf16[64,1024]{1,0:T(8,128)(2,1)S(1)}, bf16[64,1024]{1,0:T(8,128)(2,1)S(1)}, u32[]{:S(2)}, u32[]{:S(2)}) %collective-permute-start.9) | collective-permute-done | bytes 131104 | tf_op jit(solution)/shard_map/ppermute | solution.py:590
  31.0 0.3 collective-permute-start.10
  31.3 3.0 %collective-permute-done.13 = bf16[64,1024]{1,0:T(8,128)(2,1)S(1)} collective-permute-done((bf16[64,1024]{1,0:T(8,128)(2,1)S(1)}, bf16[64,1024]{1,0:T(8,128)(2,1)S(1)}, u32[]{:S(2)}, u32[]{:S(2)}) %collective-permute-start.13) | collective-permute-done | bytes 131104 | tf_op jit(solution)/shard_map/ppermute | solution.py:590
  34.4 2.3 %collective-permute-start.14 = (bf16[64,1024]{1,0:T(8,128)(2,1)S(1)}, bf16[64,1024]{1,0:T(8,128)(2,1)S(1)}, u32[]{:S(2)}, u32[]{:S(2)}) collective-permute-start(bf16[64,1024]{1,0:T(8,128)(2,1)S(1)} %add_convert_fusion.two_ref), channel_id=1, source_target_pairs={{0,1},{1,0},{2,3},{3,2},{4,5},{5,4},{6,7},{7,6},{8,9},{9,8},{10,11... | collective-permute-start | bytes 393224 | tf_op jit(solution)/shard_map/ppermute | solution.py:590
  36.7 0.4 collective-permute-done.10
  37.2 1.4 %collective-permute-start.11 = (bf16[64,1024]{1,0:T(8,128)(2,1)S(1)}, bf16[64,1024]{1,0:T(8,128)(2,1)S(1)}, u32[]{:S(2)}, u32[]{:S(2)}) collective-permute-start(bf16[64,1024]{1,0:T(8,128)(2,1)S(1)} %add_convert_fusion.2.one_ref), channel_id=1, source_target_pairs={{0,1},{1,0},{2,3},{3,2},{4,5},{5,4},{6,7},{7,6},{8,9},{9,8},{10,11... | collective-permute-start | bytes 393224 | tf_op jit(solution)/shard_map/ppermute | solution.py:590
  38.6 1.1 %shard_map.126 = bf16[1,128,512]{2,1,0:T(8,128)(2,1)} custom-call(bf16[512,1536]{1,0:T(8,128)(2,1)S(1)} %get-tuple-element.44.refs_4_.turned_ref, s32[3,1,16]{2,1,0:T(1,128)S(1)} %bitcast.6, bf16[48,512]{1,0:T(8,128)(2,1)S(1)} %get-tuple-element.58.own_slot_ref), custom_call_target="tpu_custom_call" | custom-call | flops 100000000 | bytes 4194304 | tf_op jit(solution)/shard_map/pallas_call | solution.py:577
  39.7 0.6 %copy-done.8 = bf16[64,1024]{1,0:T(8,128)(2,1)} copy-done((bf16[64,1024]{1,0:T(8,128)(2,1)}, bf16[64,1024]{1,0:T(8,128)(2,1)S(1)}, u32[]{:S(2)}) %copy-start.8) | copy-done | bytes 131096
  40.3 1.9 %shard_map.127.settled_ref = f32[128,2048]{1,0:T(8,128)} custom-call(bf16[64,1024]{1,0:T(8,128)(2,1)} %copy-done.6, bf16[64,1024]{1,0:T(8,128)(2,1)} %copy-done.5, bf16[64,1024]{1,0:T(8,128)(2,1)} %copy-done.8), custom_call_target="tpu_custom_call" | custom-call | tf_op jit(solution)/shard_map/pallas_call | solution.py:749
  42.3 0.6 %copy-done.7 = bf16[64,1024]{1,0:T(8,128)(2,1)} copy-done((bf16[64,1024]{1,0:T(8,128)(2,1)}, bf16[64,1024]{1,0:T(8,128)(2,1)S(1)}, u32[]{:S(2)}) %copy-start.7) | copy-done | bytes 131096
  42.9 1.6 %shard_map.128 = f32[128,2048]{1,0:T(8,128)} custom-call(bf16[64,1024]{1,0:T(8,128)(2,1)} %copy-done.7, f32[128,2048]{1,0:T(8,128)} %shard_map.127.settled_ref), custom_call_target="tpu_custom_call", output_to_operand_aliasing={{}: (1, {})} | custom-call | tf_op jit(solution)/shard_map/pallas_call | solution.py:756
  (28 shorter events, 0.2 us)
Async XLA Ops:
  0.6 9.5 %copy-start.1 = (bf16[1,64,512]{2,1,0:T(8,128)(2,1)S(1)}, bf16[1,64,512]{2,1,0:T(8,128)(2,1)}, u32[]{:S(2)}) copy-start(bf16[1,64,512]{2,1,0:T(8,128)(2,1)} %refs_0_.2) | copy-start | bytes 196612
  0.6 17.4 %copy-start.4 = (bf16[1,64,512]{2,1,0:T(8,128)(2,1)S(1)}, bf16[1,64,512]{2,1,0:T(8,128)(2,1)}, u32[]{:S(2)}) copy-start(bf16[1,64,512]{2,1,0:T(8,128)(2,1)} %refs_4_.2) | copy-start | bytes 196612
  2.5 5.2 %collective-permute-start = (bf16[64,512]{1,0:T(8,128)(2,1)}, bf16[64,512]{1,0:T(8,128)(2,1)S(1)}, u32[]{:S(2)}, u32[]{:S(2)}) collective-permute-start(bf16[64,512]{1,0:T(8,128)(2,1)} %shard_map.121.refs_0_), channel_id=1, source_target_pairs={{0,4},{4,0},{8,12},{12,8},{1,5},{5,1},{9,13},{13,9},{2,6},{6,2},{1... | collective-permute-start | bytes 196616 | tf_op jit(solution)/shard_map/ppermute | solution.py:590
  2.8 7.3 %collective-permute-start.1 = (bf16[64,512]{1,0:T(8,128)(2,1)}, bf16[64,512]{1,0:T(8,128)(2,1)S(1)}, u32[]{:S(2)}, u32[]{:S(2)}) collective-permute-start(bf16[64,512]{1,0:T(8,128)(2,1)} %shard_map.121.refs_0_), channel_id=1, source_target_pairs={{0,8},{4,12},{8,0},{12,4},{1,9},{5,13},{9,1},{13,5},{2,10},{6,14},... | collective-permute-start | bytes 196616 | tf_op jit(solution)/shard_map/ppermute | solution.py:590
  5.1 7.2 %collective-permute-start.2 = (bf16[1,64,512]{2,1,0:T(8,128)(2,1)}, bf16[1,64,512]{2,1,0:T(8,128)(2,1)S(1)}, u32[]{:S(2)}, u32[]{:S(2)}) collective-permute-start(bf16[1,64,512]{2,1,0:T(8,128)(2,1)} %refs_4_.2), channel_id=1, source_target_pairs={{0,4},{4,0},{8,12},{12,8},{1,5},{5,1},{9,13},{13,9},{2,6},{6,2},{1... | collective-permute-start | bytes 196616 | tf_op jit(solution)/shard_map/ppermute | solution.py:590
  6.4 5.9 %collective-permute-start.3 = (bf16[1,64,512]{2,1,0:T(8,128)(2,1)}, bf16[1,64,512]{2,1,0:T(8,128)(2,1)S(1)}, u32[]{:S(2)}, u32[]{:S(2)}) collective-permute-start(bf16[1,64,512]{2,1,0:T(8,128)(2,1)} %refs_4_.2), channel_id=1, source_target_pairs={{0,8},{4,12},{8,0},{12,4},{1,9},{5,13},{9,1},{13,5},{2,10},{6,14},... | collective-permute-start | bytes 196616 | tf_op jit(solution)/shard_map/ppermute | solution.py:590
  6.4 8.8 %collective-permute-start.4 = (bf16[64,512]{1,0:T(8,128)(2,1)}, bf16[64,512]{1,0:T(8,128)(2,1)S(1)}, u32[]{:S(2)}, u32[]{:S(2)}) collective-permute-start(bf16[64,512]{1,0:T(8,128)(2,1)} %shard_map.121.refs_0_), channel_id=1, source_target_pairs={{0,12},{4,8},{8,4},{12,0},{1,13},{5,9},{9,5},{13,1},{2,14},{6,10},... | collective-permute-start | bytes 196616 | tf_op jit(solution)/shard_map/ppermute | solution.py:590
  7.7 10.3 %collective-permute-start.5 = (bf16[1,64,512]{2,1,0:T(8,128)(2,1)}, bf16[1,64,512]{2,1,0:T(8,128)(2,1)S(1)}, u32[]{:S(2)}, u32[]{:S(2)}) collective-permute-start(bf16[1,64,512]{2,1,0:T(8,128)(2,1)} %refs_4_.2), channel_id=1, source_target_pairs={{0,12},{4,8},{8,4},{12,0},{1,13},{5,9},{9,5},{13,1},{2,14},{6,10},... | collective-permute-start | bytes 196616 | tf_op jit(solution)/shard_map/ppermute | solution.py:590
  7.9 1.6 %copy-start = (bf16[512,2048]{1,0:T(8,128)(2,1)S(1)}, bf16[512,2048]{1,0:T(8,128)(2,1)}, u32[]{:S(2)}) copy-start(bf16[512,2048]{1,0:T(8,128)(2,1)} %source_ref) | copy-start | bytes 6291460
  9.5 8.5 %copy-start.2 = (bf16[64,512]{1,0:T(8,128)(2,1)S(1)}, bf16[64,512]{1,0:T(8,128)(2,1)}, u32[]{:S(2)}) copy-start(bf16[64,512]{1,0:T(8,128)(2,1)} %shard_map.121.refs_0_) | copy-start | bytes 196612
  10.1 12.5 %collective-permute-start.6 = (bf16[1,64,512]{2,1,0:T(8,128)(2,1)S(1)}, bf16[1,64,512]{2,1,0:T(8,128)(2,1)S(1)}, u32[]{:S(2)}, u32[]{:S(2)}) collective-permute-start(bf16[1,64,512]{2,1,0:T(8,128)(2,1)S(1)} %copy-done.1), channel_id=1, source_target_pairs={{0,4},{4,0},{8,12},{12,8},{1,5},{5,1},{9,13},{13,9},{2,6},{6,2},{1... | collective-permute-start | bytes 196616 | tf_op jit(solution)/shard_map/ppermute | solution.py:590
  12.3 10.4 %collective-permute-start.7 = (bf16[1,64,512]{2,1,0:T(8,128)(2,1)S(1)}, bf16[1,64,512]{2,1,0:T(8,128)(2,1)S(1)}, u32[]{:S(2)}, u32[]{:S(2)}) collective-permute-start(bf16[1,64,512]{2,1,0:T(8,128)(2,1)S(1)} %copy-done.1), channel_id=1, source_target_pairs={{0,8},{4,12},{8,0},{12,4},{1,9},{5,13},{9,1},{13,5},{2,10},{6,14},... | collective-permute-start | bytes 196616 | tf_op jit(solution)/shard_map/ppermute | solution.py:590
  14.4 8.3 %collective-permute-start.8 = (bf16[1,64,512]{2,1,0:T(8,128)(2,1)S(1)}, bf16[1,64,512]{2,1,0:T(8,128)(2,1)S(1)}, u32[]{:S(2)}, u32[]{:S(2)}) collective-permute-start(bf16[1,64,512]{2,1,0:T(8,128)(2,1)S(1)} %copy-done.1), channel_id=1, source_target_pairs={{0,12},{4,8},{8,4},{12,0},{1,13},{5,9},{9,5},{13,1},{2,14},{6,10},... | collective-permute-start | bytes 196616 | tf_op jit(solution)/shard_map/ppermute | solution.py:590
  24.4 5.3 %collective-permute-start.12 = (bf16[64,1024]{1,0:T(8,128)(2,1)S(1)}, bf16[64,1024]{1,0:T(8,128)(2,1)S(1)}, u32[]{:S(2)}, u32[]{:S(2)}) collective-permute-start(bf16[64,1024]{1,0:T(8,128)(2,1)S(1)} %get-tuple-element.62), channel_id=1, source_target_pairs={{0,1},{1,0},{2,3},{3,2},{4,5},{5,4},{6,7},{7,6},{8,9},{9,8},{10,11... | collective-permute-start | bytes 393224 | tf_op jit(solution)/shard_map/ppermute | solution.py:590
  28.1 10.5 %copy-start.3 = (s32[1,3,16]{2,0,1:T(1,128)S(1)}, s32[1,3,16]{2,0,1:T(1,128)}, u32[]{:S(2)}) copy-start(s32[1,3,16]{2,0,1:T(1,128)} %param.14) | copy-start | bytes 580
  29.5 1.4 %collective-permute-start.9 = (bf16[64,1024]{1,0:T(8,128)(2,1)S(1)}, bf16[64,1024]{1,0:T(8,128)(2,1)S(1)}, u32[]{:S(2)}, u32[]{:S(2)}) collective-permute-start(bf16[64,1024]{1,0:T(8,128)(2,1)S(1)} %get-tuple-element.60), channel_id=1, source_target_pairs={{0,1},{1,0},{2,3},{3,2},{4,5},{5,4},{6,7},{7,6},{8,9},{9,8},{10,11... | collective-permute-start | bytes 393224 | tf_op jit(solution)/shard_map/ppermute | solution.py:590
  29.7 4.6 %collective-permute-start.13 = (bf16[64,1024]{1,0:T(8,128)(2,1)S(1)}, bf16[64,1024]{1,0:T(8,128)(2,1)S(1)}, u32[]{:S(2)}, u32[]{:S(2)}) collective-permute-start(bf16[64,1024]{1,0:T(8,128)(2,1)S(1)} %add_convert_fusion.1), channel_id=1, source_target_pairs={{0,2},{1,3},{2,0},{3,1},{4,6},{5,7},{6,4},{7,5},{8,10},{9,11},{10,... | collective-permute-start | bytes 393224 | tf_op jit(solution)/shard_map/ppermute | solution.py:590
  31.0 6.1 %collective-permute-start.10 = (bf16[64,1024]{1,0:T(8,128)(2,1)S(1)}, bf16[64,1024]{1,0:T(8,128)(2,1)S(1)}, u32[]{:S(2)}, u32[]{:S(2)}) collective-permute-start(bf16[64,1024]{1,0:T(8,128)(2,1)S(1)} %add_convert_fusion.3), channel_id=1, source_target_pairs={{0,2},{1,3},{2,0},{3,1},{4,6},{5,7},{6,4},{7,5},{8,10},{9,11},{10,... | collective-permute-start | bytes 393224 | tf_op jit(solution)/shard_map/ppermute | solution.py:590
  34.4 5.3 %copy-start.5 = (bf16[64,1024]{1,0:T(8,128)(2,1)}, bf16[64,1024]{1,0:T(8,128)(2,1)S(1)}, u32[]{:S(2)}) copy-start(bf16[64,1024]{1,0:T(8,128)(2,1)S(1)} %add_convert_fusion.two_ref) | copy-start | bytes 393220
  34.4 5.3 %collective-permute-start.14 = (bf16[64,1024]{1,0:T(8,128)(2,1)S(1)}, bf16[64,1024]{1,0:T(8,128)(2,1)S(1)}, u32[]{:S(2)}, u32[]{:S(2)}) collective-permute-start(bf16[64,1024]{1,0:T(8,128)(2,1)S(1)} %add_convert_fusion.two_ref), channel_id=1, source_target_pairs={{0,1},{1,0},{2,3},{3,2},{4,5},{5,4},{6,7},{7,6},{8,9},{9,8},{10,11... | collective-permute-start | bytes 393224 | tf_op jit(solution)/shard_map/ppermute | solution.py:590
  37.2 2.5 %copy-start.6 = (bf16[64,1024]{1,0:T(8,128)(2,1)}, bf16[64,1024]{1,0:T(8,128)(2,1)S(1)}, u32[]{:S(2)}) copy-start(bf16[64,1024]{1,0:T(8,128)(2,1)S(1)} %add_convert_fusion.2.one_ref) | copy-start | bytes 393220
  37.2 5.1 %collective-permute-start.11 = (bf16[64,1024]{1,0:T(8,128)(2,1)S(1)}, bf16[64,1024]{1,0:T(8,128)(2,1)S(1)}, u32[]{:S(2)}, u32[]{:S(2)}) collective-permute-start(bf16[64,1024]{1,0:T(8,128)(2,1)S(1)} %add_convert_fusion.2.one_ref), channel_id=1, source_target_pairs={{0,1},{1,0},{2,3},{3,2},{4,5},{5,4},{6,7},{7,6},{8,9},{9,8},{10,11... | collective-permute-start | bytes 393224 | tf_op jit(solution)/shard_map/ppermute | solution.py:590
  39.7 0.6 %copy-start.8 = (bf16[64,1024]{1,0:T(8,128)(2,1)}, bf16[64,1024]{1,0:T(8,128)(2,1)S(1)}, u32[]{:S(2)}) copy-start(bf16[64,1024]{1,0:T(8,128)(2,1)S(1)} %collective-permute-done.14.other_two_ref) | copy-start | bytes 393220
  42.3 0.6 %copy-start.7 = (bf16[64,1024]{1,0:T(8,128)(2,1)}, bf16[64,1024]{1,0:T(8,128)(2,1)S(1)}, u32[]{:S(2)}) copy-start(bf16[64,1024]{1,0:T(8,128)(2,1)S(1)} %collective-permute-done.11.other_one_ref) | copy-start | bytes 393220

commit v4 on v2

--- a/solution.py
+++ b/solution.py
@@ -200,6 +200,7 @@
 F32 = jnp.float32
 BF16 = jnp.bfloat16
 INDEX_ROWS = 16
+FAR_STEP = 3
 SAMPLE_EDGE_BYTES = 8 << 20
 
 
@@ -305,7 +306,7 @@
     mesh_cap,
     *refs,
 ):
-    packed_refs = refs[:regions]
+    packed_refs, forwarded_ref = refs[:regions], refs[regions]
     (
         weights_ref,
         mesh_out_ref,
@@ -321,18 +322,27 @@
         normed_two_ref,
         scaled_two_ref,
         packed_index,
-    ) = refs[regions:]
+    ) = refs[regions + 1 :]
     latent = weights_ref.shape[0]
     edges = slope_one_ref.shape[0] // regions
     capacity = listed // 3
     slots = regions * mesh_cap
     me = lax.axis_index("space")
-    for back, packed_ref in enumerate(packed_refs):
-        region = lax.bitwise_xor(me, back)
+
+    def unpack(packed_ref, region):
         at = lambda rows: pl.ds(pl.multiple_of(region * rows, rows), rows)
         grid_ref[at(listed), :] = packed_ref[:listed, :]
         mesh_ref[at(mesh_count), :] = packed_ref[listed : listed + mesh_count, :]
         packed_index[at(INDEX_ROWS), :] = packed_ref[listed + mesh_count :, :]
+
+    for step, packed_ref in enumerate(packed_refs):
+        region = lax.bitwise_xor(me, step)
+        if step < FAR_STEP:
+            unpack(packed_ref, region)
+        else:
+            inner = jnp.logical_and(me > 0, me < regions - 1)
+            pl.when(inner)(functools.partial(unpack, packed_ref, region))
+            pl.when(jnp.logical_not(inner))(functools.partial(unpack, forwarded_ref, region))
     index_ref[...] = packed_index[...].astype(F32).astype(jnp.int32)
 
     grid_proj = dot(grid_ref[...], weights_ref[:, :latent])
@@ -438,8 +448,8 @@
     edges = slope_ref.shape[0] // regions
     slots = regions * mesh_cap
     me = lax.axis_index("space")
-    for back, cotangent_ref in enumerate(cotangent_refs):
-        region = lax.bitwise_xor(me, back)
+    for step, cotangent_ref in enumerate(cotangent_refs):
+        region = lax.bitwise_xor(me, step)
         at = pl.ds(pl.multiple_of(region * mesh_count, mesh_count), mesh_count)
         upstream_ref[at, :] = cotangent_ref[0].astype(F32)
     agg_grad = moments_back(normed_ref[...], scaled_ref[:, 0:1], upstream_ref[...]).astype(BF16)
@@ -472,15 +482,52 @@
         mesh_grad_ref[rows, :] = grad[rows] + dot(hot, returned[s * slots : (s + 1) * slots])
 
 
-def encode_back_kernel(
+def encode_sums(d, index_ref, slope_ref, agg_grad, listed):
+    mesh_count = agg_grad.shape[0]
+    edges = slope_ref.shape[0] // (index_ref.shape[0] // INDEX_ROWS)
+    labels = slice(d * INDEX_ROWS, d * INDEX_ROWS + 1)
+    hot_sender = one_hot(index_ref[labels, :edges], listed)
+    hot_receiver = one_hot(index_ref[labels, edges:], mesh_count)
+    return edge_backward(
+        agg_grad,
+        jnp.concatenate([hot_sender, hot_receiver], axis=0),
+        hot_receiver,
+        slope_ref[d * edges : (d + 1) * edges, :],
+    ).astype(BF16)
+
+
+def encode_back_first_kernel(
     regions,
-    grid_ref,
-    mesh_ref,
+    listed,
     index_ref,
     slope_ref,
     normed_ref,
     scaled_ref,
     mesh_grad_ref,
+    agg_grad_ref,
+    sums_ref,
+):
+    mesh_count = normed_ref.shape[0] // regions
+    count = listed + mesh_count
+    agg_grad_ref[...] = moments_back(
+        normed_ref[...], scaled_ref[:, 0:1], mesh_grad_ref[...]
+    ).astype(BF16)
+    for d in range(regions // 2):
+        rows = slice(d * mesh_count, (d + 1) * mesh_count)
+        sums_ref[d * count : (d + 1) * count, :] = encode_sums(
+            d, index_ref, slope_ref, agg_grad_ref[rows, :], listed
+        )
+
+
+def encode_back_kernel(
+    regions,
+    listed,
+    grid_ref,
+    mesh_ref,
+    index_ref,
+    slope_ref,
+    agg_grad_ref,
+    sums_ref,
     own_slot_ref,
     keep_ref,
     give_ref,
@@ -490,25 +537,18 @@
 ):
     latent = mesh_ref.shape[1]
     mesh_count = mesh_ref.shape[0] // regions
-    listed = grid_ref.shape[0] // regions
+    count = listed + mesh_count
     capacity = listed // 3
-    edges = slope_ref.shape[0] // regions
     me = lax.axis_index("space")
-    agg_grad = moments_back(normed_ref[...], scaled_ref[:, 0:1], mesh_grad_ref[...]).astype(BF16)
     blank = jnp.zeros((capacity, latent), BF16)
     slot_ref[0:capacity, :] = blank
     slot_ref[regions * listed - capacity :, :] = blank
     for d in range(regions):
-        labels = slice(d * INDEX_ROWS, d * INDEX_ROWS + 1)
-        hot_sender = one_hot(index_ref[labels, :edges], listed)
-        hot_receiver = one_hot(index_ref[labels, edges:], mesh_count)
         rows = slice(d * mesh_count, (d + 1) * mesh_count)
-        sums = edge_backward(
-            agg_grad[rows],
-            jnp.concatenate([hot_sender, hot_receiver], axis=0),
-            hot_receiver,
-            slope_ref[d * edges : (d + 1) * edges, :],
-        ).astype(BF16)
+        if d < regions // 2:
+            sums = sums_ref[d * count : (d + 1) * count, :]
+        else:
+            sums = encode_sums(d, index_ref, slope_ref, agg_grad_ref[rows, :], listed)
         for j in range(3):
             source = d + j - 1
             if 0 <= source < regions:
@@ -572,8 +612,7 @@
     return (left.astype(F32) + right.astype(F32)).astype(BF16)
 
 
-def summed_half(keep, give):
-    half = added(keep, swap(give, "rep", 1))
+def summed_over_chips(half):
     bit = 2
     while bit < lax.axis_size("rep"):
         half = added(half, swap(half, "rep", bit))
@@ -622,9 +661,8 @@
         megabytes=56,
     )[0]
     packed, cotangent, weights = lax.optimization_barrier((packed, mesh_cotangent, weights))
-    steps = sorted(range(1, regions), key=lambda step: -step)
-    packs = {step: swap(packed, "space", step) for step in steps}
-    cotangents = {1: swap(cotangent, "space", 1)}
+    packs = [packed] + [swap(packed, "space", step) for step in range(1, min(regions, FAR_STEP))]
+    cotangents = [cotangent, swap(cotangent, "space", 1)]
     weights, turned = call(
         weights_kernel,
         (weights,),
@@ -633,13 +671,12 @@
         10**8,
         fetched=1,
     )
-    *packs, cotangent = lax.optimization_barrier(
-        [packed] + [packs[step] for step in range(1, regions)] + [cotangent]
-    )
-    for step in steps:
-        if step > 1:
-            cotangents[step] = swap(cotangent, "space", step)
-    cotangents = [cotangent] + [cotangents[step] for step in range(1, regions)]
+    forwarded = packed
+    if regions > FAR_STEP:
+        packs[2], packed, cotangent = lax.optimization_barrier((packs[2], packed, cotangent))
+        packs.append(lax.ppermute(packed, "space", [(1, 2), (2, 1)]))
+        forwarded = lax.ppermute(packs[2], "space", [(1, 0), (2, 3)])
+        cotangents += [swap(cotangent, "space", step) for step in (2, 3)]
     rows = regions * mesh_count
     (
         mesh_out,
@@ -656,7 +693,7 @@
         scaled_two,
     ) = call(
         functools.partial(forward_kernel, regions, listed, mesh_count, mesh_cap),
-        (*packs, weights),
+        (*packs, forwarded, weights),
         [
             (mesh_latent.shape, BF16),
             ((regions * listed, latent), BF16),
@@ -695,17 +732,18 @@
         ],
         10**9,
     )
+    agg_grad, sums = call(
+        functools.partial(encode_back_first_kernel, regions, listed),
+        (index, slope_one, normed_one, scaled_one, mesh_grad),
+        [((rows, latent), BF16), ((regions // 2 * (listed + mesh_count), latent), BF16)],
+        [],
+        10**9,
+    )
+    half_two, sums = lax.optimization_barrier((added(keep_two, swap(give_two, "rep", 1)), sums))
+    two, other_two = summed_over_chips(half_two)
     own_slots, keep_one, give_one = call(
-        functools.partial(encode_back_kernel, regions),
-        (
-            grid_all,
-            mesh_all,
-            index,
-            slope_one,
-            normed_one,
-            scaled_one,
-            mesh_grad,
-        ),
+        functools.partial(encode_back_kernel, regions, listed),
+        (grid_all, mesh_all, index, slope_one, agg_grad, sums),
         [((listed, latent), BF16)] + [((half, 2 * latent), BF16)] * 2,
         [
             ((regions * listed, latent), BF16),
@@ -714,6 +752,7 @@
         ],
         10**9,
     )
+    one, other_one = summed_over_chips(added(keep_one, swap(give_one, "rep", 1)))
     grid_grad = call(
         grid_back_kernel,
         (turned, g2m_pick, own_slots),
@@ -723,7 +762,7 @@
     )[0]
     weight_grad = call(
         finish_kernel,
-        (*summed_half(keep_one, give_one), *summed_half(keep_two, give_two)),
+        (one, other_one, two, other_two),
         [((columns, 4 * latent), F32)],
         [],
         10**6,
@@ -739,7 +778,7 @@
         edges = arguments[5].shape[0] + arguments[8].shape[0]
         latent = arguments[3].shape[0]
         fits = edges * latent * 4 <= SAMPLE_EDGE_BYTES and latent % (128 * regions) == 0
-        paired = all(n > 1 and n & (n - 1) == 0 for n in (regions, samples))
+        paired = regions in (2, 4) and samples > 1 and samples & (samples - 1) == 0
         return sharded(whole_sample_body if fits and paired else partitioned_body)(*arguments)
 
     def sharded(body):

time: 42.8 us -> 46.8 us (1.093)
  starting transfers between devices: 14.2 us -> 19.7 us
  waiting for transfers between devices: 13.6 us -> 11.8 us
    ppermute x12 -> x11, starting transfers between devices: 14.2 us -> 17.8 us  [swap(): lax.ppermute(block, axis, [(i, i ^ bits) for i in range(lax.axis_size(axi...]
    ppermute x0 -> x2, starting transfers between devices: none -> 1.95 us  [the longest x1 1.28 us: whole_sample_body(): forwarded = lax.ppermute(packs[2], 'space', [(1, 0), (2, 3)])]
    ppermute x12 -> x11, waiting for transfers between devices: 13.6 us -> 11.8 us  [swap(): lax.ppermute(block, axis, [(i, i ^ bits) for i in range(lax.axis_size(axi...]
    pallas_call x7 -> x8, Pallas kernels: 12.4 us -> 12.6 us  [call(): pl.pallas_call(kernel, out_shape=[jax.ShapeDtypeStruct(shape, kind) for s...]
  transfers between devices with their start and end apart: 12 -> 13, of which waited for: 5 -> 6; matrix products, arithmetic and copies ran while one was open for 0% -> 0% of each run, Pallas kernels for 18% -> 15%
where the time goes in v4:
time: 46.8 us; the launch traced here: 46.6 us
  starting transfers between devices  19.7 us (42%)
  Pallas kernels  12.6 us (27%)
  waiting for transfers between devices  11.8 us (25%)
  local copies, waits for them, and re-layouts  1.61 us (3%)
  between operations  0.79 us (2%)
    ppermute x11, starting transfers between devices, swap(): lax.ppermute(block, axis, [(i, i ^ bits) for i in range(lax.axis_size(axi...  17.8 us
    pallas_call x8, Pallas kernels, call(): pl.pallas_call(kernel, out_shape=[jax.ShapeDtypeStruct(shape, kind) for s...  12.6 us
    ppermute x11, waiting for transfers between devices, swap(): lax.ppermute(block, axis, [(i, i ^ bits) for i in range(lax.axis_size(axi...  11.8 us
    unnamed x8, local copies, waits for them, and re-layouts  1.61 us
    ppermute x1, starting transfers between devices, whole_sample_body(): forwarded = lax.ppermute(packs[2], 'space', [(1, 0), (2, 3)])  1.28 us
  transfers between devices with their start and end apart: 13, of which 6 were waited for; matrix products, arithmetic and copies ran while one was open for 0% of the time, Pallas kernels for 15%

profile of v4, /device:TPU:0, one launch (start us, length us, event | category | flops | bytes accessed | tf_op | source)
XLA Modules:
  0.0 46.6 jit_solution(14646005116232388910)
XLA Ops:
  0.6 0.0 copy-start.2
  0.6 1.9 %shard_map.121.refs_0_ = bf16[128,512]{1,0:T(8,128)(2,1)} custom-call(bf16[1,128,512]{2,1,0:T(8,128)(2,1)} %refs_0_.1, bf16[1,64,512]{2,1,0:T(8,128)(2,1)} %refs_1_.1, s32[3,1,16]{2,1,0:T(1,128)} %bitcast.5, s32[1,256]{1,0:T(1,128)} %bitcast.7, s32[1,256]{1,0:T(1,128)} %bitcast.8, s32[1,4,8]{2,1,0:T(4,128)} %refs_5_.1, s32[1,256]{1,0:T(1,128)} %bitcast.9, ...), custom_call_target="tpu_custom_call" | custom-call | flops 10000000 | bytes 4194304 | tf_op jit(solution)/shard_map/pallas_call | solution.py:595
  2.6 4.1 %collective-permute-start.1 = (bf16[128,512]{1,0:T(8,128)(2,1)}, bf16[128,512]{1,0:T(8,128)(2,1)S(1)}, u32[]{:S(2)}, u32[]{:S(2)}) collective-permute-start(bf16[128,512]{1,0:T(8,128)(2,1)} %shard_map.121.refs_0_), channel_id=1, source_target_pairs={{0,8},{4,12},{8,0},{12,4},{1,9},{5,13},{9,1},{13,5},{2,10},{6,14},... | collective-permute-start | bytes 393224 | tf_op jit(solution)/shard_map/ppermute | solution.py:608
  6.7 1.6 %collective-permute-start = (bf16[128,512]{1,0:T(8,128)(2,1)}, bf16[128,512]{1,0:T(8,128)(2,1)S(1)}, u32[]{:S(2)}, u32[]{:S(2)}) collective-permute-start(bf16[128,512]{1,0:T(8,128)(2,1)} %shard_map.121.refs_0_), channel_id=1, source_target_pairs={{0,4},{4,0},{8,12},{12,8},{1,5},{5,1},{9,13},{13,9},{2,6},{6,2},{1... | collective-permute-start | bytes 393224 | tf_op jit(solution)/shard_map/ppermute | solution.py:608
  8.2 5.0 %collective-permute-done.1.refs_2_ = bf16[128,512]{1,0:T(8,128)(2,1)S(1)} collective-permute-done((bf16[128,512]{1,0:T(8,128)(2,1)}, bf16[128,512]{1,0:T(8,128)(2,1)S(1)}, u32[]{:S(2)}, u32[]{:S(2)}) %collective-permute-start.1) | collective-permute-done | bytes 131104 | tf_op jit(solution)/shard_map/ppermute | solution.py:608
  13.3 1.3 %collective-permute-start.3 = (bf16[128,512]{1,0:T(8,128)(2,1)S(1)}, bf16[128,512]{1,0:T(8,128)(2,1)S(1)}, u32[]{:S(2)}, u32[]{:S(2)}) collective-permute-start(bf16[128,512]{1,0:T(8,128)(2,1)S(1)} %collective-permute-done.1.refs_2_), channel_id=1, source_target_pairs={{4,0},{8,12},{5,1},{9,13},{6,2},{10,14},{7,3},{11,15},{20,16},{24,... | collective-permute-start | bytes 393224 | tf_op jit(solution)/shard_map/ppermute | solution.py:678
  14.6 0.7 %collective-permute-start.2 = (bf16[128,512]{1,0:T(8,128)(2,1)}, bf16[128,512]{1,0:T(8,128)(2,1)S(1)}, u32[]{:S(2)}, u32[]{:S(2)}) collective-permute-start(bf16[128,512]{1,0:T(8,128)(2,1)} %shard_map.121.refs_0_), channel_id=1, source_target_pairs={{4,8},{8,4},{5,9},{9,5},{6,10},{10,6},{7,11},{11,7},{20,24},{24,20... | collective-permute-start | bytes 393224 | tf_op jit(solution)/shard_map/ppermute | solution.py:677
  15.2 6.5 %collective-permute-start.4 = (bf16[1,64,512]{2,1,0:T(8,128)(2,1)}, bf16[1,64,512]{2,1,0:T(8,128)(2,1)S(1)}, u32[]{:S(2)}, u32[]{:S(2)}) collective-permute-start(bf16[1,64,512]{2,1,0:T(8,128)(2,1)} %refs_0_.2), channel_id=1, source_target_pairs={{0,4},{4,0},{8,12},{12,8},{1,5},{5,1},{9,13},{13,9},{2,6},{6,2},{1... | collective-permute-start | bytes 196616 | tf_op jit(solution)/shard_map/ppermute | solution.py:608
  21.7 1.6 %copy-done = bf16[512,2048]{1,0:T(8,128)(2,1)S(1)} copy-done((bf16[512,2048]{1,0:T(8,128)(2,1)S(1)}, bf16[512,2048]{1,0:T(8,128)(2,1)}, u32[]{:S(2)}) %copy-start) | copy-done | bytes 2097176
  23.3 0.6 %shard_map.122 = (bf16[512,2048]{1,0:T(8,128)(2,1)S(1)}, bf16[512,1536]{1,0:T(8,128)(2,1)S(1)}) custom-call(bf16[512,2048]{1,0:T(8,128)(2,1)S(1)} %copy-done), custom_call_target="tpu_custom_call" | custom-call | flops 100000000 | bytes 4194304 | tf_op jit(solution)/shard_map/pallas_call | solution.py:595
  23.9 0.1 collective-permute-start.5
  24.0 2.4 %collective-permute-start.6 = (bf16[1,64,512]{2,1,0:T(8,128)(2,1)S(1)}, bf16[1,64,512]{2,1,0:T(8,128)(2,1)S(1)}, u32[]{:S(2)}, u32[]{:S(2)}) collective-permute-start(bf16[1,64,512]{2,1,0:T(8,128)(2,1)S(1)} %copy-done.2), channel_id=1, source_target_pairs={{0,12},{4,8},{8,4},{12,0},{1,13},{5,9},{9,5},{13,1},{2,14},{6,10},... | collective-permute-start | bytes 196616 | tf_op jit(solution)/shard_map/ppermute | solution.py:608
  26.4 0.0 collective-permute-done.3.refs_4_
  26.4 4.7 %shard_map.123 = (bf16[1,64,512]{2,1,0:T(8,128)(2,1)}, bf16[192,512]{1,0:T(8,128)(2,1)S(1)}, bf16[256,512]{1,0:T(8,128)(2,1)S(1)}, bf16[256,512]{1,0:T(8,128)(2,...) custom-call(bf16[128,512]{1,0:T(8,128)(2,1)S(1)} %copy-done.1, ...), custom_call_target="tpu_custom_call" | custom-call | flops 2000000000 | bytes 4194304 | tf_op jit(solution)/shard_map/pallas_call | solution.py:595
  31.1 0.2 collective-permute-done.5.refs_2_
  31.3 0.0 collective-permute-done.6.refs_3_
  31.3 1.7 %shard_map.124 = (f32[256,512]{1,0:T(8,128)S(1)}, bf16[64,1024]{1,0:T(8,128)(2,1)S(1)}, bf16[64,1024]{1,0:T(8,128)(2,1)S(1)}) custom-call(bf16[1,64,512]{2,1,0:T(8,128)(2,1)S(1)} %copy-done.2, bf16[1,64,512]{2,1,0:T(8,128)(2,1)S(1)} %collective-permute-done.4.refs_1_, bf16[1,64,512]{2,1,0:T(8,128)(2,1)S(1)} %collective-permute-done.5.refs_2_, ...), custom_call_target="tpu_custom_call" | custom-call | flops 1000000000 | bytes 4194304 | tf_op jit(solution)/shard_map/pallas_call | solution.py:595
  33.0 0.1 collective-permute-start.7
  33.1 0.7 %shard_map.125 = (bf16[256,512]{1,0:T(8,128)(2,1)S(1)}, bf16[224,512]{1,0:T(8,128)(2,1)S(1)}) custom-call(s32[64,512]{1,0:T(8,128)S(1)} %get-tuple-element.43.refs_7_.index_ref, bf16[1024,512]{1,0:T(8,128)(2,1)S(1)} %get-tuple-element.44.slope_ref, f32[256,512]{1,0:T(8,128)S(1)} %get-tuple-element.45.normed_ref, ...), custom_call_target="tpu_custom_call" | custom-call | flops 1000000000 | bytes 4194304 | tf_op jit(solution)/shard_map/pallas_call | solution.py:595
  33.9 0.6 %collective-permute-done.7 = bf16[64,1024]{1,0:T(8,128)(2,1)S(1)} collective-permute-done((bf16[64,1024]{1,0:T(8,128)(2,1)S(1)}, bf16[64,1024]{1,0:T(8,128)(2,1)S(1)}, u32[]{:S(2)}, u32[]{:S(2)}) %collective-permute-start.7) | collective-permute-done | bytes 131104 | tf_op jit(solution)/shard_map/ppermute | solution.py:608
  34.5 0.0 copy-start.3
  34.5 0.8 %shard_map.126 = (bf16[48,512]{1,0:T(8,128)(2,1)S(1)}, bf16[64,1024]{1,0:T(8,128)(2,1)S(1)}, bf16[64,1024]{1,0:T(8,128)(2,1)S(1)}) custom-call(bf16[192,512]{1,0:T(8,128)(2,1)S(1)} %get-tuple-element.41.grid_ref, bf16[256,512]{1,0:T(8,128)(2,1)S(1)} %get-tuple-element.42.mesh_ref, s32[64,512]{1,0:T(8,128)S(1)} %get-tuple-element.43.refs_7_.index_ref, ...), custom_call_target="tpu_custom_call" | custom-call | flops 1000000000 | bytes 4194304 | tf_op jit(solution)/shard_map/pallas_call | solution.py:595
  35.3 0.2 collective-permute-start.8
  35.6 1.5 %collective-permute-start.11 = (bf16[64,1024]{1,0:T(8,128)(2,1)S(1)}, bf16[64,1024]{1,0:T(8,128)(2,1)S(1)}, u32[]{:S(2)}, u32[]{:S(2)}) collective-permute-start(bf16[64,1024]{1,0:T(8,128)(2,1)S(1)} %add_convert_fusion.3), channel_id=1, source_target_pairs={{0,2},{1,3},{2,0},{3,1},{4,6},{5,7},{6,4},{7,5},{8,10},{9,11},{10,... | collective-permute-start | bytes 393224 | tf_op jit(solution)/shard_map/ppermute | solution.py:608
  37.1 1.2 %collective-permute-start.9 = (bf16[64,1024]{1,0:T(8,128)(2,1)S(1)}, bf16[64,1024]{1,0:T(8,128)(2,1)S(1)}, u32[]{:S(2)}, u32[]{:S(2)}) collective-permute-start(bf16[64,1024]{1,0:T(8,128)(2,1)S(1)} %add_convert_fusion.2), channel_id=1, source_target_pairs={{0,2},{1,3},{2,0},{3,1},{4,6},{5,7},{6,4},{7,5},{8,10},{9,11},{10,... | collective-permute-start | bytes 393224 | tf_op jit(solution)/shard_map/ppermute | solution.py:608
  38.3 3.5 %collective-permute-done.11 = bf16[64,1024]{1,0:T(8,128)(2,1)S(1)} collective-permute-done((bf16[64,1024]{1,0:T(8,128)(2,1)S(1)}, bf16[64,1024]{1,0:T(8,128)(2,1)S(1)}, u32[]{:S(2)}, u32[]{:S(2)}) %collective-permute-start.11) | collective-permute-done | bytes 131104 | tf_op jit(solution)/shard_map/ppermute | solution.py:608
  41.9 0.1 collective-permute-start.12
  42.0 2.1 %collective-permute-done.9 = bf16[64,1024]{1,0:T(8,128)(2,1)S(1)} collective-permute-done((bf16[64,1024]{1,0:T(8,128)(2,1)S(1)}, bf16[64,1024]{1,0:T(8,128)(2,1)S(1)}, u32[]{:S(2)}, u32[]{:S(2)}) %collective-permute-start.9) | collective-permute-done | bytes 131104 | tf_op jit(solution)/shard_map/ppermute | solution.py:608
  44.2 0.1 collective-permute-start.10
  44.3 1.1 %shard_map.127 = bf16[1,128,512]{2,1,0:T(8,128)(2,1)} custom-call(bf16[512,1536]{1,0:T(8,128)(2,1)S(1)} %get-tuple-element.40.refs_4_.turned_ref, s32[3,1,16]{2,1,0:T(1,128)S(1)} %bitcast.6, bf16[48,512]{1,0:T(8,128)(2,1)S(1)} %get-tuple-element.59.own_slot_ref), custom_call_target="tpu_custom_call" | custom-call | flops 100000000 | bytes 4194304 | tf_op jit(solution)/shard_map/pallas_call | solution.py:595
  45.3 0.2 collective-permute-done.10.other_one_ref
  45.6 1.0 %shard_map.128 = f32[128,2048]{1,0:T(8,128)} custom-call(bf16[64,1024]{1,0:T(8,128)(2,1)S(1)} %add_convert_fusion.1.one_ref, bf16[64,1024]{1,0:T(8,128)(2,1)S(1)} %collective-permute-done.10.other_one_ref, bf16[64,1024]{1,0:T(8,128)(2,1)S(1)} %add_convert_fusion.two_ref, bf16[64,1024]{1,0:T(8,128)(2,1)S(1)} %collective-permute-done.12.other_two_ref), custom_call_target="tpu_custom_call" | custom-call | flops 1000000 | bytes 4194304 | tf_op jit(solution)/shard_map/pallas_call | solution.py:595
  (14 shorter events, 0.2 us)
Async XLA Ops:
  0.6 23.3 %copy-start.2 = (bf16[1,64,512]{2,1,0:T(8,128)(2,1)S(1)}, bf16[1,64,512]{2,1,0:T(8,128)(2,1)}, u32[]{:S(2)}) copy-start(bf16[1,64,512]{2,1,0:T(8,128)(2,1)} %refs_0_.2) | copy-start | bytes 196612
  2.6 10.7 %collective-permute-start.1 = (bf16[128,512]{1,0:T(8,128)(2,1)}, bf16[128,512]{1,0:T(8,128)(2,1)S(1)}, u32[]{:S(2)}, u32[]{:S(2)}) collective-permute-start(bf16[128,512]{1,0:T(8,128)(2,1)} %shard_map.121.refs_0_), channel_id=1, source_target_pairs={{0,8},{4,12},{8,0},{12,4},{1,9},{5,13},{9,1},{13,5},{2,10},{6,14},... | collective-permute-start | bytes 393224 | tf_op jit(solution)/shard_map/ppermute | solution.py:608
  6.7 17.4 %collective-permute-start = (bf16[128,512]{1,0:T(8,128)(2,1)}, bf16[128,512]{1,0:T(8,128)(2,1)S(1)}, u32[]{:S(2)}, u32[]{:S(2)}) collective-permute-start(bf16[128,512]{1,0:T(8,128)(2,1)} %shard_map.121.refs_0_), channel_id=1, source_target_pairs={{0,4},{4,0},{8,12},{12,8},{1,5},{5,1},{9,13},{13,9},{2,6},{6,2},{1... | collective-permute-start | bytes 393224 | tf_op jit(solution)/shard_map/ppermute | solution.py:608
  13.3 13.1 %collective-permute-start.3 = (bf16[128,512]{1,0:T(8,128)(2,1)S(1)}, bf16[128,512]{1,0:T(8,128)(2,1)S(1)}, u32[]{:S(2)}, u32[]{:S(2)}) collective-permute-start(bf16[128,512]{1,0:T(8,128)(2,1)S(1)} %collective-permute-done.1.refs_2_), channel_id=1, source_target_pairs={{4,0},{8,12},{5,1},{9,13},{6,2},{10,14},{7,3},{11,15},{20,16},{24,... | collective-permute-start | bytes 393224 | tf_op jit(solution)/shard_map/ppermute | solution.py:678
  14.6 11.8 %collective-permute-start.2 = (bf16[128,512]{1,0:T(8,128)(2,1)}, bf16[128,512]{1,0:T(8,128)(2,1)S(1)}, u32[]{:S(2)}, u32[]{:S(2)}) collective-permute-start(bf16[128,512]{1,0:T(8,128)(2,1)} %shard_map.121.refs_0_), channel_id=1, source_target_pairs={{4,8},{8,4},{5,9},{9,5},{6,10},{10,6},{7,11},{11,7},{20,24},{24,20... | collective-permute-start | bytes 393224 | tf_op jit(solution)/shard_map/ppermute | solution.py:677
  15.2 15.9 %collective-permute-start.4 = (bf16[1,64,512]{2,1,0:T(8,128)(2,1)}, bf16[1,64,512]{2,1,0:T(8,128)(2,1)S(1)}, u32[]{:S(2)}, u32[]{:S(2)}) collective-permute-start(bf16[1,64,512]{2,1,0:T(8,128)(2,1)} %refs_0_.2), channel_id=1, source_target_pairs={{0,4},{4,0},{8,12},{12,8},{1,5},{5,1},{9,13},{13,9},{2,6},{6,2},{1... | collective-permute-start | bytes 196616 | tf_op jit(solution)/shard_map/ppermute | solution.py:608
  21.7 1.6 %copy-start = (bf16[512,2048]{1,0:T(8,128)(2,1)S(1)}, bf16[512,2048]{1,0:T(8,128)(2,1)}, u32[]{:S(2)}) copy-start(bf16[512,2048]{1,0:T(8,128)(2,1)} %source_ref) | copy-start | bytes 6291460
  23.3 3.1 %copy-start.1 = (bf16[128,512]{1,0:T(8,128)(2,1)S(1)}, bf16[128,512]{1,0:T(8,128)(2,1)}, u32[]{:S(2)}) copy-start(bf16[128,512]{1,0:T(8,128)(2,1)} %shard_map.121.refs_0_) | copy-start | bytes 393220
  23.9 7.4 %collective-permute-start.5 = (bf16[1,64,512]{2,1,0:T(8,128)(2,1)S(1)}, bf16[1,64,512]{2,1,0:T(8,128)(2,1)S(1)}, u32[]{:S(2)}, u32[]{:S(2)}) collective-permute-start(bf16[1,64,512]{2,1,0:T(8,128)(2,1)S(1)} %copy-done.2), channel_id=1, source_target_pairs={{0,8},{4,12},{8,0},{12,4},{1,9},{5,13},{9,1},{13,5},{2,10},{6,14},... | collective-permute-start | bytes 196616 | tf_op jit(solution)/shard_map/ppermute | solution.py:608
  24.0 7.3 %collective-permute-start.6 = (bf16[1,64,512]{2,1,0:T(8,128)(2,1)S(1)}, bf16[1,64,512]{2,1,0:T(8,128)(2,1)S(1)}, u32[]{:S(2)}, u32[]{:S(2)}) collective-permute-start(bf16[1,64,512]{2,1,0:T(8,128)(2,1)S(1)} %copy-done.2), channel_id=1, source_target_pairs={{0,12},{4,8},{8,4},{12,0},{1,13},{5,9},{9,5},{13,1},{2,14},{6,10},... | collective-permute-start | bytes 196616 | tf_op jit(solution)/shard_map/ppermute | solution.py:608
  33.0 1.4 %collective-permute-start.7 = (bf16[64,1024]{1,0:T(8,128)(2,1)S(1)}, bf16[64,1024]{1,0:T(8,128)(2,1)S(1)}, u32[]{:S(2)}, u32[]{:S(2)}) collective-permute-start(bf16[64,1024]{1,0:T(8,128)(2,1)S(1)} %get-tuple-element.56), channel_id=1, source_target_pairs={{0,1},{1,0},{2,3},{3,2},{4,5},{5,4},{6,7},{7,6},{8,9},{9,8},{10,11... | collective-permute-start | bytes 393224 | tf_op jit(solution)/shard_map/ppermute | solution.py:608
  34.5 9.8 %copy-start.3 = (s32[1,3,16]{2,0,1:T(1,128)S(1)}, s32[1,3,16]{2,0,1:T(1,128)}, u32[]{:S(2)}) copy-start(s32[1,3,16]{2,0,1:T(1,128)} %param.14) | copy-start | bytes 580
  35.3 1.7 %collective-permute-start.8 = (bf16[64,1024]{1,0:T(8,128)(2,1)S(1)}, bf16[64,1024]{1,0:T(8,128)(2,1)S(1)}, u32[]{:S(2)}, u32[]{:S(2)}) collective-permute-start(bf16[64,1024]{1,0:T(8,128)(2,1)S(1)} %get-tuple-element.61), channel_id=1, source_target_pairs={{0,1},{1,0},{2,3},{3,2},{4,5},{5,4},{6,7},{7,6},{8,9},{9,8},{10,11... | collective-permute-start | bytes 393224 | tf_op jit(solution)/shard_map/ppermute | solution.py:608
  35.6 6.3 %collective-permute-start.11 = (bf16[64,1024]{1,0:T(8,128)(2,1)S(1)}, bf16[64,1024]{1,0:T(8,128)(2,1)S(1)}, u32[]{:S(2)}, u32[]{:S(2)}) collective-permute-start(bf16[64,1024]{1,0:T(8,128)(2,1)S(1)} %add_convert_fusion.3), channel_id=1, source_target_pairs={{0,2},{1,3},{2,0},{3,1},{4,6},{5,7},{6,4},{7,5},{8,10},{9,11},{10,... | collective-permute-start | bytes 393224 | tf_op jit(solution)/shard_map/ppermute | solution.py:608
  37.1 7.0 %collective-permute-start.9 = (bf16[64,1024]{1,0:T(8,128)(2,1)S(1)}, bf16[64,1024]{1,0:T(8,128)(2,1)S(1)}, u32[]{:S(2)}, u32[]{:S(2)}) collective-permute-start(bf16[64,1024]{1,0:T(8,128)(2,1)S(1)} %add_convert_fusion.2), channel_id=1, source_target_pairs={{0,2},{1,3},{2,0},{3,1},{4,6},{5,7},{6,4},{7,5},{8,10},{9,11},{10,... | collective-permute-start | bytes 393224 | tf_op jit(solution)/shard_map/ppermute | solution.py:608
  41.9 3.4 %collective-permute-start.12 = (bf16[64,1024]{1,0:T(8,128)(2,1)S(1)}, bf16[64,1024]{1,0:T(8,128)(2,1)S(1)}, u32[]{:S(2)}, u32[]{:S(2)}) collective-permute-start(bf16[64,1024]{1,0:T(8,128)(2,1)S(1)} %add_convert_fusion.two_ref), channel_id=1, source_target_pairs={{0,1},{1,0},{2,3},{3,2},{4,5},{5,4},{6,7},{7,6},{8,9},{9,8},{10,11... | collective-permute-start | bytes 393224 | tf_op jit(solution)/shard_map/ppermute | solution.py:608
  44.2 1.4 %collective-permute-start.10 = (bf16[64,1024]{1,0:T(8,128)(2,1)S(1)}, bf16[64,1024]{1,0:T(8,128)(2,1)S(1)}, u32[]{:S(2)}, u32[]{:S(2)}) collective-permute-start(bf16[64,1024]{1,0:T(8,128)(2,1)S(1)} %add_convert_fusion.1.one_ref), channel_id=1, source_target_pairs={{0,1},{1,0},{2,3},{3,2},{4,5},{5,4},{6,7},{7,6},{8,9},{9,8},{10,11... | collective-permute-start | bytes 393224 | tf_op jit(solution)/shard_map/ppermute | solution.py:608

commit v5 on v2

--- a/solution.py
+++ b/solution.py
@@ -299,12 +299,13 @@
 
 
 def forward_kernel(
-    regions,
+    steps,
     listed,
     mesh_count,
     mesh_cap,
     *refs,
 ):
+    regions = len(steps)
     packed_refs = refs[:regions]
     (
         weights_ref,
@@ -327,8 +328,8 @@
     capacity = listed // 3
     slots = regions * mesh_cap
     me = lax.axis_index("space")
-    for back, packed_ref in enumerate(packed_refs):
-        region = lax.bitwise_xor(me, back)
+    for step, packed_ref in zip(steps, packed_refs):
+        region = lax.bitwise_xor(me, step)
         at = lambda rows: pl.ds(pl.multiple_of(region * rows, rows), rows)
         grid_ref[at(listed), :] = packed_ref[:listed, :]
         mesh_ref[at(mesh_count), :] = packed_ref[listed : listed + mesh_count, :]
@@ -415,7 +416,8 @@
     give_ref[...] = share_ref[pl.ds(pl.multiple_of((1 - core) * half, half), half), :]
 
 
-def process_back_kernel(regions, mesh_cap, *refs):
+def process_back_kernel(steps, mesh_cap, *refs):
+    regions = len(steps)
     cotangent_refs = refs[:regions]
     (
         turned_ref,
@@ -438,8 +440,8 @@
     edges = slope_ref.shape[0] // regions
     slots = regions * mesh_cap
     me = lax.axis_index("space")
-    for back, cotangent_ref in enumerate(cotangent_refs):
-        region = lax.bitwise_xor(me, back)
+    for step, cotangent_ref in zip(steps, cotangent_refs):
+        region = lax.bitwise_xor(me, step)
         at = pl.ds(pl.multiple_of(region * mesh_count, mesh_count), mesh_count)
         upstream_ref[at, :] = cotangent_ref[0].astype(F32)
     agg_grad = moments_back(normed_ref[...], scaled_ref[:, 0:1], upstream_ref[...]).astype(BF16)
@@ -622,9 +624,9 @@
         megabytes=56,
     )[0]
     packed, cotangent, weights = lax.optimization_barrier((packed, mesh_cotangent, weights))
-    steps = sorted(range(1, regions), key=lambda step: -step)
-    packs = {step: swap(packed, "space", step) for step in steps}
-    cotangents = {1: swap(cotangent, "space", 1)}
+    steps = (0, *range(2, regions), 1)
+    packs = [packed] + [swap(packed, "space", step) for step in steps[1:]]
+    near = swap(cotangent, "space", 1)
     weights, turned = call(
         weights_kernel,
         (weights,),
@@ -633,13 +635,8 @@
         10**8,
         fetched=1,
     )
-    *packs, cotangent = lax.optimization_barrier(
-        [packed] + [packs[step] for step in range(1, regions)] + [cotangent]
-    )
-    for step in steps:
-        if step > 1:
-            cotangents[step] = swap(cotangent, "space", step)
-    cotangents = [cotangent] + [cotangents[step] for step in range(1, regions)]
+    turned, cotangent = lax.optimization_barrier((turned, cotangent))
+    cotangents = [cotangent] + [swap(cotangent, "space", step) for step in steps[1:-1]] + [near]
     rows = regions * mesh_count
     (
         mesh_out,
@@ -655,7 +652,7 @@
         normed_two,
         scaled_two,
     ) = call(
-        functools.partial(forward_kernel, regions, listed, mesh_count, mesh_cap),
+        functools.partial(forward_kernel, steps, listed, mesh_count, mesh_cap),
         (*packs, weights),
         [
             (mesh_latent.shape, BF16),
@@ -675,7 +672,7 @@
         2 * 10**9,
     )
     mesh_grad, keep_two, give_two = call(
-        functools.partial(process_back_kernel, regions, mesh_cap),
+        functools.partial(process_back_kernel, steps, mesh_cap),
         (
             *cotangents,
             turned,

time: 42.8 us -> 40.2 us (0.939)
  the two profiles are of different devices: /device:TPU:0 before, /device:TPU:13 now
where the time goes in v5:
time: 40.2 us; the launch traced here: 40 us
  starting transfers between devices  12.9 us (32%)
  Pallas kernels  12.4 us (31%)
  waiting for transfers between devices  12.3 us (31%)
  local copies, waits for them, and re-layouts  1.6 us (4%)
  between operations  0.71 us (2%)
    ppermute x12, starting transfers between devices, swap(): lax.ppermute(block, axis, [(i, i ^ bits) for i in range(lax.axis_size(axi...  12.9 us
    pallas_call x7, Pallas kernels, call(): pl.pallas_call(kernel, out_shape=[jax.ShapeDtypeStruct(shape, kind) for s...  12.4 us
    ppermute x12, waiting for transfers between devices, swap(): lax.ppermute(block, axis, [(i, i ^ bits) for i in range(lax.axis_size(axi...  12.3 us
    unnamed x8, local copies, waits for them, and re-layouts  1.6 us
  transfers between devices with their start and end apart: 12, of which 4 were waited for; matrix products, arithmetic and copies ran while one was open for 0% of the time, Pallas kernels for 19%

profile of v5, /device:TPU:13, one launch (start us, length us, event | category | flops | bytes accessed | tf_op | source)
XLA Modules:
  0.0 40.0 jit_solution(3900221166568798079)
XLA Ops:
  0.6 1.9 %shard_map.121.refs_0_ = bf16[128,512]{1,0:T(8,128)(2,1)} custom-call(bf16[1,128,512]{2,1,0:T(8,128)(2,1)} %refs_0_.1, bf16[1,64,512]{2,1,0:T(8,128)(2,1)} %refs_1_.1, s32[3,1,16]{2,1,0:T(1,128)} %bitcast.5, s32[1,256]{1,0:T(1,128)} %bitcast.7, s32[1,256]{1,0:T(1,128)} %bitcast.8, s32[1,4,8]{2,1,0:T(4,128)} %refs_5_.1, s32[1,256]{1,0:T(1,128)} %bitcast.9, ...), custom_call_target="tpu_custom_call" | custom-call | flops 10000000 | bytes 4194304 | tf_op jit(solution)/shard_map/pallas_call | solution.py:557
  2.5 2.4 %collective-permute-start = (bf16[128,512]{1,0:T(8,128)(2,1)}, bf16[128,512]{1,0:T(8,128)(2,1)S(1)}, u32[]{:S(2)}, u32[]{:S(2)}) collective-permute-start(bf16[128,512]{1,0:T(8,128)(2,1)} %shard_map.121.refs_0_), channel_id=1, source_target_pairs={{0,8},{4,12},{8,0},{12,4},{1,9},{5,13},{9,1},{13,5},{2,10},{6,14},... | collective-permute-start | bytes 393224 | tf_op jit(solution)/shard_map/ppermute | solution.py:570
  4.9 0.0 collective-permute-start.1
  4.9 1.3 %collective-permute-start.2 = (bf16[128,512]{1,0:T(8,128)(2,1)}, bf16[128,512]{1,0:T(8,128)(2,1)S(1)}, u32[]{:S(2)}, u32[]{:S(2)}) collective-permute-start(bf16[128,512]{1,0:T(8,128)(2,1)} %shard_map.121.refs_0_), channel_id=1, source_target_pairs={{0,4},{4,0},{8,12},{12,8},{1,5},{5,1},{9,13},{13,9},{2,6},{6,2},{1... | collective-permute-start | bytes 393224 | tf_op jit(solution)/shard_map/ppermute | solution.py:570
  6.2 1.6 %copy-done = bf16[512,2048]{1,0:T(8,128)(2,1)S(1)} copy-done((bf16[512,2048]{1,0:T(8,128)(2,1)S(1)}, bf16[512,2048]{1,0:T(8,128)(2,1)}, u32[]{:S(2)}) %copy-start) | copy-done | bytes 2097176
  7.8 0.6 %shard_map.122 = (bf16[512,2048]{1,0:T(8,128)(2,1)S(1)}, bf16[512,1536]{1,0:T(8,128)(2,1)S(1)}) custom-call(bf16[512,2048]{1,0:T(8,128)(2,1)S(1)} %copy-done), custom_call_target="tpu_custom_call" | custom-call | flops 100000000 | bytes 4194304 | tf_op jit(solution)/shard_map/pallas_call | solution.py:557
  8.4 1.5 %collective-permute-start.3 = (bf16[1,64,512]{2,1,0:T(8,128)(2,1)S(1)}, bf16[1,64,512]{2,1,0:T(8,128)(2,1)S(1)}, u32[]{:S(2)}, u32[]{:S(2)}) collective-permute-start(bf16[1,64,512]{2,1,0:T(8,128)(2,1)S(1)} %copy-done.2), channel_id=1, source_target_pairs={{0,8},{4,12},{8,0},{12,4},{1,9},{5,13},{9,1},{13,5},{2,10},{6,14},... | collective-permute-start | bytes 196616 | tf_op jit(solution)/shard_map/ppermute | solution.py:570
  9.9 0.0 collective-permute-start.4
  9.9 4.7 %collective-permute-done.refs_1_ = bf16[128,512]{1,0:T(8,128)(2,1)S(1)} collective-permute-done((bf16[128,512]{1,0:T(8,128)(2,1)}, bf16[128,512]{1,0:T(8,128)(2,1)S(1)}, u32[]{:S(2)}, u32[]{:S(2)}) %collective-permute-start) | collective-permute-done | bytes 131104 | tf_op jit(solution)/shard_map/ppermute | solution.py:570
  14.6 0.0 collective-permute-start.5
  14.6 5.1 %collective-permute-done.1.refs_2_ = bf16[128,512]{1,0:T(8,128)(2,1)S(1)} collective-permute-done((bf16[128,512]{1,0:T(8,128)(2,1)}, bf16[128,512]{1,0:T(8,128)(2,1)S(1)}, u32[]{:S(2)}, u32[]{:S(2)}) %collective-permute-start.1) | collective-permute-done | bytes 131104 | tf_op jit(solution)/shard_map/ppermute | solution.py:570
  19.6 0.0 collective-permute-done.2.refs_3_
  19.6 4.6 %shard_map.123 = (bf16[1,64,512]{2,1,0:T(8,128)(2,1)}, bf16[192,512]{1,0:T(8,128)(2,1)S(1)}, bf16[256,512]{1,0:T(8,128)(2,1)S(1)}, bf16[256,512]{1,0:T(8,128)(2,...) custom-call(bf16[128,512]{1,0:T(8,128)(2,1)S(1)} %copy-done.1, ...), custom_call_target="tpu_custom_call" | custom-call | flops 2000000000 | bytes 4194304 | tf_op jit(solution)/shard_map/pallas_call | solution.py:557
  24.3 0.0 collective-permute-done.3.refs_1_
  24.3 0.0 collective-permute-done.4.refs_2_
  24.3 0.0 collective-permute-done.5.refs_3_
  24.3 1.7 %shard_map.124 = (f32[256,512]{1,0:T(8,128)S(1)}, bf16[64,1024]{1,0:T(8,128)(2,1)S(1)}, bf16[64,1024]{1,0:T(8,128)(2,1)S(1)}) custom-call(bf16[1,64,512]{2,1,0:T(8,128)(2,1)S(1)} %copy-done.2, bf16[1,64,512]{2,1,0:T(8,128)(2,1)S(1)} %collective-permute-done.3.refs_1_, bf16[1,64,512]{2,1,0:T(8,128)(2,1)S(1)} %collective-permute-done.4.refs_2_, ...), custom_call_target="tpu_custom_call" | custom-call | flops 1000000000 | bytes 4194304 | tf_op jit(solution)/shard_map/pallas_call | solution.py:557
  26.0 1.5 %collective-permute-start.9 = (bf16[64,1024]{1,0:T(8,128)(2,1)S(1)}, bf16[64,1024]{1,0:T(8,128)(2,1)S(1)}, u32[]{:S(2)}, u32[]{:S(2)}) collective-permute-start(bf16[64,1024]{1,0:T(8,128)(2,1)S(1)} %get-tuple-element.52), channel_id=1, source_target_pairs={{0,1},{1,0},{2,3},{3,2},{4,5},{5,4},{6,7},{7,6},{8,9},{9,8},{10,11... | collective-permute-start | bytes 393224 | tf_op jit(solution)/shard_map/ppermute | solution.py:570
  27.5 1.4 %shard_map.125 = (bf16[48,512]{1,0:T(8,128)(2,1)S(1)}, bf16[64,1024]{1,0:T(8,128)(2,1)S(1)}, bf16[64,1024]{1,0:T(8,128)(2,1)S(1)}) custom-call(bf16[192,512]{1,0:T(8,128)(2,1)S(1)} %get-tuple-element.35.grid_ref, bf16[256,512]{1,0:T(8,128)(2,1)S(1)} %get-tuple-element.36.mesh_ref, s32[64,512]{1,0:T(8,128)S(1)} %get-tuple-element.37.refs_7_.index_ref, ...), custom_call_target="tpu_custom_call" | custom-call | flops 1000000000 | bytes 4194304 | tf_op jit(solution)/shard_map/pallas_call | solution.py:557
  28.9 0.1 collective-permute-start.6
  29.0 0.0 collective-permute-done.9
  29.0 1.3 %collective-permute-start.10 = (bf16[64,1024]{1,0:T(8,128)(2,1)S(1)}, bf16[64,1024]{1,0:T(8,128)(2,1)S(1)}, u32[]{:S(2)}, u32[]{:S(2)}) collective-permute-start(bf16[64,1024]{1,0:T(8,128)(2,1)S(1)} %add_convert_fusion.1), channel_id=1, source_target_pairs={{0,2},{1,3},{2,0},{3,1},{4,6},{5,7},{6,4},{7,5},{8,10},{9,11},{10,... | collective-permute-start | bytes 393224 | tf_op jit(solution)/shard_map/ppermute | solution.py:570
  30.3 0.0 collective-permute-done.6
  30.3 1.3 %collective-permute-start.7 = (bf16[64,1024]{1,0:T(8,128)(2,1)S(1)}, bf16[64,1024]{1,0:T(8,128)(2,1)S(1)}, u32[]{:S(2)}, u32[]{:S(2)}) collective-permute-start(bf16[64,1024]{1,0:T(8,128)(2,1)S(1)} %add_convert_fusion.3), channel_id=1, source_target_pairs={{0,2},{1,3},{2,0},{3,1},{4,6},{5,7},{6,4},{7,5},{8,10},{9,11},{10,... | collective-permute-start | bytes 393224 | tf_op jit(solution)/shard_map/ppermute | solution.py:570
  31.6 2.1 %collective-permute-done.10 = bf16[64,1024]{1,0:T(8,128)(2,1)S(1)} collective-permute-done((bf16[64,1024]{1,0:T(8,128)(2,1)S(1)}, bf16[64,1024]{1,0:T(8,128)(2,1)S(1)}, u32[]{:S(2)}, u32[]{:S(2)}) %collective-permute-start.10) | collective-permute-done | bytes 131104 | tf_op jit(solution)/shard_map/ppermute | solution.py:570
  33.7 2.3 %collective-permute-start.11 = (bf16[64,1024]{1,0:T(8,128)(2,1)S(1)}, bf16[64,1024]{1,0:T(8,128)(2,1)S(1)}, u32[]{:S(2)}, u32[]{:S(2)}) collective-permute-start(bf16[64,1024]{1,0:T(8,128)(2,1)S(1)} %add_convert_fusion.two_ref), channel_id=1, source_target_pairs={{0,1},{1,0},{2,3},{3,2},{4,5},{5,4},{6,7},{7,6},{8,9},{9,8},{10,11... | collective-permute-start | bytes 393224 | tf_op jit(solution)/shard_map/ppermute | solution.py:570
  36.0 0.4 %collective-permute-done.7 = bf16[64,1024]{1,0:T(8,128)(2,1)S(1)} collective-permute-done((bf16[64,1024]{1,0:T(8,128)(2,1)S(1)}, bf16[64,1024]{1,0:T(8,128)(2,1)S(1)}, u32[]{:S(2)}, u32[]{:S(2)}) %collective-permute-start.7) | collective-permute-done | bytes 131104 | tf_op jit(solution)/shard_map/ppermute | solution.py:570
  36.5 1.4 %collective-permute-start.8 = (bf16[64,1024]{1,0:T(8,128)(2,1)S(1)}, bf16[64,1024]{1,0:T(8,128)(2,1)S(1)}, u32[]{:S(2)}, u32[]{:S(2)}) collective-permute-start(bf16[64,1024]{1,0:T(8,128)(2,1)S(1)} %add_convert_fusion.2.one_ref), channel_id=1, source_target_pairs={{0,1},{1,0},{2,3},{3,2},{4,5},{5,4},{6,7},{7,6},{8,9},{9,8},{10,11... | collective-permute-start | bytes 393224 | tf_op jit(solution)/shard_map/ppermute | solution.py:570
  37.9 1.1 %shard_map.126 = bf16[1,128,512]{2,1,0:T(8,128)(2,1)} custom-call(bf16[512,1536]{1,0:T(8,128)(2,1)S(1)} %get-tuple-element.34.refs_4_.turned_ref, s32[3,1,16]{2,1,0:T(1,128)S(1)} %bitcast.6, bf16[48,512]{1,0:T(8,128)(2,1)S(1)} %get-tuple-element.48.own_slot_ref), custom_call_target="tpu_custom_call" | custom-call | flops 100000000 | bytes 4194304 | tf_op jit(solution)/shard_map/pallas_call | solution.py:557
  39.0 0.0 collective-permute-done.11.other_two_ref
  39.0 0.0 collective-permute-done.8.other_one_ref
  39.0 1.0 %shard_map.127 = f32[128,2048]{1,0:T(8,128)} custom-call(bf16[64,1024]{1,0:T(8,128)(2,1)S(1)} %add_convert_fusion.2.one_ref, bf16[64,1024]{1,0:T(8,128)(2,1)S(1)} %collective-permute-done.8.other_one_ref, bf16[64,1024]{1,0:T(8,128)(2,1)S(1)} %add_convert_fusion.two_ref, bf16[64,1024]{1,0:T(8,128)(2,1)S(1)} %collective-permute-done.11.other_two_ref), custom_call_target="tpu_custom_call" | custom-call | flops 1000000 | bytes 4194304 | tf_op jit(solution)/shard_map/pallas_call | solution.py:557
  (11 shorter events, 0.2 us)
Async XLA Ops:
  0.6 7.8 %copy-start.2 = (bf16[1,64,512]{2,1,0:T(8,128)(2,1)S(1)}, bf16[1,64,512]{2,1,0:T(8,128)(2,1)}, u32[]{:S(2)}) copy-start(bf16[1,64,512]{2,1,0:T(8,128)(2,1)} %refs_0_.2) | copy-start | bytes 196612
  2.5 12.0 %collective-permute-start = (bf16[128,512]{1,0:T(8,128)(2,1)}, bf16[128,512]{1,0:T(8,128)(2,1)S(1)}, u32[]{:S(2)}, u32[]{:S(2)}) collective-permute-start(bf16[128,512]{1,0:T(8,128)(2,1)} %shard_map.121.refs_0_), channel_id=1, source_target_pairs={{0,8},{4,12},{8,0},{12,4},{1,9},{5,13},{9,1},{13,5},{2,10},{6,14},... | collective-permute-start | bytes 393224 | tf_op jit(solution)/shard_map/ppermute | solution.py:570
  4.9 14.7 %collective-permute-start.1 = (bf16[128,512]{1,0:T(8,128)(2,1)}, bf16[128,512]{1,0:T(8,128)(2,1)S(1)}, u32[]{:S(2)}, u32[]{:S(2)}) collective-permute-start(bf16[128,512]{1,0:T(8,128)(2,1)} %shard_map.121.refs_0_), channel_id=1, source_target_pairs={{0,12},{4,8},{8,4},{12,0},{1,13},{5,9},{9,5},{13,1},{2,14},{6,10},... | collective-permute-start | bytes 393224 | tf_op jit(solution)/shard_map/ppermute | solution.py:570
  4.9 14.7 %collective-permute-start.2 = (bf16[128,512]{1,0:T(8,128)(2,1)}, bf16[128,512]{1,0:T(8,128)(2,1)S(1)}, u32[]{:S(2)}, u32[]{:S(2)}) collective-permute-start(bf16[128,512]{1,0:T(8,128)(2,1)} %shard_map.121.refs_0_), channel_id=1, source_target_pairs={{0,4},{4,0},{8,12},{12,8},{1,5},{5,1},{9,13},{13,9},{2,6},{6,2},{1... | collective-permute-start | bytes 393224 | tf_op jit(solution)/shard_map/ppermute | solution.py:570
  6.2 1.6 %copy-start = (bf16[512,2048]{1,0:T(8,128)(2,1)S(1)}, bf16[512,2048]{1,0:T(8,128)(2,1)}, u32[]{:S(2)}) copy-start(bf16[512,2048]{1,0:T(8,128)(2,1)} %source_ref) | copy-start | bytes 6291460
  7.8 11.9 %copy-start.1 = (bf16[128,512]{1,0:T(8,128)(2,1)S(1)}, bf16[128,512]{1,0:T(8,128)(2,1)}, u32[]{:S(2)}) copy-start(bf16[128,512]{1,0:T(8,128)(2,1)} %shard_map.121.refs_0_) | copy-start | bytes 393220
  8.4 15.9 %collective-permute-start.3 = (bf16[1,64,512]{2,1,0:T(8,128)(2,1)S(1)}, bf16[1,64,512]{2,1,0:T(8,128)(2,1)S(1)}, u32[]{:S(2)}, u32[]{:S(2)}) collective-permute-start(bf16[1,64,512]{2,1,0:T(8,128)(2,1)S(1)} %copy-done.2), channel_id=1, source_target_pairs={{0,8},{4,12},{8,0},{12,4},{1,9},{5,13},{9,1},{13,5},{2,10},{6,14},... | collective-permute-start | bytes 196616 | tf_op jit(solution)/shard_map/ppermute | solution.py:570
  9.9 14.4 %collective-permute-start.4 = (bf16[1,64,512]{2,1,0:T(8,128)(2,1)S(1)}, bf16[1,64,512]{2,1,0:T(8,128)(2,1)S(1)}, u32[]{:S(2)}, u32[]{:S(2)}) collective-permute-start(bf16[1,64,512]{2,1,0:T(8,128)(2,1)S(1)} %copy-done.2), channel_id=1, source_target_pairs={{0,12},{4,8},{8,4},{12,0},{1,13},{5,9},{9,5},{13,1},{2,14},{6,10},... | collective-permute-start | bytes 196616 | tf_op jit(solution)/shard_map/ppermute | solution.py:570
  14.6 9.7 %collective-permute-start.5 = (bf16[1,64,512]{2,1,0:T(8,128)(2,1)S(1)}, bf16[1,64,512]{2,1,0:T(8,128)(2,1)S(1)}, u32[]{:S(2)}, u32[]{:S(2)}) collective-permute-start(bf16[1,64,512]{2,1,0:T(8,128)(2,1)S(1)} %copy-done.2), channel_id=1, source_target_pairs={{0,4},{4,0},{8,12},{12,8},{1,5},{5,1},{9,13},{13,9},{2,6},{6,2},{1... | collective-permute-start | bytes 196616 | tf_op jit(solution)/shard_map/ppermute | solution.py:570
  26.0 3.0 %collective-permute-start.9 = (bf16[64,1024]{1,0:T(8,128)(2,1)S(1)}, bf16[64,1024]{1,0:T(8,128)(2,1)S(1)}, u32[]{:S(2)}, u32[]{:S(2)}) collective-permute-start(bf16[64,1024]{1,0:T(8,128)(2,1)S(1)} %get-tuple-element.52), channel_id=1, source_target_pairs={{0,1},{1,0},{2,3},{3,2},{4,5},{5,4},{6,7},{7,6},{8,9},{9,8},{10,11... | collective-permute-start | bytes 393224 | tf_op jit(solution)/shard_map/ppermute | solution.py:570
  27.5 10.4 %copy-start.3 = (s32[1,3,16]{2,0,1:T(1,128)S(1)}, s32[1,3,16]{2,0,1:T(1,128)}, u32[]{:S(2)}) copy-start(s32[1,3,16]{2,0,1:T(1,128)} %param.14) | copy-start | bytes 580
  28.9 1.4 %collective-permute-start.6 = (bf16[64,1024]{1,0:T(8,128)(2,1)S(1)}, bf16[64,1024]{1,0:T(8,128)(2,1)S(1)}, u32[]{:S(2)}, u32[]{:S(2)}) collective-permute-start(bf16[64,1024]{1,0:T(8,128)(2,1)S(1)} %get-tuple-element.50), channel_id=1, source_target_pairs={{0,1},{1,0},{2,3},{3,2},{4,5},{5,4},{6,7},{7,6},{8,9},{9,8},{10,11... | collective-permute-start | bytes 393224 | tf_op jit(solution)/shard_map/ppermute | solution.py:570
  29.0 4.6 %collective-permute-start.10 = (bf16[64,1024]{1,0:T(8,128)(2,1)S(1)}, bf16[64,1024]{1,0:T(8,128)(2,1)S(1)}, u32[]{:S(2)}, u32[]{:S(2)}) collective-permute-start(bf16[64,1024]{1,0:T(8,128)(2,1)S(1)} %add_convert_fusion.1), channel_id=1, source_target_pairs={{0,2},{1,3},{2,0},{3,1},{4,6},{5,7},{6,4},{7,5},{8,10},{9,11},{10,... | collective-permute-start | bytes 393224 | tf_op jit(solution)/shard_map/ppermute | solution.py:570
  30.3 6.1 %collective-permute-start.7 = (bf16[64,1024]{1,0:T(8,128)(2,1)S(1)}, bf16[64,1024]{1,0:T(8,128)(2,1)S(1)}, u32[]{:S(2)}, u32[]{:S(2)}) collective-permute-start(bf16[64,1024]{1,0:T(8,128)(2,1)S(1)} %add_convert_fusion.3), channel_id=1, source_target_pairs={{0,2},{1,3},{2,0},{3,1},{4,6},{5,7},{6,4},{7,5},{8,10},{9,11},{10,... | collective-permute-start | bytes 393224 | tf_op jit(solution)/shard_map/ppermute | solution.py:570
  33.7 5.3 %collective-permute-start.11 = (bf16[64,1024]{1,0:T(8,128)(2,1)S(1)}, bf16[64,1024]{1,0:T(8,128)(2,1)S(1)}, u32[]{:S(2)}, u32[]{:S(2)}) collective-permute-start(bf16[64,1024]{1,0:T(8,128)(2,1)S(1)} %add_convert_fusion.two_ref), channel_id=1, source_target_pairs={{0,1},{1,0},{2,3},{3,2},{4,5},{5,4},{6,7},{7,6},{8,9},{9,8},{10,11... | collective-permute-start | bytes 393224 | tf_op jit(solution)/shard_map/ppermute | solution.py:570
  36.5 2.5 %collective-permute-start.8 = (bf16[64,1024]{1,0:T(8,128)(2,1)S(1)}, bf16[64,1024]{1,0:T(8,128)(2,1)S(1)}, u32[]{:S(2)}, u32[]{:S(2)}) collective-permute-start(bf16[64,1024]{1,0:T(8,128)(2,1)S(1)} %add_convert_fusion.2.one_ref), channel_id=1, source_target_pairs={{0,1},{1,0},{2,3},{3,2},{4,5},{5,4},{6,7},{7,6},{8,9},{9,8},{10,11... | collective-permute-start | bytes 393224 | tf_op jit(solution)/shard_map/ppermute | solution.py:570

commit v6 on v5

--- a/solution.py
+++ b/solution.py
@@ -635,7 +635,7 @@
         10**8,
         fetched=1,
     )
-    turned, cotangent = lax.optimization_barrier((turned, cotangent))
+    packs[1], cotangent = lax.optimization_barrier((packs[1], cotangent))
     cotangents = [cotangent] + [swap(cotangent, "space", step) for step in steps[1:-1]] + [near]
     rows = regions * mesh_count
     (

time: 40.2 us -> 39.4 us (0.980)
  the two profiles are of different devices: /device:TPU:13 before, /device:TPU:0 now
where the time goes in v6:
time: 39.4 us; the launch traced here: 39.2 us
  starting transfers between devices  13.6 us (35%)
  Pallas kernels  12.4 us (31%)
  waiting for transfers between devices  10.7 us (27%)
  local copies, waits for them, and re-layouts  1.61 us (4%)
  between operations  0.74 us (2%)
    ppermute x12, starting transfers between devices, swap(): lax.ppermute(block, axis, [(i, i ^ bits) for i in range(lax.axis_size(axi...  13.6 us
    pallas_call x7, Pallas kernels, call(): pl.pallas_call(kernel, out_shape=[jax.ShapeDtypeStruct(shape, kind) for s...  12.4 us
    ppermute x12, waiting for transfers between devices, swap(): lax.ppermute(block, axis, [(i, i ^ bits) for i in range(lax.axis_size(axi...  10.7 us
    unnamed x8, local copies, waits for them, and re-layouts  1.61 us
  transfers between devices with their start and end apart: 12, of which 5 were waited for; matrix products, arithmetic and copies ran while one was open for 0% of the time, Pallas kernels for 20%

profile of v6, /device:TPU:0, one launch (start us, length us, event | category | flops | bytes accessed | tf_op | source)
XLA Modules:
  0.0 39.2 jit_solution(3157946265691469783)
XLA Ops:
  0.6 0.0 copy-start.2
  0.6 1.9 %shard_map.121.refs_0_ = bf16[128,512]{1,0:T(8,128)(2,1)} custom-call(bf16[1,128,512]{2,1,0:T(8,128)(2,1)} %refs_0_.1, bf16[1,64,512]{2,1,0:T(8,128)(2,1)} %refs_1_.1, s32[3,1,16]{2,1,0:T(1,128)} %bitcast.5, s32[1,256]{1,0:T(1,128)} %bitcast.7, s32[1,256]{1,0:T(1,128)} %bitcast.8, s32[1,4,8]{2,1,0:T(4,128)} %refs_5_.1, s32[1,256]{1,0:T(1,128)} %bitcast.9, ...), custom_call_target="tpu_custom_call" | custom-call | flops 10000000 | bytes 4194304 | tf_op jit(solution)/shard_map/pallas_call | solution.py:557
  2.6 4.1 %collective-permute-start = (bf16[128,512]{1,0:T(8,128)(2,1)}, bf16[128,512]{1,0:T(8,128)(2,1)S(1)}, u32[]{:S(2)}, u32[]{:S(2)}) collective-permute-start(bf16[128,512]{1,0:T(8,128)(2,1)} %shard_map.121.refs_0_), channel_id=1, source_target_pairs={{0,8},{4,12},{8,0},{12,4},{1,9},{5,13},{9,1},{13,5},{2,10},{6,14},... | collective-permute-start | bytes 393224 | tf_op jit(solution)/shard_map/ppermute | solution.py:570
  6.7 1.3 %collective-permute-start.1 = (bf16[128,512]{1,0:T(8,128)(2,1)}, bf16[128,512]{1,0:T(8,128)(2,1)S(1)}, u32[]{:S(2)}, u32[]{:S(2)}) collective-permute-start(bf16[128,512]{1,0:T(8,128)(2,1)} %shard_map.121.refs_0_), channel_id=1, source_target_pairs={{0,12},{4,8},{8,4},{12,0},{1,13},{5,9},{9,5},{13,1},{2,14},{6,10},... | collective-permute-start | bytes 393224 | tf_op jit(solution)/shard_map/ppermute | solution.py:570
  8.0 0.2 collective-permute-start.2
  8.2 1.8 %collective-permute-start.5 = (bf16[1,64,512]{2,1,0:T(8,128)(2,1)}, bf16[1,64,512]{2,1,0:T(8,128)(2,1)S(1)}, u32[]{:S(2)}, u32[]{:S(2)}) collective-permute-start(bf16[1,64,512]{2,1,0:T(8,128)(2,1)} %refs_0_.2), channel_id=1, source_target_pairs={{0,4},{4,0},{8,12},{12,8},{1,5},{5,1},{9,13},{13,9},{2,6},{6,2},{1... | collective-permute-start | bytes 196616 | tf_op jit(solution)/shard_map/ppermute | solution.py:570
  10.0 1.6 %copy-done = bf16[512,2048]{1,0:T(8,128)(2,1)S(1)} copy-done((bf16[512,2048]{1,0:T(8,128)(2,1)S(1)}, bf16[512,2048]{1,0:T(8,128)(2,1)}, u32[]{:S(2)}) %copy-start) | copy-done | bytes 2097176
  11.6 0.6 %shard_map.122 = (bf16[512,2048]{1,0:T(8,128)(2,1)S(1)}, bf16[512,1536]{1,0:T(8,128)(2,1)S(1)}) custom-call(bf16[512,2048]{1,0:T(8,128)(2,1)S(1)} %copy-done), custom_call_target="tpu_custom_call" | custom-call | flops 100000000 | bytes 4194304 | tf_op jit(solution)/shard_map/pallas_call | solution.py:557
  12.2 4.6 %collective-permute-done.refs_1_ = bf16[128,512]{1,0:T(8,128)(2,1)S(1)} collective-permute-done((bf16[128,512]{1,0:T(8,128)(2,1)}, bf16[128,512]{1,0:T(8,128)(2,1)S(1)}, u32[]{:S(2)}, u32[]{:S(2)}) %collective-permute-start) | collective-permute-done | bytes 131104 | tf_op jit(solution)/shard_map/ppermute | solution.py:570
  16.9 2.8 %collective-permute-start.4 = (bf16[1,64,512]{2,1,0:T(8,128)(2,1)S(1)}, bf16[1,64,512]{2,1,0:T(8,128)(2,1)S(1)}, u32[]{:S(2)}, u32[]{:S(2)}) collective-permute-start(bf16[1,64,512]{2,1,0:T(8,128)(2,1)S(1)} %copy-done.2), channel_id=1, source_target_pairs={{0,12},{4,8},{8,4},{12,0},{1,13},{5,9},{9,5},{13,1},{2,14},{6,10},... | collective-permute-start | bytes 196616 | tf_op jit(solution)/shard_map/ppermute | solution.py:570
  19.7 0.0 collective-permute-done.1.refs_2_
  19.7 0.0 collective-permute-done.2.refs_3_
  19.7 4.7 %shard_map.123 = (bf16[1,64,512]{2,1,0:T(8,128)(2,1)}, bf16[192,512]{1,0:T(8,128)(2,1)S(1)}, bf16[256,512]{1,0:T(8,128)(2,1)S(1)}, bf16[256,512]{1,0:T(8,128)(2,...) custom-call(bf16[128,512]{1,0:T(8,128)(2,1)S(1)} %copy-done.1, ...), custom_call_target="tpu_custom_call" | custom-call | flops 2000000000 | bytes 4194304 | tf_op jit(solution)/shard_map/pallas_call | solution.py:557
  24.3 0.0 collective-permute-done.5.refs_3_
  24.3 0.3 collective-permute-done.3.refs_1_
  24.6 0.0 collective-permute-done.4.refs_2_
  24.6 1.7 %shard_map.124 = (f32[256,512]{1,0:T(8,128)S(1)}, bf16[64,1024]{1,0:T(8,128)(2,1)S(1)}, bf16[64,1024]{1,0:T(8,128)(2,1)S(1)}) custom-call(bf16[1,64,512]{2,1,0:T(8,128)(2,1)S(1)} %copy-done.2, bf16[1,64,512]{2,1,0:T(8,128)(2,1)S(1)} %collective-permute-done.3.refs_1_, bf16[1,64,512]{2,1,0:T(8,128)(2,1)S(1)} %collective-permute-done.4.refs_2_, ...), custom_call_target="tpu_custom_call" | custom-call | flops 1000000000 | bytes 4194304 | tf_op jit(solution)/shard_map/pallas_call | solution.py:557
  26.3 0.1 collective-permute-start.9
  26.4 0.0 copy-start.3
  26.4 1.4 %shard_map.125 = (bf16[48,512]{1,0:T(8,128)(2,1)S(1)}, bf16[64,1024]{1,0:T(8,128)(2,1)S(1)}, bf16[64,1024]{1,0:T(8,128)(2,1)S(1)}) custom-call(bf16[192,512]{1,0:T(8,128)(2,1)S(1)} %get-tuple-element.35.grid_ref, bf16[256,512]{1,0:T(8,128)(2,1)S(1)} %get-tuple-element.36.mesh_ref, s32[64,512]{1,0:T(8,128)S(1)} %get-tuple-element.37.refs_7_.index_ref, ...), custom_call_target="tpu_custom_call" | custom-call | flops 1000000000 | bytes 4194304 | tf_op jit(solution)/shard_map/pallas_call | solution.py:557
  27.8 0.6 %collective-permute-start.6 = (bf16[64,1024]{1,0:T(8,128)(2,1)S(1)}, bf16[64,1024]{1,0:T(8,128)(2,1)S(1)}, u32[]{:S(2)}, u32[]{:S(2)}) collective-permute-start(bf16[64,1024]{1,0:T(8,128)(2,1)S(1)} %get-tuple-element.50), channel_id=1, source_target_pairs={{0,1},{1,0},{2,3},{3,2},{4,5},{5,4},{6,7},{7,6},{8,9},{9,8},{10,11... | collective-permute-start | bytes 393224 | tf_op jit(solution)/shard_map/ppermute | solution.py:570
  28.4 1.6 %collective-permute-start.10 = (bf16[64,1024]{1,0:T(8,128)(2,1)S(1)}, bf16[64,1024]{1,0:T(8,128)(2,1)S(1)}, u32[]{:S(2)}, u32[]{:S(2)}) collective-permute-start(bf16[64,1024]{1,0:T(8,128)(2,1)S(1)} %add_convert_fusion.1), channel_id=1, source_target_pairs={{0,2},{1,3},{2,0},{3,1},{4,6},{5,7},{6,4},{7,5},{8,10},{9,11},{10,... | collective-permute-start | bytes 393224 | tf_op jit(solution)/shard_map/ppermute | solution.py:570
  30.0 0.0 collective-permute-done.6
  30.0 1.0 %collective-permute-start.7 = (bf16[64,1024]{1,0:T(8,128)(2,1)S(1)}, bf16[64,1024]{1,0:T(8,128)(2,1)S(1)}, u32[]{:S(2)}, u32[]{:S(2)}) collective-permute-start(bf16[64,1024]{1,0:T(8,128)(2,1)S(1)} %add_convert_fusion.3), channel_id=1, source_target_pairs={{0,2},{1,3},{2,0},{3,1},{4,6},{5,7},{6,4},{7,5},{8,10},{9,11},{10,... | collective-permute-start | bytes 393224 | tf_op jit(solution)/shard_map/ppermute | solution.py:570
  31.0 3.8 %collective-permute-done.10 = bf16[64,1024]{1,0:T(8,128)(2,1)S(1)} collective-permute-done((bf16[64,1024]{1,0:T(8,128)(2,1)S(1)}, bf16[64,1024]{1,0:T(8,128)(2,1)S(1)}, u32[]{:S(2)}, u32[]{:S(2)}) %collective-permute-start.10) | collective-permute-done | bytes 131104 | tf_op jit(solution)/shard_map/ppermute | solution.py:570
  34.9 0.1 collective-permute-start.11
  34.9 1.8 %collective-permute-done.7 = bf16[64,1024]{1,0:T(8,128)(2,1)S(1)} collective-permute-done((bf16[64,1024]{1,0:T(8,128)(2,1)S(1)}, bf16[64,1024]{1,0:T(8,128)(2,1)S(1)}, u32[]{:S(2)}, u32[]{:S(2)}) %collective-permute-start.7) | collective-permute-done | bytes 131104 | tf_op jit(solution)/shard_map/ppermute | solution.py:570
  36.7 0.1 collective-permute-start.8
  36.8 1.1 %shard_map.126 = bf16[1,128,512]{2,1,0:T(8,128)(2,1)} custom-call(bf16[512,1536]{1,0:T(8,128)(2,1)S(1)} %get-tuple-element.34.refs_4_.turned_ref, s32[3,1,16]{2,1,0:T(1,128)S(1)} %bitcast.6, bf16[48,512]{1,0:T(8,128)(2,1)S(1)} %get-tuple-element.48.own_slot_ref), custom_call_target="tpu_custom_call" | custom-call | flops 100000000 | bytes 4194304 | tf_op jit(solution)/shard_map/pallas_call | solution.py:557
  37.9 0.0 collective-permute-done.11.other_two_ref
  37.9 0.2 collective-permute-done.8.other_one_ref
  38.1 1.0 %shard_map.127 = f32[128,2048]{1,0:T(8,128)} custom-call(bf16[64,1024]{1,0:T(8,128)(2,1)S(1)} %add_convert_fusion.2.one_ref, bf16[64,1024]{1,0:T(8,128)(2,1)S(1)} %collective-permute-done.8.other_one_ref, bf16[64,1024]{1,0:T(8,128)(2,1)S(1)} %add_convert_fusion.two_ref, bf16[64,1024]{1,0:T(8,128)(2,1)S(1)} %collective-permute-done.11.other_two_ref), custom_call_target="tpu_custom_call" | custom-call | flops 1000000 | bytes 4194304 | tf_op jit(solution)/shard_map/pallas_call | solution.py:557
  (11 shorter events, 0.2 us)
Async XLA Ops:
  0.6 16.2 %copy-start.2 = (bf16[1,64,512]{2,1,0:T(8,128)(2,1)S(1)}, bf16[1,64,512]{2,1,0:T(8,128)(2,1)}, u32[]{:S(2)}) copy-start(bf16[1,64,512]{2,1,0:T(8,128)(2,1)} %refs_0_.2) | copy-start | bytes 196612
  2.6 14.3 %collective-permute-start = (bf16[128,512]{1,0:T(8,128)(2,1)}, bf16[128,512]{1,0:T(8,128)(2,1)S(1)}, u32[]{:S(2)}, u32[]{:S(2)}) collective-permute-start(bf16[128,512]{1,0:T(8,128)(2,1)} %shard_map.121.refs_0_), channel_id=1, source_target_pairs={{0,8},{4,12},{8,0},{12,4},{1,9},{5,13},{9,1},{13,5},{2,10},{6,14},... | collective-permute-start | bytes 393224 | tf_op jit(solution)/shard_map/ppermute | solution.py:570
  6.7 13.0 %collective-permute-start.1 = (bf16[128,512]{1,0:T(8,128)(2,1)}, bf16[128,512]{1,0:T(8,128)(2,1)S(1)}, u32[]{:S(2)}, u32[]{:S(2)}) collective-permute-start(bf16[128,512]{1,0:T(8,128)(2,1)} %shard_map.121.refs_0_), channel_id=1, source_target_pairs={{0,12},{4,8},{8,4},{12,0},{1,13},{5,9},{9,5},{13,1},{2,14},{6,10},... | collective-permute-start | bytes 393224 | tf_op jit(solution)/shard_map/ppermute | solution.py:570
  8.0 11.7 %collective-permute-start.2 = (bf16[128,512]{1,0:T(8,128)(2,1)}, bf16[128,512]{1,0:T(8,128)(2,1)S(1)}, u32[]{:S(2)}, u32[]{:S(2)}) collective-permute-start(bf16[128,512]{1,0:T(8,128)(2,1)} %shard_map.121.refs_0_), channel_id=1, source_target_pairs={{0,4},{4,0},{8,12},{12,8},{1,5},{5,1},{9,13},{13,9},{2,6},{6,2},{1... | collective-permute-start | bytes 393224 | tf_op jit(solution)/shard_map/ppermute | solution.py:570
  8.2 16.1 %collective-permute-start.5 = (bf16[1,64,512]{2,1,0:T(8,128)(2,1)}, bf16[1,64,512]{2,1,0:T(8,128)(2,1)S(1)}, u32[]{:S(2)}, u32[]{:S(2)}) collective-permute-start(bf16[1,64,512]{2,1,0:T(8,128)(2,1)} %refs_0_.2), channel_id=1, source_target_pairs={{0,4},{4,0},{8,12},{12,8},{1,5},{5,1},{9,13},{13,9},{2,6},{6,2},{1... | collective-permute-start | bytes 196616 | tf_op jit(solution)/shard_map/ppermute | solution.py:570
  10.0 1.6 %copy-start = (bf16[512,2048]{1,0:T(8,128)(2,1)S(1)}, bf16[512,2048]{1,0:T(8,128)(2,1)}, u32[]{:S(2)}) copy-start(bf16[512,2048]{1,0:T(8,128)(2,1)} %source_ref) | copy-start | bytes 6291460
  11.6 8.1 %copy-start.1 = (bf16[128,512]{1,0:T(8,128)(2,1)S(1)}, bf16[128,512]{1,0:T(8,128)(2,1)}, u32[]{:S(2)}) copy-start(bf16[128,512]{1,0:T(8,128)(2,1)} %shard_map.121.refs_0_) | copy-start | bytes 393220
  16.9 7.7 %collective-permute-start.3 = (bf16[1,64,512]{2,1,0:T(8,128)(2,1)S(1)}, bf16[1,64,512]{2,1,0:T(8,128)(2,1)S(1)}, u32[]{:S(2)}, u32[]{:S(2)}) collective-permute-start(bf16[1,64,512]{2,1,0:T(8,128)(2,1)S(1)} %copy-done.2), channel_id=1, source_target_pairs={{0,8},{4,12},{8,0},{12,4},{1,9},{5,13},{9,1},{13,5},{2,10},{6,14},... | collective-permute-start | bytes 196616 | tf_op jit(solution)/shard_map/ppermute | solution.py:570
  16.9 7.7 %collective-permute-start.4 = (bf16[1,64,512]{2,1,0:T(8,128)(2,1)S(1)}, bf16[1,64,512]{2,1,0:T(8,128)(2,1)S(1)}, u32[]{:S(2)}, u32[]{:S(2)}) collective-permute-start(bf16[1,64,512]{2,1,0:T(8,128)(2,1)S(1)} %copy-done.2), channel_id=1, source_target_pairs={{0,12},{4,8},{8,4},{12,0},{1,13},{5,9},{9,5},{13,1},{2,14},{6,10},... | collective-permute-start | bytes 196616 | tf_op jit(solution)/shard_map/ppermute | solution.py:570
  26.3 2.1 %collective-permute-start.9 = (bf16[64,1024]{1,0:T(8,128)(2,1)S(1)}, bf16[64,1024]{1,0:T(8,128)(2,1)S(1)}, u32[]{:S(2)}, u32[]{:S(2)}) collective-permute-start(bf16[64,1024]{1,0:T(8,128)(2,1)S(1)} %get-tuple-element.52), channel_id=1, source_target_pairs={{0,1},{1,0},{2,3},{3,2},{4,5},{5,4},{6,7},{7,6},{8,9},{9,8},{10,11... | collective-permute-start | bytes 393224 | tf_op jit(solution)/shard_map/ppermute | solution.py:570
  26.4 10.4 %copy-start.3 = (s32[1,3,16]{2,0,1:T(1,128)S(1)}, s32[1,3,16]{2,0,1:T(1,128)}, u32[]{:S(2)}) copy-start(s32[1,3,16]{2,0,1:T(1,128)} %param.14) | copy-start | bytes 580
  27.8 2.2 %collective-permute-start.6 = (bf16[64,1024]{1,0:T(8,128)(2,1)S(1)}, bf16[64,1024]{1,0:T(8,128)(2,1)S(1)}, u32[]{:S(2)}, u32[]{:S(2)}) collective-permute-start(bf16[64,1024]{1,0:T(8,128)(2,1)S(1)} %get-tuple-element.50), channel_id=1, source_target_pairs={{0,1},{1,0},{2,3},{3,2},{4,5},{5,4},{6,7},{7,6},{8,9},{9,8},{10,11... | collective-permute-start | bytes 393224 | tf_op jit(solution)/shard_map/ppermute | solution.py:570
  28.4 6.4 %collective-permute-start.10 = (bf16[64,1024]{1,0:T(8,128)(2,1)S(1)}, bf16[64,1024]{1,0:T(8,128)(2,1)S(1)}, u32[]{:S(2)}, u32[]{:S(2)}) collective-permute-start(bf16[64,1024]{1,0:T(8,128)(2,1)S(1)} %add_convert_fusion.1), channel_id=1, source_target_pairs={{0,2},{1,3},{2,0},{3,1},{4,6},{5,7},{6,4},{7,5},{8,10},{9,11},{10,... | collective-permute-start | bytes 393224 | tf_op jit(solution)/shard_map/ppermute | solution.py:570
  30.0 6.7 %collective-permute-start.7 = (bf16[64,1024]{1,0:T(8,128)(2,1)S(1)}, bf16[64,1024]{1,0:T(8,128)(2,1)S(1)}, u32[]{:S(2)}, u32[]{:S(2)}) collective-permute-start(bf16[64,1024]{1,0:T(8,128)(2,1)S(1)} %add_convert_fusion.3), channel_id=1, source_target_pairs={{0,2},{1,3},{2,0},{3,1},{4,6},{5,7},{6,4},{7,5},{8,10},{9,11},{10,... | collective-permute-start | bytes 393224 | tf_op jit(solution)/shard_map/ppermute | solution.py:570
  34.9 3.0 %collective-permute-start.11 = (bf16[64,1024]{1,0:T(8,128)(2,1)S(1)}, bf16[64,1024]{1,0:T(8,128)(2,1)S(1)}, u32[]{:S(2)}, u32[]{:S(2)}) collective-permute-start(bf16[64,1024]{1,0:T(8,128)(2,1)S(1)} %add_convert_fusion.two_ref), channel_id=1, source_target_pairs={{0,1},{1,0},{2,3},{3,2},{4,5},{5,4},{6,7},{7,6},{8,9},{9,8},{10,11... | collective-permute-start | bytes 393224 | tf_op jit(solution)/shard_map/ppermute | solution.py:570
  36.7 1.4 %collective-permute-start.8 = (bf16[64,1024]{1,0:T(8,128)(2,1)S(1)}, bf16[64,1024]{1,0:T(8,128)(2,1)S(1)}, u32[]{:S(2)}, u32[]{:S(2)}) collective-permute-start(bf16[64,1024]{1,0:T(8,128)(2,1)S(1)} %add_convert_fusion.2.one_ref), channel_id=1, source_target_pairs={{0,1},{1,0},{2,3},{3,2},{4,5},{5,4},{6,7},{7,6},{8,9},{9,8},{10,11... | collective-permute-start | bytes 393224 | tf_op jit(solution)/shard_map/ppermute | solution.py:570

commit v7 on v6

--- a/solution.py
+++ b/solution.py
@@ -199,7 +199,7 @@
 
 F32 = jnp.float32
 BF16 = jnp.bfloat16
-INDEX_ROWS = 16
+INDEX_ROWS = 8
 SAMPLE_EDGE_BYTES = 8 << 20
 
 
@@ -288,14 +288,35 @@
         ].T
 
 
-def edge_forward(table, hot, hot_receiver, slope_ref, first):
-    activation = dot_first(hot, table)
-    squash = 0.5 + 0.5 * jnp.tanh(0.5 * activation)
-    message = activation * squash
-    slope_ref[first : first + activation.shape[0], :] = (
-        squash + message * (1.0 - squash)
-    ).astype(BF16)
-    return dot(hot_receiver, message.astype(BF16))
+def edge_blocks(edges):
+    size = min(edges, 128)
+    return [(first, min(size, edges - first)) for first in range(0, edges, size)]
+
+
+def edge_forward(tables, hot_ref, turned_hot_ref, slope_ref, message_ref, mesh_count):
+    regions = len(tables)
+    edges = slope_ref.shape[0] // regions
+    count = hot_ref.shape[0] // regions
+    work = [(d, first, size) for d in range(regions) for first, size in edge_blocks(edges)]
+
+    def gathered(d, first, size):
+        rows = slice(d * edges + first, d * edges + first + size)
+        return dot(turned_hot_ref[rows, :], tables[d])
+
+    sums = []
+    activation = gathered(*work[0])
+    for n, (d, first, size) in enumerate(work):
+        coming = gathered(*work[n + 1]) if n + 1 < len(work) else None
+        squash = 0.5 + 0.5 * jnp.tanh(0.5 * activation)
+        message = activation * squash
+        rows = slice(d * edges + first, d * edges + first + size)
+        slope_ref[rows, :] = (squash + message * (1.0 - squash)).astype(BF16)
+        message_ref[rows, :] = message.astype(BF16)
+        activation = coming
+        if first + size == edges:
+            hot = hot_ref[(d + 1) * count - mesh_count : (d + 1) * count, :]
+            sums.append(dot(hot, message_ref[d * edges : (d + 1) * edges, :]))
+    return sums
 
 
 def forward_kernel(
@@ -314,14 +335,20 @@
         mesh_ref,
         first_ref,
         sent_ref,
-        index_ref,
+        hot_one_ref,
+        hot_two_ref,
+        turned_one_ref,
+        turned_two_ref,
+        hot_sent_ref,
         slope_one_ref,
         slope_two_ref,
         normed_one_ref,
         scaled_one_ref,
         normed_two_ref,
         scaled_two_ref,
-        packed_index,
+        index_ref,
+        message_ref,
+        sum_ref,
     ) = refs[regions:]
     latent = weights_ref.shape[0]
     edges = slope_one_ref.shape[0] // regions
@@ -333,80 +360,111 @@
         at = lambda rows: pl.ds(pl.multiple_of(region * rows, rows), rows)
         grid_ref[at(listed), :] = packed_ref[:listed, :]
         mesh_ref[at(mesh_count), :] = packed_ref[listed : listed + mesh_count, :]
-        packed_index[at(INDEX_ROWS), :] = packed_ref[listed + mesh_count :, :]
-    index_ref[...] = packed_index[...].astype(F32).astype(jnp.int32)
+        index_ref[at(INDEX_ROWS), :] = packed_ref[listed + mesh_count :, :].astype(F32)
 
     grid_proj = dot(grid_ref[...], weights_ref[:, :latent])
     mesh_proj = dot(mesh_ref[...], weights_ref[:, latent : 2 * latent])
+    for d in range(regions):
+        index = index_ref[d * INDEX_ROWS : (d + 1) * INDEX_ROWS, :].astype(jnp.int32)
+        for row, senders, hot_ref, turned_ref in (
+            (0, listed, hot_one_ref, turned_one_ref),
+            (1, slots, hot_two_ref, turned_two_ref),
+        ):
+            count = senders + mesh_count
+            hot = jnp.concatenate(
+                [
+                    one_hot(index[row : row + 1, :edges], senders),
+                    one_hot(index[row : row + 1, edges:], mesh_count),
+                ],
+                axis=0,
+            )
+            hot_ref[d * count : (d + 1) * count, :] = hot
+            turned_ref[d * edges : (d + 1) * edges, :] = hot.T
+        hot_sent_ref[d * mesh_count : (d + 1) * mesh_count, :] = one_hot(
+            index[2:3, :slots], mesh_count
+        )
+
     blank = jnp.zeros((capacity, latent), F32)
+    tables = []
     for d in range(regions):
-        hot_sender = one_hot(index_ref[d * INDEX_ROWS : d * INDEX_ROWS + 1, :edges], listed)
-        hot_receiver = one_hot(
-            index_ref[d * INDEX_ROWS : d * INDEX_ROWS + 1, edges:], mesh_count
-        )
         before = (d - 1) * listed + 2 * capacity
         within = d * listed + capacity
         after = (d + 1) * listed
-        table = jnp.concatenate(
-            [
-                grid_proj[before : before + capacity] if d > 0 else blank,
-                grid_proj[within : within + capacity],
-                grid_proj[after : after + capacity] if d < regions - 1 else blank,
-                mesh_proj[d * mesh_count : (d + 1) * mesh_count],
-            ],
-            axis=0,
-        ).astype(BF16)
-        summed = edge_forward(
-            table,
-            jnp.concatenate([hot_sender, hot_receiver], axis=0),
-            hot_receiver,
-            slope_one_ref,
-            d * edges,
+        tables.append(
+            jnp.concatenate(
+                [
+                    grid_proj[before : before + capacity] if d > 0 else blank,
+                    grid_proj[within : within + capacity],
+                    grid_proj[after : after + capacity] if d < regions - 1 else blank,
+                    mesh_proj[d * mesh_count : (d + 1) * mesh_count],
+                ],
+                axis=0,
+            ).astype(BF16)
         )
-        centred, scaled = row_moments(summed)
-        normed = centred * scaled
-        rows = slice(d * mesh_count, (d + 1) * mesh_count)
-        normed_one_ref[rows, :] = normed
-        scaled_one_ref[rows, :] = jnp.broadcast_to(scaled, (mesh_count, scaled_one_ref.shape[1]))
-        first_ref[rows, :] = (mesh_ref[rows, :].astype(F32) + normed).astype(BF16)
+    sums = edge_forward(
+        tables, hot_one_ref, turned_one_ref, slope_one_ref, message_ref, mesh_count
+    )
+    for d in range(regions):
+        sum_ref[d * mesh_count : (d + 1) * mesh_count, :] = sums[d]
+    centred, scaled = row_moments(sum_ref[...])
+    normed = centred * scaled
+    normed_one_ref[...] = normed
+    scaled_one_ref[...] = jnp.broadcast_to(scaled, scaled_one_ref.shape)
+    first_ref[...] = (mesh_ref[...].astype(F32) + normed).astype(BF16)
 
     for s in range(regions):
-        hot = one_hot(index_ref[s * INDEX_ROWS + 2 : s * INDEX_ROWS + 3, :slots], mesh_count)
+        rows = slice(s * mesh_count, (s + 1) * mesh_count)
         sent_ref[s * slots : (s + 1) * slots, :] = dot_first(
-            hot, first_ref[s * mesh_count : (s + 1) * mesh_count, :]
+            hot_sent_ref[rows, :], first_ref[rows, :]
         ).astype(BF16)
     sent_proj = dot(sent_ref[...], weights_ref[:, 2 * latent : 3 * latent])
     first_proj = dot(first_ref[...], weights_ref[:, 3 * latent :])
+    tables = []
     for d in range(regions):
-        hot_sender = one_hot(index_ref[d * INDEX_ROWS + 1 : d * INDEX_ROWS + 2, :edges], slots)
-        hot_receiver = one_hot(
-            index_ref[d * INDEX_ROWS + 1 : d * INDEX_ROWS + 2, edges:], mesh_count
-        )
         pieces = [
             sent_proj[s * slots + d * mesh_cap : s * slots + (d + 1) * mesh_cap]
             for s in range(regions)
         ]
-        table = jnp.concatenate(
-            pieces + [first_proj[d * mesh_count : (d + 1) * mesh_count]], axis=0
-        ).astype(BF16)
-        summed = edge_forward(
-            table,
-            jnp.concatenate([hot_sender, hot_receiver], axis=0),
-            hot_receiver,
-            slope_two_ref,
-            d * edges,
+        tables.append(
+            jnp.concatenate(
+                pieces + [first_proj[d * mesh_count : (d + 1) * mesh_count]], axis=0
+            ).astype(BF16)
         )
-        centred, scaled = row_moments(summed)
-        rows = slice(d * mesh_count, (d + 1) * mesh_count)
-        normed_two_ref[rows, :] = centred * scaled
-        scaled_two_ref[rows, :] = jnp.broadcast_to(scaled, (mesh_count, scaled_two_ref.shape[1]))
+    sums = edge_forward(
+        tables, hot_two_ref, turned_two_ref, slope_two_ref, message_ref, mesh_count
+    )
+    for d in range(regions):
+        sum_ref[d * mesh_count : (d + 1) * mesh_count, :] = sums[d]
+    centred, scaled = row_moments(sum_ref[...])
+    normed_two_ref[...] = centred * scaled
+    scaled_two_ref[...] = jnp.broadcast_to(scaled, scaled_two_ref.shape)
     own = pl.ds(pl.multiple_of(me * mesh_count, mesh_count), mesh_count)
     mesh_out_ref[0] = (first_ref[own, :].astype(F32) + normed_two_ref[own, :]).astype(BF16)
 
 
-def edge_backward(agg_grad, hot, hot_receiver, slope):
-    edge_grad = (dot_first(hot_receiver, agg_grad) * slope.astype(F32)).astype(BF16)
-    return dot(hot, edge_grad)
+def edge_backward(regions, agg_grad, hot_ref, turned_hot_ref, slope_ref, edge_grad_ref):
+    edges = slope_ref.shape[0] // regions
+    count = hot_ref.shape[0] // regions
+    mesh_count = agg_grad.shape[0] // regions
+    blank = jnp.zeros((count - mesh_count, agg_grad.shape[1]), BF16)
+    work = [(d, first, size) for d in range(regions) for first, size in edge_blocks(edges)]
+
+    def gathered(d, first, size):
+        rows = slice(d * edges + first, d * edges + first + size)
+        table = jnp.concatenate([blank, agg_grad[d * mesh_count : (d + 1) * mesh_count]], axis=0)
+        return dot(turned_hot_ref[rows, :], table)
+
+    sums = []
+    upstream = gathered(*work[0])
+    for n, (d, first, size) in enumerate(work):
+        coming = gathered(*work[n + 1]) if n + 1 < len(work) else None
+        rows = slice(d * edges + first, d * edges + first + size)
+        edge_grad_ref[rows, :] = (upstream * slope_ref[rows, :].astype(F32)).astype(BF16)
+        upstream = coming
+        if first + size == edges:
+            hot = hot_ref[d * count : (d + 1) * count, :]
+            sums.append(dot(hot, edge_grad_ref[d * edges : (d + 1) * edges, :]))
+    return sums
 
 
 def halve(share_ref, keep_ref, give_ref):
@@ -423,7 +481,9 @@
         turned_ref,
         first_ref,
         sent_ref,
-        index_ref,
+        hot_ref,
+        turned_hot_ref,
+        hot_sent_ref,
         slope_ref,
         normed_ref,
         scaled_ref,
@@ -434,10 +494,10 @@
         slot_ref,
         recv_ref,
         share_ref,
+        edge_grad_ref,
     ) = refs[regions:]
     latent = first_ref.shape[1]
     mesh_count = first_ref.shape[0] // regions
-    edges = slope_ref.shape[0] // regions
     slots = regions * mesh_cap
     me = lax.axis_index("space")
     for step, cotangent_ref in zip(steps, cotangent_refs):
@@ -445,21 +505,14 @@
         at = pl.ds(pl.multiple_of(region * mesh_count, mesh_count), mesh_count)
         upstream_ref[at, :] = cotangent_ref[0].astype(F32)
     agg_grad = moments_back(normed_ref[...], scaled_ref[:, 0:1], upstream_ref[...]).astype(BF16)
-    for d in range(regions):
-        labels = slice(d * INDEX_ROWS + 1, d * INDEX_ROWS + 2)
-        hot_sender = one_hot(index_ref[labels, :edges], slots)
-        hot_receiver = one_hot(index_ref[labels, edges:], mesh_count)
-        rows = slice(d * mesh_count, (d + 1) * mesh_count)
-        sums = edge_backward(
-            agg_grad[rows],
-            jnp.concatenate([hot_sender, hot_receiver], axis=0),
-            hot_receiver,
-            slope_ref[d * edges : (d + 1) * edges, :],
-        )
+    all_sums = edge_backward(
+        regions, agg_grad, hot_ref, turned_hot_ref, slope_ref, edge_grad_ref
+    )
+    for d, sums in enumerate(all_sums):
         for s in range(regions):
             first = s * slots + d * mesh_cap
             slot_ref[first : first + mesh_cap, :] = sums[s * mesh_cap : (s + 1) * mesh_cap]
-        recv_ref[rows, :] = sums[slots:].astype(BF16)
+        recv_ref[d * mesh_count : (d + 1) * mesh_count, :] = sums[slots:].astype(BF16)
     slot_sum = slot_ref[...].astype(BF16)
     columns = share_ref.shape[0]
     mine = pl.ds(pl.multiple_of(me * columns, columns), columns)
@@ -469,16 +522,18 @@
     returned = dot(slot_sum, turned_ref[:, latent : 2 * latent]).astype(BF16)
     grad = upstream_ref[...] + dot(recv_ref[...], turned_ref[:, 2 * latent :])
     for s in range(regions):
-        hot = one_hot(index_ref[s * INDEX_ROWS + 2 : s * INDEX_ROWS + 3, :slots], mesh_count)
         rows = slice(s * mesh_count, (s + 1) * mesh_count)
-        mesh_grad_ref[rows, :] = grad[rows] + dot(hot, returned[s * slots : (s + 1) * slots])
+        mesh_grad_ref[rows, :] = grad[rows] + dot(
+            hot_sent_ref[rows, :], returned[s * slots : (s + 1) * slots]
+        )
 
 
 def encode_back_kernel(
     regions,
     grid_ref,
     mesh_ref,
-    index_ref,
+    hot_ref,
+    turned_hot_ref,
     slope_ref,
     normed_ref,
     scaled_ref,
@@ -489,34 +544,28 @@
     slot_ref,
     recv_ref,
     share_ref,
+    edge_grad_ref,
 ):
     latent = mesh_ref.shape[1]
     mesh_count = mesh_ref.shape[0] // regions
     listed = grid_ref.shape[0] // regions
     capacity = listed // 3
-    edges = slope_ref.shape[0] // regions
     me = lax.axis_index("space")
     agg_grad = moments_back(normed_ref[...], scaled_ref[:, 0:1], mesh_grad_ref[...]).astype(BF16)
     blank = jnp.zeros((capacity, latent), BF16)
     slot_ref[0:capacity, :] = blank
     slot_ref[regions * listed - capacity :, :] = blank
-    for d in range(regions):
-        labels = slice(d * INDEX_ROWS, d * INDEX_ROWS + 1)
-        hot_sender = one_hot(index_ref[labels, :edges], listed)
-        hot_receiver = one_hot(index_ref[labels, edges:], mesh_count)
-        rows = slice(d * mesh_count, (d + 1) * mesh_count)
-        sums = edge_backward(
-            agg_grad[rows],
-            jnp.concatenate([hot_sender, hot_receiver], axis=0),
-            hot_receiver,
-            slope_ref[d * edges : (d + 1) * edges, :],
-        ).astype(BF16)
+    all_sums = edge_backward(
+        regions, agg_grad, hot_ref, turned_hot_ref, slope_ref, edge_grad_ref
+    )
+    for d, sums in enumerate(all_sums):
+        sums = sums.astype(BF16)
         for j in range(3):
             source = d + j - 1
             if 0 <= source < regions:
                 first = source * listed + (2 - j) * capacity
                 slot_ref[first : first + capacity, :] = sums[j * capacity : (j + 1) * capacity]
-        recv_ref[rows, :] = sums[listed:]
+        recv_ref[d * mesh_count : (d + 1) * mesh_count, :] = sums[listed:]
     columns = share_ref.shape[0]
     mine = pl.ds(pl.multiple_of(me * columns, columns), columns)
     share_ref[:, :latent] = dot_first(grid_ref[:, mine], slot_ref[...]).astype(BF16)
@@ -638,13 +687,18 @@
     packs[1], cotangent = lax.optimization_barrier((packs[1], cotangent))
     cotangents = [cotangent] + [swap(cotangent, "space", step) for step in steps[1:-1]] + [near]
     rows = regions * mesh_count
+    slots = regions * mesh_cap
     (
         mesh_out,
         grid_all,
         mesh_all,
         mesh_first,
         mesh_sent,
-        index,
+        hot_one,
+        hot_two,
+        turned_one,
+        turned_two,
+        hot_sent,
         slope_one,
         slope_two,
         normed_one,
@@ -659,8 +713,12 @@
             ((regions * listed, latent), BF16),
             ((rows, latent), BF16),
             ((rows, latent), BF16),
-            ((regions * regions * mesh_cap, latent), BF16),
-            ((regions * INDEX_ROWS, latent), jnp.int32),
+            ((regions * slots, latent), BF16),
+            ((regions * (listed + mesh_count), edges), BF16),
+            ((regions * (slots + mesh_count), edges), BF16),
+            ((regions * edges, listed + mesh_count), BF16),
+            ((regions * edges, slots + mesh_count), BF16),
+            ((rows, slots), BF16),
             ((regions * edges, latent), BF16),
             ((regions * edges, latent), BF16),
             ((rows, latent), F32),
@@ -668,7 +726,11 @@
             ((rows, latent), F32),
             ((rows, 128), F32),
         ],
-        [((regions * INDEX_ROWS, latent), BF16)],
+        [
+            ((regions * INDEX_ROWS, latent), F32),
+            ((regions * edges, latent), BF16),
+            ((rows, latent), F32),
+        ],
         2 * 10**9,
     )
     mesh_grad, keep_two, give_two = call(
@@ -678,7 +740,9 @@
             turned,
             mesh_first,
             mesh_sent,
-            index,
+            hot_two,
+            turned_two,
+            hot_sent,
             slope_two,
             normed_two,
             scaled_two,
@@ -686,9 +750,10 @@
         [((rows, latent), F32)] + [((half, 2 * latent), BF16)] * 2,
         [
             ((rows, latent), F32),
-            ((regions * regions * mesh_cap, latent), F32),
+            ((regions * slots, latent), F32),
             ((rows, latent), BF16),
             ((columns, 2 * latent), BF16),
+            ((regions * edges, latent), BF16),
         ],
         10**9,
     )
@@ -697,7 +762,8 @@
         (
             grid_all,
             mesh_all,
-            index,
+            hot_one,
+            turned_one,
             slope_one,
             normed_one,
             scaled_one,
@@ -708,6 +774,7 @@
             ((regions * listed, latent), BF16),
             ((rows, latent), BF16),
             ((columns, 2 * latent), BF16),
+            ((regions * edges, latent), BF16),
         ],
         10**9,
     )

time: 39.4 us -> 38.6 us (0.980)
  Pallas kernels: 12.4 us -> 11.7 us
    pallas_call x7, Pallas kernels: 12.4 us -> 11.7 us  [call(): pl.pallas_call(kernel, out_shape=[jax.ShapeDtypeStruct(shape, kind) for s...]
  transfers between devices with their start and end apart: 12 -> 12, of which waited for: 5 -> 5; matrix products, arithmetic and copies ran while one was open for 0% -> 0% of each run, Pallas kernels for 20% -> 19%
where the time goes in v7:
time: 38.6 us; the launch traced here: 38.5 us
  starting transfers between devices  13.6 us (35%)
  Pallas kernels  11.7 us (30%)
  waiting for transfers between devices  10.7 us (28%)
  local copies, waits for them, and re-layouts  1.61 us (4%)
  between operations  0.74 us (2%)
    ppermute x12, starting transfers between devices, swap(): lax.ppermute(block, axis, [(i, i ^ bits) for i in range(lax.axis_size(axi...  13.6 us
    pallas_call x7, Pallas kernels, call(): pl.pallas_call(kernel, out_shape=[jax.ShapeDtypeStruct(shape, kind) for s...  11.7 us
    ppermute x12, waiting for transfers between devices, swap(): lax.ppermute(block, axis, [(i, i ^ bits) for i in range(lax.axis_size(axi...  10.7 us
    unnamed x8, local copies, waits for them, and re-layouts  1.61 us
  transfers between devices with their start and end apart: 12, of which 5 were waited for; matrix products, arithmetic and copies ran while one was open for 0% of the time, Pallas kernels for 19%

profile of v7, /device:TPU:0, one launch (start us, length us, event | category | flops | bytes accessed | tf_op | source)
XLA Modules:
  0.0 38.5 jit_solution(10159372365872639897)
XLA Ops:
  0.6 0.0 copy-start.2
  0.6 1.9 %shard_map.121.refs_0_ = bf16[120,512]{1,0:T(8,128)(2,1)} custom-call(bf16[1,128,512]{2,1,0:T(8,128)(2,1)} %refs_0_.1, bf16[1,64,512]{2,1,0:T(8,128)(2,1)} %refs_1_.1, s32[3,1,16]{2,1,0:T(1,128)} %bitcast.5, s32[1,256]{1,0:T(1,128)} %bitcast.7, s32[1,256]{1,0:T(1,128)} %bitcast.8, s32[1,4,8]{2,1,0:T(4,128)} %refs_5_.1, s32[1,256]{1,0:T(1,128)} %bitcast.9, ...), custom_call_target="tpu_custom_call" | custom-call | flops 10000000 | bytes 4194304 | tf_op jit(solution)/shard_map/pallas_call | solution.py:606
  2.5 4.1 %collective-permute-start = (bf16[120,512]{1,0:T(8,128)(2,1)}, bf16[120,512]{1,0:T(8,128)(2,1)S(1)}, u32[]{:S(2)}, u32[]{:S(2)}) collective-permute-start(bf16[120,512]{1,0:T(8,128)(2,1)} %shard_map.121.refs_0_), channel_id=1, source_target_pairs={{0,8},{4,12},{8,0},{12,4},{1,9},{5,13},{9,1},{13,5},{2,10},{6,14},... | collective-permute-start | bytes 368648 | tf_op jit(solution)/shard_map/ppermute | solution.py:619
  6.6 1.3 %collective-permute-start.1 = (bf16[120,512]{1,0:T(8,128)(2,1)}, bf16[120,512]{1,0:T(8,128)(2,1)S(1)}, u32[]{:S(2)}, u32[]{:S(2)}) collective-permute-start(bf16[120,512]{1,0:T(8,128)(2,1)} %shard_map.121.refs_0_), channel_id=1, source_target_pairs={{0,12},{4,8},{8,4},{12,0},{1,13},{5,9},{9,5},{13,1},{2,14},{6,10},... | collective-permute-start | bytes 368648 | tf_op jit(solution)/shard_map/ppermute | solution.py:619
  8.0 0.2 collective-permute-start.2
  8.2 1.8 %collective-permute-start.5 = (bf16[1,64,512]{2,1,0:T(8,128)(2,1)}, bf16[1,64,512]{2,1,0:T(8,128)(2,1)S(1)}, u32[]{:S(2)}, u32[]{:S(2)}) collective-permute-start(bf16[1,64,512]{2,1,0:T(8,128)(2,1)} %refs_0_.2), channel_id=1, source_target_pairs={{0,4},{4,0},{8,12},{12,8},{1,5},{5,1},{9,13},{13,9},{2,6},{6,2},{1... | collective-permute-start | bytes 196616 | tf_op jit(solution)/shard_map/ppermute | solution.py:619
  10.0 1.6 %copy-done = bf16[512,2048]{1,0:T(8,128)(2,1)S(1)} copy-done((bf16[512,2048]{1,0:T(8,128)(2,1)S(1)}, bf16[512,2048]{1,0:T(8,128)(2,1)}, u32[]{:S(2)}) %copy-start) | copy-done | bytes 2097176
  11.6 0.6 %shard_map.122 = (bf16[512,2048]{1,0:T(8,128)(2,1)S(1)}, bf16[512,1536]{1,0:T(8,128)(2,1)S(1)}) custom-call(bf16[512,2048]{1,0:T(8,128)(2,1)S(1)} %copy-done), custom_call_target="tpu_custom_call" | custom-call | flops 100000000 | bytes 4194304 | tf_op jit(solution)/shard_map/pallas_call | solution.py:606
  12.2 4.1 %collective-permute-done.refs_1_ = bf16[120,512]{1,0:T(8,128)(2,1)S(1)} collective-permute-done((bf16[120,512]{1,0:T(8,128)(2,1)}, bf16[120,512]{1,0:T(8,128)(2,1)S(1)}, u32[]{:S(2)}, u32[]{:S(2)}) %collective-permute-start) | collective-permute-done | bytes 122912 | tf_op jit(solution)/shard_map/ppermute | solution.py:619
  16.3 0.0 collective-permute-start.3
  16.3 2.8 %collective-permute-start.4 = (bf16[1,64,512]{2,1,0:T(8,128)(2,1)S(1)}, bf16[1,64,512]{2,1,0:T(8,128)(2,1)S(1)}, u32[]{:S(2)}, u32[]{:S(2)}) collective-permute-start(bf16[1,64,512]{2,1,0:T(8,128)(2,1)S(1)} %copy-done.2), channel_id=1, source_target_pairs={{0,12},{4,8},{8,4},{12,0},{1,13},{5,9},{9,5},{13,1},{2,14},{6,10},... | collective-permute-start | bytes 196616 | tf_op jit(solution)/shard_map/ppermute | solution.py:619
  19.1 4.2 %shard_map.123 = (bf16[1,64,512]{2,1,0:T(8,128)(2,1)}, bf16[192,512]{1,0:T(8,128)(2,1)S(1)}, bf16[256,512]{1,0:T(8,128)(2,1)S(1)}, bf16[256,512]{1,0:T(8,128)(2,...) custom-call(bf16[120,512]{1,0:T(8,128)(2,1)S(1)} %copy-done.1, ...), custom_call_target="tpu_custom_call" | custom-call | flops 2000000000 | bytes 4194304 | tf_op jit(solution)/shard_map/pallas_call | solution.py:606
  23.3 0.0 collective-permute-done.5.refs_3_
  23.3 0.7 %collective-permute-done.3.refs_1_ = bf16[1,64,512]{2,1,0:T(8,128)(2,1)S(1)} collective-permute-done((bf16[1,64,512]{2,1,0:T(8,128)(2,1)S(1)}, bf16[1,64,512]{2,1,0:T(8,128)(2,1)S(1)}, u32[]{:S(2)}, u32[]{:S(2)}) %collective-permute-start.3) | collective-permute-done | bytes 65568 | tf_op jit(solution)/shard_map/ppermute | solution.py:619
  24.1 0.0 collective-permute-done.4.refs_2_
  24.1 1.6 %shard_map.124 = (f32[256,512]{1,0:T(8,128)S(1)}, bf16[64,1024]{1,0:T(8,128)(2,1)S(1)}, bf16[64,1024]{1,0:T(8,128)(2,1)S(1)}) custom-call(bf16[1,64,512]{2,1,0:T(8,128)(2,1)S(1)} %copy-done.2, bf16[1,64,512]{2,1,0:T(8,128)(2,1)S(1)} %collective-permute-done.3.refs_1_, bf16[1,64,512]{2,1,0:T(8,128)(2,1)S(1)} %collective-permute-done.4.refs_2_, ...), custom_call_target="tpu_custom_call" | custom-call | flops 1000000000 | bytes 4194304 | tf_op jit(solution)/shard_map/pallas_call | solution.py:606
  25.7 0.1 collective-permute-start.9
  25.7 0.0 copy-start.3
  25.8 1.3 %shard_map.125 = (bf16[48,512]{1,0:T(8,128)(2,1)S(1)}, bf16[64,1024]{1,0:T(8,128)(2,1)S(1)}, bf16[64,1024]{1,0:T(8,128)(2,1)S(1)}) custom-call(bf16[192,512]{1,0:T(8,128)(2,1)S(1)} %get-tuple-element.39.grid_ref, bf16[256,512]{1,0:T(8,128)(2,1)S(1)} %get-tuple-element.40.mesh_ref, bf16[448,256]{1,0:T(8,128)(2,1)S(1)} %get-tuple-element.41.hot_ref, ...), custom_call_target="tpu_custom_call" | custom-call | flops 1000000000 | bytes 4194304 | tf_op jit(solution)/shard_map/pallas_call | solution.py:606
  27.1 0.6 %collective-permute-start.6 = (bf16[64,1024]{1,0:T(8,128)(2,1)S(1)}, bf16[64,1024]{1,0:T(8,128)(2,1)S(1)}, u32[]{:S(2)}, u32[]{:S(2)}) collective-permute-start(bf16[64,1024]{1,0:T(8,128)(2,1)S(1)} %get-tuple-element.58), channel_id=1, source_target_pairs={{0,1},{1,0},{2,3},{3,2},{4,5},{5,4},{6,7},{7,6},{8,9},{9,8},{10,11... | collective-permute-start | bytes 393224 | tf_op jit(solution)/shard_map/ppermute | solution.py:619
  27.6 0.0 collective-permute-done.9
  27.7 1.6 %collective-permute-start.10 = (bf16[64,1024]{1,0:T(8,128)(2,1)S(1)}, bf16[64,1024]{1,0:T(8,128)(2,1)S(1)}, u32[]{:S(2)}, u32[]{:S(2)}) collective-permute-start(bf16[64,1024]{1,0:T(8,128)(2,1)S(1)} %add_convert_fusion.1), channel_id=1, source_target_pairs={{0,2},{1,3},{2,0},{3,1},{4,6},{5,7},{6,4},{7,5},{8,10},{9,11},{10,... | collective-permute-start | bytes 393224 | tf_op jit(solution)/shard_map/ppermute | solution.py:619
  29.3 0.0 collective-permute-done.6
  29.3 1.0 %collective-permute-start.7 = (bf16[64,1024]{1,0:T(8,128)(2,1)S(1)}, bf16[64,1024]{1,0:T(8,128)(2,1)S(1)}, u32[]{:S(2)}, u32[]{:S(2)}) collective-permute-start(bf16[64,1024]{1,0:T(8,128)(2,1)S(1)} %add_convert_fusion.3), channel_id=1, source_target_pairs={{0,2},{1,3},{2,0},{3,1},{4,6},{5,7},{6,4},{7,5},{8,10},{9,11},{10,... | collective-permute-start | bytes 393224 | tf_op jit(solution)/shard_map/ppermute | solution.py:619
  30.3 3.8 %collective-permute-done.10 = bf16[64,1024]{1,0:T(8,128)(2,1)S(1)} collective-permute-done((bf16[64,1024]{1,0:T(8,128)(2,1)S(1)}, bf16[64,1024]{1,0:T(8,128)(2,1)S(1)}, u32[]{:S(2)}, u32[]{:S(2)}) %collective-permute-start.10) | collective-permute-done | bytes 131104 | tf_op jit(solution)/shard_map/ppermute | solution.py:619
  34.1 0.1 collective-permute-start.11
  34.2 1.8 %collective-permute-done.7 = bf16[64,1024]{1,0:T(8,128)(2,1)S(1)} collective-permute-done((bf16[64,1024]{1,0:T(8,128)(2,1)S(1)}, bf16[64,1024]{1,0:T(8,128)(2,1)S(1)}, u32[]{:S(2)}, u32[]{:S(2)}) %collective-permute-start.7) | collective-permute-done | bytes 131104 | tf_op jit(solution)/shard_map/ppermute | solution.py:619
  36.0 0.1 collective-permute-start.8
  36.1 1.1 %shard_map.126 = bf16[1,128,512]{2,1,0:T(8,128)(2,1)} custom-call(bf16[512,1536]{1,0:T(8,128)(2,1)S(1)} %get-tuple-element.38.refs_4_.turned_ref, s32[3,1,16]{2,1,0:T(1,128)S(1)} %bitcast.6, bf16[48,512]{1,0:T(8,128)(2,1)S(1)} %get-tuple-element.56.own_slot_ref), custom_call_target="tpu_custom_call" | custom-call | flops 100000000 | bytes 4194304 | tf_op jit(solution)/shard_map/pallas_call | solution.py:606
  37.2 0.0 collective-permute-done.11.other_two_ref
  37.2 0.2 collective-permute-done.8.other_one_ref
  37.4 1.0 %shard_map.127 = f32[128,2048]{1,0:T(8,128)} custom-call(bf16[64,1024]{1,0:T(8,128)(2,1)S(1)} %add_convert_fusion.2.one_ref, bf16[64,1024]{1,0:T(8,128)(2,1)S(1)} %collective-permute-done.8.other_one_ref, bf16[64,1024]{1,0:T(8,128)(2,1)S(1)} %add_convert_fusion.two_ref, bf16[64,1024]{1,0:T(8,128)(2,1)S(1)} %collective-permute-done.11.other_two_ref), custom_call_target="tpu_custom_call" | custom-call | flops 1000000 | bytes 4194304 | tf_op jit(solution)/shard_map/pallas_call | solution.py:606
  (11 shorter events, 0.2 us)
Async XLA Ops:
  0.6 15.7 %copy-start.2 = (bf16[1,64,512]{2,1,0:T(8,128)(2,1)S(1)}, bf16[1,64,512]{2,1,0:T(8,128)(2,1)}, u32[]{:S(2)}) copy-start(bf16[1,64,512]{2,1,0:T(8,128)(2,1)} %refs_0_.2) | copy-start | bytes 196612
  2.5 13.8 %collective-permute-start = (bf16[120,512]{1,0:T(8,128)(2,1)}, bf16[120,512]{1,0:T(8,128)(2,1)S(1)}, u32[]{:S(2)}, u32[]{:S(2)}) collective-permute-start(bf16[120,512]{1,0:T(8,128)(2,1)} %shard_map.121.refs_0_), channel_id=1, source_target_pairs={{0,8},{4,12},{8,0},{12,4},{1,9},{5,13},{9,1},{13,5},{2,10},{6,14},... | collective-permute-start | bytes 368648 | tf_op jit(solution)/shard_map/ppermute | solution.py:619
  6.6 12.5 %collective-permute-start.1 = (bf16[120,512]{1,0:T(8,128)(2,1)}, bf16[120,512]{1,0:T(8,128)(2,1)S(1)}, u32[]{:S(2)}, u32[]{:S(2)}) collective-permute-start(bf16[120,512]{1,0:T(8,128)(2,1)} %shard_map.121.refs_0_), channel_id=1, source_target_pairs={{0,12},{4,8},{8,4},{12,0},{1,13},{5,9},{9,5},{13,1},{2,14},{6,10},... | collective-permute-start | bytes 368648 | tf_op jit(solution)/shard_map/ppermute | solution.py:619
  8.0 11.1 %collective-permute-start.2 = (bf16[120,512]{1,0:T(8,128)(2,1)}, bf16[120,512]{1,0:T(8,128)(2,1)S(1)}, u32[]{:S(2)}, u32[]{:S(2)}) collective-permute-start(bf16[120,512]{1,0:T(8,128)(2,1)} %shard_map.121.refs_0_), channel_id=1, source_target_pairs={{0,4},{4,0},{8,12},{12,8},{1,5},{5,1},{9,13},{13,9},{2,6},{6,2},{1... | collective-permute-start | bytes 368648 | tf_op jit(solution)/shard_map/ppermute | solution.py:619
  8.2 15.1 %collective-permute-start.5 = (bf16[1,64,512]{2,1,0:T(8,128)(2,1)}, bf16[1,64,512]{2,1,0:T(8,128)(2,1)S(1)}, u32[]{:S(2)}, u32[]{:S(2)}) collective-permute-start(bf16[1,64,512]{2,1,0:T(8,128)(2,1)} %refs_0_.2), channel_id=1, source_target_pairs={{0,4},{4,0},{8,12},{12,8},{1,5},{5,1},{9,13},{13,9},{2,6},{6,2},{1... | collective-permute-start | bytes 196616 | tf_op jit(solution)/shard_map/ppermute | solution.py:619
  10.0 1.6 %copy-start = (bf16[512,2048]{1,0:T(8,128)(2,1)S(1)}, bf16[512,2048]{1,0:T(8,128)(2,1)}, u32[]{:S(2)}) copy-start(bf16[512,2048]{1,0:T(8,128)(2,1)} %source_ref) | copy-start | bytes 6291460
  11.6 7.5 %copy-start.1 = (bf16[120,512]{1,0:T(8,128)(2,1)S(1)}, bf16[120,512]{1,0:T(8,128)(2,1)}, u32[]{:S(2)}) copy-start(bf16[120,512]{1,0:T(8,128)(2,1)} %shard_map.121.refs_0_) | copy-start | bytes 368644
  16.3 7.7 %collective-permute-start.3 = (bf16[1,64,512]{2,1,0:T(8,128)(2,1)S(1)}, bf16[1,64,512]{2,1,0:T(8,128)(2,1)S(1)}, u32[]{:S(2)}, u32[]{:S(2)}) collective-permute-start(bf16[1,64,512]{2,1,0:T(8,128)(2,1)S(1)} %copy-done.2), channel_id=1, source_target_pairs={{0,8},{4,12},{8,0},{12,4},{1,9},{5,13},{9,1},{13,5},{2,10},{6,14},... | collective-permute-start | bytes 196616 | tf_op jit(solution)/shard_map/ppermute | solution.py:619
  16.3 7.7 %collective-permute-start.4 = (bf16[1,64,512]{2,1,0:T(8,128)(2,1)S(1)}, bf16[1,64,512]{2,1,0:T(8,128)(2,1)S(1)}, u32[]{:S(2)}, u32[]{:S(2)}) collective-permute-start(bf16[1,64,512]{2,1,0:T(8,128)(2,1)S(1)} %copy-done.2), channel_id=1, source_target_pairs={{0,12},{4,8},{8,4},{12,0},{1,13},{5,9},{9,5},{13,1},{2,14},{6,10},... | collective-permute-start | bytes 196616 | tf_op jit(solution)/shard_map/ppermute | solution.py:619
  25.7 2.0 %collective-permute-start.9 = (bf16[64,1024]{1,0:T(8,128)(2,1)S(1)}, bf16[64,1024]{1,0:T(8,128)(2,1)S(1)}, u32[]{:S(2)}, u32[]{:S(2)}) collective-permute-start(bf16[64,1024]{1,0:T(8,128)(2,1)S(1)} %get-tuple-element.60), channel_id=1, source_target_pairs={{0,1},{1,0},{2,3},{3,2},{4,5},{5,4},{6,7},{7,6},{8,9},{9,8},{10,11... | collective-permute-start | bytes 393224 | tf_op jit(solution)/shard_map/ppermute | solution.py:619
  25.7 10.4 %copy-start.3 = (s32[1,3,16]{2,0,1:T(1,128)S(1)}, s32[1,3,16]{2,0,1:T(1,128)}, u32[]{:S(2)}) copy-start(s32[1,3,16]{2,0,1:T(1,128)} %param.14) | copy-start | bytes 580
  27.1 2.2 %collective-permute-start.6 = (bf16[64,1024]{1,0:T(8,128)(2,1)S(1)}, bf16[64,1024]{1,0:T(8,128)(2,1)S(1)}, u32[]{:S(2)}, u32[]{:S(2)}) collective-permute-start(bf16[64,1024]{1,0:T(8,128)(2,1)S(1)} %get-tuple-element.58), channel_id=1, source_target_pairs={{0,1},{1,0},{2,3},{3,2},{4,5},{5,4},{6,7},{7,6},{8,9},{9,8},{10,11... | collective-permute-start | bytes 393224 | tf_op jit(solution)/shard_map/ppermute | solution.py:619
  27.7 6.4 %collective-permute-start.10 = (bf16[64,1024]{1,0:T(8,128)(2,1)S(1)}, bf16[64,1024]{1,0:T(8,128)(2,1)S(1)}, u32[]{:S(2)}, u32[]{:S(2)}) collective-permute-start(bf16[64,1024]{1,0:T(8,128)(2,1)S(1)} %add_convert_fusion.1), channel_id=1, source_target_pairs={{0,2},{1,3},{2,0},{3,1},{4,6},{5,7},{6,4},{7,5},{8,10},{9,11},{10,... | collective-permute-start | bytes 393224 | tf_op jit(solution)/shard_map/ppermute | solution.py:619
  29.3 6.7 %collective-permute-start.7 = (bf16[64,1024]{1,0:T(8,128)(2,1)S(1)}, bf16[64,1024]{1,0:T(8,128)(2,1)S(1)}, u32[]{:S(2)}, u32[]{:S(2)}) collective-permute-start(bf16[64,1024]{1,0:T(8,128)(2,1)S(1)} %add_convert_fusion.3), channel_id=1, source_target_pairs={{0,2},{1,3},{2,0},{3,1},{4,6},{5,7},{6,4},{7,5},{8,10},{9,11},{10,... | collective-permute-start | bytes 393224 | tf_op jit(solution)/shard_map/ppermute | solution.py:619
  34.1 3.0 %collective-permute-start.11 = (bf16[64,1024]{1,0:T(8,128)(2,1)S(1)}, bf16[64,1024]{1,0:T(8,128)(2,1)S(1)}, u32[]{:S(2)}, u32[]{:S(2)}) collective-permute-start(bf16[64,1024]{1,0:T(8,128)(2,1)S(1)} %add_convert_fusion.two_ref), channel_id=1, source_target_pairs={{0,1},{1,0},{2,3},{3,2},{4,5},{5,4},{6,7},{7,6},{8,9},{9,8},{10,11... | collective-permute-start | bytes 393224 | tf_op jit(solution)/shard_map/ppermute | solution.py:619
  36.0 1.4 %collective-permute-start.8 = (bf16[64,1024]{1,0:T(8,128)(2,1)S(1)}, bf16[64,1024]{1,0:T(8,128)(2,1)S(1)}, u32[]{:S(2)}, u32[]{:S(2)}) collective-permute-start(bf16[64,1024]{1,0:T(8,128)(2,1)S(1)} %add_convert_fusion.2.one_ref), channel_id=1, source_target_pairs={{0,1},{1,0},{2,3},{3,2},{4,5},{5,4},{6,7},{7,6},{8,9},{9,8},{10,11... | collective-permute-start | bytes 393224 | tf_op jit(solution)/shard_map/ppermute | solution.py:619

commit v8 on v7

--- a/solution.py
+++ b/solution.py
@@ -684,7 +684,7 @@
         10**8,
         fetched=1,
     )
-    packs[1], cotangent = lax.optimization_barrier((packs[1], cotangent))
+    near, cotangent = lax.optimization_barrier((near, cotangent))
     cotangents = [cotangent] + [swap(cotangent, "space", step) for step in steps[1:-1]] + [near]
     rows = regions * mesh_count
     slots = regions * mesh_cap

time: 38.6 us -> 40.7 us (1.054)
  waiting for transfers between devices: 10.7 us -> 12 us
  starting transfers between devices: 13.6 us -> 14.3 us
    ppermute x12, waiting for transfers between devices: 10.7 us -> 12 us  [swap(): lax.ppermute(block, axis, [(i, i ^ bits) for i in range(lax.axis_size(axi...]
    ppermute x12, starting transfers between devices: 13.6 us -> 14.3 us  [swap(): lax.ppermute(block, axis, [(i, i ^ bits) for i in range(lax.axis_size(axi...]
  transfers between devices with their start and end apart: 12 -> 12, of which waited for: 5 -> 5; matrix products, arithmetic and copies ran while one was open for 0% -> 0% of each run, Pallas kernels for 19% -> 18%
where the time goes in v8:
time: 40.7 us; the launch traced here: 40.5 us
  starting transfers between devices  14.3 us (35%)
  waiting for transfers between devices  12 us (29%)
  Pallas kernels  11.7 us (29%)
  local copies, waits for them, and re-layouts  1.61 us (4%)
  between operations  0.75 us (2%)
    ppermute x12, starting transfers between devices, swap(): lax.ppermute(block, axis, [(i, i ^ bits) for i in range(lax.axis_size(axi...  14.3 us
    ppermute x12, waiting for transfers between devices, swap(): lax.ppermute(block, axis, [(i, i ^ bits) for i in range(lax.axis_size(axi...  12 us
    pallas_call x7, Pallas kernels, call(): pl.pallas_call(kernel, out_shape=[jax.ShapeDtypeStruct(shape, kind) for s...  11.7 us
    unnamed x8, local copies, waits for them, and re-layouts  1.61 us
  transfers between devices with their start and end apart: 12, of which 5 were waited for; matrix products, arithmetic and copies ran while one was open for 0% of the time, Pallas kernels for 18%

profile of v8, /device:TPU:0, one launch (start us, length us, event | category | flops | bytes accessed | tf_op | source)
XLA Modules:
  0.0 40.5 jit_solution(11853988185519700445)
XLA Ops:
  0.6 0.0 copy-start.2
  0.6 1.9 %shard_map.121.refs_0_ = bf16[120,512]{1,0:T(8,128)(2,1)} custom-call(bf16[1,128,512]{2,1,0:T(8,128)(2,1)} %refs_0_.1, bf16[1,64,512]{2,1,0:T(8,128)(2,1)} %refs_1_.1, s32[3,1,16]{2,1,0:T(1,128)} %bitcast.5, s32[1,256]{1,0:T(1,128)} %bitcast.7, s32[1,256]{1,0:T(1,128)} %bitcast.8, s32[1,4,8]{2,1,0:T(4,128)} %refs_5_.1, s32[1,256]{1,0:T(1,128)} %bitcast.9, ...), custom_call_target="tpu_custom_call" | custom-call | flops 10000000 | bytes 4194304 | tf_op jit(solution)/shard_map/pallas_call | solution.py:606
  2.5 4.1 %collective-permute-start = (bf16[120,512]{1,0:T(8,128)(2,1)}, bf16[120,512]{1,0:T(8,128)(2,1)S(1)}, u32[]{:S(2)}, u32[]{:S(2)}) collective-permute-start(bf16[120,512]{1,0:T(8,128)(2,1)} %shard_map.121.refs_0_), channel_id=1, source_target_pairs={{0,8},{4,12},{8,0},{12,4},{1,9},{5,13},{9,1},{13,5},{2,10},{6,14},... | collective-permute-start | bytes 368648 | tf_op jit(solution)/shard_map/ppermute | solution.py:619
  6.6 1.3 %collective-permute-start.1 = (bf16[120,512]{1,0:T(8,128)(2,1)}, bf16[120,512]{1,0:T(8,128)(2,1)S(1)}, u32[]{:S(2)}, u32[]{:S(2)}) collective-permute-start(bf16[120,512]{1,0:T(8,128)(2,1)} %shard_map.121.refs_0_), channel_id=1, source_target_pairs={{0,12},{4,8},{8,4},{12,0},{1,13},{5,9},{9,5},{13,1},{2,14},{6,10},... | collective-permute-start | bytes 368648 | tf_op jit(solution)/shard_map/ppermute | solution.py:619
  8.0 0.2 collective-permute-start.2
  8.2 1.8 %collective-permute-start.3 = (bf16[1,64,512]{2,1,0:T(8,128)(2,1)}, bf16[1,64,512]{2,1,0:T(8,128)(2,1)S(1)}, u32[]{:S(2)}, u32[]{:S(2)}) collective-permute-start(bf16[1,64,512]{2,1,0:T(8,128)(2,1)} %refs_0_.2), channel_id=1, source_target_pairs={{0,4},{4,0},{8,12},{12,8},{1,5},{5,1},{9,13},{13,9},{2,6},{6,2},{1... | collective-permute-start | bytes 196616 | tf_op jit(solution)/shard_map/ppermute | solution.py:619
  10.0 1.6 %copy-done = bf16[512,2048]{1,0:T(8,128)(2,1)S(1)} copy-done((bf16[512,2048]{1,0:T(8,128)(2,1)S(1)}, bf16[512,2048]{1,0:T(8,128)(2,1)}, u32[]{:S(2)}) %copy-start) | copy-done | bytes 2097176
  11.6 0.6 %shard_map.122 = (bf16[512,2048]{1,0:T(8,128)(2,1)S(1)}, bf16[512,1536]{1,0:T(8,128)(2,1)S(1)}) custom-call(bf16[512,2048]{1,0:T(8,128)(2,1)S(1)} %copy-done), custom_call_target="tpu_custom_call" | custom-call | flops 100000000 | bytes 4194304 | tf_op jit(solution)/shard_map/pallas_call | solution.py:606
  12.2 6.0 %collective-permute-done.3.refs_3_ = bf16[1,64,512]{2,1,0:T(8,128)(2,1)S(1)} collective-permute-done((bf16[1,64,512]{2,1,0:T(8,128)(2,1)}, bf16[1,64,512]{2,1,0:T(8,128)(2,1)S(1)}, u32[]{:S(2)}, u32[]{:S(2)}) %collective-permute-start.3) | collective-permute-done | bytes 65568 | tf_op jit(solution)/shard_map/ppermute | solution.py:619
  18.2 1.7 %collective-permute-start.4 = (bf16[1,64,512]{2,1,0:T(8,128)(2,1)S(1)}, bf16[1,64,512]{2,1,0:T(8,128)(2,1)S(1)}, u32[]{:S(2)}, u32[]{:S(2)}) collective-permute-start(bf16[1,64,512]{2,1,0:T(8,128)(2,1)S(1)} %copy-done.2), channel_id=1, source_target_pairs={{0,8},{4,12},{8,0},{12,4},{1,9},{5,13},{9,1},{13,5},{2,10},{6,14},... | collective-permute-start | bytes 196616 | tf_op jit(solution)/shard_map/ppermute | solution.py:619
  19.9 1.8 %collective-permute-start.5 = (bf16[1,64,512]{2,1,0:T(8,128)(2,1)S(1)}, bf16[1,64,512]{2,1,0:T(8,128)(2,1)S(1)}, u32[]{:S(2)}, u32[]{:S(2)}) collective-permute-start(bf16[1,64,512]{2,1,0:T(8,128)(2,1)S(1)} %copy-done.2), channel_id=1, source_target_pairs={{0,12},{4,8},{8,4},{12,0},{1,13},{5,9},{9,5},{13,1},{2,14},{6,10},... | collective-permute-start | bytes 196616 | tf_op jit(solution)/shard_map/ppermute | solution.py:619
  21.8 0.0 collective-permute-done.refs_1_
  21.8 0.0 collective-permute-done.1.refs_2_
  21.8 0.0 collective-permute-done.2.refs_3_
  21.8 4.2 %shard_map.123 = (bf16[1,64,512]{2,1,0:T(8,128)(2,1)}, bf16[192,512]{1,0:T(8,128)(2,1)S(1)}, bf16[256,512]{1,0:T(8,128)(2,1)S(1)}, bf16[256,512]{1,0:T(8,128)(2,...) custom-call(bf16[120,512]{1,0:T(8,128)(2,1)S(1)} %copy-done.1, ...), custom_call_target="tpu_custom_call" | custom-call | flops 2000000000 | bytes 4194304 | tf_op jit(solution)/shard_map/pallas_call | solution.py:606
  26.0 0.1 collective-permute-done.5.refs_2_
  26.1 1.6 %shard_map.124 = (f32[256,512]{1,0:T(8,128)S(1)}, bf16[64,1024]{1,0:T(8,128)(2,1)S(1)}, bf16[64,1024]{1,0:T(8,128)(2,1)S(1)}) custom-call(bf16[1,64,512]{2,1,0:T(8,128)(2,1)S(1)} %copy-done.2, bf16[1,64,512]{2,1,0:T(8,128)(2,1)S(1)} %collective-permute-done.4.refs_1_, bf16[1,64,512]{2,1,0:T(8,128)(2,1)S(1)} %collective-permute-done.5.refs_2_, ...), custom_call_target="tpu_custom_call" | custom-call | flops 1000000000 | bytes 4194304 | tf_op jit(solution)/shard_map/pallas_call | solution.py:606
  27.7 0.1 collective-permute-start.9
  27.8 0.0 copy-start.3
  27.8 1.3 %shard_map.125 = (bf16[48,512]{1,0:T(8,128)(2,1)S(1)}, bf16[64,1024]{1,0:T(8,128)(2,1)S(1)}, bf16[64,1024]{1,0:T(8,128)(2,1)S(1)}) custom-call(bf16[192,512]{1,0:T(8,128)(2,1)S(1)} %get-tuple-element.37.grid_ref, bf16[256,512]{1,0:T(8,128)(2,1)S(1)} %get-tuple-element.38.mesh_ref, bf16[448,256]{1,0:T(8,128)(2,1)S(1)} %get-tuple-element.39.hot_ref, ...), custom_call_target="tpu_custom_call" | custom-call | flops 1000000000 | bytes 4194304 | tf_op jit(solution)/shard_map/pallas_call | solution.py:606
  29.1 0.6 %collective-permute-start.6 = (bf16[64,1024]{1,0:T(8,128)(2,1)S(1)}, bf16[64,1024]{1,0:T(8,128)(2,1)S(1)}, u32[]{:S(2)}, u32[]{:S(2)}) collective-permute-start(bf16[64,1024]{1,0:T(8,128)(2,1)S(1)} %get-tuple-element.58), channel_id=1, source_target_pairs={{0,1},{1,0},{2,3},{3,2},{4,5},{5,4},{6,7},{7,6},{8,9},{9,8},{10,11... | collective-permute-start | bytes 393224 | tf_op jit(solution)/shard_map/ppermute | solution.py:619
  29.7 0.0 collective-permute-done.9
  29.7 1.5 %collective-permute-start.10 = (bf16[64,1024]{1,0:T(8,128)(2,1)S(1)}, bf16[64,1024]{1,0:T(8,128)(2,1)S(1)}, u32[]{:S(2)}, u32[]{:S(2)}) collective-permute-start(bf16[64,1024]{1,0:T(8,128)(2,1)S(1)} %add_convert_fusion.1), channel_id=1, source_target_pairs={{0,2},{1,3},{2,0},{3,1},{4,6},{5,7},{6,4},{7,5},{8,10},{9,11},{10,... | collective-permute-start | bytes 393224 | tf_op jit(solution)/shard_map/ppermute | solution.py:619
  31.3 1.0 %collective-permute-start.7 = (bf16[64,1024]{1,0:T(8,128)(2,1)S(1)}, bf16[64,1024]{1,0:T(8,128)(2,1)S(1)}, u32[]{:S(2)}, u32[]{:S(2)}) collective-permute-start(bf16[64,1024]{1,0:T(8,128)(2,1)S(1)} %add_convert_fusion.3), channel_id=1, source_target_pairs={{0,2},{1,3},{2,0},{3,1},{4,6},{5,7},{6,4},{7,5},{8,10},{9,11},{10,... | collective-permute-start | bytes 393224 | tf_op jit(solution)/shard_map/ppermute | solution.py:619
  32.3 3.9 %collective-permute-done.10 = bf16[64,1024]{1,0:T(8,128)(2,1)S(1)} collective-permute-done((bf16[64,1024]{1,0:T(8,128)(2,1)S(1)}, bf16[64,1024]{1,0:T(8,128)(2,1)S(1)}, u32[]{:S(2)}, u32[]{:S(2)}) %collective-permute-start.10) | collective-permute-done | bytes 131104 | tf_op jit(solution)/shard_map/ppermute | solution.py:619
  36.2 0.1 collective-permute-start.11
  36.3 1.8 %collective-permute-done.7 = bf16[64,1024]{1,0:T(8,128)(2,1)S(1)} collective-permute-done((bf16[64,1024]{1,0:T(8,128)(2,1)S(1)}, bf16[64,1024]{1,0:T(8,128)(2,1)S(1)}, u32[]{:S(2)}, u32[]{:S(2)}) %collective-permute-start.7) | collective-permute-done | bytes 131104 | tf_op jit(solution)/shard_map/ppermute | solution.py:619
  38.1 0.1 collective-permute-start.8
  38.2 1.1 %shard_map.126 = bf16[1,128,512]{2,1,0:T(8,128)(2,1)} custom-call(bf16[512,1536]{1,0:T(8,128)(2,1)S(1)} %get-tuple-element.36.refs_4_.turned_ref, s32[3,1,16]{2,1,0:T(1,128)S(1)} %bitcast.6, bf16[48,512]{1,0:T(8,128)(2,1)S(1)} %get-tuple-element.56.own_slot_ref), custom_call_target="tpu_custom_call" | custom-call | flops 100000000 | bytes 4194304 | tf_op jit(solution)/shard_map/pallas_call | solution.py:606
  39.2 0.0 collective-permute-done.11.other_two_ref
  39.2 0.2 collective-permute-done.8.other_one_ref
  39.5 1.0 %shard_map.127 = f32[128,2048]{1,0:T(8,128)} custom-call(bf16[64,1024]{1,0:T(8,128)(2,1)S(1)} %add_convert_fusion.2.one_ref, bf16[64,1024]{1,0:T(8,128)(2,1)S(1)} %collective-permute-done.8.other_one_ref, bf16[64,1024]{1,0:T(8,128)(2,1)S(1)} %add_convert_fusion.two_ref, bf16[64,1024]{1,0:T(8,128)(2,1)S(1)} %collective-permute-done.11.other_two_ref), custom_call_target="tpu_custom_call" | custom-call | flops 1000000 | bytes 4194304 | tf_op jit(solution)/shard_map/pallas_call | solution.py:606
  (11 shorter events, 0.2 us)
Async XLA Ops:
  0.6 17.6 %copy-start.2 = (bf16[1,64,512]{2,1,0:T(8,128)(2,1)S(1)}, bf16[1,64,512]{2,1,0:T(8,128)(2,1)}, u32[]{:S(2)}) copy-start(bf16[1,64,512]{2,1,0:T(8,128)(2,1)} %refs_0_.2) | copy-start | bytes 196612
  2.5 19.2 %collective-permute-start = (bf16[120,512]{1,0:T(8,128)(2,1)}, bf16[120,512]{1,0:T(8,128)(2,1)S(1)}, u32[]{:S(2)}, u32[]{:S(2)}) collective-permute-start(bf16[120,512]{1,0:T(8,128)(2,1)} %shard_map.121.refs_0_), channel_id=1, source_target_pairs={{0,8},{4,12},{8,0},{12,4},{1,9},{5,13},{9,1},{13,5},{2,10},{6,14},... | collective-permute-start | bytes 368648 | tf_op jit(solution)/shard_map/ppermute | solution.py:619
  6.6 15.1 %collective-permute-start.1 = (bf16[120,512]{1,0:T(8,128)(2,1)}, bf16[120,512]{1,0:T(8,128)(2,1)S(1)}, u32[]{:S(2)}, u32[]{:S(2)}) collective-permute-start(bf16[120,512]{1,0:T(8,128)(2,1)} %shard_map.121.refs_0_), channel_id=1, source_target_pairs={{0,12},{4,8},{8,4},{12,0},{1,13},{5,9},{9,5},{13,1},{2,14},{6,10},... | collective-permute-start | bytes 368648 | tf_op jit(solution)/shard_map/ppermute | solution.py:619
  8.0 13.8 %collective-permute-start.2 = (bf16[120,512]{1,0:T(8,128)(2,1)}, bf16[120,512]{1,0:T(8,128)(2,1)S(1)}, u32[]{:S(2)}, u32[]{:S(2)}) collective-permute-start(bf16[120,512]{1,0:T(8,128)(2,1)} %shard_map.121.refs_0_), channel_id=1, source_target_pairs={{0,4},{4,0},{8,12},{12,8},{1,5},{5,1},{9,13},{13,9},{2,6},{6,2},{1... | collective-permute-start | bytes 368648 | tf_op jit(solution)/shard_map/ppermute | solution.py:619
  8.2 10.0 %collective-permute-start.3 = (bf16[1,64,512]{2,1,0:T(8,128)(2,1)}, bf16[1,64,512]{2,1,0:T(8,128)(2,1)S(1)}, u32[]{:S(2)}, u32[]{:S(2)}) collective-permute-start(bf16[1,64,512]{2,1,0:T(8,128)(2,1)} %refs_0_.2), channel_id=1, source_target_pairs={{0,4},{4,0},{8,12},{12,8},{1,5},{5,1},{9,13},{13,9},{2,6},{6,2},{1... | collective-permute-start | bytes 196616 | tf_op jit(solution)/shard_map/ppermute | solution.py:619
  10.0 1.6 %copy-start = (bf16[512,2048]{1,0:T(8,128)(2,1)S(1)}, bf16[512,2048]{1,0:T(8,128)(2,1)}, u32[]{:S(2)}) copy-start(bf16[512,2048]{1,0:T(8,128)(2,1)} %source_ref) | copy-start | bytes 6291460
  11.6 10.2 %copy-start.1 = (bf16[120,512]{1,0:T(8,128)(2,1)S(1)}, bf16[120,512]{1,0:T(8,128)(2,1)}, u32[]{:S(2)}) copy-start(bf16[120,512]{1,0:T(8,128)(2,1)} %shard_map.121.refs_0_) | copy-start | bytes 368644
  18.2 7.7 %collective-permute-start.4 = (bf16[1,64,512]{2,1,0:T(8,128)(2,1)S(1)}, bf16[1,64,512]{2,1,0:T(8,128)(2,1)S(1)}, u32[]{:S(2)}, u32[]{:S(2)}) collective-permute-start(bf16[1,64,512]{2,1,0:T(8,128)(2,1)S(1)} %copy-done.2), channel_id=1, source_target_pairs={{0,8},{4,12},{8,0},{12,4},{1,9},{5,13},{9,1},{13,5},{2,10},{6,14},... | collective-permute-start | bytes 196616 | tf_op jit(solution)/shard_map/ppermute | solution.py:619
  19.9 6.2 %collective-permute-start.5 = (bf16[1,64,512]{2,1,0:T(8,128)(2,1)S(1)}, bf16[1,64,512]{2,1,0:T(8,128)(2,1)S(1)}, u32[]{:S(2)}, u32[]{:S(2)}) collective-permute-start(bf16[1,64,512]{2,1,0:T(8,128)(2,1)S(1)} %copy-done.2), channel_id=1, source_target_pairs={{0,12},{4,8},{8,4},{12,0},{1,13},{5,9},{9,5},{13,1},{2,14},{6,10},... | collective-permute-start | bytes 196616 | tf_op jit(solution)/shard_map/ppermute | solution.py:619
  27.7 2.0 %collective-permute-start.9 = (bf16[64,1024]{1,0:T(8,128)(2,1)S(1)}, bf16[64,1024]{1,0:T(8,128)(2,1)S(1)}, u32[]{:S(2)}, u32[]{:S(2)}) collective-permute-start(bf16[64,1024]{1,0:T(8,128)(2,1)S(1)} %get-tuple-element.60), channel_id=1, source_target_pairs={{0,1},{1,0},{2,3},{3,2},{4,5},{5,4},{6,7},{7,6},{8,9},{9,8},{10,11... | collective-permute-start | bytes 393224 | tf_op jit(solution)/shard_map/ppermute | solution.py:619
  27.8 10.4 %copy-start.3 = (s32[1,3,16]{2,0,1:T(1,128)S(1)}, s32[1,3,16]{2,0,1:T(1,128)}, u32[]{:S(2)}) copy-start(s32[1,3,16]{2,0,1:T(1,128)} %param.14) | copy-start | bytes 580
  29.1 2.1 %collective-permute-start.6 = (bf16[64,1024]{1,0:T(8,128)(2,1)S(1)}, bf16[64,1024]{1,0:T(8,128)(2,1)S(1)}, u32[]{:S(2)}, u32[]{:S(2)}) collective-permute-start(bf16[64,1024]{1,0:T(8,128)(2,1)S(1)} %get-tuple-element.58), channel_id=1, source_target_pairs={{0,1},{1,0},{2,3},{3,2},{4,5},{5,4},{6,7},{7,6},{8,9},{9,8},{10,11... | collective-permute-start | bytes 393224 | tf_op jit(solution)/shard_map/ppermute | solution.py:619
  29.7 6.4 %collective-permute-start.10 = (bf16[64,1024]{1,0:T(8,128)(2,1)S(1)}, bf16[64,1024]{1,0:T(8,128)(2,1)S(1)}, u32[]{:S(2)}, u32[]{:S(2)}) collective-permute-start(bf16[64,1024]{1,0:T(8,128)(2,1)S(1)} %add_convert_fusion.1), channel_id=1, source_target_pairs={{0,2},{1,3},{2,0},{3,1},{4,6},{5,7},{6,4},{7,5},{8,10},{9,11},{10,... | collective-permute-start | bytes 393224 | tf_op jit(solution)/shard_map/ppermute | solution.py:619
  31.3 6.7 %collective-permute-start.7 = (bf16[64,1024]{1,0:T(8,128)(2,1)S(1)}, bf16[64,1024]{1,0:T(8,128)(2,1)S(1)}, u32[]{:S(2)}, u32[]{:S(2)}) collective-permute-start(bf16[64,1024]{1,0:T(8,128)(2,1)S(1)} %add_convert_fusion.3), channel_id=1, source_target_pairs={{0,2},{1,3},{2,0},{3,1},{4,6},{5,7},{6,4},{7,5},{8,10},{9,11},{10,... | collective-permute-start | bytes 393224 | tf_op jit(solution)/shard_map/ppermute | solution.py:619
  36.2 3.0 %collective-permute-start.11 = (bf16[64,1024]{1,0:T(8,128)(2,1)S(1)}, bf16[64,1024]{1,0:T(8,128)(2,1)S(1)}, u32[]{:S(2)}, u32[]{:S(2)}) collective-permute-start(bf16[64,1024]{1,0:T(8,128)(2,1)S(1)} %add_convert_fusion.two_ref), channel_id=1, source_target_pairs={{0,1},{1,0},{2,3},{3,2},{4,5},{5,4},{6,7},{7,6},{8,9},{9,8},{10,11... | collective-permute-start | bytes 393224 | tf_op jit(solution)/shard_map/ppermute | solution.py:619
  38.1 1.4 %collective-permute-start.8 = (bf16[64,1024]{1,0:T(8,128)(2,1)S(1)}, bf16[64,1024]{1,0:T(8,128)(2,1)S(1)}, u32[]{:S(2)}, u32[]{:S(2)}) collective-permute-start(bf16[64,1024]{1,0:T(8,128)(2,1)S(1)} %add_convert_fusion.2.one_ref), channel_id=1, source_target_pairs={{0,1},{1,0},{2,3},{3,2},{4,5},{5,4},{6,7},{7,6},{8,9},{9,8},{10,11... | collective-permute-start | bytes 393224 | tf_op jit(solution)/shard_map/ppermute | solution.py:619

commit v9 on v7

--- a/solution.py
+++ b/solution.py
@@ -356,7 +356,7 @@
     slots = regions * mesh_cap
     me = lax.axis_index("space")
     for step, packed_ref in zip(steps, packed_refs):
-        region = lax.bitwise_xor(me, step)
+        region = lax.rem(me + (regions - step), regions)
         at = lambda rows: pl.ds(pl.multiple_of(region * rows, rows), rows)
         grid_ref[at(listed), :] = packed_ref[:listed, :]
         mesh_ref[at(mesh_count), :] = packed_ref[listed : listed + mesh_count, :]
@@ -501,7 +501,7 @@
     slots = regions * mesh_cap
     me = lax.axis_index("space")
     for step, cotangent_ref in zip(steps, cotangent_refs):
-        region = lax.bitwise_xor(me, step)
+        region = lax.rem(me + (regions - step), regions)
         at = pl.ds(pl.multiple_of(region * mesh_count, mesh_count), mesh_count)
         upstream_ref[at, :] = cotangent_ref[0].astype(F32)
     agg_grad = moments_back(normed_ref[...], scaled_ref[:, 0:1], upstream_ref[...]).astype(BF16)
@@ -617,6 +617,11 @@
 
 def swap(block, axis, bits):
     return lax.ppermute(block, axis, [(i, i ^ bits) for i in range(lax.axis_size(axis))])
+
+
+def shifted(block, step):
+    count = lax.axis_size("space")
+    return lax.ppermute(block, "space", [(i, (i + step) % count) for i in range(count)])
 
 
 def added(left, right):
@@ -673,9 +678,8 @@
         megabytes=56,
     )[0]
     packed, cotangent, weights = lax.optimization_barrier((packed, mesh_cotangent, weights))
-    steps = (0, *range(2, regions), 1)
-    packs = [packed] + [swap(packed, "space", step) for step in steps[1:]]
-    near = swap(cotangent, "space", 1)
+    steps = (0, *sorted(range(1, regions), key=lambda step: -min(step, regions - step)))
+    packs = [packed] + [shifted(packed, step) for step in steps[1:]]
     weights, turned = call(
         weights_kernel,
         (weights,),
@@ -685,7 +689,7 @@
         fetched=1,
     )
     packs[1], cotangent = lax.optimization_barrier((packs[1], cotangent))
-    cotangents = [cotangent] + [swap(cotangent, "space", step) for step in steps[1:-1]] + [near]
+    cotangents = [cotangent] + [shifted(cotangent, step) for step in steps[1:]]
     rows = regions * mesh_count
     slots = regions * mesh_cap
     (
@@ -803,7 +807,7 @@
         edges = arguments[5].shape[0] + arguments[8].shape[0]
         latent = arguments[3].shape[0]
         fits = edges * latent * 4 <= SAMPLE_EDGE_BYTES and latent % (128 * regions) == 0
-        paired = all(n > 1 and n & (n - 1) == 0 for n in (regions, samples))
+        paired = regions > 1 and samples > 1 and samples & (samples - 1) == 0
         return sharded(whole_sample_body if fits and paired else partitioned_body)(*arguments)
 
     def sharded(body):

time: 38.6 us -> 39.1 us (1.013)
  starting transfers between devices: 13.6 us -> 15.3 us
  waiting for transfers between devices: 10.7 us -> 9.28 us
    ppermute x0 -> x6, starting transfers between devices: none -> 11.8 us  [shifted(): lax.ppermute(block, 'space', [(i, (i + step) % count) for i in range(coun...]
    ppermute x12 -> x6, starting transfers between devices: 13.6 us -> 3.59 us  [swap(): lax.ppermute(block, axis, [(i, i ^ bits) for i in range(lax.axis_size(axi...]
    ppermute x12 -> x6, waiting for transfers between devices: 10.7 us -> 5.63 us  [swap(): lax.ppermute(block, axis, [(i, i ^ bits) for i in range(lax.axis_size(axi...]
    ppermute x0 -> x6, waiting for transfers between devices: none -> 3.65 us  [shifted(): lax.ppermute(block, 'space', [(i, (i + step) % count) for i in range(coun...]
  transfers between devices with their start and end apart: 12 -> 12, of which waited for: 5 -> 4; matrix products, arithmetic and copies ran while one was open for 0% -> 0% of each run, Pallas kernels for 19% -> 19%
where the time goes in v9:
time: 39.1 us; the launch traced here: 38.9 us
  starting transfers between devices  15.3 us (39%)
  Pallas kernels  11.8 us (30%)
  waiting for transfers between devices  9.28 us (24%)
  local copies, waits for them, and re-layouts  1.6 us (4%)
  between operations  0.74 us (2%)
    pallas_call x7, Pallas kernels, call(): pl.pallas_call(kernel, out_shape=[jax.ShapeDtypeStruct(shape, kind) for s...  11.8 us
    ppermute x6, starting transfers between devices, shifted(): lax.ppermute(block, 'space', [(i, (i + step) % count) for i in range(coun...  11.8 us
    ppermute x6, waiting for transfers between devices, swap(): lax.ppermute(block, axis, [(i, i ^ bits) for i in range(lax.axis_size(axi...  5.63 us
    ppermute x6, waiting for transfers between devices, shifted(): lax.ppermute(block, 'space', [(i, (i + step) % count) for i in range(coun...  3.65 us
    ppermute x6, starting transfers between devices, swap(): lax.ppermute(block, axis, [(i, i ^ bits) for i in range(lax.axis_size(axi...  3.59 us
    unnamed x8, local copies, waits for them, and re-layouts  1.6 us
  transfers between devices with their start and end apart: 12, of which 4 were waited for; matrix products, arithmetic and copies ran while one was open for 0% of the time, Pallas kernels for 19%

profile of v9, /device:TPU:0, one launch (start us, length us, event | category | flops | bytes accessed | tf_op | source)
XLA Modules:
  0.0 38.9 jit_solution(10495670165253385486)
XLA Ops:
  0.6 1.9 %shard_map.121.refs_0_ = bf16[120,512]{1,0:T(8,128)(2,1)} custom-call(bf16[1,128,512]{2,1,0:T(8,128)(2,1)} %refs_0_.1, bf16[1,64,512]{2,1,0:T(8,128)(2,1)} %refs_1_.1, s32[3,1,16]{2,1,0:T(1,128)} %bitcast.5, s32[1,256]{1,0:T(1,128)} %bitcast.7, s32[1,256]{1,0:T(1,128)} %bitcast.8, s32[1,4,8]{2,1,0:T(4,128)} %refs_5_.1, s32[1,256]{1,0:T(1,128)} %bitcast.9, ...), custom_call_target="tpu_custom_call" | custom-call | flops 10000000 | bytes 4194304 | tf_op jit(solution)/shard_map/pallas_call | solution.py:606
  2.5 4.1 %collective-permute-start = (bf16[120,512]{1,0:T(8,128)(2,1)}, bf16[120,512]{1,0:T(8,128)(2,1)S(1)}, u32[]{:S(2)}, u32[]{:S(2)}) collective-permute-start(bf16[120,512]{1,0:T(8,128)(2,1)} %shard_map.121.refs_0_), channel_id=1, source_target_pairs={{0,8},{4,12},{8,0},{12,4},{1,9},{5,13},{9,1},{13,5},{2,10},{6,14},... | collective-permute-start | bytes 368648 | tf_op jit(solution)/shard_map/ppermute | solution.py:624
  6.6 1.6 %collective-permute-start.1 = (bf16[120,512]{1,0:T(8,128)(2,1)}, bf16[120,512]{1,0:T(8,128)(2,1)S(1)}, u32[]{:S(2)}, u32[]{:S(2)}) collective-permute-start(bf16[120,512]{1,0:T(8,128)(2,1)} %shard_map.121.refs_0_), channel_id=1, source_target_pairs={{0,4},{4,8},{8,12},{12,0},{1,5},{5,9},{9,13},{13,1},{2,6},{6,10},{... | collective-permute-start | bytes 368648 | tf_op jit(solution)/shard_map/ppermute | solution.py:624
  8.2 2.2 %collective-permute-start.2 = (bf16[120,512]{1,0:T(8,128)(2,1)}, bf16[120,512]{1,0:T(8,128)(2,1)S(1)}, u32[]{:S(2)}, u32[]{:S(2)}) collective-permute-start(bf16[120,512]{1,0:T(8,128)(2,1)} %shard_map.121.refs_0_), channel_id=1, source_target_pairs={{0,12},{4,0},{8,4},{12,8},{1,13},{5,1},{9,5},{13,9},{2,14},{6,2},{... | collective-permute-start | bytes 368648 | tf_op jit(solution)/shard_map/ppermute | solution.py:624
  10.5 1.6 %copy-done = bf16[512,2048]{1,0:T(8,128)(2,1)S(1)} copy-done((bf16[512,2048]{1,0:T(8,128)(2,1)S(1)}, bf16[512,2048]{1,0:T(8,128)(2,1)}, u32[]{:S(2)}) %copy-start) | copy-done | bytes 2097176
  12.1 0.6 %shard_map.122 = (bf16[512,2048]{1,0:T(8,128)(2,1)S(1)}, bf16[512,1536]{1,0:T(8,128)(2,1)S(1)}) custom-call(bf16[512,2048]{1,0:T(8,128)(2,1)S(1)} %copy-done), custom_call_target="tpu_custom_call" | custom-call | flops 100000000 | bytes 4194304 | tf_op jit(solution)/shard_map/pallas_call | solution.py:606
  12.7 3.6 %collective-permute-done.refs_1_ = bf16[120,512]{1,0:T(8,128)(2,1)S(1)} collective-permute-done((bf16[120,512]{1,0:T(8,128)(2,1)}, bf16[120,512]{1,0:T(8,128)(2,1)S(1)}, u32[]{:S(2)}, u32[]{:S(2)}) %collective-permute-start) | collective-permute-done | bytes 122912 | tf_op jit(solution)/shard_map/ppermute | solution.py:624
  16.3 0.0 collective-permute-start.3
  16.3 3.3 %collective-permute-start.4 = (bf16[1,64,512]{2,1,0:T(8,128)(2,1)S(1)}, bf16[1,64,512]{2,1,0:T(8,128)(2,1)S(1)}, u32[]{:S(2)}, u32[]{:S(2)}) collective-permute-start(bf16[1,64,512]{2,1,0:T(8,128)(2,1)S(1)} %copy-done.2), channel_id=1, source_target_pairs={{0,4},{4,8},{8,12},{12,0},{1,5},{5,9},{9,13},{13,1},{2,6},{6,10},{... | collective-permute-start | bytes 196616 | tf_op jit(solution)/shard_map/ppermute | solution.py:624
  19.6 0.5 %collective-permute-start.5 = (bf16[1,64,512]{2,1,0:T(8,128)(2,1)S(1)}, bf16[1,64,512]{2,1,0:T(8,128)(2,1)S(1)}, u32[]{:S(2)}, u32[]{:S(2)}) collective-permute-start(bf16[1,64,512]{2,1,0:T(8,128)(2,1)S(1)} %copy-done.2), channel_id=1, source_target_pairs={{0,12},{4,0},{8,4},{12,8},{1,13},{5,1},{9,5},{13,9},{2,14},{6,2},{... | collective-permute-start | bytes 196616 | tf_op jit(solution)/shard_map/ppermute | solution.py:624
  20.1 0.0 collective-permute-done.1.refs_2_
  20.2 0.0 collective-permute-done.2.refs_3_
  20.2 4.2 %shard_map.123 = (bf16[1,64,512]{2,1,0:T(8,128)(2,1)}, bf16[192,512]{1,0:T(8,128)(2,1)S(1)}, bf16[256,512]{1,0:T(8,128)(2,1)S(1)}, bf16[256,512]{1,0:T(8,128)(2,...) custom-call(bf16[120,512]{1,0:T(8,128)(2,1)S(1)} %copy-done.1, ...), custom_call_target="tpu_custom_call" | custom-call | flops 2000000000 | bytes 4194304 | tf_op jit(solution)/shard_map/pallas_call | solution.py:606
  24.4 0.0 collective-permute-done.3.refs_1_
  24.4 0.0 collective-permute-done.4.refs_2_
  24.4 0.0 collective-permute-done.5.refs_3_
  24.4 1.7 %shard_map.124 = (f32[256,512]{1,0:T(8,128)S(1)}, bf16[64,1024]{1,0:T(8,128)(2,1)S(1)}, bf16[64,1024]{1,0:T(8,128)(2,1)S(1)}) custom-call(bf16[1,64,512]{2,1,0:T(8,128)(2,1)S(1)} %copy-done.2, bf16[1,64,512]{2,1,0:T(8,128)(2,1)S(1)} %collective-permute-done.3.refs_1_, bf16[1,64,512]{2,1,0:T(8,128)(2,1)S(1)} %collective-permute-done.4.refs_2_, ...), custom_call_target="tpu_custom_call" | custom-call | flops 1000000000 | bytes 4194304 | tf_op jit(solution)/shard_map/pallas_call | solution.py:606
  26.0 0.1 collective-permute-start.9
  26.1 0.0 copy-start.3
  26.1 1.3 %shard_map.125 = (bf16[48,512]{1,0:T(8,128)(2,1)S(1)}, bf16[64,1024]{1,0:T(8,128)(2,1)S(1)}, bf16[64,1024]{1,0:T(8,128)(2,1)S(1)}) custom-call(bf16[192,512]{1,0:T(8,128)(2,1)S(1)} %get-tuple-element.39.grid_ref, bf16[256,512]{1,0:T(8,128)(2,1)S(1)} %get-tuple-element.40.mesh_ref, bf16[448,256]{1,0:T(8,128)(2,1)S(1)} %get-tuple-element.41.hot_ref, ...), custom_call_target="tpu_custom_call" | custom-call | flops 1000000000 | bytes 4194304 | tf_op jit(solution)/shard_map/pallas_call | solution.py:606
  27.5 0.6 %collective-permute-start.6 = (bf16[64,1024]{1,0:T(8,128)(2,1)S(1)}, bf16[64,1024]{1,0:T(8,128)(2,1)S(1)}, u32[]{:S(2)}, u32[]{:S(2)}) collective-permute-start(bf16[64,1024]{1,0:T(8,128)(2,1)S(1)} %get-tuple-element.58), channel_id=1, source_target_pairs={{0,1},{1,0},{2,3},{3,2},{4,5},{5,4},{6,7},{7,6},{8,9},{9,8},{10,11... | collective-permute-start | bytes 393224 | tf_op jit(solution)/shard_map/ppermute | solution.py:619
  28.0 0.0 collective-permute-done.9
  28.1 1.9 %collective-permute-start.10 = (bf16[64,1024]{1,0:T(8,128)(2,1)S(1)}, bf16[64,1024]{1,0:T(8,128)(2,1)S(1)}, u32[]{:S(2)}, u32[]{:S(2)}) collective-permute-start(bf16[64,1024]{1,0:T(8,128)(2,1)S(1)} %add_convert_fusion.1), channel_id=1, source_target_pairs={{0,2},{1,3},{2,0},{3,1},{4,6},{5,7},{6,4},{7,5},{8,10},{9,11},{10,... | collective-permute-start | bytes 393224 | tf_op jit(solution)/shard_map/ppermute | solution.py:619
  29.9 0.0 collective-permute-done.6
  30.0 1.0 %collective-permute-start.7 = (bf16[64,1024]{1,0:T(8,128)(2,1)S(1)}, bf16[64,1024]{1,0:T(8,128)(2,1)S(1)}, u32[]{:S(2)}, u32[]{:S(2)}) collective-permute-start(bf16[64,1024]{1,0:T(8,128)(2,1)S(1)} %add_convert_fusion.3), channel_id=1, source_target_pairs={{0,2},{1,3},{2,0},{3,1},{4,6},{5,7},{6,4},{7,5},{8,10},{9,11},{10,... | collective-permute-start | bytes 393224 | tf_op jit(solution)/shard_map/ppermute | solution.py:619
  30.9 3.5 %collective-permute-done.10 = bf16[64,1024]{1,0:T(8,128)(2,1)S(1)} collective-permute-done((bf16[64,1024]{1,0:T(8,128)(2,1)S(1)}, bf16[64,1024]{1,0:T(8,128)(2,1)S(1)}, u32[]{:S(2)}, u32[]{:S(2)}) %collective-permute-start.10) | collective-permute-done | bytes 131104 | tf_op jit(solution)/shard_map/ppermute | solution.py:619
  34.5 0.1 collective-permute-start.11
  34.6 1.8 %collective-permute-done.7 = bf16[64,1024]{1,0:T(8,128)(2,1)S(1)} collective-permute-done((bf16[64,1024]{1,0:T(8,128)(2,1)S(1)}, bf16[64,1024]{1,0:T(8,128)(2,1)S(1)}, u32[]{:S(2)}, u32[]{:S(2)}) %collective-permute-start.7) | collective-permute-done | bytes 131104 | tf_op jit(solution)/shard_map/ppermute | solution.py:619
  36.5 0.1 collective-permute-start.8
  36.6 1.1 %shard_map.126 = bf16[1,128,512]{2,1,0:T(8,128)(2,1)} custom-call(bf16[512,1536]{1,0:T(8,128)(2,1)S(1)} %get-tuple-element.38.refs_4_.turned_ref, s32[3,1,16]{2,1,0:T(1,128)S(1)} %bitcast.6, bf16[48,512]{1,0:T(8,128)(2,1)S(1)} %get-tuple-element.56.own_slot_ref), custom_call_target="tpu_custom_call" | custom-call | flops 100000000 | bytes 4194304 | tf_op jit(solution)/shard_map/pallas_call | solution.py:606
  37.6 0.2 collective-permute-done.8.other_one_ref
  37.9 1.0 %shard_map.127 = f32[128,2048]{1,0:T(8,128)} custom-call(bf16[64,1024]{1,0:T(8,128)(2,1)S(1)} %add_convert_fusion.2.one_ref, bf16[64,1024]{1,0:T(8,128)(2,1)S(1)} %collective-permute-done.8.other_one_ref, bf16[64,1024]{1,0:T(8,128)(2,1)S(1)} %add_convert_fusion.two_ref, bf16[64,1024]{1,0:T(8,128)(2,1)S(1)} %collective-permute-done.11.other_two_ref), custom_call_target="tpu_custom_call" | custom-call | flops 1000000 | bytes 4194304 | tf_op jit(solution)/shard_map/pallas_call | solution.py:606
  (11 shorter events, 0.2 us)
Async XLA Ops:
  0.6 15.7 %copy-start.2 = (bf16[1,64,512]{2,1,0:T(8,128)(2,1)S(1)}, bf16[1,64,512]{2,1,0:T(8,128)(2,1)}, u32[]{:S(2)}) copy-start(bf16[1,64,512]{2,1,0:T(8,128)(2,1)} %refs_0_.2) | copy-start | bytes 196612
  2.5 13.8 %collective-permute-start = (bf16[120,512]{1,0:T(8,128)(2,1)}, bf16[120,512]{1,0:T(8,128)(2,1)S(1)}, u32[]{:S(2)}, u32[]{:S(2)}) collective-permute-start(bf16[120,512]{1,0:T(8,128)(2,1)} %shard_map.121.refs_0_), channel_id=1, source_target_pairs={{0,8},{4,12},{8,0},{12,4},{1,9},{5,13},{9,1},{13,5},{2,10},{6,14},... | collective-permute-start | bytes 368648 | tf_op jit(solution)/shard_map/ppermute | solution.py:624
  6.6 13.5 %collective-permute-start.1 = (bf16[120,512]{1,0:T(8,128)(2,1)}, bf16[120,512]{1,0:T(8,128)(2,1)S(1)}, u32[]{:S(2)}, u32[]{:S(2)}) collective-permute-start(bf16[120,512]{1,0:T(8,128)(2,1)} %shard_map.121.refs_0_), channel_id=1, source_target_pairs={{0,4},{4,8},{8,12},{12,0},{1,5},{5,9},{9,13},{13,1},{2,6},{6,10},{... | collective-permute-start | bytes 368648 | tf_op jit(solution)/shard_map/ppermute | solution.py:624
  8.2 11.9 %collective-permute-start.2 = (bf16[120,512]{1,0:T(8,128)(2,1)}, bf16[120,512]{1,0:T(8,128)(2,1)S(1)}, u32[]{:S(2)}, u32[]{:S(2)}) collective-permute-start(bf16[120,512]{1,0:T(8,128)(2,1)} %shard_map.121.refs_0_), channel_id=1, source_target_pairs={{0,12},{4,0},{8,4},{12,8},{1,13},{5,1},{9,5},{13,9},{2,14},{6,2},{... | collective-permute-start | bytes 368648 | tf_op jit(solution)/shard_map/ppermute | solution.py:624
  10.5 1.6 %copy-start = (bf16[512,2048]{1,0:T(8,128)(2,1)S(1)}, bf16[512,2048]{1,0:T(8,128)(2,1)}, u32[]{:S(2)}) copy-start(bf16[512,2048]{1,0:T(8,128)(2,1)} %source_ref) | copy-start | bytes 6291460
  12.1 8.1 %copy-start.1 = (bf16[120,512]{1,0:T(8,128)(2,1)S(1)}, bf16[120,512]{1,0:T(8,128)(2,1)}, u32[]{:S(2)}) copy-start(bf16[120,512]{1,0:T(8,128)(2,1)} %shard_map.121.refs_0_) | copy-start | bytes 368644
  16.3 8.1 %collective-permute-start.3 = (bf16[1,64,512]{2,1,0:T(8,128)(2,1)S(1)}, bf16[1,64,512]{2,1,0:T(8,128)(2,1)S(1)}, u32[]{:S(2)}, u32[]{:S(2)}) collective-permute-start(bf16[1,64,512]{2,1,0:T(8,128)(2,1)S(1)} %copy-done.2), channel_id=1, source_target_pairs={{0,8},{4,12},{8,0},{12,4},{1,9},{5,13},{9,1},{13,5},{2,10},{6,14},... | collective-permute-start | bytes 196616 | tf_op jit(solution)/shard_map/ppermute | solution.py:624
  16.3 8.1 %collective-permute-start.4 = (bf16[1,64,512]{2,1,0:T(8,128)(2,1)S(1)}, bf16[1,64,512]{2,1,0:T(8,128)(2,1)S(1)}, u32[]{:S(2)}, u32[]{:S(2)}) collective-permute-start(bf16[1,64,512]{2,1,0:T(8,128)(2,1)S(1)} %copy-done.2), channel_id=1, source_target_pairs={{0,4},{4,8},{8,12},{12,0},{1,5},{5,9},{9,13},{13,1},{2,6},{6,10},{... | collective-permute-start | bytes 196616 | tf_op jit(solution)/shard_map/ppermute | solution.py:624
  19.6 4.7 %collective-permute-start.5 = (bf16[1,64,512]{2,1,0:T(8,128)(2,1)S(1)}, bf16[1,64,512]{2,1,0:T(8,128)(2,1)S(1)}, u32[]{:S(2)}, u32[]{:S(2)}) collective-permute-start(bf16[1,64,512]{2,1,0:T(8,128)(2,1)S(1)} %copy-done.2), channel_id=1, source_target_pairs={{0,12},{4,0},{8,4},{12,8},{1,13},{5,1},{9,5},{13,9},{2,14},{6,2},{... | collective-permute-start | bytes 196616 | tf_op jit(solution)/shard_map/ppermute | solution.py:624
  26.0 2.0 %collective-permute-start.9 = (bf16[64,1024]{1,0:T(8,128)(2,1)S(1)}, bf16[64,1024]{1,0:T(8,128)(2,1)S(1)}, u32[]{:S(2)}, u32[]{:S(2)}) collective-permute-start(bf16[64,1024]{1,0:T(8,128)(2,1)S(1)} %get-tuple-element.60), channel_id=1, source_target_pairs={{0,1},{1,0},{2,3},{3,2},{4,5},{5,4},{6,7},{7,6},{8,9},{9,8},{10,11... | collective-permute-start | bytes 393224 | tf_op jit(solution)/shard_map/ppermute | solution.py:619
  26.1 10.4 %copy-start.3 = (s32[1,3,16]{2,0,1:T(1,128)S(1)}, s32[1,3,16]{2,0,1:T(1,128)}, u32[]{:S(2)}) copy-start(s32[1,3,16]{2,0,1:T(1,128)} %param.14) | copy-start | bytes 580
  27.5 2.5 %collective-permute-start.6 = (bf16[64,1024]{1,0:T(8,128)(2,1)S(1)}, bf16[64,1024]{1,0:T(8,128)(2,1)S(1)}, u32[]{:S(2)}, u32[]{:S(2)}) collective-permute-start(bf16[64,1024]{1,0:T(8,128)(2,1)S(1)} %get-tuple-element.58), channel_id=1, source_target_pairs={{0,1},{1,0},{2,3},{3,2},{4,5},{5,4},{6,7},{7,6},{8,9},{9,8},{10,11... | collective-permute-start | bytes 393224 | tf_op jit(solution)/shard_map/ppermute | solution.py:619
  28.1 6.4 %collective-permute-start.10 = (bf16[64,1024]{1,0:T(8,128)(2,1)S(1)}, bf16[64,1024]{1,0:T(8,128)(2,1)S(1)}, u32[]{:S(2)}, u32[]{:S(2)}) collective-permute-start(bf16[64,1024]{1,0:T(8,128)(2,1)S(1)} %add_convert_fusion.1), channel_id=1, source_target_pairs={{0,2},{1,3},{2,0},{3,1},{4,6},{5,7},{6,4},{7,5},{8,10},{9,11},{10,... | collective-permute-start | bytes 393224 | tf_op jit(solution)/shard_map/ppermute | solution.py:619
  30.0 6.5 %collective-permute-start.7 = (bf16[64,1024]{1,0:T(8,128)(2,1)S(1)}, bf16[64,1024]{1,0:T(8,128)(2,1)S(1)}, u32[]{:S(2)}, u32[]{:S(2)}) collective-permute-start(bf16[64,1024]{1,0:T(8,128)(2,1)S(1)} %add_convert_fusion.3), channel_id=1, source_target_pairs={{0,2},{1,3},{2,0},{3,1},{4,6},{5,7},{6,4},{7,5},{8,10},{9,11},{10,... | collective-permute-start | bytes 393224 | tf_op jit(solution)/shard_map/ppermute | solution.py:619
  34.5 3.1 %collective-permute-start.11 = (bf16[64,1024]{1,0:T(8,128)(2,1)S(1)}, bf16[64,1024]{1,0:T(8,128)(2,1)S(1)}, u32[]{:S(2)}, u32[]{:S(2)}) collective-permute-start(bf16[64,1024]{1,0:T(8,128)(2,1)S(1)} %add_convert_fusion.two_ref), channel_id=1, source_target_pairs={{0,1},{1,0},{2,3},{3,2},{4,5},{5,4},{6,7},{7,6},{8,9},{9,8},{10,11... | collective-permute-start | bytes 393224 | tf_op jit(solution)/shard_map/ppermute | solution.py:619
  36.5 1.4 %collective-permute-start.8 = (bf16[64,1024]{1,0:T(8,128)(2,1)S(1)}, bf16[64,1024]{1,0:T(8,128)(2,1)S(1)}, u32[]{:S(2)}, u32[]{:S(2)}) collective-permute-start(bf16[64,1024]{1,0:T(8,128)(2,1)S(1)} %add_convert_fusion.2.one_ref), channel_id=1, source_target_pairs={{0,1},{1,0},{2,3},{3,2},{4,5},{5,4},{6,7},{7,6},{8,9},{9,8},{10,11... | collective-permute-start | bytes 393224 | tf_op jit(solution)/shard_map/ppermute | solution.py:619

commit v10 on v7

--- a/solution.py
+++ b/solution.py
@@ -587,15 +587,37 @@
     grid_grad_ref[0] = total.astype(BF16)
 
 
-def finish_kernel(one_ref, other_one_ref, two_ref, other_two_ref, weight_grad_ref):
-    half, width = one_ref.shape
+def place(pairs, stages, semaphores):
+    copies = []
+    for n, (block_ref, target) in enumerate(pairs):
+        stages[n][...] = block_ref[...].astype(F32)
+        copies.append(pltpu.make_async_copy(stages[n], target, semaphores.at[n]))
+        copies[n].start()
+    for copy in copies:
+        copy.wait()
+
+
+def half_rows(half):
     core = lax.bitwise_and(lax.axis_index("rep"), 1)
     mine = pl.ds(pl.multiple_of(core * half, half), half)
-    other = pl.ds(pl.multiple_of((1 - core) * half, half), half)
-    weight_grad_ref[mine, :width] = one_ref[...].astype(F32)
-    weight_grad_ref[other, :width] = other_one_ref[...].astype(F32)
-    weight_grad_ref[mine, width:] = two_ref[...].astype(F32)
-    weight_grad_ref[other, width:] = other_two_ref[...].astype(F32)
+    return mine, pl.ds(pl.multiple_of((1 - core) * half, half), half)
+
+
+def finish_kernel(
+    one_ref, other_one_ref, two_ref, other_two_ref, weight_grad_ref, *scratch
+):
+    half, width = one_ref.shape
+    mine, other = half_rows(half)
+    place(
+        [
+            (two_ref, weight_grad_ref.at[mine, width:]),
+            (other_two_ref, weight_grad_ref.at[other, width:]),
+            (one_ref, weight_grad_ref.at[mine, :width]),
+            (other_one_ref, weight_grad_ref.at[other, :width]),
+        ],
+        scratch[:4],
+        scratch[4],
+    )
 
 
 VMEM = pl.BlockSpec(memory_space=pltpu.VMEM)
@@ -623,13 +645,12 @@
     return (left.astype(F32) + right.astype(F32)).astype(BF16)
 
 
-def summed_half(keep, give):
-    half = added(keep, swap(give, "rep", 1))
+def summed_over_chips(half):
     bit = 2
     while bit < lax.axis_size("rep"):
         half = added(half, swap(half, "rep", bit))
         bit *= 2
-    return half, swap(half, "rep", 1)
+    return half
 
 
 def whole_sample_body(
@@ -675,7 +696,6 @@
     packed, cotangent, weights = lax.optimization_barrier((packed, mesh_cotangent, weights))
     steps = (0, *range(2, regions), 1)
     packs = [packed] + [swap(packed, "space", step) for step in steps[1:]]
-    near = swap(cotangent, "space", 1)
     weights, turned = call(
         weights_kernel,
         (weights,),
@@ -685,7 +705,7 @@
         fetched=1,
     )
     packs[1], cotangent = lax.optimization_barrier((packs[1], cotangent))
-    cotangents = [cotangent] + [swap(cotangent, "space", step) for step in steps[1:-1]] + [near]
+    cotangents = [cotangent] + [swap(cotangent, "space", step) for step in steps[1:]]
     rows = regions * mesh_count
     slots = regions * mesh_cap
     (
@@ -778,6 +798,9 @@
         ],
         10**9,
     )
+    half_one = added(keep_one, swap(give_one, "rep", 1))
+    half_two = added(keep_two, swap(give_two, "rep", 1))
+    half_one, own_slots = lax.optimization_barrier((half_one, own_slots))
     grid_grad = call(
         grid_back_kernel,
         (turned, g2m_pick, own_slots),
@@ -785,13 +808,17 @@
         [],
         10**8,
     )[0]
-    weight_grad = call(
+    two = summed_over_chips(half_two)
+    one, grid_grad = lax.optimization_barrier((summed_over_chips(half_one), grid_grad))
+    weight_grad = pl.pallas_call(
         finish_kernel,
-        (*summed_half(keep_one, give_one), *summed_half(keep_two, give_two)),
-        [((columns, 4 * latent), F32)],
-        [],
-        10**6,
-    )[0]
+        out_shape=jax.ShapeDtypeStruct((columns, 4 * latent), F32),
+        in_specs=[VMEM] * 4,
+        out_specs=pl.BlockSpec(memory_space=pltpu.HBM),
+        scratch_shapes=[pltpu.VMEM((half, 2 * latent), F32)] * 4
+        + [pltpu.SemaphoreType.DMA((4,))],
+        compiler_params=pltpu.CompilerParams(vmem_limit_bytes=40 << 20),
+    )(one, swap(one, "rep", 1), two, swap(two, "rep", 1))
     return (mesh_out, grid_grad, weight_grad)
 
 

time: 38.6 us -> 39 us (1.010)
  waiting for transfers between devices: 10.7 us -> 12.1 us
  starting transfers between devices: 13.6 us -> 12.5 us
    ppermute x12, waiting for transfers between devices: 10.7 us -> 12.1 us  [swap(): lax.ppermute(block, axis, [(i, i ^ bits) for i in range(lax.axis_size(axi...]
    ppermute x12, starting transfers between devices: 13.6 us -> 12.5 us  [swap(): lax.ppermute(block, axis, [(i, i ^ bits) for i in range(lax.axis_size(axi...]
    pallas_call x7 -> x6, Pallas kernels: 11.7 us -> 10.7 us  [call(): pl.pallas_call(kernel, out_shape=[jax.ShapeDtypeStruct(shape, kind) for s...]
    pallas_call x0 -> x1, Pallas kernels: none -> 1.01 us  [whole_sample_body(): pl.pallas_call(finish_kernel, out_shape=jax.ShapeDtypeStruct((columns, 4...]
  transfers between devices with their start and end apart: 12 -> 12, of which waited for: 5 -> 6; matrix products, arithmetic and copies ran while one was open for 0% -> 0% of each run, Pallas kernels for 19% -> 19%
where the time goes in v10:
time: 39 us; the launch traced here: 38.8 us
  starting transfers between devices  12.5 us (32%)
  waiting for transfers between devices  12.1 us (31%)
  Pallas kernels  11.7 us (30%)
  local copies, waits for them, and re-layouts  1.6 us (4%)
  between operations  0.74 us (2%)
    ppermute x12, starting transfers between devices, swap(): lax.ppermute(block, axis, [(i, i ^ bits) for i in range(lax.axis_size(axi...  12.5 us
    ppermute x12, waiting for transfers between devices, swap(): lax.ppermute(block, axis, [(i, i ^ bits) for i in range(lax.axis_size(axi...  12.1 us
    pallas_call x6, Pallas kernels, call(): pl.pallas_call(kernel, out_shape=[jax.ShapeDtypeStruct(shape, kind) for s...  10.7 us
    unnamed x8, local copies, waits for them, and re-layouts  1.6 us
    pallas_call x1, Pallas kernels, whole_sample_body(): pl.pallas_call(finish_kernel, out_shape=jax.ShapeDtypeStruct((columns, 4...  1.01 us
  transfers between devices with their start and end apart: 12, of which 6 were waited for; matrix products, arithmetic and copies ran while one was open for 0% of the time, Pallas kernels for 19%

profile of v10, /device:TPU:0, one launch (start us, length us, event | category | flops | bytes accessed | tf_op | source)
XLA Modules:
  0.0 38.8 jit_solution(17471042243518981619)
XLA Ops:
  0.6 1.9 %shard_map.121.refs_0_ = bf16[120,512]{1,0:T(8,128)(2,1)} custom-call(bf16[1,128,512]{2,1,0:T(8,128)(2,1)} %refs_0_.1, bf16[1,64,512]{2,1,0:T(8,128)(2,1)} %refs_1_.1, s32[3,1,16]{2,1,0:T(1,128)} %bitcast.5, s32[1,256]{1,0:T(1,128)} %bitcast.7, s32[1,256]{1,0:T(1,128)} %bitcast.8, s32[1,4,8]{2,1,0:T(4,128)} %refs_5_.1, s32[1,256]{1,0:T(1,128)} %bitcast.9, ...), custom_call_target="tpu_custom_call" | custom-call | flops 10000000 | bytes 4194304 | tf_op jit(solution)/shard_map/pallas_call | solution.py:628
  2.5 4.1 %collective-permute-start = (bf16[120,512]{1,0:T(8,128)(2,1)}, bf16[120,512]{1,0:T(8,128)(2,1)S(1)}, u32[]{:S(2)}, u32[]{:S(2)}) collective-permute-start(bf16[120,512]{1,0:T(8,128)(2,1)} %shard_map.121.refs_0_), channel_id=1, source_target_pairs={{0,8},{4,12},{8,0},{12,4},{1,9},{5,13},{9,1},{13,5},{2,10},{6,14},... | collective-permute-start | bytes 368648 | tf_op jit(solution)/shard_map/ppermute | solution.py:641
  6.6 1.3 %collective-permute-start.1 = (bf16[120,512]{1,0:T(8,128)(2,1)}, bf16[120,512]{1,0:T(8,128)(2,1)S(1)}, u32[]{:S(2)}, u32[]{:S(2)}) collective-permute-start(bf16[120,512]{1,0:T(8,128)(2,1)} %shard_map.121.refs_0_), channel_id=1, source_target_pairs={{0,12},{4,8},{8,4},{12,0},{1,13},{5,9},{9,5},{13,1},{2,14},{6,10},... | collective-permute-start | bytes 368648 | tf_op jit(solution)/shard_map/ppermute | solution.py:641
  8.0 0.2 collective-permute-start.2
  8.2 1.6 %copy-done = bf16[512,2048]{1,0:T(8,128)(2,1)S(1)} copy-done((bf16[512,2048]{1,0:T(8,128)(2,1)S(1)}, bf16[512,2048]{1,0:T(8,128)(2,1)}, u32[]{:S(2)}) %copy-start) | copy-done | bytes 2097176
  9.8 0.6 %shard_map.122 = (bf16[512,2048]{1,0:T(8,128)(2,1)S(1)}, bf16[512,1536]{1,0:T(8,128)(2,1)S(1)}) custom-call(bf16[512,2048]{1,0:T(8,128)(2,1)S(1)} %copy-done), custom_call_target="tpu_custom_call" | custom-call | flops 100000000 | bytes 4194304 | tf_op jit(solution)/shard_map/pallas_call | solution.py:628
  10.4 5.9 %collective-permute-done.refs_1_ = bf16[120,512]{1,0:T(8,128)(2,1)S(1)} collective-permute-done((bf16[120,512]{1,0:T(8,128)(2,1)}, bf16[120,512]{1,0:T(8,128)(2,1)S(1)}, u32[]{:S(2)}, u32[]{:S(2)}) %collective-permute-start) | collective-permute-done | bytes 122912 | tf_op jit(solution)/shard_map/ppermute | solution.py:641
  16.3 0.0 collective-permute-start.3
  16.3 2.8 %collective-permute-start.4 = (bf16[1,64,512]{2,1,0:T(8,128)(2,1)S(1)}, bf16[1,64,512]{2,1,0:T(8,128)(2,1)S(1)}, u32[]{:S(2)}, u32[]{:S(2)}) collective-permute-start(bf16[1,64,512]{2,1,0:T(8,128)(2,1)S(1)} %copy-done.2), channel_id=1, source_target_pairs={{0,12},{4,8},{8,4},{12,0},{1,13},{5,9},{9,5},{13,1},{2,14},{6,10},... | collective-permute-start | bytes 196616 | tf_op jit(solution)/shard_map/ppermute | solution.py:641
  19.1 0.7 %collective-permute-start.5 = (bf16[1,64,512]{2,1,0:T(8,128)(2,1)S(1)}, bf16[1,64,512]{2,1,0:T(8,128)(2,1)S(1)}, u32[]{:S(2)}, u32[]{:S(2)}) collective-permute-start(bf16[1,64,512]{2,1,0:T(8,128)(2,1)S(1)} %copy-done.2), channel_id=1, source_target_pairs={{0,4},{4,0},{8,12},{12,8},{1,5},{5,1},{9,13},{13,9},{2,6},{6,2},{1... | collective-permute-start | bytes 196616 | tf_op jit(solution)/shard_map/ppermute | solution.py:641
  19.8 0.0 collective-permute-done.1.refs_2_
  19.8 0.0 collective-permute-done.2.refs_3_
  19.8 4.2 %shard_map.123 = (bf16[1,64,512]{2,1,0:T(8,128)(2,1)}, bf16[192,512]{1,0:T(8,128)(2,1)S(1)}, bf16[256,512]{1,0:T(8,128)(2,1)S(1)}, bf16[256,512]{1,0:T(8,128)(2,...) custom-call(bf16[120,512]{1,0:T(8,128)(2,1)S(1)} %copy-done.1, ...), custom_call_target="tpu_custom_call" | custom-call | flops 2000000000 | bytes 4194304 | tf_op jit(solution)/shard_map/pallas_call | solution.py:628
  24.0 0.1 collective-permute-done.3.refs_1_
  24.1 0.0 collective-permute-done.4.refs_2_
  24.1 0.4 %collective-permute-done.5.refs_3_ = bf16[1,64,512]{2,1,0:T(8,128)(2,1)S(1)} collective-permute-done((bf16[1,64,512]{2,1,0:T(8,128)(2,1)S(1)}, bf16[1,64,512]{2,1,0:T(8,128)(2,1)S(1)}, u32[]{:S(2)}, u32[]{:S(2)}) %collective-permute-start.5) | collective-permute-done | bytes 65568 | tf_op jit(solution)/shard_map/ppermute | solution.py:641
  24.5 1.6 %shard_map.124 = (f32[256,512]{1,0:T(8,128)S(1)}, bf16[64,1024]{1,0:T(8,128)(2,1)S(1)}, bf16[64,1024]{1,0:T(8,128)(2,1)S(1)}) custom-call(bf16[1,64,512]{2,1,0:T(8,128)(2,1)S(1)} %copy-done.2, bf16[1,64,512]{2,1,0:T(8,128)(2,1)S(1)} %collective-permute-done.3.refs_1_, bf16[1,64,512]{2,1,0:T(8,128)(2,1)S(1)} %collective-permute-done.4.refs_2_, ...), custom_call_target="tpu_custom_call" | custom-call | flops 1000000000 | bytes 4194304 | tf_op jit(solution)/shard_map/pallas_call | solution.py:628
  26.1 0.1 collective-permute-start.9
  26.1 0.0 copy-start.3
  26.1 1.3 %shard_map.125 = (bf16[48,512]{1,0:T(8,128)(2,1)S(1)}, bf16[64,1024]{1,0:T(8,128)(2,1)S(1)}, bf16[64,1024]{1,0:T(8,128)(2,1)S(1)}) custom-call(bf16[192,512]{1,0:T(8,128)(2,1)S(1)} %get-tuple-element.42.grid_ref, bf16[256,512]{1,0:T(8,128)(2,1)S(1)} %get-tuple-element.43.mesh_ref, bf16[448,256]{1,0:T(8,128)(2,1)S(1)} %get-tuple-element.44.hot_ref, ...), custom_call_target="tpu_custom_call" | custom-call | flops 1000000000 | bytes 4194304 | tf_op jit(solution)/shard_map/pallas_call | solution.py:628
  27.5 0.5 %collective-permute-start.6 = (bf16[64,1024]{1,0:T(8,128)(2,1)S(1)}, bf16[64,1024]{1,0:T(8,128)(2,1)S(1)}, u32[]{:S(2)}, u32[]{:S(2)}) collective-permute-start(bf16[64,1024]{1,0:T(8,128)(2,1)S(1)} %get-tuple-element.61), channel_id=1, source_target_pairs={{0,1},{1,0},{2,3},{3,2},{4,5},{5,4},{6,7},{7,6},{8,9},{9,8},{10,11... | collective-permute-start | bytes 393224 | tf_op jit(solution)/shard_map/ppermute | solution.py:641
  28.0 0.0 collective-permute-done.9
  28.1 1.7 %collective-permute-start.10 = (bf16[64,1024]{1,0:T(8,128)(2,1)S(1)}, bf16[64,1024]{1,0:T(8,128)(2,1)S(1)}, u32[]{:S(2)}, u32[]{:S(2)}) collective-permute-start(bf16[64,1024]{1,0:T(8,128)(2,1)S(1)} %add_convert_fusion.1), channel_id=1, source_target_pairs={{0,2},{1,3},{2,0},{3,1},{4,6},{5,7},{6,4},{7,5},{8,10},{9,11},{10,... | collective-permute-start | bytes 393224 | tf_op jit(solution)/shard_map/ppermute | solution.py:641
  29.8 1.0 %collective-permute-start.7 = (bf16[64,1024]{1,0:T(8,128)(2,1)S(1)}, bf16[64,1024]{1,0:T(8,128)(2,1)S(1)}, u32[]{:S(2)}, u32[]{:S(2)}) collective-permute-start(bf16[64,1024]{1,0:T(8,128)(2,1)S(1)} %add_convert_fusion.3), channel_id=1, source_target_pairs={{0,2},{1,3},{2,0},{3,1},{4,6},{5,7},{6,4},{7,5},{8,10},{9,11},{10,... | collective-permute-start | bytes 393224 | tf_op jit(solution)/shard_map/ppermute | solution.py:641
  30.7 1.1 %shard_map.126 = bf16[1,128,512]{2,1,0:T(8,128)(2,1)} custom-call(bf16[512,1536]{1,0:T(8,128)(2,1)S(1)} %get-tuple-element.50.refs_4_.turned_ref, s32[3,1,16]{2,1,0:T(1,128)S(1)} %bitcast.6, bf16[48,512]{1,0:T(8,128)(2,1)S(1)} %get-tuple-element.64.own_slot_ref), custom_call_target="tpu_custom_call" | custom-call | flops 100000000 | bytes 4194304 | tf_op jit(solution)/shard_map/pallas_call | solution.py:628
  31.8 2.7 %collective-permute-done.10 = bf16[64,1024]{1,0:T(8,128)(2,1)S(1)} collective-permute-done((bf16[64,1024]{1,0:T(8,128)(2,1)S(1)}, bf16[64,1024]{1,0:T(8,128)(2,1)S(1)}, u32[]{:S(2)}, u32[]{:S(2)}) %collective-permute-start.10) | collective-permute-done | bytes 131104 | tf_op jit(solution)/shard_map/ppermute | solution.py:641
  34.5 0.1 collective-permute-start.11
  34.6 1.8 %collective-permute-done.7 = bf16[64,1024]{1,0:T(8,128)(2,1)S(1)} collective-permute-done((bf16[64,1024]{1,0:T(8,128)(2,1)S(1)}, bf16[64,1024]{1,0:T(8,128)(2,1)S(1)}, u32[]{:S(2)}, u32[]{:S(2)}) %collective-permute-start.7) | collective-permute-done | bytes 131104 | tf_op jit(solution)/shard_map/ppermute | solution.py:641
  36.4 0.1 collective-permute-start.8
  36.5 0.0 collective-permute-done.11.other_two_ref
  36.5 1.3 %collective-permute-done.8.other_one_ref = bf16[64,1024]{1,0:T(8,128)(2,1)S(1)} collective-permute-done((bf16[64,1024]{1,0:T(8,128)(2,1)S(1)}, bf16[64,1024]{1,0:T(8,128)(2,1)S(1)}, u32[]{:S(2)}, u32[]{:S(2)}) %collective-permute-start.8) | collective-permute-done | bytes 131104 | tf_op jit(solution)/shard_map/ppermute | solution.py:641
  37.8 1.0 %shard_map.127 = f32[128,2048]{1,0:T(8,128)} custom-call(bf16[64,1024]{1,0:T(8,128)(2,1)S(1)} %add_convert_fusion.2.one_ref, bf16[64,1024]{1,0:T(8,128)(2,1)S(1)} %collective-permute-done.8.other_one_ref, bf16[64,1024]{1,0:T(8,128)(2,1)S(1)} %add_convert_fusion.two_ref, bf16[64,1024]{1,0:T(8,128)(2,1)S(1)} %collective-permute-done.11.other_two_ref), custom_call_target="tpu_custom_call" | custom-call | tf_op jit(solution)/shard_map/pallas_call | solution.py:813
  (11 shorter events, 0.2 us)
Async XLA Ops:
  0.6 15.7 %copy-start.2 = (bf16[1,64,512]{2,1,0:T(8,128)(2,1)S(1)}, bf16[1,64,512]{2,1,0:T(8,128)(2,1)}, u32[]{:S(2)}) copy-start(bf16[1,64,512]{2,1,0:T(8,128)(2,1)} %refs_0_.2) | copy-start | bytes 196612
  2.5 13.8 %collective-permute-start = (bf16[120,512]{1,0:T(8,128)(2,1)}, bf16[120,512]{1,0:T(8,128)(2,1)S(1)}, u32[]{:S(2)}, u32[]{:S(2)}) collective-permute-start(bf16[120,512]{1,0:T(8,128)(2,1)} %shard_map.121.refs_0_), channel_id=1, source_target_pairs={{0,8},{4,12},{8,0},{12,4},{1,9},{5,13},{9,1},{13,5},{2,10},{6,14},... | collective-permute-start | bytes 368648 | tf_op jit(solution)/shard_map/ppermute | solution.py:641
  6.6 13.2 %collective-permute-start.1 = (bf16[120,512]{1,0:T(8,128)(2,1)}, bf16[120,512]{1,0:T(8,128)(2,1)S(1)}, u32[]{:S(2)}, u32[]{:S(2)}) collective-permute-start(bf16[120,512]{1,0:T(8,128)(2,1)} %shard_map.121.refs_0_), channel_id=1, source_target_pairs={{0,12},{4,8},{8,4},{12,0},{1,13},{5,9},{9,5},{13,1},{2,14},{6,10},... | collective-permute-start | bytes 368648 | tf_op jit(solution)/shard_map/ppermute | solution.py:641
  8.0 11.8 %collective-permute-start.2 = (bf16[120,512]{1,0:T(8,128)(2,1)}, bf16[120,512]{1,0:T(8,128)(2,1)S(1)}, u32[]{:S(2)}, u32[]{:S(2)}) collective-permute-start(bf16[120,512]{1,0:T(8,128)(2,1)} %shard_map.121.refs_0_), channel_id=1, source_target_pairs={{0,4},{4,0},{8,12},{12,8},{1,5},{5,1},{9,13},{13,9},{2,6},{6,2},{1... | collective-permute-start | bytes 368648 | tf_op jit(solution)/shard_map/ppermute | solution.py:641
  8.2 1.6 %copy-start = (bf16[512,2048]{1,0:T(8,128)(2,1)S(1)}, bf16[512,2048]{1,0:T(8,128)(2,1)}, u32[]{:S(2)}) copy-start(bf16[512,2048]{1,0:T(8,128)(2,1)} %source_ref) | copy-start | bytes 6291460
  9.8 10.0 %copy-start.1 = (bf16[120,512]{1,0:T(8,128)(2,1)S(1)}, bf16[120,512]{1,0:T(8,128)(2,1)}, u32[]{:S(2)}) copy-start(bf16[120,512]{1,0:T(8,128)(2,1)} %shard_map.121.refs_0_) | copy-start | bytes 368644
  16.3 7.7 %collective-permute-start.3 = (bf16[1,64,512]{2,1,0:T(8,128)(2,1)S(1)}, bf16[1,64,512]{2,1,0:T(8,128)(2,1)S(1)}, u32[]{:S(2)}, u32[]{:S(2)}) collective-permute-start(bf16[1,64,512]{2,1,0:T(8,128)(2,1)S(1)} %copy-done.2), channel_id=1, source_target_pairs={{0,8},{4,12},{8,0},{12,4},{1,9},{5,13},{9,1},{13,5},{2,10},{6,14},... | collective-permute-start | bytes 196616 | tf_op jit(solution)/shard_map/ppermute | solution.py:641
  16.3 7.7 %collective-permute-start.4 = (bf16[1,64,512]{2,1,0:T(8,128)(2,1)S(1)}, bf16[1,64,512]{2,1,0:T(8,128)(2,1)S(1)}, u32[]{:S(2)}, u32[]{:S(2)}) collective-permute-start(bf16[1,64,512]{2,1,0:T(8,128)(2,1)S(1)} %copy-done.2), channel_id=1, source_target_pairs={{0,12},{4,8},{8,4},{12,0},{1,13},{5,9},{9,5},{13,1},{2,14},{6,10},... | collective-permute-start | bytes 196616 | tf_op jit(solution)/shard_map/ppermute | solution.py:641
  19.1 5.3 %collective-permute-start.5 = (bf16[1,64,512]{2,1,0:T(8,128)(2,1)S(1)}, bf16[1,64,512]{2,1,0:T(8,128)(2,1)S(1)}, u32[]{:S(2)}, u32[]{:S(2)}) collective-permute-start(bf16[1,64,512]{2,1,0:T(8,128)(2,1)S(1)} %copy-done.2), channel_id=1, source_target_pairs={{0,4},{4,0},{8,12},{12,8},{1,5},{5,1},{9,13},{13,9},{2,6},{6,2},{1... | collective-permute-start | bytes 196616 | tf_op jit(solution)/shard_map/ppermute | solution.py:641
  26.1 2.0 %collective-permute-start.9 = (bf16[64,1024]{1,0:T(8,128)(2,1)S(1)}, bf16[64,1024]{1,0:T(8,128)(2,1)S(1)}, u32[]{:S(2)}, u32[]{:S(2)}) collective-permute-start(bf16[64,1024]{1,0:T(8,128)(2,1)S(1)} %get-tuple-element.68), channel_id=1, source_target_pairs={{0,1},{1,0},{2,3},{3,2},{4,5},{5,4},{6,7},{7,6},{8,9},{9,8},{10,11... | collective-permute-start | bytes 393224 | tf_op jit(solution)/shard_map/ppermute | solution.py:641
  26.1 4.6 %copy-start.3 = (s32[1,3,16]{2,0,1:T(1,128)S(1)}, s32[1,3,16]{2,0,1:T(1,128)}, u32[]{:S(2)}) copy-start(s32[1,3,16]{2,0,1:T(1,128)} %param.14) | copy-start | bytes 580
  27.5 2.3 %collective-permute-start.6 = (bf16[64,1024]{1,0:T(8,128)(2,1)S(1)}, bf16[64,1024]{1,0:T(8,128)(2,1)S(1)}, u32[]{:S(2)}, u32[]{:S(2)}) collective-permute-start(bf16[64,1024]{1,0:T(8,128)(2,1)S(1)} %get-tuple-element.61), channel_id=1, source_target_pairs={{0,1},{1,0},{2,3},{3,2},{4,5},{5,4},{6,7},{7,6},{8,9},{9,8},{10,11... | collective-permute-start | bytes 393224 | tf_op jit(solution)/shard_map/ppermute | solution.py:641
  28.1 6.4 %collective-permute-start.10 = (bf16[64,1024]{1,0:T(8,128)(2,1)S(1)}, bf16[64,1024]{1,0:T(8,128)(2,1)S(1)}, u32[]{:S(2)}, u32[]{:S(2)}) collective-permute-start(bf16[64,1024]{1,0:T(8,128)(2,1)S(1)} %add_convert_fusion.1), channel_id=1, source_target_pairs={{0,2},{1,3},{2,0},{3,1},{4,6},{5,7},{6,4},{7,5},{8,10},{9,11},{10,... | collective-permute-start | bytes 393224 | tf_op jit(solution)/shard_map/ppermute | solution.py:641
  29.8 6.6 %collective-permute-start.7 = (bf16[64,1024]{1,0:T(8,128)(2,1)S(1)}, bf16[64,1024]{1,0:T(8,128)(2,1)S(1)}, u32[]{:S(2)}, u32[]{:S(2)}) collective-permute-start(bf16[64,1024]{1,0:T(8,128)(2,1)S(1)} %add_convert_fusion.3), channel_id=1, source_target_pairs={{0,2},{1,3},{2,0},{3,1},{4,6},{5,7},{6,4},{7,5},{8,10},{9,11},{10,... | collective-permute-start | bytes 393224 | tf_op jit(solution)/shard_map/ppermute | solution.py:641
  34.5 2.0 %collective-permute-start.11 = (bf16[64,1024]{1,0:T(8,128)(2,1)S(1)}, bf16[64,1024]{1,0:T(8,128)(2,1)S(1)}, u32[]{:S(2)}, u32[]{:S(2)}) collective-permute-start(bf16[64,1024]{1,0:T(8,128)(2,1)S(1)} %add_convert_fusion.two_ref), channel_id=1, source_target_pairs={{0,1},{1,0},{2,3},{3,2},{4,5},{5,4},{6,7},{7,6},{8,9},{9,8},{10,11... | collective-permute-start | bytes 393224 | tf_op jit(solution)/shard_map/ppermute | solution.py:641
  36.4 1.4 %collective-permute-start.8 = (bf16[64,1024]{1,0:T(8,128)(2,1)S(1)}, bf16[64,1024]{1,0:T(8,128)(2,1)S(1)}, u32[]{:S(2)}, u32[]{:S(2)}) collective-permute-start(bf16[64,1024]{1,0:T(8,128)(2,1)S(1)} %add_convert_fusion.2.one_ref), channel_id=1, source_target_pairs={{0,1},{1,0},{2,3},{3,2},{4,5},{5,4},{6,7},{7,6},{8,9},{9,8},{10,11... | collective-permute-start | bytes 393224 | tf_op jit(solution)/shard_map/ppermute | solution.py:641

commit v11 on v8

--- a/solution.py
+++ b/solution.py
@@ -673,7 +673,7 @@
         megabytes=56,
     )[0]
     packed, cotangent, weights = lax.optimization_barrier((packed, mesh_cotangent, weights))
-    steps = (0, *range(2, regions), 1)
+    steps = tuple(range(regions))
     packs = [packed] + [swap(packed, "space", step) for step in steps[1:]]
     near = swap(cotangent, "space", 1)
     weights, turned = call(
@@ -684,8 +684,8 @@
         10**8,
         fetched=1,
     )
-    near, cotangent = lax.optimization_barrier((near, cotangent))
-    cotangents = [cotangent] + [swap(cotangent, "space", step) for step in steps[1:-1]] + [near]
+    *packs[1:3], cotangent = lax.optimization_barrier((*packs[1:3], cotangent))
+    cotangents = [cotangent, near] + [swap(cotangent, "space", step) for step in steps[2:]]
     rows = regions * mesh_count
     slots = regions * mesh_cap
     (

time: 40.7 us -> 40.4 us (level)
  starting transfers between devices: 14.3 us -> 11.5 us
  waiting for transfers between devices: 12 us -> 14.5 us
    ppermute x12, starting transfers between devices: 14.3 us -> 11.5 us  [swap(): lax.ppermute(block, axis, [(i, i ^ bits) for i in range(lax.axis_size(axi...]
    ppermute x12, waiting for transfers between devices: 12 us -> 14.5 us  [swap(): lax.ppermute(block, axis, [(i, i ^ bits) for i in range(lax.axis_size(axi...]
where the time goes in v11:
time: 40.4 us; the launch traced here: 40.2 us
  waiting for transfers between devices  14.5 us (36%)
  Pallas kernels  11.7 us (29%)
  starting transfers between devices  11.5 us (28%)
  local copies, waits for them, and re-layouts  1.61 us (4%)
  between operations  0.75 us (2%)
    ppermute x12, waiting for transfers between devices, swap(): lax.ppermute(block, axis, [(i, i ^ bits) for i in range(lax.axis_size(axi...  14.5 us
    pallas_call x7, Pallas kernels, call(): pl.pallas_call(kernel, out_shape=[jax.ShapeDtypeStruct(shape, kind) for s...  11.7 us
    ppermute x12, starting transfers between devices, swap(): lax.ppermute(block, axis, [(i, i ^ bits) for i in range(lax.axis_size(axi...  11.5 us
    unnamed x8, local copies, waits for them, and re-layouts  1.61 us
  transfers between devices with their start and end apart: 12, of which 5 were waited for; matrix products, arithmetic and copies ran while one was open for 0% of the time, Pallas kernels for 18%

profile of v11, /device:TPU:0, one launch (start us, length us, event | category | flops | bytes accessed | tf_op | source)
XLA Modules:
  0.0 40.2 jit_solution(5747871520171103150)
XLA Ops:
  0.6 0.0 copy-start.2
  0.6 1.9 %shard_map.121.refs_0_ = bf16[120,512]{1,0:T(8,128)(2,1)} custom-call(bf16[1,128,512]{2,1,0:T(8,128)(2,1)} %refs_0_.1, bf16[1,64,512]{2,1,0:T(8,128)(2,1)} %refs_1_.1, s32[3,1,16]{2,1,0:T(1,128)} %bitcast.5, s32[1,256]{1,0:T(1,128)} %bitcast.7, s32[1,256]{1,0:T(1,128)} %bitcast.8, s32[1,4,8]{2,1,0:T(4,128)} %refs_5_.1, s32[1,256]{1,0:T(1,128)} %bitcast.9, ...), custom_call_target="tpu_custom_call" | custom-call | flops 10000000 | bytes 4194304 | tf_op jit(solution)/shard_map/pallas_call | solution.py:606
  2.5 3.1 %collective-permute-start = (bf16[120,512]{1,0:T(8,128)(2,1)}, bf16[120,512]{1,0:T(8,128)(2,1)S(1)}, u32[]{:S(2)}, u32[]{:S(2)}) collective-permute-start(bf16[120,512]{1,0:T(8,128)(2,1)} %shard_map.121.refs_0_), channel_id=1, source_target_pairs={{0,4},{4,0},{8,12},{12,8},{1,5},{5,1},{9,13},{13,9},{2,6},{6,2},{1... | collective-permute-start | bytes 368648 | tf_op jit(solution)/shard_map/ppermute | solution.py:619
  5.6 2.6 %collective-permute-start.1 = (bf16[120,512]{1,0:T(8,128)(2,1)}, bf16[120,512]{1,0:T(8,128)(2,1)S(1)}, u32[]{:S(2)}, u32[]{:S(2)}) collective-permute-start(bf16[120,512]{1,0:T(8,128)(2,1)} %shard_map.121.refs_0_), channel_id=1, source_target_pairs={{0,8},{4,12},{8,0},{12,4},{1,9},{5,13},{9,1},{13,5},{2,10},{6,14},... | collective-permute-start | bytes 368648 | tf_op jit(solution)/shard_map/ppermute | solution.py:619
  8.2 0.0 collective-permute-start.2
  8.2 0.9 %collective-permute-start.3 = (bf16[1,64,512]{2,1,0:T(8,128)(2,1)}, bf16[1,64,512]{2,1,0:T(8,128)(2,1)S(1)}, u32[]{:S(2)}, u32[]{:S(2)}) collective-permute-start(bf16[1,64,512]{2,1,0:T(8,128)(2,1)} %refs_0_.2), channel_id=1, source_target_pairs={{0,4},{4,0},{8,12},{12,8},{1,5},{5,1},{9,13},{13,9},{2,6},{6,2},{1... | collective-permute-start | bytes 196616 | tf_op jit(solution)/shard_map/ppermute | solution.py:619
  9.1 1.6 %copy-done = bf16[512,2048]{1,0:T(8,128)(2,1)S(1)} copy-done((bf16[512,2048]{1,0:T(8,128)(2,1)S(1)}, bf16[512,2048]{1,0:T(8,128)(2,1)}, u32[]{:S(2)}) %copy-start) | copy-done | bytes 2097176
  10.7 0.6 %shard_map.122 = (bf16[512,2048]{1,0:T(8,128)(2,1)S(1)}, bf16[512,1536]{1,0:T(8,128)(2,1)S(1)}) custom-call(bf16[512,2048]{1,0:T(8,128)(2,1)S(1)} %copy-done), custom_call_target="tpu_custom_call" | custom-call | flops 100000000 | bytes 4194304 | tf_op jit(solution)/shard_map/pallas_call | solution.py:606
  11.3 0.0 collective-permute-done.refs_1_
  11.3 8.3 %collective-permute-done.1.refs_2_ = bf16[120,512]{1,0:T(8,128)(2,1)S(1)} collective-permute-done((bf16[120,512]{1,0:T(8,128)(2,1)}, bf16[120,512]{1,0:T(8,128)(2,1)S(1)}, u32[]{:S(2)}, u32[]{:S(2)}) %collective-permute-start.1) | collective-permute-done | bytes 122912 | tf_op jit(solution)/shard_map/ppermute | solution.py:619
  19.6 0.0 collective-permute-start.4
  19.6 1.6 %collective-permute-start.5 = (bf16[1,64,512]{2,1,0:T(8,128)(2,1)S(1)}, bf16[1,64,512]{2,1,0:T(8,128)(2,1)S(1)}, u32[]{:S(2)}, u32[]{:S(2)}) collective-permute-start(bf16[1,64,512]{2,1,0:T(8,128)(2,1)S(1)} %copy-done.2), channel_id=1, source_target_pairs={{0,12},{4,8},{8,4},{12,0},{1,13},{5,9},{9,5},{13,1},{2,14},{6,10},... | collective-permute-start | bytes 196616 | tf_op jit(solution)/shard_map/ppermute | solution.py:619
  21.2 0.0 collective-permute-done.2.refs_3_
  21.3 4.2 %shard_map.123 = (bf16[1,64,512]{2,1,0:T(8,128)(2,1)}, bf16[192,512]{1,0:T(8,128)(2,1)S(1)}, bf16[256,512]{1,0:T(8,128)(2,1)S(1)}, bf16[256,512]{1,0:T(8,128)(2,...) custom-call(bf16[120,512]{1,0:T(8,128)(2,1)S(1)} %copy-done.1, ...), custom_call_target="tpu_custom_call" | custom-call | flops 2000000000 | bytes 4194304 | tf_op jit(solution)/shard_map/pallas_call | solution.py:606
  25.4 0.0 collective-permute-done.3.refs_1_
  25.4 0.0 collective-permute-done.4.refs_2_
  25.4 0.4 collective-permute-done.5.refs_3_
  25.8 1.6 %shard_map.124 = (f32[256,512]{1,0:T(8,128)S(1)}, bf16[64,1024]{1,0:T(8,128)(2,1)S(1)}, bf16[64,1024]{1,0:T(8,128)(2,1)S(1)}) custom-call(bf16[1,64,512]{2,1,0:T(8,128)(2,1)S(1)} %copy-done.2, bf16[1,64,512]{2,1,0:T(8,128)(2,1)S(1)} %collective-permute-done.3.refs_1_, bf16[1,64,512]{2,1,0:T(8,128)(2,1)S(1)} %collective-permute-done.4.refs_2_, ...), custom_call_target="tpu_custom_call" | custom-call | flops 1000000000 | bytes 4194304 | tf_op jit(solution)/shard_map/pallas_call | solution.py:606
  27.4 0.1 collective-permute-start.9
  27.5 0.0 copy-start.3
  27.5 1.3 %shard_map.125 = (bf16[48,512]{1,0:T(8,128)(2,1)S(1)}, bf16[64,1024]{1,0:T(8,128)(2,1)S(1)}, bf16[64,1024]{1,0:T(8,128)(2,1)S(1)}) custom-call(bf16[192,512]{1,0:T(8,128)(2,1)S(1)} %get-tuple-element.41.grid_ref, bf16[256,512]{1,0:T(8,128)(2,1)S(1)} %get-tuple-element.42.mesh_ref, bf16[448,256]{1,0:T(8,128)(2,1)S(1)} %get-tuple-element.43.hot_ref, ...), custom_call_target="tpu_custom_call" | custom-call | flops 1000000000 | bytes 4194304 | tf_op jit(solution)/shard_map/pallas_call | solution.py:606
  28.8 0.5 %collective-permute-start.6 = (bf16[64,1024]{1,0:T(8,128)(2,1)S(1)}, bf16[64,1024]{1,0:T(8,128)(2,1)S(1)}, u32[]{:S(2)}, u32[]{:S(2)}) collective-permute-start(bf16[64,1024]{1,0:T(8,128)(2,1)S(1)} %get-tuple-element.60), channel_id=1, source_target_pairs={{0,1},{1,0},{2,3},{3,2},{4,5},{5,4},{6,7},{7,6},{8,9},{9,8},{10,11... | collective-permute-start | bytes 393224 | tf_op jit(solution)/shard_map/ppermute | solution.py:619
  29.4 1.6 %collective-permute-start.10 = (bf16[64,1024]{1,0:T(8,128)(2,1)S(1)}, bf16[64,1024]{1,0:T(8,128)(2,1)S(1)}, u32[]{:S(2)}, u32[]{:S(2)}) collective-permute-start(bf16[64,1024]{1,0:T(8,128)(2,1)S(1)} %add_convert_fusion.1), channel_id=1, source_target_pairs={{0,2},{1,3},{2,0},{3,1},{4,6},{5,7},{6,4},{7,5},{8,10},{9,11},{10,... | collective-permute-start | bytes 393224 | tf_op jit(solution)/shard_map/ppermute | solution.py:619
  31.0 1.0 %collective-permute-start.7 = (bf16[64,1024]{1,0:T(8,128)(2,1)S(1)}, bf16[64,1024]{1,0:T(8,128)(2,1)S(1)}, u32[]{:S(2)}, u32[]{:S(2)}) collective-permute-start(bf16[64,1024]{1,0:T(8,128)(2,1)S(1)} %add_convert_fusion.3), channel_id=1, source_target_pairs={{0,2},{1,3},{2,0},{3,1},{4,6},{5,7},{6,4},{7,5},{8,10},{9,11},{10,... | collective-permute-start | bytes 393224 | tf_op jit(solution)/shard_map/ppermute | solution.py:619
  32.0 3.9 %collective-permute-done.10 = bf16[64,1024]{1,0:T(8,128)(2,1)S(1)} collective-permute-done((bf16[64,1024]{1,0:T(8,128)(2,1)S(1)}, bf16[64,1024]{1,0:T(8,128)(2,1)S(1)}, u32[]{:S(2)}, u32[]{:S(2)}) %collective-permute-start.10) | collective-permute-done | bytes 131104 | tf_op jit(solution)/shard_map/ppermute | solution.py:619
  35.9 0.1 collective-permute-start.11
  35.9 1.8 %collective-permute-done.7 = bf16[64,1024]{1,0:T(8,128)(2,1)S(1)} collective-permute-done((bf16[64,1024]{1,0:T(8,128)(2,1)S(1)}, bf16[64,1024]{1,0:T(8,128)(2,1)S(1)}, u32[]{:S(2)}, u32[]{:S(2)}) %collective-permute-start.7) | collective-permute-done | bytes 131104 | tf_op jit(solution)/shard_map/ppermute | solution.py:619
  37.7 0.1 collective-permute-start.8
  37.8 1.1 %shard_map.126 = bf16[1,128,512]{2,1,0:T(8,128)(2,1)} custom-call(bf16[512,1536]{1,0:T(8,128)(2,1)S(1)} %get-tuple-element.40.refs_4_.turned_ref, s32[3,1,16]{2,1,0:T(1,128)S(1)} %bitcast.6, bf16[48,512]{1,0:T(8,128)(2,1)S(1)} %get-tuple-element.58.own_slot_ref), custom_call_target="tpu_custom_call" | custom-call | flops 100000000 | bytes 4194304 | tf_op jit(solution)/shard_map/pallas_call | solution.py:606
  38.9 0.0 collective-permute-done.11.other_two_ref
  38.9 0.2 collective-permute-done.8.other_one_ref
  39.2 1.0 %shard_map.127 = f32[128,2048]{1,0:T(8,128)} custom-call(bf16[64,1024]{1,0:T(8,128)(2,1)S(1)} %add_convert_fusion.2.one_ref, bf16[64,1024]{1,0:T(8,128)(2,1)S(1)} %collective-permute-done.8.other_one_ref, bf16[64,1024]{1,0:T(8,128)(2,1)S(1)} %add_convert_fusion.two_ref, bf16[64,1024]{1,0:T(8,128)(2,1)S(1)} %collective-permute-done.11.other_two_ref), custom_call_target="tpu_custom_call" | custom-call | flops 1000000 | bytes 4194304 | tf_op jit(solution)/shard_map/pallas_call | solution.py:606
  (11 shorter events, 0.2 us)
Async XLA Ops:
  0.6 19.0 %copy-start.2 = (bf16[1,64,512]{2,1,0:T(8,128)(2,1)S(1)}, bf16[1,64,512]{2,1,0:T(8,128)(2,1)}, u32[]{:S(2)}) copy-start(bf16[1,64,512]{2,1,0:T(8,128)(2,1)} %refs_0_.2) | copy-start | bytes 196612
  2.5 8.8 %collective-permute-start = (bf16[120,512]{1,0:T(8,128)(2,1)}, bf16[120,512]{1,0:T(8,128)(2,1)S(1)}, u32[]{:S(2)}, u32[]{:S(2)}) collective-permute-start(bf16[120,512]{1,0:T(8,128)(2,1)} %shard_map.121.refs_0_), channel_id=1, source_target_pairs={{0,4},{4,0},{8,12},{12,8},{1,5},{5,1},{9,13},{13,9},{2,6},{6,2},{1... | collective-permute-start | bytes 368648 | tf_op jit(solution)/shard_map/ppermute | solution.py:619
  5.6 14.0 %collective-permute-start.1 = (bf16[120,512]{1,0:T(8,128)(2,1)}, bf16[120,512]{1,0:T(8,128)(2,1)S(1)}, u32[]{:S(2)}, u32[]{:S(2)}) collective-permute-start(bf16[120,512]{1,0:T(8,128)(2,1)} %shard_map.121.refs_0_), channel_id=1, source_target_pairs={{0,8},{4,12},{8,0},{12,4},{1,9},{5,13},{9,1},{13,5},{2,10},{6,14},... | collective-permute-start | bytes 368648 | tf_op jit(solution)/shard_map/ppermute | solution.py:619
  8.2 13.0 %collective-permute-start.2 = (bf16[120,512]{1,0:T(8,128)(2,1)}, bf16[120,512]{1,0:T(8,128)(2,1)S(1)}, u32[]{:S(2)}, u32[]{:S(2)}) collective-permute-start(bf16[120,512]{1,0:T(8,128)(2,1)} %shard_map.121.refs_0_), channel_id=1, source_target_pairs={{0,12},{4,8},{8,4},{12,0},{1,13},{5,9},{9,5},{13,1},{2,14},{6,10},... | collective-permute-start | bytes 368648 | tf_op jit(solution)/shard_map/ppermute | solution.py:619
  8.2 17.2 %collective-permute-start.3 = (bf16[1,64,512]{2,1,0:T(8,128)(2,1)}, bf16[1,64,512]{2,1,0:T(8,128)(2,1)S(1)}, u32[]{:S(2)}, u32[]{:S(2)}) collective-permute-start(bf16[1,64,512]{2,1,0:T(8,128)(2,1)} %refs_0_.2), channel_id=1, source_target_pairs={{0,4},{4,0},{8,12},{12,8},{1,5},{5,1},{9,13},{13,9},{2,6},{6,2},{1... | collective-permute-start | bytes 196616 | tf_op jit(solution)/shard_map/ppermute | solution.py:619
  9.1 1.6 %copy-start = (bf16[512,2048]{1,0:T(8,128)(2,1)S(1)}, bf16[512,2048]{1,0:T(8,128)(2,1)}, u32[]{:S(2)}) copy-start(bf16[512,2048]{1,0:T(8,128)(2,1)} %source_ref) | copy-start | bytes 6291460
  10.7 10.5 %copy-start.1 = (bf16[120,512]{1,0:T(8,128)(2,1)S(1)}, bf16[120,512]{1,0:T(8,128)(2,1)}, u32[]{:S(2)}) copy-start(bf16[120,512]{1,0:T(8,128)(2,1)} %shard_map.121.refs_0_) | copy-start | bytes 368644
  19.6 5.8 %collective-permute-start.4 = (bf16[1,64,512]{2,1,0:T(8,128)(2,1)S(1)}, bf16[1,64,512]{2,1,0:T(8,128)(2,1)S(1)}, u32[]{:S(2)}, u32[]{:S(2)}) collective-permute-start(bf16[1,64,512]{2,1,0:T(8,128)(2,1)S(1)} %copy-done.2), channel_id=1, source_target_pairs={{0,8},{4,12},{8,0},{12,4},{1,9},{5,13},{9,1},{13,5},{2,10},{6,14},... | collective-permute-start | bytes 196616 | tf_op jit(solution)/shard_map/ppermute | solution.py:619
  19.6 6.2 %collective-permute-start.5 = (bf16[1,64,512]{2,1,0:T(8,128)(2,1)S(1)}, bf16[1,64,512]{2,1,0:T(8,128)(2,1)S(1)}, u32[]{:S(2)}, u32[]{:S(2)}) collective-permute-start(bf16[1,64,512]{2,1,0:T(8,128)(2,1)S(1)} %copy-done.2), channel_id=1, source_target_pairs={{0,12},{4,8},{8,4},{12,0},{1,13},{5,9},{9,5},{13,1},{2,14},{6,10},... | collective-permute-start | bytes 196616 | tf_op jit(solution)/shard_map/ppermute | solution.py:619
  27.4 2.0 %collective-permute-start.9 = (bf16[64,1024]{1,0:T(8,128)(2,1)S(1)}, bf16[64,1024]{1,0:T(8,128)(2,1)S(1)}, u32[]{:S(2)}, u32[]{:S(2)}) collective-permute-start(bf16[64,1024]{1,0:T(8,128)(2,1)S(1)} %get-tuple-element.62), channel_id=1, source_target_pairs={{0,1},{1,0},{2,3},{3,2},{4,5},{5,4},{6,7},{7,6},{8,9},{9,8},{10,11... | collective-permute-start | bytes 393224 | tf_op jit(solution)/shard_map/ppermute | solution.py:619
  27.5 10.4 %copy-start.3 = (s32[1,3,16]{2,0,1:T(1,128)S(1)}, s32[1,3,16]{2,0,1:T(1,128)}, u32[]{:S(2)}) copy-start(s32[1,3,16]{2,0,1:T(1,128)} %param.14) | copy-start | bytes 580
  28.8 2.2 %collective-permute-start.6 = (bf16[64,1024]{1,0:T(8,128)(2,1)S(1)}, bf16[64,1024]{1,0:T(8,128)(2,1)S(1)}, u32[]{:S(2)}, u32[]{:S(2)}) collective-permute-start(bf16[64,1024]{1,0:T(8,128)(2,1)S(1)} %get-tuple-element.60), channel_id=1, source_target_pairs={{0,1},{1,0},{2,3},{3,2},{4,5},{5,4},{6,7},{7,6},{8,9},{9,8},{10,11... | collective-permute-start | bytes 393224 | tf_op jit(solution)/shard_map/ppermute | solution.py:619
  29.4 6.4 %collective-permute-start.10 = (bf16[64,1024]{1,0:T(8,128)(2,1)S(1)}, bf16[64,1024]{1,0:T(8,128)(2,1)S(1)}, u32[]{:S(2)}, u32[]{:S(2)}) collective-permute-start(bf16[64,1024]{1,0:T(8,128)(2,1)S(1)} %add_convert_fusion.1), channel_id=1, source_target_pairs={{0,2},{1,3},{2,0},{3,1},{4,6},{5,7},{6,4},{7,5},{8,10},{9,11},{10,... | collective-permute-start | bytes 393224 | tf_op jit(solution)/shard_map/ppermute | solution.py:619
  31.0 6.7 %collective-permute-start.7 = (bf16[64,1024]{1,0:T(8,128)(2,1)S(1)}, bf16[64,1024]{1,0:T(8,128)(2,1)S(1)}, u32[]{:S(2)}, u32[]{:S(2)}) collective-permute-start(bf16[64,1024]{1,0:T(8,128)(2,1)S(1)} %add_convert_fusion.3), channel_id=1, source_target_pairs={{0,2},{1,3},{2,0},{3,1},{4,6},{5,7},{6,4},{7,5},{8,10},{9,11},{10,... | collective-permute-start | bytes 393224 | tf_op jit(solution)/shard_map/ppermute | solution.py:619
  35.9 3.1 %collective-permute-start.11 = (bf16[64,1024]{1,0:T(8,128)(2,1)S(1)}, bf16[64,1024]{1,0:T(8,128)(2,1)S(1)}, u32[]{:S(2)}, u32[]{:S(2)}) collective-permute-start(bf16[64,1024]{1,0:T(8,128)(2,1)S(1)} %add_convert_fusion.two_ref), channel_id=1, source_target_pairs={{0,1},{1,0},{2,3},{3,2},{4,5},{5,4},{6,7},{7,6},{8,9},{9,8},{10,11... | collective-permute-start | bytes 393224 | tf_op jit(solution)/shard_map/ppermute | solution.py:619
  37.7 1.4 %collective-permute-start.8 = (bf16[64,1024]{1,0:T(8,128)(2,1)S(1)}, bf16[64,1024]{1,0:T(8,128)(2,1)S(1)}, u32[]{:S(2)}, u32[]{:S(2)}) collective-permute-start(bf16[64,1024]{1,0:T(8,128)(2,1)S(1)} %add_convert_fusion.2.one_ref), channel_id=1, source_target_pairs={{0,1},{1,0},{2,3},{3,2},{4,5},{5,4},{6,7},{7,6},{8,9},{9,8},{10,11... | collective-permute-start | bytes 393224 | tf_op jit(solution)/shard_map/ppermute | solution.py:619

commit v12 on v8

--- a/solution.py
+++ b/solution.py
@@ -241,12 +241,11 @@
 
 
 def pack_kernel(*refs):
-    sources, packed_ref, index_ref = refs[:8], refs[8], refs[9]
-    local, semaphores = refs[10:18], refs[18]
+    sources, packed_ref, index_ref = refs[:7], refs[7], refs[8]
+    local, semaphores = refs[9:16], refs[16]
     fetch(list(zip(sources, local)), semaphores)
     (
         grid_ref,
-        mesh_ref,
         g2m_pick_ref,
         g2m_sender_ref,
         g2m_receiver_ref,
@@ -255,7 +254,6 @@
         m2m_receiver_ref,
     ) = local
     lists, _, capacity = g2m_pick_ref.shape
-    mesh_count = mesh_ref.shape[1]
     regions, mesh_cap = m2m_pick_ref.shape[1:]
     edges = g2m_sender_ref.shape[1]
     grid_rows = grid_ref[0]
@@ -263,7 +261,6 @@
         picked = one_hot(g2m_pick_ref[i], grid_rows.shape[0])
         packed_ref[i * capacity : (i + 1) * capacity, :] = dot_first(picked, grid_rows).astype(BF16)
     first = lists * capacity
-    packed_ref[first : first + mesh_count, :] = mesh_ref[0]
     index_ref[...] = jnp.zeros_like(index_ref)
     index_ref[0:1, 0:edges] = g2m_sender_ref[...].astype(F32)
     index_ref[0:1, edges : 2 * edges] = g2m_receiver_ref[...].astype(F32)
@@ -276,7 +273,7 @@
     lane = lax.broadcasted_iota(jnp.int32, (regions, slots), 1)
     owned = lane // mesh_cap == lax.broadcasted_iota(jnp.int32, (regions, slots), 0)
     index_ref[2:3, 0:slots] = jnp.sum(jnp.where(owned, spread, 0.0), 0, keepdims=True)
-    packed_ref[first + mesh_count :, :] = index_ref[...].astype(BF16)
+    packed_ref[first:, :] = index_ref[...].astype(BF16)
 
 
 def weights_kernel(source_ref, weights_ref, turned_ref, semaphores):
@@ -327,7 +324,11 @@
     *refs,
 ):
     regions = len(steps)
-    packed_refs = refs[:regions]
+    blocks = []
+    for step in steps:
+        taken = 2
+        blocks.append((step, refs[:taken]))
+        refs = refs[taken:]
     (
         weights_ref,
         mesh_out_ref,
@@ -349,18 +350,19 @@
         index_ref,
         message_ref,
         sum_ref,
-    ) = refs[regions:]
+    ) = refs
     latent = weights_ref.shape[0]
     edges = slope_one_ref.shape[0] // regions
     capacity = listed // 3
     slots = regions * mesh_cap
     me = lax.axis_index("space")
-    for step, packed_ref in zip(steps, packed_refs):
+    for step, block_refs in blocks:
         region = lax.bitwise_xor(me, step)
         at = lambda rows: pl.ds(pl.multiple_of(region * rows, rows), rows)
-        grid_ref[at(listed), :] = packed_ref[:listed, :]
-        mesh_ref[at(mesh_count), :] = packed_ref[listed : listed + mesh_count, :]
-        index_ref[at(INDEX_ROWS), :] = packed_ref[listed + mesh_count :, :].astype(F32)
+        listed_ref, latent_ref = block_refs
+        mesh_ref[at(mesh_count), :] = latent_ref[0]
+        grid_ref[at(listed), :] = listed_ref[:listed, :]
+        index_ref[at(INDEX_ROWS), :] = listed_ref[listed:, :].astype(F32)
 
     grid_proj = dot(grid_ref[...], weights_ref[:, :latent])
     mesh_proj = dot(mesh_ref[...], weights_ref[:, latent : 2 * latent])
@@ -655,7 +657,6 @@
     g2m_pick = g2m_pick.transpose(1, 0, 2)
     sources = (
         grid_latent,
-        mesh_latent,
         g2m_pick,
         g2m_sender.reshape(1, -1),
         g2m_receiver.reshape(1, -1),
@@ -663,19 +664,18 @@
         m2m_sender.reshape(1, -1),
         m2m_receiver.reshape(1, -1),
     )
-    packed = call(
+    (listed_rows,) = call(
         pack_kernel,
         sources,
-        [((listed + mesh_count + INDEX_ROWS, latent), BF16)],
+        [((listed + INDEX_ROWS, latent), BF16)],
         [((INDEX_ROWS, latent), F32)] + [(source.shape, source.dtype) for source in sources],
         10**7,
         fetched=len(sources),
         megabytes=56,
-    )[0]
-    packed, cotangent, weights = lax.optimization_barrier((packed, mesh_cotangent, weights))
+    )
     steps = (0, *range(2, regions), 1)
-    packs = [packed] + [swap(packed, "space", step) for step in steps[1:]]
-    near = swap(cotangent, "space", 1)
+    latents = [mesh_latent] + [swap(mesh_latent, "space", step) for step in steps[1:]]
+    *latents[1:], weights = lax.optimization_barrier((*latents[1:], weights))
     weights, turned = call(
         weights_kernel,
         (weights,),
@@ -684,8 +684,11 @@
         10**8,
         fetched=1,
     )
-    near, cotangent = lax.optimization_barrier((near, cotangent))
-    cotangents = [cotangent] + [swap(cotangent, "space", step) for step in steps[1:-1]] + [near]
+    turned, cotangent = lax.optimization_barrier((turned, mesh_cotangent))
+    packs = [listed_rows, mesh_latent]
+    for step, latent_block in zip(steps[1:], latents[1:]):
+        packs += [swap(listed_rows, "space", step), latent_block]
+    cotangents = [cotangent] + [swap(cotangent, "space", step) for step in steps[1:]]
     rows = regions * mesh_count
     slots = regions * mesh_cap
     (

time: 40.7 us -> 38.6 us (0.948)
  waiting for transfers between devices: 12 us -> 6.61 us
  starting transfers between devices: 14.3 us -> 17.6 us
    ppermute x12 -> x15, waiting for transfers between devices: 12 us -> 6.61 us  [swap(): lax.ppermute(block, axis, [(i, i ^ bits) for i in range(lax.axis_size(axi...]
    ppermute x12 -> x15, starting transfers between devices: 14.3 us -> 17.6 us  [swap(): lax.ppermute(block, axis, [(i, i ^ bits) for i in range(lax.axis_size(axi...]
    unnamed x8 -> x10, local copies, waits for them, and re-layouts: 1.61 us -> 1.6 us
  transfers between devices with their start and end apart: 12 -> 15, of which waited for: 5 -> 4; matrix products, arithmetic and copies ran while one was open for 0% -> 0% of each run, Pallas kernels for 18% -> 24%
where the time goes in v12:
time: 38.6 us; the launch traced here: 38.4 us
  starting transfers between devices  17.6 us (46%)
  Pallas kernels  11.7 us (30%)
  waiting for transfers between devices  6.61 us (17%)
  local copies, waits for them, and re-layouts  1.6 us (4%)
  between operations  0.8 us (2%)
    ppermute x15, starting transfers between devices, swap(): lax.ppermute(block, axis, [(i, i ^ bits) for i in range(lax.axis_size(axi...  17.6 us
    pallas_call x7, Pallas kernels, call(): pl.pallas_call(kernel, out_shape=[jax.ShapeDtypeStruct(shape, kind) for s...  11.7 us
    ppermute x15, waiting for transfers between devices, swap(): lax.ppermute(block, axis, [(i, i ^ bits) for i in range(lax.axis_size(axi...  6.61 us
    unnamed x10, local copies, waits for them, and re-layouts  1.6 us
  transfers between devices with their start and end apart: 15, of which 4 were waited for; matrix products, arithmetic and copies ran while one was open for 0% of the time, Pallas kernels for 24%

profile of v12, /device:TPU:0, one launch (start us, length us, event | category | flops | bytes accessed | tf_op | source)
XLA Modules:
  0.0 38.4 jit_solution(10072608708330779162)
XLA Ops:
  0.7 4.1 %collective-permute-start.1 = (bf16[1,64,512]{2,1,0:T(8,128)(2,1)}, bf16[1,64,512]{2,1,0:T(8,128)(2,1)S(1)}, u32[]{:S(2)}, u32[]{:S(2)}) collective-permute-start(bf16[1,64,512]{2,1,0:T(8,128)(2,1)} %refs_1_.1), channel_id=1, source_target_pairs={{0,8},{4,12},{8,0},{12,4},{1,9},{5,13},{9,1},{13,5},{2,10},{6,14},... | collective-permute-start | bytes 196616 | tf_op jit(solution)/shard_map/ppermute | solution.py:621
  4.8 1.3 %collective-permute-start.2 = (bf16[1,64,512]{2,1,0:T(8,128)(2,1)}, bf16[1,64,512]{2,1,0:T(8,128)(2,1)S(1)}, u32[]{:S(2)}, u32[]{:S(2)}) collective-permute-start(bf16[1,64,512]{2,1,0:T(8,128)(2,1)} %refs_1_.1), channel_id=1, source_target_pairs={{0,12},{4,8},{8,4},{12,0},{1,13},{5,9},{9,5},{13,1},{2,14},{6,10},... | collective-permute-start | bytes 196616 | tf_op jit(solution)/shard_map/ppermute | solution.py:621
  6.1 0.2 collective-permute-start.3
  6.3 1.8 %shard_map.121.refs_0_ = bf16[56,512]{1,0:T(8,128)(2,1)} custom-call(bf16[1,128,512]{2,1,0:T(8,128)(2,1)} %refs_0_.1, s32[3,1,16]{2,1,0:T(1,128)} %bitcast.5, s32[1,256]{1,0:T(1,128)} %bitcast.7, s32[1,256]{1,0:T(1,128)} %bitcast.8, s32[1,4,8]{2,1,0:T(4,128)} %refs_4_.1, s32[1,256]{1,0:T(1,128)} %bitcast.9, s32[1,256]{1,0:T(1,128)} %bitcast.10), custom_call_target="tpu_custom_call" | custom-call | flops 10000000 | bytes 4194304 | tf_op jit(solution)/shard_map/pallas_call | solution.py:608
  8.2 2.9 %collective-permute-start = (bf16[56,512]{1,0:T(8,128)(2,1)}, bf16[56,512]{1,0:T(8,128)(2,1)S(1)}, u32[]{:S(2)}, u32[]{:S(2)}) collective-permute-start(bf16[56,512]{1,0:T(8,128)(2,1)} %shard_map.121.refs_0_), channel_id=1, source_target_pairs={{0,8},{4,12},{8,0},{12,4},{1,9},{5,13},{9,1},{13,5},{2,10},{6,14},... | collective-permute-start | bytes 172040 | tf_op jit(solution)/shard_map/ppermute | solution.py:621
  11.0 1.3 %collective-permute-start.4 = (bf16[56,512]{1,0:T(8,128)(2,1)}, bf16[56,512]{1,0:T(8,128)(2,1)S(1)}, u32[]{:S(2)}, u32[]{:S(2)}) collective-permute-start(bf16[56,512]{1,0:T(8,128)(2,1)} %shard_map.121.refs_0_), channel_id=1, source_target_pairs={{0,12},{4,8},{8,4},{12,0},{1,13},{5,9},{9,5},{13,1},{2,14},{6,10},... | collective-permute-start | bytes 172040 | tf_op jit(solution)/shard_map/ppermute | solution.py:621
  12.4 0.0 collective-permute-done.3.refs_7_
  12.4 0.0 copy-start
  12.4 1.6 %copy-done = bf16[512,2048]{1,0:T(8,128)(2,1)S(1)} copy-done((bf16[512,2048]{1,0:T(8,128)(2,1)S(1)}, bf16[512,2048]{1,0:T(8,128)(2,1)}, u32[]{:S(2)}) %copy-start) | copy-done | bytes 2097176
  14.0 0.6 %shard_map.122 = (bf16[512,2048]{1,0:T(8,128)(2,1)S(1)}, bf16[512,1536]{1,0:T(8,128)(2,1)S(1)}) custom-call(bf16[512,2048]{1,0:T(8,128)(2,1)S(1)} %copy-done), custom_call_target="tpu_custom_call" | custom-call | flops 100000000 | bytes 4194304 | tf_op jit(solution)/shard_map/pallas_call | solution.py:608
  14.6 3.2 %collective-permute-start.6 = (bf16[1,64,512]{2,1,0:T(8,128)(2,1)S(1)}, bf16[1,64,512]{2,1,0:T(8,128)(2,1)S(1)}, u32[]{:S(2)}, u32[]{:S(2)}) collective-permute-start(bf16[1,64,512]{2,1,0:T(8,128)(2,1)S(1)} %copy-done.1), channel_id=1, source_target_pairs={{0,8},{4,12},{8,0},{12,4},{1,9},{5,13},{9,1},{13,5},{2,10},{6,14},... | collective-permute-start | bytes 196616 | tf_op jit(solution)/shard_map/ppermute | solution.py:621
  17.9 1.2 %collective-permute-start.7 = (bf16[1,64,512]{2,1,0:T(8,128)(2,1)S(1)}, bf16[1,64,512]{2,1,0:T(8,128)(2,1)S(1)}, u32[]{:S(2)}, u32[]{:S(2)}) collective-permute-start(bf16[1,64,512]{2,1,0:T(8,128)(2,1)S(1)} %copy-done.1), channel_id=1, source_target_pairs={{0,12},{4,8},{8,4},{12,0},{1,13},{5,9},{9,5},{13,1},{2,14},{6,10},... | collective-permute-start | bytes 196616 | tf_op jit(solution)/shard_map/ppermute | solution.py:621
  19.1 0.0 collective-permute-done.refs_2_
  19.1 0.0 collective-permute-start.8
  19.1 0.0 collective-permute-done.5.refs_6_
  19.1 4.2 %shard_map.123 = (bf16[1,64,512]{2,1,0:T(8,128)(2,1)}, bf16[192,512]{1,0:T(8,128)(2,1)S(1)}, bf16[256,512]{1,0:T(8,128)(2,1)S(1)}, bf16[256,512]{1,0:T(8,128)(2,...) custom-call(bf16[56,512]{1,0:T(8,128)(2,1)S(1)} %copy-done.2, ...), custom_call_target="tpu_custom_call" | custom-call | flops 2000000000 | bytes 4194304 | tf_op jit(solution)/shard_map/pallas_call | solution.py:608
  23.3 0.0 collective-permute-done.6.refs_1_
  23.3 0.7 %collective-permute-done.7.refs_2_ = bf16[1,64,512]{2,1,0:T(8,128)(2,1)S(1)} collective-permute-done((bf16[1,64,512]{2,1,0:T(8,128)(2,1)S(1)}, bf16[1,64,512]{2,1,0:T(8,128)(2,1)S(1)}, u32[]{:S(2)}, u32[]{:S(2)}) %collective-permute-start.7) | collective-permute-done | bytes 65568 | tf_op jit(solution)/shard_map/ppermute | solution.py:621
  24.1 1.6 %shard_map.124 = (f32[256,512]{1,0:T(8,128)S(1)}, bf16[64,1024]{1,0:T(8,128)(2,1)S(1)}, bf16[64,1024]{1,0:T(8,128)(2,1)S(1)}) custom-call(bf16[1,64,512]{2,1,0:T(8,128)(2,1)S(1)} %copy-done.1, bf16[1,64,512]{2,1,0:T(8,128)(2,1)S(1)} %collective-permute-done.6.refs_1_, bf16[1,64,512]{2,1,0:T(8,128)(2,1)S(1)} %collective-permute-done.7.refs_2_, ...), custom_call_target="tpu_custom_call" | custom-call | flops 1000000000 | bytes 4194304 | tf_op jit(solution)/shard_map/pallas_call | solution.py:608
  25.7 0.1 collective-permute-start.12
  25.7 0.0 copy-start.3
  25.7 1.3 %shard_map.125 = (bf16[48,512]{1,0:T(8,128)(2,1)S(1)}, bf16[64,1024]{1,0:T(8,128)(2,1)S(1)}, bf16[64,1024]{1,0:T(8,128)(2,1)S(1)}) custom-call(bf16[192,512]{1,0:T(8,128)(2,1)S(1)} %get-tuple-element.41.grid_ref, bf16[256,512]{1,0:T(8,128)(2,1)S(1)} %get-tuple-element.42.mesh_ref, bf16[448,256]{1,0:T(8,128)(2,1)S(1)} %get-tuple-element.43.hot_ref, ...), custom_call_target="tpu_custom_call" | custom-call | flops 1000000000 | bytes 4194304 | tf_op jit(solution)/shard_map/pallas_call | solution.py:608
  27.0 0.5 %collective-permute-start.9 = (bf16[64,1024]{1,0:T(8,128)(2,1)S(1)}, bf16[64,1024]{1,0:T(8,128)(2,1)S(1)}, u32[]{:S(2)}, u32[]{:S(2)}) collective-permute-start(bf16[64,1024]{1,0:T(8,128)(2,1)S(1)} %get-tuple-element.60), channel_id=1, source_target_pairs={{0,1},{1,0},{2,3},{3,2},{4,5},{5,4},{6,7},{7,6},{8,9},{9,8},{10,11... | collective-permute-start | bytes 393224 | tf_op jit(solution)/shard_map/ppermute | solution.py:621
  27.6 1.6 %collective-permute-start.13 = (bf16[64,1024]{1,0:T(8,128)(2,1)S(1)}, bf16[64,1024]{1,0:T(8,128)(2,1)S(1)}, u32[]{:S(2)}, u32[]{:S(2)}) collective-permute-start(bf16[64,1024]{1,0:T(8,128)(2,1)S(1)} %add_convert_fusion.1), channel_id=1, source_target_pairs={{0,2},{1,3},{2,0},{3,1},{4,6},{5,7},{6,4},{7,5},{8,10},{9,11},{10,... | collective-permute-start | bytes 393224 | tf_op jit(solution)/shard_map/ppermute | solution.py:621
  29.2 1.0 %collective-permute-start.10 = (bf16[64,1024]{1,0:T(8,128)(2,1)S(1)}, bf16[64,1024]{1,0:T(8,128)(2,1)S(1)}, u32[]{:S(2)}, u32[]{:S(2)}) collective-permute-start(bf16[64,1024]{1,0:T(8,128)(2,1)S(1)} %add_convert_fusion.3), channel_id=1, source_target_pairs={{0,2},{1,3},{2,0},{3,1},{4,6},{5,7},{6,4},{7,5},{8,10},{9,11},{10,... | collective-permute-start | bytes 393224 | tf_op jit(solution)/shard_map/ppermute | solution.py:621
  30.2 3.9 %collective-permute-done.13 = bf16[64,1024]{1,0:T(8,128)(2,1)S(1)} collective-permute-done((bf16[64,1024]{1,0:T(8,128)(2,1)S(1)}, bf16[64,1024]{1,0:T(8,128)(2,1)S(1)}, u32[]{:S(2)}, u32[]{:S(2)}) %collective-permute-start.13) | collective-permute-done | bytes 131104 | tf_op jit(solution)/shard_map/ppermute | solution.py:621
  34.1 0.1 collective-permute-start.14
  34.2 1.8 %collective-permute-done.10 = bf16[64,1024]{1,0:T(8,128)(2,1)S(1)} collective-permute-done((bf16[64,1024]{1,0:T(8,128)(2,1)S(1)}, bf16[64,1024]{1,0:T(8,128)(2,1)S(1)}, u32[]{:S(2)}, u32[]{:S(2)}) %collective-permute-start.10) | collective-permute-done | bytes 131104 | tf_op jit(solution)/shard_map/ppermute | solution.py:621
  36.0 0.1 collective-permute-start.11
  36.1 1.1 %shard_map.126 = bf16[1,128,512]{2,1,0:T(8,128)(2,1)} custom-call(bf16[512,1536]{1,0:T(8,128)(2,1)S(1)} %get-tuple-element.40.refs_4_.turned_ref, s32[3,1,16]{2,1,0:T(1,128)S(1)} %bitcast.6, bf16[48,512]{1,0:T(8,128)(2,1)S(1)} %get-tuple-element.58.own_slot_ref), custom_call_target="tpu_custom_call" | custom-call | flops 100000000 | bytes 4194304 | tf_op jit(solution)/shard_map/pallas_call | solution.py:608
  37.2 0.2 collective-permute-done.11.other_one_ref
  37.4 1.0 %shard_map.127 = f32[128,2048]{1,0:T(8,128)} custom-call(bf16[64,1024]{1,0:T(8,128)(2,1)S(1)} %add_convert_fusion.2.one_ref, bf16[64,1024]{1,0:T(8,128)(2,1)S(1)} %collective-permute-done.11.other_one_ref, bf16[64,1024]{1,0:T(8,128)(2,1)S(1)} %add_convert_fusion.two_ref, bf16[64,1024]{1,0:T(8,128)(2,1)S(1)} %collective-permute-done.14.other_two_ref), custom_call_target="tpu_custom_call" | custom-call | flops 1000000 | bytes 4194304 | tf_op jit(solution)/shard_map/pallas_call | solution.py:608
  (19 shorter events, 0.2 us)
Async XLA Ops:
  0.6 18.5 %copy-start.4 = (bf16[1,64,512]{2,1,0:T(8,128)(2,1)S(1)}, bf16[1,64,512]{2,1,0:T(8,128)(2,1)}, u32[]{:S(2)}) copy-start(bf16[1,64,512]{2,1,0:T(8,128)(2,1)} %refs_1_.1) | copy-start | bytes 196612
  0.6 14.0 %copy-start.1 = (bf16[1,64,512]{2,1,0:T(8,128)(2,1)S(1)}, bf16[1,64,512]{2,1,0:T(8,128)(2,1)}, u32[]{:S(2)}) copy-start(bf16[1,64,512]{2,1,0:T(8,128)(2,1)} %refs_0_.2) | copy-start | bytes 196612
  0.7 11.7 %collective-permute-start.1 = (bf16[1,64,512]{2,1,0:T(8,128)(2,1)}, bf16[1,64,512]{2,1,0:T(8,128)(2,1)S(1)}, u32[]{:S(2)}, u32[]{:S(2)}) collective-permute-start(bf16[1,64,512]{2,1,0:T(8,128)(2,1)} %refs_1_.1), channel_id=1, source_target_pairs={{0,8},{4,12},{8,0},{12,4},{1,9},{5,13},{9,1},{13,5},{2,10},{6,14},... | collective-permute-start | bytes 196616 | tf_op jit(solution)/shard_map/ppermute | solution.py:621
  4.8 7.6 %collective-permute-start.2 = (bf16[1,64,512]{2,1,0:T(8,128)(2,1)}, bf16[1,64,512]{2,1,0:T(8,128)(2,1)S(1)}, u32[]{:S(2)}, u32[]{:S(2)}) collective-permute-start(bf16[1,64,512]{2,1,0:T(8,128)(2,1)} %refs_1_.1), channel_id=1, source_target_pairs={{0,12},{4,8},{8,4},{12,0},{1,13},{5,9},{9,5},{13,1},{2,14},{6,10},... | collective-permute-start | bytes 196616 | tf_op jit(solution)/shard_map/ppermute | solution.py:621
  6.1 6.3 %collective-permute-start.3 = (bf16[1,64,512]{2,1,0:T(8,128)(2,1)}, bf16[1,64,512]{2,1,0:T(8,128)(2,1)S(1)}, u32[]{:S(2)}, u32[]{:S(2)}) collective-permute-start(bf16[1,64,512]{2,1,0:T(8,128)(2,1)} %refs_1_.1), channel_id=1, source_target_pairs={{0,4},{4,0},{8,12},{12,8},{1,5},{5,1},{9,13},{13,9},{2,6},{6,2},{1... | collective-permute-start | bytes 196616 | tf_op jit(solution)/shard_map/ppermute | solution.py:621
  8.2 10.9 %collective-permute-start = (bf16[56,512]{1,0:T(8,128)(2,1)}, bf16[56,512]{1,0:T(8,128)(2,1)S(1)}, u32[]{:S(2)}, u32[]{:S(2)}) collective-permute-start(bf16[56,512]{1,0:T(8,128)(2,1)} %shard_map.121.refs_0_), channel_id=1, source_target_pairs={{0,8},{4,12},{8,0},{12,4},{1,9},{5,13},{9,1},{13,5},{2,10},{6,14},... | collective-permute-start | bytes 172040 | tf_op jit(solution)/shard_map/ppermute | solution.py:621
  11.0 8.0 %collective-permute-start.4 = (bf16[56,512]{1,0:T(8,128)(2,1)}, bf16[56,512]{1,0:T(8,128)(2,1)S(1)}, u32[]{:S(2)}, u32[]{:S(2)}) collective-permute-start(bf16[56,512]{1,0:T(8,128)(2,1)} %shard_map.121.refs_0_), channel_id=1, source_target_pairs={{0,12},{4,8},{8,4},{12,0},{1,13},{5,9},{9,5},{13,1},{2,14},{6,10},... | collective-permute-start | bytes 172040 | tf_op jit(solution)/shard_map/ppermute | solution.py:621
  12.4 6.7 %collective-permute-start.5 = (bf16[56,512]{1,0:T(8,128)(2,1)}, bf16[56,512]{1,0:T(8,128)(2,1)S(1)}, u32[]{:S(2)}, u32[]{:S(2)}) collective-permute-start(bf16[56,512]{1,0:T(8,128)(2,1)} %shard_map.121.refs_0_), channel_id=1, source_target_pairs={{0,4},{4,0},{8,12},{12,8},{1,5},{5,1},{9,13},{13,9},{2,6},{6,2},{1... | collective-permute-start | bytes 172040 | tf_op jit(solution)/shard_map/ppermute | solution.py:621
  12.4 1.6 %copy-start = (bf16[512,2048]{1,0:T(8,128)(2,1)S(1)}, bf16[512,2048]{1,0:T(8,128)(2,1)}, u32[]{:S(2)}) copy-start(bf16[512,2048]{1,0:T(8,128)(2,1)} %source_ref) | copy-start | bytes 6291460
  14.0 5.1 %copy-start.2 = (bf16[56,512]{1,0:T(8,128)(2,1)S(1)}, bf16[56,512]{1,0:T(8,128)(2,1)}, u32[]{:S(2)}) copy-start(bf16[56,512]{1,0:T(8,128)(2,1)} %shard_map.121.refs_0_) | copy-start | bytes 172036
  14.6 8.7 %collective-permute-start.6 = (bf16[1,64,512]{2,1,0:T(8,128)(2,1)S(1)}, bf16[1,64,512]{2,1,0:T(8,128)(2,1)S(1)}, u32[]{:S(2)}, u32[]{:S(2)}) collective-permute-start(bf16[1,64,512]{2,1,0:T(8,128)(2,1)S(1)} %copy-done.1), channel_id=1, source_target_pairs={{0,8},{4,12},{8,0},{12,4},{1,9},{5,13},{9,1},{13,5},{2,10},{6,14},... | collective-permute-start | bytes 196616 | tf_op jit(solution)/shard_map/ppermute | solution.py:621
  17.9 6.2 %collective-permute-start.7 = (bf16[1,64,512]{2,1,0:T(8,128)(2,1)S(1)}, bf16[1,64,512]{2,1,0:T(8,128)(2,1)S(1)}, u32[]{:S(2)}, u32[]{:S(2)}) collective-permute-start(bf16[1,64,512]{2,1,0:T(8,128)(2,1)S(1)} %copy-done.1), channel_id=1, source_target_pairs={{0,12},{4,8},{8,4},{12,0},{1,13},{5,9},{9,5},{13,1},{2,14},{6,10},... | collective-permute-start | bytes 196616 | tf_op jit(solution)/shard_map/ppermute | solution.py:621
  19.1 5.0 %collective-permute-start.8 = (bf16[1,64,512]{2,1,0:T(8,128)(2,1)S(1)}, bf16[1,64,512]{2,1,0:T(8,128)(2,1)S(1)}, u32[]{:S(2)}, u32[]{:S(2)}) collective-permute-start(bf16[1,64,512]{2,1,0:T(8,128)(2,1)S(1)} %copy-done.1), channel_id=1, source_target_pairs={{0,4},{4,0},{8,12},{12,8},{1,5},{5,1},{9,13},{13,9},{2,6},{6,2},{1... | collective-permute-start | bytes 196616 | tf_op jit(solution)/shard_map/ppermute | solution.py:621
  25.7 1.9 %collective-permute-start.12 = (bf16[64,1024]{1,0:T(8,128)(2,1)S(1)}, bf16[64,1024]{1,0:T(8,128)(2,1)S(1)}, u32[]{:S(2)}, u32[]{:S(2)}) collective-permute-start(bf16[64,1024]{1,0:T(8,128)(2,1)S(1)} %get-tuple-element.62), channel_id=1, source_target_pairs={{0,1},{1,0},{2,3},{3,2},{4,5},{5,4},{6,7},{7,6},{8,9},{9,8},{10,11... | collective-permute-start | bytes 393224 | tf_op jit(solution)/shard_map/ppermute | solution.py:621
  25.7 10.3 %copy-start.3 = (s32[1,3,16]{2,0,1:T(1,128)S(1)}, s32[1,3,16]{2,0,1:T(1,128)}, u32[]{:S(2)}) copy-start(s32[1,3,16]{2,0,1:T(1,128)} %param.14) | copy-start | bytes 580
  27.0 2.2 %collective-permute-start.9 = (bf16[64,1024]{1,0:T(8,128)(2,1)S(1)}, bf16[64,1024]{1,0:T(8,128)(2,1)S(1)}, u32[]{:S(2)}, u32[]{:S(2)}) collective-permute-start(bf16[64,1024]{1,0:T(8,128)(2,1)S(1)} %get-tuple-element.60), channel_id=1, source_target_pairs={{0,1},{1,0},{2,3},{3,2},{4,5},{5,4},{6,7},{7,6},{8,9},{9,8},{10,11... | collective-permute-start | bytes 393224 | tf_op jit(solution)/shard_map/ppermute | solution.py:621
  27.6 6.4 %collective-permute-start.13 = (bf16[64,1024]{1,0:T(8,128)(2,1)S(1)}, bf16[64,1024]{1,0:T(8,128)(2,1)S(1)}, u32[]{:S(2)}, u32[]{:S(2)}) collective-permute-start(bf16[64,1024]{1,0:T(8,128)(2,1)S(1)} %add_convert_fusion.1), channel_id=1, source_target_pairs={{0,2},{1,3},{2,0},{3,1},{4,6},{5,7},{6,4},{7,5},{8,10},{9,11},{10,... | collective-permute-start | bytes 393224 | tf_op jit(solution)/shard_map/ppermute | solution.py:621
  29.2 6.7 %collective-permute-start.10 = (bf16[64,1024]{1,0:T(8,128)(2,1)S(1)}, bf16[64,1024]{1,0:T(8,128)(2,1)S(1)}, u32[]{:S(2)}, u32[]{:S(2)}) collective-permute-start(bf16[64,1024]{1,0:T(8,128)(2,1)S(1)} %add_convert_fusion.3), channel_id=1, source_target_pairs={{0,2},{1,3},{2,0},{3,1},{4,6},{5,7},{6,4},{7,5},{8,10},{9,11},{10,... | collective-permute-start | bytes 393224 | tf_op jit(solution)/shard_map/ppermute | solution.py:621
  34.1 3.1 %collective-permute-start.14 = (bf16[64,1024]{1,0:T(8,128)(2,1)S(1)}, bf16[64,1024]{1,0:T(8,128)(2,1)S(1)}, u32[]{:S(2)}, u32[]{:S(2)}) collective-permute-start(bf16[64,1024]{1,0:T(8,128)(2,1)S(1)} %add_convert_fusion.two_ref), channel_id=1, source_target_pairs={{0,1},{1,0},{2,3},{3,2},{4,5},{5,4},{6,7},{7,6},{8,9},{9,8},{10,11... | collective-permute-start | bytes 393224 | tf_op jit(solution)/shard_map/ppermute | solution.py:621
  36.0 1.4 %collective-permute-start.11 = (bf16[64,1024]{1,0:T(8,128)(2,1)S(1)}, bf16[64,1024]{1,0:T(8,128)(2,1)S(1)}, u32[]{:S(2)}, u32[]{:S(2)}) collective-permute-start(bf16[64,1024]{1,0:T(8,128)(2,1)S(1)} %add_convert_fusion.2.one_ref), channel_id=1, source_target_pairs={{0,1},{1,0},{2,3},{3,2},{4,5},{5,4},{6,7},{7,6},{8,9},{9,8},{10,11... | collective-permute-start | bytes 393224 | tf_op jit(solution)/shard_map/ppermute | solution.py:621

commit v13 on v12

--- a/solution.py
+++ b/solution.py
@@ -211,6 +211,10 @@
     return lax.dot_general(left, right, (((0,), (0,)), ((), ())), preferred_element_type=F32)
 
 
+def dot_last(left, right):
+    return lax.dot_general(left, right, (((1,), (1,)), ((), ())), preferred_element_type=F32)
+
+
 def one_hot(labels, count):
     rows = lax.broadcasted_iota(jnp.int32, (count, labels.shape[-1]), 0)
     return (rows == labels).astype(F32).astype(BF16)
@@ -241,8 +245,10 @@
 
 
 def pack_kernel(*refs):
-    sources, packed_ref, index_ref = refs[:7], refs[7], refs[8]
-    local, semaphores = refs[9:16], refs[16]
+    *sources, weights_source_ref, packed_ref, weights_ref, index_ref = refs[:11]
+    local, semaphores = refs[11:18], refs[18]
+    weights_copy = pltpu.make_async_copy(weights_source_ref, weights_ref, semaphores.at[7])
+    weights_copy.start()
     fetch(list(zip(sources, local)), semaphores)
     (
         grid_ref,
@@ -274,15 +280,7 @@
     owned = lane // mesh_cap == lax.broadcasted_iota(jnp.int32, (regions, slots), 0)
     index_ref[2:3, 0:slots] = jnp.sum(jnp.where(owned, spread, 0.0), 0, keepdims=True)
     packed_ref[first:, :] = index_ref[...].astype(BF16)
-
-
-def weights_kernel(source_ref, weights_ref, turned_ref, semaphores):
-    fetch([(source_ref, weights_ref)], semaphores)
-    latent = weights_ref.shape[0]
-    for n, block in enumerate((0, 2, 3)):
-        turned_ref[:, n * latent : (n + 1) * latent] = weights_ref[
-            :, block * latent : (block + 1) * latent
-        ].T
+    weights_copy.wait()
 
 
 def edge_blocks(edges):
@@ -480,7 +478,7 @@
     regions = len(steps)
     cotangent_refs = refs[:regions]
     (
-        turned_ref,
+        weights_ref,
         first_ref,
         sent_ref,
         hot_ref,
@@ -521,8 +519,8 @@
     share_ref[:, :latent] = dot_first(sent_ref[:, mine], slot_sum).astype(BF16)
     share_ref[:, latent:] = dot_first(first_ref[:, mine], recv_ref[...]).astype(BF16)
     halve(share_ref, keep_ref, give_ref)
-    returned = dot(slot_sum, turned_ref[:, latent : 2 * latent]).astype(BF16)
-    grad = upstream_ref[...] + dot(recv_ref[...], turned_ref[:, 2 * latent :])
+    returned = dot_last(slot_sum, weights_ref[:, 2 * latent : 3 * latent]).astype(BF16)
+    grad = upstream_ref[...] + dot_last(recv_ref[...], weights_ref[:, 3 * latent :])
     for s in range(regions):
         rows = slice(s * mesh_count, (s + 1) * mesh_count)
         mesh_grad_ref[rows, :] = grad[rows] + dot(
@@ -577,10 +575,10 @@
     own_slot_ref[...] = slot_ref[own, :]
 
 
-def grid_back_kernel(turned_ref, pick_ref, own_slot_ref, grid_grad_ref):
+def grid_back_kernel(weights_ref, pick_ref, own_slot_ref, grid_grad_ref):
     lists, _, capacity = pick_ref.shape
     latent = own_slot_ref.shape[1]
-    returned = dot(own_slot_ref[...], turned_ref[:, :latent]).astype(BF16)
+    returned = dot_last(own_slot_ref[...], weights_ref[:, :latent]).astype(BF16)
     total = None
     for i in range(lists):
         owner = one_hot(pick_ref[i], grid_grad_ref.shape[1])
@@ -603,8 +601,12 @@
 VMEM = pl.BlockSpec(memory_space=pltpu.VMEM)
 
 
-def call(kernel, operands, outputs, scratch, flops, fetched=0, megabytes=40):
+def call(kernel, operands, outputs, scratch, flops, fetched=0):
     hbm = pl.BlockSpec(memory_space=pltpu.HBM)
+    operands = [
+        pltpu.with_memory_space_constraint(operand, pltpu.HBM) if n < fetched else operand
+        for n, operand in enumerate(operands)
+    ]
     return pl.pallas_call(
         kernel,
         out_shape=[jax.ShapeDtypeStruct(shape, kind) for shape, kind in outputs],
@@ -612,7 +614,7 @@
         out_specs=[VMEM] * len(outputs),
         scratch_shapes=[pltpu.VMEM(shape, kind) for shape, kind in scratch]
         + ([pltpu.SemaphoreType.DMA((fetched,))] if fetched else []),
-        compiler_params=pltpu.CompilerParams(vmem_limit_bytes=megabytes << 20),
+        compiler_params=pltpu.CompilerParams(vmem_limit_bytes=40 << 20),
         cost_estimate=pl.CostEstimate(flops=flops, bytes_accessed=4 << 20, transcendentals=0),
     )(*operands)
 
@@ -664,31 +666,21 @@
         m2m_sender.reshape(1, -1),
         m2m_receiver.reshape(1, -1),
     )
-    (listed_rows,) = call(
+    listed_rows, weights = call(
         pack_kernel,
-        sources,
-        [((listed + INDEX_ROWS, latent), BF16)],
+        (*sources, weights),
+        [((listed + INDEX_ROWS, latent), BF16), (weights.shape, BF16)],
         [((INDEX_ROWS, latent), F32)] + [(source.shape, source.dtype) for source in sources],
         10**7,
-        fetched=len(sources),
-        megabytes=56,
+        fetched=len(sources) + 1,
     )
     steps = (0, *range(2, regions), 1)
     latents = [mesh_latent] + [swap(mesh_latent, "space", step) for step in steps[1:]]
-    *latents[1:], weights = lax.optimization_barrier((*latents[1:], weights))
-    weights, turned = call(
-        weights_kernel,
-        (weights,),
-        [(weights.shape, BF16), ((latent, 3 * latent), BF16)],
-        [],
-        10**8,
-        fetched=1,
-    )
-    turned, cotangent = lax.optimization_barrier((turned, mesh_cotangent))
+    *latents[1:], cotangent = lax.optimization_barrier((*latents[1:], mesh_cotangent))
     packs = [listed_rows, mesh_latent]
     for step, latent_block in zip(steps[1:], latents[1:]):
         packs += [swap(listed_rows, "space", step), latent_block]
-    cotangents = [cotangent] + [swap(cotangent, "space", step) for step in steps[1:]]
+    cotangents = [mesh_cotangent] + [swap(cotangent, "space", step) for step in steps[1:]]
     rows = regions * mesh_count
     slots = regions * mesh_cap
     (
@@ -740,7 +732,7 @@
         functools.partial(process_back_kernel, steps, mesh_cap),
         (
             *cotangents,
-            turned,
+            weights,
             mesh_first,
             mesh_sent,
             hot_two,
@@ -783,7 +775,7 @@
     )
     grid_grad = call(
         grid_back_kernel,
-        (turned, g2m_pick, own_slots),
+        (weights, g2m_pick, own_slots),
         [(grid_latent.shape, BF16)],
         [],
         10**8,

time: 38.6 us -> 40.4 us (1.047)
  waiting for transfers between devices: 6.61 us -> 11.1 us
  local copies, waits for them, and re-layouts: 1.6 us -> 0.01 us
  starting transfers between devices: 17.6 us -> 17 us
    ppermute x15, waiting for transfers between devices: 6.61 us -> 11.1 us  [swap(): lax.ppermute(block, axis, [(i, i ^ bits) for i in range(lax.axis_size(axi...]
    unnamed x10 -> x6, local copies, waits for them, and re-layouts: 1.6 us -> 0.01 us
    ppermute x15, starting transfers between devices: 17.6 us -> 17 us  [swap(): lax.ppermute(block, axis, [(i, i ^ bits) for i in range(lax.axis_size(axi...]
    pallas_call x7 -> x6, Pallas kernels: 11.7 us -> 11.3 us  [call(): pl.pallas_call(kernel, out_shape=[jax.ShapeDtypeStruct(shape, kind) for s...]
  transfers between devices with their start and end apart: 15 -> 15, of which waited for: 4 -> 5; matrix products, arithmetic and copies ran while one was open for 0% -> 0% of each run, Pallas kernels for 24% -> 18%
where the time goes in v13:
time: 40.4 us; the launch traced here: 40.3 us
  starting transfers between devices  17 us (42%)
  Pallas kernels  11.3 us (28%)
  waiting for transfers between devices  11.1 us (27%)
  between operations  0.75 us (2%)
    ppermute x15, starting transfers between devices, swap(): lax.ppermute(block, axis, [(i, i ^ bits) for i in range(lax.axis_size(axi...  17 us
    pallas_call x6, Pallas kernels, call(): pl.pallas_call(kernel, out_shape=[jax.ShapeDtypeStruct(shape, kind) for s...  11.3 us
    ppermute x15, waiting for transfers between devices, swap(): lax.ppermute(block, axis, [(i, i ^ bits) for i in range(lax.axis_size(axi...  11.1 us
  transfers between devices with their start and end apart: 15, of which 5 were waited for; matrix products, arithmetic and copies ran while one was open for 0% of the time, Pallas kernels for 18%

profile of v13, /device:TPU:0, one launch (start us, length us, event | category | flops | bytes accessed | tf_op | source)
XLA Modules:
  0.0 40.3 jit_solution(2906597682853873044)
XLA Ops:
  0.7 5.1 %collective-permute-start.2 = (bf16[1,64,512]{2,1,0:T(8,128)(2,1)}, bf16[1,64,512]{2,1,0:T(8,128)(2,1)S(1)}, u32[]{:S(2)}, u32[]{:S(2)}) collective-permute-start(bf16[1,64,512]{2,1,0:T(8,128)(2,1)} %refs_1_.1), channel_id=1, source_target_pairs={{0,12},{4,8},{8,4},{12,0},{1,13},{5,9},{9,5},{13,1},{2,14},{6,10},... | collective-permute-start | bytes 196616 | tf_op jit(solution)/shard_map/ppermute | solution.py:623
  5.8 0.0 collective-permute-start.1
  5.8 0.6 %collective-permute-start.3 = (bf16[1,64,512]{2,1,0:T(8,128)(2,1)}, bf16[1,64,512]{2,1,0:T(8,128)(2,1)S(1)}, u32[]{:S(2)}, u32[]{:S(2)}) collective-permute-start(bf16[1,64,512]{2,1,0:T(8,128)(2,1)} %refs_1_.1), channel_id=1, source_target_pairs={{0,4},{4,0},{8,12},{12,8},{1,5},{5,1},{9,13},{13,9},{2,6},{6,2},{1... | collective-permute-start | bytes 196616 | tf_op jit(solution)/shard_map/ppermute | solution.py:623
  6.4 1.8 %shard_map.121 = (bf16[56,512]{1,0:T(8,128)(2,1)S(1)}, bf16[512,2048]{1,0:T(8,128)(2,1)S(1)}) custom-call(bf16[1,128,512]{2,1,0:T(8,128)(2,1)} %refs_0_.2, s32[3,1,16]{2,1,0:T(1,128)} %bitcast.5, s32[1,256]{1,0:T(1,128)} %bitcast.7, s32[1,256]{1,0:T(1,128)} %bitcast.8, s32[1,4,8]{2,1,0:T(4,128)} %refs_4_.1, s32[1,256]{1,0:T(1,128)} %bitcast.9, ...), custom_call_target="tpu_custom_call" | custom-call | flops 10000000 | bytes 4194304 | tf_op jit(solution)/shard_map/pallas_call | solution.py:610
  8.3 1.5 %collective-permute-start.5 = (bf16[56,512]{1,0:T(8,128)(2,1)S(1)}, bf16[56,512]{1,0:T(8,128)(2,1)S(1)}, u32[]{:S(2)}, u32[]{:S(2)}) collective-permute-start(bf16[56,512]{1,0:T(8,128)(2,1)S(1)} %get-tuple-element.31.refs_0_), channel_id=1, source_target_pairs={{0,4},{4,0},{8,12},{12,8},{1,5},{5,1},{9,13},{13,9},{2,6},{6,2},{1... | collective-permute-start | bytes 172040 | tf_op jit(solution)/shard_map/ppermute | solution.py:623
  9.7 2.4 %collective-permute-start.4 = (bf16[56,512]{1,0:T(8,128)(2,1)S(1)}, bf16[56,512]{1,0:T(8,128)(2,1)S(1)}, u32[]{:S(2)}, u32[]{:S(2)}) collective-permute-start(bf16[56,512]{1,0:T(8,128)(2,1)S(1)} %get-tuple-element.31.refs_0_), channel_id=1, source_target_pairs={{0,12},{4,8},{8,4},{12,0},{1,13},{5,9},{9,5},{13,1},{2,14},{6,10},... | collective-permute-start | bytes 172040 | tf_op jit(solution)/shard_map/ppermute | solution.py:623
  12.2 0.5 %collective-permute-start = (bf16[56,512]{1,0:T(8,128)(2,1)S(1)}, bf16[56,512]{1,0:T(8,128)(2,1)S(1)}, u32[]{:S(2)}, u32[]{:S(2)}) collective-permute-start(bf16[56,512]{1,0:T(8,128)(2,1)S(1)} %get-tuple-element.31.refs_0_), channel_id=1, source_target_pairs={{0,8},{4,12},{8,0},{12,4},{1,9},{5,13},{9,1},{13,5},{2,10},{6,14},... | collective-permute-start | bytes 172040 | tf_op jit(solution)/shard_map/ppermute | solution.py:623
  12.6 0.0 collective-permute-done.1.refs_3_
  12.6 0.0 collective-permute-done.3.refs_7_
  12.7 1.5 %collective-permute-start.8 = (bf16[1,64,512]{2,1,0:T(8,128)(2,1)S(1)}, bf16[1,64,512]{2,1,0:T(8,128)(2,1)S(1)}, u32[]{:S(2)}, u32[]{:S(2)}) collective-permute-start(bf16[1,64,512]{2,1,0:T(8,128)(2,1)S(1)} %copy-done), channel_id=1, source_target_pairs={{0,4},{4,0},{8,12},{12,8},{1,5},{5,1},{9,13},{13,9},{2,6},{6,2},{1... | collective-permute-start | bytes 196616 | tf_op jit(solution)/shard_map/ppermute | solution.py:623
  14.2 2.4 %collective-permute-start.7 = (bf16[1,64,512]{2,1,0:T(8,128)(2,1)S(1)}, bf16[1,64,512]{2,1,0:T(8,128)(2,1)S(1)}, u32[]{:S(2)}, u32[]{:S(2)}) collective-permute-start(bf16[1,64,512]{2,1,0:T(8,128)(2,1)S(1)} %copy-done), channel_id=1, source_target_pairs={{0,12},{4,8},{8,4},{12,0},{1,13},{5,9},{9,5},{13,1},{2,14},{6,10},... | collective-permute-start | bytes 196616 | tf_op jit(solution)/shard_map/ppermute | solution.py:623
  16.6 0.0 collective-permute-done.5.refs_6_
  16.6 0.0 collective-permute-start.6
  16.6 4.0 %collective-permute-done.refs_2_ = bf16[56,512]{1,0:T(8,128)(2,1)S(1)} collective-permute-done((bf16[56,512]{1,0:T(8,128)(2,1)S(1)}, bf16[56,512]{1,0:T(8,128)(2,1)S(1)}, u32[]{:S(2)}, u32[]{:S(2)}) %collective-permute-start) | collective-permute-done | bytes 57376 | tf_op jit(solution)/shard_map/ppermute | solution.py:623
  20.6 4.2 %shard_map.122 = (bf16[1,64,512]{2,1,0:T(8,128)(2,1)}, bf16[192,512]{1,0:T(8,128)(2,1)S(1)}, bf16[256,512]{1,0:T(8,128)(2,1)S(1)}, bf16[256,512]{1,0:T(8,128)(2,...) custom-call(bf16[56,512]{1,0:T(8,128)(2,1)S(1)} %get-tuple-element.3, ...), custom_call_target="tpu_custom_call" | custom-call | flops 2000000000 | bytes 4194304 | tf_op jit(solution)/shard_map/pallas_call | solution.py:610
  24.8 0.0 collective-permute-done.6.refs_1_
  24.8 1.8 %shard_map.123 = (f32[256,512]{1,0:T(8,128)S(1)}, bf16[64,1024]{1,0:T(8,128)(2,1)S(1)}, bf16[64,1024]{1,0:T(8,128)(2,1)S(1)}) custom-call(bf16[1,64,512]{2,1,0:T(8,128)(2,1)S(1)} %copy-done, bf16[1,64,512]{2,1,0:T(8,128)(2,1)S(1)} %collective-permute-done.6.refs_1_, bf16[1,64,512]{2,1,0:T(8,128)(2,1)S(1)} %collective-permute-done.7.refs_2_, ...), custom_call_target="tpu_custom_call" | custom-call | flops 1000000000 | bytes 4194304 | tf_op jit(solution)/shard_map/pallas_call | solution.py:610
  26.6 0.0 copy-start.1
  26.6 1.3 %shard_map.124 = (bf16[48,512]{1,0:T(8,128)(2,1)S(1)}, bf16[64,1024]{1,0:T(8,128)(2,1)S(1)}, bf16[64,1024]{1,0:T(8,128)(2,1)S(1)}) custom-call(bf16[192,512]{1,0:T(8,128)(2,1)S(1)} %get-tuple-element.37.grid_ref, bf16[256,512]{1,0:T(8,128)(2,1)S(1)} %get-tuple-element.38.mesh_ref, bf16[448,256]{1,0:T(8,128)(2,1)S(1)} %get-tuple-element.39.hot_ref, ...), custom_call_target="tpu_custom_call" | custom-call | flops 1000000000 | bytes 4194304 | tf_op jit(solution)/shard_map/pallas_call | solution.py:610
  27.9 0.1 collective-permute-start.9
  28.0 0.5 %collective-permute-start.12 = (bf16[64,1024]{1,0:T(8,128)(2,1)S(1)}, bf16[64,1024]{1,0:T(8,128)(2,1)S(1)}, u32[]{:S(2)}, u32[]{:S(2)}) collective-permute-start(bf16[64,1024]{1,0:T(8,128)(2,1)S(1)} %get-tuple-element.58), channel_id=1, source_target_pairs={{0,1},{1,0},{2,3},{3,2},{4,5},{5,4},{6,7},{7,6},{8,9},{9,8},{10,11... | collective-permute-start | bytes 393224 | tf_op jit(solution)/shard_map/ppermute | solution.py:623
  28.5 0.8 %collective-permute-done.9 = bf16[64,1024]{1,0:T(8,128)(2,1)S(1)} collective-permute-done((bf16[64,1024]{1,0:T(8,128)(2,1)S(1)}, bf16[64,1024]{1,0:T(8,128)(2,1)S(1)}, u32[]{:S(2)}, u32[]{:S(2)}) %collective-permute-start.9) | collective-permute-done | bytes 131104 | tf_op jit(solution)/shard_map/ppermute | solution.py:623
  29.4 1.5 %collective-permute-start.10 = (bf16[64,1024]{1,0:T(8,128)(2,1)S(1)}, bf16[64,1024]{1,0:T(8,128)(2,1)S(1)}, u32[]{:S(2)}, u32[]{:S(2)}) collective-permute-start(bf16[64,1024]{1,0:T(8,128)(2,1)S(1)} %add_convert_fusion.3), channel_id=1, source_target_pairs={{0,2},{1,3},{2,0},{3,1},{4,6},{5,7},{6,4},{7,5},{8,10},{9,11},{10,... | collective-permute-start | bytes 393224 | tf_op jit(solution)/shard_map/ppermute | solution.py:623
  31.0 0.6 %collective-permute-start.13 = (bf16[64,1024]{1,0:T(8,128)(2,1)S(1)}, bf16[64,1024]{1,0:T(8,128)(2,1)S(1)}, u32[]{:S(2)}, u32[]{:S(2)}) collective-permute-start(bf16[64,1024]{1,0:T(8,128)(2,1)S(1)} %add_convert_fusion.1), channel_id=1, source_target_pairs={{0,2},{1,3},{2,0},{3,1},{4,6},{5,7},{6,4},{7,5},{8,10},{9,11},{10,... | collective-permute-start | bytes 393224 | tf_op jit(solution)/shard_map/ppermute | solution.py:623
  31.6 4.2 %collective-permute-done.10 = bf16[64,1024]{1,0:T(8,128)(2,1)S(1)} collective-permute-done((bf16[64,1024]{1,0:T(8,128)(2,1)S(1)}, bf16[64,1024]{1,0:T(8,128)(2,1)S(1)}, u32[]{:S(2)}, u32[]{:S(2)}) %collective-permute-start.10) | collective-permute-done | bytes 131104 | tf_op jit(solution)/shard_map/ppermute | solution.py:623
  35.8 0.1 collective-permute-start.11
  35.9 1.9 %collective-permute-done.13 = bf16[64,1024]{1,0:T(8,128)(2,1)S(1)} collective-permute-done((bf16[64,1024]{1,0:T(8,128)(2,1)S(1)}, bf16[64,1024]{1,0:T(8,128)(2,1)S(1)}, u32[]{:S(2)}, u32[]{:S(2)}) %collective-permute-start.13) | collective-permute-done | bytes 131104 | tf_op jit(solution)/shard_map/ppermute | solution.py:623
  37.8 0.1 collective-permute-start.14
  37.9 1.2 %shard_map.125 = bf16[1,128,512]{2,1,0:T(8,128)(2,1)} custom-call(bf16[512,2048]{1,0:T(8,128)(2,1)S(1)} %get-tuple-element.35.refs_8_.refs_4_.weights_ref, s32[3,1,16]{2,1,0:T(1,128)S(1)} %bitcast.6, bf16[48,512]{1,0:T(8,128)(2,1)S(1)} %get-tuple-element.54.own_slot_ref), custom_call_target="tpu_custom_call" | custom-call | flops 100000000 | bytes 4194304 | tf_op jit(solution)/shard_map/pallas_call | solution.py:610
  39.1 0.0 collective-permute-done.11.other_one_ref
  39.1 0.2 collective-permute-done.14.other_two_ref
  39.2 1.0 %shard_map.126 = f32[128,2048]{1,0:T(8,128)} custom-call(bf16[64,1024]{1,0:T(8,128)(2,1)S(1)} %add_convert_fusion.2.one_ref, bf16[64,1024]{1,0:T(8,128)(2,1)S(1)} %collective-permute-done.11.other_one_ref, bf16[64,1024]{1,0:T(8,128)(2,1)S(1)} %add_convert_fusion.two_ref, bf16[64,1024]{1,0:T(8,128)(2,1)S(1)} %collective-permute-done.14.other_two_ref), custom_call_target="tpu_custom_call" | custom-call | flops 1000000 | bytes 4194304 | tf_op jit(solution)/shard_map/pallas_call | solution.py:610
  (14 shorter events, 0.2 us)
Async XLA Ops:
  0.6 20.0 %copy-start.2 = (bf16[1,64,512]{2,1,0:T(8,128)(2,1)S(1)}, bf16[1,64,512]{2,1,0:T(8,128)(2,1)}, u32[]{:S(2)}) copy-start(bf16[1,64,512]{2,1,0:T(8,128)(2,1)} %refs_1_.1) | copy-start | bytes 196612
  0.6 12.0 %copy-start = (bf16[1,64,512]{2,1,0:T(8,128)(2,1)S(1)}, bf16[1,64,512]{2,1,0:T(8,128)(2,1)}, u32[]{:S(2)}) copy-start(bf16[1,64,512]{2,1,0:T(8,128)(2,1)} %refs_0_.3) | copy-start | bytes 196612
  0.7 11.5 %collective-permute-start.2 = (bf16[1,64,512]{2,1,0:T(8,128)(2,1)}, bf16[1,64,512]{2,1,0:T(8,128)(2,1)S(1)}, u32[]{:S(2)}, u32[]{:S(2)}) collective-permute-start(bf16[1,64,512]{2,1,0:T(8,128)(2,1)} %refs_1_.1), channel_id=1, source_target_pairs={{0,12},{4,8},{8,4},{12,0},{1,13},{5,9},{9,5},{13,1},{2,14},{6,10},... | collective-permute-start | bytes 196616 | tf_op jit(solution)/shard_map/ppermute | solution.py:623
  5.8 6.9 %collective-permute-start.1 = (bf16[1,64,512]{2,1,0:T(8,128)(2,1)}, bf16[1,64,512]{2,1,0:T(8,128)(2,1)S(1)}, u32[]{:S(2)}, u32[]{:S(2)}) collective-permute-start(bf16[1,64,512]{2,1,0:T(8,128)(2,1)} %refs_1_.1), channel_id=1, source_target_pairs={{0,8},{4,12},{8,0},{12,4},{1,9},{5,13},{9,1},{13,5},{2,10},{6,14},... | collective-permute-start | bytes 196616 | tf_op jit(solution)/shard_map/ppermute | solution.py:623
  5.8 6.9 %collective-permute-start.3 = (bf16[1,64,512]{2,1,0:T(8,128)(2,1)}, bf16[1,64,512]{2,1,0:T(8,128)(2,1)S(1)}, u32[]{:S(2)}, u32[]{:S(2)}) collective-permute-start(bf16[1,64,512]{2,1,0:T(8,128)(2,1)} %refs_1_.1), channel_id=1, source_target_pairs={{0,4},{4,0},{8,12},{12,8},{1,5},{5,1},{9,13},{13,9},{2,6},{6,2},{1... | collective-permute-start | bytes 196616 | tf_op jit(solution)/shard_map/ppermute | solution.py:623
  8.3 8.4 %collective-permute-start.5 = (bf16[56,512]{1,0:T(8,128)(2,1)S(1)}, bf16[56,512]{1,0:T(8,128)(2,1)S(1)}, u32[]{:S(2)}, u32[]{:S(2)}) collective-permute-start(bf16[56,512]{1,0:T(8,128)(2,1)S(1)} %get-tuple-element.31.refs_0_), channel_id=1, source_target_pairs={{0,4},{4,0},{8,12},{12,8},{1,5},{5,1},{9,13},{13,9},{2,6},{6,2},{1... | collective-permute-start | bytes 172040 | tf_op jit(solution)/shard_map/ppermute | solution.py:623
  9.7 6.9 %collective-permute-start.4 = (bf16[56,512]{1,0:T(8,128)(2,1)S(1)}, bf16[56,512]{1,0:T(8,128)(2,1)S(1)}, u32[]{:S(2)}, u32[]{:S(2)}) collective-permute-start(bf16[56,512]{1,0:T(8,128)(2,1)S(1)} %get-tuple-element.31.refs_0_), channel_id=1, source_target_pairs={{0,12},{4,8},{8,4},{12,0},{1,13},{5,9},{9,5},{13,1},{2,14},{6,10},... | collective-permute-start | bytes 172040 | tf_op jit(solution)/shard_map/ppermute | solution.py:623
  12.2 8.5 %collective-permute-start = (bf16[56,512]{1,0:T(8,128)(2,1)S(1)}, bf16[56,512]{1,0:T(8,128)(2,1)S(1)}, u32[]{:S(2)}, u32[]{:S(2)}) collective-permute-start(bf16[56,512]{1,0:T(8,128)(2,1)S(1)} %get-tuple-element.31.refs_0_), channel_id=1, source_target_pairs={{0,8},{4,12},{8,0},{12,4},{1,9},{5,13},{9,1},{13,5},{2,10},{6,14},... | collective-permute-start | bytes 172040 | tf_op jit(solution)/shard_map/ppermute | solution.py:623
  12.7 12.2 %collective-permute-start.8 = (bf16[1,64,512]{2,1,0:T(8,128)(2,1)S(1)}, bf16[1,64,512]{2,1,0:T(8,128)(2,1)S(1)}, u32[]{:S(2)}, u32[]{:S(2)}) collective-permute-start(bf16[1,64,512]{2,1,0:T(8,128)(2,1)S(1)} %copy-done), channel_id=1, source_target_pairs={{0,4},{4,0},{8,12},{12,8},{1,5},{5,1},{9,13},{13,9},{2,6},{6,2},{1... | collective-permute-start | bytes 196616 | tf_op jit(solution)/shard_map/ppermute | solution.py:623
  14.2 10.6 %collective-permute-start.7 = (bf16[1,64,512]{2,1,0:T(8,128)(2,1)S(1)}, bf16[1,64,512]{2,1,0:T(8,128)(2,1)S(1)}, u32[]{:S(2)}, u32[]{:S(2)}) collective-permute-start(bf16[1,64,512]{2,1,0:T(8,128)(2,1)S(1)} %copy-done), channel_id=1, source_target_pairs={{0,12},{4,8},{8,4},{12,0},{1,13},{5,9},{9,5},{13,1},{2,14},{6,10},... | collective-permute-start | bytes 196616 | tf_op jit(solution)/shard_map/ppermute | solution.py:623
  16.6 8.2 %collective-permute-start.6 = (bf16[1,64,512]{2,1,0:T(8,128)(2,1)S(1)}, bf16[1,64,512]{2,1,0:T(8,128)(2,1)S(1)}, u32[]{:S(2)}, u32[]{:S(2)}) collective-permute-start(bf16[1,64,512]{2,1,0:T(8,128)(2,1)S(1)} %copy-done), channel_id=1, source_target_pairs={{0,8},{4,12},{8,0},{12,4},{1,9},{5,13},{9,1},{13,5},{2,10},{6,14},... | collective-permute-start | bytes 196616 | tf_op jit(solution)/shard_map/ppermute | solution.py:623
  26.6 11.3 %copy-start.1 = (s32[1,3,16]{2,0,1:T(1,128)S(1)}, s32[1,3,16]{2,0,1:T(1,128)}, u32[]{:S(2)}) copy-start(s32[1,3,16]{2,0,1:T(1,128)} %param.14) | copy-start | bytes 580
  27.9 1.4 %collective-permute-start.9 = (bf16[64,1024]{1,0:T(8,128)(2,1)S(1)}, bf16[64,1024]{1,0:T(8,128)(2,1)S(1)}, u32[]{:S(2)}, u32[]{:S(2)}) collective-permute-start(bf16[64,1024]{1,0:T(8,128)(2,1)S(1)} %get-tuple-element.56), channel_id=1, source_target_pairs={{0,1},{1,0},{2,3},{3,2},{4,5},{5,4},{6,7},{7,6},{8,9},{9,8},{10,11... | collective-permute-start | bytes 393224 | tf_op jit(solution)/shard_map/ppermute | solution.py:623
  28.0 2.9 %collective-permute-start.12 = (bf16[64,1024]{1,0:T(8,128)(2,1)S(1)}, bf16[64,1024]{1,0:T(8,128)(2,1)S(1)}, u32[]{:S(2)}, u32[]{:S(2)}) collective-permute-start(bf16[64,1024]{1,0:T(8,128)(2,1)S(1)} %get-tuple-element.58), channel_id=1, source_target_pairs={{0,1},{1,0},{2,3},{3,2},{4,5},{5,4},{6,7},{7,6},{8,9},{9,8},{10,11... | collective-permute-start | bytes 393224 | tf_op jit(solution)/shard_map/ppermute | solution.py:623
  29.4 6.4 %collective-permute-start.10 = (bf16[64,1024]{1,0:T(8,128)(2,1)S(1)}, bf16[64,1024]{1,0:T(8,128)(2,1)S(1)}, u32[]{:S(2)}, u32[]{:S(2)}) collective-permute-start(bf16[64,1024]{1,0:T(8,128)(2,1)S(1)} %add_convert_fusion.3), channel_id=1, source_target_pairs={{0,2},{1,3},{2,0},{3,1},{4,6},{5,7},{6,4},{7,5},{8,10},{9,11},{10,... | collective-permute-start | bytes 393224 | tf_op jit(solution)/shard_map/ppermute | solution.py:623
  31.0 6.8 %collective-permute-start.13 = (bf16[64,1024]{1,0:T(8,128)(2,1)S(1)}, bf16[64,1024]{1,0:T(8,128)(2,1)S(1)}, u32[]{:S(2)}, u32[]{:S(2)}) collective-permute-start(bf16[64,1024]{1,0:T(8,128)(2,1)S(1)} %add_convert_fusion.1), channel_id=1, source_target_pairs={{0,2},{1,3},{2,0},{3,1},{4,6},{5,7},{6,4},{7,5},{8,10},{9,11},{10,... | collective-permute-start | bytes 393224 | tf_op jit(solution)/shard_map/ppermute | solution.py:623
  35.8 3.3 %collective-permute-start.11 = (bf16[64,1024]{1,0:T(8,128)(2,1)S(1)}, bf16[64,1024]{1,0:T(8,128)(2,1)S(1)}, u32[]{:S(2)}, u32[]{:S(2)}) collective-permute-start(bf16[64,1024]{1,0:T(8,128)(2,1)S(1)} %add_convert_fusion.2.one_ref), channel_id=1, source_target_pairs={{0,1},{1,0},{2,3},{3,2},{4,5},{5,4},{6,7},{7,6},{8,9},{9,8},{10,11... | collective-permute-start | bytes 393224 | tf_op jit(solution)/shard_map/ppermute | solution.py:623
  37.8 1.4 %collective-permute-start.14 = (bf16[64,1024]{1,0:T(8,128)(2,1)S(1)}, bf16[64,1024]{1,0:T(8,128)(2,1)S(1)}, u32[]{:S(2)}, u32[]{:S(2)}) collective-permute-start(bf16[64,1024]{1,0:T(8,128)(2,1)S(1)} %add_convert_fusion.two_ref), channel_id=1, source_target_pairs={{0,1},{1,0},{2,3},{3,2},{4,5},{5,4},{6,7},{7,6},{8,9},{9,8},{10,11... | collective-permute-start | bytes 393224 | tf_op jit(solution)/shard_map/ppermute | solution.py:623

commit v14 on v12

--- a/solution.py
+++ b/solution.py
@@ -603,8 +603,12 @@
 VMEM = pl.BlockSpec(memory_space=pltpu.VMEM)
 
 
-def call(kernel, operands, outputs, scratch, flops, fetched=0, megabytes=40):
+def call(kernel, operands, outputs, scratch, flops, fetched=0):
     hbm = pl.BlockSpec(memory_space=pltpu.HBM)
+    operands = [
+        pltpu.with_memory_space_constraint(operand, pltpu.HBM) if n < fetched else operand
+        for n, operand in enumerate(operands)
+    ]
     return pl.pallas_call(
         kernel,
         out_shape=[jax.ShapeDtypeStruct(shape, kind) for shape, kind in outputs],
@@ -612,7 +616,7 @@
         out_specs=[VMEM] * len(outputs),
         scratch_shapes=[pltpu.VMEM(shape, kind) for shape, kind in scratch]
         + ([pltpu.SemaphoreType.DMA((fetched,))] if fetched else []),
-        compiler_params=pltpu.CompilerParams(vmem_limit_bytes=megabytes << 20),
+        compiler_params=pltpu.CompilerParams(vmem_limit_bytes=40 << 20),
         cost_estimate=pl.CostEstimate(flops=flops, bytes_accessed=4 << 20, transcendentals=0),
     )(*operands)
 
@@ -671,7 +675,6 @@
         [((INDEX_ROWS, latent), F32)] + [(source.shape, source.dtype) for source in sources],
         10**7,
         fetched=len(sources),
-        megabytes=56,
     )
     steps = (0, *range(2, regions), 1)
     latents = [mesh_latent] + [swap(mesh_latent, "space", step) for step in steps[1:]]
@@ -688,7 +691,10 @@
     packs = [listed_rows, mesh_latent]
     for step, latent_block in zip(steps[1:], latents[1:]):
         packs += [swap(listed_rows, "space", step), latent_block]
-    cotangents = [cotangent] + [swap(cotangent, "space", step) for step in steps[1:]]
+    near = swap(mesh_cotangent, "space", 1)
+    cotangents = [mesh_cotangent] + [
+        near if step == 1 else swap(cotangent, "space", step) for step in steps[1:]
+    ]
     rows = regions * mesh_count
     slots = regions * mesh_cap
     (

time: 38.6 us -> 39.1 us (1.013)
  starting transfers between devices: 17.6 us -> 19.2 us
  local copies, waits for them, and re-layouts: 1.6 us -> 0.02 us
  Pallas kernels: 11.7 us -> 12.5 us
    unnamed x10 -> x6, local copies, waits for them, and re-layouts: 1.6 us -> 0.02 us
    ppermute x15, starting transfers between devices: 17.6 us -> 19.2 us  [swap(): lax.ppermute(block, axis, [(i, i ^ bits) for i in range(lax.axis_size(axi...]
    pallas_call x7, Pallas kernels: 11.7 us -> 12.5 us  [call(): pl.pallas_call(kernel, out_shape=[jax.ShapeDtypeStruct(shape, kind) for s...]
  transfers between devices with their start and end apart: 15 -> 15, of which waited for: 4 -> 4; matrix products, arithmetic and copies ran while one was open for 0% -> 0% of each run, Pallas kernels for 24% -> 25%
where the time goes in v14:
time: 39.1 us; the launch traced here: 38.9 us
  starting transfers between devices  19.2 us (49%)
  Pallas kernels  12.5 us (32%)
  waiting for transfers between devices  6.3 us (16%)
  between operations  0.76 us (2%)
    ppermute x15, starting transfers between devices, swap(): lax.ppermute(block, axis, [(i, i ^ bits) for i in range(lax.axis_size(axi...  19.2 us
    pallas_call x7, Pallas kernels, call(): pl.pallas_call(kernel, out_shape=[jax.ShapeDtypeStruct(shape, kind) for s...  12.5 us
    ppermute x15, waiting for transfers between devices, swap(): lax.ppermute(block, axis, [(i, i ^ bits) for i in range(lax.axis_size(axi...  6.3 us
  transfers between devices with their start and end apart: 15, of which 4 were waited for; matrix products, arithmetic and copies ran while one was open for 0% of the time, Pallas kernels for 25%

profile of v14, /device:TPU:0, one launch (start us, length us, event | category | flops | bytes accessed | tf_op | source)
XLA Modules:
  0.0 38.9 jit_solution(12340763627975726450)
XLA Ops:
  0.6 0.0 copy-start
  0.7 4.1 %collective-permute-start.1 = (bf16[1,64,512]{2,1,0:T(8,128)(2,1)}, bf16[1,64,512]{2,1,0:T(8,128)(2,1)S(1)}, u32[]{:S(2)}, u32[]{:S(2)}) collective-permute-start(bf16[1,64,512]{2,1,0:T(8,128)(2,1)} %refs_1_.1), channel_id=1, source_target_pairs={{0,8},{4,12},{8,0},{12,4},{1,9},{5,13},{9,1},{13,5},{2,10},{6,14},... | collective-permute-start | bytes 196616 | tf_op jit(solution)/shard_map/ppermute | solution.py:625
  4.8 1.3 %collective-permute-start.2 = (bf16[1,64,512]{2,1,0:T(8,128)(2,1)}, bf16[1,64,512]{2,1,0:T(8,128)(2,1)S(1)}, u32[]{:S(2)}, u32[]{:S(2)}) collective-permute-start(bf16[1,64,512]{2,1,0:T(8,128)(2,1)} %refs_1_.1), channel_id=1, source_target_pairs={{0,12},{4,8},{8,4},{12,0},{1,13},{5,9},{9,5},{13,1},{2,14},{6,10},... | collective-permute-start | bytes 196616 | tf_op jit(solution)/shard_map/ppermute | solution.py:625
  6.1 0.2 collective-permute-start.3
  6.3 1.2 %shard_map.121.refs_0_ = bf16[56,512]{1,0:T(8,128)(2,1)S(1)} custom-call(bf16[1,128,512]{2,1,0:T(8,128)(2,1)} %refs_0_.2, s32[3,1,16]{2,1,0:T(1,128)} %bitcast.5, s32[1,256]{1,0:T(1,128)} %bitcast.7, s32[1,256]{1,0:T(1,128)} %bitcast.8, s32[1,4,8]{2,1,0:T(4,128)} %refs_4_.1, s32[1,256]{1,0:T(1,128)} %bitcast.9, s32[1,256]{1,0:T(1,128)} %bitcast.10), custom_call_target="tpu_custom_call" | custom-call | flops 10000000 | bytes 4194304 | tf_op jit(solution)/shard_map/pallas_call | solution.py:612
  7.5 2.9 %collective-permute-start = (bf16[56,512]{1,0:T(8,128)(2,1)S(1)}, bf16[56,512]{1,0:T(8,128)(2,1)S(1)}, u32[]{:S(2)}, u32[]{:S(2)}) collective-permute-start(bf16[56,512]{1,0:T(8,128)(2,1)S(1)} %shard_map.121.refs_0_), channel_id=1, source_target_pairs={{0,8},{4,12},{8,0},{12,4},{1,9},{5,13},{9,1},{13,5},{2,10},{6,14},... | collective-permute-start | bytes 172040 | tf_op jit(solution)/shard_map/ppermute | solution.py:625
  10.4 1.3 %collective-permute-start.4 = (bf16[56,512]{1,0:T(8,128)(2,1)S(1)}, bf16[56,512]{1,0:T(8,128)(2,1)S(1)}, u32[]{:S(2)}, u32[]{:S(2)}) collective-permute-start(bf16[56,512]{1,0:T(8,128)(2,1)S(1)} %shard_map.121.refs_0_), channel_id=1, source_target_pairs={{0,12},{4,8},{8,4},{12,0},{1,13},{5,9},{9,5},{13,1},{2,14},{6,10},... | collective-permute-start | bytes 172040 | tf_op jit(solution)/shard_map/ppermute | solution.py:625
  11.8 0.0 collective-permute-done.1.refs_3_
  11.8 0.0 collective-permute-start.5
  11.8 0.0 collective-permute-done.2.refs_5_
  11.8 2.5 %collective-permute-start.8 = (bf16[1,64,512]{2,1,0:T(8,128)(2,1)}, bf16[1,64,512]{2,1,0:T(8,128)(2,1)S(1)}, u32[]{:S(2)}, u32[]{:S(2)}) collective-permute-start(bf16[1,64,512]{2,1,0:T(8,128)(2,1)} %refs_0_.3), channel_id=1, source_target_pairs={{0,4},{4,0},{8,12},{12,8},{1,5},{5,1},{9,13},{13,9},{2,6},{6,2},{1... | collective-permute-start | bytes 196616 | tf_op jit(solution)/shard_map/ppermute | solution.py:625
  14.2 2.1 %shard_map.122 = (bf16[512,2048]{1,0:T(8,128)(2,1)S(1)}, bf16[512,1536]{1,0:T(8,128)(2,1)S(1)}) custom-call(bf16[512,2048]{1,0:T(8,128)(2,1)} %source_ref), custom_call_target="tpu_custom_call" | custom-call | flops 100000000 | bytes 4194304 | tf_op jit(solution)/shard_map/pallas_call | solution.py:612
  16.3 2.0 %collective-permute-start.6 = (bf16[1,64,512]{2,1,0:T(8,128)(2,1)S(1)}, bf16[1,64,512]{2,1,0:T(8,128)(2,1)S(1)}, u32[]{:S(2)}, u32[]{:S(2)}) collective-permute-start(bf16[1,64,512]{2,1,0:T(8,128)(2,1)S(1)} %copy-done), channel_id=1, source_target_pairs={{0,8},{4,12},{8,0},{12,4},{1,9},{5,13},{9,1},{13,5},{2,10},{6,14},... | collective-permute-start | bytes 196616 | tf_op jit(solution)/shard_map/ppermute | solution.py:625
  18.4 0.0 collective-permute-done.refs_2_
  18.4 1.5 %collective-permute-start.7 = (bf16[1,64,512]{2,1,0:T(8,128)(2,1)S(1)}, bf16[1,64,512]{2,1,0:T(8,128)(2,1)S(1)}, u32[]{:S(2)}, u32[]{:S(2)}) collective-permute-start(bf16[1,64,512]{2,1,0:T(8,128)(2,1)S(1)} %copy-done), channel_id=1, source_target_pairs={{0,12},{4,8},{8,4},{12,0},{1,13},{5,9},{9,5},{13,1},{2,14},{6,10},... | collective-permute-start | bytes 196616 | tf_op jit(solution)/shard_map/ppermute | solution.py:625
  19.9 0.0 collective-permute-done.4.refs_4_
  19.9 4.2 %shard_map.123 = (bf16[1,64,512]{2,1,0:T(8,128)(2,1)}, bf16[192,512]{1,0:T(8,128)(2,1)S(1)}, bf16[256,512]{1,0:T(8,128)(2,1)S(1)}, bf16[256,512]{1,0:T(8,128)(2,...) custom-call(bf16[56,512]{1,0:T(8,128)(2,1)S(1)} %shard_map.121.refs_, ...), custom_call_target="tpu_custom_call" | custom-call | flops 2000000000 | bytes 4194304 | tf_op jit(solution)/shard_map/pallas_call | solution.py:612
  24.1 0.4 %collective-permute-done.7.refs_2_ = bf16[1,64,512]{2,1,0:T(8,128)(2,1)S(1)} collective-permute-done((bf16[1,64,512]{2,1,0:T(8,128)(2,1)S(1)}, bf16[1,64,512]{2,1,0:T(8,128)(2,1)S(1)}, u32[]{:S(2)}, u32[]{:S(2)}) %collective-permute-start.7) | collective-permute-done | bytes 65568 | tf_op jit(solution)/shard_map/ppermute | solution.py:625
  24.5 1.6 %shard_map.124 = (f32[256,512]{1,0:T(8,128)S(1)}, bf16[64,1024]{1,0:T(8,128)(2,1)S(1)}, bf16[64,1024]{1,0:T(8,128)(2,1)S(1)}) custom-call(bf16[1,64,512]{2,1,0:T(8,128)(2,1)S(1)} %copy-done, bf16[1,64,512]{2,1,0:T(8,128)(2,1)S(1)} %collective-permute-done.6.refs_1_, bf16[1,64,512]{2,1,0:T(8,128)(2,1)S(1)} %collective-permute-done.7.refs_2_, ...), custom_call_target="tpu_custom_call" | custom-call | flops 1000000000 | bytes 4194304 | tf_op jit(solution)/shard_map/pallas_call | solution.py:612
  26.1 0.1 collective-permute-start.12
  26.2 0.0 copy-start.1
  26.2 1.3 %shard_map.125 = (bf16[48,512]{1,0:T(8,128)(2,1)S(1)}, bf16[64,1024]{1,0:T(8,128)(2,1)S(1)}, bf16[64,1024]{1,0:T(8,128)(2,1)S(1)}) custom-call(bf16[192,512]{1,0:T(8,128)(2,1)S(1)} %get-tuple-element.41.grid_ref, bf16[256,512]{1,0:T(8,128)(2,1)S(1)} %get-tuple-element.42.mesh_ref, bf16[448,256]{1,0:T(8,128)(2,1)S(1)} %get-tuple-element.43.hot_ref, ...), custom_call_target="tpu_custom_call" | custom-call | flops 1000000000 | bytes 4194304 | tf_op jit(solution)/shard_map/pallas_call | solution.py:612
  27.5 0.5 %collective-permute-start.9 = (bf16[64,1024]{1,0:T(8,128)(2,1)S(1)}, bf16[64,1024]{1,0:T(8,128)(2,1)S(1)}, u32[]{:S(2)}, u32[]{:S(2)}) collective-permute-start(bf16[64,1024]{1,0:T(8,128)(2,1)S(1)} %get-tuple-element.60), channel_id=1, source_target_pairs={{0,1},{1,0},{2,3},{3,2},{4,5},{5,4},{6,7},{7,6},{8,9},{9,8},{10,11... | collective-permute-start | bytes 393224 | tf_op jit(solution)/shard_map/ppermute | solution.py:625
  28.1 1.6 %collective-permute-start.13 = (bf16[64,1024]{1,0:T(8,128)(2,1)S(1)}, bf16[64,1024]{1,0:T(8,128)(2,1)S(1)}, u32[]{:S(2)}, u32[]{:S(2)}) collective-permute-start(bf16[64,1024]{1,0:T(8,128)(2,1)S(1)} %add_convert_fusion.1), channel_id=1, source_target_pairs={{0,2},{1,3},{2,0},{3,1},{4,6},{5,7},{6,4},{7,5},{8,10},{9,11},{10,... | collective-permute-start | bytes 393224 | tf_op jit(solution)/shard_map/ppermute | solution.py:625
  29.7 1.0 %collective-permute-start.10 = (bf16[64,1024]{1,0:T(8,128)(2,1)S(1)}, bf16[64,1024]{1,0:T(8,128)(2,1)S(1)}, u32[]{:S(2)}, u32[]{:S(2)}) collective-permute-start(bf16[64,1024]{1,0:T(8,128)(2,1)S(1)} %add_convert_fusion.3), channel_id=1, source_target_pairs={{0,2},{1,3},{2,0},{3,1},{4,6},{5,7},{6,4},{7,5},{8,10},{9,11},{10,... | collective-permute-start | bytes 393224 | tf_op jit(solution)/shard_map/ppermute | solution.py:625
  30.7 3.9 %collective-permute-done.13 = bf16[64,1024]{1,0:T(8,128)(2,1)S(1)} collective-permute-done((bf16[64,1024]{1,0:T(8,128)(2,1)S(1)}, bf16[64,1024]{1,0:T(8,128)(2,1)S(1)}, u32[]{:S(2)}, u32[]{:S(2)}) %collective-permute-start.13) | collective-permute-done | bytes 131104 | tf_op jit(solution)/shard_map/ppermute | solution.py:625
  34.6 0.1 collective-permute-start.14
  34.6 1.8 %collective-permute-done.10 = bf16[64,1024]{1,0:T(8,128)(2,1)S(1)} collective-permute-done((bf16[64,1024]{1,0:T(8,128)(2,1)S(1)}, bf16[64,1024]{1,0:T(8,128)(2,1)S(1)}, u32[]{:S(2)}, u32[]{:S(2)}) %collective-permute-start.10) | collective-permute-done | bytes 131104 | tf_op jit(solution)/shard_map/ppermute | solution.py:625
  36.4 0.1 collective-permute-start.11
  36.5 1.1 %shard_map.126 = bf16[1,128,512]{2,1,0:T(8,128)(2,1)} custom-call(bf16[512,1536]{1,0:T(8,128)(2,1)S(1)} %get-tuple-element.40.refs_4_.turned_ref, s32[3,1,16]{2,1,0:T(1,128)S(1)} %bitcast.6, bf16[48,512]{1,0:T(8,128)(2,1)S(1)} %get-tuple-element.58.own_slot_ref), custom_call_target="tpu_custom_call" | custom-call | flops 100000000 | bytes 4194304 | tf_op jit(solution)/shard_map/pallas_call | solution.py:612
  37.6 0.2 collective-permute-done.11.other_one_ref
  37.9 1.0 %shard_map.127 = f32[128,2048]{1,0:T(8,128)} custom-call(bf16[64,1024]{1,0:T(8,128)(2,1)S(1)} %add_convert_fusion.2.one_ref, bf16[64,1024]{1,0:T(8,128)(2,1)S(1)} %collective-permute-done.11.other_one_ref, bf16[64,1024]{1,0:T(8,128)(2,1)S(1)} %add_convert_fusion.two_ref, bf16[64,1024]{1,0:T(8,128)(2,1)S(1)} %collective-permute-done.14.other_two_ref), custom_call_target="tpu_custom_call" | custom-call | flops 1000000 | bytes 4194304 | tf_op jit(solution)/shard_map/pallas_call | solution.py:612
  (15 shorter events, 0.2 us)
Async XLA Ops:
  0.6 19.3 %copy-start.2 = (bf16[1,64,512]{2,1,0:T(8,128)(2,1)S(1)}, bf16[1,64,512]{2,1,0:T(8,128)(2,1)}, u32[]{:S(2)}) copy-start(bf16[1,64,512]{2,1,0:T(8,128)(2,1)} %refs_1_.1) | copy-start | bytes 196612
  0.6 15.7 %copy-start = (bf16[1,64,512]{2,1,0:T(8,128)(2,1)S(1)}, bf16[1,64,512]{2,1,0:T(8,128)(2,1)}, u32[]{:S(2)}) copy-start(bf16[1,64,512]{2,1,0:T(8,128)(2,1)} %refs_0_.3) | copy-start | bytes 196612
  0.7 11.1 %collective-permute-start.1 = (bf16[1,64,512]{2,1,0:T(8,128)(2,1)}, bf16[1,64,512]{2,1,0:T(8,128)(2,1)S(1)}, u32[]{:S(2)}, u32[]{:S(2)}) collective-permute-start(bf16[1,64,512]{2,1,0:T(8,128)(2,1)} %refs_1_.1), channel_id=1, source_target_pairs={{0,8},{4,12},{8,0},{12,4},{1,9},{5,13},{9,1},{13,5},{2,10},{6,14},... | collective-permute-start | bytes 196616 | tf_op jit(solution)/shard_map/ppermute | solution.py:625
  4.8 7.0 %collective-permute-start.2 = (bf16[1,64,512]{2,1,0:T(8,128)(2,1)}, bf16[1,64,512]{2,1,0:T(8,128)(2,1)S(1)}, u32[]{:S(2)}, u32[]{:S(2)}) collective-permute-start(bf16[1,64,512]{2,1,0:T(8,128)(2,1)} %refs_1_.1), channel_id=1, source_target_pairs={{0,12},{4,8},{8,4},{12,0},{1,13},{5,9},{9,5},{13,1},{2,14},{6,10},... | collective-permute-start | bytes 196616 | tf_op jit(solution)/shard_map/ppermute | solution.py:625
  6.1 8.1 %collective-permute-start.3 = (bf16[1,64,512]{2,1,0:T(8,128)(2,1)}, bf16[1,64,512]{2,1,0:T(8,128)(2,1)S(1)}, u32[]{:S(2)}, u32[]{:S(2)}) collective-permute-start(bf16[1,64,512]{2,1,0:T(8,128)(2,1)} %refs_1_.1), channel_id=1, source_target_pairs={{0,4},{4,0},{8,12},{12,8},{1,5},{5,1},{9,13},{13,9},{2,6},{6,2},{1... | collective-permute-start | bytes 196616 | tf_op jit(solution)/shard_map/ppermute | solution.py:625
  7.5 10.8 %collective-permute-start = (bf16[56,512]{1,0:T(8,128)(2,1)S(1)}, bf16[56,512]{1,0:T(8,128)(2,1)S(1)}, u32[]{:S(2)}, u32[]{:S(2)}) collective-permute-start(bf16[56,512]{1,0:T(8,128)(2,1)S(1)} %shard_map.121.refs_0_), channel_id=1, source_target_pairs={{0,8},{4,12},{8,0},{12,4},{1,9},{5,13},{9,1},{13,5},{2,10},{6,14},... | collective-permute-start | bytes 172040 | tf_op jit(solution)/shard_map/ppermute | solution.py:625
  10.4 9.5 %collective-permute-start.4 = (bf16[56,512]{1,0:T(8,128)(2,1)S(1)}, bf16[56,512]{1,0:T(8,128)(2,1)S(1)}, u32[]{:S(2)}, u32[]{:S(2)}) collective-permute-start(bf16[56,512]{1,0:T(8,128)(2,1)S(1)} %shard_map.121.refs_0_), channel_id=1, source_target_pairs={{0,12},{4,8},{8,4},{12,0},{1,13},{5,9},{9,5},{13,1},{2,14},{6,10},... | collective-permute-start | bytes 172040 | tf_op jit(solution)/shard_map/ppermute | solution.py:625
  11.8 8.1 %collective-permute-start.5 = (bf16[56,512]{1,0:T(8,128)(2,1)S(1)}, bf16[56,512]{1,0:T(8,128)(2,1)S(1)}, u32[]{:S(2)}, u32[]{:S(2)}) collective-permute-start(bf16[56,512]{1,0:T(8,128)(2,1)S(1)} %shard_map.121.refs_0_), channel_id=1, source_target_pairs={{0,4},{4,0},{8,12},{12,8},{1,5},{5,1},{9,13},{13,9},{2,6},{6,2},{1... | collective-permute-start | bytes 172040 | tf_op jit(solution)/shard_map/ppermute | solution.py:625
  11.8 12.3 %collective-permute-start.8 = (bf16[1,64,512]{2,1,0:T(8,128)(2,1)}, bf16[1,64,512]{2,1,0:T(8,128)(2,1)S(1)}, u32[]{:S(2)}, u32[]{:S(2)}) collective-permute-start(bf16[1,64,512]{2,1,0:T(8,128)(2,1)} %refs_0_.3), channel_id=1, source_target_pairs={{0,4},{4,0},{8,12},{12,8},{1,5},{5,1},{9,13},{13,9},{2,6},{6,2},{1... | collective-permute-start | bytes 196616 | tf_op jit(solution)/shard_map/ppermute | solution.py:625
  16.3 7.8 %collective-permute-start.6 = (bf16[1,64,512]{2,1,0:T(8,128)(2,1)S(1)}, bf16[1,64,512]{2,1,0:T(8,128)(2,1)S(1)}, u32[]{:S(2)}, u32[]{:S(2)}) collective-permute-start(bf16[1,64,512]{2,1,0:T(8,128)(2,1)S(1)} %copy-done), channel_id=1, source_target_pairs={{0,8},{4,12},{8,0},{12,4},{1,9},{5,13},{9,1},{13,5},{2,10},{6,14},... | collective-permute-start | bytes 196616 | tf_op jit(solution)/shard_map/ppermute | solution.py:625
  18.4 6.2 %collective-permute-start.7 = (bf16[1,64,512]{2,1,0:T(8,128)(2,1)S(1)}, bf16[1,64,512]{2,1,0:T(8,128)(2,1)S(1)}, u32[]{:S(2)}, u32[]{:S(2)}) collective-permute-start(bf16[1,64,512]{2,1,0:T(8,128)(2,1)S(1)} %copy-done), channel_id=1, source_target_pairs={{0,12},{4,8},{8,4},{12,0},{1,13},{5,9},{9,5},{13,1},{2,14},{6,10},... | collective-permute-start | bytes 196616 | tf_op jit(solution)/shard_map/ppermute | solution.py:625
  26.1 1.9 %collective-permute-start.12 = (bf16[64,1024]{1,0:T(8,128)(2,1)S(1)}, bf16[64,1024]{1,0:T(8,128)(2,1)S(1)}, u32[]{:S(2)}, u32[]{:S(2)}) collective-permute-start(bf16[64,1024]{1,0:T(8,128)(2,1)S(1)} %get-tuple-element.62), channel_id=1, source_target_pairs={{0,1},{1,0},{2,3},{3,2},{4,5},{5,4},{6,7},{7,6},{8,9},{9,8},{10,11... | collective-permute-start | bytes 393224 | tf_op jit(solution)/shard_map/ppermute | solution.py:625
  26.2 10.3 %copy-start.1 = (s32[1,3,16]{2,0,1:T(1,128)S(1)}, s32[1,3,16]{2,0,1:T(1,128)}, u32[]{:S(2)}) copy-start(s32[1,3,16]{2,0,1:T(1,128)} %param.14) | copy-start | bytes 580
  27.5 2.2 %collective-permute-start.9 = (bf16[64,1024]{1,0:T(8,128)(2,1)S(1)}, bf16[64,1024]{1,0:T(8,128)(2,1)S(1)}, u32[]{:S(2)}, u32[]{:S(2)}) collective-permute-start(bf16[64,1024]{1,0:T(8,128)(2,1)S(1)} %get-tuple-element.60), channel_id=1, source_target_pairs={{0,1},{1,0},{2,3},{3,2},{4,5},{5,4},{6,7},{7,6},{8,9},{9,8},{10,11... | collective-permute-start | bytes 393224 | tf_op jit(solution)/shard_map/ppermute | solution.py:625
  28.1 6.4 %collective-permute-start.13 = (bf16[64,1024]{1,0:T(8,128)(2,1)S(1)}, bf16[64,1024]{1,0:T(8,128)(2,1)S(1)}, u32[]{:S(2)}, u32[]{:S(2)}) collective-permute-start(bf16[64,1024]{1,0:T(8,128)(2,1)S(1)} %add_convert_fusion.1), channel_id=1, source_target_pairs={{0,2},{1,3},{2,0},{3,1},{4,6},{5,7},{6,4},{7,5},{8,10},{9,11},{10,... | collective-permute-start | bytes 393224 | tf_op jit(solution)/shard_map/ppermute | solution.py:625
  29.7 6.7 %collective-permute-start.10 = (bf16[64,1024]{1,0:T(8,128)(2,1)S(1)}, bf16[64,1024]{1,0:T(8,128)(2,1)S(1)}, u32[]{:S(2)}, u32[]{:S(2)}) collective-permute-start(bf16[64,1024]{1,0:T(8,128)(2,1)S(1)} %add_convert_fusion.3), channel_id=1, source_target_pairs={{0,2},{1,3},{2,0},{3,1},{4,6},{5,7},{6,4},{7,5},{8,10},{9,11},{10,... | collective-permute-start | bytes 393224 | tf_op jit(solution)/shard_map/ppermute | solution.py:625
  34.6 3.1 %collective-permute-start.14 = (bf16[64,1024]{1,0:T(8,128)(2,1)S(1)}, bf16[64,1024]{1,0:T(8,128)(2,1)S(1)}, u32[]{:S(2)}, u32[]{:S(2)}) collective-permute-start(bf16[64,1024]{1,0:T(8,128)(2,1)S(1)} %add_convert_fusion.two_ref), channel_id=1, source_target_pairs={{0,1},{1,0},{2,3},{3,2},{4,5},{5,4},{6,7},{7,6},{8,9},{9,8},{10,11... | collective-permute-start | bytes 393224 | tf_op jit(solution)/shard_map/ppermute | solution.py:625
  36.4 1.4 %collective-permute-start.11 = (bf16[64,1024]{1,0:T(8,128)(2,1)S(1)}, bf16[64,1024]{1,0:T(8,128)(2,1)S(1)}, u32[]{:S(2)}, u32[]{:S(2)}) collective-permute-start(bf16[64,1024]{1,0:T(8,128)(2,1)S(1)} %add_convert_fusion.2.one_ref), channel_id=1, source_target_pairs={{0,1},{1,0},{2,3},{3,2},{4,5},{5,4},{6,7},{7,6},{8,9},{9,8},{10,11... | collective-permute-start | bytes 393224 | tf_op jit(solution)/shard_map/ppermute | solution.py:625

commit v15 on v10

--- a/solution.py
+++ b/solution.py
@@ -603,9 +603,7 @@
     return mine, pl.ds(pl.multiple_of((1 - core) * half, half), half)
 
 
-def finish_kernel(
-    one_ref, other_one_ref, two_ref, other_two_ref, weight_grad_ref, *scratch
-):
+def settle_kernel(one_ref, two_ref, other_two_ref, weight_grad_ref, *scratch):
     half, width = one_ref.shape
     mine, other = half_rows(half)
     place(
@@ -613,18 +611,27 @@
             (two_ref, weight_grad_ref.at[mine, width:]),
             (other_two_ref, weight_grad_ref.at[other, width:]),
             (one_ref, weight_grad_ref.at[mine, :width]),
-            (other_one_ref, weight_grad_ref.at[other, :width]),
         ],
-        scratch[:4],
-        scratch[4],
-    )
+        scratch[:3],
+        scratch[3],
+    )
+
+
+def finish_kernel(other_one_ref, settled_ref, weight_grad_ref, stage, semaphores):
+    half, width = other_one_ref.shape
+    _, other = half_rows(half)
+    place([(other_one_ref, weight_grad_ref.at[other, :width])], [stage], semaphores)
 
 
 VMEM = pl.BlockSpec(memory_space=pltpu.VMEM)
 
 
-def call(kernel, operands, outputs, scratch, flops, fetched=0, megabytes=40):
+def call(kernel, operands, outputs, scratch, flops, fetched=0):
     hbm = pl.BlockSpec(memory_space=pltpu.HBM)
+    operands = [
+        pltpu.with_memory_space_constraint(operand, pltpu.HBM) if n < fetched else operand
+        for n, operand in enumerate(operands)
+    ]
     return pl.pallas_call(
         kernel,
         out_shape=[jax.ShapeDtypeStruct(shape, kind) for shape, kind in outputs],
@@ -632,7 +639,7 @@
         out_specs=[VMEM] * len(outputs),
         scratch_shapes=[pltpu.VMEM(shape, kind) for shape, kind in scratch]
         + ([pltpu.SemaphoreType.DMA((fetched,))] if fetched else []),
-        compiler_params=pltpu.CompilerParams(vmem_limit_bytes=megabytes << 20),
+        compiler_params=pltpu.CompilerParams(vmem_limit_bytes=40 << 20),
         cost_estimate=pl.CostEstimate(flops=flops, bytes_accessed=4 << 20, transcendentals=0),
     )(*operands)
 
@@ -691,11 +698,11 @@
         [((INDEX_ROWS, latent), F32)] + [(source.shape, source.dtype) for source in sources],
         10**7,
         fetched=len(sources),
-        megabytes=56,
     )[0]
     packed, cotangent, weights = lax.optimization_barrier((packed, mesh_cotangent, weights))
     steps = (0, *range(2, regions), 1)
     packs = [packed] + [swap(packed, "space", step) for step in steps[1:]]
+    near = swap(cotangent, "space", 1)
     weights, turned = call(
         weights_kernel,
         (weights,),
@@ -705,7 +712,7 @@
         fetched=1,
     )
     packs[1], cotangent = lax.optimization_barrier((packs[1], cotangent))
-    cotangents = [cotangent] + [swap(cotangent, "space", step) for step in steps[1:]]
+    cotangents = [cotangent] + [swap(cotangent, "space", step) for step in steps[1:-1]] + [near]
     rows = regions * mesh_count
     slots = regions * mesh_cap
     (
@@ -810,15 +817,27 @@
     )[0]
     two = summed_over_chips(half_two)
     one, grid_grad = lax.optimization_barrier((summed_over_chips(half_one), grid_grad))
+    hbm = pl.BlockSpec(memory_space=pltpu.HBM)
+    stage = pltpu.VMEM((half, 2 * latent), F32)
+    weight_shape = pltpu.HBM((columns, 4 * latent), F32)
+    limit = pltpu.CompilerParams(vmem_limit_bytes=40 << 20)
+    settled = pl.pallas_call(
+        settle_kernel,
+        out_shape=weight_shape,
+        in_specs=[VMEM] * 3,
+        out_specs=hbm,
+        scratch_shapes=[stage] * 3 + [pltpu.SemaphoreType.DMA((3,))],
+        compiler_params=limit,
+    )(one, two, swap(two, "rep", 1))
     weight_grad = pl.pallas_call(
         finish_kernel,
-        out_shape=jax.ShapeDtypeStruct((columns, 4 * latent), F32),
-        in_specs=[VMEM] * 4,
-        out_specs=pl.BlockSpec(memory_space=pltpu.HBM),
-        scratch_shapes=[pltpu.VMEM((half, 2 * latent), F32)] * 4
-        + [pltpu.SemaphoreType.DMA((4,))],
-        compiler_params=pltpu.CompilerParams(vmem_limit_bytes=40 << 20),
-    )(one, swap(one, "rep", 1), two, swap(two, "rep", 1))
+        out_shape=weight_shape,
+        in_specs=[VMEM, hbm],
+        out_specs=hbm,
+        scratch_shapes=[stage, pltpu.SemaphoreType.DMA((1,))],
+        input_output_aliases={1: 0},
+        compiler_params=limit,
+    )(swap(one, "rep", 1), settled)
     return (mesh_out, grid_grad, weight_grad)
 
 

time: 39 us -> 37.5 us (0.962)
  waiting for transfers between devices: 12.1 us -> 9.69 us
  local copies, waits for them, and re-layouts: 1.6 us -> 0.01 us
  Pallas kernels: 11.7 us -> 13.1 us
  starting transfers between devices: 12.5 us -> 13.6 us
    ppermute x12, waiting for transfers between devices: 12.1 us -> 9.69 us  [swap(): lax.ppermute(block, axis, [(i, i ^ bits) for i in range(lax.axis_size(axi...]
    unnamed x8 -> x4, local copies, waits for them, and re-layouts: 1.6 us -> 0.01 us
    ppermute x12, starting transfers between devices: 12.5 us -> 13.6 us  [swap(): lax.ppermute(block, axis, [(i, i ^ bits) for i in range(lax.axis_size(axi...]
    pallas_call x6, Pallas kernels: 10.7 us -> 11.5 us  [call(): pl.pallas_call(kernel, out_shape=[jax.ShapeDtypeStruct(shape, kind) for s...]
    pallas_call x1 -> x2, Pallas kernels: 1.01 us -> 1.65 us  [the longest x1 0.92 us: whole_sample_body(): pl.pallas_call(settle_kernel, out_shape=weight_shape, in_specs=[VMEM] * 3...]
  transfers between devices with their start and end apart: 12 -> 12, of which waited for: 6 -> 5; matrix products, arithmetic and copies ran while one was open for 0% -> 0% of each run, Pallas kernels for 19% -> 26%
where the time goes in v15:
time: 37.5 us; the launch traced here: 37.3 us
  starting transfers between devices  13.6 us (36%)
  Pallas kernels  13.1 us (35%)
  waiting for transfers between devices  9.69 us (26%)
  between operations  0.74 us (2%)
    ppermute x12, starting transfers between devices, swap(): lax.ppermute(block, axis, [(i, i ^ bits) for i in range(lax.axis_size(axi...  13.6 us
    pallas_call x6, Pallas kernels, call(): pl.pallas_call(kernel, out_shape=[jax.ShapeDtypeStruct(shape, kind) for s...  11.5 us
    ppermute x12, waiting for transfers between devices, swap(): lax.ppermute(block, axis, [(i, i ^ bits) for i in range(lax.axis_size(axi...  9.69 us
    pallas_call x1, Pallas kernels, whole_sample_body(): pl.pallas_call(settle_kernel, out_shape=weight_shape, in_specs=[VMEM] * 3...  0.92 us
  transfers between devices with their start and end apart: 12, of which 5 were waited for; matrix products, arithmetic and copies ran while one was open for 0% of the time, Pallas kernels for 26%

profile of v15, /device:TPU:0, one launch (start us, length us, event | category | flops | bytes accessed | tf_op | source)
XLA Modules:
  0.0 37.3 jit_solution(5064051591577493814)
XLA Ops:
  0.6 0.0 copy-start
  0.6 1.2 %shard_map.121.refs_0_ = bf16[120,512]{1,0:T(8,128)(2,1)S(1)} custom-call(bf16[1,128,512]{2,1,0:T(8,128)(2,1)} %refs_0_.1, bf16[1,64,512]{2,1,0:T(8,128)(2,1)} %refs_1_.1, s32[3,1,16]{2,1,0:T(1,128)} %bitcast.5, s32[1,256]{1,0:T(1,128)} %bitcast.7, s32[1,256]{1,0:T(1,128)} %bitcast.8, s32[1,4,8]{2,1,0:T(4,128)} %refs_5_.1, s32[1,256]{1,0:T(1,128)} %bitcast.9, ...), custom_call_target="tpu_custom_call" | custom-call | flops 10000000 | bytes 4194304 | tf_op jit(solution)/shard_map/pallas_call | solution.py:635
  1.9 4.1 %collective-permute-start = (bf16[120,512]{1,0:T(8,128)(2,1)S(1)}, bf16[120,512]{1,0:T(8,128)(2,1)S(1)}, u32[]{:S(2)}, u32[]{:S(2)}) collective-permute-start(bf16[120,512]{1,0:T(8,128)(2,1)S(1)} %shard_map.121.refs_0_), channel_id=1, source_target_pairs={{0,8},{4,12},{8,0},{12,4},{1,9},{5,13},{9,1},{13,5},{2,10},{6,14},... | collective-permute-start | bytes 368648 | tf_op jit(solution)/shard_map/ppermute | solution.py:648
  6.0 1.3 %collective-permute-start.1 = (bf16[120,512]{1,0:T(8,128)(2,1)S(1)}, bf16[120,512]{1,0:T(8,128)(2,1)S(1)}, u32[]{:S(2)}, u32[]{:S(2)}) collective-permute-start(bf16[120,512]{1,0:T(8,128)(2,1)S(1)} %shard_map.121.refs_0_), channel_id=1, source_target_pairs={{0,12},{4,8},{8,4},{12,0},{1,13},{5,9},{9,5},{13,1},{2,14},{6,10},... | collective-permute-start | bytes 368648 | tf_op jit(solution)/shard_map/ppermute | solution.py:648
  7.3 0.2 collective-permute-start.2
  7.6 1.8 %collective-permute-start.5 = (bf16[1,64,512]{2,1,0:T(8,128)(2,1)}, bf16[1,64,512]{2,1,0:T(8,128)(2,1)S(1)}, u32[]{:S(2)}, u32[]{:S(2)}) collective-permute-start(bf16[1,64,512]{2,1,0:T(8,128)(2,1)} %refs_0_.2), channel_id=1, source_target_pairs={{0,4},{4,0},{8,12},{12,8},{1,5},{5,1},{9,13},{13,9},{2,6},{6,2},{1... | collective-permute-start | bytes 196616 | tf_op jit(solution)/shard_map/ppermute | solution.py:648
  9.4 2.1 %shard_map.122 = (bf16[512,2048]{1,0:T(8,128)(2,1)S(1)}, bf16[512,1536]{1,0:T(8,128)(2,1)S(1)}) custom-call(bf16[512,2048]{1,0:T(8,128)(2,1)} %source_ref), custom_call_target="tpu_custom_call" | custom-call | flops 100000000 | bytes 4194304 | tf_op jit(solution)/shard_map/pallas_call | solution.py:635
  11.4 4.0 %collective-permute-done.refs_1_ = bf16[120,512]{1,0:T(8,128)(2,1)S(1)} collective-permute-done((bf16[120,512]{1,0:T(8,128)(2,1)S(1)}, bf16[120,512]{1,0:T(8,128)(2,1)S(1)}, u32[]{:S(2)}, u32[]{:S(2)}) %collective-permute-start) | collective-permute-done | bytes 122912 | tf_op jit(solution)/shard_map/ppermute | solution.py:648
  15.5 0.0 collective-permute-start.3
  15.5 2.8 %collective-permute-start.4 = (bf16[1,64,512]{2,1,0:T(8,128)(2,1)S(1)}, bf16[1,64,512]{2,1,0:T(8,128)(2,1)S(1)}, u32[]{:S(2)}, u32[]{:S(2)}) collective-permute-start(bf16[1,64,512]{2,1,0:T(8,128)(2,1)S(1)} %copy-done), channel_id=1, source_target_pairs={{0,12},{4,8},{8,4},{12,0},{1,13},{5,9},{9,5},{13,1},{2,14},{6,10},... | collective-permute-start | bytes 196616 | tf_op jit(solution)/shard_map/ppermute | solution.py:648
  18.3 0.0 collective-permute-done.1.refs_2_
  18.3 4.2 %shard_map.123 = (bf16[1,64,512]{2,1,0:T(8,128)(2,1)}, bf16[192,512]{1,0:T(8,128)(2,1)S(1)}, bf16[256,512]{1,0:T(8,128)(2,1)S(1)}, bf16[256,512]{1,0:T(8,128)(2,...) custom-call(bf16[120,512]{1,0:T(8,128)(2,1)S(1)} %shard_map.121.refs, ...), custom_call_target="tpu_custom_call" | custom-call | flops 2000000000 | bytes 4194304 | tf_op jit(solution)/shard_map/pallas_call | solution.py:635
  22.4 0.0 collective-permute-done.5.refs_3_
  22.4 0.8 %collective-permute-done.3.refs_1_ = bf16[1,64,512]{2,1,0:T(8,128)(2,1)S(1)} collective-permute-done((bf16[1,64,512]{2,1,0:T(8,128)(2,1)S(1)}, bf16[1,64,512]{2,1,0:T(8,128)(2,1)S(1)}, u32[]{:S(2)}, u32[]{:S(2)}) %collective-permute-start.3) | collective-permute-done | bytes 65568 | tf_op jit(solution)/shard_map/ppermute | solution.py:648
  23.2 1.6 %shard_map.124 = (f32[256,512]{1,0:T(8,128)S(1)}, bf16[64,1024]{1,0:T(8,128)(2,1)S(1)}, bf16[64,1024]{1,0:T(8,128)(2,1)S(1)}) custom-call(bf16[1,64,512]{2,1,0:T(8,128)(2,1)S(1)} %copy-done, bf16[1,64,512]{2,1,0:T(8,128)(2,1)S(1)} %collective-permute-done.3.refs_1_, bf16[1,64,512]{2,1,0:T(8,128)(2,1)S(1)} %collective-permute-done.4.refs_2_, ...), custom_call_target="tpu_custom_call" | custom-call | flops 1000000000 | bytes 4194304 | tf_op jit(solution)/shard_map/pallas_call | solution.py:635
  24.8 0.1 collective-permute-start.9
  24.9 0.0 copy-start.1
  24.9 1.3 %shard_map.125 = (bf16[48,512]{1,0:T(8,128)(2,1)S(1)}, bf16[64,1024]{1,0:T(8,128)(2,1)S(1)}, bf16[64,1024]{1,0:T(8,128)(2,1)S(1)}) custom-call(bf16[192,512]{1,0:T(8,128)(2,1)S(1)} %get-tuple-element.42.grid_ref, bf16[256,512]{1,0:T(8,128)(2,1)S(1)} %get-tuple-element.43.mesh_ref, bf16[448,256]{1,0:T(8,128)(2,1)S(1)} %get-tuple-element.44.hot_ref, ...), custom_call_target="tpu_custom_call" | custom-call | flops 1000000000 | bytes 4194304 | tf_op jit(solution)/shard_map/pallas_call | solution.py:635
  26.2 0.5 %collective-permute-start.6 = (bf16[64,1024]{1,0:T(8,128)(2,1)S(1)}, bf16[64,1024]{1,0:T(8,128)(2,1)S(1)}, u32[]{:S(2)}, u32[]{:S(2)}) collective-permute-start(bf16[64,1024]{1,0:T(8,128)(2,1)S(1)} %get-tuple-element.61), channel_id=1, source_target_pairs={{0,1},{1,0},{2,3},{3,2},{4,5},{5,4},{6,7},{7,6},{8,9},{9,8},{10,11... | collective-permute-start | bytes 393224 | tf_op jit(solution)/shard_map/ppermute | solution.py:648
  26.8 0.0 collective-permute-done.9
  26.8 1.6 %collective-permute-start.10 = (bf16[64,1024]{1,0:T(8,128)(2,1)S(1)}, bf16[64,1024]{1,0:T(8,128)(2,1)S(1)}, u32[]{:S(2)}, u32[]{:S(2)}) collective-permute-start(bf16[64,1024]{1,0:T(8,128)(2,1)S(1)} %add_convert_fusion.1), channel_id=1, source_target_pairs={{0,2},{1,3},{2,0},{3,1},{4,6},{5,7},{6,4},{7,5},{8,10},{9,11},{10,... | collective-permute-start | bytes 393224 | tf_op jit(solution)/shard_map/ppermute | solution.py:648
  28.4 0.0 collective-permute-done.6
  28.4 1.0 %collective-permute-start.7 = (bf16[64,1024]{1,0:T(8,128)(2,1)S(1)}, bf16[64,1024]{1,0:T(8,128)(2,1)S(1)}, u32[]{:S(2)}, u32[]{:S(2)}) collective-permute-start(bf16[64,1024]{1,0:T(8,128)(2,1)S(1)} %add_convert_fusion.3), channel_id=1, source_target_pairs={{0,2},{1,3},{2,0},{3,1},{4,6},{5,7},{6,4},{7,5},{8,10},{9,11},{10,... | collective-permute-start | bytes 393224 | tf_op jit(solution)/shard_map/ppermute | solution.py:648
  29.4 1.1 %shard_map.126 = bf16[1,128,512]{2,1,0:T(8,128)(2,1)} custom-call(bf16[512,1536]{1,0:T(8,128)(2,1)S(1)} %get-tuple-element.50.refs_4_.turned_ref, s32[3,1,16]{2,1,0:T(1,128)S(1)} %bitcast.6, bf16[48,512]{1,0:T(8,128)(2,1)S(1)} %get-tuple-element.64.own_slot_ref), custom_call_target="tpu_custom_call" | custom-call | flops 100000000 | bytes 4194304 | tf_op jit(solution)/shard_map/pallas_call | solution.py:635
  30.5 2.7 %collective-permute-done.10 = bf16[64,1024]{1,0:T(8,128)(2,1)S(1)} collective-permute-done((bf16[64,1024]{1,0:T(8,128)(2,1)S(1)}, bf16[64,1024]{1,0:T(8,128)(2,1)S(1)}, u32[]{:S(2)}, u32[]{:S(2)}) %collective-permute-start.10) | collective-permute-done | bytes 131104 | tf_op jit(solution)/shard_map/ppermute | solution.py:648
  33.3 0.1 collective-permute-start.11
  33.4 1.8 %collective-permute-done.7 = bf16[64,1024]{1,0:T(8,128)(2,1)S(1)} collective-permute-done((bf16[64,1024]{1,0:T(8,128)(2,1)S(1)}, bf16[64,1024]{1,0:T(8,128)(2,1)S(1)}, u32[]{:S(2)}, u32[]{:S(2)}) %collective-permute-start.7) | collective-permute-done | bytes 131104 | tf_op jit(solution)/shard_map/ppermute | solution.py:648
  35.2 0.1 collective-permute-start.8
  35.2 0.0 collective-permute-done.11.other_two_ref
  35.2 0.9 %shard_map.127.settled_ref = f32[128,2048]{1,0:T(8,128)} custom-call(bf16[64,1024]{1,0:T(8,128)(2,1)S(1)} %add_convert_fusion.2.one_ref, bf16[64,1024]{1,0:T(8,128)(2,1)S(1)} %add_convert_fusion.two_ref, bf16[64,1024]{1,0:T(8,128)(2,1)S(1)} %collective-permute-done.11.other_two_ref), custom_call_target="tpu_custom_call" | custom-call | tf_op jit(solution)/shard_map/pallas_call | solution.py:824
  36.2 0.4 %collective-permute-done.8.other_one_ref = bf16[64,1024]{1,0:T(8,128)(2,1)S(1)} collective-permute-done((bf16[64,1024]{1,0:T(8,128)(2,1)S(1)}, bf16[64,1024]{1,0:T(8,128)(2,1)S(1)}, u32[]{:S(2)}, u32[]{:S(2)}) %collective-permute-start.8) | collective-permute-done | bytes 131104 | tf_op jit(solution)/shard_map/ppermute | solution.py:648
  36.6 0.7 %shard_map.128 = f32[128,2048]{1,0:T(8,128)} custom-call(bf16[64,1024]{1,0:T(8,128)(2,1)S(1)} %collective-permute-done.8.other_one_ref, f32[128,2048]{1,0:T(8,128)} %shard_map.127.settled_ref), custom_call_target="tpu_custom_call", output_to_operand_aliasing={{}: (1, {})} | custom-call | tf_op jit(solution)/shard_map/pallas_call | solution.py:832
  (8 shorter events, 0.2 us)
Async XLA Ops:
  0.6 14.8 %copy-start = (bf16[1,64,512]{2,1,0:T(8,128)(2,1)S(1)}, bf16[1,64,512]{2,1,0:T(8,128)(2,1)}, u32[]{:S(2)}) copy-start(bf16[1,64,512]{2,1,0:T(8,128)(2,1)} %refs_0_.2) | copy-start | bytes 196612
  1.9 13.6 %collective-permute-start = (bf16[120,512]{1,0:T(8,128)(2,1)S(1)}, bf16[120,512]{1,0:T(8,128)(2,1)S(1)}, u32[]{:S(2)}, u32[]{:S(2)}) collective-permute-start(bf16[120,512]{1,0:T(8,128)(2,1)S(1)} %shard_map.121.refs_0_), channel_id=1, source_target_pairs={{0,8},{4,12},{8,0},{12,4},{1,9},{5,13},{9,1},{13,5},{2,10},{6,14},... | collective-permute-start | bytes 368648 | tf_op jit(solution)/shard_map/ppermute | solution.py:648
  6.0 12.3 %collective-permute-start.1 = (bf16[120,512]{1,0:T(8,128)(2,1)S(1)}, bf16[120,512]{1,0:T(8,128)(2,1)S(1)}, u32[]{:S(2)}, u32[]{:S(2)}) collective-permute-start(bf16[120,512]{1,0:T(8,128)(2,1)S(1)} %shard_map.121.refs_0_), channel_id=1, source_target_pairs={{0,12},{4,8},{8,4},{12,0},{1,13},{5,9},{9,5},{13,1},{2,14},{6,10},... | collective-permute-start | bytes 368648 | tf_op jit(solution)/shard_map/ppermute | solution.py:648
  7.3 10.9 %collective-permute-start.2 = (bf16[120,512]{1,0:T(8,128)(2,1)S(1)}, bf16[120,512]{1,0:T(8,128)(2,1)S(1)}, u32[]{:S(2)}, u32[]{:S(2)}) collective-permute-start(bf16[120,512]{1,0:T(8,128)(2,1)S(1)} %shard_map.121.refs_0_), channel_id=1, source_target_pairs={{0,4},{4,0},{8,12},{12,8},{1,5},{5,1},{9,13},{13,9},{2,6},{6,2},{1... | collective-permute-start | bytes 368648 | tf_op jit(solution)/shard_map/ppermute | solution.py:648
  7.6 14.9 %collective-permute-start.5 = (bf16[1,64,512]{2,1,0:T(8,128)(2,1)}, bf16[1,64,512]{2,1,0:T(8,128)(2,1)S(1)}, u32[]{:S(2)}, u32[]{:S(2)}) collective-permute-start(bf16[1,64,512]{2,1,0:T(8,128)(2,1)} %refs_0_.2), channel_id=1, source_target_pairs={{0,4},{4,0},{8,12},{12,8},{1,5},{5,1},{9,13},{13,9},{2,6},{6,2},{1... | collective-permute-start | bytes 196616 | tf_op jit(solution)/shard_map/ppermute | solution.py:648
  15.5 7.7 %collective-permute-start.3 = (bf16[1,64,512]{2,1,0:T(8,128)(2,1)S(1)}, bf16[1,64,512]{2,1,0:T(8,128)(2,1)S(1)}, u32[]{:S(2)}, u32[]{:S(2)}) collective-permute-start(bf16[1,64,512]{2,1,0:T(8,128)(2,1)S(1)} %copy-done), channel_id=1, source_target_pairs={{0,8},{4,12},{8,0},{12,4},{1,9},{5,13},{9,1},{13,5},{2,10},{6,14},... | collective-permute-start | bytes 196616 | tf_op jit(solution)/shard_map/ppermute | solution.py:648
  15.5 7.7 %collective-permute-start.4 = (bf16[1,64,512]{2,1,0:T(8,128)(2,1)S(1)}, bf16[1,64,512]{2,1,0:T(8,128)(2,1)S(1)}, u32[]{:S(2)}, u32[]{:S(2)}) collective-permute-start(bf16[1,64,512]{2,1,0:T(8,128)(2,1)S(1)} %copy-done), channel_id=1, source_target_pairs={{0,12},{4,8},{8,4},{12,0},{1,13},{5,9},{9,5},{13,1},{2,14},{6,10},... | collective-permute-start | bytes 196616 | tf_op jit(solution)/shard_map/ppermute | solution.py:648
  24.8 2.0 %collective-permute-start.9 = (bf16[64,1024]{1,0:T(8,128)(2,1)S(1)}, bf16[64,1024]{1,0:T(8,128)(2,1)S(1)}, u32[]{:S(2)}, u32[]{:S(2)}) collective-permute-start(bf16[64,1024]{1,0:T(8,128)(2,1)S(1)} %get-tuple-element.68), channel_id=1, source_target_pairs={{0,1},{1,0},{2,3},{3,2},{4,5},{5,4},{6,7},{7,6},{8,9},{9,8},{10,11... | collective-permute-start | bytes 393224 | tf_op jit(solution)/shard_map/ppermute | solution.py:648
  24.9 4.5 %copy-start.1 = (s32[1,3,16]{2,0,1:T(1,128)S(1)}, s32[1,3,16]{2,0,1:T(1,128)}, u32[]{:S(2)}) copy-start(s32[1,3,16]{2,0,1:T(1,128)} %param.14) | copy-start | bytes 580
  26.2 2.2 %collective-permute-start.6 = (bf16[64,1024]{1,0:T(8,128)(2,1)S(1)}, bf16[64,1024]{1,0:T(8,128)(2,1)S(1)}, u32[]{:S(2)}, u32[]{:S(2)}) collective-permute-start(bf16[64,1024]{1,0:T(8,128)(2,1)S(1)} %get-tuple-element.61), channel_id=1, source_target_pairs={{0,1},{1,0},{2,3},{3,2},{4,5},{5,4},{6,7},{7,6},{8,9},{9,8},{10,11... | collective-permute-start | bytes 393224 | tf_op jit(solution)/shard_map/ppermute | solution.py:648
  26.8 6.4 %collective-permute-start.10 = (bf16[64,1024]{1,0:T(8,128)(2,1)S(1)}, bf16[64,1024]{1,0:T(8,128)(2,1)S(1)}, u32[]{:S(2)}, u32[]{:S(2)}) collective-permute-start(bf16[64,1024]{1,0:T(8,128)(2,1)S(1)} %add_convert_fusion.1), channel_id=1, source_target_pairs={{0,2},{1,3},{2,0},{3,1},{4,6},{5,7},{6,4},{7,5},{8,10},{9,11},{10,... | collective-permute-start | bytes 393224 | tf_op jit(solution)/shard_map/ppermute | solution.py:648
  28.4 6.7 %collective-permute-start.7 = (bf16[64,1024]{1,0:T(8,128)(2,1)S(1)}, bf16[64,1024]{1,0:T(8,128)(2,1)S(1)}, u32[]{:S(2)}, u32[]{:S(2)}) collective-permute-start(bf16[64,1024]{1,0:T(8,128)(2,1)S(1)} %add_convert_fusion.3), channel_id=1, source_target_pairs={{0,2},{1,3},{2,0},{3,1},{4,6},{5,7},{6,4},{7,5},{8,10},{9,11},{10,... | collective-permute-start | bytes 393224 | tf_op jit(solution)/shard_map/ppermute | solution.py:648
  33.3 2.0 %collective-permute-start.11 = (bf16[64,1024]{1,0:T(8,128)(2,1)S(1)}, bf16[64,1024]{1,0:T(8,128)(2,1)S(1)}, u32[]{:S(2)}, u32[]{:S(2)}) collective-permute-start(bf16[64,1024]{1,0:T(8,128)(2,1)S(1)} %add_convert_fusion.two_ref), channel_id=1, source_target_pairs={{0,1},{1,0},{2,3},{3,2},{4,5},{5,4},{6,7},{7,6},{8,9},{9,8},{10,11... | collective-permute-start | bytes 393224 | tf_op jit(solution)/shard_map/ppermute | solution.py:648
  35.2 1.4 %collective-permute-start.8 = (bf16[64,1024]{1,0:T(8,128)(2,1)S(1)}, bf16[64,1024]{1,0:T(8,128)(2,1)S(1)}, u32[]{:S(2)}, u32[]{:S(2)}) collective-permute-start(bf16[64,1024]{1,0:T(8,128)(2,1)S(1)} %add_convert_fusion.2.one_ref), channel_id=1, source_target_pairs={{0,1},{1,0},{2,3},{3,2},{4,5},{5,4},{6,7},{7,6},{8,9},{9,8},{10,11... | collective-permute-start | bytes 393224 | tf_op jit(solution)/shard_map/ppermute | solution.py:648

commit v16 on v15

--- a/solution.py
+++ b/solution.py
@@ -307,11 +307,12 @@
     activation = gathered(*work[0])
     for n, (d, first, size) in enumerate(work):
         coming = gathered(*work[n + 1]) if n + 1 < len(work) else None
+        activation = activation.astype(BF16)
         squash = 0.5 + 0.5 * jnp.tanh(0.5 * activation)
         message = activation * squash
         rows = slice(d * edges + first, d * edges + first + size)
-        slope_ref[rows, :] = (squash + message * (1.0 - squash)).astype(BF16)
-        message_ref[rows, :] = message.astype(BF16)
+        slope_ref[rows, :] = squash + message * (1.0 - squash)
+        message_ref[rows, :] = message
         activation = coming
         if first + size == edges:
             hot = hot_ref[(d + 1) * count - mesh_count : (d + 1) * count, :]
@@ -459,7 +460,7 @@
     for n, (d, first, size) in enumerate(work):
         coming = gathered(*work[n + 1]) if n + 1 < len(work) else None
         rows = slice(d * edges + first, d * edges + first + size)
-        edge_grad_ref[rows, :] = (upstream * slope_ref[rows, :].astype(F32)).astype(BF16)
+        edge_grad_ref[rows, :] = upstream.astype(BF16) * slope_ref[rows, :]
         upstream = coming
         if first + size == edges:
             hot = hot_ref[d * count : (d + 1) * count, :]

time: 37.5 us -> 37.5 us (level)
  waiting for transfers between devices: 9.69 us -> 10.1 us
    ppermute x12, waiting for transfers between devices: 9.69 us -> 10.1 us  [swap(): lax.ppermute(block, axis, [(i, i ^ bits) for i in range(lax.axis_size(axi...]
  transfers between devices with their start and end apart: 12 -> 12, of which waited for: 5 -> 5; matrix products, arithmetic and copies ran while one was open for 0% -> 0% of each run, Pallas kernels for 26% -> 25%
where the time goes in v16:
time: 37.5 us; the launch traced here: 37.3 us
  starting transfers between devices  13.6 us (36%)
  Pallas kernels  12.8 us (34%)
  waiting for transfers between devices  10.1 us (27%)
  between operations  0.74 us (2%)
    ppermute x12, starting transfers between devices, swap(): lax.ppermute(block, axis, [(i, i ^ bits) for i in range(lax.axis_size(axi...  13.6 us
    pallas_call x6, Pallas kernels, call(): pl.pallas_call(kernel, out_shape=[jax.ShapeDtypeStruct(shape, kind) for s...  11.1 us
    ppermute x12, waiting for transfers between devices, swap(): lax.ppermute(block, axis, [(i, i ^ bits) for i in range(lax.axis_size(axi...  10.1 us
    pallas_call x1, Pallas kernels, whole_sample_body(): pl.pallas_call(settle_kernel, out_shape=weight_shape, in_specs=[VMEM] * 3...  0.92 us
  transfers between devices with their start and end apart: 12, of which 5 were waited for; matrix products, arithmetic and copies ran while one was open for 0% of the time, Pallas kernels for 25%

profile of v16, /device:TPU:0, one launch (start us, length us, event | category | flops | bytes accessed | tf_op | source)
XLA Modules:
  0.0 37.3 jit_solution(6029072370538311063)
XLA Ops:
  0.6 0.0 copy-start
  0.6 1.2 %shard_map.121.refs_0_ = bf16[120,512]{1,0:T(8,128)(2,1)S(1)} custom-call(bf16[1,128,512]{2,1,0:T(8,128)(2,1)} %refs_0_.1, bf16[1,64,512]{2,1,0:T(8,128)(2,1)} %refs_1_.1, s32[3,1,16]{2,1,0:T(1,128)} %bitcast.5, s32[1,256]{1,0:T(1,128)} %bitcast.7, s32[1,256]{1,0:T(1,128)} %bitcast.8, s32[1,4,8]{2,1,0:T(4,128)} %refs_5_.1, s32[1,256]{1,0:T(1,128)} %bitcast.9, ...), custom_call_target="tpu_custom_call" | custom-call | flops 10000000 | bytes 4194304 | tf_op jit(solution)/shard_map/pallas_call | solution.py:636
  1.9 4.1 %collective-permute-start = (bf16[120,512]{1,0:T(8,128)(2,1)S(1)}, bf16[120,512]{1,0:T(8,128)(2,1)S(1)}, u32[]{:S(2)}, u32[]{:S(2)}) collective-permute-start(bf16[120,512]{1,0:T(8,128)(2,1)S(1)} %shard_map.121.refs_0_), channel_id=1, source_target_pairs={{0,8},{4,12},{8,0},{12,4},{1,9},{5,13},{9,1},{13,5},{2,10},{6,14},... | collective-permute-start | bytes 368648 | tf_op jit(solution)/shard_map/ppermute | solution.py:649
  6.0 1.3 %collective-permute-start.1 = (bf16[120,512]{1,0:T(8,128)(2,1)S(1)}, bf16[120,512]{1,0:T(8,128)(2,1)S(1)}, u32[]{:S(2)}, u32[]{:S(2)}) collective-permute-start(bf16[120,512]{1,0:T(8,128)(2,1)S(1)} %shard_map.121.refs_0_), channel_id=1, source_target_pairs={{0,12},{4,8},{8,4},{12,0},{1,13},{5,9},{9,5},{13,1},{2,14},{6,10},... | collective-permute-start | bytes 368648 | tf_op jit(solution)/shard_map/ppermute | solution.py:649
  7.3 0.2 collective-permute-start.2
  7.6 1.8 %collective-permute-start.5 = (bf16[1,64,512]{2,1,0:T(8,128)(2,1)}, bf16[1,64,512]{2,1,0:T(8,128)(2,1)S(1)}, u32[]{:S(2)}, u32[]{:S(2)}) collective-permute-start(bf16[1,64,512]{2,1,0:T(8,128)(2,1)} %refs_0_.2), channel_id=1, source_target_pairs={{0,4},{4,0},{8,12},{12,8},{1,5},{5,1},{9,13},{13,9},{2,6},{6,2},{1... | collective-permute-start | bytes 196616 | tf_op jit(solution)/shard_map/ppermute | solution.py:649
  9.4 2.1 %shard_map.122 = (bf16[512,2048]{1,0:T(8,128)(2,1)S(1)}, bf16[512,1536]{1,0:T(8,128)(2,1)S(1)}) custom-call(bf16[512,2048]{1,0:T(8,128)(2,1)} %source_ref), custom_call_target="tpu_custom_call" | custom-call | flops 100000000 | bytes 4194304 | tf_op jit(solution)/shard_map/pallas_call | solution.py:636
  11.4 4.0 %collective-permute-done.refs_1_ = bf16[120,512]{1,0:T(8,128)(2,1)S(1)} collective-permute-done((bf16[120,512]{1,0:T(8,128)(2,1)S(1)}, bf16[120,512]{1,0:T(8,128)(2,1)S(1)}, u32[]{:S(2)}, u32[]{:S(2)}) %collective-permute-start) | collective-permute-done | bytes 122912 | tf_op jit(solution)/shard_map/ppermute | solution.py:649
  15.5 0.0 collective-permute-start.3
  15.5 2.8 %collective-permute-start.4 = (bf16[1,64,512]{2,1,0:T(8,128)(2,1)S(1)}, bf16[1,64,512]{2,1,0:T(8,128)(2,1)S(1)}, u32[]{:S(2)}, u32[]{:S(2)}) collective-permute-start(bf16[1,64,512]{2,1,0:T(8,128)(2,1)S(1)} %copy-done), channel_id=1, source_target_pairs={{0,12},{4,8},{8,4},{12,0},{1,13},{5,9},{9,5},{13,1},{2,14},{6,10},... | collective-permute-start | bytes 196616 | tf_op jit(solution)/shard_map/ppermute | solution.py:649
  18.3 0.0 collective-permute-done.1.refs_2_
  18.3 0.0 collective-permute-done.2.refs_3_
  18.3 3.8 %shard_map.123 = (bf16[1,64,512]{2,1,0:T(8,128)(2,1)}, bf16[192,512]{1,0:T(8,128)(2,1)S(1)}, bf16[256,512]{1,0:T(8,128)(2,1)S(1)}, bf16[256,512]{1,0:T(8,128)(2,...) custom-call(bf16[120,512]{1,0:T(8,128)(2,1)S(1)} %shard_map.121.refs, ...), custom_call_target="tpu_custom_call" | custom-call | flops 2000000000 | bytes 4194304 | tf_op jit(solution)/shard_map/pallas_call | solution.py:636
  22.1 0.0 collective-permute-done.5.refs_3_
  22.1 1.1 %collective-permute-done.3.refs_1_ = bf16[1,64,512]{2,1,0:T(8,128)(2,1)S(1)} collective-permute-done((bf16[1,64,512]{2,1,0:T(8,128)(2,1)S(1)}, bf16[1,64,512]{2,1,0:T(8,128)(2,1)S(1)}, u32[]{:S(2)}, u32[]{:S(2)}) %collective-permute-start.3) | collective-permute-done | bytes 65568 | tf_op jit(solution)/shard_map/ppermute | solution.py:649
  23.2 1.6 %shard_map.124 = (f32[256,512]{1,0:T(8,128)S(1)}, bf16[64,1024]{1,0:T(8,128)(2,1)S(1)}, bf16[64,1024]{1,0:T(8,128)(2,1)S(1)}) custom-call(bf16[1,64,512]{2,1,0:T(8,128)(2,1)S(1)} %copy-done, bf16[1,64,512]{2,1,0:T(8,128)(2,1)S(1)} %collective-permute-done.3.refs_1_, bf16[1,64,512]{2,1,0:T(8,128)(2,1)S(1)} %collective-permute-done.4.refs_2_, ...), custom_call_target="tpu_custom_call" | custom-call | flops 1000000000 | bytes 4194304 | tf_op jit(solution)/shard_map/pallas_call | solution.py:636
  24.8 0.1 collective-permute-start.9
  24.9 0.0 copy-start.1
  24.9 1.3 %shard_map.125 = (bf16[48,512]{1,0:T(8,128)(2,1)S(1)}, bf16[64,1024]{1,0:T(8,128)(2,1)S(1)}, bf16[64,1024]{1,0:T(8,128)(2,1)S(1)}) custom-call(bf16[192,512]{1,0:T(8,128)(2,1)S(1)} %get-tuple-element.42.grid_ref, bf16[256,512]{1,0:T(8,128)(2,1)S(1)} %get-tuple-element.43.mesh_ref, bf16[448,256]{1,0:T(8,128)(2,1)S(1)} %get-tuple-element.44.hot_ref, ...), custom_call_target="tpu_custom_call" | custom-call | flops 1000000000 | bytes 4194304 | tf_op jit(solution)/shard_map/pallas_call | solution.py:636
  26.2 0.6 %collective-permute-start.6 = (bf16[64,1024]{1,0:T(8,128)(2,1)S(1)}, bf16[64,1024]{1,0:T(8,128)(2,1)S(1)}, u32[]{:S(2)}, u32[]{:S(2)}) collective-permute-start(bf16[64,1024]{1,0:T(8,128)(2,1)S(1)} %get-tuple-element.61), channel_id=1, source_target_pairs={{0,1},{1,0},{2,3},{3,2},{4,5},{5,4},{6,7},{7,6},{8,9},{9,8},{10,11... | collective-permute-start | bytes 393224 | tf_op jit(solution)/shard_map/ppermute | solution.py:649
  26.8 0.0 collective-permute-done.9
  26.8 1.6 %collective-permute-start.10 = (bf16[64,1024]{1,0:T(8,128)(2,1)S(1)}, bf16[64,1024]{1,0:T(8,128)(2,1)S(1)}, u32[]{:S(2)}, u32[]{:S(2)}) collective-permute-start(bf16[64,1024]{1,0:T(8,128)(2,1)S(1)} %add_convert_fusion.1), channel_id=1, source_target_pairs={{0,2},{1,3},{2,0},{3,1},{4,6},{5,7},{6,4},{7,5},{8,10},{9,11},{10,... | collective-permute-start | bytes 393224 | tf_op jit(solution)/shard_map/ppermute | solution.py:649
  28.5 1.0 %collective-permute-start.7 = (bf16[64,1024]{1,0:T(8,128)(2,1)S(1)}, bf16[64,1024]{1,0:T(8,128)(2,1)S(1)}, u32[]{:S(2)}, u32[]{:S(2)}) collective-permute-start(bf16[64,1024]{1,0:T(8,128)(2,1)S(1)} %add_convert_fusion.3), channel_id=1, source_target_pairs={{0,2},{1,3},{2,0},{3,1},{4,6},{5,7},{6,4},{7,5},{8,10},{9,11},{10,... | collective-permute-start | bytes 393224 | tf_op jit(solution)/shard_map/ppermute | solution.py:649
  29.4 1.1 %shard_map.126 = bf16[1,128,512]{2,1,0:T(8,128)(2,1)} custom-call(bf16[512,1536]{1,0:T(8,128)(2,1)S(1)} %get-tuple-element.50.refs_4_.turned_ref, s32[3,1,16]{2,1,0:T(1,128)S(1)} %bitcast.6, bf16[48,512]{1,0:T(8,128)(2,1)S(1)} %get-tuple-element.64.own_slot_ref), custom_call_target="tpu_custom_call" | custom-call | flops 100000000 | bytes 4194304 | tf_op jit(solution)/shard_map/pallas_call | solution.py:636
  30.5 2.7 %collective-permute-done.10 = bf16[64,1024]{1,0:T(8,128)(2,1)S(1)} collective-permute-done((bf16[64,1024]{1,0:T(8,128)(2,1)S(1)}, bf16[64,1024]{1,0:T(8,128)(2,1)S(1)}, u32[]{:S(2)}, u32[]{:S(2)}) %collective-permute-start.10) | collective-permute-done | bytes 131104 | tf_op jit(solution)/shard_map/ppermute | solution.py:649
  33.3 0.1 collective-permute-start.11
  33.4 1.8 %collective-permute-done.7 = bf16[64,1024]{1,0:T(8,128)(2,1)S(1)} collective-permute-done((bf16[64,1024]{1,0:T(8,128)(2,1)S(1)}, bf16[64,1024]{1,0:T(8,128)(2,1)S(1)}, u32[]{:S(2)}, u32[]{:S(2)}) %collective-permute-start.7) | collective-permute-done | bytes 131104 | tf_op jit(solution)/shard_map/ppermute | solution.py:649
  35.2 0.1 collective-permute-start.8
  35.3 0.0 collective-permute-done.11.other_two_ref
  35.3 0.9 %shard_map.127.settled_ref = f32[128,2048]{1,0:T(8,128)} custom-call(bf16[64,1024]{1,0:T(8,128)(2,1)S(1)} %add_convert_fusion.2.one_ref, bf16[64,1024]{1,0:T(8,128)(2,1)S(1)} %add_convert_fusion.two_ref, bf16[64,1024]{1,0:T(8,128)(2,1)S(1)} %collective-permute-done.11.other_two_ref), custom_call_target="tpu_custom_call" | custom-call | tf_op jit(solution)/shard_map/pallas_call | solution.py:825
  36.2 0.4 %collective-permute-done.8.other_one_ref = bf16[64,1024]{1,0:T(8,128)(2,1)S(1)} collective-permute-done((bf16[64,1024]{1,0:T(8,128)(2,1)S(1)}, bf16[64,1024]{1,0:T(8,128)(2,1)S(1)}, u32[]{:S(2)}, u32[]{:S(2)}) %collective-permute-start.8) | collective-permute-done | bytes 131104 | tf_op jit(solution)/shard_map/ppermute | solution.py:649
  36.6 0.7 %shard_map.128 = f32[128,2048]{1,0:T(8,128)} custom-call(bf16[64,1024]{1,0:T(8,128)(2,1)S(1)} %collective-permute-done.8.other_one_ref, f32[128,2048]{1,0:T(8,128)} %shard_map.127.settled_ref), custom_call_target="tpu_custom_call", output_to_operand_aliasing={{}: (1, {})} | custom-call | tf_op jit(solution)/shard_map/pallas_call | solution.py:833
  (8 shorter events, 0.1 us)
Async XLA Ops:
  0.6 14.8 %copy-start = (bf16[1,64,512]{2,1,0:T(8,128)(2,1)S(1)}, bf16[1,64,512]{2,1,0:T(8,128)(2,1)}, u32[]{:S(2)}) copy-start(bf16[1,64,512]{2,1,0:T(8,128)(2,1)} %refs_0_.2) | copy-start | bytes 196612
  1.9 13.6 %collective-permute-start = (bf16[120,512]{1,0:T(8,128)(2,1)S(1)}, bf16[120,512]{1,0:T(8,128)(2,1)S(1)}, u32[]{:S(2)}, u32[]{:S(2)}) collective-permute-start(bf16[120,512]{1,0:T(8,128)(2,1)S(1)} %shard_map.121.refs_0_), channel_id=1, source_target_pairs={{0,8},{4,12},{8,0},{12,4},{1,9},{5,13},{9,1},{13,5},{2,10},{6,14},... | collective-permute-start | bytes 368648 | tf_op jit(solution)/shard_map/ppermute | solution.py:649
  6.0 12.3 %collective-permute-start.1 = (bf16[120,512]{1,0:T(8,128)(2,1)S(1)}, bf16[120,512]{1,0:T(8,128)(2,1)S(1)}, u32[]{:S(2)}, u32[]{:S(2)}) collective-permute-start(bf16[120,512]{1,0:T(8,128)(2,1)S(1)} %shard_map.121.refs_0_), channel_id=1, source_target_pairs={{0,12},{4,8},{8,4},{12,0},{1,13},{5,9},{9,5},{13,1},{2,14},{6,10},... | collective-permute-start | bytes 368648 | tf_op jit(solution)/shard_map/ppermute | solution.py:649
  7.3 10.9 %collective-permute-start.2 = (bf16[120,512]{1,0:T(8,128)(2,1)S(1)}, bf16[120,512]{1,0:T(8,128)(2,1)S(1)}, u32[]{:S(2)}, u32[]{:S(2)}) collective-permute-start(bf16[120,512]{1,0:T(8,128)(2,1)S(1)} %shard_map.121.refs_0_), channel_id=1, source_target_pairs={{0,4},{4,0},{8,12},{12,8},{1,5},{5,1},{9,13},{13,9},{2,6},{6,2},{1... | collective-permute-start | bytes 368648 | tf_op jit(solution)/shard_map/ppermute | solution.py:649
  7.6 14.5 %collective-permute-start.5 = (bf16[1,64,512]{2,1,0:T(8,128)(2,1)}, bf16[1,64,512]{2,1,0:T(8,128)(2,1)S(1)}, u32[]{:S(2)}, u32[]{:S(2)}) collective-permute-start(bf16[1,64,512]{2,1,0:T(8,128)(2,1)} %refs_0_.2), channel_id=1, source_target_pairs={{0,4},{4,0},{8,12},{12,8},{1,5},{5,1},{9,13},{13,9},{2,6},{6,2},{1... | collective-permute-start | bytes 196616 | tf_op jit(solution)/shard_map/ppermute | solution.py:649
  15.5 7.7 %collective-permute-start.3 = (bf16[1,64,512]{2,1,0:T(8,128)(2,1)S(1)}, bf16[1,64,512]{2,1,0:T(8,128)(2,1)S(1)}, u32[]{:S(2)}, u32[]{:S(2)}) collective-permute-start(bf16[1,64,512]{2,1,0:T(8,128)(2,1)S(1)} %copy-done), channel_id=1, source_target_pairs={{0,8},{4,12},{8,0},{12,4},{1,9},{5,13},{9,1},{13,5},{2,10},{6,14},... | collective-permute-start | bytes 196616 | tf_op jit(solution)/shard_map/ppermute | solution.py:649
  15.5 7.7 %collective-permute-start.4 = (bf16[1,64,512]{2,1,0:T(8,128)(2,1)S(1)}, bf16[1,64,512]{2,1,0:T(8,128)(2,1)S(1)}, u32[]{:S(2)}, u32[]{:S(2)}) collective-permute-start(bf16[1,64,512]{2,1,0:T(8,128)(2,1)S(1)} %copy-done), channel_id=1, source_target_pairs={{0,12},{4,8},{8,4},{12,0},{1,13},{5,9},{9,5},{13,1},{2,14},{6,10},... | collective-permute-start | bytes 196616 | tf_op jit(solution)/shard_map/ppermute | solution.py:649
  24.8 2.0 %collective-permute-start.9 = (bf16[64,1024]{1,0:T(8,128)(2,1)S(1)}, bf16[64,1024]{1,0:T(8,128)(2,1)S(1)}, u32[]{:S(2)}, u32[]{:S(2)}) collective-permute-start(bf16[64,1024]{1,0:T(8,128)(2,1)S(1)} %get-tuple-element.68), channel_id=1, source_target_pairs={{0,1},{1,0},{2,3},{3,2},{4,5},{5,4},{6,7},{7,6},{8,9},{9,8},{10,11... | collective-permute-start | bytes 393224 | tf_op jit(solution)/shard_map/ppermute | solution.py:649
  24.9 4.5 %copy-start.1 = (s32[1,3,16]{2,0,1:T(1,128)S(1)}, s32[1,3,16]{2,0,1:T(1,128)}, u32[]{:S(2)}) copy-start(s32[1,3,16]{2,0,1:T(1,128)} %param.14) | copy-start | bytes 580
  26.2 2.2 %collective-permute-start.6 = (bf16[64,1024]{1,0:T(8,128)(2,1)S(1)}, bf16[64,1024]{1,0:T(8,128)(2,1)S(1)}, u32[]{:S(2)}, u32[]{:S(2)}) collective-permute-start(bf16[64,1024]{1,0:T(8,128)(2,1)S(1)} %get-tuple-element.61), channel_id=1, source_target_pairs={{0,1},{1,0},{2,3},{3,2},{4,5},{5,4},{6,7},{7,6},{8,9},{9,8},{10,11... | collective-permute-start | bytes 393224 | tf_op jit(solution)/shard_map/ppermute | solution.py:649
  26.8 6.4 %collective-permute-start.10 = (bf16[64,1024]{1,0:T(8,128)(2,1)S(1)}, bf16[64,1024]{1,0:T(8,128)(2,1)S(1)}, u32[]{:S(2)}, u32[]{:S(2)}) collective-permute-start(bf16[64,1024]{1,0:T(8,128)(2,1)S(1)} %add_convert_fusion.1), channel_id=1, source_target_pairs={{0,2},{1,3},{2,0},{3,1},{4,6},{5,7},{6,4},{7,5},{8,10},{9,11},{10,... | collective-permute-start | bytes 393224 | tf_op jit(solution)/shard_map/ppermute | solution.py:649
  28.5 6.7 %collective-permute-start.7 = (bf16[64,1024]{1,0:T(8,128)(2,1)S(1)}, bf16[64,1024]{1,0:T(8,128)(2,1)S(1)}, u32[]{:S(2)}, u32[]{:S(2)}) collective-permute-start(bf16[64,1024]{1,0:T(8,128)(2,1)S(1)} %add_convert_fusion.3), channel_id=1, source_target_pairs={{0,2},{1,3},{2,0},{3,1},{4,6},{5,7},{6,4},{7,5},{8,10},{9,11},{10,... | collective-permute-start | bytes 393224 | tf_op jit(solution)/shard_map/ppermute | solution.py:649
  33.3 2.0 %collective-permute-start.11 = (bf16[64,1024]{1,0:T(8,128)(2,1)S(1)}, bf16[64,1024]{1,0:T(8,128)(2,1)S(1)}, u32[]{:S(2)}, u32[]{:S(2)}) collective-permute-start(bf16[64,1024]{1,0:T(8,128)(2,1)S(1)} %add_convert_fusion.two_ref), channel_id=1, source_target_pairs={{0,1},{1,0},{2,3},{3,2},{4,5},{5,4},{6,7},{7,6},{8,9},{9,8},{10,11... | collective-permute-start | bytes 393224 | tf_op jit(solution)/shard_map/ppermute | solution.py:649
  35.2 1.4 %collective-permute-start.8 = (bf16[64,1024]{1,0:T(8,128)(2,1)S(1)}, bf16[64,1024]{1,0:T(8,128)(2,1)S(1)}, u32[]{:S(2)}, u32[]{:S(2)}) collective-permute-start(bf16[64,1024]{1,0:T(8,128)(2,1)S(1)} %add_convert_fusion.2.one_ref), channel_id=1, source_target_pairs={{0,1},{1,0},{2,3},{3,2},{4,5},{5,4},{6,7},{7,6},{8,9},{9,8},{10,11... | collective-permute-start | bytes 393224 | tf_op jit(solution)/shard_map/ppermute | solution.py:649

commit v17 on v16

--- a/solution.py
+++ b/solution.py
@@ -443,28 +443,30 @@
     mesh_out_ref[0] = (first_ref[own, :].astype(F32) + normed_two_ref[own, :]).astype(BF16)
 
 
-def edge_backward(regions, agg_grad, hot_ref, turned_hot_ref, slope_ref, edge_grad_ref):
-    edges = slope_ref.shape[0] // regions
-    count = hot_ref.shape[0] // regions
-    mesh_count = agg_grad.shape[0] // regions
-    blank = jnp.zeros((count - mesh_count, agg_grad.shape[1]), BF16)
-    work = [(d, first, size) for d in range(regions) for first, size in edge_blocks(edges)]
-
-    def gathered(d, first, size):
-        rows = slice(d * edges + first, d * edges + first + size)
-        table = jnp.concatenate([blank, agg_grad[d * mesh_count : (d + 1) * mesh_count]], axis=0)
-        return dot(turned_hot_ref[rows, :], table)
+def edge_backward(regions, agg_grad_ref, hot_ref, turned_hot_ref, slope_ref, edge_grad_ref):
+    mesh_count = agg_grad_ref.shape[0] // len(regions)
+    edges = edge_grad_ref.shape[0] // len(regions)
+    count = turned_hot_ref.shape[1]
+    blank = jnp.zeros((count - mesh_count, agg_grad_ref.shape[1]), BF16)
+    work = [(n, first, size) for n in range(len(regions)) for first, size in edge_blocks(edges)]
+
+    def at(n, first, size):
+        return pl.ds(pl.multiple_of(regions[n] * edges + first, size), size)
+
+    def gathered(n, first, size):
+        own = agg_grad_ref[n * mesh_count : (n + 1) * mesh_count, :]
+        return dot(turned_hot_ref[at(n, first, size), :], jnp.concatenate([blank, own], axis=0))
 
     sums = []
     upstream = gathered(*work[0])
-    for n, (d, first, size) in enumerate(work):
-        coming = gathered(*work[n + 1]) if n + 1 < len(work) else None
-        rows = slice(d * edges + first, d * edges + first + size)
-        edge_grad_ref[rows, :] = upstream.astype(BF16) * slope_ref[rows, :]
+    for k, (n, first, size) in enumerate(work):
+        coming = gathered(*work[k + 1]) if k + 1 < len(work) else None
+        rows = slice(n * edges + first, n * edges + first + size)
+        edge_grad_ref[rows, :] = upstream.astype(BF16) * slope_ref[at(n, first, size), :]
         upstream = coming
         if first + size == edges:
-            hot = hot_ref[d * count : (d + 1) * count, :]
-            sums.append(dot(hot, edge_grad_ref[d * edges : (d + 1) * edges, :]))
+            hot = hot_ref[pl.ds(pl.multiple_of(regions[n] * count, count), count), :]
+            sums.append(dot(hot, edge_grad_ref[n * edges : (n + 1) * edges, :]))
     return sums
 
 
@@ -475,13 +477,56 @@
     give_ref[...] = share_ref[pl.ds(pl.multiple_of((1 - core) * half, half), half), :]
 
 
-def process_back_kernel(steps, mesh_cap, *refs):
-    regions = len(steps)
-    cotangent_refs = refs[:regions]
+def process_back_part(
+    steps, mesh_count, cotangent_refs, hot_ref, turned_hot_ref, slope_ref, normed_ref, scaled_ref,
+    agg_grad_ref, edge_grad_ref,
+):
+    me = lax.axis_index("space")
+    regions = [lax.bitwise_xor(me, step) for step in steps]
+    for n, (region, cotangent_ref) in enumerate(zip(regions, cotangent_refs)):
+        rows = pl.ds(pl.multiple_of(region * mesh_count, mesh_count), mesh_count)
+        agg_grad_ref[n * mesh_count : (n + 1) * mesh_count, :] = moments_back(
+            normed_ref[rows, :], scaled_ref[rows, 0:1], cotangent_ref[0].astype(F32)
+        ).astype(BF16)
+    return regions, edge_backward(
+        regions, agg_grad_ref, hot_ref, turned_hot_ref, slope_ref, edge_grad_ref
+    )
+
+
+def near_back_kernel(steps, *refs):
+    cotangent_refs, refs = refs[: len(steps)], refs[len(steps) :]
+    (
+        hot_ref,
+        turned_hot_ref,
+        slope_ref,
+        normed_ref,
+        scaled_ref,
+        *whole_refs,
+    ) = refs[:9]
+    sums_ref, *column_refs = refs[9:14]
+    agg_grad_ref, edge_grad_ref = refs[14:]
+    mesh_count = agg_grad_ref.shape[0] // len(steps)
+    count = turned_hot_ref.shape[1]
+    _, all_sums = process_back_part(
+        steps, mesh_count, cotangent_refs, hot_ref, turned_hot_ref, slope_ref, normed_ref,
+        scaled_ref, agg_grad_ref, edge_grad_ref,
+    )
+    for n, sums in enumerate(all_sums):
+        sums_ref[n * count : (n + 1) * count, :] = sums
+    columns = column_refs[0].shape[0]
+    mine = pl.ds(pl.multiple_of(lax.axis_index("space") * columns, columns), columns)
+    for whole_ref, column_ref in zip(whole_refs, column_refs):
+        column_ref[...] = whole_ref[:, mine].T
+
+
+def far_back_kernel(near, far, mesh_cap, *refs):
+    regions = len(near) + len(far)
+    cotangent_refs, refs = refs[:regions], refs[regions:]
     (
         turned_ref,
-        first_ref,
-        sent_ref,
+        first_columns_ref,
+        sent_columns_ref,
+        near_sums_ref,
         hot_ref,
         turned_hot_ref,
         hot_sent_ref,
@@ -495,30 +540,34 @@
         slot_ref,
         recv_ref,
         share_ref,
+        agg_grad_ref,
         edge_grad_ref,
-    ) = refs[regions:]
-    latent = first_ref.shape[1]
-    mesh_count = first_ref.shape[0] // regions
+    ) = refs
+    latent = normed_ref.shape[1]
+    mesh_count = normed_ref.shape[0] // regions
+    count = turned_hot_ref.shape[1]
     slots = regions * mesh_cap
     me = lax.axis_index("space")
-    for step, cotangent_ref in zip(steps, cotangent_refs):
-        region = lax.bitwise_xor(me, step)
-        at = pl.ds(pl.multiple_of(region * mesh_count, mesh_count), mesh_count)
-        upstream_ref[at, :] = cotangent_ref[0].astype(F32)
-    agg_grad = moments_back(normed_ref[...], scaled_ref[:, 0:1], upstream_ref[...]).astype(BF16)
-    all_sums = edge_backward(
-        regions, agg_grad, hot_ref, turned_hot_ref, slope_ref, edge_grad_ref
-    )
-    for d, sums in enumerate(all_sums):
+    far_regions, all_sums = process_back_part(
+        far, mesh_count, cotangent_refs[len(near) :], hot_ref, turned_hot_ref, slope_ref,
+        normed_ref, scaled_ref, agg_grad_ref, edge_grad_ref,
+    )
+    near_regions = [lax.bitwise_xor(me, step) for step in near]
+    near_sums = [near_sums_ref[n * count : (n + 1) * count, :] for n in range(len(near))]
+    for region, sums in zip(near_regions + far_regions, near_sums + all_sums):
         for s in range(regions):
-            first = s * slots + d * mesh_cap
-            slot_ref[first : first + mesh_cap, :] = sums[s * mesh_cap : (s + 1) * mesh_cap]
-        recv_ref[d * mesh_count : (d + 1) * mesh_count, :] = sums[slots:].astype(BF16)
+            slot_ref[pl.ds(pl.multiple_of(s * slots + region * mesh_cap, mesh_cap), mesh_cap), :] = (
+                sums[s * mesh_cap : (s + 1) * mesh_cap]
+            )
+        recv_ref[pl.ds(pl.multiple_of(region * mesh_count, mesh_count), mesh_count), :] = sums[
+            slots:
+        ].astype(BF16)
+    for region, cotangent_ref in zip(near_regions + far_regions, cotangent_refs):
+        rows = pl.ds(pl.multiple_of(region * mesh_count, mesh_count), mesh_count)
+        upstream_ref[rows, :] = cotangent_ref[0].astype(F32)
     slot_sum = slot_ref[...].astype(BF16)
-    columns = share_ref.shape[0]
-    mine = pl.ds(pl.multiple_of(me * columns, columns), columns)
-    share_ref[:, :latent] = dot_first(sent_ref[:, mine], slot_sum).astype(BF16)
-    share_ref[:, latent:] = dot_first(first_ref[:, mine], recv_ref[...]).astype(BF16)
+    share_ref[:, :latent] = dot(sent_columns_ref[...], slot_sum).astype(BF16)
+    share_ref[:, latent:] = dot(first_columns_ref[...], recv_ref[...]).astype(BF16)
     halve(share_ref, keep_ref, give_ref)
     returned = dot(slot_sum, turned_ref[:, latent : 2 * latent]).astype(BF16)
     grad = upstream_ref[...] + dot(recv_ref[...], turned_ref[:, 2 * latent :])
@@ -531,8 +580,8 @@
 
 def encode_back_kernel(
     regions,
-    grid_ref,
-    mesh_ref,
+    grid_columns_ref,
+    mesh_columns_ref,
     hot_ref,
     turned_hot_ref,
     slope_ref,
@@ -545,19 +594,22 @@
     slot_ref,
     recv_ref,
     share_ref,
+    agg_grad_ref,
     edge_grad_ref,
 ):
-    latent = mesh_ref.shape[1]
-    mesh_count = mesh_ref.shape[0] // regions
-    listed = grid_ref.shape[0] // regions
+    latent = normed_ref.shape[1]
+    mesh_count = normed_ref.shape[0] // regions
+    listed = slot_ref.shape[0] // regions
     capacity = listed // 3
     me = lax.axis_index("space")
-    agg_grad = moments_back(normed_ref[...], scaled_ref[:, 0:1], mesh_grad_ref[...]).astype(BF16)
+    agg_grad_ref[...] = moments_back(
+        normed_ref[...], scaled_ref[:, 0:1], mesh_grad_ref[...]
+    ).astype(BF16)
     blank = jnp.zeros((capacity, latent), BF16)
     slot_ref[0:capacity, :] = blank
     slot_ref[regions * listed - capacity :, :] = blank
     all_sums = edge_backward(
-        regions, agg_grad, hot_ref, turned_hot_ref, slope_ref, edge_grad_ref
+        range(regions), agg_grad_ref, hot_ref, turned_hot_ref, slope_ref, edge_grad_ref
     )
     for d, sums in enumerate(all_sums):
         sums = sums.astype(BF16)
@@ -567,10 +619,8 @@
                 first = source * listed + (2 - j) * capacity
                 slot_ref[first : first + capacity, :] = sums[j * capacity : (j + 1) * capacity]
         recv_ref[d * mesh_count : (d + 1) * mesh_count, :] = sums[listed:]
-    columns = share_ref.shape[0]
-    mine = pl.ds(pl.multiple_of(me * columns, columns), columns)
-    share_ref[:, :latent] = dot_first(grid_ref[:, mine], slot_ref[...]).astype(BF16)
-    share_ref[:, latent:] = dot_first(mesh_ref[:, mine], recv_ref[...]).astype(BF16)
+    share_ref[:, :latent] = dot(grid_columns_ref[...], slot_ref[...]).astype(BF16)
+    share_ref[:, latent:] = dot(mesh_columns_ref[...], recv_ref[...]).astype(BF16)
     halve(share_ref, keep_ref, give_ref)
     own = pl.ds(pl.multiple_of(me * listed, listed), listed)
     own_slot_ref[...] = slot_ref[own, :]
@@ -761,13 +811,41 @@
         ],
         2 * 10**9,
     )
+    by_step = dict(zip(steps, cotangents))
+    near, far = (0, 1), tuple(step for step in steps if step > 1)
+    count = slots + mesh_count
+    near_sums, grid_columns, mesh_columns, sent_columns, first_columns = call(
+        functools.partial(near_back_kernel, near),
+        (
+            *(by_step[step] for step in near),
+            hot_two,
+            turned_two,
+            slope_two,
+            normed_two,
+            scaled_two,
+            grid_all,
+            mesh_all,
+            mesh_sent,
+            mesh_first,
+        ),
+        [
+            ((len(near) * count, latent), F32),
+            ((columns, regions * listed), BF16),
+            ((columns, rows), BF16),
+            ((columns, regions * slots), BF16),
+            ((columns, rows), BF16),
+        ],
+        [((len(near) * mesh_count, latent), BF16), ((len(near) * edges, latent), BF16)],
+        10**9,
+    )
     mesh_grad, keep_two, give_two = call(
-        functools.partial(process_back_kernel, steps, mesh_cap),
+        functools.partial(far_back_kernel, near, far, mesh_cap),
         (
-            *cotangents,
+            *(by_step[step] for step in near + far),
             turned,
-            mesh_first,
-            mesh_sent,
+            first_columns,
+            sent_columns,
+            near_sums,
             hot_two,
             turned_two,
             hot_sent,
@@ -781,15 +859,16 @@
             ((regions * slots, latent), F32),
             ((rows, latent), BF16),
             ((columns, 2 * latent), BF16),
-            ((regions * edges, latent), BF16),
+            ((len(far) * mesh_count, latent), BF16),
+            ((len(far) * edges, latent), BF16),
         ],
         10**9,
     )
     own_slots, keep_one, give_one = call(
         functools.partial(encode_back_kernel, regions),
         (
-            grid_all,
-            mesh_all,
+            grid_columns,
+            mesh_columns,
             hot_one,
             turned_one,
             slope_one,
@@ -802,6 +881,7 @@
             ((regions * listed, latent), BF16),
             ((rows, latent), BF16),
             ((columns, 2 * latent), BF16),
+            ((rows, latent), BF16),
             ((regions * edges, latent), BF16),
         ],
         10**9,
@@ -850,7 +930,7 @@
         edges = arguments[5].shape[0] + arguments[8].shape[0]
         latent = arguments[3].shape[0]
         fits = edges * latent * 4 <= SAMPLE_EDGE_BYTES and latent % (128 * regions) == 0
-        paired = all(n > 1 and n & (n - 1) == 0 for n in (regions, samples))
+        paired = regions > 2 and samples > 1 and not (regions & (regions - 1) | samples & (samples - 1))
         return sharded(whole_sample_body if fits and paired else partitioned_body)(*arguments)
 
     def sharded(body):

time: 37.5 us -> 37 us (0.987)
  waiting for transfers between devices: 10.1 us -> 9.4 us
    ppermute x12, waiting for transfers between devices: 10.1 us -> 9.4 us  [swap(): lax.ppermute(block, axis, [(i, i ^ bits) for i in range(lax.axis_size(axi...]
    pallas_call x6 -> x7, Pallas kernels: 11.1 us -> 11.3 us  [call(): pl.pallas_call(kernel, out_shape=[jax.ShapeDtypeStruct(shape, kind) for s...]
  transfers between devices with their start and end apart: 12 -> 12, of which waited for: 5 -> 5; matrix products, arithmetic and copies ran while one was open for 0% -> 0% of each run, Pallas kernels for 25% -> 27%
where the time goes in v17:
time: 37 us; the launch traced here: 36.9 us
  starting transfers between devices  13.6 us (37%)
  Pallas kernels  13 us (35%)
  waiting for transfers between devices  9.4 us (25%)
  between operations  0.74 us (2%)
    ppermute x12, starting transfers between devices, swap(): lax.ppermute(block, axis, [(i, i ^ bits) for i in range(lax.axis_size(axi...  13.6 us
    pallas_call x7, Pallas kernels, call(): pl.pallas_call(kernel, out_shape=[jax.ShapeDtypeStruct(shape, kind) for s...  11.3 us
    ppermute x12, waiting for transfers between devices, swap(): lax.ppermute(block, axis, [(i, i ^ bits) for i in range(lax.axis_size(axi...  9.4 us
    pallas_call x1, Pallas kernels, whole_sample_body(): pl.pallas_call(settle_kernel, out_shape=weight_shape, in_specs=[VMEM] * 3...  0.92 us
  transfers between devices with their start and end apart: 12, of which 5 were waited for; matrix products, arithmetic and copies ran while one was open for 0% of the time, Pallas kernels for 27%

profile of v17, /device:TPU:0, one launch (start us, length us, event | category | flops | bytes accessed | tf_op | source)
XLA Modules:
  0.0 36.9 jit_solution(5439655699595640965)
XLA Ops:
  0.6 0.0 copy-start
  0.6 1.2 %shard_map.121.refs_0_ = bf16[120,512]{1,0:T(8,128)(2,1)S(1)} custom-call(bf16[1,128,512]{2,1,0:T(8,128)(2,1)} %refs_0_.1, bf16[1,64,512]{2,1,0:T(8,128)(2,1)} %refs_1_.1, s32[3,1,16]{2,1,0:T(1,128)} %bitcast.5, s32[1,256]{1,0:T(1,128)} %bitcast.7, s32[1,256]{1,0:T(1,128)} %bitcast.8, s32[1,4,8]{2,1,0:T(4,128)} %refs_5_.1, s32[1,256]{1,0:T(1,128)} %bitcast.9, ...), custom_call_target="tpu_custom_call" | custom-call | flops 10000000 | bytes 4194304 | tf_op jit(solution)/shard_map/pallas_call | solution.py:686
  1.9 4.1 %collective-permute-start = (bf16[120,512]{1,0:T(8,128)(2,1)S(1)}, bf16[120,512]{1,0:T(8,128)(2,1)S(1)}, u32[]{:S(2)}, u32[]{:S(2)}) collective-permute-start(bf16[120,512]{1,0:T(8,128)(2,1)S(1)} %shard_map.121.refs_0_), channel_id=1, source_target_pairs={{0,8},{4,12},{8,0},{12,4},{1,9},{5,13},{9,1},{13,5},{2,10},{6,14},... | collective-permute-start | bytes 368648 | tf_op jit(solution)/shard_map/ppermute | solution.py:699
  6.0 1.3 %collective-permute-start.1 = (bf16[120,512]{1,0:T(8,128)(2,1)S(1)}, bf16[120,512]{1,0:T(8,128)(2,1)S(1)}, u32[]{:S(2)}, u32[]{:S(2)}) collective-permute-start(bf16[120,512]{1,0:T(8,128)(2,1)S(1)} %shard_map.121.refs_0_), channel_id=1, source_target_pairs={{0,12},{4,8},{8,4},{12,0},{1,13},{5,9},{9,5},{13,1},{2,14},{6,10},... | collective-permute-start | bytes 368648 | tf_op jit(solution)/shard_map/ppermute | solution.py:699
  7.3 0.2 collective-permute-start.2
  7.6 1.8 %collective-permute-start.3 = (bf16[1,64,512]{2,1,0:T(8,128)(2,1)}, bf16[1,64,512]{2,1,0:T(8,128)(2,1)S(1)}, u32[]{:S(2)}, u32[]{:S(2)}) collective-permute-start(bf16[1,64,512]{2,1,0:T(8,128)(2,1)} %refs_0_.3), channel_id=1, source_target_pairs={{0,4},{4,0},{8,12},{12,8},{1,5},{5,1},{9,13},{13,9},{2,6},{6,2},{1... | collective-permute-start | bytes 196616 | tf_op jit(solution)/shard_map/ppermute | solution.py:699
  9.4 2.1 %shard_map.122 = (bf16[512,2048]{1,0:T(8,128)(2,1)S(1)}, bf16[512,1536]{1,0:T(8,128)(2,1)S(1)}) custom-call(bf16[512,2048]{1,0:T(8,128)(2,1)} %source_ref), custom_call_target="tpu_custom_call" | custom-call | flops 100000000 | bytes 4194304 | tf_op jit(solution)/shard_map/pallas_call | solution.py:686
  11.4 4.0 %collective-permute-done.refs_1_ = bf16[120,512]{1,0:T(8,128)(2,1)S(1)} collective-permute-done((bf16[120,512]{1,0:T(8,128)(2,1)S(1)}, bf16[120,512]{1,0:T(8,128)(2,1)S(1)}, u32[]{:S(2)}, u32[]{:S(2)}) %collective-permute-start) | collective-permute-done | bytes 122912 | tf_op jit(solution)/shard_map/ppermute | solution.py:699
  15.5 0.0 collective-permute-start.4
  15.5 2.8 %collective-permute-start.5 = (bf16[1,64,512]{2,1,0:T(8,128)(2,1)S(1)}, bf16[1,64,512]{2,1,0:T(8,128)(2,1)S(1)}, u32[]{:S(2)}, u32[]{:S(2)}) collective-permute-start(bf16[1,64,512]{2,1,0:T(8,128)(2,1)S(1)} %copy-done), channel_id=1, source_target_pairs={{0,12},{4,8},{8,4},{12,0},{1,13},{5,9},{9,5},{13,1},{2,14},{6,10},... | collective-permute-start | bytes 196616 | tf_op jit(solution)/shard_map/ppermute | solution.py:699
  18.3 0.0 collective-permute-done.2.refs_3_
  18.3 3.8 %shard_map.123 = (bf16[1,64,512]{2,1,0:T(8,128)(2,1)}, bf16[192,512]{1,0:T(8,128)(2,1)S(1)}, bf16[256,512]{1,0:T(8,128)(2,1)S(1)}, bf16[256,512]{1,0:T(8,128)(2,...) custom-call(bf16[120,512]{1,0:T(8,128)(2,1)S(1)} %shard_map.121.refs, ...), custom_call_target="tpu_custom_call" | custom-call | flops 2000000000 | bytes 4194304 | tf_op jit(solution)/shard_map/pallas_call | solution.py:686
  22.1 0.0 collective-permute-done.3.refs_1_
  22.1 0.7 %shard_map.124 = (f32[192,512]{1,0:T(8,128)S(1)}, bf16[128,192]{1,0:T(8,128)(2,1)S(1)}, bf16[128,256]{1,0:T(8,128)(2,1)S(1)}, bf16[128,128]{1,0:T(8,128)(2,1)S(1)}, bf16[128,256]{1,0:T(8,128)(2,1)S(1)}) custom-call(bf16[1,64,512]{2,1,0:T(8,128)(2,1)S(1)} %copy-done, bf16[1,64,512]{2,1,0:T(8,128)(2,1)S(1)} %collective-permute-done.3.refs_1_, ...), custom_call_target="tpu_custom_call" | custom-call | flops 1000000000 | bytes 4194304 | tf_op jit(solution)/shard_map/pallas_call | solution.py:686
  22.7 0.5 %collective-permute-done.4.refs_2_ = bf16[1,64,512]{2,1,0:T(8,128)(2,1)S(1)} collective-permute-done((bf16[1,64,512]{2,1,0:T(8,128)(2,1)S(1)}, bf16[1,64,512]{2,1,0:T(8,128)(2,1)S(1)}, u32[]{:S(2)}, u32[]{:S(2)}) %collective-permute-start.4) | collective-permute-done | bytes 65568 | tf_op jit(solution)/shard_map/ppermute | solution.py:699
  23.2 0.0 collective-permute-done.5.refs_3_
  23.2 1.2 %shard_map.125 = (f32[256,512]{1,0:T(8,128)S(1)}, bf16[64,1024]{1,0:T(8,128)(2,1)S(1)}, bf16[64,1024]{1,0:T(8,128)(2,1)S(1)}) custom-call(bf16[1,64,512]{2,1,0:T(8,128)(2,1)S(1)} %copy-done, bf16[1,64,512]{2,1,0:T(8,128)(2,1)S(1)} %collective-permute-done.3.refs_1_, bf16[1,64,512]{2,1,0:T(8,128)(2,1)S(1)} %collective-permute-done.4.refs_2_, ...), custom_call_target="tpu_custom_call" | custom-call | flops 1000000000 | bytes 4194304 | tf_op jit(solution)/shard_map/pallas_call | solution.py:686
  24.4 0.1 collective-permute-start.9
  24.5 0.0 copy-start.1
  24.5 1.3 %shard_map.126 = (bf16[48,512]{1,0:T(8,128)(2,1)S(1)}, bf16[64,1024]{1,0:T(8,128)(2,1)S(1)}, bf16[64,1024]{1,0:T(8,128)(2,1)S(1)}) custom-call(bf16[128,192]{1,0:T(8,128)(2,1)S(1)} %get-tuple-element.57.grid_columns_ref, bf16[128,256]{1,0:T(8,128)(2,1)S(1)} %get-tuple-element.58.mesh_columns_ref, bf16[448,256]{1,0:T(8,128)(2,1)S(1)} %get-tuple-element.59.hot_ref, ...), custom_call_target="tpu_custom_call" | custom-call | flops 1000000000 | bytes 4194304 | tf_op jit(solution)/shard_map/pallas_call | solution.py:686
  25.8 0.5 %collective-permute-start.6 = (bf16[64,1024]{1,0:T(8,128)(2,1)S(1)}, bf16[64,1024]{1,0:T(8,128)(2,1)S(1)}, u32[]{:S(2)}, u32[]{:S(2)}) collective-permute-start(bf16[64,1024]{1,0:T(8,128)(2,1)S(1)} %get-tuple-element.71), channel_id=1, source_target_pairs={{0,1},{1,0},{2,3},{3,2},{4,5},{5,4},{6,7},{7,6},{8,9},{9,8},{10,11... | collective-permute-start | bytes 393224 | tf_op jit(solution)/shard_map/ppermute | solution.py:699
  26.4 1.6 %collective-permute-start.10 = (bf16[64,1024]{1,0:T(8,128)(2,1)S(1)}, bf16[64,1024]{1,0:T(8,128)(2,1)S(1)}, u32[]{:S(2)}, u32[]{:S(2)}) collective-permute-start(bf16[64,1024]{1,0:T(8,128)(2,1)S(1)} %add_convert_fusion.1), channel_id=1, source_target_pairs={{0,2},{1,3},{2,0},{3,1},{4,6},{5,7},{6,4},{7,5},{8,10},{9,11},{10,... | collective-permute-start | bytes 393224 | tf_op jit(solution)/shard_map/ppermute | solution.py:699
  28.0 1.0 %collective-permute-start.7 = (bf16[64,1024]{1,0:T(8,128)(2,1)S(1)}, bf16[64,1024]{1,0:T(8,128)(2,1)S(1)}, u32[]{:S(2)}, u32[]{:S(2)}) collective-permute-start(bf16[64,1024]{1,0:T(8,128)(2,1)S(1)} %add_convert_fusion.3), channel_id=1, source_target_pairs={{0,2},{1,3},{2,0},{3,1},{4,6},{5,7},{6,4},{7,5},{8,10},{9,11},{10,... | collective-permute-start | bytes 393224 | tf_op jit(solution)/shard_map/ppermute | solution.py:699
  29.0 1.1 %shard_map.127 = bf16[1,128,512]{2,1,0:T(8,128)(2,1)} custom-call(bf16[512,1536]{1,0:T(8,128)(2,1)S(1)} %get-tuple-element.64.refs_4_.turned_ref, s32[3,1,16]{2,1,0:T(1,128)S(1)} %bitcast.6, bf16[48,512]{1,0:T(8,128)(2,1)S(1)} %get-tuple-element.74.own_slot_ref), custom_call_target="tpu_custom_call" | custom-call | flops 100000000 | bytes 4194304 | tf_op jit(solution)/shard_map/pallas_call | solution.py:686
  30.1 2.7 %collective-permute-done.10 = bf16[64,1024]{1,0:T(8,128)(2,1)S(1)} collective-permute-done((bf16[64,1024]{1,0:T(8,128)(2,1)S(1)}, bf16[64,1024]{1,0:T(8,128)(2,1)S(1)}, u32[]{:S(2)}, u32[]{:S(2)}) %collective-permute-start.10) | collective-permute-done | bytes 131104 | tf_op jit(solution)/shard_map/ppermute | solution.py:699
  32.9 0.1 collective-permute-start.11
  32.9 1.8 %collective-permute-done.7 = bf16[64,1024]{1,0:T(8,128)(2,1)S(1)} collective-permute-done((bf16[64,1024]{1,0:T(8,128)(2,1)S(1)}, bf16[64,1024]{1,0:T(8,128)(2,1)S(1)}, u32[]{:S(2)}, u32[]{:S(2)}) %collective-permute-start.7) | collective-permute-done | bytes 131104 | tf_op jit(solution)/shard_map/ppermute | solution.py:699
  34.7 0.1 collective-permute-start.8
  34.8 0.0 collective-permute-done.11.other_two_ref
  34.8 0.9 %shard_map.128.settled_ref = f32[128,2048]{1,0:T(8,128)} custom-call(bf16[64,1024]{1,0:T(8,128)(2,1)S(1)} %add_convert_fusion.2.one_ref, bf16[64,1024]{1,0:T(8,128)(2,1)S(1)} %add_convert_fusion.two_ref, bf16[64,1024]{1,0:T(8,128)(2,1)S(1)} %collective-permute-done.11.other_two_ref), custom_call_target="tpu_custom_call" | custom-call | tf_op jit(solution)/shard_map/pallas_call | solution.py:905
  35.8 0.4 %collective-permute-done.8.other_one_ref = bf16[64,1024]{1,0:T(8,128)(2,1)S(1)} collective-permute-done((bf16[64,1024]{1,0:T(8,128)(2,1)S(1)}, bf16[64,1024]{1,0:T(8,128)(2,1)S(1)}, u32[]{:S(2)}, u32[]{:S(2)}) %collective-permute-start.8) | collective-permute-done | bytes 131104 | tf_op jit(solution)/shard_map/ppermute | solution.py:699
  36.1 0.7 %shard_map.129 = f32[128,2048]{1,0:T(8,128)} custom-call(bf16[64,1024]{1,0:T(8,128)(2,1)S(1)} %collective-permute-done.8.other_one_ref, f32[128,2048]{1,0:T(8,128)} %shard_map.128.settled_ref), custom_call_target="tpu_custom_call", output_to_operand_aliasing={{}: (1, {})} | custom-call | tf_op jit(solution)/shard_map/pallas_call | solution.py:913
  (9 shorter events, 0.2 us)
Async XLA Ops:
  0.6 14.8 %copy-start = (bf16[1,64,512]{2,1,0:T(8,128)(2,1)S(1)}, bf16[1,64,512]{2,1,0:T(8,128)(2,1)}, u32[]{:S(2)}) copy-start(bf16[1,64,512]{2,1,0:T(8,128)(2,1)} %refs_0_.3) | copy-start | bytes 196612
  1.9 13.6 %collective-permute-start = (bf16[120,512]{1,0:T(8,128)(2,1)S(1)}, bf16[120,512]{1,0:T(8,128)(2,1)S(1)}, u32[]{:S(2)}, u32[]{:S(2)}) collective-permute-start(bf16[120,512]{1,0:T(8,128)(2,1)S(1)} %shard_map.121.refs_0_), channel_id=1, source_target_pairs={{0,8},{4,12},{8,0},{12,4},{1,9},{5,13},{9,1},{13,5},{2,10},{6,14},... | collective-permute-start | bytes 368648 | tf_op jit(solution)/shard_map/ppermute | solution.py:699
  6.0 12.3 %collective-permute-start.1 = (bf16[120,512]{1,0:T(8,128)(2,1)S(1)}, bf16[120,512]{1,0:T(8,128)(2,1)S(1)}, u32[]{:S(2)}, u32[]{:S(2)}) collective-permute-start(bf16[120,512]{1,0:T(8,128)(2,1)S(1)} %shard_map.121.refs_0_), channel_id=1, source_target_pairs={{0,12},{4,8},{8,4},{12,0},{1,13},{5,9},{9,5},{13,1},{2,14},{6,10},... | collective-permute-start | bytes 368648 | tf_op jit(solution)/shard_map/ppermute | solution.py:699
  7.3 10.9 %collective-permute-start.2 = (bf16[120,512]{1,0:T(8,128)(2,1)S(1)}, bf16[120,512]{1,0:T(8,128)(2,1)S(1)}, u32[]{:S(2)}, u32[]{:S(2)}) collective-permute-start(bf16[120,512]{1,0:T(8,128)(2,1)S(1)} %shard_map.121.refs_0_), channel_id=1, source_target_pairs={{0,4},{4,0},{8,12},{12,8},{1,5},{5,1},{9,13},{13,9},{2,6},{6,2},{1... | collective-permute-start | bytes 368648 | tf_op jit(solution)/shard_map/ppermute | solution.py:699
  7.6 14.5 %collective-permute-start.3 = (bf16[1,64,512]{2,1,0:T(8,128)(2,1)}, bf16[1,64,512]{2,1,0:T(8,128)(2,1)S(1)}, u32[]{:S(2)}, u32[]{:S(2)}) collective-permute-start(bf16[1,64,512]{2,1,0:T(8,128)(2,1)} %refs_0_.3), channel_id=1, source_target_pairs={{0,4},{4,0},{8,12},{12,8},{1,5},{5,1},{9,13},{13,9},{2,6},{6,2},{1... | collective-permute-start | bytes 196616 | tf_op jit(solution)/shard_map/ppermute | solution.py:699
  15.5 7.7 %collective-permute-start.4 = (bf16[1,64,512]{2,1,0:T(8,128)(2,1)S(1)}, bf16[1,64,512]{2,1,0:T(8,128)(2,1)S(1)}, u32[]{:S(2)}, u32[]{:S(2)}) collective-permute-start(bf16[1,64,512]{2,1,0:T(8,128)(2,1)S(1)} %copy-done), channel_id=1, source_target_pairs={{0,8},{4,12},{8,0},{12,4},{1,9},{5,13},{9,1},{13,5},{2,10},{6,14},... | collective-permute-start | bytes 196616 | tf_op jit(solution)/shard_map/ppermute | solution.py:699
  15.5 7.7 %collective-permute-start.5 = (bf16[1,64,512]{2,1,0:T(8,128)(2,1)S(1)}, bf16[1,64,512]{2,1,0:T(8,128)(2,1)S(1)}, u32[]{:S(2)}, u32[]{:S(2)}) collective-permute-start(bf16[1,64,512]{2,1,0:T(8,128)(2,1)S(1)} %copy-done), channel_id=1, source_target_pairs={{0,12},{4,8},{8,4},{12,0},{1,13},{5,9},{9,5},{13,1},{2,14},{6,10},... | collective-permute-start | bytes 196616 | tf_op jit(solution)/shard_map/ppermute | solution.py:699
  24.4 1.9 %collective-permute-start.9 = (bf16[64,1024]{1,0:T(8,128)(2,1)S(1)}, bf16[64,1024]{1,0:T(8,128)(2,1)S(1)}, u32[]{:S(2)}, u32[]{:S(2)}) collective-permute-start(bf16[64,1024]{1,0:T(8,128)(2,1)S(1)} %get-tuple-element.78), channel_id=1, source_target_pairs={{0,1},{1,0},{2,3},{3,2},{4,5},{5,4},{6,7},{7,6},{8,9},{9,8},{10,11... | collective-permute-start | bytes 393224 | tf_op jit(solution)/shard_map/ppermute | solution.py:699
  24.5 4.5 %copy-start.1 = (s32[1,3,16]{2,0,1:T(1,128)S(1)}, s32[1,3,16]{2,0,1:T(1,128)}, u32[]{:S(2)}) copy-start(s32[1,3,16]{2,0,1:T(1,128)} %param.14) | copy-start | bytes 580
  25.8 2.2 %collective-permute-start.6 = (bf16[64,1024]{1,0:T(8,128)(2,1)S(1)}, bf16[64,1024]{1,0:T(8,128)(2,1)S(1)}, u32[]{:S(2)}, u32[]{:S(2)}) collective-permute-start(bf16[64,1024]{1,0:T(8,128)(2,1)S(1)} %get-tuple-element.71), channel_id=1, source_target_pairs={{0,1},{1,0},{2,3},{3,2},{4,5},{5,4},{6,7},{7,6},{8,9},{9,8},{10,11... | collective-permute-start | bytes 393224 | tf_op jit(solution)/shard_map/ppermute | solution.py:699
  26.4 6.4 %collective-permute-start.10 = (bf16[64,1024]{1,0:T(8,128)(2,1)S(1)}, bf16[64,1024]{1,0:T(8,128)(2,1)S(1)}, u32[]{:S(2)}, u32[]{:S(2)}) collective-permute-start(bf16[64,1024]{1,0:T(8,128)(2,1)S(1)} %add_convert_fusion.1), channel_id=1, source_target_pairs={{0,2},{1,3},{2,0},{3,1},{4,6},{5,7},{6,4},{7,5},{8,10},{9,11},{10,... | collective-permute-start | bytes 393224 | tf_op jit(solution)/shard_map/ppermute | solution.py:699
  28.0 6.7 %collective-permute-start.7 = (bf16[64,1024]{1,0:T(8,128)(2,1)S(1)}, bf16[64,1024]{1,0:T(8,128)(2,1)S(1)}, u32[]{:S(2)}, u32[]{:S(2)}) collective-permute-start(bf16[64,1024]{1,0:T(8,128)(2,1)S(1)} %add_convert_fusion.3), channel_id=1, source_target_pairs={{0,2},{1,3},{2,0},{3,1},{4,6},{5,7},{6,4},{7,5},{8,10},{9,11},{10,... | collective-permute-start | bytes 393224 | tf_op jit(solution)/shard_map/ppermute | solution.py:699
  32.9 2.0 %collective-permute-start.11 = (bf16[64,1024]{1,0:T(8,128)(2,1)S(1)}, bf16[64,1024]{1,0:T(8,128)(2,1)S(1)}, u32[]{:S(2)}, u32[]{:S(2)}) collective-permute-start(bf16[64,1024]{1,0:T(8,128)(2,1)S(1)} %add_convert_fusion.two_ref), channel_id=1, source_target_pairs={{0,1},{1,0},{2,3},{3,2},{4,5},{5,4},{6,7},{7,6},{8,9},{9,8},{10,11... | collective-permute-start | bytes 393224 | tf_op jit(solution)/shard_map/ppermute | solution.py:699
  34.7 1.4 %collective-permute-start.8 = (bf16[64,1024]{1,0:T(8,128)(2,1)S(1)}, bf16[64,1024]{1,0:T(8,128)(2,1)S(1)}, u32[]{:S(2)}, u32[]{:S(2)}) collective-permute-start(bf16[64,1024]{1,0:T(8,128)(2,1)S(1)} %add_convert_fusion.2.one_ref), channel_id=1, source_target_pairs={{0,1},{1,0},{2,3},{3,2},{4,5},{5,4},{6,7},{7,6},{8,9},{9,8},{10,11... | collective-permute-start | bytes 393224 | tf_op jit(solution)/shard_map/ppermute | solution.py:699

commit v18 on v17

--- a/solution.py
+++ b/solution.py
@@ -331,7 +331,6 @@
     packed_refs = refs[:regions]
     (
         weights_ref,
-        mesh_out_ref,
         grid_ref,
         mesh_ref,
         first_ref,
@@ -357,7 +356,7 @@
     slots = regions * mesh_cap
     me = lax.axis_index("space")
     for step, packed_ref in zip(steps, packed_refs):
-        region = lax.bitwise_xor(me, step)
+        region = lax.rem(me + (regions - step), regions)
         at = lambda rows: pl.ds(pl.multiple_of(region * rows, rows), rows)
         grid_ref[at(listed), :] = packed_ref[:listed, :]
         mesh_ref[at(mesh_count), :] = packed_ref[listed : listed + mesh_count, :]
@@ -439,8 +438,6 @@
     centred, scaled = row_moments(sum_ref[...])
     normed_two_ref[...] = centred * scaled
     scaled_two_ref[...] = jnp.broadcast_to(scaled, scaled_two_ref.shape)
-    own = pl.ds(pl.multiple_of(me * mesh_count, mesh_count), mesh_count)
-    mesh_out_ref[0] = (first_ref[own, :].astype(F32) + normed_two_ref[own, :]).astype(BF16)
 
 
 def edge_backward(regions, agg_grad_ref, hot_ref, turned_hot_ref, slope_ref, edge_grad_ref):
@@ -626,7 +623,13 @@
     own_slot_ref[...] = slot_ref[own, :]
 
 
-def grid_back_kernel(turned_ref, pick_ref, own_slot_ref, grid_grad_ref):
+def results_kernel(
+    turned_ref, pick_ref, own_slot_ref, first_ref, normed_ref, grid_grad_ref, mesh_out_ref
+):
+    mesh_count = mesh_out_ref.shape[1]
+    me = lax.axis_index("space")
+    own = pl.ds(pl.multiple_of(me * mesh_count, mesh_count), mesh_count)
+    mesh_out_ref[0] = (first_ref[own, :].astype(F32) + normed_ref[own, :]).astype(BF16)
     lists, _, capacity = pick_ref.shape
     latent = own_slot_ref.shape[1]
     returned = dot(own_slot_ref[...], turned_ref[:, :latent]).astype(BF16)
@@ -697,6 +700,11 @@
 
 def swap(block, axis, bits):
     return lax.ppermute(block, axis, [(i, i ^ bits) for i in range(lax.axis_size(axis))])
+
+
+def shifted(block, step):
+    count = lax.axis_size("space")
+    return lax.ppermute(block, "space", [(i, (i + step) % count) for i in range(count)])
 
 
 def added(left, right):
@@ -751,8 +759,9 @@
         fetched=len(sources),
     )[0]
     packed, cotangent, weights = lax.optimization_barrier((packed, mesh_cotangent, weights))
+    ring = (0, *sorted(range(1, regions), key=lambda step: -min(step, regions - step)))
+    packs = [packed] + [shifted(packed, step) for step in ring[1:]]
     steps = (0, *range(2, regions), 1)
-    packs = [packed] + [swap(packed, "space", step) for step in steps[1:]]
     near = swap(cotangent, "space", 1)
     weights, turned = call(
         weights_kernel,
@@ -767,7 +776,6 @@
     rows = regions * mesh_count
     slots = regions * mesh_cap
     (
-        mesh_out,
         grid_all,
         mesh_all,
         mesh_first,
@@ -784,10 +792,9 @@
         normed_two,
         scaled_two,
     ) = call(
-        functools.partial(forward_kernel, steps, listed, mesh_count, mesh_cap),
+        functools.partial(forward_kernel, ring, listed, mesh_count, mesh_cap),
         (*packs, weights),
         [
-            (mesh_latent.shape, BF16),
             ((regions * listed, latent), BF16),
             ((rows, latent), BF16),
             ((rows, latent), BF16),
@@ -889,13 +896,13 @@
     half_one = added(keep_one, swap(give_one, "rep", 1))
     half_two = added(keep_two, swap(give_two, "rep", 1))
     half_one, own_slots = lax.optimization_barrier((half_one, own_slots))
-    grid_grad = call(
-        grid_back_kernel,
-        (turned, g2m_pick, own_slots),
-        [(grid_latent.shape, BF16)],
+    grid_grad, mesh_out = call(
+        results_kernel,
+        (turned, g2m_pick, own_slots, mesh_first, normed_two),
+        [(grid_latent.shape, BF16), (mesh_latent.shape, BF16)],
         [],
         10**8,
-    )[0]
+    )
     two = summed_over_chips(half_two)
     one, grid_grad = lax.optimization_barrier((summed_over_chips(half_one), grid_grad))
     hbm = pl.BlockSpec(memory_space=pltpu.HBM)

time: 37 us -> 36.8 us (level)
  the two profiles are of different devices: /device:TPU:0 before, /device:TPU:19 now
where the time goes in v18:
time: 36.8 us; the launch traced here: 36.6 us
  starting transfers between devices  15.3 us (42%)
  Pallas kernels  12.3 us (33%)
  waiting for transfers between devices  8.04 us (22%)
  between operations  0.75 us (2%)
    ppermute x9, starting transfers between devices, swap(): lax.ppermute(block, axis, [(i, i ^ bits) for i in range(lax.axis_size(axi...  12.8 us
    pallas_call x7, Pallas kernels, call(): pl.pallas_call(kernel, out_shape=[jax.ShapeDtypeStruct(shape, kind) for s...  10.7 us
    ppermute x3, waiting for transfers between devices, shifted(): lax.ppermute(block, 'space', [(i, (i + step) % count) for i in range(coun...  4.63 us
    ppermute x9, waiting for transfers between devices, swap(): lax.ppermute(block, axis, [(i, i ^ bits) for i in range(lax.axis_size(axi...  3.41 us
    ppermute x3, starting transfers between devices, shifted(): lax.ppermute(block, 'space', [(i, (i + step) % count) for i in range(coun...  2.55 us
    pallas_call x1, Pallas kernels, whole_sample_body(): pl.pallas_call(settle_kernel, out_shape=weight_shape, in_specs=[VMEM] * 3...  0.92 us
  transfers between devices with their start and end apart: 12, of which 5 were waited for; matrix products, arithmetic and copies ran while one was open for 0% of the time, Pallas kernels for 25%

profile of v18, /device:TPU:19, one launch (start us, length us, event | category | flops | bytes accessed | tf_op | source)
XLA Modules:
  0.0 36.6 jit_solution(2085497218011672128)
XLA Ops:
  0.6 0.0 copy-start
  0.6 1.2 %shard_map.121.refs_0_ = bf16[120,512]{1,0:T(8,128)(2,1)S(1)} custom-call(bf16[1,128,512]{2,1,0:T(8,128)(2,1)} %refs_0_.1, bf16[1,64,512]{2,1,0:T(8,128)(2,1)} %refs_1_.1, s32[3,1,16]{2,1,0:T(1,128)} %bitcast.5, s32[1,256]{1,0:T(1,128)} %bitcast.7, s32[1,256]{1,0:T(1,128)} %bitcast.8, s32[1,4,8]{2,1,0:T(4,128)} %refs_5_.1, s32[1,256]{1,0:T(1,128)} %bitcast.9, ...), custom_call_target="tpu_custom_call" | custom-call | flops 10000000 | bytes 4194304 | tf_op jit(solution)/shard_map/pallas_call | solution.py:689
  1.9 0.1 collective-permute-start
  2.0 1.3 %collective-permute-start.2 = (bf16[120,512]{1,0:T(8,128)(2,1)S(1)}, bf16[120,512]{1,0:T(8,128)(2,1)S(1)}, u32[]{:S(2)}, u32[]{:S(2)}) collective-permute-start(bf16[120,512]{1,0:T(8,128)(2,1)S(1)} %shard_map.121.refs_0_), channel_id=1, source_target_pairs={{0,4},{4,8},{8,12},{12,0},{1,5},{5,9},{9,13},{13,1},{2,6},{6,10},{... | collective-permute-start | bytes 368648 | tf_op jit(solution)/shard_map/ppermute | solution.py:707
  3.3 1.1 %collective-permute-start.3 = (bf16[120,512]{1,0:T(8,128)(2,1)S(1)}, bf16[120,512]{1,0:T(8,128)(2,1)S(1)}, u32[]{:S(2)}, u32[]{:S(2)}) collective-permute-start(bf16[120,512]{1,0:T(8,128)(2,1)S(1)} %shard_map.121.refs_0_), channel_id=1, source_target_pairs={{0,12},{4,0},{8,4},{12,8},{1,13},{5,1},{9,5},{13,9},{2,14},{6,2},{... | collective-permute-start | bytes 368648 | tf_op jit(solution)/shard_map/ppermute | solution.py:707
  4.4 1.1 %collective-permute-start.1 = (bf16[1,64,512]{2,1,0:T(8,128)(2,1)}, bf16[1,64,512]{2,1,0:T(8,128)(2,1)S(1)}, u32[]{:S(2)}, u32[]{:S(2)}) collective-permute-start(bf16[1,64,512]{2,1,0:T(8,128)(2,1)} %refs_0_.3), channel_id=1, source_target_pairs={{0,4},{4,0},{8,12},{12,8},{1,5},{5,1},{9,13},{13,9},{2,6},{6,2},{1... | collective-permute-start | bytes 196616 | tf_op jit(solution)/shard_map/ppermute | solution.py:702
  5.5 2.1 %shard_map.122 = (bf16[512,2048]{1,0:T(8,128)(2,1)S(1)}, bf16[512,1536]{1,0:T(8,128)(2,1)S(1)}) custom-call(bf16[512,2048]{1,0:T(8,128)(2,1)} %source_ref), custom_call_target="tpu_custom_call" | custom-call | flops 100000000 | bytes 4194304 | tf_op jit(solution)/shard_map/pallas_call | solution.py:689
  7.6 0.0 collective-permute-done.refs_1_
  7.6 4.3 %collective-permute-start.4 = (bf16[1,64,512]{2,1,0:T(8,128)(2,1)S(1)}, bf16[1,64,512]{2,1,0:T(8,128)(2,1)S(1)}, u32[]{:S(2)}, u32[]{:S(2)}) collective-permute-start(bf16[1,64,512]{2,1,0:T(8,128)(2,1)S(1)} %copy-done), channel_id=1, source_target_pairs={{0,8},{4,12},{8,0},{12,4},{1,9},{5,13},{9,1},{13,5},{2,10},{6,14},... | collective-permute-start | bytes 196616 | tf_op jit(solution)/shard_map/ppermute | solution.py:702
  11.9 2.3 %collective-permute-start.5 = (bf16[1,64,512]{2,1,0:T(8,128)(2,1)S(1)}, bf16[1,64,512]{2,1,0:T(8,128)(2,1)S(1)}, u32[]{:S(2)}, u32[]{:S(2)}) collective-permute-start(bf16[1,64,512]{2,1,0:T(8,128)(2,1)S(1)} %copy-done), channel_id=1, source_target_pairs={{0,12},{4,8},{8,4},{12,0},{1,13},{5,9},{9,5},{13,1},{2,14},{6,10},... | collective-permute-start | bytes 196616 | tf_op jit(solution)/shard_map/ppermute | solution.py:702
  14.2 4.6 %collective-permute-done.2.refs_2_ = bf16[120,512]{1,0:T(8,128)(2,1)S(1)} collective-permute-done((bf16[120,512]{1,0:T(8,128)(2,1)S(1)}, bf16[120,512]{1,0:T(8,128)(2,1)S(1)}, u32[]{:S(2)}, u32[]{:S(2)}) %collective-permute-start.2) | collective-permute-done | bytes 122912 | tf_op jit(solution)/shard_map/ppermute | solution.py:707
  18.9 0.0 collective-permute-done.3.refs_3_
  18.9 3.1 %shard_map.123 = (bf16[192,512]{1,0:T(8,128)(2,1)S(1)}, bf16[256,512]{1,0:T(8,128)(2,1)S(1)}, bf16[256,512]{1,0:T(8,128)(2,1)S(1)}, bf16[128,512]{1,0:T(8,128)(2...) custom-call(bf16[120,512]{1,0:T(8,128)(2,1)S(1)} %shard_map.121.refs, ...), custom_call_target="tpu_custom_call" | custom-call | flops 2000000000 | bytes 4194304 | tf_op jit(solution)/shard_map/pallas_call | solution.py:689
  22.0 0.0 collective-permute-done.1.refs_1_
  22.0 0.7 %shard_map.124 = (f32[192,512]{1,0:T(8,128)S(1)}, bf16[128,192]{1,0:T(8,128)(2,1)S(1)}, bf16[128,256]{1,0:T(8,128)(2,1)S(1)}, bf16[128,128]{1,0:T(8,128)(2,1)S(1)}, bf16[128,256]{1,0:T(8,128)(2,1)S(1)}) custom-call(bf16[1,64,512]{2,1,0:T(8,128)(2,1)S(1)} %copy-done, bf16[1,64,512]{2,1,0:T(8,128)(2,1)S(1)} %collective-permute-done.1.refs_1_, ...), custom_call_target="tpu_custom_call" | custom-call | flops 1000000000 | bytes 4194304 | tf_op jit(solution)/shard_map/pallas_call | solution.py:689
  22.7 0.0 collective-permute-done.4.refs_2_
  22.7 0.0 collective-permute-done.5.refs_3_
  22.7 1.2 %shard_map.125 = (f32[256,512]{1,0:T(8,128)S(1)}, bf16[64,1024]{1,0:T(8,128)(2,1)S(1)}, bf16[64,1024]{1,0:T(8,128)(2,1)S(1)}) custom-call(bf16[1,64,512]{2,1,0:T(8,128)(2,1)S(1)} %copy-done, bf16[1,64,512]{2,1,0:T(8,128)(2,1)S(1)} %collective-permute-done.1.refs_1_, bf16[1,64,512]{2,1,0:T(8,128)(2,1)S(1)} %collective-permute-done.4.refs_2_, ...), custom_call_target="tpu_custom_call" | custom-call | flops 1000000000 | bytes 4194304 | tf_op jit(solution)/shard_map/pallas_call | solution.py:689
  23.9 0.7 %collective-permute-start.9 = (bf16[64,1024]{1,0:T(8,128)(2,1)S(1)}, bf16[64,1024]{1,0:T(8,128)(2,1)S(1)}, u32[]{:S(2)}, u32[]{:S(2)}) collective-permute-start(bf16[64,1024]{1,0:T(8,128)(2,1)S(1)} %get-tuple-element.80), channel_id=1, source_target_pairs={{0,1},{1,0},{2,3},{3,2},{4,5},{5,4},{6,7},{7,6},{8,9},{9,8},{10,11... | collective-permute-start | bytes 393224 | tf_op jit(solution)/shard_map/ppermute | solution.py:702
  24.6 1.3 %shard_map.126 = (bf16[48,512]{1,0:T(8,128)(2,1)S(1)}, bf16[64,1024]{1,0:T(8,128)(2,1)S(1)}, bf16[64,1024]{1,0:T(8,128)(2,1)S(1)}) custom-call(bf16[128,192]{1,0:T(8,128)(2,1)S(1)} %get-tuple-element.58.grid_columns_ref, bf16[128,256]{1,0:T(8,128)(2,1)S(1)} %get-tuple-element.59.mesh_columns_ref, bf16[448,256]{1,0:T(8,128)(2,1)S(1)} %get-tuple-element.60.hot_ref, ...), custom_call_target="tpu_custom_call" | custom-call | flops 1000000000 | bytes 4194304 | tf_op jit(solution)/shard_map/pallas_call | solution.py:689
  25.9 0.1 collective-permute-start.6
  26.0 0.3 collective-permute-start.10
  26.3 1.0 %collective-permute-done.6 = bf16[64,1024]{1,0:T(8,128)(2,1)S(1)} collective-permute-done((bf16[64,1024]{1,0:T(8,128)(2,1)S(1)}, bf16[64,1024]{1,0:T(8,128)(2,1)S(1)}, u32[]{:S(2)}, u32[]{:S(2)}) %collective-permute-start.6) | collective-permute-done | bytes 131104 | tf_op jit(solution)/shard_map/ppermute | solution.py:702
  27.3 0.3 collective-permute-start.7
  27.6 1.1 %shard_map.127 = (bf16[1,128,512]{2,1,0:T(8,128)(2,1)}, bf16[1,64,512]{2,1,0:T(8,128)(2,1)}) custom-call(bf16[512,1536]{1,0:T(8,128)(2,1)S(1)} %get-tuple-element.43.refs_4_.turned_ref, s32[3,1,16]{2,1,0:T(1,128)S(1)} %bitcast.6, bf16[48,512]{1,0:T(8,128)(2,1)S(1)} %get-tuple-element.73.own_slot_ref, ...), custom_call_target="tpu_custom_call" | custom-call | flops 100000000 | bytes 4194304 | tf_op jit(solution)/shard_map/pallas_call | solution.py:689
  28.7 1.9 %collective-permute-done.10 = bf16[64,1024]{1,0:T(8,128)(2,1)S(1)} collective-permute-done((bf16[64,1024]{1,0:T(8,128)(2,1)S(1)}, bf16[64,1024]{1,0:T(8,128)(2,1)S(1)}, u32[]{:S(2)}, u32[]{:S(2)}) %collective-permute-start.10) | collective-permute-done | bytes 131104 | tf_op jit(solution)/shard_map/ppermute | solution.py:702
  30.7 2.3 %collective-permute-start.11 = (bf16[64,1024]{1,0:T(8,128)(2,1)S(1)}, bf16[64,1024]{1,0:T(8,128)(2,1)S(1)}, u32[]{:S(2)}, u32[]{:S(2)}) collective-permute-start(bf16[64,1024]{1,0:T(8,128)(2,1)S(1)} %add_convert_fusion.two_ref), channel_id=1, source_target_pairs={{0,1},{1,0},{2,3},{3,2},{4,5},{5,4},{6,7},{7,6},{8,9},{9,8},{10,11... | collective-permute-start | bytes 393224 | tf_op jit(solution)/shard_map/ppermute | solution.py:702
  33.0 0.5 %collective-permute-done.7 = bf16[64,1024]{1,0:T(8,128)(2,1)S(1)} collective-permute-done((bf16[64,1024]{1,0:T(8,128)(2,1)S(1)}, bf16[64,1024]{1,0:T(8,128)(2,1)S(1)}, u32[]{:S(2)}, u32[]{:S(2)}) %collective-permute-start.7) | collective-permute-done | bytes 131104 | tf_op jit(solution)/shard_map/ppermute | solution.py:702
  33.5 1.4 %collective-permute-start.8 = (bf16[64,1024]{1,0:T(8,128)(2,1)S(1)}, bf16[64,1024]{1,0:T(8,128)(2,1)S(1)}, u32[]{:S(2)}, u32[]{:S(2)}) collective-permute-start(bf16[64,1024]{1,0:T(8,128)(2,1)S(1)} %add_convert_fusion.2.one_ref), channel_id=1, source_target_pairs={{0,1},{1,0},{2,3},{3,2},{4,5},{5,4},{6,7},{7,6},{8,9},{9,8},{10,11... | collective-permute-start | bytes 393224 | tf_op jit(solution)/shard_map/ppermute | solution.py:702
  34.9 0.9 %shard_map.128.settled_ref = f32[128,2048]{1,0:T(8,128)} custom-call(bf16[64,1024]{1,0:T(8,128)(2,1)S(1)} %add_convert_fusion.2.one_ref, bf16[64,1024]{1,0:T(8,128)(2,1)S(1)} %add_convert_fusion.two_ref, bf16[64,1024]{1,0:T(8,128)(2,1)S(1)} %collective-permute-done.11.other_two_ref), custom_call_target="tpu_custom_call" | custom-call | tf_op jit(solution)/shard_map/pallas_call | solution.py:912
  35.8 0.1 collective-permute-done.8.other_one_ref
  35.9 0.7 %shard_map.129 = f32[128,2048]{1,0:T(8,128)} custom-call(bf16[64,1024]{1,0:T(8,128)(2,1)S(1)} %collective-permute-done.8.other_one_ref, f32[128,2048]{1,0:T(8,128)} %shard_map.128.settled_ref), custom_call_target="tpu_custom_call", output_to_operand_aliasing={{}: (1, {})} | custom-call | tf_op jit(solution)/shard_map/pallas_call | solution.py:920
  (9 shorter events, 0.1 us)
Async XLA Ops:
  0.6 7.0 %copy-start = (bf16[1,64,512]{2,1,0:T(8,128)(2,1)S(1)}, bf16[1,64,512]{2,1,0:T(8,128)(2,1)}, u32[]{:S(2)}) copy-start(bf16[1,64,512]{2,1,0:T(8,128)(2,1)} %refs_0_.3) | copy-start | bytes 196612
  1.9 5.7 %collective-permute-start = (bf16[120,512]{1,0:T(8,128)(2,1)S(1)}, bf16[120,512]{1,0:T(8,128)(2,1)S(1)}, u32[]{:S(2)}, u32[]{:S(2)}) collective-permute-start(bf16[120,512]{1,0:T(8,128)(2,1)S(1)} %shard_map.121.refs_0_), channel_id=1, source_target_pairs={{0,8},{4,12},{8,0},{12,4},{1,9},{5,13},{9,1},{13,5},{2,10},{6,14},... | collective-permute-start | bytes 368648 | tf_op jit(solution)/shard_map/ppermute | solution.py:707
  2.0 16.8 %collective-permute-start.2 = (bf16[120,512]{1,0:T(8,128)(2,1)S(1)}, bf16[120,512]{1,0:T(8,128)(2,1)S(1)}, u32[]{:S(2)}, u32[]{:S(2)}) collective-permute-start(bf16[120,512]{1,0:T(8,128)(2,1)S(1)} %shard_map.121.refs_0_), channel_id=1, source_target_pairs={{0,4},{4,8},{8,12},{12,0},{1,5},{5,9},{9,13},{13,1},{2,6},{6,10},{... | collective-permute-start | bytes 368648 | tf_op jit(solution)/shard_map/ppermute | solution.py:707
  3.3 15.5 %collective-permute-start.3 = (bf16[120,512]{1,0:T(8,128)(2,1)S(1)}, bf16[120,512]{1,0:T(8,128)(2,1)S(1)}, u32[]{:S(2)}, u32[]{:S(2)}) collective-permute-start(bf16[120,512]{1,0:T(8,128)(2,1)S(1)} %shard_map.121.refs_0_), channel_id=1, source_target_pairs={{0,12},{4,0},{8,4},{12,8},{1,13},{5,1},{9,5},{13,9},{2,14},{6,2},{... | collective-permute-start | bytes 368648 | tf_op jit(solution)/shard_map/ppermute | solution.py:707
  4.4 17.5 %collective-permute-start.1 = (bf16[1,64,512]{2,1,0:T(8,128)(2,1)}, bf16[1,64,512]{2,1,0:T(8,128)(2,1)S(1)}, u32[]{:S(2)}, u32[]{:S(2)}) collective-permute-start(bf16[1,64,512]{2,1,0:T(8,128)(2,1)} %refs_0_.3), channel_id=1, source_target_pairs={{0,4},{4,0},{8,12},{12,8},{1,5},{5,1},{9,13},{13,9},{2,6},{6,2},{1... | collective-permute-start | bytes 196616 | tf_op jit(solution)/shard_map/ppermute | solution.py:702
  7.6 15.1 %collective-permute-start.4 = (bf16[1,64,512]{2,1,0:T(8,128)(2,1)S(1)}, bf16[1,64,512]{2,1,0:T(8,128)(2,1)S(1)}, u32[]{:S(2)}, u32[]{:S(2)}) collective-permute-start(bf16[1,64,512]{2,1,0:T(8,128)(2,1)S(1)} %copy-done), channel_id=1, source_target_pairs={{0,8},{4,12},{8,0},{12,4},{1,9},{5,13},{9,1},{13,5},{2,10},{6,14},... | collective-permute-start | bytes 196616 | tf_op jit(solution)/shard_map/ppermute | solution.py:702
  11.9 10.7 %collective-permute-start.5 = (bf16[1,64,512]{2,1,0:T(8,128)(2,1)S(1)}, bf16[1,64,512]{2,1,0:T(8,128)(2,1)S(1)}, u32[]{:S(2)}, u32[]{:S(2)}) collective-permute-start(bf16[1,64,512]{2,1,0:T(8,128)(2,1)S(1)} %copy-done), channel_id=1, source_target_pairs={{0,12},{4,8},{8,4},{12,0},{1,13},{5,9},{9,5},{13,1},{2,14},{6,10},... | collective-permute-start | bytes 196616 | tf_op jit(solution)/shard_map/ppermute | solution.py:702
  23.9 2.1 %collective-permute-start.9 = (bf16[64,1024]{1,0:T(8,128)(2,1)S(1)}, bf16[64,1024]{1,0:T(8,128)(2,1)S(1)}, u32[]{:S(2)}, u32[]{:S(2)}) collective-permute-start(bf16[64,1024]{1,0:T(8,128)(2,1)S(1)} %get-tuple-element.80), channel_id=1, source_target_pairs={{0,1},{1,0},{2,3},{3,2},{4,5},{5,4},{6,7},{7,6},{8,9},{9,8},{10,11... | collective-permute-start | bytes 393224 | tf_op jit(solution)/shard_map/ppermute | solution.py:702
  24.6 3.1 %copy-start.1 = (s32[1,3,16]{2,0,1:T(1,128)S(1)}, s32[1,3,16]{2,0,1:T(1,128)}, u32[]{:S(2)}) copy-start(s32[1,3,16]{2,0,1:T(1,128)} %param.14) | copy-start | bytes 580
  25.9 1.4 %collective-permute-start.6 = (bf16[64,1024]{1,0:T(8,128)(2,1)S(1)}, bf16[64,1024]{1,0:T(8,128)(2,1)S(1)}, u32[]{:S(2)}, u32[]{:S(2)}) collective-permute-start(bf16[64,1024]{1,0:T(8,128)(2,1)S(1)} %get-tuple-element.71), channel_id=1, source_target_pairs={{0,1},{1,0},{2,3},{3,2},{4,5},{5,4},{6,7},{7,6},{8,9},{9,8},{10,11... | collective-permute-start | bytes 393224 | tf_op jit(solution)/shard_map/ppermute | solution.py:702
  26.0 4.7 %collective-permute-start.10 = (bf16[64,1024]{1,0:T(8,128)(2,1)S(1)}, bf16[64,1024]{1,0:T(8,128)(2,1)S(1)}, u32[]{:S(2)}, u32[]{:S(2)}) collective-permute-start(bf16[64,1024]{1,0:T(8,128)(2,1)S(1)} %add_convert_fusion.1), channel_id=1, source_target_pairs={{0,2},{1,3},{2,0},{3,1},{4,6},{5,7},{6,4},{7,5},{8,10},{9,11},{10,... | collective-permute-start | bytes 393224 | tf_op jit(solution)/shard_map/ppermute | solution.py:702
  27.3 6.1 %collective-permute-start.7 = (bf16[64,1024]{1,0:T(8,128)(2,1)S(1)}, bf16[64,1024]{1,0:T(8,128)(2,1)S(1)}, u32[]{:S(2)}, u32[]{:S(2)}) collective-permute-start(bf16[64,1024]{1,0:T(8,128)(2,1)S(1)} %add_convert_fusion.3), channel_id=1, source_target_pairs={{0,2},{1,3},{2,0},{3,1},{4,6},{5,7},{6,4},{7,5},{8,10},{9,11},{10,... | collective-permute-start | bytes 393224 | tf_op jit(solution)/shard_map/ppermute | solution.py:702
  30.7 4.2 %collective-permute-start.11 = (bf16[64,1024]{1,0:T(8,128)(2,1)S(1)}, bf16[64,1024]{1,0:T(8,128)(2,1)S(1)}, u32[]{:S(2)}, u32[]{:S(2)}) collective-permute-start(bf16[64,1024]{1,0:T(8,128)(2,1)S(1)} %add_convert_fusion.two_ref), channel_id=1, source_target_pairs={{0,1},{1,0},{2,3},{3,2},{4,5},{5,4},{6,7},{7,6},{8,9},{9,8},{10,11... | collective-permute-start | bytes 393224 | tf_op jit(solution)/shard_map/ppermute | solution.py:702
  33.5 2.4 %collective-permute-start.8 = (bf16[64,1024]{1,0:T(8,128)(2,1)S(1)}, bf16[64,1024]{1,0:T(8,128)(2,1)S(1)}, u32[]{:S(2)}, u32[]{:S(2)}) collective-permute-start(bf16[64,1024]{1,0:T(8,128)(2,1)S(1)} %add_convert_fusion.2.one_ref), channel_id=1, source_target_pairs={{0,1},{1,0},{2,3},{3,2},{4,5},{5,4},{6,7},{7,6},{8,9},{9,8},{10,11... | collective-permute-start | bytes 393224 | tf_op jit(solution)/shard_map/ppermute | solution.py:702

commit v19 on v18

--- a/solution.py
+++ b/solution.py
@@ -356,7 +356,7 @@
     slots = regions * mesh_cap
     me = lax.axis_index("space")
     for step, packed_ref in zip(steps, packed_refs):
-        region = lax.rem(me + (regions - step), regions)
+        region = lax.bitwise_xor(me, step)
         at = lambda rows: pl.ds(pl.multiple_of(region * rows, rows), rows)
         grid_ref[at(listed), :] = packed_ref[:listed, :]
         mesh_ref[at(mesh_count), :] = packed_ref[listed : listed + mesh_count, :]
@@ -702,11 +702,6 @@
     return lax.ppermute(block, axis, [(i, i ^ bits) for i in range(lax.axis_size(axis))])
 
 
-def shifted(block, step):
-    count = lax.axis_size("space")
-    return lax.ppermute(block, "space", [(i, (i + step) % count) for i in range(count)])
-
-
 def added(left, right):
     return (left.astype(F32) + right.astype(F32)).astype(BF16)
 
@@ -759,9 +754,8 @@
         fetched=len(sources),
     )[0]
     packed, cotangent, weights = lax.optimization_barrier((packed, mesh_cotangent, weights))
-    ring = (0, *sorted(range(1, regions), key=lambda step: -min(step, regions - step)))
-    packs = [packed] + [shifted(packed, step) for step in ring[1:]]
     steps = (0, *range(2, regions), 1)
+    packs = [packed] + [swap(packed, "space", step) for step in steps[1:]]
     near = swap(cotangent, "space", 1)
     weights, turned = call(
         weights_kernel,
@@ -792,7 +786,7 @@
         normed_two,
         scaled_two,
     ) = call(
-        functools.partial(forward_kernel, ring, listed, mesh_count, mesh_cap),
+        functools.partial(forward_kernel, steps, listed, mesh_count, mesh_cap),
         (*packs, weights),
         [
             ((regions * listed, latent), BF16),

time: 36.8 us -> 37 us (level)
  the two profiles are of different devices: /device:TPU:19 before, /device:TPU:0 now
where the time goes in v19:
time: 37 us; the launch traced here: 36.9 us
  starting transfers between devices  13.6 us (37%)
  Pallas kernels  12.3 us (33%)
  waiting for transfers between devices  10 us (27%)
  between operations  0.76 us (2%)
    ppermute x12, starting transfers between devices, swap(): lax.ppermute(block, axis, [(i, i ^ bits) for i in range(lax.axis_size(axi...  13.6 us
    pallas_call x7, Pallas kernels, call(): pl.pallas_call(kernel, out_shape=[jax.ShapeDtypeStruct(shape, kind) for s...  10.7 us
    ppermute x12, waiting for transfers between devices, swap(): lax.ppermute(block, axis, [(i, i ^ bits) for i in range(lax.axis_size(axi...  10 us
    pallas_call x1, Pallas kernels, whole_sample_body(): pl.pallas_call(settle_kernel, out_shape=weight_shape, in_specs=[VMEM] * 3...  0.92 us
  transfers between devices with their start and end apart: 12, of which 5 were waited for; matrix products, arithmetic and copies ran while one was open for 0% of the time, Pallas kernels for 25%

profile of v19, /device:TPU:0, one launch (start us, length us, event | category | flops | bytes accessed | tf_op | source)
XLA Modules:
  0.0 36.9 jit_solution(5273569803891294511)
XLA Ops:
  0.6 0.0 copy-start
  0.6 1.2 %shard_map.121.refs_0_ = bf16[120,512]{1,0:T(8,128)(2,1)S(1)} custom-call(bf16[1,128,512]{2,1,0:T(8,128)(2,1)} %refs_0_.1, bf16[1,64,512]{2,1,0:T(8,128)(2,1)} %refs_1_.1, s32[3,1,16]{2,1,0:T(1,128)} %bitcast.5, s32[1,256]{1,0:T(1,128)} %bitcast.7, s32[1,256]{1,0:T(1,128)} %bitcast.8, s32[1,4,8]{2,1,0:T(4,128)} %refs_5_.1, s32[1,256]{1,0:T(1,128)} %bitcast.9, ...), custom_call_target="tpu_custom_call" | custom-call | flops 10000000 | bytes 4194304 | tf_op jit(solution)/shard_map/pallas_call | solution.py:689
  1.9 4.1 %collective-permute-start = (bf16[120,512]{1,0:T(8,128)(2,1)S(1)}, bf16[120,512]{1,0:T(8,128)(2,1)S(1)}, u32[]{:S(2)}, u32[]{:S(2)}) collective-permute-start(bf16[120,512]{1,0:T(8,128)(2,1)S(1)} %shard_map.121.refs_0_), channel_id=1, source_target_pairs={{0,8},{4,12},{8,0},{12,4},{1,9},{5,13},{9,1},{13,5},{2,10},{6,14},... | collective-permute-start | bytes 368648 | tf_op jit(solution)/shard_map/ppermute | solution.py:702
  6.0 1.3 %collective-permute-start.2 = (bf16[120,512]{1,0:T(8,128)(2,1)S(1)}, bf16[120,512]{1,0:T(8,128)(2,1)S(1)}, u32[]{:S(2)}, u32[]{:S(2)}) collective-permute-start(bf16[120,512]{1,0:T(8,128)(2,1)S(1)} %shard_map.121.refs_0_), channel_id=1, source_target_pairs={{0,12},{4,8},{8,4},{12,0},{1,13},{5,9},{9,5},{13,1},{2,14},{6,10},... | collective-permute-start | bytes 368648 | tf_op jit(solution)/shard_map/ppermute | solution.py:702
  7.3 0.2 collective-permute-start.3
  7.6 1.8 %collective-permute-start.1 = (bf16[1,64,512]{2,1,0:T(8,128)(2,1)}, bf16[1,64,512]{2,1,0:T(8,128)(2,1)S(1)}, u32[]{:S(2)}, u32[]{:S(2)}) collective-permute-start(bf16[1,64,512]{2,1,0:T(8,128)(2,1)} %refs_0_.3), channel_id=1, source_target_pairs={{0,4},{4,0},{8,12},{12,8},{1,5},{5,1},{9,13},{13,9},{2,6},{6,2},{1... | collective-permute-start | bytes 196616 | tf_op jit(solution)/shard_map/ppermute | solution.py:702
  9.4 2.1 %shard_map.122 = (bf16[512,2048]{1,0:T(8,128)(2,1)S(1)}, bf16[512,1536]{1,0:T(8,128)(2,1)S(1)}) custom-call(bf16[512,2048]{1,0:T(8,128)(2,1)} %source_ref), custom_call_target="tpu_custom_call" | custom-call | flops 100000000 | bytes 4194304 | tf_op jit(solution)/shard_map/pallas_call | solution.py:689
  11.4 4.0 %collective-permute-done.refs_1_ = bf16[120,512]{1,0:T(8,128)(2,1)S(1)} collective-permute-done((bf16[120,512]{1,0:T(8,128)(2,1)S(1)}, bf16[120,512]{1,0:T(8,128)(2,1)S(1)}, u32[]{:S(2)}, u32[]{:S(2)}) %collective-permute-start) | collective-permute-done | bytes 122912 | tf_op jit(solution)/shard_map/ppermute | solution.py:702
  15.5 0.0 collective-permute-start.4
  15.5 2.8 %collective-permute-start.5 = (bf16[1,64,512]{2,1,0:T(8,128)(2,1)S(1)}, bf16[1,64,512]{2,1,0:T(8,128)(2,1)S(1)}, u32[]{:S(2)}, u32[]{:S(2)}) collective-permute-start(bf16[1,64,512]{2,1,0:T(8,128)(2,1)S(1)} %copy-done), channel_id=1, source_target_pairs={{0,12},{4,8},{8,4},{12,0},{1,13},{5,9},{9,5},{13,1},{2,14},{6,10},... | collective-permute-start | bytes 196616 | tf_op jit(solution)/shard_map/ppermute | solution.py:702
  18.3 0.0 collective-permute-done.2.refs_2_
  18.3 0.0 collective-permute-done.3.refs_3_
  18.3 3.1 %shard_map.123 = (bf16[192,512]{1,0:T(8,128)(2,1)S(1)}, bf16[256,512]{1,0:T(8,128)(2,1)S(1)}, bf16[256,512]{1,0:T(8,128)(2,1)S(1)}, bf16[128,512]{1,0:T(8,128)(2...) custom-call(bf16[120,512]{1,0:T(8,128)(2,1)S(1)} %shard_map.121.refs, ...), custom_call_target="tpu_custom_call" | custom-call | flops 2000000000 | bytes 4194304 | tf_op jit(solution)/shard_map/pallas_call | solution.py:689
  21.4 0.0 collective-permute-done.1.refs_1_
  21.4 0.7 %shard_map.124 = (f32[192,512]{1,0:T(8,128)S(1)}, bf16[128,192]{1,0:T(8,128)(2,1)S(1)}, bf16[128,256]{1,0:T(8,128)(2,1)S(1)}, bf16[128,128]{1,0:T(8,128)(2,1)S(1)}, bf16[128,256]{1,0:T(8,128)(2,1)S(1)}) custom-call(bf16[1,64,512]{2,1,0:T(8,128)(2,1)S(1)} %copy-done, bf16[1,64,512]{2,1,0:T(8,128)(2,1)S(1)} %collective-permute-done.1.refs_1_, ...), custom_call_target="tpu_custom_call" | custom-call | flops 1000000000 | bytes 4194304 | tf_op jit(solution)/shard_map/pallas_call | solution.py:689
  22.1 1.1 %collective-permute-done.4.refs_2_ = bf16[1,64,512]{2,1,0:T(8,128)(2,1)S(1)} collective-permute-done((bf16[1,64,512]{2,1,0:T(8,128)(2,1)S(1)}, bf16[1,64,512]{2,1,0:T(8,128)(2,1)S(1)}, u32[]{:S(2)}, u32[]{:S(2)}) %collective-permute-start.4) | collective-permute-done | bytes 65568 | tf_op jit(solution)/shard_map/ppermute | solution.py:702
  23.2 0.0 collective-permute-done.5.refs_3_
  23.2 1.2 %shard_map.125 = (f32[256,512]{1,0:T(8,128)S(1)}, bf16[64,1024]{1,0:T(8,128)(2,1)S(1)}, bf16[64,1024]{1,0:T(8,128)(2,1)S(1)}) custom-call(bf16[1,64,512]{2,1,0:T(8,128)(2,1)S(1)} %copy-done, bf16[1,64,512]{2,1,0:T(8,128)(2,1)S(1)} %collective-permute-done.1.refs_1_, bf16[1,64,512]{2,1,0:T(8,128)(2,1)S(1)} %collective-permute-done.4.refs_2_, ...), custom_call_target="tpu_custom_call" | custom-call | flops 1000000000 | bytes 4194304 | tf_op jit(solution)/shard_map/pallas_call | solution.py:689
  24.4 0.1 collective-permute-start.9
  24.5 0.0 copy-start.1
  24.5 1.3 %shard_map.126 = (bf16[48,512]{1,0:T(8,128)(2,1)S(1)}, bf16[64,1024]{1,0:T(8,128)(2,1)S(1)}, bf16[64,1024]{1,0:T(8,128)(2,1)S(1)}) custom-call(bf16[128,192]{1,0:T(8,128)(2,1)S(1)} %get-tuple-element.58.grid_columns_ref, bf16[128,256]{1,0:T(8,128)(2,1)S(1)} %get-tuple-element.59.mesh_columns_ref, bf16[448,256]{1,0:T(8,128)(2,1)S(1)} %get-tuple-element.60.hot_ref, ...), custom_call_target="tpu_custom_call" | custom-call | flops 1000000000 | bytes 4194304 | tf_op jit(solution)/shard_map/pallas_call | solution.py:689
  25.8 0.5 %collective-permute-start.6 = (bf16[64,1024]{1,0:T(8,128)(2,1)S(1)}, bf16[64,1024]{1,0:T(8,128)(2,1)S(1)}, u32[]{:S(2)}, u32[]{:S(2)}) collective-permute-start(bf16[64,1024]{1,0:T(8,128)(2,1)S(1)} %get-tuple-element.71), channel_id=1, source_target_pairs={{0,1},{1,0},{2,3},{3,2},{4,5},{5,4},{6,7},{7,6},{8,9},{9,8},{10,11... | collective-permute-start | bytes 393224 | tf_op jit(solution)/shard_map/ppermute | solution.py:702
  26.4 1.6 %collective-permute-start.10 = (bf16[64,1024]{1,0:T(8,128)(2,1)S(1)}, bf16[64,1024]{1,0:T(8,128)(2,1)S(1)}, u32[]{:S(2)}, u32[]{:S(2)}) collective-permute-start(bf16[64,1024]{1,0:T(8,128)(2,1)S(1)} %add_convert_fusion.1), channel_id=1, source_target_pairs={{0,2},{1,3},{2,0},{3,1},{4,6},{5,7},{6,4},{7,5},{8,10},{9,11},{10,... | collective-permute-start | bytes 393224 | tf_op jit(solution)/shard_map/ppermute | solution.py:702
  28.0 1.0 %collective-permute-start.7 = (bf16[64,1024]{1,0:T(8,128)(2,1)S(1)}, bf16[64,1024]{1,0:T(8,128)(2,1)S(1)}, u32[]{:S(2)}, u32[]{:S(2)}) collective-permute-start(bf16[64,1024]{1,0:T(8,128)(2,1)S(1)} %add_convert_fusion.3), channel_id=1, source_target_pairs={{0,2},{1,3},{2,0},{3,1},{4,6},{5,7},{6,4},{7,5},{8,10},{9,11},{10,... | collective-permute-start | bytes 393224 | tf_op jit(solution)/shard_map/ppermute | solution.py:702
  29.0 1.1 %shard_map.127 = (bf16[1,128,512]{2,1,0:T(8,128)(2,1)}, bf16[1,64,512]{2,1,0:T(8,128)(2,1)}) custom-call(bf16[512,1536]{1,0:T(8,128)(2,1)S(1)} %get-tuple-element.43.refs_4_.turned_ref, s32[3,1,16]{2,1,0:T(1,128)S(1)} %bitcast.6, bf16[48,512]{1,0:T(8,128)(2,1)S(1)} %get-tuple-element.73.own_slot_ref, ...), custom_call_target="tpu_custom_call" | custom-call | flops 100000000 | bytes 4194304 | tf_op jit(solution)/shard_map/pallas_call | solution.py:689
  30.1 2.7 %collective-permute-done.10 = bf16[64,1024]{1,0:T(8,128)(2,1)S(1)} collective-permute-done((bf16[64,1024]{1,0:T(8,128)(2,1)S(1)}, bf16[64,1024]{1,0:T(8,128)(2,1)S(1)}, u32[]{:S(2)}, u32[]{:S(2)}) %collective-permute-start.10) | collective-permute-done | bytes 131104 | tf_op jit(solution)/shard_map/ppermute | solution.py:702
  32.9 0.1 collective-permute-start.11
  32.9 1.8 %collective-permute-done.7 = bf16[64,1024]{1,0:T(8,128)(2,1)S(1)} collective-permute-done((bf16[64,1024]{1,0:T(8,128)(2,1)S(1)}, bf16[64,1024]{1,0:T(8,128)(2,1)S(1)}, u32[]{:S(2)}, u32[]{:S(2)}) %collective-permute-start.7) | collective-permute-done | bytes 131104 | tf_op jit(solution)/shard_map/ppermute | solution.py:702
  34.7 0.1 collective-permute-start.8
  34.8 0.9 %shard_map.128.settled_ref = f32[128,2048]{1,0:T(8,128)} custom-call(bf16[64,1024]{1,0:T(8,128)(2,1)S(1)} %add_convert_fusion.2.one_ref, bf16[64,1024]{1,0:T(8,128)(2,1)S(1)} %add_convert_fusion.two_ref, bf16[64,1024]{1,0:T(8,128)(2,1)S(1)} %collective-permute-done.11.other_two_ref), custom_call_target="tpu_custom_call" | custom-call | tf_op jit(solution)/shard_map/pallas_call | solution.py:906
  35.8 0.4 %collective-permute-done.8.other_one_ref = bf16[64,1024]{1,0:T(8,128)(2,1)S(1)} collective-permute-done((bf16[64,1024]{1,0:T(8,128)(2,1)S(1)}, bf16[64,1024]{1,0:T(8,128)(2,1)S(1)}, u32[]{:S(2)}, u32[]{:S(2)}) %collective-permute-start.8) | collective-permute-done | bytes 131104 | tf_op jit(solution)/shard_map/ppermute | solution.py:702
  36.1 0.7 %shard_map.129 = f32[128,2048]{1,0:T(8,128)} custom-call(bf16[64,1024]{1,0:T(8,128)(2,1)S(1)} %collective-permute-done.8.other_one_ref, f32[128,2048]{1,0:T(8,128)} %shard_map.128.settled_ref), custom_call_target="tpu_custom_call", output_to_operand_aliasing={{}: (1, {})} | custom-call | tf_op jit(solution)/shard_map/pallas_call | solution.py:914
  (9 shorter events, 0.1 us)
Async XLA Ops:
  0.6 14.8 %copy-start = (bf16[1,64,512]{2,1,0:T(8,128)(2,1)S(1)}, bf16[1,64,512]{2,1,0:T(8,128)(2,1)}, u32[]{:S(2)}) copy-start(bf16[1,64,512]{2,1,0:T(8,128)(2,1)} %refs_0_.3) | copy-start | bytes 196612
  1.9 13.6 %collective-permute-start = (bf16[120,512]{1,0:T(8,128)(2,1)S(1)}, bf16[120,512]{1,0:T(8,128)(2,1)S(1)}, u32[]{:S(2)}, u32[]{:S(2)}) collective-permute-start(bf16[120,512]{1,0:T(8,128)(2,1)S(1)} %shard_map.121.refs_0_), channel_id=1, source_target_pairs={{0,8},{4,12},{8,0},{12,4},{1,9},{5,13},{9,1},{13,5},{2,10},{6,14},... | collective-permute-start | bytes 368648 | tf_op jit(solution)/shard_map/ppermute | solution.py:702
  6.0 12.3 %collective-permute-start.2 = (bf16[120,512]{1,0:T(8,128)(2,1)S(1)}, bf16[120,512]{1,0:T(8,128)(2,1)S(1)}, u32[]{:S(2)}, u32[]{:S(2)}) collective-permute-start(bf16[120,512]{1,0:T(8,128)(2,1)S(1)} %shard_map.121.refs_0_), channel_id=1, source_target_pairs={{0,12},{4,8},{8,4},{12,0},{1,13},{5,9},{9,5},{13,1},{2,14},{6,10},... | collective-permute-start | bytes 368648 | tf_op jit(solution)/shard_map/ppermute | solution.py:702
  7.3 10.9 %collective-permute-start.3 = (bf16[120,512]{1,0:T(8,128)(2,1)S(1)}, bf16[120,512]{1,0:T(8,128)(2,1)S(1)}, u32[]{:S(2)}, u32[]{:S(2)}) collective-permute-start(bf16[120,512]{1,0:T(8,128)(2,1)S(1)} %shard_map.121.refs_0_), channel_id=1, source_target_pairs={{0,4},{4,0},{8,12},{12,8},{1,5},{5,1},{9,13},{13,9},{2,6},{6,2},{1... | collective-permute-start | bytes 368648 | tf_op jit(solution)/shard_map/ppermute | solution.py:702
  7.6 13.8 %collective-permute-start.1 = (bf16[1,64,512]{2,1,0:T(8,128)(2,1)}, bf16[1,64,512]{2,1,0:T(8,128)(2,1)S(1)}, u32[]{:S(2)}, u32[]{:S(2)}) collective-permute-start(bf16[1,64,512]{2,1,0:T(8,128)(2,1)} %refs_0_.3), channel_id=1, source_target_pairs={{0,4},{4,0},{8,12},{12,8},{1,5},{5,1},{9,13},{13,9},{2,6},{6,2},{1... | collective-permute-start | bytes 196616 | tf_op jit(solution)/shard_map/ppermute | solution.py:702
  15.5 7.7 %collective-permute-start.4 = (bf16[1,64,512]{2,1,0:T(8,128)(2,1)S(1)}, bf16[1,64,512]{2,1,0:T(8,128)(2,1)S(1)}, u32[]{:S(2)}, u32[]{:S(2)}) collective-permute-start(bf16[1,64,512]{2,1,0:T(8,128)(2,1)S(1)} %copy-done), channel_id=1, source_target_pairs={{0,8},{4,12},{8,0},{12,4},{1,9},{5,13},{9,1},{13,5},{2,10},{6,14},... | collective-permute-start | bytes 196616 | tf_op jit(solution)/shard_map/ppermute | solution.py:702
  15.5 7.7 %collective-permute-start.5 = (bf16[1,64,512]{2,1,0:T(8,128)(2,1)S(1)}, bf16[1,64,512]{2,1,0:T(8,128)(2,1)S(1)}, u32[]{:S(2)}, u32[]{:S(2)}) collective-permute-start(bf16[1,64,512]{2,1,0:T(8,128)(2,1)S(1)} %copy-done), channel_id=1, source_target_pairs={{0,12},{4,8},{8,4},{12,0},{1,13},{5,9},{9,5},{13,1},{2,14},{6,10},... | collective-permute-start | bytes 196616 | tf_op jit(solution)/shard_map/ppermute | solution.py:702
  24.4 1.9 %collective-permute-start.9 = (bf16[64,1024]{1,0:T(8,128)(2,1)S(1)}, bf16[64,1024]{1,0:T(8,128)(2,1)S(1)}, u32[]{:S(2)}, u32[]{:S(2)}) collective-permute-start(bf16[64,1024]{1,0:T(8,128)(2,1)S(1)} %get-tuple-element.80), channel_id=1, source_target_pairs={{0,1},{1,0},{2,3},{3,2},{4,5},{5,4},{6,7},{7,6},{8,9},{9,8},{10,11... | collective-permute-start | bytes 393224 | tf_op jit(solution)/shard_map/ppermute | solution.py:702
  24.5 4.5 %copy-start.1 = (s32[1,3,16]{2,0,1:T(1,128)S(1)}, s32[1,3,16]{2,0,1:T(1,128)}, u32[]{:S(2)}) copy-start(s32[1,3,16]{2,0,1:T(1,128)} %param.14) | copy-start | bytes 580
  25.8 2.2 %collective-permute-start.6 = (bf16[64,1024]{1,0:T(8,128)(2,1)S(1)}, bf16[64,1024]{1,0:T(8,128)(2,1)S(1)}, u32[]{:S(2)}, u32[]{:S(2)}) collective-permute-start(bf16[64,1024]{1,0:T(8,128)(2,1)S(1)} %get-tuple-element.71), channel_id=1, source_target_pairs={{0,1},{1,0},{2,3},{3,2},{4,5},{5,4},{6,7},{7,6},{8,9},{9,8},{10,11... | collective-permute-start | bytes 393224 | tf_op jit(solution)/shard_map/ppermute | solution.py:702
  26.4 6.4 %collective-permute-start.10 = (bf16[64,1024]{1,0:T(8,128)(2,1)S(1)}, bf16[64,1024]{1,0:T(8,128)(2,1)S(1)}, u32[]{:S(2)}, u32[]{:S(2)}) collective-permute-start(bf16[64,1024]{1,0:T(8,128)(2,1)S(1)} %add_convert_fusion.1), channel_id=1, source_target_pairs={{0,2},{1,3},{2,0},{3,1},{4,6},{5,7},{6,4},{7,5},{8,10},{9,11},{10,... | collective-permute-start | bytes 393224 | tf_op jit(solution)/shard_map/ppermute | solution.py:702
  28.0 6.7 %collective-permute-start.7 = (bf16[64,1024]{1,0:T(8,128)(2,1)S(1)}, bf16[64,1024]{1,0:T(8,128)(2,1)S(1)}, u32[]{:S(2)}, u32[]{:S(2)}) collective-permute-start(bf16[64,1024]{1,0:T(8,128)(2,1)S(1)} %add_convert_fusion.3), channel_id=1, source_target_pairs={{0,2},{1,3},{2,0},{3,1},{4,6},{5,7},{6,4},{7,5},{8,10},{9,11},{10,... | collective-permute-start | bytes 393224 | tf_op jit(solution)/shard_map/ppermute | solution.py:702
  32.9 2.0 %collective-permute-start.11 = (bf16[64,1024]{1,0:T(8,128)(2,1)S(1)}, bf16[64,1024]{1,0:T(8,128)(2,1)S(1)}, u32[]{:S(2)}, u32[]{:S(2)}) collective-permute-start(bf16[64,1024]{1,0:T(8,128)(2,1)S(1)} %add_convert_fusion.two_ref), channel_id=1, source_target_pairs={{0,1},{1,0},{2,3},{3,2},{4,5},{5,4},{6,7},{7,6},{8,9},{9,8},{10,11... | collective-permute-start | bytes 393224 | tf_op jit(solution)/shard_map/ppermute | solution.py:702
  34.7 1.4 %collective-permute-start.8 = (bf16[64,1024]{1,0:T(8,128)(2,1)S(1)}, bf16[64,1024]{1,0:T(8,128)(2,1)S(1)}, u32[]{:S(2)}, u32[]{:S(2)}) collective-permute-start(bf16[64,1024]{1,0:T(8,128)(2,1)S(1)} %add_convert_fusion.2.one_ref), channel_id=1, source_target_pairs={{0,1},{1,0},{2,3},{3,2},{4,5},{5,4},{6,7},{7,6},{8,9},{9,8},{10,11... | collective-permute-start | bytes 393224 | tf_op jit(solution)/shard_map/ppermute | solution.py:702

commit v20 on v19

--- a/solution.py
+++ b/solution.py
@@ -765,8 +765,13 @@
         10**8,
         fetched=1,
     )
-    packs[1], cotangent = lax.optimization_barrier((packs[1], cotangent))
-    cotangents = [cotangent] + [swap(cotangent, "space", step) for step in steps[1:-1]] + [near]
+    turned, early = lax.optimization_barrier((turned, cotangent))
+    packs[1], late = lax.optimization_barrier((packs[1], cotangent))
+    cotangents = (
+        [cotangent, swap(late, "space", steps[1])]
+        + [swap(early, "space", step) for step in steps[2:-1]]
+        + [near]
+    )
     rows = regions * mesh_count
     slots = regions * mesh_cap
     (

time: 37 us -> 36.8 us (level)
  transfers between devices with their start and end apart: 12 -> 12, of which waited for: 5 -> 6; matrix products, arithmetic and copies ran while one was open for 0% -> 0% of each run, Pallas kernels for 25% -> 25%
where the time goes in v20:
time: 36.8 us; the launch traced here: 36.5 us
  starting transfers between devices  13.3 us (36%)
  Pallas kernels  12.3 us (33%)
  waiting for transfers between devices  9.96 us (27%)
  between operations  0.77 us (2%)
    ppermute x12, starting transfers between devices, swap(): lax.ppermute(block, axis, [(i, i ^ bits) for i in range(lax.axis_size(axi...  13.3 us
    pallas_call x7, Pallas kernels, call(): pl.pallas_call(kernel, out_shape=[jax.ShapeDtypeStruct(shape, kind) for s...  10.7 us
    ppermute x12, waiting for transfers between devices, swap(): lax.ppermute(block, axis, [(i, i ^ bits) for i in range(lax.axis_size(axi...  9.96 us
    pallas_call x1, Pallas kernels, whole_sample_body(): pl.pallas_call(settle_kernel, out_shape=weight_shape, in_specs=[VMEM] * 3...  0.92 us
  transfers between devices with their start and end apart: 12, of which 6 were waited for; matrix products, arithmetic and copies ran while one was open for 0% of the time, Pallas kernels for 25%

profile of v20, /device:TPU:0, one launch (start us, length us, event | category | flops | bytes accessed | tf_op | source)
XLA Modules:
  0.0 36.5 jit_solution(8942020563515944527)
XLA Ops:
  0.6 0.0 copy-start
  0.6 1.2 %shard_map.121.refs_0_ = bf16[120,512]{1,0:T(8,128)(2,1)S(1)} custom-call(bf16[1,128,512]{2,1,0:T(8,128)(2,1)} %refs_0_.1, bf16[1,64,512]{2,1,0:T(8,128)(2,1)} %refs_1_.1, s32[3,1,16]{2,1,0:T(1,128)} %bitcast.5, s32[1,256]{1,0:T(1,128)} %bitcast.7, s32[1,256]{1,0:T(1,128)} %bitcast.8, s32[1,4,8]{2,1,0:T(4,128)} %refs_5_.1, s32[1,256]{1,0:T(1,128)} %bitcast.9, ...), custom_call_target="tpu_custom_call" | custom-call | flops 10000000 | bytes 4194304 | tf_op jit(solution)/shard_map/pallas_call | solution.py:689
  1.9 4.1 %collective-permute-start.1 = (bf16[120,512]{1,0:T(8,128)(2,1)S(1)}, bf16[120,512]{1,0:T(8,128)(2,1)S(1)}, u32[]{:S(2)}, u32[]{:S(2)}) collective-permute-start(bf16[120,512]{1,0:T(8,128)(2,1)S(1)} %shard_map.121.refs_0_), channel_id=1, source_target_pairs={{0,8},{4,12},{8,0},{12,4},{1,9},{5,13},{9,1},{13,5},{2,10},{6,14},... | collective-permute-start | bytes 368648 | tf_op jit(solution)/shard_map/ppermute | solution.py:702
  6.0 1.3 %collective-permute-start.2 = (bf16[120,512]{1,0:T(8,128)(2,1)S(1)}, bf16[120,512]{1,0:T(8,128)(2,1)S(1)}, u32[]{:S(2)}, u32[]{:S(2)}) collective-permute-start(bf16[120,512]{1,0:T(8,128)(2,1)S(1)} %shard_map.121.refs_0_), channel_id=1, source_target_pairs={{0,12},{4,8},{8,4},{12,0},{1,13},{5,9},{9,5},{13,1},{2,14},{6,10},... | collective-permute-start | bytes 368648 | tf_op jit(solution)/shard_map/ppermute | solution.py:702
  7.3 0.2 collective-permute-start.3
  7.6 1.8 %collective-permute-start = (bf16[1,64,512]{2,1,0:T(8,128)(2,1)}, bf16[1,64,512]{2,1,0:T(8,128)(2,1)S(1)}, u32[]{:S(2)}, u32[]{:S(2)}) collective-permute-start(bf16[1,64,512]{2,1,0:T(8,128)(2,1)} %refs_0_.3), channel_id=1, source_target_pairs={{0,4},{4,0},{8,12},{12,8},{1,5},{5,1},{9,13},{13,9},{2,6},{6,2},{1... | collective-permute-start | bytes 196616 | tf_op jit(solution)/shard_map/ppermute | solution.py:702
  9.4 2.1 %shard_map.122 = (bf16[512,2048]{1,0:T(8,128)(2,1)S(1)}, bf16[512,1536]{1,0:T(8,128)(2,1)S(1)}) custom-call(bf16[512,2048]{1,0:T(8,128)(2,1)} %source_ref), custom_call_target="tpu_custom_call" | custom-call | flops 100000000 | bytes 4194304 | tf_op jit(solution)/shard_map/pallas_call | solution.py:689
  11.5 2.5 %collective-permute-start.5 = (bf16[1,64,512]{2,1,0:T(8,128)(2,1)S(1)}, bf16[1,64,512]{2,1,0:T(8,128)(2,1)S(1)}, u32[]{:S(2)}, u32[]{:S(2)}) collective-permute-start(bf16[1,64,512]{2,1,0:T(8,128)(2,1)S(1)} %copy-done), channel_id=1, source_target_pairs={{0,12},{4,8},{8,4},{12,0},{1,13},{5,9},{9,5},{13,1},{2,14},{6,10},... | collective-permute-start | bytes 196616 | tf_op jit(solution)/shard_map/ppermute | solution.py:702
  14.0 1.5 %collective-permute-done.1.refs_1_ = bf16[120,512]{1,0:T(8,128)(2,1)S(1)} collective-permute-done((bf16[120,512]{1,0:T(8,128)(2,1)S(1)}, bf16[120,512]{1,0:T(8,128)(2,1)S(1)}, u32[]{:S(2)}, u32[]{:S(2)}) %collective-permute-start.1) | collective-permute-done | bytes 122912 | tf_op jit(solution)/shard_map/ppermute | solution.py:702
  15.5 0.0 collective-permute-start.4
  15.5 0.0 collective-permute-done.2.refs_2_
  15.5 1.8 %collective-permute-done.3.refs_3_ = bf16[120,512]{1,0:T(8,128)(2,1)S(1)} collective-permute-done((bf16[120,512]{1,0:T(8,128)(2,1)S(1)}, bf16[120,512]{1,0:T(8,128)(2,1)S(1)}, u32[]{:S(2)}, u32[]{:S(2)}) %collective-permute-start.3) | collective-permute-done | bytes 122912 | tf_op jit(solution)/shard_map/ppermute | solution.py:702
  17.2 3.1 %shard_map.123 = (bf16[192,512]{1,0:T(8,128)(2,1)S(1)}, bf16[256,512]{1,0:T(8,128)(2,1)S(1)}, bf16[256,512]{1,0:T(8,128)(2,1)S(1)}, bf16[128,512]{1,0:T(8,128)(2...) custom-call(bf16[120,512]{1,0:T(8,128)(2,1)S(1)} %shard_map.121.refs, ...), custom_call_target="tpu_custom_call" | custom-call | flops 2000000000 | bytes 4194304 | tf_op jit(solution)/shard_map/pallas_call | solution.py:689
  20.4 0.7 %shard_map.124 = (f32[192,512]{1,0:T(8,128)S(1)}, bf16[128,192]{1,0:T(8,128)(2,1)S(1)}, bf16[128,256]{1,0:T(8,128)(2,1)S(1)}, bf16[128,128]{1,0:T(8,128)(2,1)S(1)}, bf16[128,256]{1,0:T(8,128)(2,1)S(1)}) custom-call(bf16[1,64,512]{2,1,0:T(8,128)(2,1)S(1)} %copy-done, bf16[1,64,512]{2,1,0:T(8,128)(2,1)S(1)} %collective-permute-done.refs_1_, ...), custom_call_target="tpu_custom_call" | custom-call | flops 1000000000 | bytes 4194304 | tf_op jit(solution)/shard_map/pallas_call | solution.py:689
  21.0 0.0 collective-permute-done.5.refs_3_
  21.1 1.8 %collective-permute-done.4.refs_2_ = bf16[1,64,512]{2,1,0:T(8,128)(2,1)S(1)} collective-permute-done((bf16[1,64,512]{2,1,0:T(8,128)(2,1)S(1)}, bf16[1,64,512]{2,1,0:T(8,128)(2,1)S(1)}, u32[]{:S(2)}, u32[]{:S(2)}) %collective-permute-start.4) | collective-permute-done | bytes 65568 | tf_op jit(solution)/shard_map/ppermute | solution.py:702
  22.9 1.2 %shard_map.125 = (f32[256,512]{1,0:T(8,128)S(1)}, bf16[64,1024]{1,0:T(8,128)(2,1)S(1)}, bf16[64,1024]{1,0:T(8,128)(2,1)S(1)}) custom-call(bf16[1,64,512]{2,1,0:T(8,128)(2,1)S(1)} %copy-done, bf16[1,64,512]{2,1,0:T(8,128)(2,1)S(1)} %collective-permute-done.refs_1_, bf16[1,64,512]{2,1,0:T(8,128)(2,1)S(1)} %collective-permute-done.4.refs_2_, ...), custom_call_target="tpu_custom_call" | custom-call | flops 1000000000 | bytes 4194304 | tf_op jit(solution)/shard_map/pallas_call | solution.py:689
  24.1 0.1 collective-permute-start.9
  24.2 0.0 copy-start.1
  24.2 1.3 %shard_map.126 = (bf16[48,512]{1,0:T(8,128)(2,1)S(1)}, bf16[64,1024]{1,0:T(8,128)(2,1)S(1)}, bf16[64,1024]{1,0:T(8,128)(2,1)S(1)}) custom-call(bf16[128,192]{1,0:T(8,128)(2,1)S(1)} %get-tuple-element.60.grid_columns_ref, bf16[128,256]{1,0:T(8,128)(2,1)S(1)} %get-tuple-element.61.mesh_columns_ref, bf16[448,256]{1,0:T(8,128)(2,1)S(1)} %get-tuple-element.62.hot_ref, ...), custom_call_target="tpu_custom_call" | custom-call | flops 1000000000 | bytes 4194304 | tf_op jit(solution)/shard_map/pallas_call | solution.py:689
  25.5 0.6 %collective-permute-start.6 = (bf16[64,1024]{1,0:T(8,128)(2,1)S(1)}, bf16[64,1024]{1,0:T(8,128)(2,1)S(1)}, u32[]{:S(2)}, u32[]{:S(2)}) collective-permute-start(bf16[64,1024]{1,0:T(8,128)(2,1)S(1)} %get-tuple-element.75), channel_id=1, source_target_pairs={{0,1},{1,0},{2,3},{3,2},{4,5},{5,4},{6,7},{7,6},{8,9},{9,8},{10,11... | collective-permute-start | bytes 393224 | tf_op jit(solution)/shard_map/ppermute | solution.py:702
  26.0 0.0 collective-permute-done.9
  26.1 1.6 %collective-permute-start.10 = (bf16[64,1024]{1,0:T(8,128)(2,1)S(1)}, bf16[64,1024]{1,0:T(8,128)(2,1)S(1)}, u32[]{:S(2)}, u32[]{:S(2)}) collective-permute-start(bf16[64,1024]{1,0:T(8,128)(2,1)S(1)} %add_convert_fusion.1), channel_id=1, source_target_pairs={{0,2},{1,3},{2,0},{3,1},{4,6},{5,7},{6,4},{7,5},{8,10},{9,11},{10,... | collective-permute-start | bytes 393224 | tf_op jit(solution)/shard_map/ppermute | solution.py:702
  27.7 1.0 %collective-permute-start.7 = (bf16[64,1024]{1,0:T(8,128)(2,1)S(1)}, bf16[64,1024]{1,0:T(8,128)(2,1)S(1)}, u32[]{:S(2)}, u32[]{:S(2)}) collective-permute-start(bf16[64,1024]{1,0:T(8,128)(2,1)S(1)} %add_convert_fusion.3), channel_id=1, source_target_pairs={{0,2},{1,3},{2,0},{3,1},{4,6},{5,7},{6,4},{7,5},{8,10},{9,11},{10,... | collective-permute-start | bytes 393224 | tf_op jit(solution)/shard_map/ppermute | solution.py:702
  28.7 1.1 %shard_map.127 = (bf16[1,128,512]{2,1,0:T(8,128)(2,1)}, bf16[1,64,512]{2,1,0:T(8,128)(2,1)}) custom-call(bf16[512,1536]{1,0:T(8,128)(2,1)S(1)} %get-tuple-element.47.refs_4_.turned_ref, s32[3,1,16]{2,1,0:T(1,128)S(1)} %bitcast.6, bf16[48,512]{1,0:T(8,128)(2,1)S(1)} %get-tuple-element.77.own_slot_ref, ...), custom_call_target="tpu_custom_call" | custom-call | flops 100000000 | bytes 4194304 | tf_op jit(solution)/shard_map/pallas_call | solution.py:689
  29.8 2.7 %collective-permute-done.10 = bf16[64,1024]{1,0:T(8,128)(2,1)S(1)} collective-permute-done((bf16[64,1024]{1,0:T(8,128)(2,1)S(1)}, bf16[64,1024]{1,0:T(8,128)(2,1)S(1)}, u32[]{:S(2)}, u32[]{:S(2)}) %collective-permute-start.10) | collective-permute-done | bytes 131104 | tf_op jit(solution)/shard_map/ppermute | solution.py:702
  32.5 0.1 collective-permute-start.11
  32.6 1.8 %collective-permute-done.7 = bf16[64,1024]{1,0:T(8,128)(2,1)S(1)} collective-permute-done((bf16[64,1024]{1,0:T(8,128)(2,1)S(1)}, bf16[64,1024]{1,0:T(8,128)(2,1)S(1)}, u32[]{:S(2)}, u32[]{:S(2)}) %collective-permute-start.7) | collective-permute-done | bytes 131104 | tf_op jit(solution)/shard_map/ppermute | solution.py:702
  34.4 0.1 collective-permute-start.8
  34.5 0.9 %shard_map.128.settled_ref = f32[128,2048]{1,0:T(8,128)} custom-call(bf16[64,1024]{1,0:T(8,128)(2,1)S(1)} %add_convert_fusion.2.one_ref, bf16[64,1024]{1,0:T(8,128)(2,1)S(1)} %add_convert_fusion.two_ref, bf16[64,1024]{1,0:T(8,128)(2,1)S(1)} %collective-permute-done.11.other_two_ref), custom_call_target="tpu_custom_call" | custom-call | tf_op jit(solution)/shard_map/pallas_call | solution.py:911
  35.4 0.4 %collective-permute-done.8.other_one_ref = bf16[64,1024]{1,0:T(8,128)(2,1)S(1)} collective-permute-done((bf16[64,1024]{1,0:T(8,128)(2,1)S(1)}, bf16[64,1024]{1,0:T(8,128)(2,1)S(1)}, u32[]{:S(2)}, u32[]{:S(2)}) %collective-permute-start.8) | collective-permute-done | bytes 131104 | tf_op jit(solution)/shard_map/ppermute | solution.py:702
  35.8 0.7 %shard_map.129 = f32[128,2048]{1,0:T(8,128)} custom-call(bf16[64,1024]{1,0:T(8,128)(2,1)S(1)} %collective-permute-done.8.other_one_ref, f32[128,2048]{1,0:T(8,128)} %shard_map.128.settled_ref), custom_call_target="tpu_custom_call", output_to_operand_aliasing={{}: (1, {})} | custom-call | tf_op jit(solution)/shard_map/pallas_call | solution.py:919
  (9 shorter events, 0.1 us)
Async XLA Ops:
  0.6 10.8 %copy-start = (bf16[1,64,512]{2,1,0:T(8,128)(2,1)S(1)}, bf16[1,64,512]{2,1,0:T(8,128)(2,1)}, u32[]{:S(2)}) copy-start(bf16[1,64,512]{2,1,0:T(8,128)(2,1)} %refs_0_.3) | copy-start | bytes 196612
  1.9 13.6 %collective-permute-start.1 = (bf16[120,512]{1,0:T(8,128)(2,1)S(1)}, bf16[120,512]{1,0:T(8,128)(2,1)S(1)}, u32[]{:S(2)}, u32[]{:S(2)}) collective-permute-start(bf16[120,512]{1,0:T(8,128)(2,1)S(1)} %shard_map.121.refs_0_), channel_id=1, source_target_pairs={{0,8},{4,12},{8,0},{12,4},{1,9},{5,13},{9,1},{13,5},{2,10},{6,14},... | collective-permute-start | bytes 368648 | tf_op jit(solution)/shard_map/ppermute | solution.py:702
  6.0 9.5 %collective-permute-start.2 = (bf16[120,512]{1,0:T(8,128)(2,1)S(1)}, bf16[120,512]{1,0:T(8,128)(2,1)S(1)}, u32[]{:S(2)}, u32[]{:S(2)}) collective-permute-start(bf16[120,512]{1,0:T(8,128)(2,1)S(1)} %shard_map.121.refs_0_), channel_id=1, source_target_pairs={{0,12},{4,8},{8,4},{12,0},{1,13},{5,9},{9,5},{13,1},{2,14},{6,10},... | collective-permute-start | bytes 368648 | tf_op jit(solution)/shard_map/ppermute | solution.py:702
  7.3 9.9 %collective-permute-start.3 = (bf16[120,512]{1,0:T(8,128)(2,1)S(1)}, bf16[120,512]{1,0:T(8,128)(2,1)S(1)}, u32[]{:S(2)}, u32[]{:S(2)}) collective-permute-start(bf16[120,512]{1,0:T(8,128)(2,1)S(1)} %shard_map.121.refs_0_), channel_id=1, source_target_pairs={{0,4},{4,0},{8,12},{12,8},{1,5},{5,1},{9,13},{13,9},{2,6},{6,2},{1... | collective-permute-start | bytes 368648 | tf_op jit(solution)/shard_map/ppermute | solution.py:702
  7.6 12.8 %collective-permute-start = (bf16[1,64,512]{2,1,0:T(8,128)(2,1)}, bf16[1,64,512]{2,1,0:T(8,128)(2,1)S(1)}, u32[]{:S(2)}, u32[]{:S(2)}) collective-permute-start(bf16[1,64,512]{2,1,0:T(8,128)(2,1)} %refs_0_.3), channel_id=1, source_target_pairs={{0,4},{4,0},{8,12},{12,8},{1,5},{5,1},{9,13},{13,9},{2,6},{6,2},{1... | collective-permute-start | bytes 196616 | tf_op jit(solution)/shard_map/ppermute | solution.py:702
  11.5 9.6 %collective-permute-start.5 = (bf16[1,64,512]{2,1,0:T(8,128)(2,1)S(1)}, bf16[1,64,512]{2,1,0:T(8,128)(2,1)S(1)}, u32[]{:S(2)}, u32[]{:S(2)}) collective-permute-start(bf16[1,64,512]{2,1,0:T(8,128)(2,1)S(1)} %copy-done), channel_id=1, source_target_pairs={{0,12},{4,8},{8,4},{12,0},{1,13},{5,9},{9,5},{13,1},{2,14},{6,10},... | collective-permute-start | bytes 196616 | tf_op jit(solution)/shard_map/ppermute | solution.py:702
  15.5 7.4 %collective-permute-start.4 = (bf16[1,64,512]{2,1,0:T(8,128)(2,1)S(1)}, bf16[1,64,512]{2,1,0:T(8,128)(2,1)S(1)}, u32[]{:S(2)}, u32[]{:S(2)}) collective-permute-start(bf16[1,64,512]{2,1,0:T(8,128)(2,1)S(1)} %copy-done), channel_id=1, source_target_pairs={{0,8},{4,12},{8,0},{12,4},{1,9},{5,13},{9,1},{13,5},{2,10},{6,14},... | collective-permute-start | bytes 196616 | tf_op jit(solution)/shard_map/ppermute | solution.py:702
  24.1 1.9 %collective-permute-start.9 = (bf16[64,1024]{1,0:T(8,128)(2,1)S(1)}, bf16[64,1024]{1,0:T(8,128)(2,1)S(1)}, u32[]{:S(2)}, u32[]{:S(2)}) collective-permute-start(bf16[64,1024]{1,0:T(8,128)(2,1)S(1)} %get-tuple-element.84), channel_id=1, source_target_pairs={{0,1},{1,0},{2,3},{3,2},{4,5},{5,4},{6,7},{7,6},{8,9},{9,8},{10,11... | collective-permute-start | bytes 393224 | tf_op jit(solution)/shard_map/ppermute | solution.py:702
  24.2 4.5 %copy-start.1 = (s32[1,3,16]{2,0,1:T(1,128)S(1)}, s32[1,3,16]{2,0,1:T(1,128)}, u32[]{:S(2)}) copy-start(s32[1,3,16]{2,0,1:T(1,128)} %param.14) | copy-start | bytes 580
  25.5 2.2 %collective-permute-start.6 = (bf16[64,1024]{1,0:T(8,128)(2,1)S(1)}, bf16[64,1024]{1,0:T(8,128)(2,1)S(1)}, u32[]{:S(2)}, u32[]{:S(2)}) collective-permute-start(bf16[64,1024]{1,0:T(8,128)(2,1)S(1)} %get-tuple-element.75), channel_id=1, source_target_pairs={{0,1},{1,0},{2,3},{3,2},{4,5},{5,4},{6,7},{7,6},{8,9},{9,8},{10,11... | collective-permute-start | bytes 393224 | tf_op jit(solution)/shard_map/ppermute | solution.py:702
  26.1 6.4 %collective-permute-start.10 = (bf16[64,1024]{1,0:T(8,128)(2,1)S(1)}, bf16[64,1024]{1,0:T(8,128)(2,1)S(1)}, u32[]{:S(2)}, u32[]{:S(2)}) collective-permute-start(bf16[64,1024]{1,0:T(8,128)(2,1)S(1)} %add_convert_fusion.1), channel_id=1, source_target_pairs={{0,2},{1,3},{2,0},{3,1},{4,6},{5,7},{6,4},{7,5},{8,10},{9,11},{10,... | collective-permute-start | bytes 393224 | tf_op jit(solution)/shard_map/ppermute | solution.py:702
  27.7 6.7 %collective-permute-start.7 = (bf16[64,1024]{1,0:T(8,128)(2,1)S(1)}, bf16[64,1024]{1,0:T(8,128)(2,1)S(1)}, u32[]{:S(2)}, u32[]{:S(2)}) collective-permute-start(bf16[64,1024]{1,0:T(8,128)(2,1)S(1)} %add_convert_fusion.3), channel_id=1, source_target_pairs={{0,2},{1,3},{2,0},{3,1},{4,6},{5,7},{6,4},{7,5},{8,10},{9,11},{10,... | collective-permute-start | bytes 393224 | tf_op jit(solution)/shard_map/ppermute | solution.py:702
  32.5 2.0 %collective-permute-start.11 = (bf16[64,1024]{1,0:T(8,128)(2,1)S(1)}, bf16[64,1024]{1,0:T(8,128)(2,1)S(1)}, u32[]{:S(2)}, u32[]{:S(2)}) collective-permute-start(bf16[64,1024]{1,0:T(8,128)(2,1)S(1)} %add_convert_fusion.two_ref), channel_id=1, source_target_pairs={{0,1},{1,0},{2,3},{3,2},{4,5},{5,4},{6,7},{7,6},{8,9},{9,8},{10,11... | collective-permute-start | bytes 393224 | tf_op jit(solution)/shard_map/ppermute | solution.py:702
  34.4 1.4 %collective-permute-start.8 = (bf16[64,1024]{1,0:T(8,128)(2,1)S(1)}, bf16[64,1024]{1,0:T(8,128)(2,1)S(1)}, u32[]{:S(2)}, u32[]{:S(2)}) collective-permute-start(bf16[64,1024]{1,0:T(8,128)(2,1)S(1)} %add_convert_fusion.2.one_ref), channel_id=1, source_target_pairs={{0,1},{1,0},{2,3},{3,2},{4,5},{5,4},{6,7},{7,6},{8,9},{9,8},{10,11... | collective-permute-start | bytes 393224 | tf_op jit(solution)/shard_map/ppermute | solution.py:702

commit v21 on v18

--- a/solution.py
+++ b/solution.py
@@ -771,7 +771,7 @@
         10**8,
         fetched=1,
     )
-    packs[1], cotangent = lax.optimization_barrier((packs[1], cotangent))
+    *packs[1:3], cotangent = lax.optimization_barrier((*packs[1:3], cotangent))
     cotangents = [cotangent] + [swap(cotangent, "space", step) for step in steps[1:-1]] + [near]
     rows = regions * mesh_count
     slots = regions * mesh_cap

time: 36.8 us -> 39.9 us (1.084)
  the two profiles are of different devices: /device:TPU:19 before, /device:TPU:0 now
where the time goes in v21:
time: 39.9 us; the launch traced here: 39.7 us
  starting transfers between devices  16.1 us (40%)
  Pallas kernels  12.3 us (31%)
  waiting for transfers between devices  10.4 us (26%)
  between operations  0.77 us (2%)
    pallas_call x7, Pallas kernels, call(): pl.pallas_call(kernel, out_shape=[jax.ShapeDtypeStruct(shape, kind) for s...  10.7 us
    ppermute x9, starting transfers between devices, swap(): lax.ppermute(block, axis, [(i, i ^ bits) for i in range(lax.axis_size(axi...  8.16 us
    ppermute x3, starting transfers between devices, shifted(): lax.ppermute(block, 'space', [(i, (i + step) % count) for i in range(coun...  7.93 us
    ppermute x9, waiting for transfers between devices, swap(): lax.ppermute(block, axis, [(i, i ^ bits) for i in range(lax.axis_size(axi...  6.81 us
    ppermute x3, waiting for transfers between devices, shifted(): lax.ppermute(block, 'space', [(i, (i + step) % count) for i in range(coun...  3.57 us
    pallas_call x1, Pallas kernels, whole_sample_body(): pl.pallas_call(settle_kernel, out_shape=weight_shape, in_specs=[VMEM] * 3...  0.92 us
  transfers between devices with their start and end apart: 12, of which 5 were waited for; matrix products, arithmetic and copies ran while one was open for 0% of the time, Pallas kernels for 23%

profile of v21, /device:TPU:0, one launch (start us, length us, event | category | flops | bytes accessed | tf_op | source)
XLA Modules:
  0.0 39.7 jit_solution(5898204178454362578)
XLA Ops:
  0.6 0.0 copy-start
  0.6 1.2 %shard_map.121.refs_0_ = bf16[120,512]{1,0:T(8,128)(2,1)S(1)} custom-call(bf16[1,128,512]{2,1,0:T(8,128)(2,1)} %refs_0_.1, bf16[1,64,512]{2,1,0:T(8,128)(2,1)} %refs_1_.1, s32[3,1,16]{2,1,0:T(1,128)} %bitcast.5, s32[1,256]{1,0:T(1,128)} %bitcast.7, s32[1,256]{1,0:T(1,128)} %bitcast.8, s32[1,4,8]{2,1,0:T(4,128)} %refs_5_.1, s32[1,256]{1,0:T(1,128)} %bitcast.9, ...), custom_call_target="tpu_custom_call" | custom-call | flops 10000000 | bytes 4194304 | tf_op jit(solution)/shard_map/pallas_call | solution.py:689
  1.9 4.1 %collective-permute-start = (bf16[120,512]{1,0:T(8,128)(2,1)S(1)}, bf16[120,512]{1,0:T(8,128)(2,1)S(1)}, u32[]{:S(2)}, u32[]{:S(2)}) collective-permute-start(bf16[120,512]{1,0:T(8,128)(2,1)S(1)} %shard_map.121.refs_0_), channel_id=1, source_target_pairs={{0,8},{4,12},{8,0},{12,4},{1,9},{5,13},{9,1},{13,5},{2,10},{6,14},... | collective-permute-start | bytes 368648 | tf_op jit(solution)/shard_map/ppermute | solution.py:707
  6.0 1.6 %collective-permute-start.1 = (bf16[120,512]{1,0:T(8,128)(2,1)S(1)}, bf16[120,512]{1,0:T(8,128)(2,1)S(1)}, u32[]{:S(2)}, u32[]{:S(2)}) collective-permute-start(bf16[120,512]{1,0:T(8,128)(2,1)S(1)} %shard_map.121.refs_0_), channel_id=1, source_target_pairs={{0,4},{4,8},{8,12},{12,0},{1,5},{5,9},{9,13},{13,1},{2,6},{6,10},{... | collective-permute-start | bytes 368648 | tf_op jit(solution)/shard_map/ppermute | solution.py:707
  7.6 2.2 %collective-permute-start.3 = (bf16[120,512]{1,0:T(8,128)(2,1)S(1)}, bf16[120,512]{1,0:T(8,128)(2,1)S(1)}, u32[]{:S(2)}, u32[]{:S(2)}) collective-permute-start(bf16[120,512]{1,0:T(8,128)(2,1)S(1)} %shard_map.121.refs_0_), channel_id=1, source_target_pairs={{0,12},{4,0},{8,4},{12,8},{1,13},{5,1},{9,5},{13,9},{2,14},{6,2},{... | collective-permute-start | bytes 368648 | tf_op jit(solution)/shard_map/ppermute | solution.py:707
  9.8 0.0 collective-permute-start.2
  9.8 2.1 %shard_map.122 = (bf16[512,2048]{1,0:T(8,128)(2,1)S(1)}, bf16[512,1536]{1,0:T(8,128)(2,1)S(1)}) custom-call(bf16[512,2048]{1,0:T(8,128)(2,1)} %source_ref), custom_call_target="tpu_custom_call" | custom-call | flops 100000000 | bytes 4194304 | tf_op jit(solution)/shard_map/pallas_call | solution.py:689
  11.9 3.6 %collective-permute-done.refs_1_ = bf16[120,512]{1,0:T(8,128)(2,1)S(1)} collective-permute-done((bf16[120,512]{1,0:T(8,128)(2,1)S(1)}, bf16[120,512]{1,0:T(8,128)(2,1)S(1)}, u32[]{:S(2)}, u32[]{:S(2)}) %collective-permute-start) | collective-permute-done | bytes 122912 | tf_op jit(solution)/shard_map/ppermute | solution.py:707
  15.5 0.0 collective-permute-done.1.refs_2_
  15.5 4.4 %collective-permute-start.4 = (bf16[1,64,512]{2,1,0:T(8,128)(2,1)S(1)}, bf16[1,64,512]{2,1,0:T(8,128)(2,1)S(1)}, u32[]{:S(2)}, u32[]{:S(2)}) collective-permute-start(bf16[1,64,512]{2,1,0:T(8,128)(2,1)S(1)} %copy-done), channel_id=1, source_target_pairs={{0,8},{4,12},{8,0},{12,4},{1,9},{5,13},{9,1},{13,5},{2,10},{6,14},... | collective-permute-start | bytes 196616 | tf_op jit(solution)/shard_map/ppermute | solution.py:702
  19.9 0.4 %collective-permute-start.5 = (bf16[1,64,512]{2,1,0:T(8,128)(2,1)S(1)}, bf16[1,64,512]{2,1,0:T(8,128)(2,1)S(1)}, u32[]{:S(2)}, u32[]{:S(2)}) collective-permute-start(bf16[1,64,512]{2,1,0:T(8,128)(2,1)S(1)} %copy-done), channel_id=1, source_target_pairs={{0,12},{4,8},{8,4},{12,0},{1,13},{5,9},{9,5},{13,1},{2,14},{6,10},... | collective-permute-start | bytes 196616 | tf_op jit(solution)/shard_map/ppermute | solution.py:702
  20.4 3.1 %shard_map.123 = (bf16[192,512]{1,0:T(8,128)(2,1)S(1)}, bf16[256,512]{1,0:T(8,128)(2,1)S(1)}, bf16[256,512]{1,0:T(8,128)(2,1)S(1)}, bf16[128,512]{1,0:T(8,128)(2...) custom-call(bf16[120,512]{1,0:T(8,128)(2,1)S(1)} %shard_map.121.refs, ...), custom_call_target="tpu_custom_call" | custom-call | flops 2000000000 | bytes 4194304 | tf_op jit(solution)/shard_map/pallas_call | solution.py:689
  23.5 0.7 %shard_map.124 = (f32[192,512]{1,0:T(8,128)S(1)}, bf16[128,192]{1,0:T(8,128)(2,1)S(1)}, bf16[128,256]{1,0:T(8,128)(2,1)S(1)}, bf16[128,128]{1,0:T(8,128)(2,1)S(1)}, bf16[128,256]{1,0:T(8,128)(2,1)S(1)}) custom-call(bf16[1,64,512]{2,1,0:T(8,128)(2,1)S(1)} %copy-done, bf16[1,64,512]{2,1,0:T(8,128)(2,1)S(1)} %collective-permute-done.2.refs_1_, ...), custom_call_target="tpu_custom_call" | custom-call | flops 1000000000 | bytes 4194304 | tf_op jit(solution)/shard_map/pallas_call | solution.py:689
  24.2 0.0 collective-permute-done.4.refs_2_
  24.2 1.9 %collective-permute-done.5.refs_3_ = bf16[1,64,512]{2,1,0:T(8,128)(2,1)S(1)} collective-permute-done((bf16[1,64,512]{2,1,0:T(8,128)(2,1)S(1)}, bf16[1,64,512]{2,1,0:T(8,128)(2,1)S(1)}, u32[]{:S(2)}, u32[]{:S(2)}) %collective-permute-start.5) | collective-permute-done | bytes 65568 | tf_op jit(solution)/shard_map/ppermute | solution.py:702
  26.0 1.2 %shard_map.125 = (f32[256,512]{1,0:T(8,128)S(1)}, bf16[64,1024]{1,0:T(8,128)(2,1)S(1)}, bf16[64,1024]{1,0:T(8,128)(2,1)S(1)}) custom-call(bf16[1,64,512]{2,1,0:T(8,128)(2,1)S(1)} %copy-done, bf16[1,64,512]{2,1,0:T(8,128)(2,1)S(1)} %collective-permute-done.2.refs_1_, bf16[1,64,512]{2,1,0:T(8,128)(2,1)S(1)} %collective-permute-done.4.refs_2_, ...), custom_call_target="tpu_custom_call" | custom-call | flops 1000000000 | bytes 4194304 | tf_op jit(solution)/shard_map/pallas_call | solution.py:689
  27.2 0.1 collective-permute-start.9
  27.3 0.0 copy-start.1
  27.3 1.3 %shard_map.126 = (bf16[48,512]{1,0:T(8,128)(2,1)S(1)}, bf16[64,1024]{1,0:T(8,128)(2,1)S(1)}, bf16[64,1024]{1,0:T(8,128)(2,1)S(1)}) custom-call(bf16[128,192]{1,0:T(8,128)(2,1)S(1)} %get-tuple-element.60.grid_columns_ref, bf16[128,256]{1,0:T(8,128)(2,1)S(1)} %get-tuple-element.61.mesh_columns_ref, bf16[448,256]{1,0:T(8,128)(2,1)S(1)} %get-tuple-element.62.hot_ref, ...), custom_call_target="tpu_custom_call" | custom-call | flops 1000000000 | bytes 4194304 | tf_op jit(solution)/shard_map/pallas_call | solution.py:689
  28.6 0.6 %collective-permute-start.6 = (bf16[64,1024]{1,0:T(8,128)(2,1)S(1)}, bf16[64,1024]{1,0:T(8,128)(2,1)S(1)}, u32[]{:S(2)}, u32[]{:S(2)}) collective-permute-start(bf16[64,1024]{1,0:T(8,128)(2,1)S(1)} %get-tuple-element.73), channel_id=1, source_target_pairs={{0,1},{1,0},{2,3},{3,2},{4,5},{5,4},{6,7},{7,6},{8,9},{9,8},{10,11... | collective-permute-start | bytes 393224 | tf_op jit(solution)/shard_map/ppermute | solution.py:702
  29.2 0.0 collective-permute-done.9
  29.2 1.6 %collective-permute-start.10 = (bf16[64,1024]{1,0:T(8,128)(2,1)S(1)}, bf16[64,1024]{1,0:T(8,128)(2,1)S(1)}, u32[]{:S(2)}, u32[]{:S(2)}) collective-permute-start(bf16[64,1024]{1,0:T(8,128)(2,1)S(1)} %add_convert_fusion.1), channel_id=1, source_target_pairs={{0,2},{1,3},{2,0},{3,1},{4,6},{5,7},{6,4},{7,5},{8,10},{9,11},{10,... | collective-permute-start | bytes 393224 | tf_op jit(solution)/shard_map/ppermute | solution.py:702
  30.8 0.0 collective-permute-done.6
  30.8 1.0 %collective-permute-start.7 = (bf16[64,1024]{1,0:T(8,128)(2,1)S(1)}, bf16[64,1024]{1,0:T(8,128)(2,1)S(1)}, u32[]{:S(2)}, u32[]{:S(2)}) collective-permute-start(bf16[64,1024]{1,0:T(8,128)(2,1)S(1)} %add_convert_fusion.3), channel_id=1, source_target_pairs={{0,2},{1,3},{2,0},{3,1},{4,6},{5,7},{6,4},{7,5},{8,10},{9,11},{10,... | collective-permute-start | bytes 393224 | tf_op jit(solution)/shard_map/ppermute | solution.py:702
  31.8 1.1 %shard_map.127 = (bf16[1,128,512]{2,1,0:T(8,128)(2,1)}, bf16[1,64,512]{2,1,0:T(8,128)(2,1)}) custom-call(bf16[512,1536]{1,0:T(8,128)(2,1)S(1)} %get-tuple-element.44.refs_4_.turned_ref, s32[3,1,16]{2,1,0:T(1,128)S(1)} %bitcast.6, bf16[48,512]{1,0:T(8,128)(2,1)S(1)} %get-tuple-element.75.own_slot_ref, ...), custom_call_target="tpu_custom_call" | custom-call | flops 100000000 | bytes 4194304 | tf_op jit(solution)/shard_map/pallas_call | solution.py:689
  32.9 2.8 %collective-permute-done.10 = bf16[64,1024]{1,0:T(8,128)(2,1)S(1)} collective-permute-done((bf16[64,1024]{1,0:T(8,128)(2,1)S(1)}, bf16[64,1024]{1,0:T(8,128)(2,1)S(1)}, u32[]{:S(2)}, u32[]{:S(2)}) %collective-permute-start.10) | collective-permute-done | bytes 131104 | tf_op jit(solution)/shard_map/ppermute | solution.py:702
  35.7 0.1 collective-permute-start.11
  35.8 1.8 %collective-permute-done.7 = bf16[64,1024]{1,0:T(8,128)(2,1)S(1)} collective-permute-done((bf16[64,1024]{1,0:T(8,128)(2,1)S(1)}, bf16[64,1024]{1,0:T(8,128)(2,1)S(1)}, u32[]{:S(2)}, u32[]{:S(2)}) %collective-permute-start.7) | collective-permute-done | bytes 131104 | tf_op jit(solution)/shard_map/ppermute | solution.py:702
  37.6 0.1 collective-permute-start.8
  37.6 0.9 %shard_map.128.settled_ref = f32[128,2048]{1,0:T(8,128)} custom-call(bf16[64,1024]{1,0:T(8,128)(2,1)S(1)} %add_convert_fusion.2.one_ref, bf16[64,1024]{1,0:T(8,128)(2,1)S(1)} %add_convert_fusion.two_ref, bf16[64,1024]{1,0:T(8,128)(2,1)S(1)} %collective-permute-done.11.other_two_ref), custom_call_target="tpu_custom_call" | custom-call | tf_op jit(solution)/shard_map/pallas_call | solution.py:912
  38.6 0.4 collective-permute-done.8.other_one_ref
  39.0 0.7 %shard_map.129 = f32[128,2048]{1,0:T(8,128)} custom-call(bf16[64,1024]{1,0:T(8,128)(2,1)S(1)} %collective-permute-done.8.other_one_ref, f32[128,2048]{1,0:T(8,128)} %shard_map.128.settled_ref), custom_call_target="tpu_custom_call", output_to_operand_aliasing={{}: (1, {})} | custom-call | tf_op jit(solution)/shard_map/pallas_call | solution.py:920
  (9 shorter events, 0.1 us)
Async XLA Ops:
  0.6 14.8 %copy-start = (bf16[1,64,512]{2,1,0:T(8,128)(2,1)S(1)}, bf16[1,64,512]{2,1,0:T(8,128)(2,1)}, u32[]{:S(2)}) copy-start(bf16[1,64,512]{2,1,0:T(8,128)(2,1)} %refs_0_.3) | copy-start | bytes 196612
  1.9 13.6 %collective-permute-start = (bf16[120,512]{1,0:T(8,128)(2,1)S(1)}, bf16[120,512]{1,0:T(8,128)(2,1)S(1)}, u32[]{:S(2)}, u32[]{:S(2)}) collective-permute-start(bf16[120,512]{1,0:T(8,128)(2,1)S(1)} %shard_map.121.refs_0_), channel_id=1, source_target_pairs={{0,8},{4,12},{8,0},{12,4},{1,9},{5,13},{9,1},{13,5},{2,10},{6,14},... | collective-permute-start | bytes 368648 | tf_op jit(solution)/shard_map/ppermute | solution.py:707
  6.0 9.5 %collective-permute-start.1 = (bf16[120,512]{1,0:T(8,128)(2,1)S(1)}, bf16[120,512]{1,0:T(8,128)(2,1)S(1)}, u32[]{:S(2)}, u32[]{:S(2)}) collective-permute-start(bf16[120,512]{1,0:T(8,128)(2,1)S(1)} %shard_map.121.refs_0_), channel_id=1, source_target_pairs={{0,4},{4,8},{8,12},{12,0},{1,5},{5,9},{9,13},{13,1},{2,6},{6,10},{... | collective-permute-start | bytes 368648 | tf_op jit(solution)/shard_map/ppermute | solution.py:707
  7.6 12.8 %collective-permute-start.3 = (bf16[120,512]{1,0:T(8,128)(2,1)S(1)}, bf16[120,512]{1,0:T(8,128)(2,1)S(1)}, u32[]{:S(2)}, u32[]{:S(2)}) collective-permute-start(bf16[120,512]{1,0:T(8,128)(2,1)S(1)} %shard_map.121.refs_0_), channel_id=1, source_target_pairs={{0,12},{4,0},{8,4},{12,8},{1,13},{5,1},{9,5},{13,9},{2,14},{6,2},{... | collective-permute-start | bytes 368648 | tf_op jit(solution)/shard_map/ppermute | solution.py:707
  9.8 13.7 %collective-permute-start.2 = (bf16[1,64,512]{2,1,0:T(8,128)(2,1)}, bf16[1,64,512]{2,1,0:T(8,128)(2,1)S(1)}, u32[]{:S(2)}, u32[]{:S(2)}) collective-permute-start(bf16[1,64,512]{2,1,0:T(8,128)(2,1)} %refs_0_.3), channel_id=1, source_target_pairs={{0,4},{4,0},{8,12},{12,8},{1,5},{5,1},{9,13},{13,9},{2,6},{6,2},{1... | collective-permute-start | bytes 196616 | tf_op jit(solution)/shard_map/ppermute | solution.py:702
  15.5 8.7 %collective-permute-start.4 = (bf16[1,64,512]{2,1,0:T(8,128)(2,1)S(1)}, bf16[1,64,512]{2,1,0:T(8,128)(2,1)S(1)}, u32[]{:S(2)}, u32[]{:S(2)}) collective-permute-start(bf16[1,64,512]{2,1,0:T(8,128)(2,1)S(1)} %copy-done), channel_id=1, source_target_pairs={{0,8},{4,12},{8,0},{12,4},{1,9},{5,13},{9,1},{13,5},{2,10},{6,14},... | collective-permute-start | bytes 196616 | tf_op jit(solution)/shard_map/ppermute | solution.py:702
  19.9 6.1 %collective-permute-start.5 = (bf16[1,64,512]{2,1,0:T(8,128)(2,1)S(1)}, bf16[1,64,512]{2,1,0:T(8,128)(2,1)S(1)}, u32[]{:S(2)}, u32[]{:S(2)}) collective-permute-start(bf16[1,64,512]{2,1,0:T(8,128)(2,1)S(1)} %copy-done), channel_id=1, source_target_pairs={{0,12},{4,8},{8,4},{12,0},{1,13},{5,9},{9,5},{13,1},{2,14},{6,10},... | collective-permute-start | bytes 196616 | tf_op jit(solution)/shard_map/ppermute | solution.py:702
  27.2 1.9 %collective-permute-start.9 = (bf16[64,1024]{1,0:T(8,128)(2,1)S(1)}, bf16[64,1024]{1,0:T(8,128)(2,1)S(1)}, u32[]{:S(2)}, u32[]{:S(2)}) collective-permute-start(bf16[64,1024]{1,0:T(8,128)(2,1)S(1)} %get-tuple-element.82), channel_id=1, source_target_pairs={{0,1},{1,0},{2,3},{3,2},{4,5},{5,4},{6,7},{7,6},{8,9},{9,8},{10,11... | collective-permute-start | bytes 393224 | tf_op jit(solution)/shard_map/ppermute | solution.py:702
  27.3 4.5 %copy-start.1 = (s32[1,3,16]{2,0,1:T(1,128)S(1)}, s32[1,3,16]{2,0,1:T(1,128)}, u32[]{:S(2)}) copy-start(s32[1,3,16]{2,0,1:T(1,128)} %param.14) | copy-start | bytes 580
  28.6 2.1 %collective-permute-start.6 = (bf16[64,1024]{1,0:T(8,128)(2,1)S(1)}, bf16[64,1024]{1,0:T(8,128)(2,1)S(1)}, u32[]{:S(2)}, u32[]{:S(2)}) collective-permute-start(bf16[64,1024]{1,0:T(8,128)(2,1)S(1)} %get-tuple-element.73), channel_id=1, source_target_pairs={{0,1},{1,0},{2,3},{3,2},{4,5},{5,4},{6,7},{7,6},{8,9},{9,8},{10,11... | collective-permute-start | bytes 393224 | tf_op jit(solution)/shard_map/ppermute | solution.py:702
  29.2 6.4 %collective-permute-start.10 = (bf16[64,1024]{1,0:T(8,128)(2,1)S(1)}, bf16[64,1024]{1,0:T(8,128)(2,1)S(1)}, u32[]{:S(2)}, u32[]{:S(2)}) collective-permute-start(bf16[64,1024]{1,0:T(8,128)(2,1)S(1)} %add_convert_fusion.1), channel_id=1, source_target_pairs={{0,2},{1,3},{2,0},{3,1},{4,6},{5,7},{6,4},{7,5},{8,10},{9,11},{10,... | collective-permute-start | bytes 393224 | tf_op jit(solution)/shard_map/ppermute | solution.py:702
  30.8 6.7 %collective-permute-start.7 = (bf16[64,1024]{1,0:T(8,128)(2,1)S(1)}, bf16[64,1024]{1,0:T(8,128)(2,1)S(1)}, u32[]{:S(2)}, u32[]{:S(2)}) collective-permute-start(bf16[64,1024]{1,0:T(8,128)(2,1)S(1)} %add_convert_fusion.3), channel_id=1, source_target_pairs={{0,2},{1,3},{2,0},{3,1},{4,6},{5,7},{6,4},{7,5},{8,10},{9,11},{10,... | collective-permute-start | bytes 393224 | tf_op jit(solution)/shard_map/ppermute | solution.py:702
  35.7 2.0 %collective-permute-start.11 = (bf16[64,1024]{1,0:T(8,128)(2,1)S(1)}, bf16[64,1024]{1,0:T(8,128)(2,1)S(1)}, u32[]{:S(2)}, u32[]{:S(2)}) collective-permute-start(bf16[64,1024]{1,0:T(8,128)(2,1)S(1)} %add_convert_fusion.two_ref), channel_id=1, source_target_pairs={{0,1},{1,0},{2,3},{3,2},{4,5},{5,4},{6,7},{7,6},{8,9},{9,8},{10,11... | collective-permute-start | bytes 393224 | tf_op jit(solution)/shard_map/ppermute | solution.py:702
  37.6 1.4 %collective-permute-start.8 = (bf16[64,1024]{1,0:T(8,128)(2,1)S(1)}, bf16[64,1024]{1,0:T(8,128)(2,1)S(1)}, u32[]{:S(2)}, u32[]{:S(2)}) collective-permute-start(bf16[64,1024]{1,0:T(8,128)(2,1)S(1)} %add_convert_fusion.2.one_ref), channel_id=1, source_target_pairs={{0,1},{1,0},{2,3},{3,2},{4,5},{5,4},{6,7},{7,6},{8,9},{9,8},{10,11... | collective-permute-start | bytes 393224 | tf_op jit(solution)/shard_map/ppermute | solution.py:702

commit v22 on v20

--- a/solution.py
+++ b/solution.py
@@ -288,8 +288,8 @@
         ].T
 
 
-def edge_blocks(edges):
-    size = min(edges, 128)
+def edge_blocks(edges, size):
+    size = min(edges, size)
     return [(first, min(size, edges - first)) for first in range(0, edges, size)]
 
 
@@ -297,7 +297,7 @@
     regions = len(tables)
     edges = slope_ref.shape[0] // regions
     count = hot_ref.shape[0] // regions
-    work = [(d, first, size) for d in range(regions) for first, size in edge_blocks(edges)]
+    work = [(d, first, size) for d in range(regions) for first, size in edge_blocks(edges, 128)]
 
     def gathered(d, first, size):
         rows = slice(d * edges + first, d * edges + first + size)
@@ -445,7 +445,7 @@
     edges = edge_grad_ref.shape[0] // len(regions)
     count = turned_hot_ref.shape[1]
     blank = jnp.zeros((count - mesh_count, agg_grad_ref.shape[1]), BF16)
-    work = [(n, first, size) for n in range(len(regions)) for first, size in edge_blocks(edges)]
+    work = [(n, first, size) for n in range(len(regions)) for first, size in edge_blocks(edges, 256)]
 
     def at(n, first, size):
         return pl.ds(pl.multiple_of(regions[n] * edges + first, size), size)

time: 36.8 us -> 36.4 us (0.989)
  Pallas kernels: 12.3 us -> 11.8 us
    pallas_call x7, Pallas kernels: 10.7 us -> 10.2 us  [call(): pl.pallas_call(kernel, out_shape=[jax.ShapeDtypeStruct(shape, kind) for s...]
  transfers between devices with their start and end apart: 12 -> 12, of which waited for: 6 -> 6; matrix products, arithmetic and copies ran while one was open for 0% -> 0% of each run, Pallas kernels for 25% -> 24%
where the time goes in v22:
time: 36.4 us; the launch traced here: 36.2 us
  starting transfers between devices  13.3 us (37%)
  Pallas kernels  11.8 us (32%)
  waiting for transfers between devices  10.1 us (28%)
  between operations  0.78 us (2%)
    ppermute x12, starting transfers between devices, swap(): lax.ppermute(block, axis, [(i, i ^ bits) for i in range(lax.axis_size(axi...  13.3 us
    pallas_call x7, Pallas kernels, call(): pl.pallas_call(kernel, out_shape=[jax.ShapeDtypeStruct(shape, kind) for s...  10.2 us
    ppermute x12, waiting for transfers between devices, swap(): lax.ppermute(block, axis, [(i, i ^ bits) for i in range(lax.axis_size(axi...  10.1 us
    pallas_call x1, Pallas kernels, whole_sample_body(): pl.pallas_call(settle_kernel, out_shape=weight_shape, in_specs=[VMEM] * 3...  0.92 us
    pallas_call x1, Pallas kernels, whole_sample_body(): pl.pallas_call(finish_kernel, out_shape=weight_shape, in_specs=[VMEM, hbm...  0.73 us
  transfers between devices with their start and end apart: 12, of which 6 were waited for; matrix products, arithmetic and copies ran while one was open for 0% of the time, Pallas kernels for 24%

profile of v22, /device:TPU:0, one launch (start us, length us, event | category | flops | bytes accessed | tf_op | source)
XLA Modules:
  0.0 36.2 jit_solution(17825456871752547515)
XLA Ops:
  0.6 0.0 copy-start
  0.6 1.2 %shard_map.121.refs_0_ = bf16[120,512]{1,0:T(8,128)(2,1)S(1)} custom-call(bf16[1,128,512]{2,1,0:T(8,128)(2,1)} %refs_0_.1, bf16[1,64,512]{2,1,0:T(8,128)(2,1)} %refs_1_.1, s32[3,1,16]{2,1,0:T(1,128)} %bitcast.5, s32[1,256]{1,0:T(1,128)} %bitcast.7, s32[1,256]{1,0:T(1,128)} %bitcast.8, s32[1,4,8]{2,1,0:T(4,128)} %refs_5_.1, s32[1,256]{1,0:T(1,128)} %bitcast.9, ...), custom_call_target="tpu_custom_call" | custom-call | flops 10000000 | bytes 4194304 | tf_op jit(solution)/shard_map/pallas_call | solution.py:689
  1.9 4.1 %collective-permute-start.1 = (bf16[120,512]{1,0:T(8,128)(2,1)S(1)}, bf16[120,512]{1,0:T(8,128)(2,1)S(1)}, u32[]{:S(2)}, u32[]{:S(2)}) collective-permute-start(bf16[120,512]{1,0:T(8,128)(2,1)S(1)} %shard_map.121.refs_0_), channel_id=1, source_target_pairs={{0,8},{4,12},{8,0},{12,4},{1,9},{5,13},{9,1},{13,5},{2,10},{6,14},... | collective-permute-start | bytes 368648 | tf_op jit(solution)/shard_map/ppermute | solution.py:702
  6.0 1.3 %collective-permute-start.2 = (bf16[120,512]{1,0:T(8,128)(2,1)S(1)}, bf16[120,512]{1,0:T(8,128)(2,1)S(1)}, u32[]{:S(2)}, u32[]{:S(2)}) collective-permute-start(bf16[120,512]{1,0:T(8,128)(2,1)S(1)} %shard_map.121.refs_0_), channel_id=1, source_target_pairs={{0,12},{4,8},{8,4},{12,0},{1,13},{5,9},{9,5},{13,1},{2,14},{6,10},... | collective-permute-start | bytes 368648 | tf_op jit(solution)/shard_map/ppermute | solution.py:702
  7.3 0.2 collective-permute-start.3
  7.6 1.8 %collective-permute-start = (bf16[1,64,512]{2,1,0:T(8,128)(2,1)}, bf16[1,64,512]{2,1,0:T(8,128)(2,1)S(1)}, u32[]{:S(2)}, u32[]{:S(2)}) collective-permute-start(bf16[1,64,512]{2,1,0:T(8,128)(2,1)} %refs_0_.3), channel_id=1, source_target_pairs={{0,4},{4,0},{8,12},{12,8},{1,5},{5,1},{9,13},{13,9},{2,6},{6,2},{1... | collective-permute-start | bytes 196616 | tf_op jit(solution)/shard_map/ppermute | solution.py:702
  9.4 2.1 %shard_map.122 = (bf16[512,2048]{1,0:T(8,128)(2,1)S(1)}, bf16[512,1536]{1,0:T(8,128)(2,1)S(1)}) custom-call(bf16[512,2048]{1,0:T(8,128)(2,1)} %source_ref), custom_call_target="tpu_custom_call" | custom-call | flops 100000000 | bytes 4194304 | tf_op jit(solution)/shard_map/pallas_call | solution.py:689
  11.5 2.5 %collective-permute-start.5 = (bf16[1,64,512]{2,1,0:T(8,128)(2,1)S(1)}, bf16[1,64,512]{2,1,0:T(8,128)(2,1)S(1)}, u32[]{:S(2)}, u32[]{:S(2)}) collective-permute-start(bf16[1,64,512]{2,1,0:T(8,128)(2,1)S(1)} %copy-done), channel_id=1, source_target_pairs={{0,12},{4,8},{8,4},{12,0},{1,13},{5,9},{9,5},{13,1},{2,14},{6,10},... | collective-permute-start | bytes 196616 | tf_op jit(solution)/shard_map/ppermute | solution.py:702
  14.0 1.5 %collective-permute-done.1.refs_1_ = bf16[120,512]{1,0:T(8,128)(2,1)S(1)} collective-permute-done((bf16[120,512]{1,0:T(8,128)(2,1)S(1)}, bf16[120,512]{1,0:T(8,128)(2,1)S(1)}, u32[]{:S(2)}, u32[]{:S(2)}) %collective-permute-start.1) | collective-permute-done | bytes 122912 | tf_op jit(solution)/shard_map/ppermute | solution.py:702
  15.5 0.0 collective-permute-start.4
  15.5 0.0 collective-permute-done.2.refs_2_
  15.5 1.8 %collective-permute-done.3.refs_3_ = bf16[120,512]{1,0:T(8,128)(2,1)S(1)} collective-permute-done((bf16[120,512]{1,0:T(8,128)(2,1)S(1)}, bf16[120,512]{1,0:T(8,128)(2,1)S(1)}, u32[]{:S(2)}, u32[]{:S(2)}) %collective-permute-start.3) | collective-permute-done | bytes 122912 | tf_op jit(solution)/shard_map/ppermute | solution.py:702
  17.2 3.1 %shard_map.123 = (bf16[192,512]{1,0:T(8,128)(2,1)S(1)}, bf16[256,512]{1,0:T(8,128)(2,1)S(1)}, bf16[256,512]{1,0:T(8,128)(2,1)S(1)}, bf16[128,512]{1,0:T(8,128)(2...) custom-call(bf16[120,512]{1,0:T(8,128)(2,1)S(1)} %shard_map.121.refs, ...), custom_call_target="tpu_custom_call" | custom-call | flops 2000000000 | bytes 4194304 | tf_op jit(solution)/shard_map/pallas_call | solution.py:689
  20.4 0.0 collective-permute-done.refs_1_
  20.4 0.6 %shard_map.124 = (f32[192,512]{1,0:T(8,128)S(1)}, bf16[128,192]{1,0:T(8,128)(2,1)S(1)}, bf16[128,256]{1,0:T(8,128)(2,1)S(1)}, bf16[128,128]{1,0:T(8,128)(2,1)S(1)}, bf16[128,256]{1,0:T(8,128)(2,1)S(1)}) custom-call(bf16[1,64,512]{2,1,0:T(8,128)(2,1)S(1)} %copy-done, bf16[1,64,512]{2,1,0:T(8,128)(2,1)S(1)} %collective-permute-done.refs_1_, ...), custom_call_target="tpu_custom_call" | custom-call | flops 1000000000 | bytes 4194304 | tf_op jit(solution)/shard_map/pallas_call | solution.py:689
  20.9 1.9 %collective-permute-done.4.refs_2_ = bf16[1,64,512]{2,1,0:T(8,128)(2,1)S(1)} collective-permute-done((bf16[1,64,512]{2,1,0:T(8,128)(2,1)S(1)}, bf16[1,64,512]{2,1,0:T(8,128)(2,1)S(1)}, u32[]{:S(2)}, u32[]{:S(2)}) %collective-permute-start.4) | collective-permute-done | bytes 65568 | tf_op jit(solution)/shard_map/ppermute | solution.py:702
  22.9 1.1 %shard_map.125 = (f32[256,512]{1,0:T(8,128)S(1)}, bf16[64,1024]{1,0:T(8,128)(2,1)S(1)}, bf16[64,1024]{1,0:T(8,128)(2,1)S(1)}) custom-call(bf16[1,64,512]{2,1,0:T(8,128)(2,1)S(1)} %copy-done, bf16[1,64,512]{2,1,0:T(8,128)(2,1)S(1)} %collective-permute-done.refs_1_, bf16[1,64,512]{2,1,0:T(8,128)(2,1)S(1)} %collective-permute-done.4.refs_2_, ...), custom_call_target="tpu_custom_call" | custom-call | flops 1000000000 | bytes 4194304 | tf_op jit(solution)/shard_map/pallas_call | solution.py:689
  24.0 0.1 collective-permute-start.9
  24.1 0.0 copy-start.1
  24.1 1.1 %shard_map.126 = (bf16[48,512]{1,0:T(8,128)(2,1)S(1)}, bf16[64,1024]{1,0:T(8,128)(2,1)S(1)}, bf16[64,1024]{1,0:T(8,128)(2,1)S(1)}) custom-call(bf16[128,192]{1,0:T(8,128)(2,1)S(1)} %get-tuple-element.60.grid_columns_ref, bf16[128,256]{1,0:T(8,128)(2,1)S(1)} %get-tuple-element.61.mesh_columns_ref, bf16[448,256]{1,0:T(8,128)(2,1)S(1)} %get-tuple-element.62.hot_ref, ...), custom_call_target="tpu_custom_call" | custom-call | flops 1000000000 | bytes 4194304 | tf_op jit(solution)/shard_map/pallas_call | solution.py:689
  25.1 0.5 %collective-permute-start.6 = (bf16[64,1024]{1,0:T(8,128)(2,1)S(1)}, bf16[64,1024]{1,0:T(8,128)(2,1)S(1)}, u32[]{:S(2)}, u32[]{:S(2)}) collective-permute-start(bf16[64,1024]{1,0:T(8,128)(2,1)S(1)} %get-tuple-element.75), channel_id=1, source_target_pairs={{0,1},{1,0},{2,3},{3,2},{4,5},{5,4},{6,7},{7,6},{8,9},{9,8},{10,11... | collective-permute-start | bytes 393224 | tf_op jit(solution)/shard_map/ppermute | solution.py:702
  25.7 1.6 %collective-permute-start.10 = (bf16[64,1024]{1,0:T(8,128)(2,1)S(1)}, bf16[64,1024]{1,0:T(8,128)(2,1)S(1)}, u32[]{:S(2)}, u32[]{:S(2)}) collective-permute-start(bf16[64,1024]{1,0:T(8,128)(2,1)S(1)} %add_convert_fusion.1), channel_id=1, source_target_pairs={{0,2},{1,3},{2,0},{3,1},{4,6},{5,7},{6,4},{7,5},{8,10},{9,11},{10,... | collective-permute-start | bytes 393224 | tf_op jit(solution)/shard_map/ppermute | solution.py:702
  27.3 0.0 collective-permute-done.6
  27.4 1.0 %collective-permute-start.7 = (bf16[64,1024]{1,0:T(8,128)(2,1)S(1)}, bf16[64,1024]{1,0:T(8,128)(2,1)S(1)}, u32[]{:S(2)}, u32[]{:S(2)}) collective-permute-start(bf16[64,1024]{1,0:T(8,128)(2,1)S(1)} %add_convert_fusion.3), channel_id=1, source_target_pairs={{0,2},{1,3},{2,0},{3,1},{4,6},{5,7},{6,4},{7,5},{8,10},{9,11},{10,... | collective-permute-start | bytes 393224 | tf_op jit(solution)/shard_map/ppermute | solution.py:702
  28.3 1.1 %shard_map.127 = (bf16[1,128,512]{2,1,0:T(8,128)(2,1)}, bf16[1,64,512]{2,1,0:T(8,128)(2,1)}) custom-call(bf16[512,1536]{1,0:T(8,128)(2,1)S(1)} %get-tuple-element.47.refs_4_.turned_ref, s32[3,1,16]{2,1,0:T(1,128)S(1)} %bitcast.6, bf16[48,512]{1,0:T(8,128)(2,1)S(1)} %get-tuple-element.77.own_slot_ref, ...), custom_call_target="tpu_custom_call" | custom-call | flops 100000000 | bytes 4194304 | tf_op jit(solution)/shard_map/pallas_call | solution.py:689
  29.4 2.7 %collective-permute-done.10 = bf16[64,1024]{1,0:T(8,128)(2,1)S(1)} collective-permute-done((bf16[64,1024]{1,0:T(8,128)(2,1)S(1)}, bf16[64,1024]{1,0:T(8,128)(2,1)S(1)}, u32[]{:S(2)}, u32[]{:S(2)}) %collective-permute-start.10) | collective-permute-done | bytes 131104 | tf_op jit(solution)/shard_map/ppermute | solution.py:702
  32.2 0.1 collective-permute-start.11
  32.3 1.8 %collective-permute-done.7 = bf16[64,1024]{1,0:T(8,128)(2,1)S(1)} collective-permute-done((bf16[64,1024]{1,0:T(8,128)(2,1)S(1)}, bf16[64,1024]{1,0:T(8,128)(2,1)S(1)}, u32[]{:S(2)}, u32[]{:S(2)}) %collective-permute-start.7) | collective-permute-done | bytes 131104 | tf_op jit(solution)/shard_map/ppermute | solution.py:702
  34.1 0.1 collective-permute-start.8
  34.1 0.9 %shard_map.128.settled_ref = f32[128,2048]{1,0:T(8,128)} custom-call(bf16[64,1024]{1,0:T(8,128)(2,1)S(1)} %add_convert_fusion.2.one_ref, bf16[64,1024]{1,0:T(8,128)(2,1)S(1)} %add_convert_fusion.two_ref, bf16[64,1024]{1,0:T(8,128)(2,1)S(1)} %collective-permute-done.11.other_two_ref), custom_call_target="tpu_custom_call" | custom-call | tf_op jit(solution)/shard_map/pallas_call | solution.py:911
  35.1 0.4 %collective-permute-done.8.other_one_ref = bf16[64,1024]{1,0:T(8,128)(2,1)S(1)} collective-permute-done((bf16[64,1024]{1,0:T(8,128)(2,1)S(1)}, bf16[64,1024]{1,0:T(8,128)(2,1)S(1)}, u32[]{:S(2)}, u32[]{:S(2)}) %collective-permute-start.8) | collective-permute-done | bytes 131104 | tf_op jit(solution)/shard_map/ppermute | solution.py:702
  35.5 0.7 %shard_map.129 = f32[128,2048]{1,0:T(8,128)} custom-call(bf16[64,1024]{1,0:T(8,128)(2,1)S(1)} %collective-permute-done.8.other_one_ref, f32[128,2048]{1,0:T(8,128)} %shard_map.128.settled_ref), custom_call_target="tpu_custom_call", output_to_operand_aliasing={{}: (1, {})} | custom-call | tf_op jit(solution)/shard_map/pallas_call | solution.py:919
  (9 shorter events, 0.1 us)
Async XLA Ops:
  0.6 10.8 %copy-start = (bf16[1,64,512]{2,1,0:T(8,128)(2,1)S(1)}, bf16[1,64,512]{2,1,0:T(8,128)(2,1)}, u32[]{:S(2)}) copy-start(bf16[1,64,512]{2,1,0:T(8,128)(2,1)} %refs_0_.3) | copy-start | bytes 196612
  1.9 13.6 %collective-permute-start.1 = (bf16[120,512]{1,0:T(8,128)(2,1)S(1)}, bf16[120,512]{1,0:T(8,128)(2,1)S(1)}, u32[]{:S(2)}, u32[]{:S(2)}) collective-permute-start(bf16[120,512]{1,0:T(8,128)(2,1)S(1)} %shard_map.121.refs_0_), channel_id=1, source_target_pairs={{0,8},{4,12},{8,0},{12,4},{1,9},{5,13},{9,1},{13,5},{2,10},{6,14},... | collective-permute-start | bytes 368648 | tf_op jit(solution)/shard_map/ppermute | solution.py:702
  6.0 9.5 %collective-permute-start.2 = (bf16[120,512]{1,0:T(8,128)(2,1)S(1)}, bf16[120,512]{1,0:T(8,128)(2,1)S(1)}, u32[]{:S(2)}, u32[]{:S(2)}) collective-permute-start(bf16[120,512]{1,0:T(8,128)(2,1)S(1)} %shard_map.121.refs_0_), channel_id=1, source_target_pairs={{0,12},{4,8},{8,4},{12,0},{1,13},{5,9},{9,5},{13,1},{2,14},{6,10},... | collective-permute-start | bytes 368648 | tf_op jit(solution)/shard_map/ppermute | solution.py:702
  7.3 9.9 %collective-permute-start.3 = (bf16[120,512]{1,0:T(8,128)(2,1)S(1)}, bf16[120,512]{1,0:T(8,128)(2,1)S(1)}, u32[]{:S(2)}, u32[]{:S(2)}) collective-permute-start(bf16[120,512]{1,0:T(8,128)(2,1)S(1)} %shard_map.121.refs_0_), channel_id=1, source_target_pairs={{0,4},{4,0},{8,12},{12,8},{1,5},{5,1},{9,13},{13,9},{2,6},{6,2},{1... | collective-permute-start | bytes 368648 | tf_op jit(solution)/shard_map/ppermute | solution.py:702
  7.6 12.8 %collective-permute-start = (bf16[1,64,512]{2,1,0:T(8,128)(2,1)}, bf16[1,64,512]{2,1,0:T(8,128)(2,1)S(1)}, u32[]{:S(2)}, u32[]{:S(2)}) collective-permute-start(bf16[1,64,512]{2,1,0:T(8,128)(2,1)} %refs_0_.3), channel_id=1, source_target_pairs={{0,4},{4,0},{8,12},{12,8},{1,5},{5,1},{9,13},{13,9},{2,6},{6,2},{1... | collective-permute-start | bytes 196616 | tf_op jit(solution)/shard_map/ppermute | solution.py:702
  11.5 9.5 %collective-permute-start.5 = (bf16[1,64,512]{2,1,0:T(8,128)(2,1)S(1)}, bf16[1,64,512]{2,1,0:T(8,128)(2,1)S(1)}, u32[]{:S(2)}, u32[]{:S(2)}) collective-permute-start(bf16[1,64,512]{2,1,0:T(8,128)(2,1)S(1)} %copy-done), channel_id=1, source_target_pairs={{0,12},{4,8},{8,4},{12,0},{1,13},{5,9},{9,5},{13,1},{2,14},{6,10},... | collective-permute-start | bytes 196616 | tf_op jit(solution)/shard_map/ppermute | solution.py:702
  15.5 7.4 %collective-permute-start.4 = (bf16[1,64,512]{2,1,0:T(8,128)(2,1)S(1)}, bf16[1,64,512]{2,1,0:T(8,128)(2,1)S(1)}, u32[]{:S(2)}, u32[]{:S(2)}) collective-permute-start(bf16[1,64,512]{2,1,0:T(8,128)(2,1)S(1)} %copy-done), channel_id=1, source_target_pairs={{0,8},{4,12},{8,0},{12,4},{1,9},{5,13},{9,1},{13,5},{2,10},{6,14},... | collective-permute-start | bytes 196616 | tf_op jit(solution)/shard_map/ppermute | solution.py:702
  24.0 1.7 %collective-permute-start.9 = (bf16[64,1024]{1,0:T(8,128)(2,1)S(1)}, bf16[64,1024]{1,0:T(8,128)(2,1)S(1)}, u32[]{:S(2)}, u32[]{:S(2)}) collective-permute-start(bf16[64,1024]{1,0:T(8,128)(2,1)S(1)} %get-tuple-element.84), channel_id=1, source_target_pairs={{0,1},{1,0},{2,3},{3,2},{4,5},{5,4},{6,7},{7,6},{8,9},{9,8},{10,11... | collective-permute-start | bytes 393224 | tf_op jit(solution)/shard_map/ppermute | solution.py:702
  24.1 4.3 %copy-start.1 = (s32[1,3,16]{2,0,1:T(1,128)S(1)}, s32[1,3,16]{2,0,1:T(1,128)}, u32[]{:S(2)}) copy-start(s32[1,3,16]{2,0,1:T(1,128)} %param.14) | copy-start | bytes 580
  25.1 2.2 %collective-permute-start.6 = (bf16[64,1024]{1,0:T(8,128)(2,1)S(1)}, bf16[64,1024]{1,0:T(8,128)(2,1)S(1)}, u32[]{:S(2)}, u32[]{:S(2)}) collective-permute-start(bf16[64,1024]{1,0:T(8,128)(2,1)S(1)} %get-tuple-element.75), channel_id=1, source_target_pairs={{0,1},{1,0},{2,3},{3,2},{4,5},{5,4},{6,7},{7,6},{8,9},{9,8},{10,11... | collective-permute-start | bytes 393224 | tf_op jit(solution)/shard_map/ppermute | solution.py:702
  25.7 6.4 %collective-permute-start.10 = (bf16[64,1024]{1,0:T(8,128)(2,1)S(1)}, bf16[64,1024]{1,0:T(8,128)(2,1)S(1)}, u32[]{:S(2)}, u32[]{:S(2)}) collective-permute-start(bf16[64,1024]{1,0:T(8,128)(2,1)S(1)} %add_convert_fusion.1), channel_id=1, source_target_pairs={{0,2},{1,3},{2,0},{3,1},{4,6},{5,7},{6,4},{7,5},{8,10},{9,11},{10,... | collective-permute-start | bytes 393224 | tf_op jit(solution)/shard_map/ppermute | solution.py:702
  27.4 6.7 %collective-permute-start.7 = (bf16[64,1024]{1,0:T(8,128)(2,1)S(1)}, bf16[64,1024]{1,0:T(8,128)(2,1)S(1)}, u32[]{:S(2)}, u32[]{:S(2)}) collective-permute-start(bf16[64,1024]{1,0:T(8,128)(2,1)S(1)} %add_convert_fusion.3), channel_id=1, source_target_pairs={{0,2},{1,3},{2,0},{3,1},{4,6},{5,7},{6,4},{7,5},{8,10},{9,11},{10,... | collective-permute-start | bytes 393224 | tf_op jit(solution)/shard_map/ppermute | solution.py:702
  32.2 2.0 %collective-permute-start.11 = (bf16[64,1024]{1,0:T(8,128)(2,1)S(1)}, bf16[64,1024]{1,0:T(8,128)(2,1)S(1)}, u32[]{:S(2)}, u32[]{:S(2)}) collective-permute-start(bf16[64,1024]{1,0:T(8,128)(2,1)S(1)} %add_convert_fusion.two_ref), channel_id=1, source_target_pairs={{0,1},{1,0},{2,3},{3,2},{4,5},{5,4},{6,7},{7,6},{8,9},{9,8},{10,11... | collective-permute-start | bytes 393224 | tf_op jit(solution)/shard_map/ppermute | solution.py:702
  34.1 1.4 %collective-permute-start.8 = (bf16[64,1024]{1,0:T(8,128)(2,1)S(1)}, bf16[64,1024]{1,0:T(8,128)(2,1)S(1)}, u32[]{:S(2)}, u32[]{:S(2)}) collective-permute-start(bf16[64,1024]{1,0:T(8,128)(2,1)S(1)} %add_convert_fusion.2.one_ref), channel_id=1, source_target_pairs={{0,1},{1,0},{2,3},{3,2},{4,5},{5,4},{6,7},{7,6},{8,9},{9,8},{10,11... | collective-permute-start | bytes 393224 | tf_op jit(solution)/shard_map/ppermute | solution.py:702

commit v23 on v22

--- a/solution.py
+++ b/solution.py
@@ -297,7 +297,7 @@
     regions = len(tables)
     edges = slope_ref.shape[0] // regions
     count = hot_ref.shape[0] // regions
-    work = [(d, first, size) for d in range(regions) for first, size in edge_blocks(edges, 128)]
+    work = [(d, first, size) for d in range(regions) for first, size in edge_blocks(edges, 256)]
 
     def gathered(d, first, size):
         rows = slice(d * edges + first, d * edges + first + size)

time: 36.4 us -> 36.4 us (level)
  waiting for transfers between devices: 10.1 us -> 10.5 us
    ppermute x12, waiting for transfers between devices: 10.1 us -> 10.5 us  [swap(): lax.ppermute(block, axis, [(i, i ^ bits) for i in range(lax.axis_size(axi...]
    pallas_call x7, Pallas kernels: 10.2 us -> 9.82 us  [call(): pl.pallas_call(kernel, out_shape=[jax.ShapeDtypeStruct(shape, kind) for s...]
  transfers between devices with their start and end apart: 12 -> 12, of which waited for: 6 -> 6; matrix products, arithmetic and copies ran while one was open for 0% -> 0% of each run, Pallas kernels for 24% -> 23%
where the time goes in v23:
time: 36.4 us; the launch traced here: 36.2 us
  starting transfers between devices  13.3 us (37%)
  Pallas kernels  11.5 us (32%)
  waiting for transfers between devices  10.5 us (29%)
  between operations  0.78 us (2%)
    ppermute x12, starting transfers between devices, swap(): lax.ppermute(block, axis, [(i, i ^ bits) for i in range(lax.axis_size(axi...  13.3 us
    ppermute x12, waiting for transfers between devices, swap(): lax.ppermute(block, axis, [(i, i ^ bits) for i in range(lax.axis_size(axi...  10.5 us
    pallas_call x7, Pallas kernels, call(): pl.pallas_call(kernel, out_shape=[jax.ShapeDtypeStruct(shape, kind) for s...  9.82 us
    pallas_call x1, Pallas kernels, whole_sample_body(): pl.pallas_call(settle_kernel, out_shape=weight_shape, in_specs=[VMEM] * 3...  0.92 us
    pallas_call x1, Pallas kernels, whole_sample_body(): pl.pallas_call(finish_kernel, out_shape=weight_shape, in_specs=[VMEM, hbm...  0.73 us
  transfers between devices with their start and end apart: 12, of which 6 were waited for; matrix products, arithmetic and copies ran while one was open for 0% of the time, Pallas kernels for 23%

profile of v23, /device:TPU:0, one launch (start us, length us, event | category | flops | bytes accessed | tf_op | source)
XLA Modules:
  0.0 36.2 jit_solution(13844432270659199498)
XLA Ops:
  0.6 0.0 copy-start
  0.6 1.2 %shard_map.121.refs_0_ = bf16[120,512]{1,0:T(8,128)(2,1)S(1)} custom-call(bf16[1,128,512]{2,1,0:T(8,128)(2,1)} %refs_0_.1, bf16[1,64,512]{2,1,0:T(8,128)(2,1)} %refs_1_.1, s32[3,1,16]{2,1,0:T(1,128)} %bitcast.5, s32[1,256]{1,0:T(1,128)} %bitcast.7, s32[1,256]{1,0:T(1,128)} %bitcast.8, s32[1,4,8]{2,1,0:T(4,128)} %refs_5_.1, s32[1,256]{1,0:T(1,128)} %bitcast.9, ...), custom_call_target="tpu_custom_call" | custom-call | flops 10000000 | bytes 4194304 | tf_op jit(solution)/shard_map/pallas_call | solution.py:689
  1.9 4.1 %collective-permute-start.1 = (bf16[120,512]{1,0:T(8,128)(2,1)S(1)}, bf16[120,512]{1,0:T(8,128)(2,1)S(1)}, u32[]{:S(2)}, u32[]{:S(2)}) collective-permute-start(bf16[120,512]{1,0:T(8,128)(2,1)S(1)} %shard_map.121.refs_0_), channel_id=1, source_target_pairs={{0,8},{4,12},{8,0},{12,4},{1,9},{5,13},{9,1},{13,5},{2,10},{6,14},... | collective-permute-start | bytes 368648 | tf_op jit(solution)/shard_map/ppermute | solution.py:702
  6.0 1.3 %collective-permute-start.2 = (bf16[120,512]{1,0:T(8,128)(2,1)S(1)}, bf16[120,512]{1,0:T(8,128)(2,1)S(1)}, u32[]{:S(2)}, u32[]{:S(2)}) collective-permute-start(bf16[120,512]{1,0:T(8,128)(2,1)S(1)} %shard_map.121.refs_0_), channel_id=1, source_target_pairs={{0,12},{4,8},{8,4},{12,0},{1,13},{5,9},{9,5},{13,1},{2,14},{6,10},... | collective-permute-start | bytes 368648 | tf_op jit(solution)/shard_map/ppermute | solution.py:702
  7.3 0.2 collective-permute-start.3
  7.6 1.8 %collective-permute-start = (bf16[1,64,512]{2,1,0:T(8,128)(2,1)}, bf16[1,64,512]{2,1,0:T(8,128)(2,1)S(1)}, u32[]{:S(2)}, u32[]{:S(2)}) collective-permute-start(bf16[1,64,512]{2,1,0:T(8,128)(2,1)} %refs_0_.3), channel_id=1, source_target_pairs={{0,4},{4,0},{8,12},{12,8},{1,5},{5,1},{9,13},{13,9},{2,6},{6,2},{1... | collective-permute-start | bytes 196616 | tf_op jit(solution)/shard_map/ppermute | solution.py:702
  9.4 2.1 %shard_map.122 = (bf16[512,2048]{1,0:T(8,128)(2,1)S(1)}, bf16[512,1536]{1,0:T(8,128)(2,1)S(1)}) custom-call(bf16[512,2048]{1,0:T(8,128)(2,1)} %source_ref), custom_call_target="tpu_custom_call" | custom-call | flops 100000000 | bytes 4194304 | tf_op jit(solution)/shard_map/pallas_call | solution.py:689
  11.5 2.5 %collective-permute-start.5 = (bf16[1,64,512]{2,1,0:T(8,128)(2,1)S(1)}, bf16[1,64,512]{2,1,0:T(8,128)(2,1)S(1)}, u32[]{:S(2)}, u32[]{:S(2)}) collective-permute-start(bf16[1,64,512]{2,1,0:T(8,128)(2,1)S(1)} %copy-done), channel_id=1, source_target_pairs={{0,12},{4,8},{8,4},{12,0},{1,13},{5,9},{9,5},{13,1},{2,14},{6,10},... | collective-permute-start | bytes 196616 | tf_op jit(solution)/shard_map/ppermute | solution.py:702
  14.0 1.5 %collective-permute-done.1.refs_1_ = bf16[120,512]{1,0:T(8,128)(2,1)S(1)} collective-permute-done((bf16[120,512]{1,0:T(8,128)(2,1)S(1)}, bf16[120,512]{1,0:T(8,128)(2,1)S(1)}, u32[]{:S(2)}, u32[]{:S(2)}) %collective-permute-start.1) | collective-permute-done | bytes 122912 | tf_op jit(solution)/shard_map/ppermute | solution.py:702
  15.5 0.0 collective-permute-start.4
  15.5 0.0 collective-permute-done.2.refs_2_
  15.5 1.8 %collective-permute-done.3.refs_3_ = bf16[120,512]{1,0:T(8,128)(2,1)S(1)} collective-permute-done((bf16[120,512]{1,0:T(8,128)(2,1)S(1)}, bf16[120,512]{1,0:T(8,128)(2,1)S(1)}, u32[]{:S(2)}, u32[]{:S(2)}) %collective-permute-start.3) | collective-permute-done | bytes 122912 | tf_op jit(solution)/shard_map/ppermute | solution.py:702
  17.2 2.7 %shard_map.123 = (bf16[192,512]{1,0:T(8,128)(2,1)S(1)}, bf16[256,512]{1,0:T(8,128)(2,1)S(1)}, bf16[256,512]{1,0:T(8,128)(2,1)S(1)}, bf16[128,512]{1,0:T(8,128)(2...) custom-call(bf16[120,512]{1,0:T(8,128)(2,1)S(1)} %shard_map.121.refs, ...), custom_call_target="tpu_custom_call" | custom-call | flops 2000000000 | bytes 4194304 | tf_op jit(solution)/shard_map/pallas_call | solution.py:689
  20.0 0.0 collective-permute-done.refs_1_
  20.0 0.6 %shard_map.124 = (f32[192,512]{1,0:T(8,128)S(1)}, bf16[128,192]{1,0:T(8,128)(2,1)S(1)}, bf16[128,256]{1,0:T(8,128)(2,1)S(1)}, bf16[128,128]{1,0:T(8,128)(2,1)S(1)}, bf16[128,256]{1,0:T(8,128)(2,1)S(1)}) custom-call(bf16[1,64,512]{2,1,0:T(8,128)(2,1)S(1)} %copy-done, bf16[1,64,512]{2,1,0:T(8,128)(2,1)S(1)} %collective-permute-done.refs_1_, ...), custom_call_target="tpu_custom_call" | custom-call | flops 1000000000 | bytes 4194304 | tf_op jit(solution)/shard_map/pallas_call | solution.py:689
  20.6 0.0 collective-permute-done.5.refs_3_
  20.6 2.3 %collective-permute-done.4.refs_2_ = bf16[1,64,512]{2,1,0:T(8,128)(2,1)S(1)} collective-permute-done((bf16[1,64,512]{2,1,0:T(8,128)(2,1)S(1)}, bf16[1,64,512]{2,1,0:T(8,128)(2,1)S(1)}, u32[]{:S(2)}, u32[]{:S(2)}) %collective-permute-start.4) | collective-permute-done | bytes 65568 | tf_op jit(solution)/shard_map/ppermute | solution.py:702
  22.9 1.1 %shard_map.125 = (f32[256,512]{1,0:T(8,128)S(1)}, bf16[64,1024]{1,0:T(8,128)(2,1)S(1)}, bf16[64,1024]{1,0:T(8,128)(2,1)S(1)}) custom-call(bf16[1,64,512]{2,1,0:T(8,128)(2,1)S(1)} %copy-done, bf16[1,64,512]{2,1,0:T(8,128)(2,1)S(1)} %collective-permute-done.refs_1_, bf16[1,64,512]{2,1,0:T(8,128)(2,1)S(1)} %collective-permute-done.4.refs_2_, ...), custom_call_target="tpu_custom_call" | custom-call | flops 1000000000 | bytes 4194304 | tf_op jit(solution)/shard_map/pallas_call | solution.py:689
  24.0 0.1 collective-permute-start.9
  24.1 0.0 copy-start.1
  24.1 1.1 %shard_map.126 = (bf16[48,512]{1,0:T(8,128)(2,1)S(1)}, bf16[64,1024]{1,0:T(8,128)(2,1)S(1)}, bf16[64,1024]{1,0:T(8,128)(2,1)S(1)}) custom-call(bf16[128,192]{1,0:T(8,128)(2,1)S(1)} %get-tuple-element.60.grid_columns_ref, bf16[128,256]{1,0:T(8,128)(2,1)S(1)} %get-tuple-element.61.mesh_columns_ref, bf16[448,256]{1,0:T(8,128)(2,1)S(1)} %get-tuple-element.62.hot_ref, ...), custom_call_target="tpu_custom_call" | custom-call | flops 1000000000 | bytes 4194304 | tf_op jit(solution)/shard_map/pallas_call | solution.py:689
  25.1 0.5 %collective-permute-start.6 = (bf16[64,1024]{1,0:T(8,128)(2,1)S(1)}, bf16[64,1024]{1,0:T(8,128)(2,1)S(1)}, u32[]{:S(2)}, u32[]{:S(2)}) collective-permute-start(bf16[64,1024]{1,0:T(8,128)(2,1)S(1)} %get-tuple-element.75), channel_id=1, source_target_pairs={{0,1},{1,0},{2,3},{3,2},{4,5},{5,4},{6,7},{7,6},{8,9},{9,8},{10,11... | collective-permute-start | bytes 393224 | tf_op jit(solution)/shard_map/ppermute | solution.py:702
  25.7 1.6 %collective-permute-start.10 = (bf16[64,1024]{1,0:T(8,128)(2,1)S(1)}, bf16[64,1024]{1,0:T(8,128)(2,1)S(1)}, u32[]{:S(2)}, u32[]{:S(2)}) collective-permute-start(bf16[64,1024]{1,0:T(8,128)(2,1)S(1)} %add_convert_fusion.1), channel_id=1, source_target_pairs={{0,2},{1,3},{2,0},{3,1},{4,6},{5,7},{6,4},{7,5},{8,10},{9,11},{10,... | collective-permute-start | bytes 393224 | tf_op jit(solution)/shard_map/ppermute | solution.py:702
  27.4 1.0 %collective-permute-start.7 = (bf16[64,1024]{1,0:T(8,128)(2,1)S(1)}, bf16[64,1024]{1,0:T(8,128)(2,1)S(1)}, u32[]{:S(2)}, u32[]{:S(2)}) collective-permute-start(bf16[64,1024]{1,0:T(8,128)(2,1)S(1)} %add_convert_fusion.3), channel_id=1, source_target_pairs={{0,2},{1,3},{2,0},{3,1},{4,6},{5,7},{6,4},{7,5},{8,10},{9,11},{10,... | collective-permute-start | bytes 393224 | tf_op jit(solution)/shard_map/ppermute | solution.py:702
  28.3 1.1 %shard_map.127 = (bf16[1,128,512]{2,1,0:T(8,128)(2,1)}, bf16[1,64,512]{2,1,0:T(8,128)(2,1)}) custom-call(bf16[512,1536]{1,0:T(8,128)(2,1)S(1)} %get-tuple-element.47.refs_4_.turned_ref, s32[3,1,16]{2,1,0:T(1,128)S(1)} %bitcast.6, bf16[48,512]{1,0:T(8,128)(2,1)S(1)} %get-tuple-element.77.own_slot_ref, ...), custom_call_target="tpu_custom_call" | custom-call | flops 100000000 | bytes 4194304 | tf_op jit(solution)/shard_map/pallas_call | solution.py:689
  29.4 2.7 %collective-permute-done.10 = bf16[64,1024]{1,0:T(8,128)(2,1)S(1)} collective-permute-done((bf16[64,1024]{1,0:T(8,128)(2,1)S(1)}, bf16[64,1024]{1,0:T(8,128)(2,1)S(1)}, u32[]{:S(2)}, u32[]{:S(2)}) %collective-permute-start.10) | collective-permute-done | bytes 131104 | tf_op jit(solution)/shard_map/ppermute | solution.py:702
  32.2 0.1 collective-permute-start.11
  32.3 1.8 %collective-permute-done.7 = bf16[64,1024]{1,0:T(8,128)(2,1)S(1)} collective-permute-done((bf16[64,1024]{1,0:T(8,128)(2,1)S(1)}, bf16[64,1024]{1,0:T(8,128)(2,1)S(1)}, u32[]{:S(2)}, u32[]{:S(2)}) %collective-permute-start.7) | collective-permute-done | bytes 131104 | tf_op jit(solution)/shard_map/ppermute | solution.py:702
  34.1 0.1 collective-permute-start.8
  34.1 0.9 %shard_map.128.settled_ref = f32[128,2048]{1,0:T(8,128)} custom-call(bf16[64,1024]{1,0:T(8,128)(2,1)S(1)} %add_convert_fusion.2.one_ref, bf16[64,1024]{1,0:T(8,128)(2,1)S(1)} %add_convert_fusion.two_ref, bf16[64,1024]{1,0:T(8,128)(2,1)S(1)} %collective-permute-done.11.other_two_ref), custom_call_target="tpu_custom_call" | custom-call | tf_op jit(solution)/shard_map/pallas_call | solution.py:911
  35.1 0.4 %collective-permute-done.8.other_one_ref = bf16[64,1024]{1,0:T(8,128)(2,1)S(1)} collective-permute-done((bf16[64,1024]{1,0:T(8,128)(2,1)S(1)}, bf16[64,1024]{1,0:T(8,128)(2,1)S(1)}, u32[]{:S(2)}, u32[]{:S(2)}) %collective-permute-start.8) | collective-permute-done | bytes 131104 | tf_op jit(solution)/shard_map/ppermute | solution.py:702
  35.5 0.7 %shard_map.129 = f32[128,2048]{1,0:T(8,128)} custom-call(bf16[64,1024]{1,0:T(8,128)(2,1)S(1)} %collective-permute-done.8.other_one_ref, f32[128,2048]{1,0:T(8,128)} %shard_map.128.settled_ref), custom_call_target="tpu_custom_call", output_to_operand_aliasing={{}: (1, {})} | custom-call | tf_op jit(solution)/shard_map/pallas_call | solution.py:919
  (9 shorter events, 0.1 us)
Async XLA Ops:
  0.6 10.8 %copy-start = (bf16[1,64,512]{2,1,0:T(8,128)(2,1)S(1)}, bf16[1,64,512]{2,1,0:T(8,128)(2,1)}, u32[]{:S(2)}) copy-start(bf16[1,64,512]{2,1,0:T(8,128)(2,1)} %refs_0_.3) | copy-start | bytes 196612
  1.9 13.6 %collective-permute-start.1 = (bf16[120,512]{1,0:T(8,128)(2,1)S(1)}, bf16[120,512]{1,0:T(8,128)(2,1)S(1)}, u32[]{:S(2)}, u32[]{:S(2)}) collective-permute-start(bf16[120,512]{1,0:T(8,128)(2,1)S(1)} %shard_map.121.refs_0_), channel_id=1, source_target_pairs={{0,8},{4,12},{8,0},{12,4},{1,9},{5,13},{9,1},{13,5},{2,10},{6,14},... | collective-permute-start | bytes 368648 | tf_op jit(solution)/shard_map/ppermute | solution.py:702
  6.0 9.5 %collective-permute-start.2 = (bf16[120,512]{1,0:T(8,128)(2,1)S(1)}, bf16[120,512]{1,0:T(8,128)(2,1)S(1)}, u32[]{:S(2)}, u32[]{:S(2)}) collective-permute-start(bf16[120,512]{1,0:T(8,128)(2,1)S(1)} %shard_map.121.refs_0_), channel_id=1, source_target_pairs={{0,12},{4,8},{8,4},{12,0},{1,13},{5,9},{9,5},{13,1},{2,14},{6,10},... | collective-permute-start | bytes 368648 | tf_op jit(solution)/shard_map/ppermute | solution.py:702
  7.3 9.9 %collective-permute-start.3 = (bf16[120,512]{1,0:T(8,128)(2,1)S(1)}, bf16[120,512]{1,0:T(8,128)(2,1)S(1)}, u32[]{:S(2)}, u32[]{:S(2)}) collective-permute-start(bf16[120,512]{1,0:T(8,128)(2,1)S(1)} %shard_map.121.refs_0_), channel_id=1, source_target_pairs={{0,4},{4,0},{8,12},{12,8},{1,5},{5,1},{9,13},{13,9},{2,6},{6,2},{1... | collective-permute-start | bytes 368648 | tf_op jit(solution)/shard_map/ppermute | solution.py:702
  7.6 12.4 %collective-permute-start = (bf16[1,64,512]{2,1,0:T(8,128)(2,1)}, bf16[1,64,512]{2,1,0:T(8,128)(2,1)S(1)}, u32[]{:S(2)}, u32[]{:S(2)}) collective-permute-start(bf16[1,64,512]{2,1,0:T(8,128)(2,1)} %refs_0_.3), channel_id=1, source_target_pairs={{0,4},{4,0},{8,12},{12,8},{1,5},{5,1},{9,13},{13,9},{2,6},{6,2},{1... | collective-permute-start | bytes 196616 | tf_op jit(solution)/shard_map/ppermute | solution.py:702
  11.5 9.1 %collective-permute-start.5 = (bf16[1,64,512]{2,1,0:T(8,128)(2,1)S(1)}, bf16[1,64,512]{2,1,0:T(8,128)(2,1)S(1)}, u32[]{:S(2)}, u32[]{:S(2)}) collective-permute-start(bf16[1,64,512]{2,1,0:T(8,128)(2,1)S(1)} %copy-done), channel_id=1, source_target_pairs={{0,12},{4,8},{8,4},{12,0},{1,13},{5,9},{9,5},{13,1},{2,14},{6,10},... | collective-permute-start | bytes 196616 | tf_op jit(solution)/shard_map/ppermute | solution.py:702
  15.5 7.4 %collective-permute-start.4 = (bf16[1,64,512]{2,1,0:T(8,128)(2,1)S(1)}, bf16[1,64,512]{2,1,0:T(8,128)(2,1)S(1)}, u32[]{:S(2)}, u32[]{:S(2)}) collective-permute-start(bf16[1,64,512]{2,1,0:T(8,128)(2,1)S(1)} %copy-done), channel_id=1, source_target_pairs={{0,8},{4,12},{8,0},{12,4},{1,9},{5,13},{9,1},{13,5},{2,10},{6,14},... | collective-permute-start | bytes 196616 | tf_op jit(solution)/shard_map/ppermute | solution.py:702
  24.0 1.7 %collective-permute-start.9 = (bf16[64,1024]{1,0:T(8,128)(2,1)S(1)}, bf16[64,1024]{1,0:T(8,128)(2,1)S(1)}, u32[]{:S(2)}, u32[]{:S(2)}) collective-permute-start(bf16[64,1024]{1,0:T(8,128)(2,1)S(1)} %get-tuple-element.84), channel_id=1, source_target_pairs={{0,1},{1,0},{2,3},{3,2},{4,5},{5,4},{6,7},{7,6},{8,9},{9,8},{10,11... | collective-permute-start | bytes 393224 | tf_op jit(solution)/shard_map/ppermute | solution.py:702
  24.1 4.3 %copy-start.1 = (s32[1,3,16]{2,0,1:T(1,128)S(1)}, s32[1,3,16]{2,0,1:T(1,128)}, u32[]{:S(2)}) copy-start(s32[1,3,16]{2,0,1:T(1,128)} %param.14) | copy-start | bytes 580
  25.1 2.2 %collective-permute-start.6 = (bf16[64,1024]{1,0:T(8,128)(2,1)S(1)}, bf16[64,1024]{1,0:T(8,128)(2,1)S(1)}, u32[]{:S(2)}, u32[]{:S(2)}) collective-permute-start(bf16[64,1024]{1,0:T(8,128)(2,1)S(1)} %get-tuple-element.75), channel_id=1, source_target_pairs={{0,1},{1,0},{2,3},{3,2},{4,5},{5,4},{6,7},{7,6},{8,9},{9,8},{10,11... | collective-permute-start | bytes 393224 | tf_op jit(solution)/shard_map/ppermute | solution.py:702
  25.7 6.4 %collective-permute-start.10 = (bf16[64,1024]{1,0:T(8,128)(2,1)S(1)}, bf16[64,1024]{1,0:T(8,128)(2,1)S(1)}, u32[]{:S(2)}, u32[]{:S(2)}) collective-permute-start(bf16[64,1024]{1,0:T(8,128)(2,1)S(1)} %add_convert_fusion.1), channel_id=1, source_target_pairs={{0,2},{1,3},{2,0},{3,1},{4,6},{5,7},{6,4},{7,5},{8,10},{9,11},{10,... | collective-permute-start | bytes 393224 | tf_op jit(solution)/shard_map/ppermute | solution.py:702
  27.4 6.7 %collective-permute-start.7 = (bf16[64,1024]{1,0:T(8,128)(2,1)S(1)}, bf16[64,1024]{1,0:T(8,128)(2,1)S(1)}, u32[]{:S(2)}, u32[]{:S(2)}) collective-permute-start(bf16[64,1024]{1,0:T(8,128)(2,1)S(1)} %add_convert_fusion.3), channel_id=1, source_target_pairs={{0,2},{1,3},{2,0},{3,1},{4,6},{5,7},{6,4},{7,5},{8,10},{9,11},{10,... | collective-permute-start | bytes 393224 | tf_op jit(solution)/shard_map/ppermute | solution.py:702
  32.2 2.0 %collective-permute-start.11 = (bf16[64,1024]{1,0:T(8,128)(2,1)S(1)}, bf16[64,1024]{1,0:T(8,128)(2,1)S(1)}, u32[]{:S(2)}, u32[]{:S(2)}) collective-permute-start(bf16[64,1024]{1,0:T(8,128)(2,1)S(1)} %add_convert_fusion.two_ref), channel_id=1, source_target_pairs={{0,1},{1,0},{2,3},{3,2},{4,5},{5,4},{6,7},{7,6},{8,9},{9,8},{10,11... | collective-permute-start | bytes 393224 | tf_op jit(solution)/shard_map/ppermute | solution.py:702
  34.1 1.4 %collective-permute-start.8 = (bf16[64,1024]{1,0:T(8,128)(2,1)S(1)}, bf16[64,1024]{1,0:T(8,128)(2,1)S(1)}, u32[]{:S(2)}, u32[]{:S(2)}) collective-permute-start(bf16[64,1024]{1,0:T(8,128)(2,1)S(1)} %add_convert_fusion.2.one_ref), channel_id=1, source_target_pairs={{0,1},{1,0},{2,3},{3,2},{4,5},{5,4},{6,7},{7,6},{8,9},{9,8},{10,11... | collective-permute-start | bytes 393224 | tf_op jit(solution)/shard_map/ppermute | solution.py:702

commit v24 on v23

--- a/solution.py
+++ b/solution.py
@@ -765,13 +765,8 @@
         10**8,
         fetched=1,
     )
-    turned, early = lax.optimization_barrier((turned, cotangent))
-    packs[1], late = lax.optimization_barrier((packs[1], cotangent))
-    cotangents = (
-        [cotangent, swap(late, "space", steps[1])]
-        + [swap(early, "space", step) for step in steps[2:-1]]
-        + [near]
-    )
+    turned, cotangent = lax.optimization_barrier((turned, cotangent))
+    cotangents = [cotangent] + [swap(cotangent, "space", step) for step in steps[1:-1]] + [near]
     rows = regions * mesh_count
     slots = regions * mesh_cap
     (

time: 36.4 us -> 35.7 us (0.981)
  waiting for transfers between devices: 10.5 us -> 7.74 us
  starting transfers between devices: 13.3 us -> 15.4 us
    ppermute x12, waiting for transfers between devices: 10.5 us -> 7.74 us  [swap(): lax.ppermute(block, axis, [(i, i ^ bits) for i in range(lax.axis_size(axi...]
    ppermute x12, starting transfers between devices: 13.3 us -> 15.4 us  [swap(): lax.ppermute(block, axis, [(i, i ^ bits) for i in range(lax.axis_size(axi...]
  transfers between devices with their start and end apart: 12 -> 12, of which waited for: 6 -> 5; matrix products, arithmetic and copies ran while one was open for 0% -> 0% of each run, Pallas kernels for 23% -> 24%
where the time goes in v24:
time: 35.7 us; the launch traced here: 35.5 us
  starting transfers between devices  15.4 us (43%)
  Pallas kernels  11.5 us (32%)
  waiting for transfers between devices  7.74 us (22%)
  between operations  0.77 us (2%)
    ppermute x12, starting transfers between devices, swap(): lax.ppermute(block, axis, [(i, i ^ bits) for i in range(lax.axis_size(axi...  15.4 us
    pallas_call x7, Pallas kernels, call(): pl.pallas_call(kernel, out_shape=[jax.ShapeDtypeStruct(shape, kind) for s...  9.83 us
    ppermute x12, waiting for transfers between devices, swap(): lax.ppermute(block, axis, [(i, i ^ bits) for i in range(lax.axis_size(axi...  7.74 us
    pallas_call x1, Pallas kernels, whole_sample_body(): pl.pallas_call(settle_kernel, out_shape=weight_shape, in_specs=[VMEM] * 3...  0.92 us
    pallas_call x1, Pallas kernels, whole_sample_body(): pl.pallas_call(finish_kernel, out_shape=weight_shape, in_specs=[VMEM, hbm...  0.73 us
  transfers between devices with their start and end apart: 12, of which 5 were waited for; matrix products, arithmetic and copies ran while one was open for 0% of the time, Pallas kernels for 24%

profile of v24, /device:TPU:0, one launch (start us, length us, event | category | flops | bytes accessed | tf_op | source)
XLA Modules:
  0.0 35.5 jit_solution(14623321163541183677)
XLA Ops:
  0.6 0.0 copy-start
  0.6 1.2 %shard_map.121.refs_0_ = bf16[120,512]{1,0:T(8,128)(2,1)S(1)} custom-call(bf16[1,128,512]{2,1,0:T(8,128)(2,1)} %refs_0_.1, bf16[1,64,512]{2,1,0:T(8,128)(2,1)} %refs_1_.1, s32[3,1,16]{2,1,0:T(1,128)} %bitcast.5, s32[1,256]{1,0:T(1,128)} %bitcast.7, s32[1,256]{1,0:T(1,128)} %bitcast.8, s32[1,4,8]{2,1,0:T(4,128)} %refs_5_.1, s32[1,256]{1,0:T(1,128)} %bitcast.9, ...), custom_call_target="tpu_custom_call" | custom-call | flops 10000000 | bytes 4194304 | tf_op jit(solution)/shard_map/pallas_call | solution.py:689
  1.9 4.1 %collective-permute-start.1 = (bf16[120,512]{1,0:T(8,128)(2,1)S(1)}, bf16[120,512]{1,0:T(8,128)(2,1)S(1)}, u32[]{:S(2)}, u32[]{:S(2)}) collective-permute-start(bf16[120,512]{1,0:T(8,128)(2,1)S(1)} %shard_map.121.refs_0_), channel_id=1, source_target_pairs={{0,8},{4,12},{8,0},{12,4},{1,9},{5,13},{9,1},{13,5},{2,10},{6,14},... | collective-permute-start | bytes 368648 | tf_op jit(solution)/shard_map/ppermute | solution.py:702
  6.0 1.3 %collective-permute-start.2 = (bf16[120,512]{1,0:T(8,128)(2,1)S(1)}, bf16[120,512]{1,0:T(8,128)(2,1)S(1)}, u32[]{:S(2)}, u32[]{:S(2)}) collective-permute-start(bf16[120,512]{1,0:T(8,128)(2,1)S(1)} %shard_map.121.refs_0_), channel_id=1, source_target_pairs={{0,12},{4,8},{8,4},{12,0},{1,13},{5,9},{9,5},{13,1},{2,14},{6,10},... | collective-permute-start | bytes 368648 | tf_op jit(solution)/shard_map/ppermute | solution.py:702
  7.3 0.2 collective-permute-start.3
  7.6 1.8 %collective-permute-start = (bf16[1,64,512]{2,1,0:T(8,128)(2,1)}, bf16[1,64,512]{2,1,0:T(8,128)(2,1)S(1)}, u32[]{:S(2)}, u32[]{:S(2)}) collective-permute-start(bf16[1,64,512]{2,1,0:T(8,128)(2,1)} %refs_0_.3), channel_id=1, source_target_pairs={{0,4},{4,0},{8,12},{12,8},{1,5},{5,1},{9,13},{13,9},{2,6},{6,2},{1... | collective-permute-start | bytes 196616 | tf_op jit(solution)/shard_map/ppermute | solution.py:702
  9.4 2.1 %shard_map.122 = (bf16[512,2048]{1,0:T(8,128)(2,1)S(1)}, bf16[512,1536]{1,0:T(8,128)(2,1)S(1)}) custom-call(bf16[512,2048]{1,0:T(8,128)(2,1)} %source_ref), custom_call_target="tpu_custom_call" | custom-call | flops 100000000 | bytes 4194304 | tf_op jit(solution)/shard_map/pallas_call | solution.py:689
  11.5 1.8 %collective-permute-start.4 = (bf16[1,64,512]{2,1,0:T(8,128)(2,1)S(1)}, bf16[1,64,512]{2,1,0:T(8,128)(2,1)S(1)}, u32[]{:S(2)}, u32[]{:S(2)}) collective-permute-start(bf16[1,64,512]{2,1,0:T(8,128)(2,1)S(1)} %copy-done), channel_id=1, source_target_pairs={{0,8},{4,12},{8,0},{12,4},{1,9},{5,13},{9,1},{13,5},{2,10},{6,14},... | collective-permute-start | bytes 196616 | tf_op jit(solution)/shard_map/ppermute | solution.py:702
  13.2 2.3 %collective-permute-done.1.refs_1_ = bf16[120,512]{1,0:T(8,128)(2,1)S(1)} collective-permute-done((bf16[120,512]{1,0:T(8,128)(2,1)S(1)}, bf16[120,512]{1,0:T(8,128)(2,1)S(1)}, u32[]{:S(2)}, u32[]{:S(2)}) %collective-permute-start.1) | collective-permute-done | bytes 122912 | tf_op jit(solution)/shard_map/ppermute | solution.py:702
  15.5 2.8 %collective-permute-start.5 = (bf16[1,64,512]{2,1,0:T(8,128)(2,1)S(1)}, bf16[1,64,512]{2,1,0:T(8,128)(2,1)S(1)}, u32[]{:S(2)}, u32[]{:S(2)}) collective-permute-start(bf16[1,64,512]{2,1,0:T(8,128)(2,1)S(1)} %copy-done), channel_id=1, source_target_pairs={{0,12},{4,8},{8,4},{12,0},{1,13},{5,9},{9,5},{13,1},{2,14},{6,10},... | collective-permute-start | bytes 196616 | tf_op jit(solution)/shard_map/ppermute | solution.py:702
  18.3 0.0 collective-permute-done.2.refs_2_
  18.3 0.0 collective-permute-done.3.refs_3_
  18.3 2.7 %shard_map.123 = (bf16[192,512]{1,0:T(8,128)(2,1)S(1)}, bf16[256,512]{1,0:T(8,128)(2,1)S(1)}, bf16[256,512]{1,0:T(8,128)(2,1)S(1)}, bf16[128,512]{1,0:T(8,128)(2...) custom-call(bf16[120,512]{1,0:T(8,128)(2,1)S(1)} %shard_map.121.refs, ...), custom_call_target="tpu_custom_call" | custom-call | flops 2000000000 | bytes 4194304 | tf_op jit(solution)/shard_map/pallas_call | solution.py:689
  21.0 0.0 collective-permute-done.refs_1_
  21.0 0.6 %shard_map.124 = (f32[192,512]{1,0:T(8,128)S(1)}, bf16[128,192]{1,0:T(8,128)(2,1)S(1)}, bf16[128,256]{1,0:T(8,128)(2,1)S(1)}, bf16[128,128]{1,0:T(8,128)(2,1)S(1)}, bf16[128,256]{1,0:T(8,128)(2,1)S(1)}) custom-call(bf16[1,64,512]{2,1,0:T(8,128)(2,1)S(1)} %copy-done, bf16[1,64,512]{2,1,0:T(8,128)(2,1)S(1)} %collective-permute-done.refs_1_, ...), custom_call_target="tpu_custom_call" | custom-call | flops 1000000000 | bytes 4194304 | tf_op jit(solution)/shard_map/pallas_call | solution.py:689
  21.6 0.6 %collective-permute-done.4.refs_2_ = bf16[1,64,512]{2,1,0:T(8,128)(2,1)S(1)} collective-permute-done((bf16[1,64,512]{2,1,0:T(8,128)(2,1)S(1)}, bf16[1,64,512]{2,1,0:T(8,128)(2,1)S(1)}, u32[]{:S(2)}, u32[]{:S(2)}) %collective-permute-start.4) | collective-permute-done | bytes 65568 | tf_op jit(solution)/shard_map/ppermute | solution.py:702
  22.2 1.1 %shard_map.125 = (f32[256,512]{1,0:T(8,128)S(1)}, bf16[64,1024]{1,0:T(8,128)(2,1)S(1)}, bf16[64,1024]{1,0:T(8,128)(2,1)S(1)}) custom-call(bf16[1,64,512]{2,1,0:T(8,128)(2,1)S(1)} %copy-done, bf16[1,64,512]{2,1,0:T(8,128)(2,1)S(1)} %collective-permute-done.refs_1_, bf16[1,64,512]{2,1,0:T(8,128)(2,1)S(1)} %collective-permute-done.4.refs_2_, ...), custom_call_target="tpu_custom_call" | custom-call | flops 1000000000 | bytes 4194304 | tf_op jit(solution)/shard_map/pallas_call | solution.py:689
  23.3 0.1 collective-permute-start.9
  23.4 0.0 copy-start.1
  23.4 1.1 %shard_map.126 = (bf16[48,512]{1,0:T(8,128)(2,1)S(1)}, bf16[64,1024]{1,0:T(8,128)(2,1)S(1)}, bf16[64,1024]{1,0:T(8,128)(2,1)S(1)}) custom-call(bf16[128,192]{1,0:T(8,128)(2,1)S(1)} %get-tuple-element.58.grid_columns_ref, bf16[128,256]{1,0:T(8,128)(2,1)S(1)} %get-tuple-element.59.mesh_columns_ref, bf16[448,256]{1,0:T(8,128)(2,1)S(1)} %get-tuple-element.60.hot_ref, ...), custom_call_target="tpu_custom_call" | custom-call | flops 1000000000 | bytes 4194304 | tf_op jit(solution)/shard_map/pallas_call | solution.py:689
  24.4 0.5 %collective-permute-start.6 = (bf16[64,1024]{1,0:T(8,128)(2,1)S(1)}, bf16[64,1024]{1,0:T(8,128)(2,1)S(1)}, u32[]{:S(2)}, u32[]{:S(2)}) collective-permute-start(bf16[64,1024]{1,0:T(8,128)(2,1)S(1)} %get-tuple-element.71), channel_id=1, source_target_pairs={{0,1},{1,0},{2,3},{3,2},{4,5},{5,4},{6,7},{7,6},{8,9},{9,8},{10,11... | collective-permute-start | bytes 393224 | tf_op jit(solution)/shard_map/ppermute | solution.py:702
  25.0 0.0 collective-permute-done.9
  25.0 1.6 %collective-permute-start.10 = (bf16[64,1024]{1,0:T(8,128)(2,1)S(1)}, bf16[64,1024]{1,0:T(8,128)(2,1)S(1)}, u32[]{:S(2)}, u32[]{:S(2)}) collective-permute-start(bf16[64,1024]{1,0:T(8,128)(2,1)S(1)} %add_convert_fusion.1), channel_id=1, source_target_pairs={{0,2},{1,3},{2,0},{3,1},{4,6},{5,7},{6,4},{7,5},{8,10},{9,11},{10,... | collective-permute-start | bytes 393224 | tf_op jit(solution)/shard_map/ppermute | solution.py:702
  26.7 1.0 %collective-permute-start.7 = (bf16[64,1024]{1,0:T(8,128)(2,1)S(1)}, bf16[64,1024]{1,0:T(8,128)(2,1)S(1)}, u32[]{:S(2)}, u32[]{:S(2)}) collective-permute-start(bf16[64,1024]{1,0:T(8,128)(2,1)S(1)} %add_convert_fusion.3), channel_id=1, source_target_pairs={{0,2},{1,3},{2,0},{3,1},{4,6},{5,7},{6,4},{7,5},{8,10},{9,11},{10,... | collective-permute-start | bytes 393224 | tf_op jit(solution)/shard_map/ppermute | solution.py:702
  27.6 1.1 %shard_map.127 = (bf16[1,128,512]{2,1,0:T(8,128)(2,1)}, bf16[1,64,512]{2,1,0:T(8,128)(2,1)}) custom-call(bf16[512,1536]{1,0:T(8,128)(2,1)S(1)} %get-tuple-element.45.refs_4_.turned_ref, s32[3,1,16]{2,1,0:T(1,128)S(1)} %bitcast.6, bf16[48,512]{1,0:T(8,128)(2,1)S(1)} %get-tuple-element.73.own_slot_ref, ...), custom_call_target="tpu_custom_call" | custom-call | flops 100000000 | bytes 4194304 | tf_op jit(solution)/shard_map/pallas_call | solution.py:689
  28.7 2.7 %collective-permute-done.10 = bf16[64,1024]{1,0:T(8,128)(2,1)S(1)} collective-permute-done((bf16[64,1024]{1,0:T(8,128)(2,1)S(1)}, bf16[64,1024]{1,0:T(8,128)(2,1)S(1)}, u32[]{:S(2)}, u32[]{:S(2)}) %collective-permute-start.10) | collective-permute-done | bytes 131104 | tf_op jit(solution)/shard_map/ppermute | solution.py:702
  31.5 0.1 collective-permute-start.11
  31.6 1.8 %collective-permute-done.7 = bf16[64,1024]{1,0:T(8,128)(2,1)S(1)} collective-permute-done((bf16[64,1024]{1,0:T(8,128)(2,1)S(1)}, bf16[64,1024]{1,0:T(8,128)(2,1)S(1)}, u32[]{:S(2)}, u32[]{:S(2)}) %collective-permute-start.7) | collective-permute-done | bytes 131104 | tf_op jit(solution)/shard_map/ppermute | solution.py:702
  33.4 0.1 collective-permute-start.8
  33.4 0.9 %shard_map.128.settled_ref = f32[128,2048]{1,0:T(8,128)} custom-call(bf16[64,1024]{1,0:T(8,128)(2,1)S(1)} %add_convert_fusion.2.one_ref, bf16[64,1024]{1,0:T(8,128)(2,1)S(1)} %add_convert_fusion.two_ref, bf16[64,1024]{1,0:T(8,128)(2,1)S(1)} %collective-permute-done.11.other_two_ref), custom_call_target="tpu_custom_call" | custom-call | tf_op jit(solution)/shard_map/pallas_call | solution.py:906
  34.4 0.4 %collective-permute-done.8.other_one_ref = bf16[64,1024]{1,0:T(8,128)(2,1)S(1)} collective-permute-done((bf16[64,1024]{1,0:T(8,128)(2,1)S(1)}, bf16[64,1024]{1,0:T(8,128)(2,1)S(1)}, u32[]{:S(2)}, u32[]{:S(2)}) %collective-permute-start.8) | collective-permute-done | bytes 131104 | tf_op jit(solution)/shard_map/ppermute | solution.py:702
  34.8 0.7 %shard_map.129 = f32[128,2048]{1,0:T(8,128)} custom-call(bf16[64,1024]{1,0:T(8,128)(2,1)S(1)} %collective-permute-done.8.other_one_ref, f32[128,2048]{1,0:T(8,128)} %shard_map.128.settled_ref), custom_call_target="tpu_custom_call", output_to_operand_aliasing={{}: (1, {})} | custom-call | tf_op jit(solution)/shard_map/pallas_call | solution.py:914
  (9 shorter events, 0.1 us)
Async XLA Ops:
  0.6 10.8 %copy-start = (bf16[1,64,512]{2,1,0:T(8,128)(2,1)S(1)}, bf16[1,64,512]{2,1,0:T(8,128)(2,1)}, u32[]{:S(2)}) copy-start(bf16[1,64,512]{2,1,0:T(8,128)(2,1)} %refs_0_.3) | copy-start | bytes 196612
  1.9 13.6 %collective-permute-start.1 = (bf16[120,512]{1,0:T(8,128)(2,1)S(1)}, bf16[120,512]{1,0:T(8,128)(2,1)S(1)}, u32[]{:S(2)}, u32[]{:S(2)}) collective-permute-start(bf16[120,512]{1,0:T(8,128)(2,1)S(1)} %shard_map.121.refs_0_), channel_id=1, source_target_pairs={{0,8},{4,12},{8,0},{12,4},{1,9},{5,13},{9,1},{13,5},{2,10},{6,14},... | collective-permute-start | bytes 368648 | tf_op jit(solution)/shard_map/ppermute | solution.py:702
  6.0 12.3 %collective-permute-start.2 = (bf16[120,512]{1,0:T(8,128)(2,1)S(1)}, bf16[120,512]{1,0:T(8,128)(2,1)S(1)}, u32[]{:S(2)}, u32[]{:S(2)}) collective-permute-start(bf16[120,512]{1,0:T(8,128)(2,1)S(1)} %shard_map.121.refs_0_), channel_id=1, source_target_pairs={{0,12},{4,8},{8,4},{12,0},{1,13},{5,9},{9,5},{13,1},{2,14},{6,10},... | collective-permute-start | bytes 368648 | tf_op jit(solution)/shard_map/ppermute | solution.py:702
  7.3 10.9 %collective-permute-start.3 = (bf16[120,512]{1,0:T(8,128)(2,1)S(1)}, bf16[120,512]{1,0:T(8,128)(2,1)S(1)}, u32[]{:S(2)}, u32[]{:S(2)}) collective-permute-start(bf16[120,512]{1,0:T(8,128)(2,1)S(1)} %shard_map.121.refs_0_), channel_id=1, source_target_pairs={{0,4},{4,0},{8,12},{12,8},{1,5},{5,1},{9,13},{13,9},{2,6},{6,2},{1... | collective-permute-start | bytes 368648 | tf_op jit(solution)/shard_map/ppermute | solution.py:702
  7.6 13.4 %collective-permute-start = (bf16[1,64,512]{2,1,0:T(8,128)(2,1)}, bf16[1,64,512]{2,1,0:T(8,128)(2,1)S(1)}, u32[]{:S(2)}, u32[]{:S(2)}) collective-permute-start(bf16[1,64,512]{2,1,0:T(8,128)(2,1)} %refs_0_.3), channel_id=1, source_target_pairs={{0,4},{4,0},{8,12},{12,8},{1,5},{5,1},{9,13},{13,9},{2,6},{6,2},{1... | collective-permute-start | bytes 196616 | tf_op jit(solution)/shard_map/ppermute | solution.py:702
  11.5 10.7 %collective-permute-start.4 = (bf16[1,64,512]{2,1,0:T(8,128)(2,1)S(1)}, bf16[1,64,512]{2,1,0:T(8,128)(2,1)S(1)}, u32[]{:S(2)}, u32[]{:S(2)}) collective-permute-start(bf16[1,64,512]{2,1,0:T(8,128)(2,1)S(1)} %copy-done), channel_id=1, source_target_pairs={{0,8},{4,12},{8,0},{12,4},{1,9},{5,13},{9,1},{13,5},{2,10},{6,14},... | collective-permute-start | bytes 196616 | tf_op jit(solution)/shard_map/ppermute | solution.py:702
  15.5 6.7 %collective-permute-start.5 = (bf16[1,64,512]{2,1,0:T(8,128)(2,1)S(1)}, bf16[1,64,512]{2,1,0:T(8,128)(2,1)S(1)}, u32[]{:S(2)}, u32[]{:S(2)}) collective-permute-start(bf16[1,64,512]{2,1,0:T(8,128)(2,1)S(1)} %copy-done), channel_id=1, source_target_pairs={{0,12},{4,8},{8,4},{12,0},{1,13},{5,9},{9,5},{13,1},{2,14},{6,10},... | collective-permute-start | bytes 196616 | tf_op jit(solution)/shard_map/ppermute | solution.py:702
  23.3 1.7 %collective-permute-start.9 = (bf16[64,1024]{1,0:T(8,128)(2,1)S(1)}, bf16[64,1024]{1,0:T(8,128)(2,1)S(1)}, u32[]{:S(2)}, u32[]{:S(2)}) collective-permute-start(bf16[64,1024]{1,0:T(8,128)(2,1)S(1)} %get-tuple-element.80), channel_id=1, source_target_pairs={{0,1},{1,0},{2,3},{3,2},{4,5},{5,4},{6,7},{7,6},{8,9},{9,8},{10,11... | collective-permute-start | bytes 393224 | tf_op jit(solution)/shard_map/ppermute | solution.py:702
  23.4 4.3 %copy-start.1 = (s32[1,3,16]{2,0,1:T(1,128)S(1)}, s32[1,3,16]{2,0,1:T(1,128)}, u32[]{:S(2)}) copy-start(s32[1,3,16]{2,0,1:T(1,128)} %param.14) | copy-start | bytes 580
  24.4 2.2 %collective-permute-start.6 = (bf16[64,1024]{1,0:T(8,128)(2,1)S(1)}, bf16[64,1024]{1,0:T(8,128)(2,1)S(1)}, u32[]{:S(2)}, u32[]{:S(2)}) collective-permute-start(bf16[64,1024]{1,0:T(8,128)(2,1)S(1)} %get-tuple-element.71), channel_id=1, source_target_pairs={{0,1},{1,0},{2,3},{3,2},{4,5},{5,4},{6,7},{7,6},{8,9},{9,8},{10,11... | collective-permute-start | bytes 393224 | tf_op jit(solution)/shard_map/ppermute | solution.py:702
  25.0 6.4 %collective-permute-start.10 = (bf16[64,1024]{1,0:T(8,128)(2,1)S(1)}, bf16[64,1024]{1,0:T(8,128)(2,1)S(1)}, u32[]{:S(2)}, u32[]{:S(2)}) collective-permute-start(bf16[64,1024]{1,0:T(8,128)(2,1)S(1)} %add_convert_fusion.1), channel_id=1, source_target_pairs={{0,2},{1,3},{2,0},{3,1},{4,6},{5,7},{6,4},{7,5},{8,10},{9,11},{10,... | collective-permute-start | bytes 393224 | tf_op jit(solution)/shard_map/ppermute | solution.py:702
  26.7 6.7 %collective-permute-start.7 = (bf16[64,1024]{1,0:T(8,128)(2,1)S(1)}, bf16[64,1024]{1,0:T(8,128)(2,1)S(1)}, u32[]{:S(2)}, u32[]{:S(2)}) collective-permute-start(bf16[64,1024]{1,0:T(8,128)(2,1)S(1)} %add_convert_fusion.3), channel_id=1, source_target_pairs={{0,2},{1,3},{2,0},{3,1},{4,6},{5,7},{6,4},{7,5},{8,10},{9,11},{10,... | collective-permute-start | bytes 393224 | tf_op jit(solution)/shard_map/ppermute | solution.py:702
  31.5 2.0 %collective-permute-start.11 = (bf16[64,1024]{1,0:T(8,128)(2,1)S(1)}, bf16[64,1024]{1,0:T(8,128)(2,1)S(1)}, u32[]{:S(2)}, u32[]{:S(2)}) collective-permute-start(bf16[64,1024]{1,0:T(8,128)(2,1)S(1)} %add_convert_fusion.two_ref), channel_id=1, source_target_pairs={{0,1},{1,0},{2,3},{3,2},{4,5},{5,4},{6,7},{7,6},{8,9},{9,8},{10,11... | collective-permute-start | bytes 393224 | tf_op jit(solution)/shard_map/ppermute | solution.py:702
  33.4 1.4 %collective-permute-start.8 = (bf16[64,1024]{1,0:T(8,128)(2,1)S(1)}, bf16[64,1024]{1,0:T(8,128)(2,1)S(1)}, u32[]{:S(2)}, u32[]{:S(2)}) collective-permute-start(bf16[64,1024]{1,0:T(8,128)(2,1)S(1)} %add_convert_fusion.2.one_ref), channel_id=1, source_target_pairs={{0,1},{1,0},{2,3},{3,2},{4,5},{5,4},{6,7},{7,6},{8,9},{9,8},{10,11... | collective-permute-start | bytes 393224 | tf_op jit(solution)/shard_map/ppermute | solution.py:702

commit v25 on v24

--- a/solution.py
+++ b/solution.py
@@ -765,7 +765,6 @@
         10**8,
         fetched=1,
     )
-    turned, cotangent = lax.optimization_barrier((turned, cotangent))
     cotangents = [cotangent] + [swap(cotangent, "space", step) for step in steps[1:-1]] + [near]
     rows = regions * mesh_count
     slots = regions * mesh_cap

time: 35.7 us -> 35.7 us (level)
  no operation moved by 1% of the time
where the time goes in v25:
time: 35.7 us; the launch traced here: 35.5 us
  starting transfers between devices  15.3 us (43%)
  Pallas kernels  11.5 us (32%)
  waiting for transfers between devices  7.82 us (22%)
  between operations  0.76 us (2%)
    ppermute x12, starting transfers between devices, swap(): lax.ppermute(block, axis, [(i, i ^ bits) for i in range(lax.axis_size(axi...  15.3 us
    pallas_call x7, Pallas kernels, call(): pl.pallas_call(kernel, out_shape=[jax.ShapeDtypeStruct(shape, kind) for s...  9.82 us
    ppermute x12, waiting for transfers between devices, swap(): lax.ppermute(block, axis, [(i, i ^ bits) for i in range(lax.axis_size(axi...  7.82 us
    pallas_call x1, Pallas kernels, whole_sample_body(): pl.pallas_call(settle_kernel, out_shape=weight_shape, in_specs=[VMEM] * 3...  0.92 us
    pallas_call x1, Pallas kernels, whole_sample_body(): pl.pallas_call(finish_kernel, out_shape=weight_shape, in_specs=[VMEM, hbm...  0.73 us
  transfers between devices with their start and end apart: 12, of which 5 were waited for; matrix products, arithmetic and copies ran while one was open for 0% of the time, Pallas kernels for 24%

profile of v25, /device:TPU:0, one launch (start us, length us, event | category | flops | bytes accessed | tf_op | source)
XLA Modules:
  0.0 35.5 jit_solution(10425024997939509164)
XLA Ops:
  0.6 0.0 copy-start
  0.6 1.2 %shard_map.121.refs_0_ = bf16[120,512]{1,0:T(8,128)(2,1)S(1)} custom-call(bf16[1,128,512]{2,1,0:T(8,128)(2,1)} %refs_0_.1, bf16[1,64,512]{2,1,0:T(8,128)(2,1)} %refs_1_.1, s32[3,1,16]{2,1,0:T(1,128)} %bitcast.5, s32[1,256]{1,0:T(1,128)} %bitcast.7, s32[1,256]{1,0:T(1,128)} %bitcast.8, s32[1,4,8]{2,1,0:T(4,128)} %refs_5_.1, s32[1,256]{1,0:T(1,128)} %bitcast.9, ...), custom_call_target="tpu_custom_call" | custom-call | flops 10000000 | bytes 4194304 | tf_op jit(solution)/shard_map/pallas_call | solution.py:689
  1.9 4.1 %collective-permute-start.1 = (bf16[120,512]{1,0:T(8,128)(2,1)S(1)}, bf16[120,512]{1,0:T(8,128)(2,1)S(1)}, u32[]{:S(2)}, u32[]{:S(2)}) collective-permute-start(bf16[120,512]{1,0:T(8,128)(2,1)S(1)} %shard_map.121.refs_0_), channel_id=1, source_target_pairs={{0,8},{4,12},{8,0},{12,4},{1,9},{5,13},{9,1},{13,5},{2,10},{6,14},... | collective-permute-start | bytes 368648 | tf_op jit(solution)/shard_map/ppermute | solution.py:702
  6.0 1.3 %collective-permute-start.2 = (bf16[120,512]{1,0:T(8,128)(2,1)S(1)}, bf16[120,512]{1,0:T(8,128)(2,1)S(1)}, u32[]{:S(2)}, u32[]{:S(2)}) collective-permute-start(bf16[120,512]{1,0:T(8,128)(2,1)S(1)} %shard_map.121.refs_0_), channel_id=1, source_target_pairs={{0,12},{4,8},{8,4},{12,0},{1,13},{5,9},{9,5},{13,1},{2,14},{6,10},... | collective-permute-start | bytes 368648 | tf_op jit(solution)/shard_map/ppermute | solution.py:702
  7.3 0.2 collective-permute-start.3
  7.6 1.8 %collective-permute-start = (bf16[1,64,512]{2,1,0:T(8,128)(2,1)}, bf16[1,64,512]{2,1,0:T(8,128)(2,1)S(1)}, u32[]{:S(2)}, u32[]{:S(2)}) collective-permute-start(bf16[1,64,512]{2,1,0:T(8,128)(2,1)} %refs_0_.3), channel_id=1, source_target_pairs={{0,4},{4,0},{8,12},{12,8},{1,5},{5,1},{9,13},{13,9},{2,6},{6,2},{1... | collective-permute-start | bytes 196616 | tf_op jit(solution)/shard_map/ppermute | solution.py:702
  9.4 1.7 %collective-permute-start.4 = (bf16[1,64,512]{2,1,0:T(8,128)(2,1)}, bf16[1,64,512]{2,1,0:T(8,128)(2,1)S(1)}, u32[]{:S(2)}, u32[]{:S(2)}) collective-permute-start(bf16[1,64,512]{2,1,0:T(8,128)(2,1)} %refs_0_.3), channel_id=1, source_target_pairs={{0,8},{4,12},{8,0},{12,4},{1,9},{5,13},{9,1},{13,5},{2,10},{6,14},... | collective-permute-start | bytes 196616 | tf_op jit(solution)/shard_map/ppermute | solution.py:702
  11.1 2.1 %shard_map.122 = (bf16[512,2048]{1,0:T(8,128)(2,1)S(1)}, bf16[512,1536]{1,0:T(8,128)(2,1)S(1)}) custom-call(bf16[512,2048]{1,0:T(8,128)(2,1)} %source_ref), custom_call_target="tpu_custom_call" | custom-call | flops 100000000 | bytes 4194304 | tf_op jit(solution)/shard_map/pallas_call | solution.py:689
  13.1 2.3 %collective-permute-done.1.refs_1_ = bf16[120,512]{1,0:T(8,128)(2,1)S(1)} collective-permute-done((bf16[120,512]{1,0:T(8,128)(2,1)S(1)}, bf16[120,512]{1,0:T(8,128)(2,1)S(1)}, u32[]{:S(2)}, u32[]{:S(2)}) %collective-permute-start.1) | collective-permute-done | bytes 122912 | tf_op jit(solution)/shard_map/ppermute | solution.py:702
  15.5 2.8 %collective-permute-start.5 = (bf16[1,64,512]{2,1,0:T(8,128)(2,1)S(1)}, bf16[1,64,512]{2,1,0:T(8,128)(2,1)S(1)}, u32[]{:S(2)}, u32[]{:S(2)}) collective-permute-start(bf16[1,64,512]{2,1,0:T(8,128)(2,1)S(1)} %copy-done), channel_id=1, source_target_pairs={{0,12},{4,8},{8,4},{12,0},{1,13},{5,9},{9,5},{13,1},{2,14},{6,10},... | collective-permute-start | bytes 196616 | tf_op jit(solution)/shard_map/ppermute | solution.py:702
  18.3 0.0 collective-permute-done.2.refs_2_
  18.3 0.0 collective-permute-done.3.refs_3_
  18.3 2.7 %shard_map.123 = (bf16[192,512]{1,0:T(8,128)(2,1)S(1)}, bf16[256,512]{1,0:T(8,128)(2,1)S(1)}, bf16[256,512]{1,0:T(8,128)(2,1)S(1)}, bf16[128,512]{1,0:T(8,128)(2...) custom-call(bf16[120,512]{1,0:T(8,128)(2,1)S(1)} %shard_map.121.refs, ...), custom_call_target="tpu_custom_call" | custom-call | flops 2000000000 | bytes 4194304 | tf_op jit(solution)/shard_map/pallas_call | solution.py:689
  21.0 0.0 collective-permute-done.refs_1_
  21.0 0.6 %shard_map.124 = (f32[192,512]{1,0:T(8,128)S(1)}, bf16[128,192]{1,0:T(8,128)(2,1)S(1)}, bf16[128,256]{1,0:T(8,128)(2,1)S(1)}, bf16[128,128]{1,0:T(8,128)(2,1)S(1)}, bf16[128,256]{1,0:T(8,128)(2,1)S(1)}) custom-call(bf16[1,64,512]{2,1,0:T(8,128)(2,1)S(1)} %copy-done, bf16[1,64,512]{2,1,0:T(8,128)(2,1)S(1)} %collective-permute-done.refs_1_, ...), custom_call_target="tpu_custom_call" | custom-call | flops 1000000000 | bytes 4194304 | tf_op jit(solution)/shard_map/pallas_call | solution.py:689
  21.6 0.6 %collective-permute-done.4.refs_2_ = bf16[1,64,512]{2,1,0:T(8,128)(2,1)S(1)} collective-permute-done((bf16[1,64,512]{2,1,0:T(8,128)(2,1)}, bf16[1,64,512]{2,1,0:T(8,128)(2,1)S(1)}, u32[]{:S(2)}, u32[]{:S(2)}) %collective-permute-start.4) | collective-permute-done | bytes 65568 | tf_op jit(solution)/shard_map/ppermute | solution.py:702
  22.2 1.1 %shard_map.125 = (f32[256,512]{1,0:T(8,128)S(1)}, bf16[64,1024]{1,0:T(8,128)(2,1)S(1)}, bf16[64,1024]{1,0:T(8,128)(2,1)S(1)}) custom-call(bf16[1,64,512]{2,1,0:T(8,128)(2,1)S(1)} %copy-done, bf16[1,64,512]{2,1,0:T(8,128)(2,1)S(1)} %collective-permute-done.refs_1_, bf16[1,64,512]{2,1,0:T(8,128)(2,1)S(1)} %collective-permute-done.4.refs_2_, ...), custom_call_target="tpu_custom_call" | custom-call | flops 1000000000 | bytes 4194304 | tf_op jit(solution)/shard_map/pallas_call | solution.py:689
  23.3 0.1 collective-permute-start.9
  23.4 0.0 copy-start.1
  23.4 1.1 %shard_map.126 = (bf16[48,512]{1,0:T(8,128)(2,1)S(1)}, bf16[64,1024]{1,0:T(8,128)(2,1)S(1)}, bf16[64,1024]{1,0:T(8,128)(2,1)S(1)}) custom-call(bf16[128,192]{1,0:T(8,128)(2,1)S(1)} %get-tuple-element.54.grid_columns_ref, bf16[128,256]{1,0:T(8,128)(2,1)S(1)} %get-tuple-element.55.mesh_columns_ref, bf16[448,256]{1,0:T(8,128)(2,1)S(1)} %get-tuple-element.56.hot_ref, ...), custom_call_target="tpu_custom_call" | custom-call | flops 1000000000 | bytes 4194304 | tf_op jit(solution)/shard_map/pallas_call | solution.py:689
  24.4 0.5 %collective-permute-start.6 = (bf16[64,1024]{1,0:T(8,128)(2,1)S(1)}, bf16[64,1024]{1,0:T(8,128)(2,1)S(1)}, u32[]{:S(2)}, u32[]{:S(2)}) collective-permute-start(bf16[64,1024]{1,0:T(8,128)(2,1)S(1)} %get-tuple-element.67), channel_id=1, source_target_pairs={{0,1},{1,0},{2,3},{3,2},{4,5},{5,4},{6,7},{7,6},{8,9},{9,8},{10,11... | collective-permute-start | bytes 393224 | tf_op jit(solution)/shard_map/ppermute | solution.py:702
  25.0 0.0 collective-permute-done.9
  25.0 1.6 %collective-permute-start.10 = (bf16[64,1024]{1,0:T(8,128)(2,1)S(1)}, bf16[64,1024]{1,0:T(8,128)(2,1)S(1)}, u32[]{:S(2)}, u32[]{:S(2)}) collective-permute-start(bf16[64,1024]{1,0:T(8,128)(2,1)S(1)} %add_convert_fusion.1), channel_id=1, source_target_pairs={{0,2},{1,3},{2,0},{3,1},{4,6},{5,7},{6,4},{7,5},{8,10},{9,11},{10,... | collective-permute-start | bytes 393224 | tf_op jit(solution)/shard_map/ppermute | solution.py:702
  26.7 1.0 %collective-permute-start.7 = (bf16[64,1024]{1,0:T(8,128)(2,1)S(1)}, bf16[64,1024]{1,0:T(8,128)(2,1)S(1)}, u32[]{:S(2)}, u32[]{:S(2)}) collective-permute-start(bf16[64,1024]{1,0:T(8,128)(2,1)S(1)} %add_convert_fusion.3), channel_id=1, source_target_pairs={{0,2},{1,3},{2,0},{3,1},{4,6},{5,7},{6,4},{7,5},{8,10},{9,11},{10,... | collective-permute-start | bytes 393224 | tf_op jit(solution)/shard_map/ppermute | solution.py:702
  27.6 1.1 %shard_map.127 = (bf16[1,128,512]{2,1,0:T(8,128)(2,1)}, bf16[1,64,512]{2,1,0:T(8,128)(2,1)}) custom-call(bf16[512,1536]{1,0:T(8,128)(2,1)S(1)} %get-tuple-element.41.refs_4_.turned_ref, s32[3,1,16]{2,1,0:T(1,128)S(1)} %bitcast.6, bf16[48,512]{1,0:T(8,128)(2,1)S(1)} %get-tuple-element.69.own_slot_ref, ...), custom_call_target="tpu_custom_call" | custom-call | flops 100000000 | bytes 4194304 | tf_op jit(solution)/shard_map/pallas_call | solution.py:689
  28.7 2.7 %collective-permute-done.10 = bf16[64,1024]{1,0:T(8,128)(2,1)S(1)} collective-permute-done((bf16[64,1024]{1,0:T(8,128)(2,1)S(1)}, bf16[64,1024]{1,0:T(8,128)(2,1)S(1)}, u32[]{:S(2)}, u32[]{:S(2)}) %collective-permute-start.10) | collective-permute-done | bytes 131104 | tf_op jit(solution)/shard_map/ppermute | solution.py:702
  31.5 0.1 collective-permute-start.11
  31.6 1.8 %collective-permute-done.7 = bf16[64,1024]{1,0:T(8,128)(2,1)S(1)} collective-permute-done((bf16[64,1024]{1,0:T(8,128)(2,1)S(1)}, bf16[64,1024]{1,0:T(8,128)(2,1)S(1)}, u32[]{:S(2)}, u32[]{:S(2)}) %collective-permute-start.7) | collective-permute-done | bytes 131104 | tf_op jit(solution)/shard_map/ppermute | solution.py:702
  33.4 0.1 collective-permute-start.8
  33.4 0.9 %shard_map.128.settled_ref = f32[128,2048]{1,0:T(8,128)} custom-call(bf16[64,1024]{1,0:T(8,128)(2,1)S(1)} %add_convert_fusion.2.one_ref, bf16[64,1024]{1,0:T(8,128)(2,1)S(1)} %add_convert_fusion.two_ref, bf16[64,1024]{1,0:T(8,128)(2,1)S(1)} %collective-permute-done.11.other_two_ref), custom_call_target="tpu_custom_call" | custom-call | tf_op jit(solution)/shard_map/pallas_call | solution.py:905
  34.4 0.4 %collective-permute-done.8.other_one_ref = bf16[64,1024]{1,0:T(8,128)(2,1)S(1)} collective-permute-done((bf16[64,1024]{1,0:T(8,128)(2,1)S(1)}, bf16[64,1024]{1,0:T(8,128)(2,1)S(1)}, u32[]{:S(2)}, u32[]{:S(2)}) %collective-permute-start.8) | collective-permute-done | bytes 131104 | tf_op jit(solution)/shard_map/ppermute | solution.py:702
  34.8 0.7 %shard_map.129 = f32[128,2048]{1,0:T(8,128)} custom-call(bf16[64,1024]{1,0:T(8,128)(2,1)S(1)} %collective-permute-done.8.other_one_ref, f32[128,2048]{1,0:T(8,128)} %shard_map.128.settled_ref), custom_call_target="tpu_custom_call", output_to_operand_aliasing={{}: (1, {})} | custom-call | tf_op jit(solution)/shard_map/pallas_call | solution.py:913
  (9 shorter events, 0.1 us)
Async XLA Ops:
  0.6 14.8 %copy-start = (bf16[1,64,512]{2,1,0:T(8,128)(2,1)S(1)}, bf16[1,64,512]{2,1,0:T(8,128)(2,1)}, u32[]{:S(2)}) copy-start(bf16[1,64,512]{2,1,0:T(8,128)(2,1)} %refs_0_.3) | copy-start | bytes 196612
  1.9 13.6 %collective-permute-start.1 = (bf16[120,512]{1,0:T(8,128)(2,1)S(1)}, bf16[120,512]{1,0:T(8,128)(2,1)S(1)}, u32[]{:S(2)}, u32[]{:S(2)}) collective-permute-start(bf16[120,512]{1,0:T(8,128)(2,1)S(1)} %shard_map.121.refs_0_), channel_id=1, source_target_pairs={{0,8},{4,12},{8,0},{12,4},{1,9},{5,13},{9,1},{13,5},{2,10},{6,14},... | collective-permute-start | bytes 368648 | tf_op jit(solution)/shard_map/ppermute | solution.py:702
  6.0 12.3 %collective-permute-start.2 = (bf16[120,512]{1,0:T(8,128)(2,1)S(1)}, bf16[120,512]{1,0:T(8,128)(2,1)S(1)}, u32[]{:S(2)}, u32[]{:S(2)}) collective-permute-start(bf16[120,512]{1,0:T(8,128)(2,1)S(1)} %shard_map.121.refs_0_), channel_id=1, source_target_pairs={{0,12},{4,8},{8,4},{12,0},{1,13},{5,9},{9,5},{13,1},{2,14},{6,10},... | collective-permute-start | bytes 368648 | tf_op jit(solution)/shard_map/ppermute | solution.py:702
  7.3 10.9 %collective-permute-start.3 = (bf16[120,512]{1,0:T(8,128)(2,1)S(1)}, bf16[120,512]{1,0:T(8,128)(2,1)S(1)}, u32[]{:S(2)}, u32[]{:S(2)}) collective-permute-start(bf16[120,512]{1,0:T(8,128)(2,1)S(1)} %shard_map.121.refs_0_), channel_id=1, source_target_pairs={{0,4},{4,0},{8,12},{12,8},{1,5},{5,1},{9,13},{13,9},{2,6},{6,2},{1... | collective-permute-start | bytes 368648 | tf_op jit(solution)/shard_map/ppermute | solution.py:702
  7.6 13.4 %collective-permute-start = (bf16[1,64,512]{2,1,0:T(8,128)(2,1)}, bf16[1,64,512]{2,1,0:T(8,128)(2,1)S(1)}, u32[]{:S(2)}, u32[]{:S(2)}) collective-permute-start(bf16[1,64,512]{2,1,0:T(8,128)(2,1)} %refs_0_.3), channel_id=1, source_target_pairs={{0,4},{4,0},{8,12},{12,8},{1,5},{5,1},{9,13},{13,9},{2,6},{6,2},{1... | collective-permute-start | bytes 196616 | tf_op jit(solution)/shard_map/ppermute | solution.py:702
  9.4 12.8 %collective-permute-start.4 = (bf16[1,64,512]{2,1,0:T(8,128)(2,1)}, bf16[1,64,512]{2,1,0:T(8,128)(2,1)S(1)}, u32[]{:S(2)}, u32[]{:S(2)}) collective-permute-start(bf16[1,64,512]{2,1,0:T(8,128)(2,1)} %refs_0_.3), channel_id=1, source_target_pairs={{0,8},{4,12},{8,0},{12,4},{1,9},{5,13},{9,1},{13,5},{2,10},{6,14},... | collective-permute-start | bytes 196616 | tf_op jit(solution)/shard_map/ppermute | solution.py:702
  15.5 6.7 %collective-permute-start.5 = (bf16[1,64,512]{2,1,0:T(8,128)(2,1)S(1)}, bf16[1,64,512]{2,1,0:T(8,128)(2,1)S(1)}, u32[]{:S(2)}, u32[]{:S(2)}) collective-permute-start(bf16[1,64,512]{2,1,0:T(8,128)(2,1)S(1)} %copy-done), channel_id=1, source_target_pairs={{0,12},{4,8},{8,4},{12,0},{1,13},{5,9},{9,5},{13,1},{2,14},{6,10},... | collective-permute-start | bytes 196616 | tf_op jit(solution)/shard_map/ppermute | solution.py:702
  23.3 1.7 %collective-permute-start.9 = (bf16[64,1024]{1,0:T(8,128)(2,1)S(1)}, bf16[64,1024]{1,0:T(8,128)(2,1)S(1)}, u32[]{:S(2)}, u32[]{:S(2)}) collective-permute-start(bf16[64,1024]{1,0:T(8,128)(2,1)S(1)} %get-tuple-element.76), channel_id=1, source_target_pairs={{0,1},{1,0},{2,3},{3,2},{4,5},{5,4},{6,7},{7,6},{8,9},{9,8},{10,11... | collective-permute-start | bytes 393224 | tf_op jit(solution)/shard_map/ppermute | solution.py:702
  23.4 4.3 %copy-start.1 = (s32[1,3,16]{2,0,1:T(1,128)S(1)}, s32[1,3,16]{2,0,1:T(1,128)}, u32[]{:S(2)}) copy-start(s32[1,3,16]{2,0,1:T(1,128)} %param.14) | copy-start | bytes 580
  24.4 2.2 %collective-permute-start.6 = (bf16[64,1024]{1,0:T(8,128)(2,1)S(1)}, bf16[64,1024]{1,0:T(8,128)(2,1)S(1)}, u32[]{:S(2)}, u32[]{:S(2)}) collective-permute-start(bf16[64,1024]{1,0:T(8,128)(2,1)S(1)} %get-tuple-element.67), channel_id=1, source_target_pairs={{0,1},{1,0},{2,3},{3,2},{4,5},{5,4},{6,7},{7,6},{8,9},{9,8},{10,11... | collective-permute-start | bytes 393224 | tf_op jit(solution)/shard_map/ppermute | solution.py:702
  25.0 6.4 %collective-permute-start.10 = (bf16[64,1024]{1,0:T(8,128)(2,1)S(1)}, bf16[64,1024]{1,0:T(8,128)(2,1)S(1)}, u32[]{:S(2)}, u32[]{:S(2)}) collective-permute-start(bf16[64,1024]{1,0:T(8,128)(2,1)S(1)} %add_convert_fusion.1), channel_id=1, source_target_pairs={{0,2},{1,3},{2,0},{3,1},{4,6},{5,7},{6,4},{7,5},{8,10},{9,11},{10,... | collective-permute-start | bytes 393224 | tf_op jit(solution)/shard_map/ppermute | solution.py:702
  26.7 6.7 %collective-permute-start.7 = (bf16[64,1024]{1,0:T(8,128)(2,1)S(1)}, bf16[64,1024]{1,0:T(8,128)(2,1)S(1)}, u32[]{:S(2)}, u32[]{:S(2)}) collective-permute-start(bf16[64,1024]{1,0:T(8,128)(2,1)S(1)} %add_convert_fusion.3), channel_id=1, source_target_pairs={{0,2},{1,3},{2,0},{3,1},{4,6},{5,7},{6,4},{7,5},{8,10},{9,11},{10,... | collective-permute-start | bytes 393224 | tf_op jit(solution)/shard_map/ppermute | solution.py:702
  31.5 2.0 %collective-permute-start.11 = (bf16[64,1024]{1,0:T(8,128)(2,1)S(1)}, bf16[64,1024]{1,0:T(8,128)(2,1)S(1)}, u32[]{:S(2)}, u32[]{:S(2)}) collective-permute-start(bf16[64,1024]{1,0:T(8,128)(2,1)S(1)} %add_convert_fusion.two_ref), channel_id=1, source_target_pairs={{0,1},{1,0},{2,3},{3,2},{4,5},{5,4},{6,7},{7,6},{8,9},{9,8},{10,11... | collective-permute-start | bytes 393224 | tf_op jit(solution)/shard_map/ppermute | solution.py:702
  33.4 1.4 %collective-permute-start.8 = (bf16[64,1024]{1,0:T(8,128)(2,1)S(1)}, bf16[64,1024]{1,0:T(8,128)(2,1)S(1)}, u32[]{:S(2)}, u32[]{:S(2)}) collective-permute-start(bf16[64,1024]{1,0:T(8,128)(2,1)S(1)} %add_convert_fusion.2.one_ref), channel_id=1, source_target_pairs={{0,1},{1,0},{2,3},{3,2},{4,5},{5,4},{6,7},{7,6},{8,9},{9,8},{10,11... | collective-permute-start | bytes 393224 | tf_op jit(solution)/shard_map/ppermute | solution.py:702

commit v26 on v24

--- a/solution.py
+++ b/solution.py
@@ -356,7 +356,7 @@
     slots = regions * mesh_cap
     me = lax.axis_index("space")
     for step, packed_ref in zip(steps, packed_refs):
-        region = lax.bitwise_xor(me, step)
+        region = lax.rem(me + (regions - step), regions)
         at = lambda rows: pl.ds(pl.multiple_of(region * rows, rows), rows)
         grid_ref[at(listed), :] = packed_ref[:listed, :]
         mesh_ref[at(mesh_count), :] = packed_ref[listed : listed + mesh_count, :]
@@ -702,6 +702,11 @@
     return lax.ppermute(block, axis, [(i, i ^ bits) for i in range(lax.axis_size(axis))])
 
 
+def shifted(block, step):
+    count = lax.axis_size("space")
+    return lax.ppermute(block, "space", [(i, (i + step) % count) for i in range(count)])
+
+
 def added(left, right):
     return (left.astype(F32) + right.astype(F32)).astype(BF16)
 
@@ -754,8 +759,9 @@
         fetched=len(sources),
     )[0]
     packed, cotangent, weights = lax.optimization_barrier((packed, mesh_cotangent, weights))
+    ring = (0, *sorted(range(1, regions), key=lambda step: -min(step, regions - step)))
+    packs = [packed] + [shifted(packed, step) for step in ring[1:]]
     steps = (0, *range(2, regions), 1)
-    packs = [packed] + [swap(packed, "space", step) for step in steps[1:]]
     near = swap(cotangent, "space", 1)
     weights, turned = call(
         weights_kernel,
@@ -786,7 +792,7 @@
         normed_two,
         scaled_two,
     ) = call(
-        functools.partial(forward_kernel, steps, listed, mesh_count, mesh_cap),
+        functools.partial(forward_kernel, ring, listed, mesh_count, mesh_cap),
         (*packs, weights),
         [
             ((regions * listed, latent), BF16),

time: 35.7 us -> 35.9 us (level)
  starting transfers between devices: 15.4 us -> 13.7 us
  waiting for transfers between devices: 7.74 us -> 9.43 us
    ppermute x12 -> x9, starting transfers between devices: 15.4 us -> 5.74 us  [swap(): lax.ppermute(block, axis, [(i, i ^ bits) for i in range(lax.axis_size(axi...]
    ppermute x0 -> x3, starting transfers between devices: none -> 7.93 us  [shifted(): lax.ppermute(block, 'space', [(i, (i + step) % count) for i in range(coun...]
    ppermute x0 -> x3, waiting for transfers between devices: none -> 2.93 us  [shifted(): lax.ppermute(block, 'space', [(i, (i + step) % count) for i in range(coun...]
    ppermute x12 -> x9, waiting for transfers between devices: 7.74 us -> 6.49 us  [swap(): lax.ppermute(block, axis, [(i, i ^ bits) for i in range(lax.axis_size(axi...]
where the time goes in v26:
time: 35.9 us; the launch traced here: 35.5 us
  starting transfers between devices  13.7 us (38%)
  Pallas kernels  11.5 us (32%)
  waiting for transfers between devices  9.43 us (26%)
  between operations  0.77 us (2%)
    pallas_call x7, Pallas kernels, call(): pl.pallas_call(kernel, out_shape=[jax.ShapeDtypeStruct(shape, kind) for s...  9.83 us
    ppermute x3, starting transfers between devices, shifted(): lax.ppermute(block, 'space', [(i, (i + step) % count) for i in range(coun...  7.93 us
    ppermute x9, waiting for transfers between devices, swap(): lax.ppermute(block, axis, [(i, i ^ bits) for i in range(lax.axis_size(axi...  6.49 us
    ppermute x9, starting transfers between devices, swap(): lax.ppermute(block, axis, [(i, i ^ bits) for i in range(lax.axis_size(axi...  5.74 us
    ppermute x3, waiting for transfers between devices, shifted(): lax.ppermute(block, 'space', [(i, (i + step) % count) for i in range(coun...  2.93 us
    pallas_call x1, Pallas kernels, whole_sample_body(): pl.pallas_call(settle_kernel, out_shape=weight_shape, in_specs=[VMEM] * 3...  0.92 us
    pallas_call x1, Pallas kernels, whole_sample_body(): pl.pallas_call(finish_kernel, out_shape=weight_shape, in_specs=[VMEM, hbm...  0.73 us
  transfers between devices with their start and end apart: 12, of which 5 were waited for; matrix products, arithmetic and copies ran while one was open for 0% of the time, Pallas kernels for 24%

profile of v26, /device:TPU:0, one launch (start us, length us, event | category | flops | bytes accessed | tf_op | source)
XLA Modules:
  0.0 35.5 jit_solution(11794739626853394249)
XLA Ops:
  0.6 0.0 copy-start
  0.6 1.2 %shard_map.121.refs_0_ = bf16[120,512]{1,0:T(8,128)(2,1)S(1)} custom-call(bf16[1,128,512]{2,1,0:T(8,128)(2,1)} %refs_0_.1, bf16[1,64,512]{2,1,0:T(8,128)(2,1)} %refs_1_.1, s32[3,1,16]{2,1,0:T(1,128)} %bitcast.5, s32[1,256]{1,0:T(1,128)} %bitcast.7, s32[1,256]{1,0:T(1,128)} %bitcast.8, s32[1,4,8]{2,1,0:T(4,128)} %refs_5_.1, s32[1,256]{1,0:T(1,128)} %bitcast.9, ...), custom_call_target="tpu_custom_call" | custom-call | flops 10000000 | bytes 4194304 | tf_op jit(solution)/shard_map/pallas_call | solution.py:689
  1.9 4.1 %collective-permute-start.1 = (bf16[120,512]{1,0:T(8,128)(2,1)S(1)}, bf16[120,512]{1,0:T(8,128)(2,1)S(1)}, u32[]{:S(2)}, u32[]{:S(2)}) collective-permute-start(bf16[120,512]{1,0:T(8,128)(2,1)S(1)} %shard_map.121.refs_0_), channel_id=1, source_target_pairs={{0,8},{4,12},{8,0},{12,4},{1,9},{5,13},{9,1},{13,5},{2,10},{6,14},... | collective-permute-start | bytes 368648 | tf_op jit(solution)/shard_map/ppermute | solution.py:707
  6.0 1.6 %collective-permute-start.2 = (bf16[120,512]{1,0:T(8,128)(2,1)S(1)}, bf16[120,512]{1,0:T(8,128)(2,1)S(1)}, u32[]{:S(2)}, u32[]{:S(2)}) collective-permute-start(bf16[120,512]{1,0:T(8,128)(2,1)S(1)} %shard_map.121.refs_0_), channel_id=1, source_target_pairs={{0,4},{4,8},{8,12},{12,0},{1,5},{5,9},{9,13},{13,1},{2,6},{6,10},{... | collective-permute-start | bytes 368648 | tf_op jit(solution)/shard_map/ppermute | solution.py:707
  7.6 2.2 %collective-permute-start.3 = (bf16[120,512]{1,0:T(8,128)(2,1)S(1)}, bf16[120,512]{1,0:T(8,128)(2,1)S(1)}, u32[]{:S(2)}, u32[]{:S(2)}) collective-permute-start(bf16[120,512]{1,0:T(8,128)(2,1)S(1)} %shard_map.121.refs_0_), channel_id=1, source_target_pairs={{0,12},{4,0},{8,4},{12,8},{1,13},{5,1},{9,5},{13,9},{2,14},{6,2},{... | collective-permute-start | bytes 368648 | tf_op jit(solution)/shard_map/ppermute | solution.py:707
  9.8 0.0 collective-permute-start
  9.8 2.1 %shard_map.122 = (bf16[512,2048]{1,0:T(8,128)(2,1)S(1)}, bf16[512,1536]{1,0:T(8,128)(2,1)S(1)}) custom-call(bf16[512,2048]{1,0:T(8,128)(2,1)} %source_ref), custom_call_target="tpu_custom_call" | custom-call | flops 100000000 | bytes 4194304 | tf_op jit(solution)/shard_map/pallas_call | solution.py:689
  11.9 0.6 %collective-permute-start.4 = (bf16[1,64,512]{2,1,0:T(8,128)(2,1)S(1)}, bf16[1,64,512]{2,1,0:T(8,128)(2,1)S(1)}, u32[]{:S(2)}, u32[]{:S(2)}) collective-permute-start(bf16[1,64,512]{2,1,0:T(8,128)(2,1)S(1)} %copy-done), channel_id=1, source_target_pairs={{0,8},{4,12},{8,0},{12,4},{1,9},{5,13},{9,1},{13,5},{2,10},{6,14},... | collective-permute-start | bytes 196616 | tf_op jit(solution)/shard_map/ppermute | solution.py:702
  12.5 2.9 %collective-permute-done.1.refs_1_ = bf16[120,512]{1,0:T(8,128)(2,1)S(1)} collective-permute-done((bf16[120,512]{1,0:T(8,128)(2,1)S(1)}, bf16[120,512]{1,0:T(8,128)(2,1)S(1)}, u32[]{:S(2)}, u32[]{:S(2)}) %collective-permute-start.1) | collective-permute-done | bytes 122912 | tf_op jit(solution)/shard_map/ppermute | solution.py:707
  15.5 1.8 %collective-permute-start.5 = (bf16[1,64,512]{2,1,0:T(8,128)(2,1)S(1)}, bf16[1,64,512]{2,1,0:T(8,128)(2,1)S(1)}, u32[]{:S(2)}, u32[]{:S(2)}) collective-permute-start(bf16[1,64,512]{2,1,0:T(8,128)(2,1)S(1)} %copy-done), channel_id=1, source_target_pairs={{0,12},{4,8},{8,4},{12,0},{1,13},{5,9},{9,5},{13,1},{2,14},{6,10},... | collective-permute-start | bytes 196616 | tf_op jit(solution)/shard_map/ppermute | solution.py:702
  17.2 0.0 collective-permute-done.2.refs_2_
  17.3 0.0 collective-permute-done.3.refs_3_
  17.3 2.7 %shard_map.123 = (bf16[192,512]{1,0:T(8,128)(2,1)S(1)}, bf16[256,512]{1,0:T(8,128)(2,1)S(1)}, bf16[256,512]{1,0:T(8,128)(2,1)S(1)}, bf16[128,512]{1,0:T(8,128)(2...) custom-call(bf16[120,512]{1,0:T(8,128)(2,1)S(1)} %shard_map.121.refs, ...), custom_call_target="tpu_custom_call" | custom-call | flops 2000000000 | bytes 4194304 | tf_op jit(solution)/shard_map/pallas_call | solution.py:689
  20.0 0.0 collective-permute-done.refs_1_
  20.0 0.6 %shard_map.124 = (f32[192,512]{1,0:T(8,128)S(1)}, bf16[128,192]{1,0:T(8,128)(2,1)S(1)}, bf16[128,256]{1,0:T(8,128)(2,1)S(1)}, bf16[128,128]{1,0:T(8,128)(2,1)S(1)}, bf16[128,256]{1,0:T(8,128)(2,1)S(1)}) custom-call(bf16[1,64,512]{2,1,0:T(8,128)(2,1)S(1)} %copy-done, bf16[1,64,512]{2,1,0:T(8,128)(2,1)S(1)} %collective-permute-done.refs_1_, ...), custom_call_target="tpu_custom_call" | custom-call | flops 1000000000 | bytes 4194304 | tf_op jit(solution)/shard_map/pallas_call | solution.py:689
  20.6 1.6 %collective-permute-done.4.refs_2_ = bf16[1,64,512]{2,1,0:T(8,128)(2,1)S(1)} collective-permute-done((bf16[1,64,512]{2,1,0:T(8,128)(2,1)S(1)}, bf16[1,64,512]{2,1,0:T(8,128)(2,1)S(1)}, u32[]{:S(2)}, u32[]{:S(2)}) %collective-permute-start.4) | collective-permute-done | bytes 65568 | tf_op jit(solution)/shard_map/ppermute | solution.py:702
  22.2 1.1 %shard_map.125 = (f32[256,512]{1,0:T(8,128)S(1)}, bf16[64,1024]{1,0:T(8,128)(2,1)S(1)}, bf16[64,1024]{1,0:T(8,128)(2,1)S(1)}) custom-call(bf16[1,64,512]{2,1,0:T(8,128)(2,1)S(1)} %copy-done, bf16[1,64,512]{2,1,0:T(8,128)(2,1)S(1)} %collective-permute-done.refs_1_, bf16[1,64,512]{2,1,0:T(8,128)(2,1)S(1)} %collective-permute-done.4.refs_2_, ...), custom_call_target="tpu_custom_call" | custom-call | flops 1000000000 | bytes 4194304 | tf_op jit(solution)/shard_map/pallas_call | solution.py:689
  23.3 0.1 collective-permute-start.9
  23.4 0.0 copy-start.1
  23.4 1.1 %shard_map.126 = (bf16[48,512]{1,0:T(8,128)(2,1)S(1)}, bf16[64,1024]{1,0:T(8,128)(2,1)S(1)}, bf16[64,1024]{1,0:T(8,128)(2,1)S(1)}) custom-call(bf16[128,192]{1,0:T(8,128)(2,1)S(1)} %get-tuple-element.58.grid_columns_ref, bf16[128,256]{1,0:T(8,128)(2,1)S(1)} %get-tuple-element.59.mesh_columns_ref, bf16[448,256]{1,0:T(8,128)(2,1)S(1)} %get-tuple-element.60.hot_ref, ...), custom_call_target="tpu_custom_call" | custom-call | flops 1000000000 | bytes 4194304 | tf_op jit(solution)/shard_map/pallas_call | solution.py:689
  24.4 0.5 %collective-permute-start.6 = (bf16[64,1024]{1,0:T(8,128)(2,1)S(1)}, bf16[64,1024]{1,0:T(8,128)(2,1)S(1)}, u32[]{:S(2)}, u32[]{:S(2)}) collective-permute-start(bf16[64,1024]{1,0:T(8,128)(2,1)S(1)} %get-tuple-element.71), channel_id=1, source_target_pairs={{0,1},{1,0},{2,3},{3,2},{4,5},{5,4},{6,7},{7,6},{8,9},{9,8},{10,11... | collective-permute-start | bytes 393224 | tf_op jit(solution)/shard_map/ppermute | solution.py:702
  25.0 0.0 collective-permute-done.9
  25.0 1.6 %collective-permute-start.10 = (bf16[64,1024]{1,0:T(8,128)(2,1)S(1)}, bf16[64,1024]{1,0:T(8,128)(2,1)S(1)}, u32[]{:S(2)}, u32[]{:S(2)}) collective-permute-start(bf16[64,1024]{1,0:T(8,128)(2,1)S(1)} %add_convert_fusion.1), channel_id=1, source_target_pairs={{0,2},{1,3},{2,0},{3,1},{4,6},{5,7},{6,4},{7,5},{8,10},{9,11},{10,... | collective-permute-start | bytes 393224 | tf_op jit(solution)/shard_map/ppermute | solution.py:702
  26.7 1.0 %collective-permute-start.7 = (bf16[64,1024]{1,0:T(8,128)(2,1)S(1)}, bf16[64,1024]{1,0:T(8,128)(2,1)S(1)}, u32[]{:S(2)}, u32[]{:S(2)}) collective-permute-start(bf16[64,1024]{1,0:T(8,128)(2,1)S(1)} %add_convert_fusion.3), channel_id=1, source_target_pairs={{0,2},{1,3},{2,0},{3,1},{4,6},{5,7},{6,4},{7,5},{8,10},{9,11},{10,... | collective-permute-start | bytes 393224 | tf_op jit(solution)/shard_map/ppermute | solution.py:702
  27.6 1.1 %shard_map.127 = (bf16[1,128,512]{2,1,0:T(8,128)(2,1)}, bf16[1,64,512]{2,1,0:T(8,128)(2,1)}) custom-call(bf16[512,1536]{1,0:T(8,128)(2,1)S(1)} %get-tuple-element.45.refs_4_.turned_ref, s32[3,1,16]{2,1,0:T(1,128)S(1)} %bitcast.6, bf16[48,512]{1,0:T(8,128)(2,1)S(1)} %get-tuple-element.73.own_slot_ref, ...), custom_call_target="tpu_custom_call" | custom-call | flops 100000000 | bytes 4194304 | tf_op jit(solution)/shard_map/pallas_call | solution.py:689
  28.7 2.7 %collective-permute-done.10 = bf16[64,1024]{1,0:T(8,128)(2,1)S(1)} collective-permute-done((bf16[64,1024]{1,0:T(8,128)(2,1)S(1)}, bf16[64,1024]{1,0:T(8,128)(2,1)S(1)}, u32[]{:S(2)}, u32[]{:S(2)}) %collective-permute-start.10) | collective-permute-done | bytes 131104 | tf_op jit(solution)/shard_map/ppermute | solution.py:702
  31.5 0.1 collective-permute-start.11
  31.6 1.8 %collective-permute-done.7 = bf16[64,1024]{1,0:T(8,128)(2,1)S(1)} collective-permute-done((bf16[64,1024]{1,0:T(8,128)(2,1)S(1)}, bf16[64,1024]{1,0:T(8,128)(2,1)S(1)}, u32[]{:S(2)}, u32[]{:S(2)}) %collective-permute-start.7) | collective-permute-done | bytes 131104 | tf_op jit(solution)/shard_map/ppermute | solution.py:702
  33.4 0.1 collective-permute-start.8
  33.4 0.9 %shard_map.128.settled_ref = f32[128,2048]{1,0:T(8,128)} custom-call(bf16[64,1024]{1,0:T(8,128)(2,1)S(1)} %add_convert_fusion.2.one_ref, bf16[64,1024]{1,0:T(8,128)(2,1)S(1)} %add_convert_fusion.two_ref, bf16[64,1024]{1,0:T(8,128)(2,1)S(1)} %collective-permute-done.11.other_two_ref), custom_call_target="tpu_custom_call" | custom-call | tf_op jit(solution)/shard_map/pallas_call | solution.py:912
  34.4 0.4 %collective-permute-done.8.other_one_ref = bf16[64,1024]{1,0:T(8,128)(2,1)S(1)} collective-permute-done((bf16[64,1024]{1,0:T(8,128)(2,1)S(1)}, bf16[64,1024]{1,0:T(8,128)(2,1)S(1)}, u32[]{:S(2)}, u32[]{:S(2)}) %collective-permute-start.8) | collective-permute-done | bytes 131104 | tf_op jit(solution)/shard_map/ppermute | solution.py:702
  34.8 0.7 %shard_map.129 = f32[128,2048]{1,0:T(8,128)} custom-call(bf16[64,1024]{1,0:T(8,128)(2,1)S(1)} %collective-permute-done.8.other_one_ref, f32[128,2048]{1,0:T(8,128)} %shard_map.128.settled_ref), custom_call_target="tpu_custom_call", output_to_operand_aliasing={{}: (1, {})} | custom-call | tf_op jit(solution)/shard_map/pallas_call | solution.py:920
  (9 shorter events, 0.1 us)
Async XLA Ops:
  0.6 11.3 %copy-start = (bf16[1,64,512]{2,1,0:T(8,128)(2,1)S(1)}, bf16[1,64,512]{2,1,0:T(8,128)(2,1)}, u32[]{:S(2)}) copy-start(bf16[1,64,512]{2,1,0:T(8,128)(2,1)} %refs_0_.3) | copy-start | bytes 196612
  1.9 13.6 %collective-permute-start.1 = (bf16[120,512]{1,0:T(8,128)(2,1)S(1)}, bf16[120,512]{1,0:T(8,128)(2,1)S(1)}, u32[]{:S(2)}, u32[]{:S(2)}) collective-permute-start(bf16[120,512]{1,0:T(8,128)(2,1)S(1)} %shard_map.121.refs_0_), channel_id=1, source_target_pairs={{0,8},{4,12},{8,0},{12,4},{1,9},{5,13},{9,1},{13,5},{2,10},{6,14},... | collective-permute-start | bytes 368648 | tf_op jit(solution)/shard_map/ppermute | solution.py:707
  6.0 11.3 %collective-permute-start.2 = (bf16[120,512]{1,0:T(8,128)(2,1)S(1)}, bf16[120,512]{1,0:T(8,128)(2,1)S(1)}, u32[]{:S(2)}, u32[]{:S(2)}) collective-permute-start(bf16[120,512]{1,0:T(8,128)(2,1)S(1)} %shard_map.121.refs_0_), channel_id=1, source_target_pairs={{0,4},{4,8},{8,12},{12,0},{1,5},{5,9},{9,13},{13,1},{2,6},{6,10},{... | collective-permute-start | bytes 368648 | tf_op jit(solution)/shard_map/ppermute | solution.py:707
  7.6 9.7 %collective-permute-start.3 = (bf16[120,512]{1,0:T(8,128)(2,1)S(1)}, bf16[120,512]{1,0:T(8,128)(2,1)S(1)}, u32[]{:S(2)}, u32[]{:S(2)}) collective-permute-start(bf16[120,512]{1,0:T(8,128)(2,1)S(1)} %shard_map.121.refs_0_), channel_id=1, source_target_pairs={{0,12},{4,0},{8,4},{12,8},{1,13},{5,1},{9,5},{13,9},{2,14},{6,2},{... | collective-permute-start | bytes 368648 | tf_op jit(solution)/shard_map/ppermute | solution.py:707
  9.8 10.2 %collective-permute-start = (bf16[1,64,512]{2,1,0:T(8,128)(2,1)}, bf16[1,64,512]{2,1,0:T(8,128)(2,1)S(1)}, u32[]{:S(2)}, u32[]{:S(2)}) collective-permute-start(bf16[1,64,512]{2,1,0:T(8,128)(2,1)} %refs_0_.3), channel_id=1, source_target_pairs={{0,4},{4,0},{8,12},{12,8},{1,5},{5,1},{9,13},{13,9},{2,6},{6,2},{1... | collective-permute-start | bytes 196616 | tf_op jit(solution)/shard_map/ppermute | solution.py:702
  11.9 10.3 %collective-permute-start.4 = (bf16[1,64,512]{2,1,0:T(8,128)(2,1)S(1)}, bf16[1,64,512]{2,1,0:T(8,128)(2,1)S(1)}, u32[]{:S(2)}, u32[]{:S(2)}) collective-permute-start(bf16[1,64,512]{2,1,0:T(8,128)(2,1)S(1)} %copy-done), channel_id=1, source_target_pairs={{0,8},{4,12},{8,0},{12,4},{1,9},{5,13},{9,1},{13,5},{2,10},{6,14},... | collective-permute-start | bytes 196616 | tf_op jit(solution)/shard_map/ppermute | solution.py:702
  15.5 6.7 %collective-permute-start.5 = (bf16[1,64,512]{2,1,0:T(8,128)(2,1)S(1)}, bf16[1,64,512]{2,1,0:T(8,128)(2,1)S(1)}, u32[]{:S(2)}, u32[]{:S(2)}) collective-permute-start(bf16[1,64,512]{2,1,0:T(8,128)(2,1)S(1)} %copy-done), channel_id=1, source_target_pairs={{0,12},{4,8},{8,4},{12,0},{1,13},{5,9},{9,5},{13,1},{2,14},{6,10},... | collective-permute-start | bytes 196616 | tf_op jit(solution)/shard_map/ppermute | solution.py:702
  23.3 1.7 %collective-permute-start.9 = (bf16[64,1024]{1,0:T(8,128)(2,1)S(1)}, bf16[64,1024]{1,0:T(8,128)(2,1)S(1)}, u32[]{:S(2)}, u32[]{:S(2)}) collective-permute-start(bf16[64,1024]{1,0:T(8,128)(2,1)S(1)} %get-tuple-element.80), channel_id=1, source_target_pairs={{0,1},{1,0},{2,3},{3,2},{4,5},{5,4},{6,7},{7,6},{8,9},{9,8},{10,11... | collective-permute-start | bytes 393224 | tf_op jit(solution)/shard_map/ppermute | solution.py:702
  23.4 4.3 %copy-start.1 = (s32[1,3,16]{2,0,1:T(1,128)S(1)}, s32[1,3,16]{2,0,1:T(1,128)}, u32[]{:S(2)}) copy-start(s32[1,3,16]{2,0,1:T(1,128)} %param.14) | copy-start | bytes 580
  24.4 2.2 %collective-permute-start.6 = (bf16[64,1024]{1,0:T(8,128)(2,1)S(1)}, bf16[64,1024]{1,0:T(8,128)(2,1)S(1)}, u32[]{:S(2)}, u32[]{:S(2)}) collective-permute-start(bf16[64,1024]{1,0:T(8,128)(2,1)S(1)} %get-tuple-element.71), channel_id=1, source_target_pairs={{0,1},{1,0},{2,3},{3,2},{4,5},{5,4},{6,7},{7,6},{8,9},{9,8},{10,11... | collective-permute-start | bytes 393224 | tf_op jit(solution)/shard_map/ppermute | solution.py:702
  25.0 6.4 %collective-permute-start.10 = (bf16[64,1024]{1,0:T(8,128)(2,1)S(1)}, bf16[64,1024]{1,0:T(8,128)(2,1)S(1)}, u32[]{:S(2)}, u32[]{:S(2)}) collective-permute-start(bf16[64,1024]{1,0:T(8,128)(2,1)S(1)} %add_convert_fusion.1), channel_id=1, source_target_pairs={{0,2},{1,3},{2,0},{3,1},{4,6},{5,7},{6,4},{7,5},{8,10},{9,11},{10,... | collective-permute-start | bytes 393224 | tf_op jit(solution)/shard_map/ppermute | solution.py:702
  26.7 6.7 %collective-permute-start.7 = (bf16[64,1024]{1,0:T(8,128)(2,1)S(1)}, bf16[64,1024]{1,0:T(8,128)(2,1)S(1)}, u32[]{:S(2)}, u32[]{:S(2)}) collective-permute-start(bf16[64,1024]{1,0:T(8,128)(2,1)S(1)} %add_convert_fusion.3), channel_id=1, source_target_pairs={{0,2},{1,3},{2,0},{3,1},{4,6},{5,7},{6,4},{7,5},{8,10},{9,11},{10,... | collective-permute-start | bytes 393224 | tf_op jit(solution)/shard_map/ppermute | solution.py:702
  31.5 2.0 %collective-permute-start.11 = (bf16[64,1024]{1,0:T(8,128)(2,1)S(1)}, bf16[64,1024]{1,0:T(8,128)(2,1)S(1)}, u32[]{:S(2)}, u32[]{:S(2)}) collective-permute-start(bf16[64,1024]{1,0:T(8,128)(2,1)S(1)} %add_convert_fusion.two_ref), channel_id=1, source_target_pairs={{0,1},{1,0},{2,3},{3,2},{4,5},{5,4},{6,7},{7,6},{8,9},{9,8},{10,11... | collective-permute-start | bytes 393224 | tf_op jit(solution)/shard_map/ppermute | solution.py:702
  33.4 1.4 %collective-permute-start.8 = (bf16[64,1024]{1,0:T(8,128)(2,1)S(1)}, bf16[64,1024]{1,0:T(8,128)(2,1)S(1)}, u32[]{:S(2)}, u32[]{:S(2)}) collective-permute-start(bf16[64,1024]{1,0:T(8,128)(2,1)S(1)} %add_convert_fusion.2.one_ref), channel_id=1, source_target_pairs={{0,1},{1,0},{2,3},{3,2},{4,5},{5,4},{6,7},{7,6},{8,9},{9,8},{10,11... | collective-permute-start | bytes 393224 | tf_op jit(solution)/shard_map/ppermute | solution.py:702

commit v27 on v24

--- a/solution.py
+++ b/solution.py
@@ -756,7 +756,6 @@
     packed, cotangent, weights = lax.optimization_barrier((packed, mesh_cotangent, weights))
     steps = (0, *range(2, regions), 1)
     packs = [packed] + [swap(packed, "space", step) for step in steps[1:]]
-    near = swap(cotangent, "space", 1)
     weights, turned = call(
         weights_kernel,
         (weights,),
@@ -766,7 +765,7 @@
         fetched=1,
     )
     turned, cotangent = lax.optimization_barrier((turned, cotangent))
-    cotangents = [cotangent] + [swap(cotangent, "space", step) for step in steps[1:-1]] + [near]
+    cotangents = [cotangent] + [swap(cotangent, "space", step) for step in steps[1:]]
     rows = regions * mesh_count
     slots = regions * mesh_cap
     (

time: 35.7 us -> 35.7 us (level)
  no operation moved by 1% of the time
where the time goes in v27:
time: 35.7 us; the launch traced here: 35.5 us
  starting transfers between devices  15.4 us (43%)
  Pallas kernels  11.5 us (32%)
  waiting for transfers between devices  7.74 us (22%)
  between operations  0.77 us (2%)
    ppermute x12, starting transfers between devices, swap(): lax.ppermute(block, axis, [(i, i ^ bits) for i in range(lax.axis_size(axi...  15.4 us
    pallas_call x7, Pallas kernels, call(): pl.pallas_call(kernel, out_shape=[jax.ShapeDtypeStruct(shape, kind) for s...  9.83 us
    ppermute x12, waiting for transfers between devices, swap(): lax.ppermute(block, axis, [(i, i ^ bits) for i in range(lax.axis_size(axi...  7.74 us
    pallas_call x1, Pallas kernels, whole_sample_body(): pl.pallas_call(settle_kernel, out_shape=weight_shape, in_specs=[VMEM] * 3...  0.92 us
    pallas_call x1, Pallas kernels, whole_sample_body(): pl.pallas_call(finish_kernel, out_shape=weight_shape, in_specs=[VMEM, hbm...  0.73 us
  transfers between devices with their start and end apart: 12, of which 5 were waited for; matrix products, arithmetic and copies ran while one was open for 0% of the time, Pallas kernels for 24%

profile of v27, /device:TPU:0, one launch (start us, length us, event | category | flops | bytes accessed | tf_op | source)
XLA Modules:
  0.0 35.5 jit_solution(2844704889422484130)
XLA Ops:
  0.6 1.2 %shard_map.121.refs_0_ = bf16[120,512]{1,0:T(8,128)(2,1)S(1)} custom-call(bf16[1,128,512]{2,1,0:T(8,128)(2,1)} %refs_0_.1, bf16[1,64,512]{2,1,0:T(8,128)(2,1)} %refs_1_.1, s32[3,1,16]{2,1,0:T(1,128)} %bitcast.5, s32[1,256]{1,0:T(1,128)} %bitcast.7, s32[1,256]{1,0:T(1,128)} %bitcast.8, s32[1,4,8]{2,1,0:T(4,128)} %refs_5_.1, s32[1,256]{1,0:T(1,128)} %bitcast.9, ...), custom_call_target="tpu_custom_call" | custom-call | flops 10000000 | bytes 4194304 | tf_op jit(solution)/shard_map/pallas_call | solution.py:689
  1.9 4.1 %collective-permute-start.1 = (bf16[120,512]{1,0:T(8,128)(2,1)S(1)}, bf16[120,512]{1,0:T(8,128)(2,1)S(1)}, u32[]{:S(2)}, u32[]{:S(2)}) collective-permute-start(bf16[120,512]{1,0:T(8,128)(2,1)S(1)} %shard_map.121.refs_0_), channel_id=1, source_target_pairs={{0,8},{4,12},{8,0},{12,4},{1,9},{5,13},{9,1},{13,5},{2,10},{6,14},... | collective-permute-start | bytes 368648 | tf_op jit(solution)/shard_map/ppermute | solution.py:702
  6.0 1.3 %collective-permute-start.2 = (bf16[120,512]{1,0:T(8,128)(2,1)S(1)}, bf16[120,512]{1,0:T(8,128)(2,1)S(1)}, u32[]{:S(2)}, u32[]{:S(2)}) collective-permute-start(bf16[120,512]{1,0:T(8,128)(2,1)S(1)} %shard_map.121.refs_0_), channel_id=1, source_target_pairs={{0,12},{4,8},{8,4},{12,0},{1,13},{5,9},{9,5},{13,1},{2,14},{6,10},... | collective-permute-start | bytes 368648 | tf_op jit(solution)/shard_map/ppermute | solution.py:702
  7.3 0.2 collective-permute-start.3
  7.6 2.1 %shard_map.122 = (bf16[512,2048]{1,0:T(8,128)(2,1)S(1)}, bf16[512,1536]{1,0:T(8,128)(2,1)S(1)}) custom-call(bf16[512,2048]{1,0:T(8,128)(2,1)} %source_ref), custom_call_target="tpu_custom_call" | custom-call | flops 100000000 | bytes 4194304 | tf_op jit(solution)/shard_map/pallas_call | solution.py:689
  9.7 1.9 %collective-permute-start = (bf16[1,64,512]{2,1,0:T(8,128)(2,1)S(1)}, bf16[1,64,512]{2,1,0:T(8,128)(2,1)S(1)}, u32[]{:S(2)}, u32[]{:S(2)}) collective-permute-start(bf16[1,64,512]{2,1,0:T(8,128)(2,1)S(1)} %copy-done), channel_id=1, source_target_pairs={{0,4},{4,0},{8,12},{12,8},{1,5},{5,1},{9,13},{13,9},{2,6},{6,2},{1... | collective-permute-start | bytes 196616 | tf_op jit(solution)/shard_map/ppermute | solution.py:702
  11.5 1.7 %collective-permute-start.4 = (bf16[1,64,512]{2,1,0:T(8,128)(2,1)S(1)}, bf16[1,64,512]{2,1,0:T(8,128)(2,1)S(1)}, u32[]{:S(2)}, u32[]{:S(2)}) collective-permute-start(bf16[1,64,512]{2,1,0:T(8,128)(2,1)S(1)} %copy-done), channel_id=1, source_target_pairs={{0,8},{4,12},{8,0},{12,4},{1,9},{5,13},{9,1},{13,5},{2,10},{6,14},... | collective-permute-start | bytes 196616 | tf_op jit(solution)/shard_map/ppermute | solution.py:702
  13.2 2.3 %collective-permute-done.1.refs_1_ = bf16[120,512]{1,0:T(8,128)(2,1)S(1)} collective-permute-done((bf16[120,512]{1,0:T(8,128)(2,1)S(1)}, bf16[120,512]{1,0:T(8,128)(2,1)S(1)}, u32[]{:S(2)}, u32[]{:S(2)}) %collective-permute-start.1) | collective-permute-done | bytes 122912 | tf_op jit(solution)/shard_map/ppermute | solution.py:702
  15.5 2.8 %collective-permute-start.5 = (bf16[1,64,512]{2,1,0:T(8,128)(2,1)S(1)}, bf16[1,64,512]{2,1,0:T(8,128)(2,1)S(1)}, u32[]{:S(2)}, u32[]{:S(2)}) collective-permute-start(bf16[1,64,512]{2,1,0:T(8,128)(2,1)S(1)} %copy-done), channel_id=1, source_target_pairs={{0,12},{4,8},{8,4},{12,0},{1,13},{5,9},{9,5},{13,1},{2,14},{6,10},... | collective-permute-start | bytes 196616 | tf_op jit(solution)/shard_map/ppermute | solution.py:702
  18.3 0.0 collective-permute-done.2.refs_2_
  18.3 0.0 collective-permute-done.3.refs_3_
  18.3 2.7 %shard_map.123 = (bf16[192,512]{1,0:T(8,128)(2,1)S(1)}, bf16[256,512]{1,0:T(8,128)(2,1)S(1)}, bf16[256,512]{1,0:T(8,128)(2,1)S(1)}, bf16[128,512]{1,0:T(8,128)(2...) custom-call(bf16[120,512]{1,0:T(8,128)(2,1)S(1)} %shard_map.121.refs, ...), custom_call_target="tpu_custom_call" | custom-call | flops 2000000000 | bytes 4194304 | tf_op jit(solution)/shard_map/pallas_call | solution.py:689
  21.0 0.0 collective-permute-done.refs_1_
  21.0 0.6 %shard_map.124 = (f32[192,512]{1,0:T(8,128)S(1)}, bf16[128,192]{1,0:T(8,128)(2,1)S(1)}, bf16[128,256]{1,0:T(8,128)(2,1)S(1)}, bf16[128,128]{1,0:T(8,128)(2,1)S(1)}, bf16[128,256]{1,0:T(8,128)(2,1)S(1)}) custom-call(bf16[1,64,512]{2,1,0:T(8,128)(2,1)S(1)} %copy-done, bf16[1,64,512]{2,1,0:T(8,128)(2,1)S(1)} %collective-permute-done.refs_1_, ...), custom_call_target="tpu_custom_call" | custom-call | flops 1000000000 | bytes 4194304 | tf_op jit(solution)/shard_map/pallas_call | solution.py:689
  21.6 0.6 %collective-permute-done.4.refs_2_ = bf16[1,64,512]{2,1,0:T(8,128)(2,1)S(1)} collective-permute-done((bf16[1,64,512]{2,1,0:T(8,128)(2,1)S(1)}, bf16[1,64,512]{2,1,0:T(8,128)(2,1)S(1)}, u32[]{:S(2)}, u32[]{:S(2)}) %collective-permute-start.4) | collective-permute-done | bytes 65568 | tf_op jit(solution)/shard_map/ppermute | solution.py:702
  22.2 0.0 collective-permute-done.5.refs_3_
  22.2 1.1 %shard_map.125 = (f32[256,512]{1,0:T(8,128)S(1)}, bf16[64,1024]{1,0:T(8,128)(2,1)S(1)}, bf16[64,1024]{1,0:T(8,128)(2,1)S(1)}) custom-call(bf16[1,64,512]{2,1,0:T(8,128)(2,1)S(1)} %copy-done, bf16[1,64,512]{2,1,0:T(8,128)(2,1)S(1)} %collective-permute-done.refs_1_, bf16[1,64,512]{2,1,0:T(8,128)(2,1)S(1)} %collective-permute-done.4.refs_2_, ...), custom_call_target="tpu_custom_call" | custom-call | flops 1000000000 | bytes 4194304 | tf_op jit(solution)/shard_map/pallas_call | solution.py:689
  23.3 0.1 collective-permute-start.9
  23.4 0.0 copy-start.1
  23.4 1.1 %shard_map.126 = (bf16[48,512]{1,0:T(8,128)(2,1)S(1)}, bf16[64,1024]{1,0:T(8,128)(2,1)S(1)}, bf16[64,1024]{1,0:T(8,128)(2,1)S(1)}) custom-call(bf16[128,192]{1,0:T(8,128)(2,1)S(1)} %get-tuple-element.58.grid_columns_ref, bf16[128,256]{1,0:T(8,128)(2,1)S(1)} %get-tuple-element.59.mesh_columns_ref, bf16[448,256]{1,0:T(8,128)(2,1)S(1)} %get-tuple-element.60.hot_ref, ...), custom_call_target="tpu_custom_call" | custom-call | flops 1000000000 | bytes 4194304 | tf_op jit(solution)/shard_map/pallas_call | solution.py:689
  24.4 0.5 %collective-permute-start.6 = (bf16[64,1024]{1,0:T(8,128)(2,1)S(1)}, bf16[64,1024]{1,0:T(8,128)(2,1)S(1)}, u32[]{:S(2)}, u32[]{:S(2)}) collective-permute-start(bf16[64,1024]{1,0:T(8,128)(2,1)S(1)} %get-tuple-element.71), channel_id=1, source_target_pairs={{0,1},{1,0},{2,3},{3,2},{4,5},{5,4},{6,7},{7,6},{8,9},{9,8},{10,11... | collective-permute-start | bytes 393224 | tf_op jit(solution)/shard_map/ppermute | solution.py:702
  25.0 1.6 %collective-permute-start.10 = (bf16[64,1024]{1,0:T(8,128)(2,1)S(1)}, bf16[64,1024]{1,0:T(8,128)(2,1)S(1)}, u32[]{:S(2)}, u32[]{:S(2)}) collective-permute-start(bf16[64,1024]{1,0:T(8,128)(2,1)S(1)} %add_convert_fusion.1), channel_id=1, source_target_pairs={{0,2},{1,3},{2,0},{3,1},{4,6},{5,7},{6,4},{7,5},{8,10},{9,11},{10,... | collective-permute-start | bytes 393224 | tf_op jit(solution)/shard_map/ppermute | solution.py:702
  26.6 0.0 collective-permute-done.6
  26.7 1.0 %collective-permute-start.7 = (bf16[64,1024]{1,0:T(8,128)(2,1)S(1)}, bf16[64,1024]{1,0:T(8,128)(2,1)S(1)}, u32[]{:S(2)}, u32[]{:S(2)}) collective-permute-start(bf16[64,1024]{1,0:T(8,128)(2,1)S(1)} %add_convert_fusion.3), channel_id=1, source_target_pairs={{0,2},{1,3},{2,0},{3,1},{4,6},{5,7},{6,4},{7,5},{8,10},{9,11},{10,... | collective-permute-start | bytes 393224 | tf_op jit(solution)/shard_map/ppermute | solution.py:702
  27.6 1.1 %shard_map.127 = (bf16[1,128,512]{2,1,0:T(8,128)(2,1)}, bf16[1,64,512]{2,1,0:T(8,128)(2,1)}) custom-call(bf16[512,1536]{1,0:T(8,128)(2,1)S(1)} %get-tuple-element.45.refs_4_.turned_ref, s32[3,1,16]{2,1,0:T(1,128)S(1)} %bitcast.6, bf16[48,512]{1,0:T(8,128)(2,1)S(1)} %get-tuple-element.73.own_slot_ref, ...), custom_call_target="tpu_custom_call" | custom-call | flops 100000000 | bytes 4194304 | tf_op jit(solution)/shard_map/pallas_call | solution.py:689
  28.7 2.7 %collective-permute-done.10 = bf16[64,1024]{1,0:T(8,128)(2,1)S(1)} collective-permute-done((bf16[64,1024]{1,0:T(8,128)(2,1)S(1)}, bf16[64,1024]{1,0:T(8,128)(2,1)S(1)}, u32[]{:S(2)}, u32[]{:S(2)}) %collective-permute-start.10) | collective-permute-done | bytes 131104 | tf_op jit(solution)/shard_map/ppermute | solution.py:702
  31.5 0.1 collective-permute-start.11
  31.6 1.8 %collective-permute-done.7 = bf16[64,1024]{1,0:T(8,128)(2,1)S(1)} collective-permute-done((bf16[64,1024]{1,0:T(8,128)(2,1)S(1)}, bf16[64,1024]{1,0:T(8,128)(2,1)S(1)}, u32[]{:S(2)}, u32[]{:S(2)}) %collective-permute-start.7) | collective-permute-done | bytes 131104 | tf_op jit(solution)/shard_map/ppermute | solution.py:702
  33.4 0.1 collective-permute-start.8
  33.4 0.9 %shard_map.128.settled_ref = f32[128,2048]{1,0:T(8,128)} custom-call(bf16[64,1024]{1,0:T(8,128)(2,1)S(1)} %add_convert_fusion.2.one_ref, bf16[64,1024]{1,0:T(8,128)(2,1)S(1)} %add_convert_fusion.two_ref, bf16[64,1024]{1,0:T(8,128)(2,1)S(1)} %collective-permute-done.11.other_two_ref), custom_call_target="tpu_custom_call" | custom-call | tf_op jit(solution)/shard_map/pallas_call | solution.py:905
  34.4 0.4 %collective-permute-done.8.other_one_ref = bf16[64,1024]{1,0:T(8,128)(2,1)S(1)} collective-permute-done((bf16[64,1024]{1,0:T(8,128)(2,1)S(1)}, bf16[64,1024]{1,0:T(8,128)(2,1)S(1)}, u32[]{:S(2)}, u32[]{:S(2)}) %collective-permute-start.8) | collective-permute-done | bytes 131104 | tf_op jit(solution)/shard_map/ppermute | solution.py:702
  34.8 0.7 %shard_map.129 = f32[128,2048]{1,0:T(8,128)} custom-call(bf16[64,1024]{1,0:T(8,128)(2,1)S(1)} %collective-permute-done.8.other_one_ref, f32[128,2048]{1,0:T(8,128)} %shard_map.128.settled_ref), custom_call_target="tpu_custom_call", output_to_operand_aliasing={{}: (1, {})} | custom-call | tf_op jit(solution)/shard_map/pallas_call | solution.py:913
  (9 shorter events, 0.1 us)
Async XLA Ops:
  0.6 9.0 %copy-start = (bf16[1,64,512]{2,1,0:T(8,128)(2,1)S(1)}, bf16[1,64,512]{2,1,0:T(8,128)(2,1)}, u32[]{:S(2)}) copy-start(bf16[1,64,512]{2,1,0:T(8,128)(2,1)} %refs_0_.3) | copy-start | bytes 196612
  1.9 13.6 %collective-permute-start.1 = (bf16[120,512]{1,0:T(8,128)(2,1)S(1)}, bf16[120,512]{1,0:T(8,128)(2,1)S(1)}, u32[]{:S(2)}, u32[]{:S(2)}) collective-permute-start(bf16[120,512]{1,0:T(8,128)(2,1)S(1)} %shard_map.121.refs_0_), channel_id=1, source_target_pairs={{0,8},{4,12},{8,0},{12,4},{1,9},{5,13},{9,1},{13,5},{2,10},{6,14},... | collective-permute-start | bytes 368648 | tf_op jit(solution)/shard_map/ppermute | solution.py:702
  6.0 12.3 %collective-permute-start.2 = (bf16[120,512]{1,0:T(8,128)(2,1)S(1)}, bf16[120,512]{1,0:T(8,128)(2,1)S(1)}, u32[]{:S(2)}, u32[]{:S(2)}) collective-permute-start(bf16[120,512]{1,0:T(8,128)(2,1)S(1)} %shard_map.121.refs_0_), channel_id=1, source_target_pairs={{0,12},{4,8},{8,4},{12,0},{1,13},{5,9},{9,5},{13,1},{2,14},{6,10},... | collective-permute-start | bytes 368648 | tf_op jit(solution)/shard_map/ppermute | solution.py:702
  7.3 10.9 %collective-permute-start.3 = (bf16[120,512]{1,0:T(8,128)(2,1)S(1)}, bf16[120,512]{1,0:T(8,128)(2,1)S(1)}, u32[]{:S(2)}, u32[]{:S(2)}) collective-permute-start(bf16[120,512]{1,0:T(8,128)(2,1)S(1)} %shard_map.121.refs_0_), channel_id=1, source_target_pairs={{0,4},{4,0},{8,12},{12,8},{1,5},{5,1},{9,13},{13,9},{2,6},{6,2},{1... | collective-permute-start | bytes 368648 | tf_op jit(solution)/shard_map/ppermute | solution.py:702
  9.7 11.4 %collective-permute-start = (bf16[1,64,512]{2,1,0:T(8,128)(2,1)S(1)}, bf16[1,64,512]{2,1,0:T(8,128)(2,1)S(1)}, u32[]{:S(2)}, u32[]{:S(2)}) collective-permute-start(bf16[1,64,512]{2,1,0:T(8,128)(2,1)S(1)} %copy-done), channel_id=1, source_target_pairs={{0,4},{4,0},{8,12},{12,8},{1,5},{5,1},{9,13},{13,9},{2,6},{6,2},{1... | collective-permute-start | bytes 196616 | tf_op jit(solution)/shard_map/ppermute | solution.py:702
  11.5 10.7 %collective-permute-start.4 = (bf16[1,64,512]{2,1,0:T(8,128)(2,1)S(1)}, bf16[1,64,512]{2,1,0:T(8,128)(2,1)S(1)}, u32[]{:S(2)}, u32[]{:S(2)}) collective-permute-start(bf16[1,64,512]{2,1,0:T(8,128)(2,1)S(1)} %copy-done), channel_id=1, source_target_pairs={{0,8},{4,12},{8,0},{12,4},{1,9},{5,13},{9,1},{13,5},{2,10},{6,14},... | collective-permute-start | bytes 196616 | tf_op jit(solution)/shard_map/ppermute | solution.py:702
  15.5 6.7 %collective-permute-start.5 = (bf16[1,64,512]{2,1,0:T(8,128)(2,1)S(1)}, bf16[1,64,512]{2,1,0:T(8,128)(2,1)S(1)}, u32[]{:S(2)}, u32[]{:S(2)}) collective-permute-start(bf16[1,64,512]{2,1,0:T(8,128)(2,1)S(1)} %copy-done), channel_id=1, source_target_pairs={{0,12},{4,8},{8,4},{12,0},{1,13},{5,9},{9,5},{13,1},{2,14},{6,10},... | collective-permute-start | bytes 196616 | tf_op jit(solution)/shard_map/ppermute | solution.py:702
  23.3 1.7 %collective-permute-start.9 = (bf16[64,1024]{1,0:T(8,128)(2,1)S(1)}, bf16[64,1024]{1,0:T(8,128)(2,1)S(1)}, u32[]{:S(2)}, u32[]{:S(2)}) collective-permute-start(bf16[64,1024]{1,0:T(8,128)(2,1)S(1)} %get-tuple-element.80), channel_id=1, source_target_pairs={{0,1},{1,0},{2,3},{3,2},{4,5},{5,4},{6,7},{7,6},{8,9},{9,8},{10,11... | collective-permute-start | bytes 393224 | tf_op jit(solution)/shard_map/ppermute | solution.py:702
  23.4 4.3 %copy-start.1 = (s32[1,3,16]{2,0,1:T(1,128)S(1)}, s32[1,3,16]{2,0,1:T(1,128)}, u32[]{:S(2)}) copy-start(s32[1,3,16]{2,0,1:T(1,128)} %param.14) | copy-start | bytes 580
  24.4 2.2 %collective-permute-start.6 = (bf16[64,1024]{1,0:T(8,128)(2,1)S(1)}, bf16[64,1024]{1,0:T(8,128)(2,1)S(1)}, u32[]{:S(2)}, u32[]{:S(2)}) collective-permute-start(bf16[64,1024]{1,0:T(8,128)(2,1)S(1)} %get-tuple-element.71), channel_id=1, source_target_pairs={{0,1},{1,0},{2,3},{3,2},{4,5},{5,4},{6,7},{7,6},{8,9},{9,8},{10,11... | collective-permute-start | bytes 393224 | tf_op jit(solution)/shard_map/ppermute | solution.py:702
  25.0 6.4 %collective-permute-start.10 = (bf16[64,1024]{1,0:T(8,128)(2,1)S(1)}, bf16[64,1024]{1,0:T(8,128)(2,1)S(1)}, u32[]{:S(2)}, u32[]{:S(2)}) collective-permute-start(bf16[64,1024]{1,0:T(8,128)(2,1)S(1)} %add_convert_fusion.1), channel_id=1, source_target_pairs={{0,2},{1,3},{2,0},{3,1},{4,6},{5,7},{6,4},{7,5},{8,10},{9,11},{10,... | collective-permute-start | bytes 393224 | tf_op jit(solution)/shard_map/ppermute | solution.py:702
  26.7 6.7 %collective-permute-start.7 = (bf16[64,1024]{1,0:T(8,128)(2,1)S(1)}, bf16[64,1024]{1,0:T(8,128)(2,1)S(1)}, u32[]{:S(2)}, u32[]{:S(2)}) collective-permute-start(bf16[64,1024]{1,0:T(8,128)(2,1)S(1)} %add_convert_fusion.3), channel_id=1, source_target_pairs={{0,2},{1,3},{2,0},{3,1},{4,6},{5,7},{6,4},{7,5},{8,10},{9,11},{10,... | collective-permute-start | bytes 393224 | tf_op jit(solution)/shard_map/ppermute | solution.py:702
  31.5 2.0 %collective-permute-start.11 = (bf16[64,1024]{1,0:T(8,128)(2,1)S(1)}, bf16[64,1024]{1,0:T(8,128)(2,1)S(1)}, u32[]{:S(2)}, u32[]{:S(2)}) collective-permute-start(bf16[64,1024]{1,0:T(8,128)(2,1)S(1)} %add_convert_fusion.two_ref), channel_id=1, source_target_pairs={{0,1},{1,0},{2,3},{3,2},{4,5},{5,4},{6,7},{7,6},{8,9},{9,8},{10,11... | collective-permute-start | bytes 393224 | tf_op jit(solution)/shard_map/ppermute | solution.py:702
  33.4 1.4 %collective-permute-start.8 = (bf16[64,1024]{1,0:T(8,128)(2,1)S(1)}, bf16[64,1024]{1,0:T(8,128)(2,1)S(1)}, u32[]{:S(2)}, u32[]{:S(2)}) collective-permute-start(bf16[64,1024]{1,0:T(8,128)(2,1)S(1)} %add_convert_fusion.2.one_ref), channel_id=1, source_target_pairs={{0,1},{1,0},{2,3},{3,2},{4,5},{5,4},{6,7},{7,6},{8,9},{9,8},{10,11... | collective-permute-start | bytes 393224 | tf_op jit(solution)/shard_map/ppermute | solution.py:702
